TPU v7x, 128 devices: a whole 4x4x4 slice. The times are simulated.
128 devices in a mesh: dp: 8 (over y, x_lo), seq: 16 (over x_hi, z, core).
Axes of the slice: x: 4 (x_hi: 2, x_lo: 2; x = x_hi * 2 + x_lo), y: 4, z: 4, core: 2. Of those that a mesh axis runs over, the one named last changes fastest.
Arguments:
- tokens_in: bfloat16 [8, 2048, 12288], P('dp', 'seq'), may hold values from -6 to 6
- short_filter: float32 [7, 12288], replicated, may hold values from -2 to 2
- long_filter: bfloat16 [256, 128], replicated, may hold values from -0.5 to 0.5
- out_weight: bfloat16 [4096, 4096], P('dp', 'seq'), may hold values from -0.09375 to 0.09375
- cotangent: bfloat16 [8, 2048, 4096], P('dp', None, 'seq'), may hold values from -6 to 6
Outputs:
- block_out: bfloat16 [8, 2048, 4096], P('dp', None, 'seq')
- grad_tokens: bfloat16 [8, 2048, 12288], P('dp', 'seq')
- grad_short: float32 [7, 12288], replicated
- grad_long: float32 [256, 128], replicated
- grad_weight: float32 [4096, 4096], P('dp', 'seq')
All inputs are finite; a program needn't handle non-finite values.
Results may differ from a plain program's by a relative error of at most 0.023.
Values may be sent and summed in bfloat16 or wider, within the bound.
No kernel may reach another device: no remote copies, remote signals or barrier semaphores. Data moves between devices by JAX's collectives and lax.ppermute only.
A program may use at most 192 MiB of HBM per device.

v0:
```python
import jax
import jax.numpy as jnp
from jax import lax
from jax.sharding import PartitionSpec as P


def shifted(x, axis, by):
    size = lax.axis_size(axis)
    pairs = [(i, i + by) for i in range(size) if 0 <= i + by < size]
    return lax.ppermute(x, axis, pairs)


def tap_table(filters, tap_index):
    tap_count = filters.shape[1]
    valid = (tap_index >= 0) & (tap_index < tap_count)
    clipped = jnp.clip(tap_index, 0, tap_count - 1)
    taken = jnp.take(filters, clipped, axis=1)
    return jnp.where(valid[None], taken, jnp.zeros((), filters.dtype))


def forward_table(filters):
    tap_count = filters.shape[1]
    row_pos = jnp.arange(tap_count, dtype=jnp.int32)[:, None]
    col_pos = jnp.arange(2 * tap_count, dtype=jnp.int32)[None, :]
    return tap_table(filters, row_pos + tap_count - col_pos)


def adjoint_table(filters):
    tap_count = filters.shape[1]
    row_pos = jnp.arange(tap_count, dtype=jnp.int32)[:, None]
    col_pos = jnp.arange(2 * tap_count, dtype=jnp.int32)[None, :]
    return tap_table(filters, col_pos - row_pos)


def windows(padded, row_count, tap_count, group_count):
    channels = padded.shape[1]
    blocks = row_count // tap_count
    leading = padded[:row_count].reshape(blocks, tap_count, group_count, channels // group_count)
    trailing = padded[tap_count : tap_count + row_count].reshape(
        blocks, tap_count, group_count, channels // group_count
    )
    return jnp.concatenate([leading, trailing], axis=1)


def medium_grad(grad_in, window, tap_count, group_count):
    blocks = grad_in.shape[0] // tap_count
    grad_blocks = grad_in.reshape(blocks, tap_count, group_count, -1)
    products = jnp.einsum("bigk,brgk->gir", grad_blocks, window, preferred_element_type=jnp.float32)
    flattened = products.reshape(group_count, tap_count * 2 * tap_count)
    flattened = jnp.concatenate(
        [flattened, jnp.zeros((group_count, tap_count), jnp.float32)], axis=1
    )
    skewed = flattened.reshape(group_count, tap_count, 2 * tap_count + 1)
    summed = jnp.sum(skewed[:, :, 1 : tap_count + 1], axis=1)
    return summed[:, ::-1]


def short_forward(extended, weights, row_count):
    short_taps = weights.shape[0]
    accumulated = jnp.zeros((row_count, extended.shape[1]), jnp.float32)
    for tap_index in range(short_taps):
        start_row = short_taps - 1 - tap_index
        accumulated = accumulated + weights[tap_index] * extended[
            start_row : start_row + row_count
        ].astype(jnp.float32)
    return accumulated


def short_adjoint(extended, weights, row_count):
    short_taps = weights.shape[0]
    accumulated = jnp.zeros((row_count, extended.shape[1]), jnp.float32)
    for tap_index in range(short_taps):
        accumulated = accumulated + weights[tap_index] * extended[
            tap_index : tap_index + row_count
        ].astype(jnp.float32)
    return accumulated


def short_grad(grads, extended, row_count):
    short_taps = extended.shape[0] - row_count + 1
    grads_wide = grads.astype(jnp.float32)
    pieces_list = []
    for tap_index in range(short_taps):
        start_row = short_taps - 1 - tap_index
        pieces_list.append(
            jnp.sum(
                grads_wide * extended[start_row : start_row + row_count].astype(jnp.float32), axis=0
            )
        )
    return jnp.stack(pieces_list, axis=0)


def shards(tokens_in, short_filter, long_filter, out_weight, cotangent):
    tokens = tokens_in[0]
    row_count = tokens.shape[0]
    channels = tokens.shape[1] // 3
    short_taps = short_filter.shape[0]
    tap_count = long_filter.shape[1]
    group_count = long_filter.shape[0]
    lead_rim = shifted(tokens[row_count - (short_taps - 1) :], "seq", 1)
    u_ext = jnp.concatenate([lead_rim, tokens], axis=0)
    features = short_forward(u_ext, short_filter, row_count)
    query_part = features[:, :channels]
    key_part = features[:, channels : 2 * channels]
    value_part = features[:, 2 * channels :]
    mixer_in = (key_part * value_part).astype(jnp.bfloat16)
    mixer_lead = shifted(mixer_in[row_count - (tap_count - 1) :], "seq", 1)
    padded = jnp.concatenate([jnp.zeros((1, channels), jnp.bfloat16), mixer_lead, mixer_in], axis=0)
    window = windows(padded, row_count, tap_count, group_count)
    mixed = jnp.einsum(
        "gir,brgk->bigk", forward_table(long_filter), window, preferred_element_type=jnp.float32
    )
    mixed = mixed.reshape(row_count, channels)
    gated = (query_part * mixed).astype(jnp.bfloat16)
    weights = lax.all_gather(out_weight, "dp", axis=0, tiled=True)
    upstream = cotangent[0]
    all_rows = lax.all_gather(gated, "seq", axis=0, tiled=True)
    output = jnp.dot(all_rows, weights, preferred_element_type=jnp.float32)
    weight_grad = lax.dot_general(
        all_rows, upstream, (((0,), (0,)), ((), ())), preferred_element_type=jnp.float32
    )
    grad_weight = lax.psum_scatter(
        weight_grad.astype(jnp.bfloat16), "dp", scatter_dimension=0, tiled=True
    ).astype(jnp.float32)
    grad_gated = lax.psum_scatter(
        lax.dot_general(
            upstream, weights, (((1,), (1,)), ((), ())), preferred_element_type=jnp.float32
        ).astype(jnp.bfloat16),
        "seq",
        scatter_dimension=0,
        tiled=True,
    ).astype(jnp.float32)
    grad_mixed_in = (grad_gated * query_part).astype(jnp.bfloat16)
    grad_next = shifted(grad_mixed_in[: tap_count - 1], "seq", -1)
    grad_pad = jnp.concatenate(
        [grad_mixed_in, grad_next, jnp.zeros((1, channels), jnp.bfloat16)], axis=0
    )
    grad_window = windows(grad_pad, row_count, tap_count, group_count)
    grad_mixer = jnp.einsum(
        "gpq,bqgk->bpgk",
        adjoint_table(long_filter),
        grad_window,
        preferred_element_type=jnp.float32,
    )
    grad_mixer = grad_mixer.reshape(row_count, channels)
    grad_features = jnp.concatenate(
        [grad_gated * mixed, grad_mixer * value_part, grad_mixer * key_part], axis=1
    ).astype(jnp.bfloat16)
    long_local = medium_grad(grad_mixed_in, window, tap_count, group_count)
    grad_long = lax.psum(long_local, ("dp", "seq"))
    feature_next = shifted(grad_features[: short_taps - 1], "seq", -1)
    grad_ext = jnp.concatenate([grad_features, feature_next], axis=0)
    grad_tokens = short_adjoint(grad_ext, short_filter, row_count).astype(jnp.bfloat16)
    short_local = short_grad(grad_features, u_ext, row_count)
    grad_short = lax.psum(short_local, ("dp", "seq"))
    return (
        output.astype(jnp.bfloat16)[None],
        grad_tokens[None],
        grad_short,
        grad_long,
        grad_weight,
    )


def solution(mesh):
    return jax.shard_map(
        shards,
        mesh=mesh,
        in_specs=(P("dp", "seq", None), P(), P(), P("dp", "seq"), P("dp", None, "seq")),
        out_specs=(P("dp", None, "seq"), P("dp", "seq", None), P(), P(), P("dp", "seq")),
        check_vma=False,
    )
```

profile of v0, /device:TPU:1, one launch (start us, length us, event | category | flops | bytes accessed | tf_op | source)
XLA Modules:
  0.0 927.1 jit_solution(1528548051967703106)
XLA Ops:
  7.2 0.0 all-gather.5.cloned.1.call-start
  7.2 0.7 all-gather.5.cloned.1.call-update
  7.9 0.0 reduce-scatter.3.cloned.1.call-start
  8.0 56.8 %all-gather.5.cloned.1.call-done = bf16[4096,256]{1,0:T(8,128)(2,1)} async-done(((bf16[512,256]{1,0:T(8,128)(2,1)}), bf16[4096,256]{1,0:T(8,128)(2,1)}) %all-gather.5.cloned.1.call-update) | async-done | bytes 2097168 | tf_op jit(solution)/shard_map/all_gather | solution.py:115
  64.8 9.7 %convolution_convert_fusion = bf16[2048,4096]{1,0:T(8,128)(2,1)} fusion(bf16[4096,256]{1,0:T(8,128)(2,1)} %all-gather.5.cloned.1.call-done, bf16[1,2048,256]{2,1,0:T(8,128)(2,1)S(1)} %copy-done), kind=kOutput, calls=%fused_computation.21 | convolution fusion | flops 4303355904 | bytes 19922944 | tf_op jit(solution)/shard_map/dot_general | solution.py:126
  74.5 0.0 all-gather.3.cloned.1.call-start
  74.6 1.0 slice_bitcast_fusion
  75.6 4.0 collective-permute-start
  79.6 0.2 fusion.67
  79.9 0.1 fusion.53
  80.0 2.1 collective-permute-done
  82.2 0.6 copy-done.7
  82.8 16.0 %fusion.17 = f32[128,12288]{1,0:T(8,128)} fusion(bf16[128,12288]{1,0:T(8,128)(2,1)} %bitcast.75, bf16[6,12288]{1,0:T(8,128)(2,1)S(1)} %collective-permute-done, f32[12288]{0:T(1024)S(1)} %bitcast.99, f32[12288]{0:T(1024)S(1)} %bitcast.101, f32[12288]{0:T(1024)S(1)} %bitcast.91, f32[12288]{0:T(1024)S(1)} %bitcast.93, f32[12288]{0:T(1024)S(1)} %bitcast.95, ...), kind=kLoop, calls=%fused_computation.43 | loop fusion | flops 59768832 | bytes 9928704 | tf_op jit(solution)/shard_map/add | solution.py:63
  98.8 121.9 %reduce-scatter.3.cloned.1.call-done = bf16[128,4096]{1,0:T(8,128)(2,1)} async-done(((bf16[2048,4096]{1,0:T(8,128)(2,1)}), bf16[128,4096]{1,0:T(8,128)(2,1)}) %reduce-scatter.3.cloned.1.call-update) | async-done | bytes 1048592 | tf_op jit(solution)/shard_map/reduce_scatter | solution.py:125
  220.8 2.1 fusion.40
  222.9 3.5 collective-permute-start.2
  226.4 0.1 copy.38
  226.6 0.1 copy.54
  226.6 0.1 copy.55
  226.7 129.4 %gather_fusion.1 = bf16[32768,256]{1,0:T(8,128)(2,1)} fusion(bf16[256,128]{0,1:T(8,128)(2,1)S(1)} %copy.38, s32[32768]{0:T(1024)S(1)} %broadcast_clamp_fusion), kind=kCustom, calls=%fused_computation.1.clone | custom fusion | bytes 33685504 | tf_op jit(solution)/shard_map/jit(_take)/gather | solution.py:17
  356.2 23.0 %copy.45 = bf16[128,256,256]{1,0,2:T(8,128)(2,1)} copy(bf16[128,256,256]{2,1,0:T(8,128)(2,1)} %bitcast.74) | data formatting | bytes 33554432 | tf_op jit(solution)/shard_map/jit(_take)/gather | solution.py:17
  379.2 0.1 fusion.57
  379.3 0.7 copy.42
  380.0 2.0 copy.53
  382.0 1.2 concatenate.28.clone
  383.2 11.9 %fusion = f32[256,16,128]{2,1,0:T(8,128)} fusion(bf16[128,256,256]{1,0,2:T(8,128)(2,1)} %copy.45, pred[128,256]{1,0:T(8,128)(4,1)S(1)} %get-tuple-element.38, pred[128,256]{1,0:T(8,128)(4,1)S(1)} %get-tuple-element.39, bf16[1,128,256,16]{1,3,2,0:T(8,128)(2,1)} %bitcast.86, bf16[1,128,256,16]{1,3,2,0:T(8,128)(2,1)S(1)} %bitcast.79), kind=kOutput, calls=%fused_computation.12 | convolution fusion | flops 289406976 | bytes 21037056 | tf_op jit(solution)/shard_map/gpq,bqgk->bpgk/dot_general | solution.py:139
  395.1 2.9 copy.46
  398.0 3.4 multiply_convert_fusion.1
  401.5 1.0 copy-done.2
  402.5 1.2 slice.142
  403.7 2.9 collective-permute-start.1
  406.6 129.4 %gather_fusion = bf16[32768,256]{1,0:T(8,128)(2,1)} fusion(bf16[256,128]{0,1:T(8,128)(2,1)S(1)} %copy.38, s32[32768]{0:T(1024)S(1)} %broadcast_clamp_fusion.1), kind=kCustom, calls=%fused_computation.clone | custom fusion | bytes 33685504 | tf_op jit(solution)/shard_map/jit(_take)/gather | solution.py:17
  536.1 23.0 %copy.39 = bf16[128,256,256]{1,0,2:T(8,128)(2,1)} copy(bf16[128,256,256]{2,1,0:T(8,128)(2,1)} %bitcast.73) | data formatting | bytes 33554432 | tf_op jit(solution)/shard_map/jit(_take)/gather | solution.py:17
  559.1 0.2 fusion.58
  559.3 2.3 copy.37
  561.5 2.3 copy.52
  563.8 2.6 concatenate.26.clone
  566.4 12.2 %fusion.1 = f32[256,16,128]{2,1,0:T(8,128)} fusion(bf16[128,256,256]{1,0,2:T(8,128)(2,1)} %copy.39, pred[128,256]{1,0:T(8,128)(4,1)S(1)} %get-tuple-element.37, pred[128,256]{1,0:T(8,128)(4,1)S(1)} %get-tuple-element.36, bf16[1,128,256,16]{1,3,2,0:T(8,128)(2,1)} %bitcast.81, bf16[1,128,256,16]{1,3,2,0:T(8,128)(2,1)} %bitcast.77), kind=kOutput, calls=%fused_computation.14 | convolution fusion | flops 289406976 | bytes 21037056 | tf_op jit(solution)/shard_map/gir,brgk->bigk/dot_general | solution.py:110
  578.6 2.9 copy.40
  581.6 4.3 fusion.39
  585.9 0.0 all-reduce.6.cloned.1.call-start
  586.0 1.5 pad_maximum_fusion.2
  587.5 0.7 slice.144
  588.2 3.1 collective-permute-start.3
  591.3 14.1 %fusion.43 = f32[256,128,256]{2,1,0:T(8,128)} fusion(bf16[128,256,16]{0,2,1:T(8,128)(2,1)S(1)} %bitcast.80, bf16[1,128,256,16]{1,3,2,0:T(8,128)(2,1)S(1)} %bitcast.82, bf16[1,128,256,16]{1,3,2,0:T(8,128)(2,1)S(1)} %bitcast.78), kind=kOutput, calls=%fused_computation.82 | convolution fusion | flops 272629760 | bytes 36700160 | tf_op jit(solution)/shard_map/bigk,brgk->gir/dot_general | solution.py:48
  605.4 35.0 %copy.51 = f32[256,128,256]{0,2,1:T(8,128)} copy(f32[256,128,256]{2,1,0:T(8,128)} %fusion.43) | data formatting | bytes 67108864 | tf_op jit(solution)/shard_map/reshape | solution.py:49
  640.4 22.5 %concatenate.32 = f32[256,32896]{0,1:T(8,128)} pad(f32[256,32768]{0,1:T(8,128)} %bitcast.72, f32[]{:T(128)} %constant.2.clone.1), padding=0_0x0_128 | pad | bytes 67239936 | tf_op jit(solution)/shard_map/concatenate | solution.py:50
  662.9 28.5 %reshape.106 = f32[256,128,257]{0,2,1:T(8,128)} reshape(f32[256,32896]{0,1:T(8,128)} %concatenate.32) | data formatting | bytes 67371008 | tf_op jit(solution)/shard_map/reshape | solution.py:53
  691.4 8.5 slice_reduce_fusion
  699.9 0.7 rev.3
  700.6 15.4 %fusion.30 = (f32[12288]{0:T(1024)S(1)}, f32[12288]{0:T(1024)S(1)}, f32[12288]{0:T(1024)S(1)}, f32[12288]{0:T(1024)S(1)}, f32[12288]{0:T(1024)}, /*index=5*/f32[12288]{0:T(1024)}, f32[12288]{0:T(1024)}) fusion(bf16[128,12288]{1,0:T(8,128)(2,1)} %bitcast.76, bf16[6,12288]{1,0:T(8,128)(2,1)S(1)} %copy-done.8, bf16[128,4096]{1,0:T(8,128)(2,1)S(1)} %get-tuple-element.21, ...), kind=kLoop, calls=%fused_computation.56 | loop fusion | flops 70692864 | bytes 9928704 | tf_op jit(solution)/shard_map/reduce_sum | solution.py:86
  716.0 1.9 stack.31
  717.9 0.3 reduce-scatter.5.cloned.1.call-start
  718.2 0.0 all-gather.3.cloned.1.call-done
  718.2 9.8 %convolution_convert_fusion.1 = bf16[4096,256]{1,0:T(8,128)(2,1)} fusion(bf16[2048,4096]{1,0:T(8,128)(2,1)} %all-gather.3.cloned.1.call-done, bf16[1,2048,256]{2,1,0:T(8,128)(2,1)S(1)} %copy-done), kind=kOutput, calls=%fused_computation.58 | convolution fusion | flops 4296015872 | bytes 19922944 | tf_op jit(solution)/shard_map/dot_general | solution.py:119
  728.1 0.0 reduce-scatter.5.cloned.1.call-update
  728.1 3.6 pad_maximum_fusion
  731.8 8.1 fusion.37
  739.9 124.6 %all-reduce.6.cloned.1.call-done = (f32[7,12288]{1,0:T(8,128)}, f32[256,128]{0,1:T(8,128)}) async-done(((f32[7,12288]{1,0:T(8,128)}, f32[256,128]{0,1:T(8,128)}), (f32[7,12288]{1,0:T(8,128)}, f32[256,128]{0,1:T(8,128)})) %all-reduce.6.cloned.1.call-update) | async-done | bytes 475152 | tf_op jit(solution)/shard_map/psum | solution.py:155
  864.5 1.7 copy.50
  866.2 12.1 %fusion.38 = bf16[1,2048,256]{2,1,0:T(8,128)(2,1)} fusion(bf16[2048,4096]{1,0:T(8,128)(2,1)} %all-gather.3.cloned.1.call-done, bf16[4096,256]{1,0:T(8,128)(2,1)} %all-gather.5.cloned.1.call-done), kind=kOutput, calls=%fused_computation.71 | convolution fusion | flops 4295491584 | bytes 19922944 | tf_op jit(solution)/shard_map/dot_general | solution.py:118
  878.3 39.6 %reduce-scatter.5.cloned.1.call-done = bf16[512,256]{1,0:T(8,128)(2,1)} async-done(((bf16[4096,256]{1,0:T(8,128)(2,1)}), bf16[512,256]{1,0:T(8,128)(2,1)}) %reduce-scatter.5.cloned.1.call-update) | async-done | bytes 262160 | tf_op jit(solution)/shard_map/reduce_scatter | solution.py:122
  917.9 1.8 convert_element_type.100
  919.6 0.7 copy.58
  (60 shorter events, 0.2 us)
Async XLA Ops:
  7.2 57.6 %copy-start = (bf16[1,2048,256]{2,1,0:T(8,128)(2,1)S(1)}, bf16[1,2048,256]{2,1,0:T(8,128)(2,1)}, u32[]{:S(2)}) copy-start(bf16[1,2048,256]{2,1,0:T(8,128)(2,1)} %param.11) | copy-start | bytes 3145732
  7.2 57.6 %all-gather.5.cloned.1.call-start = ((), (), s32[]{:S(2)}) async-start(), calls=%async_computation.3 | async-start | bytes 2359296 | tf_op jit(solution)/shard_map/all_gather | solution.py:115
  7.9 212.9 %reduce-scatter.3.cloned.1.call-start = ((), (), s32[]{:S(2)}) async-start(), calls=%async_computation.4 | async-start | bytes 17825792 | tf_op jit(solution)/shard_map/reduce_scatter | solution.py:125
  74.5 5.1 copy-start.24
  74.5 643.7 %all-gather.3.cloned.1.call-start = ((), (), s32[]{:S(2)}) async-start(), calls=%async_computation.2 | async-start | bytes 17825792 | tf_op jit(solution)/shard_map/all_gather | solution.py:117
  75.6 6.6 collective-permute-start
  79.8 2.3 copy-start.9
  79.8 2.3 copy-start.11
  79.9 2.3 copy-start.13
  79.9 2.3 copy-start.15
  79.9 2.3 copy-start.17
  79.9 2.3 copy-start.19
  79.9 2.3 copy-start.21
  82.2 0.7 copy-start.7
  82.8 143.6 %copy-start.25 = (bf16[256,128]{1,0:T(8,128)(2,1)S(1)}, bf16[256,128]{1,0:T(8,128)(2,1)}, u32[]{:S(2)}) copy-start(bf16[256,128]{1,0:T(8,128)(2,1)} %param.9) | copy-start | bytes 196612
  222.9 157.0 %collective-permute-start.2 = (bf16[127,4096]{1,0:T(8,128)(2,1)S(1)}, bf16[127,4096]{1,0:T(8,128)(2,1)}, u32[]{:S(2)}, u32[]{:S(2)}) collective-permute-start(bf16[127,4096]{1,0:T(8,128)(2,1)S(1)} %bitcast.83), channel_id=1, source_target_pairs={{1,0},{2,1},{3,2},{4,3},{5,4},{6,5},{7,6},{8,7},{9,8},{10,9},{11,1... | collective-permute-start | bytes 3121160 | tf_op jit(solution)/shard_map/ppermute | solution.py:10
  379.9 15.1 %copy-start.4 = (bf16[128,4096]{0,1:T(8,128)(2,1)}, bf16[128,4096]{0,1:T(8,128)(2,1)S(1)}, u32[]{:S(2)}) copy-start(bf16[128,4096]{0,1:T(8,128)(2,1)S(1)} %copy.42) | copy-start | bytes 3145732
  401.5 1.0 copy-start.2
  403.7 157.8 %collective-permute-start.1 = (bf16[127,4096]{1,0:T(8,128)(2,1)}, bf16[127,4096]{1,0:T(8,128)(2,1)}, u32[]{:S(2)}, u32[]{:S(2)}) collective-permute-start(bf16[127,4096]{1,0:T(8,128)(2,1)} %slice.142), channel_id=1, source_target_pairs={{0,1},{1,2},{2,3},{3,4},{4,5},{5,6},{6,7},{7,8},{8,9},{9,10},{10,1... | collective-permute-start | bytes 3121160 | tf_op jit(solution)/shard_map/ppermute | solution.py:10
  585.9 278.6 %all-reduce.6.cloned.1.call-start = ((), (), s32[]{:S(2)}) async-start(), calls=%async_computation.6 | async-start | bytes 1048576 | tf_op jit(solution)/shard_map/psum | solution.py:155
  586.0 5.3 copy-start.3
  586.0 5.3 copy-start.5
  586.0 5.3 copy-start.6
  588.2 140.0 %collective-permute-start.3 = (bf16[6,12288]{1,0:T(8,128)(2,1)}, bf16[6,12288]{1,0:T(8,128)(2,1)}, u32[]{:S(2)}, u32[]{:S(2)}) collective-permute-start(bf16[6,12288]{1,0:T(8,128)(2,1)} %slice.144), channel_id=1, source_target_pairs={{1,0},{2,1},{3,2},{4,3},{5,4},{6,5},{7,6},{8,7},{9,8},{10,9},{11,1... | collective-permute-start | bytes 442376 | tf_op jit(solution)/shard_map/ppermute | solution.py:10
  691.4 9.2 copy-start.8
  717.9 199.9 %reduce-scatter.5.cloned.1.call-start = ((), (), s32[]{:S(2)}) async-start(), calls=%async_computation.5 | async-start | bytes 2359296 | tf_op jit(solution)/shard_map/reduce_scatter | solution.py:122
  728.0 3.7 copy-start.10
  728.0 3.7 copy-start.12
  728.0 3.7 copy-start.14
  728.0 3.8 copy-start.16
  728.1 3.8 copy-start.18
  728.1 3.8 copy-start.20
  728.1 3.8 copy-start.22
  728.1 3.7 copy-start.1
  866.2 53.5 %copy-start.23 = (f32[7,12288]{1,0:T(8,128)S(1)}, f32[7,12288]{1,0:T(8,128)}, u32[]{:S(2)}) copy-start(f32[7,12288]{1,0:T(8,128)} %get-tuple-element.42) | copy-start | bytes 1032196
Sparse Core Ops, SparseCore 0:
  9.7 55.0 all-gather.4
  74.7 146.0 reduce-scatter.2
  586.0 109.3 all-gather.2
  718.1 146.4 all-reduce.5
  866.9 50.9 reduce-scatter.4
where the time goes:
time: 934 us; the launch traced here: 927 us
  local copies, waits for them, and re-layouts  418 us (45%)
  waiting for transfers between devices  346 us (37%)
  matrix products  69.8 us (7%)
  other arithmetic  65.1 us (7%)
  between operations  14.5 us (2%)
  starting transfers between devices  13.8 us (1%)
    gather x4, local copies, waits for them, and re-layouts, tap_table(): taken = jnp.take(filters, clipped, axis=1)  305 us
    psum x1, waiting for transfers between devices, shards(): grad_short = lax.psum(short_local, ('dp', 'seq'))  125 us
    reduce_scatter x1, waiting for transfers between devices, shards(): lax.psum_scatter(lax.dot_general(upstream, weights, (((1,), (1,)), ((), (...  122 us
    all_gather x1, waiting for transfers between devices, shards(): weights = lax.all_gather(out_weight, 'dp', axis=0, tiled=True)  56.8 us
    reduce_scatter x1, waiting for transfers between devices, shards(): lax.psum_scatter(weight_grad.astype(jnp.bfloat16), 'dp', scatter_dimensio...  39.6 us
    reshape x1, local copies, waits for them, and re-layouts, medium_grad(): flattened = products.reshape(group_count, tap_count * 2 * tap_count)  35 us
    reshape x1, local copies, waits for them, and re-layouts, medium_grad(): skewed = flattened.reshape(group_count, tap_count, 2 * tap_count + 1)  28.5 us
    concatenate x1, local copies, waits for them, and re-layouts, medium_grad(): jnp.concatenate([flattened, jnp.zeros((group_count, tap_count), jnp.float...  22.5 us
  transfers between devices with their start and end apart: 9, of which 5 were waited for; matrix products, arithmetic and copies ran while one was open for 53% of the time, Pallas kernels for 0%

commit v1 on v0

v1 whole, which is shorter than its diff:
```python
import functools

import jax
import jax.numpy as jnp
from jax import lax
from jax.experimental import pallas as pl
from jax.experimental.pallas import tpu as pltpu
from jax.sharding import PartitionSpec as P

LANES = 128
RIM = 8
VMEM = 48 * 1024 * 1024
F32 = jnp.float32
BF16 = jnp.bfloat16


def shifted(x, axis, by):
    size = lax.axis_size(axis)
    pairs = [(i, i + by) for i in range(size) if 0 <= i + by < size]
    return lax.ppermute(x, axis, pairs)


def params():
    return pltpu.CompilerParams(vmem_limit_bytes=VMEM)


def cost(flops, moved):
    return pl.CostEstimate(flops=int(flops), bytes_accessed=int(moved), transcendentals=0)


def block_width(channels, most):
    width = min(channels, most)
    while channels % width:
        width //= 2
    return width


def features_kernel(short_taps, tokens, rims, filters, query_ref, key_ref, value_ref, mixer_ref):
    rows = tokens[0].shape[0]

    def filtered(part):
        ext = jnp.concatenate([rims[part][...].astype(F32), tokens[part][...].astype(F32)], axis=0)
        total = filters[part][0:1, :] * ext[RIM : RIM + rows]
        for tap in range(1, short_taps):
            total = total + filters[part][tap : tap + 1, :] * ext[RIM - tap : RIM - tap + rows]
        return total

    query_ref[...] = filtered(0).astype(BF16)
    key, value = filtered(1), filtered(2)
    key_ref[...] = key.astype(BF16)
    value_ref[...] = value.astype(BF16)
    mixer_ref[...] = (key * value).astype(BF16)


def features_call(tokens, rim, filters):
    rows, wide = tokens.shape
    channels = wide // 3
    taps = filters.shape[0]
    width = block_width(channels, 512)
    steps = channels // width

    def spec(height, part):
        return pl.BlockSpec((height, width), lambda i, part=part: (0, i + part * steps))

    def body(*refs):
        features_kernel(taps, refs[0:3], refs[3:6], refs[6:9], *refs[9:])

    out = jax.ShapeDtypeStruct((rows, channels), BF16)
    return pl.pallas_call(
        body,
        grid=(steps,),
        in_specs=[spec(rows, p) for p in range(3)]
        + [spec(RIM, p) for p in range(3)]
        + [spec(taps, p) for p in range(3)],
        out_specs=[pl.BlockSpec((rows, width), lambda i: (0, i))] * 4,
        out_shape=[out] * 4,
        compiler_params=params(),
        cost_estimate=cost(2 * taps * rows * wide, 10 * rows * wide),
        name="features",
    )(tokens, tokens, tokens, rim, rim, rim, filters, filters, filters)


def lane_row(shape):
    row = lax.broadcasted_iota(jnp.int32, shape, 0)
    lane = lax.broadcasted_iota(jnp.int32, shape, 1)
    return row, lane


def circulant(line, taps):
    wide = jnp.broadcast_to(line.astype(F32), (taps, taps))
    return pltpu.roll(wide, 0, 1, stride=1, stride_axis=0)


def pick_groups(product, rows, per_group):
    lane = lax.broadcasted_iota(jnp.int32, (rows, LANES), 1) // per_group
    total = product[0:rows]
    for g in range(1, LANES // per_group):
        total = jnp.where(lane == g, product[g * rows : (g + 1) * rows], total)
    return total


def mix_kernel(per_group, lines_ref, prev_ref, cur_ref, query_ref, mixed_ref, gated_ref, table):
    rows, width = cur_ref.shape
    row, lane = lane_row((rows, rows))
    above = lane > row
    packed = LANES // per_group
    for block in range(width // LANES):
        at = pl.ds(block * LANES, LANES)
        for g in range(packed):
            ring = circulant(lines_ref[block * packed + g : block * packed + g + 1, :], rows)
            table[g * rows : (g + 1) * rows, 0:rows] = jnp.where(above, ring, 0.0).astype(BF16)
            table[g * rows : (g + 1) * rows, rows : 2 * rows] = jnp.where(above, 0.0, ring).astype(BF16)
        window = jnp.concatenate([prev_ref[:, at], cur_ref[:, at]], axis=0)
        product = jnp.dot(table[...], window, preferred_element_type=F32)
        mixed = pick_groups(product, rows, per_group)
        mixed_ref[:, at] = mixed.astype(BF16)
        gated_ref[:, at] = (query_ref[:, at].astype(F32) * mixed).astype(BF16)


def mix_call(lines, prev, cur, query):
    rows, channels = cur.shape
    groups, taps = lines.shape
    per_group = channels // groups
    width = block_width(channels, 512)
    steps = channels // width
    wide = pl.BlockSpec((rows, width), lambda i: (0, i))
    out = jax.ShapeDtypeStruct((rows, channels), BF16)
    return pl.pallas_call(
        functools.partial(mix_kernel, per_group),
        grid=(steps,),
        in_specs=[pl.BlockSpec((width // per_group, taps), lambda i: (i, 0)), wide, wide, wide],
        out_specs=[wide, wide],
        out_shape=[out, out],
        scratch_shapes=[pltpu.VMEM((LANES // per_group * rows, 2 * rows), BF16)],
        compiler_params=params(),
        cost_estimate=cost(2 * groups * rows * 2 * rows * LANES, 10 * rows * channels),
        name="mix",
    )(lines, prev, cur, query)


def unmix_kernel(
    per_group, lines_ref, prev_ref, cur_ref, grad_ref, next_ref, gate_grad_ref, mixed_ref,
    key_ref, value_ref, feature_ref, long_ref, table, fold,
):
    rows, width = cur_ref.shape
    row, lane = lane_row((rows, rows))
    above = lane > row
    below = lane < row
    member = lax.broadcasted_iota(jnp.int32, (rows, LANES), 1) // per_group
    packed = LANES // per_group
    for block in range(width // LANES):
        at = pl.ds(block * LANES, LANES)
        grad = grad_ref[:, at]
        for g in range(packed):
            ring = circulant(lines_ref[block * packed + g : block * packed + g + 1, :], rows)
            table[g * rows : (g + 1) * rows, 0:rows] = jnp.where(below, 0.0, ring).astype(BF16)
            table[g * rows : (g + 1) * rows, rows : 2 * rows] = jnp.where(below, ring, 0.0).astype(BF16)
        grad_window = jnp.concatenate([grad, next_ref[:, at]], axis=0)
        product = jnp.dot(table[...], grad_window, preferred_element_type=F32)
        grad_mixer = pick_groups(product, rows, per_group)
        feature_ref[0, :, at] = (gate_grad_ref[:, at].astype(F32) * mixed_ref[:, at].astype(F32)).astype(BF16)
        feature_ref[1, :, at] = (grad_mixer * value_ref[:, at].astype(F32)).astype(BF16)
        feature_ref[2, :, at] = (grad_mixer * key_ref[:, at].astype(F32)).astype(BF16)

        window = jnp.concatenate([prev_ref[:, at], cur_ref[:, at]], axis=0)
        grad_wide = grad.astype(F32)
        for g in range(packed):
            own = jnp.where(member == g, grad_wide, 0.0).astype(BF16)
            pairs = lax.dot_general(own, window, (((1,), (1,)), ((), ())), preferred_element_type=F32)
            ring = jnp.where(above, pairs[:, 0:rows], pairs[:, rows : 2 * rows])
            total = ring[0:8]
            for tile in range(1, rows // 8):
                total = total + pltpu.roll(ring[8 * tile : 8 * tile + 8], rows - 8 * tile, 1)
            fold[g * 8 : (g + 1) * 8, :] = total
        total = fold[pl.ds(0, packed, stride=8), :]
        for step in range(1, 8):
            total = total + pltpu.roll(fold[pl.ds(step, packed, stride=8), :], rows - step, 1)
        long_ref[block * packed : (block + 1) * packed, :] = total


def unmix_call(lines, prev, cur, grad, grad_next, gate_grad, mixed, key, value):
    rows, channels = cur.shape
    groups, taps = lines.shape
    per_group = channels // groups
    width = block_width(channels, 512)
    steps = channels // width
    wide = pl.BlockSpec((rows, width), lambda i: (0, i))
    line = pl.BlockSpec((width // per_group, taps), lambda i: (i, 0))
    packed = LANES // per_group
    return pl.pallas_call(
        functools.partial(unmix_kernel, per_group),
        grid=(steps,),
        in_specs=[line] + [wide] * 8,
        out_specs=[pl.BlockSpec((3, rows, width), lambda i: (0, 0, i)), line],
        out_shape=[
            jax.ShapeDtypeStruct((3, rows, channels), BF16),
            jax.ShapeDtypeStruct((groups, taps), F32),
        ],
        scratch_shapes=[
            pltpu.VMEM((packed * rows, 2 * rows), BF16),
            pltpu.VMEM((packed * 8, LANES), F32),
        ],
        compiler_params=params(),
        cost_estimate=cost(4 * groups * rows * 2 * rows * LANES, 22 * rows * channels),
        name="unmix",
    )(lines, prev, cur, grad, grad_next, gate_grad, mixed, key, value)


def short_grad_kernel(short_taps, grads_ref, tokens_ref, rim_ref, out_ref):
    rows = tokens_ref.shape[0]
    ext = jnp.concatenate([rim_ref[...].astype(F32), tokens_ref[...].astype(F32)], axis=0)
    grads = grads_ref[0].astype(F32)
    for tap in range(short_taps):
        out_ref[tap : tap + 1, :] = jnp.sum(grads * ext[RIM - tap : RIM - tap + rows], axis=0, keepdims=True)


def short_grad_call(grads, tokens, rim, short_taps):
    _, rows, channels = grads.shape
    width = block_width(channels, 512)
    steps = channels // width
    return pl.pallas_call(
        functools.partial(short_grad_kernel, short_taps),
        grid=(3, steps),
        in_specs=[
            pl.BlockSpec((1, rows, width), lambda p, i: (p, 0, i)),
            pl.BlockSpec((rows, width), lambda p, i: (0, p * steps + i)),
            pl.BlockSpec((RIM, width), lambda p, i: (0, p * steps + i)),
        ],
        out_specs=pl.BlockSpec((short_taps, width), lambda p, i: (0, p * steps + i)),
        out_shape=jax.ShapeDtypeStruct((short_taps, 3 * channels), F32),
        compiler_params=params(),
        cost_estimate=cost(6 * short_taps * rows * channels, 12 * rows * channels),
        name="short_grad",
    )(grads, tokens, rim)


def short_adjoint_kernel(short_taps, grads_ref, rim_ref, filter_ref, out_ref):
    rows = out_ref.shape[0]
    ext = jnp.concatenate([grads_ref[0].astype(F32), rim_ref[0].astype(F32)], axis=0)
    total = filter_ref[0:1, :] * ext[0:rows]
    for tap in range(1, short_taps):
        total = total + filter_ref[tap : tap + 1, :] * ext[tap : tap + rows]
    out_ref[...] = total.astype(BF16)


def short_adjoint_call(grads, rim, filters):
    _, rows, channels = grads.shape
    short_taps = filters.shape[0]
    width = block_width(channels, 512)
    steps = channels // width
    return pl.pallas_call(
        functools.partial(short_adjoint_kernel, short_taps),
        grid=(3, steps),
        in_specs=[
            pl.BlockSpec((1, rows, width), lambda p, i: (p, 0, i)),
            pl.BlockSpec((1, RIM, width), lambda p, i: (p, 0, i)),
            pl.BlockSpec((short_taps, width), lambda p, i: (0, p * steps + i)),
        ],
        out_specs=pl.BlockSpec((rows, width), lambda p, i: (0, p * steps + i)),
        out_shape=jax.ShapeDtypeStruct((rows, 3 * channels), BF16),
        compiler_params=params(),
        cost_estimate=cost(6 * short_taps * rows * channels, 12 * rows * channels),
        name="short_adjoint",
    )(grads, rim, filters)


def mirrored(lines):
    return jnp.roll(lines[:, ::-1], 1, axis=1)


def shards(tokens_in, short_filter, long_filter, out_weight, cotangent):
    tokens = tokens_in[0]
    rows = tokens.shape[0]
    short_taps = short_filter.shape[0]
    upstream = cotangent[0]
    weights = lax.all_gather(out_weight, "dp", axis=0, tiled=True)
    rim = shifted(tokens[rows - RIM :], "seq", 1)
    lines = long_filter.astype(F32)
    query, key, value, mixer = features_call(tokens, rim, short_filter)
    mixer_prev = shifted(mixer, "seq", 1)
    mixed, gated = mix_call(mirrored(lines), mixer_prev, mixer, query)
    all_rows = lax.all_gather(gated, "seq", axis=0, tiled=True)
    gate_grad = lax.psum_scatter(
        lax.dot_general(
            upstream, weights, (((1,), (1,)), ((), ())), preferred_element_type=F32
        ).astype(BF16),
        "seq",
        scatter_dimension=0,
        tiled=True,
    )
    grad_mixed = (gate_grad.astype(F32) * query.astype(F32)).astype(BF16)
    grad_next = shifted(grad_mixed, "seq", -1)
    grad_features, long_local = unmix_call(
        lines, mixer_prev, mixer, grad_mixed, grad_next, gate_grad, mixed, key, value
    )
    feature_next = shifted(grad_features[:, :RIM], "seq", -1)
    short_local = short_grad_call(grad_features, tokens, rim, short_taps)
    grad_short, grad_long = lax.psum((short_local, long_local), ("dp", "seq"))
    grad_tokens = short_adjoint_call(grad_features, feature_next, short_filter)
    output = jnp.dot(all_rows, weights, preferred_element_type=F32)
    weight_grad = lax.dot_general(
        all_rows, upstream, (((0,), (0,)), ((), ())), preferred_element_type=F32
    )
    grad_weight = lax.psum_scatter(
        weight_grad.astype(BF16), "dp", scatter_dimension=0, tiled=True
    ).astype(F32)
    return (
        output.astype(BF16)[None],
        grad_tokens[None],
        grad_short,
        mirrored(grad_long),
        grad_weight,
    )


def solution(mesh):
    return jax.shard_map(
        shards,
        mesh=mesh,
        in_specs=(P("dp", "seq", None), P(), P(), P("dp", "seq"), P("dp", None, "seq")),
        out_specs=(P("dp", None, "seq"), P("dp", "seq", None), P(), P(), P("dp", "seq")),
        check_vma=False,
    )
```

time: 934 us -> 547 us (0.59)
  local copies, waits for them, and re-layouts: 418 us -> 11.9 us
  waiting for transfers between devices: 346 us -> 411 us
  Pallas kernels: 0 us -> 60.9 us
  other arithmetic: 65.1 us -> 5.14 us
  matrix products: 69.8 us -> 28.8 us
    gather x4 -> x0, local copies, waits for them, and re-layouts: 305 us -> none  [tap_table(): taken = jnp.take(filters, clipped, axis=1)]
    reshape x4 -> x0, local copies, waits for them, and re-layouts: 69.4 us -> none  [the longest x1 35 us: medium_grad(): flattened = products.reshape(group_count, tap_count * 2 * tap_count)]
    pallas_call x0 -> x5, Pallas kernels: none -> 60.9 us  [the longest x1 16.1 us: short_grad_call(): pl.pallas_call(functools.partial(short_grad_kernel, short_taps), grid=(3,...]
    all_gather x1, waiting for transfers between devices: 0.02 us -> 57.3 us  [shards(): all_rows = lax.all_gather(gated, 'seq', axis=0, tiled=True)]
    dot_general x4 -> x1, matrix products: 50.3 us -> 9.24 us  [shards(): output = jnp.dot(all_rows, weights, preferred_element_type=F32)]
    ppermute x4, waiting for transfers between devices: 2.15 us -> 38.2 us  [shifted(): return lax.ppermute(x, axis, pairs)]
    concatenate x3 -> x0, local copies, waits for them, and re-layouts: 26.3 us -> none  [the longest x1 22.5 us: medium_grad(): jnp.concatenate([flattened, jnp.zeros((group_count, tap_count), jnp.float...]
    reduce_sum x2 -> x0, other arithmetic: 23.9 us -> none  [the longest x1 15.4 us: short_grad(): jnp.sum(grads_wide * extended[start_row:start_row + row_count].astype(jnp...]
  transfers between devices with their start and end apart: 9 -> 9, of which waited for: 5 -> 9; matrix products, arithmetic and copies ran while one was open for 53% -> 5% of each run, Pallas kernels for 0% -> 11%
where the time goes in v1:
time: 547 us; the launch traced here: 545 us
  waiting for transfers between devices  411 us (75%)
  Pallas kernels  60.9 us (11%)
  matrix products  28.8 us (5%)
  starting transfers between devices  14.1 us (3%)
  between operations  13.9 us (3%)
  local copies, waits for them, and re-layouts  11.9 us (2%)
    psum x1, waiting for transfers between devices, shards(): grad_short, grad_long = lax.psum((short_local, long_local), ('dp', 'seq'))  116 us
    reduce_scatter x1, waiting for transfers between devices, shards(): lax.psum_scatter(lax.dot_general(upstream, weights, (((1,), (1,)), ((), (...  100 us
    all_gather x1, waiting for transfers between devices, shards(): all_rows = lax.all_gather(gated, 'seq', axis=0, tiled=True)  57.3 us
    all_gather x1, waiting for transfers between devices, shards(): weights = lax.all_gather(out_weight, 'dp', axis=0, tiled=True)  56.8 us
    reduce_scatter x1, waiting for transfers between devices, shards(): lax.psum_scatter(weight_grad.astype(BF16), 'dp', scatter_dimension=0, til...  41.2 us
    ppermute x4, waiting for transfers between devices, shifted(): return lax.ppermute(x, axis, pairs)  38.2 us
    pallas_call x1, Pallas kernels, short_grad_call(): pl.pallas_call(functools.partial(short_grad_kernel, short_taps), grid=(3,...  16.1 us
    pallas_call x1, Pallas kernels, unmix_call(): pl.pallas_call(functools.partial(unmix_kernel, per_group), grid=(steps,),...  14.3 us
  transfers between devices with their start and end apart: 9, of which 9 were waited for; matrix products, arithmetic and copies ran while one was open for 5% of the time, Pallas kernels for 11%

profile of v1, /device:TPU:1, one launch (start us, length us, event | category | flops | bytes accessed | tf_op | source)
XLA Modules:
  0.0 545.4 jit_solution(13554510545967180704)
XLA Ops:
  7.2 0.0 copy-start
  7.2 0.0 all-gather.5.cloned.1.call-start
  7.2 0.7 all-gather.5.cloned.1.call-update
  7.9 0.0 reduce-scatter.3.cloned.1.call-start
  8.0 56.8 %all-gather.5.cloned.1.call-done = bf16[4096,256]{1,0:T(8,128)(2,1)} async-done(((bf16[512,256]{1,0:T(8,128)(2,1)}), bf16[4096,256]{1,0:T(8,128)(2,1)}) %all-gather.5.cloned.1.call-update) | async-done | bytes 2097168 | tf_op jit(solution)/shard_map/all_gather | solution.py:276
  64.8 0.0 copy-done
  64.8 9.7 %convolution_convert_fusion = bf16[2048,4096]{1,0:T(8,128)(2,1)} fusion(bf16[4096,256]{1,0:T(8,128)(2,1)} %all-gather.5.cloned.1.call-done, bf16[1,2048,256]{2,1,0:T(8,128)(2,1)S(1)} %copy-done), kind=kOutput, calls=%fused_computation | convolution fusion | flops 4303355904 | bytes 19922944 | tf_op jit(solution)/shard_map/dot_general | solution.py:284
  74.5 0.0 copy-start.3
  74.5 0.0 reduce-scatter.3.cloned.1.call-update
  74.5 0.0 all-gather.3.cloned.1.call-start
  74.6 1.0 slice_bitcast_fusion
  75.6 4.0 collective-permute-start
  79.5 2.6 collective-permute-done.refs_3_.refs_4_.refs_5_.rim_ref
  82.1 0.0 copy-done.3
  82.1 0.0 copy-start.10
  82.1 9.9 %features.1 = (bf16[128,4096]{1,0:T(8,128)(2,1)S(1)}, bf16[128,4096]{1,0:T(8,128)(2,1)S(1)}, bf16[128,4096]{1,0:T(8,128)(2,1)S(1)}, bf16[128,4096]{1,0:T(8,128)(2,1)}) custom-call(bf16[128,12288]{1,0:T(8,128)(2,1)} %bitcast.16, bf16[128,12288]{1,0:T(8,128)(2,1)} %bitcast.17, bf16[128,12288]{1,0:T(8,128)(2,1)} %bitcast.18, ...), custom_call_target="tpu_custom_call" | custom-call | flops 22020096 | bytes 15728640 | tf_op jit(solution)/shard_map/features/pallas_call | solution.py:69
  92.1 0.0 copy-start.6
  92.1 1.0 copy-done.6
  93.0 0.0 copy-start.7
  93.0 1.0 copy-done.7
  94.0 4.4 collective-permute-start.1
  98.4 0.0 copy-done.10
  98.4 0.1 slice.41
  98.5 0.2 slice.33
  98.7 0.1 pad_maximum_fusion.lines_ref
  98.8 11.6 %collective-permute-done.1.prev_ref = bf16[128,4096]{1,0:T(8,128)(2,1)} collective-permute-done((bf16[128,4096]{1,0:T(8,128)(2,1)}, bf16[128,4096]{1,0:T(8,128)(2,1)}, u32[]{:S(2)}, u32[]{:S(2)}) %collective-permute-start.1) | collective-permute-done | bytes 1048608 | tf_op jit(solution)/shard_map/ppermute | solution.py:20
  110.4 9.0 %mix.1 = (bf16[128,4096]{1,0:T(8,128)(2,1)S(1)}, bf16[128,4096]{1,0:T(8,128)(2,1)S(1)}) custom-call(f32[256,128]{1,0:T(8,128)S(1)} %pad_maximum_fusion.lines_ref, bf16[128,4096]{1,0:T(8,128)(2,1)} %collective-permute-done.1.prev_ref, bf16[128,4096]{1,0:T(8,128)(2,1)} %get-tuple-element.13.cur_ref, bf16[128,4096]{1,0:T(8,128)(2,1)S(1)} %get-tuple-element.14.query_ref), custom_call_target="tpu_custom_call" | custom-call | flops 2147483648 | bytes 5242880 | tf_op jit(solution)/shard_map/mix/pallas_call | solution.py:128
  119.4 0.0 copy-start.5
  119.5 1.0 copy-done.5
  120.4 0.0 copy-start.8
  120.4 1.0 copy-done.8
  121.5 0.0 all-gather.3.cloned.1.call-update
  121.5 0.0 all-reduce.3.cloned.1.call-start
  121.5 100.1 %reduce-scatter.3.cloned.1.call-done.gate_grad_ref = bf16[128,4096]{1,0:T(8,128)(2,1)} async-done(((bf16[2048,4096]{1,0:T(8,128)(2,1)}), bf16[128,4096]{1,0:T(8,128)(2,1)}) %reduce-scatter.3.cloned.1.call-update) | async-done | bytes 1048592 | tf_op jit(solution)/shard_map/reduce_scatter | solution.py:283
  221.7 0.0 copy-start.4
  221.7 1.6 multiply_convert_fusion.grad_ref
  223.2 3.2 collective-permute-start.2
  226.4 18.9 %collective-permute-done.2.next_ref = bf16[128,4096]{1,0:T(8,128)(2,1)S(1)} collective-permute-done((bf16[128,4096]{1,0:T(8,128)(2,1)S(1)}, bf16[128,4096]{1,0:T(8,128)(2,1)S(1)}, u32[]{:S(2)}, u32[]{:S(2)}) %collective-permute-start.2) | collective-permute-done | bytes 1048608 | tf_op jit(solution)/shard_map/ppermute | solution.py:20
  245.3 0.0 copy-done.4
  245.3 14.3 %unmix.1 = (bf16[3,128,4096]{2,1,0:T(8,128)(2,1)}, f32[256,128]{1,0:T(8,128)}) custom-call(f32[256,128]{1,0:T(8,128)S(1)} %convert_element_type.24.lines_ref, bf16[128,4096]{1,0:T(8,128)(2,1)} %collective-permute-done.1.prev_ref, bf16[128,4096]{1,0:T(8,128)(2,1)} %get-tuple-element.13.cur_ref, bf16[128,4096]{1,0:T(8,128)(2,1)S(1)} %multiply_convert_fusion.grad_ref, ...), custom_call_target="tpu_custom_call" | custom-call | flops 4294967296 | bytes 11534336 | tf_op jit(solution)/shard_map/unmix/pallas_call | solution.py:190
  259.6 0.0 copy-start.1
  259.6 1.9 copy-done.1
  261.5 16.1 %short_grad.1 = f32[7,12288]{1,0:T(8,128)} custom-call(bf16[3,128,4096]{2,1,0:T(8,128)(2,1)S(1)} %copy-done.1, bf16[128,12288]{1,0:T(8,128)(2,1)} %bitcast.19, bf16[8,12288]{1,0:T(8,128)(2,1)S(1)} %collective-permute-done.refs_3_.refs_4_.refs_5_.rim_ref), custom_call_target="tpu_custom_call" | custom-call | flops 22020096 | bytes 6291456 | tf_op jit(solution)/shard_map/short_grad/pallas_call | solution.py:221
  277.5 0.0 all-reduce.3.cloned.1.call-update
  277.6 0.0 reduce-scatter.5.cloned.1.call-start
  277.6 57.3 %all-gather.3.cloned.1.call-done = bf16[2048,4096]{1,0:T(8,128)(2,1)} async-done(((bf16[128,4096]{1,0:T(8,128)(2,1)}), bf16[2048,4096]{1,0:T(8,128)(2,1)}) %all-gather.3.cloned.1.call-update) | async-done | bytes 16777232 | tf_op jit(solution)/shard_map/all_gather | solution.py:282
  334.9 9.8 %convolution_convert_fusion.1 = bf16[4096,256]{1,0:T(8,128)(2,1)} fusion(bf16[2048,4096]{1,0:T(8,128)(2,1)} %all-gather.3.cloned.1.call-done, bf16[1,2048,256]{2,1,0:T(8,128)(2,1)S(1)} %copy-done), kind=kOutput, calls=%fused_computation.1 | convolution fusion | flops 4296015872 | bytes 19922944 | tf_op jit(solution)/shard_map/dot_general | solution.py:301
  344.7 0.0 reduce-scatter.5.cloned.1.call-update
  344.7 0.9 slice.36
  345.6 2.3 collective-permute-start.3
  348.0 5.1 collective-permute-done.3.rim_ref
  353.1 0.0 copy-start.2
  353.1 1.9 copy-done.2
  355.0 11.7 %short_adjoint.1 = bf16[128,12288]{1,0:T(8,128)(2,1)} custom-call(bf16[3,128,4096]{2,1,0:T(8,128)(2,1)S(1)} %copy-done.2, bf16[3,8,4096]{2,1,0:T(8,128)(2,1)S(1)} %collective-permute-done.3.rim_ref, f32[7,12288]{1,0:T(8,128)S(1)} %copy-done.3), custom_call_target="tpu_custom_call" | custom-call | flops 22020096 | bytes 6291456 | tf_op jit(solution)/shard_map/short_adjoint/pallas_call | solution.py:251
  366.7 116.3 %all-reduce.3.cloned.1.call-done = (f32[7,12288]{1,0:T(8,128)}, f32[256,128]{1,0:T(8,128)}) async-done(((f32[7,12288]{1,0:T(8,128)}, f32[256,128]{1,0:T(8,128)}), (f32[7,12288]{1,0:T(8,128)}, f32[256,128]{1,0:T(8,128)})) %all-reduce.3.cloned.1.call-update) | async-done | bytes 475152 | tf_op jit(solution)/shard_map/psum | solution.py:298
  483.0 1.0 slice.43
  484.0 0.2 slice.39
  484.2 1.7 pad_maximum_fusion.1
  485.9 0.0 copy-done.9
  485.9 9.2 %fusion = bf16[1,2048,256]{2,1,0:T(8,128)(2,1)} fusion(bf16[2048,4096]{1,0:T(8,128)(2,1)} %all-gather.3.cloned.1.call-done, bf16[4096,256]{1,0:T(8,128)(2,1)S(1)} %copy-done.9), kind=kOutput, calls=%fused_computation.3 | convolution fusion | flops 4295491584 | bytes 19922944 | tf_op jit(solution)/shard_map/dot_general | solution.py:300
  495.1 41.2 %reduce-scatter.5.cloned.1.call-done = bf16[512,256]{1,0:T(8,128)(2,1)} async-done(((bf16[4096,256]{1,0:T(8,128)(2,1)}), bf16[512,256]{1,0:T(8,128)(2,1)}) %reduce-scatter.5.cloned.1.call-update) | async-done | bytes 262160 | tf_op jit(solution)/shard_map/reduce_scatter | solution.py:304
  536.3 1.8 convert_element_type.31
  538.1 0.0 copy-done.11
  538.1 0.7 copy.12
  (4 shorter events, 0.0 us)
Async XLA Ops:
  7.2 57.6 %copy-start = (bf16[1,2048,256]{2,1,0:T(8,128)(2,1)S(1)}, bf16[1,2048,256]{2,1,0:T(8,128)(2,1)}, u32[]{:S(2)}) copy-start(bf16[1,2048,256]{2,1,0:T(8,128)(2,1)} %param.9) | copy-start | bytes 3145732
  7.2 57.6 %all-gather.5.cloned.1.call-start = ((), (), s32[]{:S(2)}) async-start(), calls=%async_computation.3 | async-start | bytes 2359296 | tf_op jit(solution)/shard_map/all_gather | solution.py:276
  7.9 213.7 %reduce-scatter.3.cloned.1.call-start = ((), (), s32[]{:S(2)}) async-start(), calls=%async_computation.4 | async-start | bytes 17825792 | tf_op jit(solution)/shard_map/reduce_scatter | solution.py:283
  74.5 7.6 %copy-start.3 = (f32[7,12288]{1,0:T(8,128)S(1)}, f32[7,12288]{1,0:T(8,128)}, u32[]{:S(2)}) copy-start(f32[7,12288]{1,0:T(8,128)} %filter_ref.1) | copy-start | bytes 1032196
  74.5 260.3 %all-gather.3.cloned.1.call-start = ((), (), s32[]{:S(2)}) async-start(), calls=%async_computation.2 | async-start | bytes 17825792 | tf_op jit(solution)/shard_map/all_gather | solution.py:282
  75.6 6.6 %collective-permute-start = (bf16[8,12288]{1,0:T(8,128)(2,1)S(1)}, bf16[8,12288]{1,0:T(8,128)(2,1)S(1)}, u32[]{:S(2)}, u32[]{:S(2)}) collective-permute-start(bf16[8,12288]{1,0:T(8,128)(2,1)S(1)} %slice_bitcast_fusion), channel_id=1, source_target_pairs={{0,1},{1,2},{2,3},{3,4},{4,5},{5,6},{6,7},{7,8},{8,9},{9,10},{10,1... | collective-permute-start | bytes 589832 | tf_op jit(solution)/shard_map/ppermute | solution.py:20
  82.1 16.3 %copy-start.10 = (bf16[256,128]{1,0:T(8,128)(2,1)S(1)}, bf16[256,128]{1,0:T(8,128)(2,1)}, u32[]{:S(2)}) copy-start(bf16[256,128]{1,0:T(8,128)(2,1)} %param.7) | copy-start | bytes 196612
  92.1 1.0 copy-start.6
  93.0 1.0 copy-start.7
  94.0 16.4 %collective-permute-start.1 = (bf16[128,4096]{1,0:T(8,128)(2,1)}, bf16[128,4096]{1,0:T(8,128)(2,1)}, u32[]{:S(2)}, u32[]{:S(2)}) collective-permute-start(bf16[128,4096]{1,0:T(8,128)(2,1)} %get-tuple-element.13.cur_ref), channel_id=1, source_target_pairs={{0,1},{1,2},{2,3},{3,4},{4,5},{5,6},{6,7},{7,8},{8,9},{9,10},{10,1... | collective-permute-start | bytes 3145736 | tf_op jit(solution)/shard_map/ppermute | solution.py:20
  119.4 1.0 copy-start.5
  120.4 1.0 copy-start.8
  121.5 361.5 %all-reduce.3.cloned.1.call-start = ((), (), s32[]{:S(2)}) async-start(), calls=%async_computation.6 | async-start | bytes 1048576 | tf_op jit(solution)/shard_map/psum | solution.py:298
  221.7 23.6 %copy-start.4 = (bf16[128,4096]{1,0:T(8,128)(2,1)S(1)}, bf16[128,4096]{1,0:T(8,128)(2,1)}, u32[]{:S(2)}) copy-start(bf16[128,4096]{1,0:T(8,128)(2,1)} %reduce-scatter.3.cloned.1.call-done.gate_grad_ref) | copy-start | bytes 3145732
  223.2 22.1 %collective-permute-start.2 = (bf16[128,4096]{1,0:T(8,128)(2,1)S(1)}, bf16[128,4096]{1,0:T(8,128)(2,1)S(1)}, u32[]{:S(2)}, u32[]{:S(2)}) collective-permute-start(bf16[128,4096]{1,0:T(8,128)(2,1)S(1)} %multiply_convert_fusion.grad_ref), channel_id=1, source_target_pairs={{1,0},{2,1},{3,2},{4,3},{5,4},{6,5},{7,6},{8,7},{9,8},{10,9},{11,1... | collective-permute-start | bytes 3145736 | tf_op jit(solution)/shard_map/ppermute | solution.py:20
  259.6 1.9 copy-start.1
  277.6 258.8 %reduce-scatter.5.cloned.1.call-start = ((), (), s32[]{:S(2)}) async-start(), calls=%async_computation.5 | async-start | bytes 2359296 | tf_op jit(solution)/shard_map/reduce_scatter | solution.py:304
  345.6 7.5 %collective-permute-start.3 = (bf16[3,8,4096]{2,1,0:T(8,128)(2,1)S(1)}, bf16[3,8,4096]{2,1,0:T(8,128)(2,1)S(1)}, u32[]{:S(2)}, u32[]{:S(2)}) collective-permute-start(bf16[3,8,4096]{2,1,0:T(8,128)(2,1)S(1)} %slice.36), channel_id=1, source_target_pairs={{1,0},{2,1},{3,2},{4,3},{5,4},{6,5},{7,6},{8,7},{9,8},{10,9},{11,1... | collective-permute-start | bytes 589832 | tf_op jit(solution)/shard_map/ppermute | solution.py:20
  353.1 1.9 copy-start.2
  355.0 130.8 %copy-start.9 = (bf16[4096,256]{1,0:T(8,128)(2,1)S(1)}, bf16[4096,256]{1,0:T(8,128)(2,1)}, u32[]{:S(2)}) copy-start(bf16[4096,256]{1,0:T(8,128)(2,1)} %all-gather.5.cloned.1.call-done) | copy-start | bytes 6291460
  485.9 52.3 %copy-start.11 = (f32[7,12288]{1,0:T(8,128)S(1)}, f32[7,12288]{1,0:T(8,128)}, u32[]{:S(2)}) copy-start(f32[7,12288]{1,0:T(8,128)} %get-tuple-element.25) | copy-start | bytes 1032196
Sparse Core Ops, SparseCore 0:
  9.7 55.0 all-gather.4
  74.7 146.9 reduce-scatter.2
  224.1 110.6 all-gather.2
  340.2 142.6 all-reduce.2
  485.4 50.9 reduce-scatter.4

commit v2 on v1

v2 whole, which is shorter than its diff:
```python
import functools
import itertools
import math

import jax
import jax.numpy as jnp
from jax import lax
from jax.experimental import pallas as pl
from jax.experimental.pallas import tpu as pltpu
from jax.sharding import PartitionSpec as P

LANES = 128
RIM = 8
VMEM = 48 * 1024 * 1024
F32 = jnp.float32
BF16 = jnp.bfloat16


PLANE = ("y", "xl", "xh")
LINE = ("xh", "z", "c")


def along(x, by):
    size = math.prod(lax.axis_size(a) for a in LINE)
    pairs = [(i, i + by) for i in range(size) if 0 <= i + by < size]
    return lax.ppermute(x, LINE, pairs)


def move(x, **steps):
    axes = tuple(a for a in ("y", "xl", "xh", "z", "c") if steps.get(a, 0) % lax.axis_size(a))
    if not axes:
        return x
    sizes = [lax.axis_size(a) for a in axes]
    pairs = []
    for at in itertools.product(*(range(n) for n in sizes)):
        to = [(p + steps[a]) % n for p, a, n in zip(at, axes, sizes)]
        pairs.append((flat(at, sizes), flat(to, sizes)))
    return lax.ppermute(x, axes, pairs)


def flat(at, sizes):
    index = 0
    for p, n in zip(at, sizes):
        index = index * n + p
    return index


FLIPS = [(0, 0), (0, 1), (1, 0), (1, 1)]


def params():
    return pltpu.CompilerParams(vmem_limit_bytes=VMEM)


def cost(flops, moved):
    return pl.CostEstimate(flops=int(flops), bytes_accessed=int(moved), transcendentals=0)


def block_width(channels, most):
    width = min(channels, most)
    while channels % width:
        width //= 2
    return width


def features_kernel(short_taps, tokens, rims, filters, query_ref, key_ref, value_ref, mixer_ref):
    rows = tokens[0].shape[0]

    def filtered(part):
        ext = jnp.concatenate([rims[part][...].astype(F32), tokens[part][...].astype(F32)], axis=0)
        total = filters[part][0:1, :] * ext[RIM : RIM + rows]
        for tap in range(1, short_taps):
            total = total + filters[part][tap : tap + 1, :] * ext[RIM - tap : RIM - tap + rows]
        return total

    query_ref[...] = filtered(0).astype(BF16)
    key, value = filtered(1), filtered(2)
    key_ref[...] = key.astype(BF16)
    value_ref[...] = value.astype(BF16)
    mixer_ref[...] = (key * value).astype(BF16)


def features_call(tokens, rim, filters):
    rows, wide = tokens.shape
    channels = wide // 3
    taps = filters.shape[0]
    width = block_width(channels, 512)
    steps = channels // width

    def spec(height, part):
        return pl.BlockSpec((height, width), lambda i, part=part: (0, i + part * steps))

    def body(*refs):
        features_kernel(taps, refs[0:3], refs[3:6], refs[6:9], *refs[9:])

    out = jax.ShapeDtypeStruct((rows, channels), BF16)
    return pl.pallas_call(
        body,
        grid=(steps,),
        in_specs=[spec(rows, p) for p in range(3)]
        + [spec(RIM, p) for p in range(3)]
        + [spec(taps, p) for p in range(3)],
        out_specs=[pl.BlockSpec((rows, width), lambda i: (0, i))] * 4,
        out_shape=[out] * 4,
        compiler_params=params(),
        cost_estimate=cost(2 * taps * rows * wide, 10 * rows * wide),
        name="features",
    )(tokens, tokens, tokens, rim, rim, rim, filters, filters, filters)


def lane_row(shape):
    row = lax.broadcasted_iota(jnp.int32, shape, 0)
    lane = lax.broadcasted_iota(jnp.int32, shape, 1)
    return row, lane


def circulant(line, taps):
    wide = jnp.broadcast_to(line.astype(F32), (taps, taps))
    return pltpu.roll(wide, 0, 1, stride=1, stride_axis=0)


def pick_groups(product, rows, per_group):
    lane = lax.broadcasted_iota(jnp.int32, (rows, LANES), 1) // per_group
    total = product[0:rows]
    for g in range(1, LANES // per_group):
        total = jnp.where(lane == g, product[g * rows : (g + 1) * rows], total)
    return total


def mix_kernel(per_group, place, lines_ref, prev_ref, cur_ref, query_ref, mixed_ref, gated_ref, table):
    rows, width = cur_ref.shape
    row, lane = lane_row((rows, rows))
    above = lane > row
    packed = LANES // per_group
    for block in range(width // LANES):
        at = pl.ds(block * LANES, LANES)
        for g in range(packed):
            ring = circulant(lines_ref[block * packed + g : block * packed + g + 1, :], rows)
            table[g * rows : (g + 1) * rows, 0:rows] = jnp.where(above, ring, 0.0).astype(BF16)
            table[g * rows : (g + 1) * rows, rows : 2 * rows] = jnp.where(above, 0.0, ring).astype(BF16)
        window = jnp.concatenate([prev_ref[:, at], cur_ref[:, at]], axis=0)
        product = jnp.dot(table[...], window, preferred_element_type=F32)
        mixed = pick_groups(product, rows, per_group)
        mixed_ref[:, at] = mixed.astype(BF16)
        gated_ref[:, at] = (query_ref[:, at].astype(F32) * mixed).astype(BF16)


def mix_call(place, lines, prev, cur, query):
    rows, channels = cur.shape
    groups, taps = lines.shape
    per_group = channels // groups
    steps = place.shape[0]
    width = channels // steps
    wide = pl.BlockSpec((rows, width), lambda i, place: (0, i))
    out = jax.ShapeDtypeStruct((rows, channels), BF16)
    return pl.pallas_call(
        functools.partial(mix_kernel, per_group),
        grid_spec=pltpu.PrefetchScalarGridSpec(
            num_scalar_prefetch=1,
            grid=(steps,),
            in_specs=[pl.BlockSpec((width // per_group, taps), lambda i, place: (i, 0)), wide, wide, wide],
            out_specs=[wide, pl.BlockSpec((rows, width), lambda i, place: (0, place[i]))],
            scratch_shapes=[pltpu.VMEM((LANES // per_group * rows, 2 * rows), BF16)],
        ),
        out_shape=[out, out],
        compiler_params=params(),
        cost_estimate=cost(2 * groups * rows * 2 * rows * LANES, 10 * rows * channels),
        name="mix",
    )(place, lines, prev, cur, query)


def gate_kernel(place, gate_grad_ref, query_ref, mixed_ref, grad_ref, feature_ref):
    gate_grad = gate_grad_ref[...].astype(F32)
    grad_ref[...] = (gate_grad * query_ref[...].astype(F32)).astype(BF16)
    feature_ref[...] = (gate_grad * mixed_ref[...].astype(F32)).astype(BF16)


def gate_call(place, gate_grad, query, mixed):
    rows, channels = query.shape
    steps = place.shape[0]
    width = channels // steps
    wide = pl.BlockSpec((rows, width), lambda i, place: (0, i))
    out = jax.ShapeDtypeStruct((rows, channels), BF16)
    return pl.pallas_call(
        gate_kernel,
        grid_spec=pltpu.PrefetchScalarGridSpec(
            num_scalar_prefetch=1,
            grid=(steps,),
            in_specs=[pl.BlockSpec((rows, width), lambda i, place: (0, place[i])), wide, wide],
            out_specs=[wide, wide],
        ),
        out_shape=[out, out],
        compiler_params=params(),
        cost_estimate=cost(2 * rows * channels, 10 * rows * channels),
        name="gate_back",
    )(place, gate_grad, query, mixed)


def tap_sums(short_taps, grads, tokens_ref, rim_ref, out_ref):
    rows = tokens_ref.shape[0]
    ext = jnp.concatenate([rim_ref[...].astype(F32), tokens_ref[...].astype(F32)], axis=0)
    for tap in range(short_taps):
        out_ref[tap : tap + 1, :] = jnp.sum(grads * ext[RIM - tap : RIM - tap + rows], axis=0, keepdims=True)
    out_ref[short_taps:8, :] = jnp.zeros((8 - short_taps, out_ref.shape[1]), F32)


def long_grad_kernel(
    per_group, short_taps, prev_ref, cur_ref, grad_ref, feature_ref, tokens_ref, rim_ref, long_ref, short_ref, fold
):
    rows, width = cur_ref.shape
    row, lane = lane_row((rows, rows))
    above = lane > row
    member = lax.broadcasted_iota(jnp.int32, (rows, LANES), 1) // per_group
    packed = LANES // per_group
    for block in range(width // LANES):
        at = pl.ds(block * LANES, LANES)
        window = jnp.concatenate([prev_ref[:, at], cur_ref[:, at]], axis=0)
        grad_wide = grad_ref[:, at].astype(F32)
        for g in range(packed):
            own = jnp.where(member == g, grad_wide, 0.0).astype(BF16)
            pairs = lax.dot_general(own, window, (((1,), (1,)), ((), ())), preferred_element_type=F32)
            ring = jnp.where(above, pairs[:, 0:rows], pairs[:, rows : 2 * rows])
            total = ring[0:8]
            for tile in range(1, rows // 8):
                total = total + pltpu.roll(ring[8 * tile : 8 * tile + 8], rows - 8 * tile, 1)
            fold[g * 8 : (g + 1) * 8, :] = total
        total = fold[pl.ds(0, packed, stride=8), :]
        for step in range(1, 8):
            total = total + pltpu.roll(fold[pl.ds(step, packed, stride=8), :], rows - step, 1)
        long_ref[block * packed : (block + 1) * packed, :] = total
    tap_sums(short_taps, feature_ref[...].astype(F32), tokens_ref, rim_ref, short_ref)


def long_grad_call(groups, short_taps, prev, cur, grad, feature, tokens, rim):
    rows, channels = cur.shape
    per_group = channels // groups
    width = block_width(channels, 512)
    steps = channels // width
    wide = pl.BlockSpec((rows, width), lambda i: (0, i))
    packed = LANES // per_group
    return pl.pallas_call(
        functools.partial(long_grad_kernel, per_group, short_taps),
        grid=(steps,),
        in_specs=[wide] * 5 + [pl.BlockSpec((RIM, width), lambda i: (0, i))],
        out_specs=[
            pl.BlockSpec((width // per_group, rows), lambda i: (i, 0)),
            pl.BlockSpec((8, width), lambda i: (0, i)),
        ],
        out_shape=[
            jax.ShapeDtypeStruct((groups, rows), F32),
            jax.ShapeDtypeStruct((8, channels), F32),
        ],
        scratch_shapes=[pltpu.VMEM((packed * 8, LANES), F32)],
        compiler_params=params(),
        cost_estimate=cost(2 * groups * rows * 2 * rows * LANES, 10 * rows * channels),
        name="long_grad",
    )(prev, cur, grad, feature, tokens, rim)


def unmix_kernel(
    per_group, short_taps, lines_ref, grad_ref, next_ref, key_ref, value_ref, key_tokens_ref, value_tokens_ref,
    key_rim_ref, value_rim_ref, feature_ref, key_sum_ref, value_sum_ref, table,
):
    rows, width = grad_ref.shape
    row, lane = lane_row((rows, rows))
    below = lane < row
    packed = LANES // per_group
    for block in range(width // LANES):
        at = pl.ds(block * LANES, LANES)
        for g in range(packed):
            ring = circulant(lines_ref[block * packed + g : block * packed + g + 1, :], rows)
            table[g * rows : (g + 1) * rows, 0:rows] = jnp.where(below, 0.0, ring).astype(BF16)
            table[g * rows : (g + 1) * rows, rows : 2 * rows] = jnp.where(below, ring, 0.0).astype(BF16)
        window = jnp.concatenate([grad_ref[:, at], next_ref[:, at]], axis=0)
        product = jnp.dot(table[...], window, preferred_element_type=F32)
        grad_mixer = pick_groups(product, rows, per_group)
        feature_ref[0, :, at] = (grad_mixer * value_ref[:, at].astype(F32)).astype(BF16)
        feature_ref[1, :, at] = (grad_mixer * key_ref[:, at].astype(F32)).astype(BF16)
    tap_sums(short_taps, feature_ref[0].astype(F32), key_tokens_ref, key_rim_ref, key_sum_ref)
    tap_sums(short_taps, feature_ref[1].astype(F32), value_tokens_ref, value_rim_ref, value_sum_ref)


def unmix_call(lines, short_taps, grad, grad_next, key, value, tokens, rim):
    rows, channels = grad.shape
    groups, taps = lines.shape
    per_group = channels // groups
    width = block_width(channels, 512)
    steps = channels // width

    def spec(height, part):
        return pl.BlockSpec((height, width), lambda i, part=part: (0, i + part * steps))

    wide = spec(rows, 0)
    packed = LANES // per_group
    sums = jax.ShapeDtypeStruct((8, channels), F32)
    return pl.pallas_call(
        functools.partial(unmix_kernel, per_group, short_taps),
        grid=(steps,),
        in_specs=[pl.BlockSpec((width // per_group, taps), lambda i: (i, 0))]
        + [wide] * 4
        + [spec(rows, 1), spec(rows, 2), spec(RIM, 1), spec(RIM, 2)],
        out_specs=[pl.BlockSpec((2, rows, width), lambda i: (0, 0, i)), spec(8, 0), spec(8, 0)],
        out_shape=[jax.ShapeDtypeStruct((2, rows, channels), BF16), sums, sums],
        scratch_shapes=[pltpu.VMEM((packed * rows, 2 * rows), BF16)],
        compiler_params=params(),
        cost_estimate=cost(2 * groups * rows * 2 * rows * LANES, 16 * rows * channels),
        name="unmix",
    )(lines, grad, grad_next, key, value, tokens, tokens, rim, rim)


def short_adjoint_kernel(short_taps, query_ref, other_ref, query_rim_ref, other_rim_ref, filter_ref, out_ref):
    rows = out_ref.shape[0]

    def filtered(grads, rim):
        ext = jnp.concatenate([grads.astype(F32), rim.astype(F32)], axis=0)
        total = filter_ref[0:1, :] * ext[0:rows]
        for tap in range(1, short_taps):
            total = total + filter_ref[tap : tap + 1, :] * ext[tap : tap + rows]
        out_ref[...] = total.astype(BF16)

    @pl.when(pl.program_id(0) == 0)
    def _():
        filtered(query_ref[...], query_rim_ref[...])

    @pl.when(pl.program_id(0) > 0)
    def _():
        filtered(other_ref[0], other_rim_ref[0])


def short_adjoint_call(query, other, query_rim, other_rim, filters):
    rows, channels = query.shape
    short_taps = filters.shape[0]
    width = block_width(channels, 1024)
    steps = channels // width

    def first(p, i):
        return jnp.where(p == 0, i, steps - 1)

    def rest(p, i):
        return jnp.where(p == 0, 0, i)

    return pl.pallas_call(
        functools.partial(short_adjoint_kernel, short_taps),
        grid=(3, steps),
        in_specs=[
            pl.BlockSpec((rows, width), lambda p, i: (0, first(p, i))),
            pl.BlockSpec((1, rows, width), lambda p, i: (jnp.maximum(p - 1, 0), 0, rest(p, i))),
            pl.BlockSpec((RIM, width), lambda p, i: (0, first(p, i))),
            pl.BlockSpec((1, RIM, width), lambda p, i: (jnp.maximum(p - 1, 0), 0, rest(p, i))),
            pl.BlockSpec((short_taps, width), lambda p, i: (0, p * steps + i)),
        ],
        out_specs=pl.BlockSpec((rows, width), lambda p, i: (0, p * steps + i)),
        out_shape=jax.ShapeDtypeStruct((rows, 3 * channels), BF16),
        compiler_params=params(),
        cost_estimate=cost(6 * short_taps * rows * channels, 12 * rows * channels),
        name="short_adjoint",
    )(query, other, query_rim, other_rim, filters)


def spread_kernel(place, query_ref, key_ref, value_ref, long_ref, out_ref):
    steps = query_ref.shape[1] // LANES
    for part, ref in enumerate((query_ref, key_ref, value_ref)):
        for i in range(steps):
            out_ref[place[part * steps + i]] = ref[:, i * LANES : (i + 1) * LANES]
    for i in range(long_ref.shape[0] // 8):
        out_ref[place[3 * steps + i]] = long_ref[8 * i : 8 * i + 8, :]


def collect_kernel(place, tiles_ref, short_ref, long_ref):
    short_taps, wide = short_ref.shape
    steps = wide // LANES
    for i in range(steps):
        short_ref[:, i * LANES : (i + 1) * LANES] = tiles_ref[place[i]][0:short_taps, :]
    for i in range(long_ref.shape[0] // 8):
        long_ref[8 * i : 8 * i + 8, :] = tiles_ref[place[steps + i]]


def in_vmem():
    return pl.BlockSpec(memory_space=pltpu.VMEM)


def total_over_devices(places, query_sum, key_sum, value_sum, long_sum, short_taps):
    ny, nz = lax.axis_size("y"), lax.axis_size("z")
    channels = query_sum.shape[1]
    count = 3 * channels // LANES + long_sum.shape[0] // 8
    tiles = pl.pallas_call(
        spread_kernel,
        in_specs=[pl.BlockSpec(memory_space=pltpu.SMEM)] + [in_vmem()] * 4,
        out_specs=in_vmem(),
        out_shape=jax.ShapeDtypeStruct((count, 8, LANES), F32),
        compiler_params=params(),
        name="spread",
    )(places, query_sum, key_sum, value_sum, long_sum)
    half = count // 2
    part = tiles[:half] + move(tiles[half:], c=1)
    size = half // nz
    part = sum([move(part[d * size : (d + 1) * size], z=d) for d in range(1, nz)], part[:size])
    whole = paired_sum([part] + [move(part, y=d) for d in range(1, ny)])
    whole = paired_sum([move(whole, xl=a, xh=b) for a, b in FLIPS])
    line = jnp.concatenate([move(whole, z=-d) for d in range(nz)], axis=0)
    tiles = jnp.concatenate([line, move(line, c=1)], axis=0)
    groups, taps = long_sum.shape
    return pl.pallas_call(
        collect_kernel,
        in_specs=[pl.BlockSpec(memory_space=pltpu.SMEM), in_vmem()],
        out_specs=[in_vmem(), in_vmem()],
        out_shape=[
            jax.ShapeDtypeStruct((short_taps, 3 * channels), F32),
            jax.ShapeDtypeStruct((groups, taps), F32),
        ],
        compiler_params=params(),
        name="collect",
    )(places, tiles)


def paired_sum(terms):
    half = len(terms) // 2
    if half == 0:
        return terms[0]
    return paired_sum([terms[i] + terms[i + half] for i in range(half)])


def gather_near(shard):
    ny = lax.axis_size("y")
    half = shard.shape[0] // 2
    top, bottom = shard[:half], shard[half:]
    return (
        jnp.stack([move(top, xl=a, xh=b) for a, b in FLIPS]),
        jnp.stack([move(bottom, y=d) for d in range(ny)]),
    )


def gather_far(wide_top, tall_bottom):
    ny = lax.axis_size("y")
    return (
        [move(wide_top, y=d) for d in range(ny)],
        [move(tall_bottom, xl=a, xh=b) for a, b in FLIPS],
    )


def piece_rows(tops, bottoms, step):
    rows = []
    for a in range(2):
        rows.append(jnp.concatenate([tops[step][2 * a + b] for b in range(2)], axis=1))
        rows.append(jnp.concatenate([bottoms[2 * a + b][step] for b in range(2)], axis=1))
    return rows


def gate_matmul_kernel(ny, *refs):
    cotangent_ref, tops, bottoms, out_ref = refs[0], refs[1 : 1 + ny], refs[1 + ny : 5 + ny], refs[5 + ny]
    left = cotangent_ref[...]
    at = 0
    for step in range(ny):
        for right in piece_rows(tops, bottoms, step):
            size = right.shape[0]
            out_ref[:, at : at + size] = lax.dot_general(
                left, right, (((1,), (1,)), ((), ())), preferred_element_type=F32
            ).astype(BF16)
            at += size


def whole(x):
    return pl.BlockSpec(x.shape, lambda *_, n=x.ndim: (0,) * n)


def gate_matmul(cotangents, tops, bottoms):
    rows, depth = cotangents.shape
    ny = len(tops)
    channels = 4 * ny * tops[0].shape[1]
    height = rows // 2
    return pl.pallas_call(
        functools.partial(gate_matmul_kernel, ny),
        grid=(rows // height,),
        in_specs=[pl.BlockSpec((height, depth), lambda i: (i, 0))] + [whole(x) for x in (*tops, *bottoms)],
        out_specs=pl.BlockSpec((height, channels), lambda i: (i, 0)),
        out_shape=jax.ShapeDtypeStruct((rows, channels), BF16),
        compiler_params=params(),
        cost_estimate=cost(2 * rows * depth * channels, 2 * (rows + depth) * channels),
        name="gate_matmul",
    )(cotangents, *tops, *bottoms)


def project_kernel(ny, *refs):
    rows_ref, turned_ref, tops, bottoms = refs[0], refs[1], refs[2 : 2 + ny], refs[2 + ny : 6 + ny]
    own_ref, other_ref = refs[6 + ny : 8 + ny]
    top_grads, bottom_grads = refs[8 + ny : 8 + 2 * ny], refs[8 + 2 * ny : 12 + 2 * ny]
    total = refs[12 + 2 * ny]
    step = pl.program_id(0)
    width = own_ref.shape[1]
    size = tops[0].shape[1]
    grads = jnp.dot(turned_ref[...], rows_ref[...], preferred_element_type=F32).astype(BF16)
    for a in range(2):
        for b in range(2):
            at = (2 * a + 1) * size
            bottom_grads[2 * a + b][step] = grads[b * width : (b + 1) * width, at : at + size]
    for d in range(ny):

        @pl.when(step == d)
        def _(d=d):
            for a in range(2):
                for b in range(2):
                    at = 2 * a * size
                    top_grads[d][2 * a + b] = grads[b * width : (b + 1) * width, at : at + size]
            right = jnp.concatenate(piece_rows(tops, bottoms, d), axis=0)
            product = jnp.dot(rows_ref[...], right, preferred_element_type=F32)
            if d == 0:
                total[...] = product
            else:
                total[...] += product

    @pl.when(step == ny - 1)
    def _():
        own_ref[...] = total[:, :width].astype(BF16)
        other_ref[...] = total[:, width:].astype(BF16)


def project(all_rows, turned, tops, bottoms):
    rows, channels = all_rows.shape
    ny = len(tops)
    size = tops[0].shape[1]
    width = turned.shape[0] // 2
    half = jax.ShapeDtypeStruct((rows, width), BF16)
    outs = (
        [half, half]
        + [jax.ShapeDtypeStruct((4, width, size), BF16)] * ny
        + [jax.ShapeDtypeStruct((ny, width, size), BF16)] * 4
    )
    results = pl.pallas_call(
        functools.partial(project_kernel, ny),
        grid=(ny,),
        in_specs=[pl.BlockSpec((rows, channels // ny), lambda i: (0, i)), whole(turned)]
        + [whole(x) for x in (*tops, *bottoms)],
        out_specs=[whole(x) for x in outs],
        out_shape=outs,
        scratch_shapes=[pltpu.VMEM((rows, 2 * width), F32)],
        compiler_params=params(),
        cost_estimate=cost(8 * rows * width * channels, 2 * (rows + 4 * width) * channels),
        name="project",
    )(all_rows, turned, *tops, *bottoms)
    return results[0], results[1], results[2 : 2 + ny], results[2 + ny :]


def plane_scatter_sum(top_grads, bottom_grads):
    ny = len(top_grads)

    def added(terms):
        total = terms[0].astype(F32)
        for term in terms[1:]:
            total = total + term.astype(F32)
        return total

    top = added([move(top_grads[d], y=-d) for d in range(ny)]).astype(BF16)
    bottom = added([move(bottom_grads[f], xl=a, xh=b) for f, (a, b) in enumerate(FLIPS)]).astype(BF16)
    top = added([move(top[f], xl=a, xh=b) for f, (a, b) in enumerate(FLIPS)])
    bottom = added([move(bottom[d], y=-d) for d in range(ny)])
    return jnp.concatenate([top, bottom], axis=1).T


def mirrored(lines):
    return jnp.roll(lines[:, ::-1], 1, axis=1)


def shards(tokens_in, short_filter, long_filter, out_weight, cotangent):
    ny, nz = lax.axis_size("y"), lax.axis_size("z")
    y, xl, xh, z, c = (lax.axis_index(a) for a in ("y", "xl", "xh", "z", "c"))
    tokens = tokens_in[0]
    rows, wide = tokens.shape
    channels = wide // 3
    short_taps = short_filter.shape[0]
    groups = long_filter.shape[0]
    upstream = cotangent[0]
    length, columns = upstream.shape
    span = length // 2

    block = jnp.arange(2 * ny, dtype=jnp.int32)
    place = ((y - block // 2) % ny) * 2 + (block + xl) % 2
    size = 3 * channels // LANES + groups // 8
    each = size // (2 * nz)
    tile = jnp.arange(size, dtype=jnp.int32)
    places = ((tile // (nz * each) + c) % 2 * nz + (tile // each - z) % nz) * each + tile % each

    wide_top, tall_bottom = gather_near(out_weight)
    mine = lax.dynamic_slice_in_dim(upstream, xh * span, span, 0)
    others = move(lax.dynamic_slice_in_dim(upstream, (1 - xh) * span, span, 0), xh=1)
    cotangents = jnp.concatenate([mine, others], axis=1)

    rim = along(tokens[rows - RIM :], 1)
    lines = long_filter.astype(F32)
    query, key, value, mixer = features_call(tokens, rim, short_filter)
    mixer_prev = along(mixer, 1)
    mixer_prev, wide_top, tall_bottom = lax.optimization_barrier((mixer_prev, wide_top, tall_bottom))
    tops, bottoms = gather_far(wide_top, tall_bottom)
    mixed, gated = mix_call(place, mirrored(lines), mixer_prev, mixer, query)

    partial = gate_matmul(cotangents, tops, bottoms)
    gate_grad = lax.psum_scatter(partial, ("z", "c"), scatter_dimension=0, tiled=True)
    all_rows = lax.all_gather(gated, ("z", "c"), axis=0, tiled=True)

    grad_mixed, query_grad = gate_call(place, gate_grad, query, mixed)
    grad_next = along(grad_mixed, -1)
    query_next = along(query_grad[:RIM], -1)
    long_sum, query_sum = long_grad_call(
        groups, short_taps, mixer_prev, mixer, grad_mixed, query_grad, tokens, rim
    )
    other_grads, key_sum, value_sum = unmix_call(
        lines, short_taps, grad_mixed, grad_next, key, value, tokens, rim
    )
    other_next = along(other_grads[:, :RIM], -1)
    grad_short, grad_long = total_over_devices(places, query_sum, key_sum, value_sum, long_sum, short_taps)
    grad_tokens = short_adjoint_call(query_grad, other_grads, query_next, other_next, short_filter)

    own, other, top_grads, bottom_grads = project(all_rows, cotangents.T, tops, bottoms)
    grad_weight = plane_scatter_sum(top_grads, bottom_grads)
    theirs = move(other, xh=1)
    output = jnp.where(xh == 0, jnp.concatenate([own, theirs], axis=0), jnp.concatenate([theirs, own], axis=0))
    return output[None], grad_tokens[None], grad_short, mirrored(grad_long), grad_weight


def solution(mesh):
    dp, seq = mesh.shape["dp"], mesh.shape["seq"]
    grid = jax.sharding.Mesh(mesh.devices.reshape(dp // 2, 2, 2, seq // 4, 2), ("y", "xl", "xh", "z", "c"))
    rows, line = ("y", "xl"), ("xh", "z", "c")
    return jax.shard_map(
        shards,
        mesh=grid,
        in_specs=(P(rows, line, None), P(), P(), P(rows, line), P(rows, None, line)),
        out_specs=(P(rows, None, line), P(rows, line, None), P(), P(), P(rows, line)),
        check_vma=False,
    )
```

time: 547 us -> 300 us (0.55)
  waiting for transfers between devices: 411 us -> 79.7 us
  starting transfers between devices: 14.1 us -> 85.9 us
  matrix products: 28.8 us -> 0 us
  Pallas kernels: 60.9 us -> 80.2 us
  local copies, waits for them, and re-layouts: 11.9 us -> 26.6 us
  other arithmetic: 5.14 us -> 10.9 us
    psum x1 -> x0, waiting for transfers between devices: 116 us -> none  [shards(): grad_short, grad_long = lax.psum((short_local, long_local), ('dp', 'seq'))]
    reduce_scatter x2 -> x1, waiting for transfers between devices: 141 us -> 32 us  [shards(): lax.psum_scatter(partial, ('z', 'c'), scatter_dimension=0, tiled=True)]
    all_gather x2 -> x1, waiting for transfers between devices: 114 us -> 14.8 us  [shards(): all_rows = lax.all_gather(gated, ('z', 'c'), axis=0, tiled=True)]
    ppermute x4 -> x45, starting transfers between devices: 13.9 us -> 85.8 us  [the longest x40 60.1 us: move(): return lax.ppermute(x, axes, pairs)]
    dot_general x3 -> x0, matrix products: 28.8 us -> none  [the longest x1 9.81 us: shards(): lax.dot_general(all_rows, upstream, (((0,), (0,)), ((), ())), preferred_e...]
    pallas_call x3 -> x8, Pallas kernels: 39.3 us -> 61.6 us  [the longest x1 14.7 us: unmix_call(): pl.pallas_call(functools.partial(unmix_kernel, per_group, short_taps), gr...]
    unnamed x25 -> x66, local copies, waits for them, and re-layouts: 8.54 us -> 19.5 us
    ppermute x4 -> x45, waiting for transfers between devices: 38.2 us -> 32.9 us  [the longest x40 30.3 us: move(): return lax.ppermute(x, axes, pairs)]
  transfers between devices with their start and end apart: 9 -> 47, of which waited for: 9 -> 14; matrix products, arithmetic and copies ran while one was open for 5% -> 7% of each run, Pallas kernels for 11% -> 20%
where the time goes in v2:
time: 300 us; the launch traced here: 298 us
  starting transfers between devices  85.9 us (29%)
  Pallas kernels  80.2 us (27%)
  waiting for transfers between devices  79.7 us (27%)
  local copies, waits for them, and re-layouts  26.6 us (9%)
  between operations  14.5 us (5%)
  other arithmetic  10.9 us (4%)
    ppermute x40, starting transfers between devices, move(): return lax.ppermute(x, axes, pairs)  60.1 us
    reduce_scatter x1, waiting for transfers between devices, shards(): lax.psum_scatter(partial, ('z', 'c'), scatter_dimension=0, tiled=True)  32 us
    ppermute x40, waiting for transfers between devices, move(): return lax.ppermute(x, axes, pairs)  30.3 us
    ppermute x5, starting transfers between devices, along(): return lax.ppermute(x, LINE, pairs)  25.7 us
    unnamed x66, local copies, waits for them, and re-layouts  19.5 us
    all_gather x1, waiting for transfers between devices, shards(): all_rows = lax.all_gather(gated, ('z', 'c'), axis=0, tiled=True)  14.8 us
    pallas_call x1, Pallas kernels, unmix_call(): pl.pallas_call(functools.partial(unmix_kernel, per_group, short_taps), gr...  14.7 us
    pallas_call x1, Pallas kernels, project(): pl.pallas_call(functools.partial(project_kernel, ny), grid=(ny,), in_spec...  14.4 us
  transfers between devices with their start and end apart: 47, of which 14 were waited for; matrix products, arithmetic and copies ran while one was open for 7% of the time, Pallas kernels for 20%

profile of v2, /device:TPU:1, one launch (start us, length us, event | category | flops | bytes accessed | tf_op | source)
XLA Modules:
  0.0 297.8 jit_solution(11078984092970253386)
XLA Ops:
  8.2 4.9 %collective-permute-start = (bf16[8,12288]{1,0:T(8,128)(2,1)S(1)}, bf16[8,12288]{1,0:T(8,128)(2,1)S(1)}, u32[]{:S(2)}, u32[]{:S(2)}) collective-permute-start(bf16[8,12288]{1,0:T(8,128)(2,1)S(1)} %slice_bitcast_fusion), channel_id=1, source_target_pairs={{0,1},{1,2},{2,3},{3,4},{4,5},{5,6},{6,7},{7,8},{8,9},{9,10},{10,1... | collective-permute-start | bytes 589832 | tf_op jit(solution)/shard_map/ppermute | solution.py:26
  13.1 2.6 collective-permute-done.refs_3_.refs_4_.refs_5_.key_rim_ref.value_rim_ref.rim_ref
  15.7 1.0 copy-done
  16.7 8.8 %features.1 = (bf16[128,4096]{1,0:T(8,128)(2,1)S(1)}, bf16[128,4096]{1,0:T(8,128)(2,1)S(1)}, bf16[128,4096]{1,0:T(8,128)(2,1)S(1)}, bf16[128,4096]{1,0:T(8,128)(2,1)S(1)}) custom-call(bf16[128,12288]{1,0:T(8,128)(2,1)} %bitcast.49, bf16[128,12288]{1,0:T(8,128)(2,1)} %bitcast.50, bf16[128,12288]{1,0:T(8,128)(2,1)} %bitcast.51, ...), custom_call_target="tpu_custom_call" | custom-call | flops 22020096 | bytes 15728640 | tf_op jit(solution)/shard_map/features/pallas_call | solution.py:97
  26.5 1.0 copy-done.6
  27.5 4.4 %collective-permute-start.1 = (bf16[128,4096]{1,0:T(8,128)(2,1)S(1)}, bf16[128,4096]{1,0:T(8,128)(2,1)}, u32[]{:S(2)}, u32[]{:S(2)}) collective-permute-start(bf16[128,4096]{1,0:T(8,128)(2,1)S(1)} %get-tuple-element.33.cur_ref), channel_id=1, source_target_pairs={{0,1},{1,2},{2,3},{3,4},{4,5},{5,6},{6,7},{7,8},{8,9},{9,10},{10,1... | collective-permute-start | bytes 3145736 | tf_op jit(solution)/shard_map/ppermute | solution.py:26
  32.6 2.7 collective-permute-start.2
  36.2 1.3 collective-permute-start.5
  37.9 2.9 collective-permute-start.6
  40.8 1.8 collective-permute-start.7
  42.6 1.0 pad_maximum_fusion.1.refs_2_.refs_1_
  44.1 1.1 collective-permute-done.7
  45.2 1.0 pad_maximum_fusion.2.refs_6_.refs_5_
  46.3 1.4 copy-done.16
  47.7 10.1 %mix.1 = (bf16[128,4096]{1,0:T(8,128)(2,1)S(1)}, bf16[128,4096]{1,0:T(8,128)(2,1)}) custom-call(s32[8]{0:T(128)S(1)} %fusion.7.place, f32[256,128]{1,0:T(8,128)S(1)} %pad_maximum_fusion.4.lines_ref, bf16[128,4096]{1,0:T(8,128)(2,1)} %collective-permute-done.1.prev_ref, bf16[128,4096]{1,0:T(8,128)(2,1)S(1)} %copy-done.16, ...), custom_call_target="tpu_custom_call" | custom-call | flops 2147483648 | bytes 5242880 | tf_op jit(solution)/shard_map/mix/pallas_call | solution.py:156
  57.9 1.3 dynamic-slice_bitcast_fusion.1
  59.2 3.0 %collective-permute-start.8 = (bf16[1024,256]{1,0:T(8,128)(2,1)S(1)}, bf16[1024,256]{1,0:T(8,128)(2,1)S(1)}, u32[]{:S(2)}, u32[]{:S(2)}) collective-permute-start(bf16[1024,256]{1,0:T(8,128)(2,1)S(1)} %get-tuple-element.71), channel_id=1, source_target_pairs={{0,8},{8,0},{1,9},{9,1},{2,10},{10,2},{3,11},{11,3},{4,12},{12,4},... | collective-permute-start | bytes 1572872 | tf_op jit(solution)/shard_map/ppermute | solution.py:38
  62.2 2.2 collective-permute-start.10
  64.4 1.1 collective-permute-start.11
  65.7 1.4 collective-permute-start.13
  67.1 1.8 collective-permute-done.8
  68.8 2.6 collective-permute-start.14
  72.1 1.0 collective-permute-start.9
  73.1 1.1 pad_maximum_fusion
  74.2 11.9 %collective-permute-done.11.refs_5_.refs_4_ = bf16[4,256,256]{2,1,0:T(8,128)(2,1)S(1)} collective-permute-done((bf16[4,256,256]{2,1,0:T(8,128)(2,1)S(1)}, bf16[4,256,256]{2,1,0:T(8,128)(2,1)S(1)}, u32[]{:S(2)}, u32[]{:S(2)}) %collective-permute-start.11) | collective-permute-done | bytes 524320 | tf_op jit(solution)/shard_map/ppermute | solution.py:38
  86.1 3.9 %collective-permute-done.13.refs_8_.refs_7_ = bf16[4,256,256]{2,1,0:T(8,128)(2,1)S(1)} collective-permute-done((bf16[4,256,256]{2,1,0:T(8,128)(2,1)S(1)}, bf16[4,256,256]{2,1,0:T(8,128)(2,1)S(1)}, u32[]{:S(2)}, u32[]{:S(2)}) %collective-permute-start.13) | collective-permute-done | bytes 524320 | tf_op jit(solution)/shard_map/ppermute | solution.py:38
  90.0 4.5 %collective-permute-done.14.refs_9_.refs_8_ = bf16[4,256,256]{2,1,0:T(8,128)(2,1)S(1)} collective-permute-done((bf16[4,256,256]{2,1,0:T(8,128)(2,1)S(1)}, bf16[4,256,256]{2,1,0:T(8,128)(2,1)S(1)}, u32[]{:S(2)}, u32[]{:S(2)}) %collective-permute-start.14) | collective-permute-done | bytes 524320 | tf_op jit(solution)/shard_map/ppermute | solution.py:38
  94.5 6.8 %gate_matmul.1 = bf16[1024,4096]{1,0:T(8,128)(2,1)} custom-call(bf16[1024,512]{1,0:T(8,128)(2,1)S(1)} %get-tuple-element.68.refs_0_, bf16[4,256,256]{2,1,0:T(8,128)(2,1)S(1)} %pad_maximum_fusion.1.refs_2_.refs_1_, bf16[4,256,256]{2,1,0:T(8,128)(2,1)S(1)} %collective-permute-done.9.refs_3_.refs_2_, ...), custom_call_target="tpu_custom_call" | custom-call | flops 4294967296 | bytes 12582912 | tf_op jit(solution)/shard_map/gate_matmul/pallas_call | solution.py:471
  105.4 2.3 copy.10.refs_1_
  107.7 14.8 %all-gather.2.cloned.1.call-done.refs_0_ = bf16[1024,4096]{1,0:T(8,128)(2,1)} async-done(((bf16[128,4096]{1,0:T(8,128)(2,1)}), bf16[1024,4096]{1,0:T(8,128)(2,1)}) %all-gather.2.cloned.1.call-update) | async-done | bytes 8388624 | tf_op jit(solution)/shard_map/all_gather | solution.py:597
  122.5 14.4 %project.1 = (bf16[1024,256]{1,0:T(8,128)(2,1)S(1)}, bf16[1024,256]{1,0:T(8,128)(2,1)S(1)}, bf16[4,256,256]{2,1,0:T(8,128)(2,1)S(1)}, bf16[4,256,256]{2,1,0:T(8,...) custom-call(bf16[1024,4096]{1,0:T(8,128)(2,1)} %all-gather.2.cloned., ...), custom_call_target="tpu_custom_call" | custom-call | flops 8589934592 | bytes 16777216 | tf_op jit(solution)/shard_map/project/pallas_call | solution.py:528
  140.9 2.5 collective-permute-start.33
  144.5 32.0 %reduce-scatter.2.cloned.1.call-done.gate_grad_ref = bf16[128,4096]{1,0:T(8,128)(2,1)} async-done(((bf16[1024,4096]{1,0:T(8,128)(2,1)}), bf16[128,4096]{1,0:T(8,128)(2,1)}) %reduce-scatter.2.cloned.1.call-update) | async-done | bytes 1048592 | tf_op jit(solution)/shard_map/reduce_scatter | solution.py:596
  176.5 1.2 copy-done.3
  177.7 3.7 %gate_back.1 = (bf16[128,4096]{1,0:T(8,128)(2,1)}, bf16[128,4096]{1,0:T(8,128)(2,1)S(1)}) custom-call(s32[8]{0:T(128)S(1)} %fusion.7.place, bf16[128,4096]{1,0:T(8,128)(2,1)S(1)} %copy-done.3, bf16[128,4096]{1,0:T(8,128)(2,1)S(1)} %get-tuple-element.35.query_ref, bf16[128,4096]{1,0:T(8,128)(2,1)S(1)} %get-tuple-element.41.mixed_ref), custom_call_target="tpu_custom_call" | custom-call | flops 1048576 | bytes 5242880 | tf_op jit(solution)/shard_map/gate_back/pallas_call | solution.py:184
  181.4 3.3 %collective-permute-start.16 = (bf16[128,4096]{1,0:T(8,128)(2,1)}, bf16[128,4096]{1,0:T(8,128)(2,1)}, u32[]{:S(2)}, u32[]{:S(2)}) collective-permute-start(bf16[128,4096]{1,0:T(8,128)(2,1)} %get-tuple-element.43.grad_ref), channel_id=1, source_target_pairs={{1,0},{2,1},{3,2},{4,3},{5,4},{6,5},{7,6},{8,7},{9,8},{10,9},{11,1... | collective-permute-start | bytes 3145736 | tf_op jit(solution)/shard_map/ppermute | solution.py:26
  185.6 2.8 collective-permute-start.39
  189.3 2.3 collective-permute-start.15
  191.6 1.8 add_convert_fusion.1
  193.5 1.2 copy-done.17
  194.7 9.9 %long_grad.1 = (f32[256,128]{1,0:T(8,128)S(1)}, f32[8,4096]{1,0:T(8,128)S(1)}) custom-call(bf16[128,4096]{1,0:T(8,128)(2,1)} %collective-permute-done.1.prev_ref, bf16[128,4096]{1,0:T(8,128)(2,1)S(1)} %copy-done.17, bf16[128,4096]{1,0:T(8,128)(2,1)} %get-tuple-element.43.grad_ref, bf16[128,4096]{1,0:T(8,128)(2,1)S(1)} %get-tuple-element.42.query_ref.feature_ref, ...), custom_call_target="tpu_custom_call" | custom-call | flops 2147483648 | bytes 5242880 | tf_op jit(solution)/shard_map/long_grad/pallas_call | solution.py:241
  204.6 1.0 collective-permute-start.36
  205.6 14.7 %unmix.1 = (bf16[2,128,4096]{2,1,0:T(8,128)(2,1)}, f32[8,4096]{1,0:T(8,128)S(1)}, f32[8,4096]{1,0:T(8,128)S(1)}) custom-call(f32[256,128]{1,0:T(8,128)S(1)} %convert_element_type.63.lines_ref, bf16[128,4096]{1,0:T(8,128)(2,1)} %get-tuple-element.43.grad_ref, bf16[128,4096]{1,0:T(8,128)(2,1)} %collective-permute-done.16.next_ref, ...), custom_call_target="tpu_custom_call" | custom-call | flops 2147483648 | bytes 8388608 | tf_op jit(solution)/shard_map/unmix/pallas_call | solution.py:296
  221.8 6.5 %collective-permute-start.19 = (f32[64,8,128]{2,1,0:T(8,128)S(1)}, f32[64,8,128]{2,1,0:T(8,128)S(1)}, u32[]{:S(2)}, u32[]{:S(2)}) collective-permute-start(f32[64,8,128]{2,1,0:T(8,128)S(1)} %slice.111), channel_id=1, source_target_pairs={{0,1},{1,0},{2,3},{3,2},{4,5},{5,4},{6,7},{7,6},{8,9},{9,8},{10,11... | collective-permute-start | bytes 786440 | tf_op jit(solution)/shard_map/ppermute | solution.py:38
  228.3 1.7 collective-permute-done.41
  230.4 1.2 maximum_select_fusion
  231.7 1.3 collective-permute-start.21
  233.1 1.3 collective-permute-start.22
  234.4 2.6 collective-permute-done.20
  237.1 1.9 collective-permute-start.38
  239.0 2.5 collective-permute-start.42
  242.0 2.5 collective-permute-start.23
  244.5 2.7 collective-permute-start.25
  247.5 1.4 collective-permute-done.24
  248.9 1.3 collective-permute-start.26
  250.2 1.0 collective-permute-start.27
  251.2 1.6 collective-permute-start.28
  253.5 11.2 %collective-permute-start.17 = (bf16[8,4096]{1,0:T(8,128)(2,1)}, bf16[8,4096]{1,0:T(8,128)(2,1)}, u32[]{:S(2)}, u32[]{:S(2)}) collective-permute-start(bf16[8,4096]{1,0:T(8,128)(2,1)} %slice.89), channel_id=1, source_target_pairs={{1,0},{2,1},{3,2},{4,3},{5,4},{6,5},{7,6},{8,7},{9,8},{10,9},{11,1... | collective-permute-start | bytes 196616 | tf_op jit(solution)/shard_map/ppermute | solution.py:26
  265.4 1.9 collective-permute-start.18
  268.0 2.4 collective-permute-start.29
  271.8 2.0 copy.11
  273.9 9.8 %short_adjoint.1 = bf16[128,12288]{1,0:T(8,128)(2,1)} custom-call(bf16[128,4096]{1,0:T(8,128)(2,1)S(1)} %get-tuple-element.42.query_ref.feature_ref, bf16[2,128,4096]{2,1,0:T(8,128)(2,1)S(1)} %copy-done.2, bf16[8,4096]{1,0:T(8,128)(2,1)} %collective-permute-done.17.query_rim_ref, bf16[2,8,4096]{2,1,0:T(8,128)(2,1)} %collective-permute-done.18.other_rim_ref, ...), custom_call_target="tpu_custom_call" | custom-call | flops 22020096 | bytes 6291456 | tf_op jit(solution)/shard_map/short_adjoint/pallas_call | solution.py:342
  284.7 1.3 collective-permute-start.32
  288.5 1.4 collect.1
  (143 shorter events, 27.1 us)
Async XLA Ops:
  7.2 115.3 %all-gather.2.cloned.1.call-start = ((), (), s32[]{:S(2)}) async-start(), calls=%async_computation.1 | async-start | bytes 9437184 | tf_op jit(solution)/shard_map/all_gather | solution.py:597
  8.2 7.5 %collective-permute-start = (bf16[8,12288]{1,0:T(8,128)(2,1)S(1)}, bf16[8,12288]{1,0:T(8,128)(2,1)S(1)}, u32[]{:S(2)}, u32[]{:S(2)}) collective-permute-start(bf16[8,12288]{1,0:T(8,128)(2,1)S(1)} %slice_bitcast_fusion), channel_id=1, source_target_pairs={{0,1},{1,2},{2,3},{3,4},{4,5},{5,6},{6,7},{7,8},{8,9},{9,10},{10,1... | collective-permute-start | bytes 589832 | tf_op jit(solution)/shard_map/ppermute | solution.py:26
  16.7 15.2 %copy-start.29 = (bf16[512,256]{1,0:T(8,128)(2,1)S(1)}, bf16[512,256]{1,0:T(8,128)(2,1)}, u32[]{:S(2)}) copy-start(bf16[512,256]{1,0:T(8,128)(2,1)} %param.8) | copy-start | bytes 786436
  16.7 20.8 %copy-start.28 = (bf16[256,128]{1,0:T(8,128)(2,1)S(1)}, bf16[256,128]{1,0:T(8,128)(2,1)}, u32[]{:S(2)}) copy-start(bf16[256,128]{1,0:T(8,128)(2,1)} %param.7) | copy-start | bytes 196612
  27.5 18.8 %copy-start.15 = (bf16[128,4096]{1,0:T(8,128)(2,1)}, bf16[128,4096]{1,0:T(8,128)(2,1)S(1)}, u32[]{:S(2)}) copy-start(bf16[128,4096]{1,0:T(8,128)(2,1)S(1)} %get-tuple-element.33.cur_ref) | copy-start | bytes 3145732
  27.5 18.8 %collective-permute-start.1 = (bf16[128,4096]{1,0:T(8,128)(2,1)S(1)}, bf16[128,4096]{1,0:T(8,128)(2,1)}, u32[]{:S(2)}, u32[]{:S(2)}) collective-permute-start(bf16[128,4096]{1,0:T(8,128)(2,1)S(1)} %get-tuple-element.33.cur_ref), channel_id=1, source_target_pairs={{0,1},{1,2},{2,3},{3,4},{4,5},{5,6},{6,7},{7,8},{8,9},{9,10},{10,1... | collective-permute-start | bytes 3145736 | tf_op jit(solution)/shard_map/ppermute | solution.py:26
  32.6 5.3 %collective-permute-start.2 = (bf16[256,256]{1,0:T(8,128)(2,1)S(1)}, bf16[256,256]{1,0:T(8,128)(2,1)S(1)}, u32[]{:S(2)}, u32[]{:S(2)}) collective-permute-start(bf16[256,256]{1,0:T(8,128)(2,1)S(1)} %get-tuple-element.84), channel_id=1, source_target_pairs={{0,8},{8,0},{1,9},{9,1},{2,10},{10,2},{3,11},{11,3},{4,12},{12,4},... | collective-permute-start | bytes 393224 | tf_op jit(solution)/shard_map/ppermute | solution.py:38
  35.3 5.5 %collective-permute-start.3 = (bf16[256,256]{1,0:T(8,128)(2,1)S(1)}, bf16[256,256]{1,0:T(8,128)(2,1)}, u32[]{:S(2)}, u32[]{:S(2)}) collective-permute-start(bf16[256,256]{1,0:T(8,128)(2,1)S(1)} %get-tuple-element.84), channel_id=1, source_target_pairs={{0,16},{16,0},{1,17},{17,1},{2,18},{18,2},{3,19},{19,3},{4,20},{20... | collective-permute-start | bytes 393224 | tf_op jit(solution)/shard_map/ppermute | solution.py:38
  35.6 7.0 %collective-permute-start.4 = (bf16[256,256]{1,0:T(8,128)(2,1)S(1)}, bf16[256,256]{1,0:T(8,128)(2,1)}, u32[]{:S(2)}, u32[]{:S(2)}) collective-permute-start(bf16[256,256]{1,0:T(8,128)(2,1)S(1)} %get-tuple-element.84), channel_id=1, source_target_pairs={{0,24},{8,16},{16,8},{24,0},{1,25},{9,17},{17,9},{25,1},{2,26},{10... | collective-permute-start | bytes 393224 | tf_op jit(solution)/shard_map/ppermute | solution.py:38
  36.2 7.5 %collective-permute-start.5 = (bf16[256,256]{1,0:T(8,128)(2,1)S(1)}, bf16[256,256]{1,0:T(8,128)(2,1)S(1)}, u32[]{:S(2)}, u32[]{:S(2)}) collective-permute-start(bf16[256,256]{1,0:T(8,128)(2,1)S(1)} %get-tuple-element.83), channel_id=1, source_target_pairs={{0,32},{32,64},{64,96},{96,0},{1,33},{33,65},{65,97},{97,1},{2,34}... | collective-permute-start | bytes 393224 | tf_op jit(solution)/shard_map/ppermute | solution.py:38
  37.9 6.2 %collective-permute-start.6 = (bf16[256,256]{1,0:T(8,128)(2,1)S(1)}, bf16[256,256]{1,0:T(8,128)(2,1)S(1)}, u32[]{:S(2)}, u32[]{:S(2)}) collective-permute-start(bf16[256,256]{1,0:T(8,128)(2,1)S(1)} %get-tuple-element.83), channel_id=1, source_target_pairs={{0,64},{32,96},{64,0},{96,32},{1,65},{33,97},{65,1},{97,33},{2,66}... | collective-permute-start | bytes 393224 | tf_op jit(solution)/shard_map/ppermute | solution.py:38
  40.8 4.4 %collective-permute-start.7 = (bf16[256,256]{1,0:T(8,128)(2,1)S(1)}, bf16[256,256]{1,0:T(8,128)(2,1)S(1)}, u32[]{:S(2)}, u32[]{:S(2)}) collective-permute-start(bf16[256,256]{1,0:T(8,128)(2,1)S(1)} %get-tuple-element.83), channel_id=1, source_target_pairs={{0,96},{32,0},{64,32},{96,64},{1,97},{33,1},{65,33},{97,65},{2,98}... | collective-permute-start | bytes 393224 | tf_op jit(solution)/shard_map/ppermute | solution.py:38
  43.6 1.6 copy-start.30
  46.3 48.2 %copy-start.14 = (bf16[4,256,256]{2,1,0:T(8,128)(2,1)}, bf16[4,256,256]{2,1,0:T(8,128)(2,1)S(1)}, u32[]{:S(2)}) copy-start(bf16[4,256,256]{2,1,0:T(8,128)(2,1)S(1)} %pad_maximum_fusion.2.refs_6_.refs_5_) | copy-start | bytes 1572868
  46.3 1.4 copy-start.16
  57.9 118.6 %reduce-scatter.2.cloned.1.call-start = ((), (), s32[]{:S(2)}) async-start(), calls=%async_computation.2 | async-start | bytes 9437184 | tf_op jit(solution)/shard_map/reduce_scatter | solution.py:596
  59.2 9.6 %collective-permute-start.8 = (bf16[1024,256]{1,0:T(8,128)(2,1)S(1)}, bf16[1024,256]{1,0:T(8,128)(2,1)S(1)}, u32[]{:S(2)}, u32[]{:S(2)}) collective-permute-start(bf16[1024,256]{1,0:T(8,128)(2,1)S(1)} %get-tuple-element.71), channel_id=1, source_target_pairs={{0,8},{8,0},{1,9},{9,1},{2,10},{10,2},{3,11},{11,3},{4,12},{12,4},... | collective-permute-start | bytes 1572872 | tf_op jit(solution)/shard_map/ppermute | solution.py:38
  62.2 9.8 %collective-permute-start.10 = (bf16[4,256,256]{2,1,0:T(8,128)(2,1)S(1)}, bf16[4,256,256]{2,1,0:T(8,128)(2,1)S(1)}, u32[]{:S(2)}, u32[]{:S(2)}) collective-permute-start(bf16[4,256,256]{2,1,0:T(8,128)(2,1)S(1)} %pad_maximum_fusion.1.refs_2_.refs_1_), channel_id=1, source_target_pairs={{0,64},{32,96},{64,0},{96,32},{1,65},{33,97},{65,1},{97,33},{2,66}... | collective-permute-start | bytes 1572872 | tf_op jit(solution)/shard_map/ppermute | solution.py:38
  64.4 21.6 %collective-permute-start.11 = (bf16[4,256,256]{2,1,0:T(8,128)(2,1)S(1)}, bf16[4,256,256]{2,1,0:T(8,128)(2,1)S(1)}, u32[]{:S(2)}, u32[]{:S(2)}) collective-permute-start(bf16[4,256,256]{2,1,0:T(8,128)(2,1)S(1)} %pad_maximum_fusion.1.refs_2_.refs_1_), channel_id=1, source_target_pairs={{0,96},{32,0},{64,32},{96,64},{1,97},{33,1},{65,33},{97,65},{2,98}... | collective-permute-start | bytes 1572872 | tf_op jit(solution)/shard_map/ppermute | solution.py:38
  65.6 20.5 %collective-permute-start.12 = (bf16[4,256,256]{2,1,0:T(8,128)(2,1)S(1)}, bf16[4,256,256]{2,1,0:T(8,128)(2,1)S(1)}, u32[]{:S(2)}, u32[]{:S(2)}) collective-permute-start(bf16[4,256,256]{2,1,0:T(8,128)(2,1)S(1)} %pad_maximum_fusion.2.refs_6_.refs_5_), channel_id=1, source_target_pairs={{0,8},{8,0},{1,9},{9,1},{2,10},{10,2},{3,11},{11,3},{4,12},{12,4},... | collective-permute-start | bytes 1572872 | tf_op jit(solution)/shard_map/ppermute | solution.py:38
  65.7 24.3 %collective-permute-start.13 = (bf16[4,256,256]{2,1,0:T(8,128)(2,1)S(1)}, bf16[4,256,256]{2,1,0:T(8,128)(2,1)S(1)}, u32[]{:S(2)}, u32[]{:S(2)}) collective-permute-start(bf16[4,256,256]{2,1,0:T(8,128)(2,1)S(1)} %pad_maximum_fusion.2.refs_6_.refs_5_), channel_id=1, source_target_pairs={{0,16},{16,0},{1,17},{17,1},{2,18},{18,2},{3,19},{19,3},{4,20},{20... | collective-permute-start | bytes 1572872 | tf_op jit(solution)/shard_map/ppermute | solution.py:38
  68.8 25.6 %collective-permute-start.14 = (bf16[4,256,256]{2,1,0:T(8,128)(2,1)S(1)}, bf16[4,256,256]{2,1,0:T(8,128)(2,1)S(1)}, u32[]{:S(2)}, u32[]{:S(2)}) collective-permute-start(bf16[4,256,256]{2,1,0:T(8,128)(2,1)S(1)} %pad_maximum_fusion.2.refs_6_.refs_5_), channel_id=1, source_target_pairs={{0,24},{8,16},{16,8},{24,0},{1,25},{9,17},{17,9},{25,1},{2,26},{10... | collective-permute-start | bytes 1572872 | tf_op jit(solution)/shard_map/ppermute | solution.py:38
  72.1 22.4 %copy-start.22 = (bf16[4,256,256]{2,1,0:T(8,128)(2,1)}, bf16[4,256,256]{2,1,0:T(8,128)(2,1)S(1)}, u32[]{:S(2)}) copy-start(bf16[4,256,256]{2,1,0:T(8,128)(2,1)S(1)} %collective-permute-done.10.refs_4_.refs_3_) | copy-start | bytes 1572868
  72.1 22.4 %collective-permute-start.9 = (bf16[4,256,256]{2,1,0:T(8,128)(2,1)S(1)}, bf16[4,256,256]{2,1,0:T(8,128)(2,1)S(1)}, u32[]{:S(2)}, u32[]{:S(2)}) collective-permute-start(bf16[4,256,256]{2,1,0:T(8,128)(2,1)S(1)} %pad_maximum_fusion.1.refs_2_.refs_1_), channel_id=1, source_target_pairs={{0,32},{32,64},{64,96},{96,0},{1,33},{33,65},{65,97},{97,1},{2,34}... | collective-permute-start | bytes 1572872 | tf_op jit(solution)/shard_map/ppermute | solution.py:38
  140.1 3.3 %copy-start.19 = (bf16[4,256,256]{2,1,0:T(8,128)(2,1)}, bf16[4,256,256]{2,1,0:T(8,128)(2,1)S(1)}, u32[]{:S(2)}) copy-start(bf16[4,256,256]{2,1,0:T(8,128)(2,1)S(1)} %get-tuple-element.60) | copy-start | bytes 1572868
  140.1 36.4 %copy-start.20 = (bf16[4,256,256]{2,1,0:T(8,128)(2,1)}, bf16[4,256,256]{2,1,0:T(8,128)(2,1)S(1)}, u32[]{:S(2)}) copy-start(bf16[4,256,256]{2,1,0:T(8,128)(2,1)S(1)} %get-tuple-element.59) | copy-start | bytes 1572868
  140.9 47.5 %collective-permute-start.33 = (bf16[4,256,256]{2,1,0:T(8,128)(2,1)}, bf16[4,256,256]{2,1,0:T(8,128)(2,1)}, u32[]{:S(2)}, u32[]{:S(2)}) collective-permute-start(bf16[4,256,256]{2,1,0:T(8,128)(2,1)} %get-tuple-element.54), channel_id=1, source_target_pairs={{0,96},{32,0},{64,32},{96,64},{1,97},{33,1},{65,33},{97,65},{2,98}... | collective-permute-start | bytes 1572872 | tf_op jit(solution)/shard_map/ppermute | solution.py:38
  143.3 45.3 %collective-permute-start.34 = (bf16[4,256,256]{2,1,0:T(8,128)(2,1)}, bf16[4,256,256]{2,1,0:T(8,128)(2,1)}, u32[]{:S(2)}, u32[]{:S(2)}) collective-permute-start(bf16[4,256,256]{2,1,0:T(8,128)(2,1)} %get-tuple-element.55), channel_id=1, source_target_pairs={{0,64},{32,96},{64,0},{96,32},{1,65},{33,97},{65,1},{97,33},{2,66}... | collective-permute-start | bytes 1572872 | tf_op jit(solution)/shard_map/ppermute | solution.py:38
  143.9 45.5 %collective-permute-start.35 = (bf16[4,256,256]{2,1,0:T(8,128)(2,1)}, bf16[4,256,256]{2,1,0:T(8,128)(2,1)}, u32[]{:S(2)}, u32[]{:S(2)}) collective-permute-start(bf16[4,256,256]{2,1,0:T(8,128)(2,1)} %get-tuple-element.56), channel_id=1, source_target_pairs={{0,32},{32,64},{64,96},{96,0},{1,33},{33,65},{65,97},{97,1},{2,34}... | collective-permute-start | bytes 1572872 | tf_op jit(solution)/shard_map/ppermute | solution.py:38
  181.4 23.2 %collective-permute-start.16 = (bf16[128,4096]{1,0:T(8,128)(2,1)}, bf16[128,4096]{1,0:T(8,128)(2,1)}, u32[]{:S(2)}, u32[]{:S(2)}) collective-permute-start(bf16[128,4096]{1,0:T(8,128)(2,1)} %get-tuple-element.43.grad_ref), channel_id=1, source_target_pairs={{1,0},{2,1},{3,2},{4,3},{5,4},{6,5},{7,6},{8,7},{9,8},{10,9},{11,1... | collective-permute-start | bytes 3145736 | tf_op jit(solution)/shard_map/ppermute | solution.py:26
  185.6 35.3 %collective-permute-start.39 = (bf16[4,256,256]{2,1,0:T(8,128)(2,1)}, bf16[4,256,256]{2,1,0:T(8,128)(2,1)S(1)}, u32[]{:S(2)}, u32[]{:S(2)}) collective-permute-start(bf16[4,256,256]{2,1,0:T(8,128)(2,1)} %copy-done.21), channel_id=1, source_target_pairs={{0,8},{8,0},{1,9},{9,1},{2,10},{10,2},{3,11},{11,3},{4,12},{12,4},... | collective-permute-start | bytes 1572872 | tf_op jit(solution)/shard_map/ppermute | solution.py:38
  188.4 33.4 %collective-permute-start.40 = (bf16[4,256,256]{2,1,0:T(8,128)(2,1)}, bf16[4,256,256]{2,1,0:T(8,128)(2,1)S(1)}, u32[]{:S(2)}, u32[]{:S(2)}) collective-permute-start(bf16[4,256,256]{2,1,0:T(8,128)(2,1)} %copy-done.20), channel_id=1, source_target_pairs={{0,16},{16,0},{1,17},{17,1},{2,18},{18,2},{3,19},{19,3},{4,20},{20... | collective-permute-start | bytes 1572872 | tf_op jit(solution)/shard_map/ppermute | solution.py:38
  188.7 41.4 %collective-permute-start.41 = (bf16[4,256,256]{2,1,0:T(8,128)(2,1)}, bf16[4,256,256]{2,1,0:T(8,128)(2,1)S(1)}, u32[]{:S(2)}, u32[]{:S(2)}) collective-permute-start(bf16[4,256,256]{2,1,0:T(8,128)(2,1)} %copy-done.19), channel_id=1, source_target_pairs={{0,24},{8,16},{16,8},{24,0},{1,25},{9,17},{17,9},{25,1},{2,26},{10... | collective-permute-start | bytes 1572872 | tf_op jit(solution)/shard_map/ppermute | solution.py:38
  189.3 41.0 %collective-permute-start.15 = (bf16[1024,256]{1,0:T(8,128)(2,1)}, bf16[1024,256]{1,0:T(8,128)(2,1)S(1)}, u32[]{:S(2)}, u32[]{:S(2)}) collective-permute-start(bf16[1024,256]{1,0:T(8,128)(2,1)} %copy-done.18), channel_id=1, source_target_pairs={{0,8},{8,0},{1,9},{9,1},{2,10},{10,2},{3,11},{11,3},{4,12},{12,4},... | collective-permute-start | bytes 1572872 | tf_op jit(solution)/shard_map/ppermute | solution.py:38
  193.4 1.2 copy-start.17
  194.7 10.9 %copy-start.5 = (bf16[128,4096]{1,0:T(8,128)(2,1)S(1)}, bf16[128,4096]{1,0:T(8,128)(2,1)}, u32[]{:S(2)}) copy-start(bf16[128,4096]{1,0:T(8,128)(2,1)} %copy-done.4) | copy-start | bytes 3145732
  194.7 10.9 %copy-start.7 = (bf16[128,4096]{1,0:T(8,128)(2,1)S(1)}, bf16[128,4096]{1,0:T(8,128)(2,1)}, u32[]{:S(2)}) copy-start(bf16[128,4096]{1,0:T(8,128)(2,1)} %copy-done.6) | copy-start | bytes 3145732
  204.6 37.4 %collective-permute-start.36 = (bf16[256,256]{1,0:T(8,128)(2,1)S(1)}, bf16[256,256]{1,0:T(8,128)(2,1)S(1)}, u32[]{:S(2)}, u32[]{:S(2)}) collective-permute-start(bf16[256,256]{1,0:T(8,128)(2,1)S(1)} %get-tuple-element.72), channel_id=1, source_target_pairs={{0,8},{8,0},{1,9},{9,1},{2,10},{10,2},{3,11},{11,3},{4,12},{12,4},... | collective-permute-start | bytes 393224 | tf_op jit(solution)/shard_map/ppermute | solution.py:38
  205.6 24.5 %copy-start.12 = (bf16[4,256,256]{2,1,0:T(8,128)(2,1)S(1)}, bf16[4,256,256]{2,1,0:T(8,128)(2,1)}, u32[]{:S(2)}) copy-start(bf16[4,256,256]{2,1,0:T(8,128)(2,1)} %copy-done.11) | copy-start | bytes 1572868
  220.2 10.1 %copy-start.10 = (bf16[1024,256]{1,0:T(8,128)(2,1)S(1)}, bf16[1024,256]{1,0:T(8,128)(2,1)}, u32[]{:S(2)}) copy-start(bf16[1024,256]{1,0:T(8,128)(2,1)} %copy-done.9) | copy-start | bytes 1572868
  220.9 23.6 %collective-permute-start.37 = (bf16[256,256]{1,0:T(8,128)(2,1)S(1)}, bf16[256,256]{1,0:T(8,128)(2,1)S(1)}, u32[]{:S(2)}, u32[]{:S(2)}) collective-permute-start(bf16[256,256]{1,0:T(8,128)(2,1)S(1)} %get-tuple-element.74), channel_id=1, source_target_pairs={{0,16},{16,0},{1,17},{17,1},{2,18},{18,2},{3,19},{19,3},{4,20},{20... | collective-permute-start | bytes 393224 | tf_op jit(solution)/shard_map/ppermute | solution.py:38
  221.8 9.8 %collective-permute-start.19 = (f32[64,8,128]{2,1,0:T(8,128)S(1)}, f32[64,8,128]{2,1,0:T(8,128)S(1)}, u32[]{:S(2)}, u32[]{:S(2)}) collective-permute-start(f32[64,8,128]{2,1,0:T(8,128)S(1)} %slice.111), channel_id=1, source_target_pairs={{0,1},{1,0},{2,3},{3,2},{4,5},{5,4},{6,7},{7,6},{8,9},{9,8},{10,11... | collective-permute-start | bytes 786440 | tf_op jit(solution)/shard_map/ppermute | solution.py:38
  231.6 33.1 %copy-start.2 = (bf16[2,128,4096]{2,1,0:T(8,128)(2,1)S(1)}, bf16[2,128,4096]{2,1,0:T(8,128)(2,1)}, u32[]{:S(2)}) copy-start(bf16[2,128,4096]{2,1,0:T(8,128)(2,1)} %get-tuple-element.46.other_ref) | copy-start | bytes 6291460
  231.7 5.4 %collective-permute-start.20 = (f32[16,8,128]{2,1,0:T(8,128)S(1)}, f32[16,8,128]{2,1,0:T(8,128)S(1)}, u32[]{:S(2)}, u32[]{:S(2)}) collective-permute-start(f32[16,8,128]{2,1,0:T(8,128)S(1)} %get-tuple-element.78), channel_id=1, source_target_pairs={{0,2},{2,4},{4,6},{6,0},{1,3},{3,5},{5,7},{7,1},{8,10},{10,12},{12... | collective-permute-start | bytes 196616 | tf_op jit(solution)/shard_map/ppermute | solution.py:38
  231.7 7.2 %collective-permute-start.21 = (f32[16,8,128]{2,1,0:T(8,128)S(1)}, f32[16,8,128]{2,1,0:T(8,128)S(1)}, u32[]{:S(2)}, u32[]{:S(2)}) collective-permute-start(f32[16,8,128]{2,1,0:T(8,128)S(1)} %get-tuple-element.80), channel_id=1, source_target_pairs={{0,4},{2,6},{4,0},{6,2},{1,5},{3,7},{5,1},{7,3},{8,12},{10,14},{12... | collective-permute-start | bytes 196616 | tf_op jit(solution)/shard_map/ppermute | solution.py:38
  233.1 8.4 %collective-permute-start.22 = (f32[16,8,128]{2,1,0:T(8,128)S(1)}, f32[16,8,128]{2,1,0:T(8,128)S(1)}, u32[]{:S(2)}, u32[]{:S(2)}) collective-permute-start(f32[16,8,128]{2,1,0:T(8,128)S(1)} %get-tuple-element.79), channel_id=1, source_target_pairs={{0,6},{2,0},{4,2},{6,4},{1,7},{3,1},{5,3},{7,5},{8,14},{10,8},{12,... | collective-permute-start | bytes 196616 | tf_op jit(solution)/shard_map/ppermute | solution.py:38
  237.1 7.5 %collective-permute-start.38 = (bf16[256,256]{1,0:T(8,128)(2,1)S(1)}, bf16[256,256]{1,0:T(8,128)(2,1)S(1)}, u32[]{:S(2)}, u32[]{:S(2)}) collective-permute-start(bf16[256,256]{1,0:T(8,128)(2,1)S(1)} %get-tuple-element.73), channel_id=1, source_target_pairs={{0,24},{8,16},{16,8},{24,0},{1,25},{9,17},{17,9},{25,1},{2,26},{10... | collective-permute-start | bytes 393224 | tf_op jit(solution)/shard_map/ppermute | solution.py:38
  239.0 12.2 %collective-permute-start.42 = (bf16[256,256]{1,0:T(8,128)(2,1)S(1)}, bf16[256,256]{1,0:T(8,128)(2,1)S(1)}, u32[]{:S(2)}, u32[]{:S(2)}) collective-permute-start(bf16[256,256]{1,0:T(8,128)(2,1)S(1)} %get-tuple-element.75), channel_id=1, source_target_pairs={{0,96},{32,0},{64,32},{96,64},{1,97},{33,1},{65,33},{97,65},{2,98}... | collective-permute-start | bytes 393224 | tf_op jit(solution)/shard_map/ppermute | solution.py:38
  241.5 11.4 %collective-permute-start.43 = (bf16[256,256]{1,0:T(8,128)(2,1)S(1)}, bf16[256,256]{1,0:T(8,128)(2,1)S(1)}, u32[]{:S(2)}, u32[]{:S(2)}) collective-permute-start(bf16[256,256]{1,0:T(8,128)(2,1)S(1)} %get-tuple-element.77), channel_id=1, source_target_pairs={{0,64},{32,96},{64,0},{96,32},{1,65},{33,97},{65,1},{97,33},{2,66}... | collective-permute-start | bytes 393224 | tf_op jit(solution)/shard_map/ppermute | solution.py:38
  242.0 5.5 %collective-permute-start.23 = (f32[16,8,128]{2,1,0:T(8,128)S(1)}, f32[16,8,128]{2,1,0:T(8,128)S(1)}, u32[]{:S(2)}, u32[]{:S(2)}) collective-permute-start(f32[16,8,128]{2,1,0:T(8,128)S(1)} %fusion.5), channel_id=1, source_target_pairs={{0,64},{32,96},{64,0},{96,32},{1,65},{33,97},{65,1},{97,33},{2,66}... | collective-permute-start | bytes 196616 | tf_op jit(solution)/shard_map/ppermute | solution.py:38
  244.5 4.3 %collective-permute-start.24 = (f32[16,8,128]{2,1,0:T(8,128)S(1)}, f32[16,8,128]{2,1,0:T(8,128)S(1)}, u32[]{:S(2)}, u32[]{:S(2)}) collective-permute-start(f32[16,8,128]{2,1,0:T(8,128)S(1)} %fusion.5), channel_id=1, source_target_pairs={{0,32},{32,64},{64,96},{96,0},{1,33},{33,65},{65,97},{97,1},{2,34}... | collective-permute-start | bytes 196616 | tf_op jit(solution)/shard_map/ppermute | solution.py:38
  244.5 4.3 %collective-permute-start.25 = (f32[16,8,128]{2,1,0:T(8,128)S(1)}, f32[16,8,128]{2,1,0:T(8,128)S(1)}, u32[]{:S(2)}, u32[]{:S(2)}) collective-permute-start(f32[16,8,128]{2,1,0:T(8,128)S(1)} %fusion.5), channel_id=1, source_target_pairs={{0,96},{32,0},{64,32},{96,64},{1,97},{33,1},{65,33},{97,65},{2,98}... | collective-permute-start | bytes 196616 | tf_op jit(solution)/shard_map/ppermute | solution.py:38
  247.3 26.6 %copy-start.1 = (f32[7,12288]{1,0:T(8,128)S(1)}, f32[7,12288]{1,0:T(8,128)}, u32[]{:S(2)}) copy-start(f32[7,12288]{1,0:T(8,128)} %filter_ref.1) | copy-start | bytes 1032196
  247.5 5.4 %collective-permute-start.44 = (bf16[256,256]{1,0:T(8,128)(2,1)S(1)}, bf16[256,256]{1,0:T(8,128)(2,1)S(1)}, u32[]{:S(2)}, u32[]{:S(2)}) collective-permute-start(bf16[256,256]{1,0:T(8,128)(2,1)S(1)} %get-tuple-element.76), channel_id=1, source_target_pairs={{0,32},{32,64},{64,96},{96,0},{1,33},{33,65},{65,97},{97,1},{2,34}... | collective-permute-start | bytes 393224 | tf_op jit(solution)/shard_map/ppermute | solution.py:38
  248.9 18.4 %collective-permute-start.26 = (f32[16,8,128]{2,1,0:T(8,128)S(1)}, f32[16,8,128]{2,1,0:T(8,128)S(1)}, u32[]{:S(2)}, u32[]{:S(2)}) collective-permute-start(f32[16,8,128]{2,1,0:T(8,128)S(1)} %add_add_fusion.1), channel_id=1, source_target_pairs={{0,16},{16,0},{1,17},{17,1},{2,18},{18,2},{3,19},{19,3},{4,20},{20... | collective-permute-start | bytes 196616 | tf_op jit(solution)/shard_map/ppermute | solution.py:38
  250.2 17.2 %collective-permute-start.27 = (f32[16,8,128]{2,1,0:T(8,128)S(1)}, f32[16,8,128]{2,1,0:T(8,128)S(1)}, u32[]{:S(2)}, u32[]{:S(2)}) collective-permute-start(f32[16,8,128]{2,1,0:T(8,128)S(1)} %add_add_fusion.1), channel_id=1, source_target_pairs={{0,8},{8,0},{1,9},{9,1},{2,10},{10,2},{3,11},{11,3},{4,12},{12,4},... | collective-permute-start | bytes 196616 | tf_op jit(solution)/shard_map/ppermute | solution.py:38
  251.2 16.1 %collective-permute-start.28 = (f32[16,8,128]{2,1,0:T(8,128)S(1)}, f32[16,8,128]{2,1,0:T(8,128)S(1)}, u32[]{:S(2)}, u32[]{:S(2)}) collective-permute-start(f32[16,8,128]{2,1,0:T(8,128)S(1)} %add_add_fusion.1), channel_id=1, source_target_pairs={{0,24},{8,16},{16,8},{24,0},{1,25},{9,17},{17,9},{25,1},{2,26},{10... | collective-permute-start | bytes 196616 | tf_op jit(solution)/shard_map/ppermute | solution.py:38
  253.5 20.3 %collective-permute-start.17 = (bf16[8,4096]{1,0:T(8,128)(2,1)}, bf16[8,4096]{1,0:T(8,128)(2,1)}, u32[]{:S(2)}, u32[]{:S(2)}) collective-permute-start(bf16[8,4096]{1,0:T(8,128)(2,1)} %slice.89), channel_id=1, source_target_pairs={{1,0},{2,1},{3,2},{4,3},{5,4},{6,5},{7,6},{8,7},{9,8},{10,9},{11,1... | collective-permute-start | bytes 196616 | tf_op jit(solution)/shard_map/ppermute | solution.py:26
  265.4 8.5 %collective-permute-start.18 = (bf16[2,8,4096]{2,1,0:T(8,128)(2,1)}, bf16[2,8,4096]{2,1,0:T(8,128)(2,1)}, u32[]{:S(2)}, u32[]{:S(2)}) collective-permute-start(bf16[2,8,4096]{2,1,0:T(8,128)(2,1)} %slice.90), channel_id=1, source_target_pairs={{1,0},{2,1},{3,2},{4,3},{5,4},{6,5},{7,6},{8,7},{9,8},{10,9},{11,1... | collective-permute-start | bytes 393224 | tf_op jit(solution)/shard_map/ppermute | solution.py:26
  268.0 15.7 %collective-permute-start.29 = (f32[16,8,128]{2,1,0:T(8,128)}, f32[16,8,128]{2,1,0:T(8,128)}, u32[]{:S(2)}, u32[]{:S(2)}) collective-permute-start(f32[16,8,128]{2,1,0:T(8,128)} %get-tuple-element.67), channel_id=1, source_target_pairs={{0,6},{2,0},{4,2},{6,4},{1,7},{3,1},{5,3},{7,5},{8,14},{10,8},{12,... | collective-permute-start | bytes 196616 | tf_op jit(solution)/shard_map/ppermute | solution.py:38
  270.4 13.3 %collective-permute-start.30 = (f32[16,8,128]{2,1,0:T(8,128)}, f32[16,8,128]{2,1,0:T(8,128)}, u32[]{:S(2)}, u32[]{:S(2)}) collective-permute-start(f32[16,8,128]{2,1,0:T(8,128)} %get-tuple-element.67), channel_id=1, source_target_pairs={{0,4},{2,6},{4,0},{6,2},{1,5},{3,7},{5,1},{7,3},{8,12},{10,14},{12... | collective-permute-start | bytes 196616 | tf_op jit(solution)/shard_map/ppermute | solution.py:38
  270.4 13.3 %collective-permute-start.31 = (f32[16,8,128]{2,1,0:T(8,128)}, f32[16,8,128]{2,1,0:T(8,128)}, u32[]{:S(2)}, u32[]{:S(2)}) collective-permute-start(f32[16,8,128]{2,1,0:T(8,128)} %get-tuple-element.67), channel_id=1, source_target_pairs={{0,2},{2,4},{4,6},{6,0},{1,3},{3,5},{5,7},{7,1},{8,10},{10,12},{12... | collective-permute-start | bytes 196616 | tf_op jit(solution)/shard_map/ppermute | solution.py:38
  273.9 12.1 %copy-start.8 = (f32[128,8,128]{2,1,0:T(8,128)S(1)}, f32[128,8,128]{2,1,0:T(8,128)}, u32[]{:S(2)}) copy-start(f32[128,8,128]{2,1,0:T(8,128)} %get-tuple-element.66) | copy-start | bytes 1572868
  284.7 3.8 %collective-permute-start.32 = (f32[64,8,128]{2,1,0:T(8,128)S(1)}, f32[64,8,128]{2,1,0:T(8,128)S(1)}, u32[]{:S(2)}, u32[]{:S(2)}) collective-permute-start(f32[64,8,128]{2,1,0:T(8,128)S(1)} %pad_maximum_fusion.3), channel_id=1, source_target_pairs={{0,1},{1,0},{2,3},{3,2},{4,5},{5,4},{6,7},{7,6},{8,9},{9,8},{10,11... | collective-permute-start | bytes 786440 | tf_op jit(solution)/shard_map/ppermute | solution.py:38
  (14 other events, 12.2 us)
Sparse Core Ops, SparseCore 0:
  58.0 64.4 all-gather.1
  124.9 51.5 reduce-scatter.1

commit v3 on v2

--- a/solution.py
+++ b/solution.py
@@ -11,7 +11,7 @@
 
 LANES = 128
 RIM = 8
-VMEM = 48 * 1024 * 1024
+MIB = 1024 * 1024
 F32 = jnp.float32
 BF16 = jnp.bfloat16
 
@@ -48,8 +48,8 @@
 FLIPS = [(0, 0), (0, 1), (1, 0), (1, 1)]
 
 
-def params():
-    return pltpu.CompilerParams(vmem_limit_bytes=VMEM)
+def params(mib=16):
+    return pltpu.CompilerParams(vmem_limit_bytes=mib * MIB)
 
 
 def cost(flops, moved):
@@ -103,7 +103,7 @@
         out_specs=[pl.BlockSpec((rows, width), lambda i: (0, i))] * 4,
         out_shape=[out] * 4,
         compiler_params=params(),
-        cost_estimate=cost(2 * taps * rows * wide, 10 * rows * wide),
+        cost_estimate=cost(0, rows * wide),
         name="features",
     )(tokens, tokens, tokens, rim, rim, rim, filters, filters, filters)
 
@@ -164,7 +164,7 @@
         ),
         out_shape=[out, out],
         compiler_params=params(),
-        cost_estimate=cost(2 * groups * rows * 2 * rows * LANES, 10 * rows * channels),
+        cost_estimate=cost(0, 2 * rows * channels),
         name="mix",
     )(place, lines, prev, cur, query)
 
@@ -308,53 +308,39 @@
     )(lines, grad, grad_next, key, value, tokens, tokens, rim, rim)
 
 
-def short_adjoint_kernel(short_taps, query_ref, other_ref, query_rim_ref, other_rim_ref, filter_ref, out_ref):
+def short_adjoint_kernel(short_taps, grads_ref, rim_ref, filter_ref, *refs):
+    out_ref = refs[-1]
     rows = out_ref.shape[0]
-
-    def filtered(grads, rim):
-        ext = jnp.concatenate([grads.astype(F32), rim.astype(F32)], axis=0)
-        total = filter_ref[0:1, :] * ext[0:rows]
-        for tap in range(1, short_taps):
-            total = total + filter_ref[tap : tap + 1, :] * ext[tap : tap + rows]
-        out_ref[...] = total.astype(BF16)
-
-    @pl.when(pl.program_id(0) == 0)
-    def _():
-        filtered(query_ref[...], query_rim_ref[...])
-
-    @pl.when(pl.program_id(0) > 0)
-    def _():
-        filtered(other_ref[0], other_rim_ref[0])
-
-
-def short_adjoint_call(query, other, query_rim, other_rim, filters):
-    rows, channels = query.shape
+    ext = jnp.concatenate([grads_ref[0].astype(F32), rim_ref[0].astype(F32)], axis=0)
+    total = filter_ref[0:1, :] * ext[0:rows]
+    for tap in range(1, short_taps):
+        total = total + filter_ref[tap : tap + 1, :] * ext[tap : tap + rows]
+    out_ref[...] = total.astype(BF16)
+
+
+def short_adjoint_call(grads, rim, filters, first, out):
+    parts, rows, channels = grads.shape
     short_taps = filters.shape[0]
     width = block_width(channels, 1024)
     steps = channels // width
-
-    def first(p, i):
-        return jnp.where(p == 0, i, steps - 1)
-
-    def rest(p, i):
-        return jnp.where(p == 0, 0, i)
-
+    result = pl.BlockSpec((rows, width), lambda p, i: (0, (p + first) * steps + i))
+    given = [] if out is None else [out]
     return pl.pallas_call(
         functools.partial(short_adjoint_kernel, short_taps),
-        grid=(3, steps),
+        grid=(parts, steps),
         in_specs=[
-            pl.BlockSpec((rows, width), lambda p, i: (0, first(p, i))),
-            pl.BlockSpec((1, rows, width), lambda p, i: (jnp.maximum(p - 1, 0), 0, rest(p, i))),
-            pl.BlockSpec((RIM, width), lambda p, i: (0, first(p, i))),
-            pl.BlockSpec((1, RIM, width), lambda p, i: (jnp.maximum(p - 1, 0), 0, rest(p, i))),
-            pl.BlockSpec((short_taps, width), lambda p, i: (0, p * steps + i)),
-        ],
-        out_specs=pl.BlockSpec((rows, width), lambda p, i: (0, p * steps + i)),
+            pl.BlockSpec((1, rows, width), lambda p, i: (p, 0, i)),
+            pl.BlockSpec((1, RIM, width), lambda p, i: (p, 0, i)),
+            pl.BlockSpec((short_taps, width), lambda p, i: (0, (p + first) * steps + i)),
+        ]
+        + [pl.BlockSpec(memory_space=pl.ANY)] * len(given),
+        out_specs=result,
         out_shape=jax.ShapeDtypeStruct((rows, 3 * channels), BF16),
-        compiler_params=params(),
-        cost_estimate=cost(6 * short_taps * rows * channels, 12 * rows * channels),
+        input_output_aliases={3: 0} if given else {},
+        compiler_params=params(),
+        cost_estimate=cost(2 * parts * short_taps * rows * channels, 4 * parts * rows * channels),
         name="short_adjoint",
-    )(query, other, query_rim, other_rim, filters)
+    )(grads, rim, filters, *given)
 
 
 def spread_kernel(place, query_ref, key_ref, value_ref, long_ref, out_ref):
@@ -474,21 +460,32 @@
         in_specs=[pl.BlockSpec((height, depth), lambda i: (i, 0))] + [whole(x) for x in (*tops, *bottoms)],
         out_specs=pl.BlockSpec((height, channels), lambda i: (i, 0)),
         out_shape=jax.ShapeDtypeStruct((rows, channels), BF16),
-        compiler_params=params(),
+        compiler_params=params(32),
         cost_estimate=cost(2 * rows * depth * channels, 2 * (rows + depth) * channels),
         name="gate_matmul",
     )(cotangents, *tops, *bottoms)
 
 
-def project_kernel(ny, *refs):
-    rows_ref, turned_ref, tops, bottoms = refs[0], refs[1], refs[2 : 2 + ny], refs[2 + ny : 6 + ny]
+def project_kernel(ny, count, place, *refs):
+    pieces, refs = refs[:count], refs[count - 1 :]
+    turned_ref, tops, bottoms = refs[1], refs[2 : 2 + ny], refs[2 + ny : 6 + ny]
     own_ref, other_ref = refs[6 + ny : 8 + ny]
     top_grads, bottom_grads = refs[8 + ny : 8 + 2 * ny], refs[8 + 2 * ny : 12 + 2 * ny]
-    total = refs[12 + 2 * ny]
+    total, turned = refs[12 + 2 * ny :]
     step = pl.program_id(0)
+    height = pieces[0].shape[0]
+    blocks = total.shape[0] // height
+
+    @pl.when(step == 0)
+    def _():
+        for j in range(blocks):
+            at = pl.multiple_of(place[j] * height, height)
+            turned[:, j * height : (j + 1) * height] = turned_ref[:, pl.ds(at, height)]
+
+    rows = jnp.concatenate([p[...] for p in pieces], axis=0)
     width = own_ref.shape[1]
     size = tops[0].shape[1]
-    grads = jnp.dot(turned_ref[...], rows_ref[...], preferred_element_type=F32).astype(BF16)
+    grads = jnp.dot(turned[...], rows, preferred_element_type=F32).astype(BF16)
     for a in range(2):
         for b in range(2):
             at = (2 * a + 1) * size
@@ -502,7 +499,7 @@
                     at = 2 * a * size
                     top_grads[d][2 * a + b] = grads[b * width : (b + 1) * width, at : at + size]
             right = jnp.concatenate(piece_rows(tops, bottoms, d), axis=0)
-            product = jnp.dot(rows_ref[...], right, preferred_element_type=F32)
+            product = jnp.dot(rows, right, preferred_element_type=F32)
             if d == 0:
                 total[...] = product
             else:
@@ -510,12 +507,23 @@
 
     @pl.when(step == ny - 1)
     def _():
-        own_ref[...] = total[:, :width].astype(BF16)
-        other_ref[...] = total[:, width:].astype(BF16)
-
-
-def project(all_rows, turned, tops, bottoms):
-    rows, channels = all_rows.shape
+        for j in range(blocks):
+            at = pl.ds(pl.multiple_of(place[j] * height, height), height)
+            own_ref[at, :] = total[j * height : (j + 1) * height, :width].astype(BF16)
+            other_ref[at, :] = total[j * height : (j + 1) * height, width:].astype(BF16)
+
+
+def line_gather(x):
+    half = x.shape[0] // 2
+    before, after = move(x, z=1), move(x, z=-1)
+    far = [move(before[:half], z=1), move(after[half:], z=-1)]
+    pieces = [x, before, after, *far]
+    return pieces + [move(p, c=1) for p in pieces]
+
+
+def project(place, pieces, turned, tops, bottoms):
+    rows = sum(p.shape[0] for p in pieces)
+    channels = pieces[0].shape[1]
     ny = len(tops)
     size = tops[0].shape[1]
     width = turned.shape[0] // 2
@@ -526,17 +534,21 @@
         + [jax.ShapeDtypeStruct((ny, width, size), BF16)] * 4
     )
     results = pl.pallas_call(
-        functools.partial(project_kernel, ny),
-        grid=(ny,),
-        in_specs=[pl.BlockSpec((rows, channels // ny), lambda i: (0, i)), whole(turned)]
-        + [whole(x) for x in (*tops, *bottoms)],
-        out_specs=[whole(x) for x in outs],
+        functools.partial(project_kernel, ny, len(pieces)),
+        grid_spec=pltpu.PrefetchScalarGridSpec(
+            num_scalar_prefetch=1,
+            grid=(ny,),
+            in_specs=[pl.BlockSpec((p.shape[0], channels // ny), lambda i, place: (0, i)) for p in pieces]
+            + [whole(turned)]
+            + [whole(x) for x in (*tops, *bottoms)],
+            out_specs=[whole(x) for x in outs],
+            scratch_shapes=[pltpu.VMEM((rows, 2 * width), F32), pltpu.VMEM(turned.shape, BF16)],
+        ),
         out_shape=outs,
-        scratch_shapes=[pltpu.VMEM((rows, 2 * width), F32)],
-        compiler_params=params(),
+        compiler_params=params(40),
         cost_estimate=cost(8 * rows * width * channels, 2 * (rows + 4 * width) * channels),
         name="project",
-    )(all_rows, turned, *tops, *bottoms)
+    )(place, *pieces, turned, *tops, *bottoms)
     return results[0], results[1], results[2 : 2 + ny], results[2 + ny :]
 
 
@@ -574,31 +586,36 @@
 
     block = jnp.arange(2 * ny, dtype=jnp.int32)
     place = ((y - block // 2) % ny) * 2 + (block + xl) % 2
+    step = jnp.arange(2 * nz, dtype=jnp.int32)
+    near = jnp.array([0, -1, 1, 2], jnp.int32)[step % nz]
+    row_place = (z + near) % nz * 2 + (step // nz + c) % 2
     size = 3 * channels // LANES + groups // 8
     each = size // (2 * nz)
     tile = jnp.arange(size, dtype=jnp.int32)
     places = ((tile // (nz * each) + c) % 2 * nz + (tile // each - z) % nz) * each + tile % each
 
+    rim = along(tokens[rows - RIM :], 1)
+    rim, out_weight = lax.optimization_barrier((rim, out_weight))
     wide_top, tall_bottom = gather_near(out_weight)
     mine = lax.dynamic_slice_in_dim(upstream, xh * span, span, 0)
     others = move(lax.dynamic_slice_in_dim(upstream, (1 - xh) * span, span, 0), xh=1)
     cotangents = jnp.concatenate([mine, others], axis=1)
 
-    rim = along(tokens[rows - RIM :], 1)
     lines = long_filter.astype(F32)
     query, key, value, mixer = features_call(tokens, rim, short_filter)
+    mixer, wide_top, tall_bottom = lax.optimization_barrier((mixer, wide_top, tall_bottom))
+    tops, bottoms = gather_far(wide_top, tall_bottom)
     mixer_prev = along(mixer, 1)
-    mixer_prev, wide_top, tall_bottom = lax.optimization_barrier((mixer_prev, wide_top, tall_bottom))
-    tops, bottoms = gather_far(wide_top, tall_bottom)
     mixed, gated = mix_call(place, mirrored(lines), mixer_prev, mixer, query)
-
+    cotangents, gated = lax.optimization_barrier((cotangents, gated))
     partial = gate_matmul(cotangents, tops, bottoms)
     gate_grad = lax.psum_scatter(partial, ("z", "c"), scatter_dimension=0, tiled=True)
-    all_rows = lax.all_gather(gated, ("z", "c"), axis=0, tiled=True)
+    pieces = line_gather(gated)
 
     grad_mixed, query_grad = gate_call(place, gate_grad, query, mixed)
     grad_next = along(grad_mixed, -1)
     query_next = along(query_grad[:RIM], -1)
+    grad_tokens = short_adjoint_call(query_grad[None], query_next[None], short_filter, 0, None)
     long_sum, query_sum = long_grad_call(
         groups, short_taps, mixer_prev, mixer, grad_mixed, query_grad, tokens, rim
     )
@@ -607,9 +624,9 @@
     )
     other_next = along(other_grads[:, :RIM], -1)
     grad_short, grad_long = total_over_devices(places, query_sum, key_sum, value_sum, long_sum, short_taps)
-    grad_tokens = short_adjoint_call(query_grad, other_grads, query_next, other_next, short_filter)
-
-    own, other, top_grads, bottom_grads = project(all_rows, cotangents.T, tops, bottoms)
+    grad_tokens = short_adjoint_call(other_grads, other_next, short_filter, 1, grad_tokens)
+
+    own, other, top_grads, bottom_grads = project(row_place, pieces, cotangents.T, tops, bottoms)
     grad_weight = plane_scatter_sum(top_grads, bottom_grads)
     theirs = move(other, xh=1)
     output = jnp.where(xh == 0, jnp.concatenate([own, theirs], axis=0), jnp.concatenate([theirs, own], axis=0))

time: 300 us -> 307 us (1.023)
  starting transfers between devices: 85.9 us -> 97.7 us
  local copies, waits for them, and re-layouts: 26.6 us -> 33.8 us
  waiting for transfers between devices: 79.7 us -> 73.1 us
    ppermute x40 -> x49, waiting for transfers between devices: 30.3 us -> 70.5 us  [move(): return lax.ppermute(x, axes, pairs)]
    reduce_scatter x1, waiting for transfers between devices: 32 us -> 0.01 us  [shards(): lax.psum_scatter(partial, ('z', 'c'), scatter_dimension=0, tiled=True)]
    ppermute x40 -> x49, starting transfers between devices: 60.1 us -> 75.9 us  [move(): return lax.ppermute(x, axes, pairs)]
    all_gather x1 -> x0, waiting for transfers between devices: 14.8 us -> none  [shards(): all_rows = lax.all_gather(gated, ('z', 'c'), axis=0, tiled=True)]
    ppermute x5, starting transfers between devices: 25.7 us -> 21.8 us  [along(): return lax.ppermute(x, LINE, pairs)]
    unnamed x66 -> x78, local copies, waits for them, and re-layouts: 19.5 us -> 22.9 us
    pallas_call x1 -> x2, Pallas kernels: 9.81 us -> 9.04 us  [short_adjoint_call(): pl.pallas_call(functools.partial(short_adjoint_kernel, short_taps), grid=...]
  transfers between devices with their start and end apart: 47 -> 55, of which waited for: 14 -> 16; matrix products, arithmetic and copies ran while one was open for 7% -> 5% of each run, Pallas kernels for 20% -> 23%
where the time goes in v3:
time: 307 us; the launch traced here: 306 us
  starting transfers between devices  97.7 us (32%)
  Pallas kernels  78.2 us (25%)
  waiting for transfers between devices  73.1 us (24%)
  local copies, waits for them, and re-layouts  33.8 us (11%)
  between operations  14.6 us (5%)
  other arithmetic  8.51 us (3%)
    ppermute x49, starting transfers between devices, move(): return lax.ppermute(x, axes, pairs)  75.9 us
    ppermute x49, waiting for transfers between devices, move(): return lax.ppermute(x, axes, pairs)  70.5 us
    unnamed x78, local copies, waits for them, and re-layouts  22.9 us
    ppermute x5, starting transfers between devices, along(): return lax.ppermute(x, LINE, pairs)  21.8 us
    pallas_call x1, Pallas kernels, project(): pl.pallas_call(functools.partial(project_kernel, ny, len(pieces)), grid_s...  15.8 us
    pallas_call x1, Pallas kernels, unmix_call(): pl.pallas_call(functools.partial(unmix_kernel, per_group, short_taps), gr...  13.9 us
    pallas_call x1, Pallas kernels, long_grad_call(): pl.pallas_call(functools.partial(long_grad_kernel, per_group, short_taps)...  10 us
    pallas_call x1, Pallas kernels, mix_call(): pl.pallas_call(functools.partial(mix_kernel, per_group), grid_spec=pltpu....  9.37 us
  transfers between devices with their start and end apart: 55, of which 16 were waited for; matrix products, arithmetic and copies ran while one was open for 5% of the time, Pallas kernels for 23%

profile of v3, /device:TPU:1, one launch (start us, length us, event | category | flops | bytes accessed | tf_op | source)
XLA Modules:
  0.0 306.0 jit_solution(2950020929110309020)
XLA Ops:
  8.2 4.9 %collective-permute-start.1 = (bf16[8,12288]{1,0:T(8,128)(2,1)S(1)}, bf16[8,12288]{1,0:T(8,128)(2,1)S(1)}, u32[]{:S(2)}, u32[]{:S(2)}) collective-permute-start(bf16[8,12288]{1,0:T(8,128)(2,1)S(1)} %slice_bitcast_fusion), channel_id=1, source_target_pairs={{0,1},{1,2},{2,3},{3,4},{4,5},{5,6},{6,7},{7,8},{8,9},{9,10},{10,1... | collective-permute-start | bytes 589832 | tf_op jit(solution)/shard_map/ppermute | solution.py:26
  13.1 2.6 collective-permute-done.1.refs_3_.refs_4_.refs_5_.key_rim_ref.value_rim_ref.rim_ref
  16.7 2.8 collective-permute-start.2
  20.4 1.3 collective-permute-start.5
  21.7 2.6 collective-permute-start.6
  24.3 1.1 collective-permute-start.7
  25.4 1.9 copy-done
  28.3 7.6 %features.1 = (bf16[128,4096]{1,0:T(8,128)(2,1)S(1)}, bf16[128,4096]{1,0:T(8,128)(2,1)S(1)}, bf16[128,4096]{1,0:T(8,128)(2,1)S(1)}, bf16[128,4096]{1,0:T(8,128)(2,1)S(1)}) custom-call(bf16[128,12288]{1,0:T(8,128)(2,1)S(1)} %bitcast.50, bf16[128,12288]{1,0:T(8,128)(2,1)S(1)} %bitcast.51, bf16[128,12288]{1,0:T(8,128)(2,1)S(1)} %bitcast.52, ...), custom_call_target="tpu_custom_call" | custom-call | bytes 1572864 | tf_op jit(solution)/shard_map/features/pallas_call | solution.py:97
  38.6 6.4 %collective-permute-start.8 = (bf16[128,4096]{1,0:T(8,128)(2,1)S(1)}, bf16[128,4096]{1,0:T(8,128)(2,1)S(1)}, u32[]{:S(2)}, u32[]{:S(2)}) collective-permute-start(bf16[128,4096]{1,0:T(8,128)(2,1)S(1)} %get-tuple-element.40.cur_ref), channel_id=1, source_target_pairs={{0,1},{1,2},{2,3},{3,4},{4,5},{5,6},{6,7},{7,8},{8,9},{9,10},{10,1... | collective-permute-start | bytes 3145736 | tf_op jit(solution)/shard_map/ppermute | solution.py:26
  45.0 2.1 dynamic-slice_bitcast_fusion.1
  47.1 3.0 collective-permute-start
  50.1 1.6 collective-permute-start.19
  52.8 8.4 %collective-permute-done = bf16[1024,256]{1,0:T(8,128)(2,1)S(1)} collective-permute-done((bf16[1024,256]{1,0:T(8,128)(2,1)S(1)}, bf16[1024,256]{1,0:T(8,128)(2,1)S(1)}, u32[]{:S(2)}, u32[]{:S(2)}) %collective-permute-start) | collective-permute-done | bytes 524320 | tf_op jit(solution)/shard_map/ppermute | solution.py:38
  61.2 2.7 collective-permute-start.21
  65.3 12.7 %collective-permute-start.23 = (bf16[4,256,256]{2,1,0:T(8,128)(2,1)}, bf16[4,256,256]{2,1,0:T(8,128)(2,1)}, u32[]{:S(2)}, u32[]{:S(2)}) collective-permute-start(bf16[4,256,256]{2,1,0:T(8,128)(2,1)} %pad_maximum_fusion.2.refs_15_.refs_5_), channel_id=1, source_target_pairs={{0,24},{8,16},{16,8},{24,0},{1,25},{9,17},{17,9},{25,1},{2,26},{10... | collective-permute-start | bytes 1572872 | tf_op jit(solution)/shard_map/ppermute | solution.py:38
  78.8 1.6 slice.90
  81.5 1.4 pad_maximum_fusion.refs_0_
  83.0 9.4 %mix.1 = (bf16[128,4096]{1,0:T(8,128)(2,1)S(1)}, bf16[128,4096]{1,0:T(8,128)(2,1)}) custom-call(s32[8]{0:T(128)S(1)} %fusion.8.place, f32[256,128]{1,0:T(8,128)S(1)} %pad_maximum_fusion.4.lines_ref, bf16[128,4096]{1,0:T(8,128)(2,1)S(1)} %copy-done.13, bf16[128,4096]{1,0:T(8,128)(2,1)S(1)} %get-tuple-element.40.cur_ref, ...), custom_call_target="tpu_custom_call" | custom-call | bytes 1048576 | tf_op jit(solution)/shard_map/mix/pallas_call | solution.py:156
  93.4 6.8 %gate_matmul.1 = bf16[1024,4096]{1,0:T(8,128)(2,1)S(1)} custom-call(bf16[1024,512]{1,0:T(8,128)(2,1)S(1)} %pad_maximum_fusion.refs_0_, bf16[4,256,256]{2,1,0:T(8,128)(2,1)} %pad_maximum_fusion.1.refs_11_.refs_1_, bf16[4,256,256]{2,1,0:T(8,128)(2,1)S(1)} %copy-done.28, bf16[4,256,256]{2,1,0:T(8,128)(2,1)} %collective-permute-done.19.refs_13_.refs_3_, ...), custom_call_target="tpu_custom_call" | custom-call | flops 4294967296 | bytes 12582912 | tf_op jit(solution)/shard_map/gate_matmul/pallas_call | solution.py:457
  100.2 3.3 %copy-done.4 = bf16[1024,4096]{1,0:T(8,128)(2,1)} copy-done((bf16[1024,4096]{1,0:T(8,128)(2,1)}, bf16[1024,4096]{1,0:T(8,128)(2,1)S(1)}, u32[]{:S(2)}) %copy-start.4) | copy-done | bytes 8388632
  103.6 1.6 collective-permute-start.9
  105.2 5.7 %collective-permute-start.10 = (bf16[128,4096]{1,0:T(8,128)(2,1)}, bf16[128,4096]{1,0:T(8,128)(2,1)}, u32[]{:S(2)}, u32[]{:S(2)}) collective-permute-start(bf16[128,4096]{1,0:T(8,128)(2,1)} %get-tuple-element.43.refs_0_), channel_id=1, source_target_pairs={{0,6},{2,0},{4,2},{6,4},{1,7},{3,1},{5,3},{7,5},{8,14},{10,8},{12,... | collective-permute-start | bytes 3145736 | tf_op jit(solution)/shard_map/ppermute | solution.py:38
  110.9 29.1 %collective-permute-done.9.refs_1_ = bf16[128,4096]{1,0:T(8,128)(2,1)} collective-permute-done((bf16[128,4096]{1,0:T(8,128)(2,1)}, bf16[128,4096]{1,0:T(8,128)(2,1)}, u32[]{:S(2)}, u32[]{:S(2)}) %collective-permute-start.9) | collective-permute-done | bytes 1048608 | tf_op jit(solution)/shard_map/ppermute | solution.py:38
  140.0 1.1 slice.120
  141.2 1.1 slice.121
  142.3 2.7 collective-permute-start.12
  145.6 14.7 %collective-permute-done.11.refs_3_ = bf16[64,4096]{1,0:T(8,128)(2,1)} collective-permute-done((bf16[64,4096]{1,0:T(8,128)(2,1)S(1)}, bf16[64,4096]{1,0:T(8,128)(2,1)}, u32[]{:S(2)}, u32[]{:S(2)}) %collective-permute-start.11) | collective-permute-done | bytes 524320 | tf_op jit(solution)/shard_map/ppermute | solution.py:38
  160.3 1.2 collective-permute-done.12.refs_4_
  162.1 1.3 copy.14.refs_10_
  163.7 1.2 copy-done.29
  164.9 15.8 %project.1 = (bf16[1024,256]{1,0:T(8,128)(2,1)S(1)}, bf16[1024,256]{1,0:T(8,128)(2,1)S(1)}, bf16[4,256,256]{2,1,0:T(8,128)(2,1)S(1)}, bf16[4,256,256]{2,1,0:T(8,...) custom-call(s32[8]{0:T(128)S(1)} %fusion.7.place, ...), custom_call_target="tpu_custom_call" | custom-call | flops 8589934592 | bytes 16777216 | tf_op jit(solution)/shard_map/project/pallas_call | solution.py:536
  186.3 1.5 collective-permute-start.44
  187.8 1.2 copy-done.17
  189.0 3.6 %gate_back.1 = (bf16[128,4096]{1,0:T(8,128)(2,1)}, bf16[128,4096]{1,0:T(8,128)(2,1)S(1)}) custom-call(s32[8]{0:T(128)S(1)} %fusion.8.place, bf16[128,4096]{1,0:T(8,128)(2,1)S(1)} %copy-done.17, bf16[128,4096]{1,0:T(8,128)(2,1)S(1)} %get-tuple-element.41.query_ref, bf16[128,4096]{1,0:T(8,128)(2,1)S(1)} %copy-done.16), custom_call_target="tpu_custom_call" | custom-call | flops 1048576 | bytes 5242880 | tf_op jit(solution)/shard_map/gate_back/pallas_call | solution.py:184
  193.6 3.0 collective-permute-start.25
  196.6 2.4 collective-permute-start.48
  201.4 2.0 collective-permute-start.50
  203.4 9.8 %collective-permute-done.44 = bf16[4,256,256]{2,1,0:T(8,128)(2,1)} collective-permute-done((bf16[4,256,256]{2,1,0:T(8,128)(2,1)}, bf16[4,256,256]{2,1,0:T(8,128)(2,1)}, u32[]{:S(2)}, u32[]{:S(2)}) %collective-permute-start.44) | collective-permute-done | bytes 524320 | tf_op jit(solution)/shard_map/ppermute | solution.py:38
  213.2 2.3 collective-permute-start.24
  215.5 1.8 add_convert_fusion.1
  217.4 1.2 copy-done.8
  218.6 1.2 copy-done.11
  219.8 1.2 copy-done.14
  221.0 10.0 %long_grad.1 = (f32[256,128]{1,0:T(8,128)S(1)}, f32[8,4096]{1,0:T(8,128)S(1)}) custom-call(bf16[128,4096]{1,0:T(8,128)(2,1)S(1)} %copy-done.14, bf16[128,4096]{1,0:T(8,128)(2,1)S(1)} %copy-done.11, bf16[128,4096]{1,0:T(8,128)(2,1)} %get-tuple-element.50.grad_ref, bf16[128,4096]{1,0:T(8,128)(2,1)S(1)} %copy-done.8, bf16[128,12288]{1,0:T(8,128)(2,1)S(1)} %bitcast.53, ...), custom_call_target="tpu_custom_call" | custom-call | flops 2147483648 | bytes 5242880 | tf_op jit(solution)/shard_map/long_grad/pallas_call | solution.py:241
  231.7 13.9 %unmix.1 = (bf16[2,128,4096]{2,1,0:T(8,128)(2,1)S(1)}, f32[8,4096]{1,0:T(8,128)S(1)}, f32[8,4096]{1,0:T(8,128)S(1)}) custom-call(f32[256,128]{1,0:T(8,128)S(1)} %convert_element_type.63.lines_ref, bf16[128,4096]{1,0:T(8,128)(2,1)} %get-tuple-element.50.grad_ref, bf16[128,4096]{1,0:T(8,128)(2,1)} %collective-permute-done.25.next_ref, ...), custom_call_target="tpu_custom_call" | custom-call | flops 2147483648 | bytes 8388608 | tf_op jit(solution)/shard_map/unmix/pallas_call | solution.py:296
  247.3 1.3 collective-permute-start.28
  248.9 1.3 maximum_select_fusion
  251.0 3.2 %collective-permute-start.30 = (f32[16,8,128]{2,1,0:T(8,128)S(1)}, f32[16,8,128]{2,1,0:T(8,128)S(1)}, u32[]{:S(2)}, u32[]{:S(2)}) collective-permute-start(f32[16,8,128]{2,1,0:T(8,128)S(1)} %get-tuple-element.91), channel_id=1, source_target_pairs={{0,4},{2,6},{4,0},{6,2},{1,5},{3,7},{5,1},{7,3},{8,12},{10,14},{12... | collective-permute-start | bytes 196616 | tf_op jit(solution)/shard_map/ppermute | solution.py:38
  254.4 1.1 collective-permute-done.29
  255.5 1.7 collective-permute-start.47
  257.9 1.9 collective-permute-start.51
  259.8 3.0 collective-permute-start.32
  262.8 2.7 collective-permute-start.34
  267.4 1.3 collective-permute-done.34
  268.8 2.1 collective-permute-start.35
  270.8 1.5 collective-permute-start.36
  273.4 5.6 %collective-permute-start.27 = (bf16[8,4096]{1,0:T(8,128)(2,1)S(1)}, bf16[8,4096]{1,0:T(8,128)(2,1)S(1)}, u32[]{:S(2)}, u32[]{:S(2)}) collective-permute-start(bf16[8,4096]{1,0:T(8,128)(2,1)S(1)} %slice.98), channel_id=1, source_target_pairs={{1,0},{2,1},{3,2},{4,3},{5,4},{6,5},{7,6},{8,7},{9,8},{10,9},{11,1... | collective-permute-start | bytes 196616 | tf_op jit(solution)/shard_map/ppermute | solution.py:26
  279.0 1.9 collective-permute-start.26
  281.0 2.4 collective-permute-start.38
  285.2 3.2 %short_adjoint.2.refs_0_ = bf16[128,12288]{1,0:T(8,128)(2,1)} custom-call(bf16[1,128,4096]{2,1,0:T(8,128)(2,1)S(1)} %bitcast.57, bf16[1,8,4096]{2,1,0:T(8,128)(2,1)S(1)} %bitcast.60, f32[7,12288]{1,0:T(8,128)S(1)} %copy-done.3), custom_call_target="tpu_custom_call" | custom-call | flops 7340032 | bytes 2097152 | tf_op jit(solution)/shard_map/short_adjoint/pallas_call | solution.py:328
  288.4 5.8 %short_adjoint.3 = bf16[128,12288]{1,0:T(8,128)(2,1)} custom-call(bf16[2,128,4096]{2,1,0:T(8,128)(2,1)S(1)} %copy-done.6, bf16[2,8,4096]{2,1,0:T(8,128)(2,1)S(1)} %collective-permute-done.26.rim_ref, f32[7,12288]{1,0:T(8,128)S(1)} %copy-done.3, bf16[128,12288]{1,0:T(8,128)(2,1)} %short_adjoint.2.refs_0_), custom_call_target="tpu_custom_call", output_to_operand_aliasing={{}: (3, {})} | custom-call | flops 14680064 | bytes 4194304 | tf_op jit(solution)/shard_map/short_adjoint/pallas_call | solution.py:328
  294.3 1.2 collective-permute-start.41
  295.6 1.1 collective-permute-done.41
  296.7 1.4 collect.1
  (177 shorter events, 32.4 us)
Async XLA Ops:
  7.2 180.6 %reduce-scatter.2.cloned.1.call-start = ((), (), s32[]{:S(2)}) async-start(), calls=%async_computation.1 | async-start | bytes 9437184 | tf_op jit(solution)/shard_map/reduce_scatter | solution.py:612
  8.2 7.5 %collective-permute-start.1 = (bf16[8,12288]{1,0:T(8,128)(2,1)S(1)}, bf16[8,12288]{1,0:T(8,128)(2,1)S(1)}, u32[]{:S(2)}, u32[]{:S(2)}) collective-permute-start(bf16[8,12288]{1,0:T(8,128)(2,1)S(1)} %slice_bitcast_fusion), channel_id=1, source_target_pairs={{0,1},{1,2},{2,3},{3,4},{4,5},{5,6},{6,7},{7,8},{8,9},{9,10},{10,1... | collective-permute-start | bytes 589832 | tf_op jit(solution)/shard_map/ppermute | solution.py:26
  16.7 7.6 %collective-permute-start.2 = (bf16[256,256]{1,0:T(8,128)(2,1)S(1)}, bf16[256,256]{1,0:T(8,128)(2,1)S(1)}, u32[]{:S(2)}, u32[]{:S(2)}) collective-permute-start(bf16[256,256]{1,0:T(8,128)(2,1)S(1)} %get-tuple-element.95), channel_id=1, source_target_pairs={{0,8},{8,0},{1,9},{9,1},{2,10},{10,2},{3,11},{11,3},{4,12},{12,4},... | collective-permute-start | bytes 393224 | tf_op jit(solution)/shard_map/ppermute | solution.py:38
  19.5 17.4 %collective-permute-start.3 = (bf16[256,256]{1,0:T(8,128)(2,1)S(1)}, bf16[256,256]{1,0:T(8,128)(2,1)S(1)}, u32[]{:S(2)}, u32[]{:S(2)}) collective-permute-start(bf16[256,256]{1,0:T(8,128)(2,1)S(1)} %get-tuple-element.95), channel_id=1, source_target_pairs={{0,16},{16,0},{1,17},{17,1},{2,18},{18,2},{3,19},{19,3},{4,20},{20... | collective-permute-start | bytes 393224 | tf_op jit(solution)/shard_map/ppermute | solution.py:38
  19.8 17.1 %collective-permute-start.4 = (bf16[256,256]{1,0:T(8,128)(2,1)S(1)}, bf16[256,256]{1,0:T(8,128)(2,1)S(1)}, u32[]{:S(2)}, u32[]{:S(2)}) collective-permute-start(bf16[256,256]{1,0:T(8,128)(2,1)S(1)} %get-tuple-element.95), channel_id=1, source_target_pairs={{0,24},{8,16},{16,8},{24,0},{1,25},{9,17},{17,9},{25,1},{2,26},{10... | collective-permute-start | bytes 393224 | tf_op jit(solution)/shard_map/ppermute | solution.py:38
  20.4 17.4 %collective-permute-start.5 = (bf16[256,256]{1,0:T(8,128)(2,1)S(1)}, bf16[256,256]{1,0:T(8,128)(2,1)S(1)}, u32[]{:S(2)}, u32[]{:S(2)}) collective-permute-start(bf16[256,256]{1,0:T(8,128)(2,1)S(1)} %get-tuple-element.94), channel_id=1, source_target_pairs={{0,32},{32,64},{64,96},{96,0},{1,33},{33,65},{65,97},{97,1},{2,34}... | collective-permute-start | bytes 393224 | tf_op jit(solution)/shard_map/ppermute | solution.py:38
  21.7 16.1 %collective-permute-start.6 = (bf16[256,256]{1,0:T(8,128)(2,1)S(1)}, bf16[256,256]{1,0:T(8,128)(2,1)S(1)}, u32[]{:S(2)}, u32[]{:S(2)}) collective-permute-start(bf16[256,256]{1,0:T(8,128)(2,1)S(1)} %get-tuple-element.94), channel_id=1, source_target_pairs={{0,64},{32,96},{64,0},{96,32},{1,65},{33,97},{65,1},{97,33},{2,66}... | collective-permute-start | bytes 393224 | tf_op jit(solution)/shard_map/ppermute | solution.py:38
  24.3 13.5 %collective-permute-start.7 = (bf16[256,256]{1,0:T(8,128)(2,1)S(1)}, bf16[256,256]{1,0:T(8,128)(2,1)S(1)}, u32[]{:S(2)}, u32[]{:S(2)}) collective-permute-start(bf16[256,256]{1,0:T(8,128)(2,1)S(1)} %get-tuple-element.94), channel_id=1, source_target_pairs={{0,96},{32,0},{64,32},{96,64},{1,97},{33,1},{65,33},{97,65},{2,98}... | collective-permute-start | bytes 393224 | tf_op jit(solution)/shard_map/ppermute | solution.py:38
  36.9 46.0 %copy-start.10 = (bf16[128,4096]{1,0:T(8,128)(2,1)}, bf16[128,4096]{1,0:T(8,128)(2,1)S(1)}, u32[]{:S(2)}) copy-start(bf16[128,4096]{1,0:T(8,128)(2,1)S(1)} %get-tuple-element.40.cur_ref) | copy-start | bytes 3145732
  36.9 41.2 %copy-start.35 = (bf16[256,128]{1,0:T(8,128)(2,1)S(1)}, bf16[256,128]{1,0:T(8,128)(2,1)}, u32[]{:S(2)}) copy-start(bf16[256,128]{1,0:T(8,128)(2,1)} %param.8) | copy-start | bytes 196612
  38.6 26.7 %collective-permute-start.8 = (bf16[128,4096]{1,0:T(8,128)(2,1)S(1)}, bf16[128,4096]{1,0:T(8,128)(2,1)S(1)}, u32[]{:S(2)}, u32[]{:S(2)}) collective-permute-start(bf16[128,4096]{1,0:T(8,128)(2,1)S(1)} %get-tuple-element.40.cur_ref), channel_id=1, source_target_pairs={{0,1},{1,2},{2,3},{3,4},{4,5},{5,6},{6,7},{7,8},{8,9},{9,10},{10,1... | collective-permute-start | bytes 3145736 | tf_op jit(solution)/shard_map/ppermute | solution.py:26
  47.1 14.2 %collective-permute-start = (bf16[1024,256]{1,0:T(8,128)(2,1)S(1)}, bf16[1024,256]{1,0:T(8,128)(2,1)S(1)}, u32[]{:S(2)}, u32[]{:S(2)}) collective-permute-start(bf16[1024,256]{1,0:T(8,128)(2,1)S(1)} %get-tuple-element.82), channel_id=1, source_target_pairs={{0,8},{8,0},{1,9},{9,1},{2,10},{10,2},{3,11},{11,3},{4,12},{12,4},... | collective-permute-start | bytes 1572872 | tf_op jit(solution)/shard_map/ppermute | solution.py:38
  50.1 14.1 %collective-permute-start.18 = (bf16[4,256,256]{2,1,0:T(8,128)(2,1)}, bf16[4,256,256]{2,1,0:T(8,128)(2,1)S(1)}, u32[]{:S(2)}, u32[]{:S(2)}) collective-permute-start(bf16[4,256,256]{2,1,0:T(8,128)(2,1)} %pad_maximum_fusion.1.refs_11_.refs_1_), channel_id=1, source_target_pairs={{0,32},{32,64},{64,96},{96,0},{1,33},{33,65},{65,97},{97,1},{2,34}... | collective-permute-start | bytes 1572872 | tf_op jit(solution)/shard_map/ppermute | solution.py:38
  50.1 43.3 %collective-permute-start.19 = (bf16[4,256,256]{2,1,0:T(8,128)(2,1)}, bf16[4,256,256]{2,1,0:T(8,128)(2,1)}, u32[]{:S(2)}, u32[]{:S(2)}) collective-permute-start(bf16[4,256,256]{2,1,0:T(8,128)(2,1)} %pad_maximum_fusion.1.refs_11_.refs_1_), channel_id=1, source_target_pairs={{0,64},{32,96},{64,0},{96,32},{1,65},{33,97},{65,1},{97,33},{2,66}... | collective-permute-start | bytes 1572872 | tf_op jit(solution)/shard_map/ppermute | solution.py:38
  51.8 41.6 %collective-permute-start.20 = (bf16[4,256,256]{2,1,0:T(8,128)(2,1)}, bf16[4,256,256]{2,1,0:T(8,128)(2,1)}, u32[]{:S(2)}, u32[]{:S(2)}) collective-permute-start(bf16[4,256,256]{2,1,0:T(8,128)(2,1)} %pad_maximum_fusion.1.refs_11_.refs_1_), channel_id=1, source_target_pairs={{0,96},{32,0},{64,32},{96,64},{1,97},{33,1},{65,33},{97,65},{2,98}... | collective-permute-start | bytes 1572872 | tf_op jit(solution)/shard_map/ppermute | solution.py:38
  61.2 32.2 %collective-permute-start.21 = (bf16[4,256,256]{2,1,0:T(8,128)(2,1)}, bf16[4,256,256]{2,1,0:T(8,128)(2,1)}, u32[]{:S(2)}, u32[]{:S(2)}) collective-permute-start(bf16[4,256,256]{2,1,0:T(8,128)(2,1)} %pad_maximum_fusion.2.refs_15_.refs_5_), channel_id=1, source_target_pairs={{0,8},{8,0},{1,9},{9,1},{2,10},{10,2},{3,11},{11,3},{4,12},{12,4},... | collective-permute-start | bytes 1572872 | tf_op jit(solution)/shard_map/ppermute | solution.py:38
  65.0 28.4 %collective-permute-start.22 = (bf16[4,256,256]{2,1,0:T(8,128)(2,1)}, bf16[4,256,256]{2,1,0:T(8,128)(2,1)}, u32[]{:S(2)}, u32[]{:S(2)}) collective-permute-start(bf16[4,256,256]{2,1,0:T(8,128)(2,1)} %pad_maximum_fusion.2.refs_15_.refs_5_), channel_id=1, source_target_pairs={{0,16},{16,0},{1,17},{17,1},{2,18},{18,2},{3,19},{19,3},{4,20},{20... | collective-permute-start | bytes 1572872 | tf_op jit(solution)/shard_map/ppermute | solution.py:38
  65.3 28.1 %collective-permute-start.23 = (bf16[4,256,256]{2,1,0:T(8,128)(2,1)}, bf16[4,256,256]{2,1,0:T(8,128)(2,1)}, u32[]{:S(2)}, u32[]{:S(2)}) collective-permute-start(bf16[4,256,256]{2,1,0:T(8,128)(2,1)} %pad_maximum_fusion.2.refs_15_.refs_5_), channel_id=1, source_target_pairs={{0,24},{8,16},{16,8},{24,0},{1,25},{9,17},{17,9},{25,1},{2,26},{10... | collective-permute-start | bytes 1572872 | tf_op jit(solution)/shard_map/ppermute | solution.py:38
  103.6 57.9 %copy-start.34 = (s32[4]{0:T(128)S(1)}, s32[4]{0:T(128)}, u32[]{:S(2)}) copy-start(s32[4]{0:T(128)} %constant.149.clone) | copy-start | bytes 52
  103.6 36.4 %collective-permute-start.9 = (bf16[128,4096]{1,0:T(8,128)(2,1)}, bf16[128,4096]{1,0:T(8,128)(2,1)}, u32[]{:S(2)}, u32[]{:S(2)}) collective-permute-start(bf16[128,4096]{1,0:T(8,128)(2,1)} %get-tuple-element.43.refs_0_), channel_id=1, source_target_pairs={{0,2},{2,4},{4,6},{6,0},{1,3},{3,5},{5,7},{7,1},{8,10},{10,12},{12... | collective-permute-start | bytes 3145736 | tf_op jit(solution)/shard_map/ppermute | solution.py:38
  105.2 36.0 %collective-permute-start.10 = (bf16[128,4096]{1,0:T(8,128)(2,1)}, bf16[128,4096]{1,0:T(8,128)(2,1)}, u32[]{:S(2)}, u32[]{:S(2)}) collective-permute-start(bf16[128,4096]{1,0:T(8,128)(2,1)} %get-tuple-element.43.refs_0_), channel_id=1, source_target_pairs={{0,6},{2,0},{4,2},{6,4},{1,7},{3,1},{5,3},{7,5},{8,14},{10,8},{12,... | collective-permute-start | bytes 3145736 | tf_op jit(solution)/shard_map/ppermute | solution.py:38
  110.9 52.6 %collective-permute-start.13 = (bf16[128,4096]{1,0:T(8,128)(2,1)}, bf16[128,4096]{1,0:T(8,128)(2,1)}, u32[]{:S(2)}, u32[]{:S(2)}) collective-permute-start(bf16[128,4096]{1,0:T(8,128)(2,1)} %get-tuple-element.43.refs_0_), channel_id=1, source_target_pairs={{0,1},{1,0},{2,3},{3,2},{4,5},{5,4},{6,7},{7,6},{8,9},{9,8},{10,11... | collective-permute-start | bytes 3145736 | tf_op jit(solution)/shard_map/ppermute | solution.py:38
  141.1 19.1 %collective-permute-start.11 = (bf16[64,4096]{1,0:T(8,128)(2,1)S(1)}, bf16[64,4096]{1,0:T(8,128)(2,1)}, u32[]{:S(2)}, u32[]{:S(2)}) collective-permute-start(bf16[64,4096]{1,0:T(8,128)(2,1)S(1)} %slice.120), channel_id=1, source_target_pairs={{0,2},{2,4},{4,6},{6,0},{1,3},{3,5},{5,7},{7,1},{8,10},{10,12},{12... | collective-permute-start | bytes 1572872 | tf_op jit(solution)/shard_map/ppermute | solution.py:38
  142.3 19.1 %collective-permute-start.12 = (bf16[64,4096]{1,0:T(8,128)(2,1)S(1)}, bf16[64,4096]{1,0:T(8,128)(2,1)}, u32[]{:S(2)}, u32[]{:S(2)}) collective-permute-start(bf16[64,4096]{1,0:T(8,128)(2,1)S(1)} %slice.121), channel_id=1, source_target_pairs={{0,6},{2,0},{4,2},{6,4},{1,7},{3,1},{5,3},{7,5},{8,14},{10,8},{12,... | collective-permute-start | bytes 1572872 | tf_op jit(solution)/shard_map/ppermute | solution.py:38
  145.1 18.7 %collective-permute-start.14 = (bf16[128,4096]{1,0:T(8,128)(2,1)}, bf16[128,4096]{1,0:T(8,128)(2,1)}, u32[]{:S(2)}, u32[]{:S(2)}) collective-permute-start(bf16[128,4096]{1,0:T(8,128)(2,1)} %collective-permute-done.9.refs_1_), channel_id=1, source_target_pairs={{0,1},{1,0},{2,3},{3,2},{4,5},{5,4},{6,7},{7,6},{8,9},{9,8},{10,11... | collective-permute-start | bytes 3145736 | tf_op jit(solution)/shard_map/ppermute | solution.py:38
  145.1 18.7 %collective-permute-start.15 = (bf16[128,4096]{1,0:T(8,128)(2,1)}, bf16[128,4096]{1,0:T(8,128)(2,1)}, u32[]{:S(2)}, u32[]{:S(2)}) collective-permute-start(bf16[128,4096]{1,0:T(8,128)(2,1)} %collective-permute-done.10.refs_2_), channel_id=1, source_target_pairs={{0,1},{1,0},{2,3},{3,2},{4,5},{5,4},{6,7},{7,6},{8,9},{9,8},{10,11... | collective-permute-start | bytes 3145736 | tf_op jit(solution)/shard_map/ppermute | solution.py:38
  160.3 3.2 %collective-permute-start.16 = (bf16[64,4096]{1,0:T(8,128)(2,1)}, bf16[64,4096]{1,0:T(8,128)(2,1)}, u32[]{:S(2)}, u32[]{:S(2)}) collective-permute-start(bf16[64,4096]{1,0:T(8,128)(2,1)} %collective-permute-done.11.refs_3_), channel_id=1, source_target_pairs={{0,1},{1,0},{2,3},{3,2},{4,5},{5,4},{6,7},{7,6},{8,9},{9,8},{10,11... | collective-permute-start | bytes 1572872 | tf_op jit(solution)/shard_map/ppermute | solution.py:38
  161.5 2.3 collective-permute-start.17
  163.5 24.3 %copy-start.16 = (bf16[128,4096]{1,0:T(8,128)(2,1)S(1)}, bf16[128,4096]{1,0:T(8,128)(2,1)}, u32[]{:S(2)}) copy-start(bf16[128,4096]{1,0:T(8,128)(2,1)} %copy-done.15) | copy-start | bytes 3145732
  186.3 13.5 %collective-permute-start.42 = (bf16[4,256,256]{2,1,0:T(8,128)(2,1)}, bf16[4,256,256]{2,1,0:T(8,128)(2,1)}, u32[]{:S(2)}, u32[]{:S(2)}) collective-permute-start(bf16[4,256,256]{2,1,0:T(8,128)(2,1)} %get-tuple-element.62), channel_id=1, source_target_pairs={{0,96},{32,0},{64,32},{96,64},{1,97},{33,1},{65,33},{97,65},{2,98}... | collective-permute-start | bytes 1572872 | tf_op jit(solution)/shard_map/ppermute | solution.py:38
  186.3 15.1 %collective-permute-start.43 = (bf16[4,256,256]{2,1,0:T(8,128)(2,1)}, bf16[4,256,256]{2,1,0:T(8,128)(2,1)}, u32[]{:S(2)}, u32[]{:S(2)}) collective-permute-start(bf16[4,256,256]{2,1,0:T(8,128)(2,1)} %get-tuple-element.63), channel_id=1, source_target_pairs={{0,64},{32,96},{64,0},{96,32},{1,65},{33,97},{65,1},{97,33},{2,66}... | collective-permute-start | bytes 1572872 | tf_op jit(solution)/shard_map/ppermute | solution.py:38
  186.3 26.9 %collective-permute-start.44 = (bf16[4,256,256]{2,1,0:T(8,128)(2,1)}, bf16[4,256,256]{2,1,0:T(8,128)(2,1)}, u32[]{:S(2)}, u32[]{:S(2)}) collective-permute-start(bf16[4,256,256]{2,1,0:T(8,128)(2,1)} %get-tuple-element.64), channel_id=1, source_target_pairs={{0,32},{32,64},{64,96},{96,0},{1,33},{33,65},{65,97},{97,1},{2,34}... | collective-permute-start | bytes 1572872 | tf_op jit(solution)/shard_map/ppermute | solution.py:38
  193.6 23.8 %copy-start.1 = (bf16[1,128,12288]{2,1,0:T(8,128)(2,1)S(1)}, bf16[1,128,12288]{2,1,0:T(8,128)(2,1)}, u32[]{:S(2)}) copy-start(bf16[1,128,12288]{2,1,0:T(8,128)(2,1)} %param.6) | copy-start | bytes 9437188
  193.6 37.5 %collective-permute-start.25 = (bf16[128,4096]{1,0:T(8,128)(2,1)}, bf16[128,4096]{1,0:T(8,128)(2,1)}, u32[]{:S(2)}, u32[]{:S(2)}) collective-permute-start(bf16[128,4096]{1,0:T(8,128)(2,1)} %get-tuple-element.50.grad_ref), channel_id=1, source_target_pairs={{1,0},{2,1},{3,2},{4,3},{5,4},{6,5},{7,6},{8,7},{9,8},{10,9},{11,1... | collective-permute-start | bytes 3145736 | tf_op jit(solution)/shard_map/ppermute | solution.py:26
  196.6 49.7 %collective-permute-start.48 = (bf16[4,256,256]{2,1,0:T(8,128)(2,1)}, bf16[4,256,256]{2,1,0:T(8,128)(2,1)S(1)}, u32[]{:S(2)}, u32[]{:S(2)}) collective-permute-start(bf16[4,256,256]{2,1,0:T(8,128)(2,1)} %copy-done.33), channel_id=1, source_target_pairs={{0,8},{8,0},{1,9},{9,1},{2,10},{10,2},{3,11},{11,3},{4,12},{12,4},... | collective-permute-start | bytes 1572872 | tf_op jit(solution)/shard_map/ppermute | solution.py:38
  199.8 47.5 %collective-permute-start.49 = (bf16[4,256,256]{2,1,0:T(8,128)(2,1)}, bf16[4,256,256]{2,1,0:T(8,128)(2,1)S(1)}, u32[]{:S(2)}, u32[]{:S(2)}) collective-permute-start(bf16[4,256,256]{2,1,0:T(8,128)(2,1)} %copy-done.32), channel_id=1, source_target_pairs={{0,16},{16,0},{1,17},{17,1},{2,18},{18,2},{3,19},{19,3},{4,20},{20... | collective-permute-start | bytes 1572872 | tf_op jit(solution)/shard_map/ppermute | solution.py:38
  201.4 47.3 %collective-permute-start.50 = (bf16[4,256,256]{2,1,0:T(8,128)(2,1)}, bf16[4,256,256]{2,1,0:T(8,128)(2,1)S(1)}, u32[]{:S(2)}, u32[]{:S(2)}) collective-permute-start(bf16[4,256,256]{2,1,0:T(8,128)(2,1)} %copy-done.31), channel_id=1, source_target_pairs={{0,24},{8,16},{16,8},{24,0},{1,25},{9,17},{17,9},{25,1},{2,26},{10... | collective-permute-start | bytes 1572872 | tf_op jit(solution)/shard_map/ppermute | solution.py:38
  213.2 35.7 %collective-permute-start.24 = (bf16[1024,256]{1,0:T(8,128)(2,1)}, bf16[1024,256]{1,0:T(8,128)(2,1)S(1)}, u32[]{:S(2)}, u32[]{:S(2)}) collective-permute-start(bf16[1024,256]{1,0:T(8,128)(2,1)} %copy-done.30), channel_id=1, source_target_pairs={{0,8},{8,0},{1,9},{9,1},{2,10},{10,2},{3,11},{11,3},{4,12},{12,4},... | collective-permute-start | bytes 1572872 | tf_op jit(solution)/shard_map/ppermute | solution.py:38
  231.1 28.7 %collective-permute-start.45 = (bf16[256,256]{1,0:T(8,128)(2,1)S(1)}, bf16[256,256]{1,0:T(8,128)(2,1)S(1)}, u32[]{:S(2)}, u32[]{:S(2)}) collective-permute-start(bf16[256,256]{1,0:T(8,128)(2,1)S(1)} %get-tuple-element.83), channel_id=1, source_target_pairs={{0,8},{8,0},{1,9},{9,1},{2,10},{10,2},{3,11},{11,3},{4,12},{12,4},... | collective-permute-start | bytes 393224 | tf_op jit(solution)/shard_map/ppermute | solution.py:38
  231.7 17.0 %copy-start.25 = (bf16[4,256,256]{2,1,0:T(8,128)(2,1)S(1)}, bf16[4,256,256]{2,1,0:T(8,128)(2,1)}, u32[]{:S(2)}) copy-start(bf16[4,256,256]{2,1,0:T(8,128)(2,1)} %copy-done.24) | copy-start | bytes 1572868
  245.6 33.4 %copy-start.5 = (bf16[2,128,4096]{2,1,0:T(8,128)(2,1)}, bf16[2,128,4096]{2,1,0:T(8,128)(2,1)S(1)}, u32[]{:S(2)}) copy-start(bf16[2,128,4096]{2,1,0:T(8,128)(2,1)S(1)} %get-tuple-element.53.grads_ref) | copy-start | bytes 6291460
  246.3 16.5 %collective-permute-start.46 = (bf16[256,256]{1,0:T(8,128)(2,1)S(1)}, bf16[256,256]{1,0:T(8,128)(2,1)S(1)}, u32[]{:S(2)}, u32[]{:S(2)}) collective-permute-start(bf16[256,256]{1,0:T(8,128)(2,1)S(1)} %get-tuple-element.85), channel_id=1, source_target_pairs={{0,16},{16,0},{1,17},{17,1},{2,18},{18,2},{3,19},{19,3},{4,20},{20... | collective-permute-start | bytes 393224 | tf_op jit(solution)/shard_map/ppermute | solution.py:38
  247.3 2.9 collective-permute-start.28
  250.2 23.2 %copy-start.9 = (bf16[128,4096]{1,0:T(8,128)(2,1)S(1)}, bf16[128,4096]{1,0:T(8,128)(2,1)}, u32[]{:S(2)}) copy-start(bf16[128,4096]{1,0:T(8,128)(2,1)} %copy-done.7) | copy-start | bytes 3145732
  250.3 5.2 %collective-permute-start.29 = (f32[16,8,128]{2,1,0:T(8,128)S(1)}, f32[16,8,128]{2,1,0:T(8,128)S(1)}, u32[]{:S(2)}, u32[]{:S(2)}) collective-permute-start(f32[16,8,128]{2,1,0:T(8,128)S(1)} %get-tuple-element.89), channel_id=1, source_target_pairs={{0,2},{2,4},{4,6},{6,0},{1,3},{3,5},{5,7},{7,1},{8,10},{10,12},{12... | collective-permute-start | bytes 196616 | tf_op jit(solution)/shard_map/ppermute | solution.py:38
  251.0 6.9 %collective-permute-start.30 = (f32[16,8,128]{2,1,0:T(8,128)S(1)}, f32[16,8,128]{2,1,0:T(8,128)S(1)}, u32[]{:S(2)}, u32[]{:S(2)}) collective-permute-start(f32[16,8,128]{2,1,0:T(8,128)S(1)} %get-tuple-element.91), channel_id=1, source_target_pairs={{0,4},{2,6},{4,0},{6,2},{1,5},{3,7},{5,1},{7,3},{8,12},{10,14},{12... | collective-permute-start | bytes 196616 | tf_op jit(solution)/shard_map/ppermute | solution.py:38
  254.2 5.5 %collective-permute-start.31 = (f32[16,8,128]{2,1,0:T(8,128)S(1)}, f32[16,8,128]{2,1,0:T(8,128)S(1)}, u32[]{:S(2)}, u32[]{:S(2)}) collective-permute-start(f32[16,8,128]{2,1,0:T(8,128)S(1)} %get-tuple-element.90), channel_id=1, source_target_pairs={{0,6},{2,0},{4,2},{6,4},{1,7},{3,1},{5,3},{7,5},{8,14},{10,8},{12,... | collective-permute-start | bytes 196616 | tf_op jit(solution)/shard_map/ppermute | solution.py:38
  255.5 7.3 %collective-permute-start.47 = (bf16[256,256]{1,0:T(8,128)(2,1)S(1)}, bf16[256,256]{1,0:T(8,128)(2,1)S(1)}, u32[]{:S(2)}, u32[]{:S(2)}) collective-permute-start(bf16[256,256]{1,0:T(8,128)(2,1)S(1)} %get-tuple-element.84), channel_id=1, source_target_pairs={{0,24},{8,16},{16,8},{24,0},{1,25},{9,17},{17,9},{25,1},{2,26},{10... | collective-permute-start | bytes 393224 | tf_op jit(solution)/shard_map/ppermute | solution.py:38
  257.9 14.5 %collective-permute-start.51 = (bf16[256,256]{1,0:T(8,128)(2,1)S(1)}, bf16[256,256]{1,0:T(8,128)(2,1)S(1)}, u32[]{:S(2)}, u32[]{:S(2)}) collective-permute-start(bf16[256,256]{1,0:T(8,128)(2,1)S(1)} %get-tuple-element.86), channel_id=1, source_target_pairs={{0,96},{32,0},{64,32},{96,64},{1,97},{33,1},{65,33},{97,65},{2,98}... | collective-permute-start | bytes 393224 | tf_op jit(solution)/shard_map/ppermute | solution.py:38
  259.7 13.6 %collective-permute-start.52 = (bf16[256,256]{1,0:T(8,128)(2,1)S(1)}, bf16[256,256]{1,0:T(8,128)(2,1)S(1)}, u32[]{:S(2)}, u32[]{:S(2)}) collective-permute-start(bf16[256,256]{1,0:T(8,128)(2,1)S(1)} %get-tuple-element.88), channel_id=1, source_target_pairs={{0,64},{32,96},{64,0},{96,32},{1,65},{33,97},{65,1},{97,33},{2,66}... | collective-permute-start | bytes 393224 | tf_op jit(solution)/shard_map/ppermute | solution.py:38
  259.8 6.0 %collective-permute-start.32 = (f32[16,8,128]{2,1,0:T(8,128)S(1)}, f32[16,8,128]{2,1,0:T(8,128)S(1)}, u32[]{:S(2)}, u32[]{:S(2)}) collective-permute-start(f32[16,8,128]{2,1,0:T(8,128)S(1)} %fusion.5), channel_id=1, source_target_pairs={{0,64},{32,96},{64,0},{96,32},{1,65},{33,97},{65,1},{97,33},{2,66}... | collective-permute-start | bytes 196616 | tf_op jit(solution)/shard_map/ppermute | solution.py:38
  262.8 4.6 %collective-permute-start.33 = (f32[16,8,128]{2,1,0:T(8,128)S(1)}, f32[16,8,128]{2,1,0:T(8,128)S(1)}, u32[]{:S(2)}, u32[]{:S(2)}) collective-permute-start(f32[16,8,128]{2,1,0:T(8,128)S(1)} %fusion.5), channel_id=1, source_target_pairs={{0,32},{32,64},{64,96},{96,0},{1,33},{33,65},{65,97},{97,1},{2,34}... | collective-permute-start | bytes 196616 | tf_op jit(solution)/shard_map/ppermute | solution.py:38
  262.8 5.9 %collective-permute-start.34 = (f32[16,8,128]{2,1,0:T(8,128)S(1)}, f32[16,8,128]{2,1,0:T(8,128)S(1)}, u32[]{:S(2)}, u32[]{:S(2)}) collective-permute-start(f32[16,8,128]{2,1,0:T(8,128)S(1)} %fusion.5), channel_id=1, source_target_pairs={{0,96},{32,0},{64,32},{96,64},{1,97},{33,1},{65,33},{97,65},{2,98}... | collective-permute-start | bytes 196616 | tf_op jit(solution)/shard_map/ppermute | solution.py:38
  265.6 19.6 %copy-start.3 = (f32[7,12288]{1,0:T(8,128)S(1)}, f32[7,12288]{1,0:T(8,128)}, u32[]{:S(2)}) copy-start(f32[7,12288]{1,0:T(8,128)} %filter_ref.3) | copy-start | bytes 1032196
  265.8 7.6 %collective-permute-start.53 = (bf16[256,256]{1,0:T(8,128)(2,1)S(1)}, bf16[256,256]{1,0:T(8,128)(2,1)S(1)}, u32[]{:S(2)}, u32[]{:S(2)}) collective-permute-start(bf16[256,256]{1,0:T(8,128)(2,1)S(1)} %get-tuple-element.87), channel_id=1, source_target_pairs={{0,32},{32,64},{64,96},{96,0},{1,33},{33,65},{65,97},{97,1},{2,34}... | collective-permute-start | bytes 393224 | tf_op jit(solution)/shard_map/ppermute | solution.py:38
  268.8 12.2 %collective-permute-start.35 = (f32[16,8,128]{2,1,0:T(8,128)S(1)}, f32[16,8,128]{2,1,0:T(8,128)S(1)}, u32[]{:S(2)}, u32[]{:S(2)}) collective-permute-start(f32[16,8,128]{2,1,0:T(8,128)S(1)} %add_add_fusion.1), channel_id=1, source_target_pairs={{0,16},{16,0},{1,17},{17,1},{2,18},{18,2},{3,19},{19,3},{4,20},{20... | collective-permute-start | bytes 196616 | tf_op jit(solution)/shard_map/ppermute | solution.py:38
  270.8 10.1 %collective-permute-start.36 = (f32[16,8,128]{2,1,0:T(8,128)S(1)}, f32[16,8,128]{2,1,0:T(8,128)S(1)}, u32[]{:S(2)}, u32[]{:S(2)}) collective-permute-start(f32[16,8,128]{2,1,0:T(8,128)S(1)} %add_add_fusion.1), channel_id=1, source_target_pairs={{0,8},{8,0},{1,9},{9,1},{2,10},{10,2},{3,11},{11,3},{4,12},{12,4},... | collective-permute-start | bytes 196616 | tf_op jit(solution)/shard_map/ppermute | solution.py:38
  272.3 8.6 %collective-permute-start.37 = (f32[16,8,128]{2,1,0:T(8,128)S(1)}, f32[16,8,128]{2,1,0:T(8,128)S(1)}, u32[]{:S(2)}, u32[]{:S(2)}) collective-permute-start(f32[16,8,128]{2,1,0:T(8,128)S(1)} %add_add_fusion.1), channel_id=1, source_target_pairs={{0,24},{8,16},{16,8},{24,0},{1,25},{9,17},{17,9},{25,1},{2,26},{10... | collective-permute-start | bytes 196616 | tf_op jit(solution)/shard_map/ppermute | solution.py:38
  273.4 11.8 %collective-permute-start.27 = (bf16[8,4096]{1,0:T(8,128)(2,1)S(1)}, bf16[8,4096]{1,0:T(8,128)(2,1)S(1)}, u32[]{:S(2)}, u32[]{:S(2)}) collective-permute-start(bf16[8,4096]{1,0:T(8,128)(2,1)S(1)} %slice.98), channel_id=1, source_target_pairs={{1,0},{2,1},{3,2},{4,3},{5,4},{6,5},{7,6},{8,7},{9,8},{10,9},{11,1... | collective-permute-start | bytes 196616 | tf_op jit(solution)/shard_map/ppermute | solution.py:26
  279.0 9.4 %collective-permute-start.26 = (bf16[2,8,4096]{2,1,0:T(8,128)(2,1)S(1)}, bf16[2,8,4096]{2,1,0:T(8,128)(2,1)S(1)}, u32[]{:S(2)}, u32[]{:S(2)}) collective-permute-start(bf16[2,8,4096]{2,1,0:T(8,128)(2,1)S(1)} %slice.97), channel_id=1, source_target_pairs={{1,0},{2,1},{3,2},{4,3},{5,4},{6,5},{7,6},{8,7},{9,8},{10,9},{11,1... | collective-permute-start | bytes 393224 | tf_op jit(solution)/shard_map/ppermute | solution.py:26
  281.0 13.2 %collective-permute-start.38 = (f32[16,8,128]{2,1,0:T(8,128)S(1)}, f32[16,8,128]{2,1,0:T(8,128)S(1)}, u32[]{:S(2)}, u32[]{:S(2)}) collective-permute-start(f32[16,8,128]{2,1,0:T(8,128)S(1)} %get-tuple-element.80), channel_id=1, source_target_pairs={{0,6},{2,0},{4,2},{6,4},{1,7},{3,1},{5,3},{7,5},{8,14},{10,8},{12,... | collective-permute-start | bytes 196616 | tf_op jit(solution)/shard_map/ppermute | solution.py:38
  283.5 10.8 %collective-permute-start.39 = (f32[16,8,128]{2,1,0:T(8,128)S(1)}, f32[16,8,128]{2,1,0:T(8,128)S(1)}, u32[]{:S(2)}, u32[]{:S(2)}) collective-permute-start(f32[16,8,128]{2,1,0:T(8,128)S(1)} %get-tuple-element.80), channel_id=1, source_target_pairs={{0,4},{2,6},{4,0},{6,2},{1,5},{3,7},{5,1},{7,3},{8,12},{10,14},{12... | collective-permute-start | bytes 196616 | tf_op jit(solution)/shard_map/ppermute | solution.py:38
  283.5 10.8 %collective-permute-start.40 = (f32[16,8,128]{2,1,0:T(8,128)S(1)}, f32[16,8,128]{2,1,0:T(8,128)S(1)}, u32[]{:S(2)}, u32[]{:S(2)}) collective-permute-start(f32[16,8,128]{2,1,0:T(8,128)S(1)} %get-tuple-element.80), channel_id=1, source_target_pairs={{0,2},{2,4},{4,6},{6,0},{1,3},{3,5},{5,7},{7,1},{8,10},{10,12},{12... | collective-permute-start | bytes 196616 | tf_op jit(solution)/shard_map/ppermute | solution.py:38
  294.3 2.4 collective-permute-start.41
  (28 other events, 83.5 us)
Sparse Core Ops, SparseCore 0:
  103.7 78.7 reduce-scatter.1

commit v4 on v3

--- a/solution.py
+++ b/solution.py
@@ -114,6 +114,11 @@
     return row, lane
 
 
+def mirror(size):
+    row, lane = lane_row((size, size))
+    return jnp.where((row + lane) % size == 0, 1.0, 0.0)
+
+
 def circulant(line, taps):
     wide = jnp.broadcast_to(line.astype(F32), (taps, taps))
     return pltpu.roll(wide, 0, 1, stride=1, stride_axis=0)
@@ -132,10 +137,11 @@
     row, lane = lane_row((rows, rows))
     above = lane > row
     packed = LANES // per_group
+    lines = jnp.dot(lines_ref[...].astype(BF16), mirror(rows).astype(BF16), preferred_element_type=F32)
     for block in range(width // LANES):
         at = pl.ds(block * LANES, LANES)
         for g in range(packed):
-            ring = circulant(lines_ref[block * packed + g : block * packed + g + 1, :], rows)
+            ring = circulant(lines[block * packed + g : block * packed + g + 1, :], rows)
             table[g * rows : (g + 1) * rows, 0:rows] = jnp.where(above, ring, 0.0).astype(BF16)
             table[g * rows : (g + 1) * rows, rows : 2 * rows] = jnp.where(above, 0.0, ring).astype(BF16)
         window = jnp.concatenate([prev_ref[:, at], cur_ref[:, at]], axis=0)
@@ -212,6 +218,7 @@
     above = lane > row
     member = lax.broadcasted_iota(jnp.int32, (rows, LANES), 1) // per_group
     packed = LANES // per_group
+    sums = []
     for block in range(width // LANES):
         at = pl.ds(block * LANES, LANES)
         window = jnp.concatenate([prev_ref[:, at], cur_ref[:, at]], axis=0)
@@ -227,7 +234,10 @@
         total = fold[pl.ds(0, packed, stride=8), :]
         for step in range(1, 8):
             total = total + pltpu.roll(fold[pl.ds(step, packed, stride=8), :], rows - step, 1)
-        long_ref[block * packed : (block + 1) * packed, :] = total
+        sums.append(total)
+    long_ref[...] = jnp.dot(
+        jnp.concatenate(sums, axis=0), mirror(rows), precision=lax.Precision.HIGHEST, preferred_element_type=F32
+    )
     tap_sums(short_taps, feature_ref[...].astype(F32), tokens_ref, rim_ref, short_ref)
 
 
@@ -343,18 +353,33 @@
     )(grads, rim, filters, *given)
 
 
-def spread_kernel(place, query_ref, key_ref, value_ref, long_ref, out_ref):
+def spread_kernel(place, query_ref, key_ref, value_ref, long_ref, own_ref, other_ref):
     steps = query_ref.shape[1] // LANES
-    for part, ref in enumerate((query_ref, key_ref, value_ref)):
-        for i in range(steps):
-            out_ref[place[part * steps + i]] = ref[:, i * LANES : (i + 1) * LANES]
-    for i in range(long_ref.shape[0] // 8):
-        out_ref[place[3 * steps + i]] = long_ref[8 * i : 8 * i + 8, :]
-
-
-def collect_kernel(place, tiles_ref, short_ref, long_ref):
+    half = own_ref.shape[0]
+    tiles = [ref[:, i * LANES : (i + 1) * LANES] for ref in (query_ref, key_ref, value_ref) for i in range(steps)]
+    tiles += [long_ref[8 * i : 8 * i + 8, :] for i in range(long_ref.shape[0] // 8)]
+    first = place[0] < half
+
+    @pl.when(first)
+    def _():
+        for i in range(half):
+            own_ref[place[i]] = tiles[i]
+            other_ref[place[half + i] - half] = tiles[half + i]
+
+    @pl.when(jnp.logical_not(first))
+    def _():
+        for i in range(half):
+            other_ref[place[i] - half] = tiles[i]
+            own_ref[place[half + i]] = tiles[half + i]
+
+
+def collect_kernel(place, *refs):
+    parts, short_ref, long_ref, tiles_ref = refs[:-3], refs[-3], refs[-2], refs[-1]
     short_taps, wide = short_ref.shape
     steps = wide // LANES
+    size = parts[0].shape[0]
+    for i, part in enumerate(parts):
+        tiles_ref[i * size : (i + 1) * size] = part[...]
     for i in range(steps):
         short_ref[:, i * LANES : (i + 1) * LANES] = tiles_ref[place[i]][0:short_taps, :]
     for i in range(long_ref.shape[0] // 8):
@@ -365,38 +390,39 @@
     return pl.BlockSpec(memory_space=pltpu.VMEM)
 
 
-def total_over_devices(places, query_sum, key_sum, value_sum, long_sum, short_taps):
+def total_over_devices(spread_to, collect_from, query_sum, key_sum, value_sum, long_sum, short_taps):
     ny, nz = lax.axis_size("y"), lax.axis_size("z")
     channels = query_sum.shape[1]
     count = 3 * channels // LANES + long_sum.shape[0] // 8
-    tiles = pl.pallas_call(
+    half = jax.ShapeDtypeStruct((count // 2, 8, LANES), F32)
+    own, other = pl.pallas_call(
         spread_kernel,
         in_specs=[pl.BlockSpec(memory_space=pltpu.SMEM)] + [in_vmem()] * 4,
-        out_specs=in_vmem(),
-        out_shape=jax.ShapeDtypeStruct((count, 8, LANES), F32),
+        out_specs=[in_vmem()] * 2,
+        out_shape=[half] * 2,
         compiler_params=params(),
         name="spread",
-    )(places, query_sum, key_sum, value_sum, long_sum)
-    half = count // 2
-    part = tiles[:half] + move(tiles[half:], c=1)
-    size = half // nz
+    )(spread_to, query_sum, key_sum, value_sum, long_sum)
+    part = own + move(other, c=1)
+    size = count // 2 // nz
     part = sum([move(part[d * size : (d + 1) * size], z=d) for d in range(1, nz)], part[:size])
     whole = paired_sum([part] + [move(part, y=d) for d in range(1, ny)])
     whole = paired_sum([move(whole, xl=a, xh=b) for a, b in FLIPS])
-    line = jnp.concatenate([move(whole, z=-d) for d in range(nz)], axis=0)
-    tiles = jnp.concatenate([line, move(line, c=1)], axis=0)
+    line = jnp.concatenate([whole, move(whole, c=1)], axis=0)
+    lines = [move(line, z=-d) for d in range(nz)]
     groups, taps = long_sum.shape
     return pl.pallas_call(
         collect_kernel,
-        in_specs=[pl.BlockSpec(memory_space=pltpu.SMEM), in_vmem()],
+        in_specs=[pl.BlockSpec(memory_space=pltpu.SMEM)] + [in_vmem()] * nz,
         out_specs=[in_vmem(), in_vmem()],
+        scratch_shapes=[pltpu.VMEM((count, 8, LANES), F32)],
         out_shape=[
             jax.ShapeDtypeStruct((short_taps, 3 * channels), F32),
             jax.ShapeDtypeStruct((groups, taps), F32),
         ],
         compiler_params=params(),
         name="collect",
-    )(places, tiles)
+    )(collect_from, *lines)
 
 
 def paired_sum(terms):
@@ -466,26 +492,16 @@
     )(cotangents, *tops, *bottoms)
 
 
-def project_kernel(ny, count, place, *refs):
-    pieces, refs = refs[:count], refs[count - 1 :]
-    turned_ref, tops, bottoms = refs[1], refs[2 : 2 + ny], refs[2 + ny : 6 + ny]
+def project_kernel(ny, *refs):
+    rows_ref, turned_ref, tops, bottoms = refs[0], refs[1], refs[2 : 2 + ny], refs[2 + ny : 6 + ny]
     own_ref, other_ref = refs[6 + ny : 8 + ny]
     top_grads, bottom_grads = refs[8 + ny : 8 + 2 * ny], refs[8 + 2 * ny : 12 + 2 * ny]
-    total, turned = refs[12 + 2 * ny :]
+    total = refs[12 + 2 * ny]
     step = pl.program_id(0)
-    height = pieces[0].shape[0]
-    blocks = total.shape[0] // height
-
-    @pl.when(step == 0)
-    def _():
-        for j in range(blocks):
-            at = pl.multiple_of(place[j] * height, height)
-            turned[:, j * height : (j + 1) * height] = turned_ref[:, pl.ds(at, height)]
-
-    rows = jnp.concatenate([p[...] for p in pieces], axis=0)
+    rows = rows_ref[...]
     width = own_ref.shape[1]
     size = tops[0].shape[1]
-    grads = jnp.dot(turned[...], rows, preferred_element_type=F32).astype(BF16)
+    grads = jnp.dot(turned_ref[...], rows, preferred_element_type=F32).astype(BF16)
     for a in range(2):
         for b in range(2):
             at = (2 * a + 1) * size
@@ -507,23 +523,12 @@
 
     @pl.when(step == ny - 1)
     def _():
-        for j in range(blocks):
-            at = pl.ds(pl.multiple_of(place[j] * height, height), height)
-            own_ref[at, :] = total[j * height : (j + 1) * height, :width].astype(BF16)
-            other_ref[at, :] = total[j * height : (j + 1) * height, width:].astype(BF16)
-
-
-def line_gather(x):
-    half = x.shape[0] // 2
-    before, after = move(x, z=1), move(x, z=-1)
-    far = [move(before[:half], z=1), move(after[half:], z=-1)]
-    pieces = [x, before, after, *far]
-    return pieces + [move(p, c=1) for p in pieces]
-
-
-def project(place, pieces, turned, tops, bottoms):
-    rows = sum(p.shape[0] for p in pieces)
-    channels = pieces[0].shape[1]
+        own_ref[...] = total[:, :width].astype(BF16)
+        other_ref[...] = total[:, width:].astype(BF16)
+
+
+def project(all_rows, turned, tops, bottoms):
+    rows, channels = all_rows.shape
     ny = len(tops)
     size = tops[0].shape[1]
     width = turned.shape[0] // 2
@@ -534,21 +539,17 @@
         + [jax.ShapeDtypeStruct((ny, width, size), BF16)] * 4
     )
     results = pl.pallas_call(
-        functools.partial(project_kernel, ny, len(pieces)),
-        grid_spec=pltpu.PrefetchScalarGridSpec(
-            num_scalar_prefetch=1,
-            grid=(ny,),
-            in_specs=[pl.BlockSpec((p.shape[0], channels // ny), lambda i, place: (0, i)) for p in pieces]
-            + [whole(turned)]
-            + [whole(x) for x in (*tops, *bottoms)],
-            out_specs=[whole(x) for x in outs],
-            scratch_shapes=[pltpu.VMEM((rows, 2 * width), F32), pltpu.VMEM(turned.shape, BF16)],
-        ),
+        functools.partial(project_kernel, ny),
+        grid=(ny,),
+        in_specs=[pl.BlockSpec((rows, channels // ny), lambda i: (0, i)), whole(turned)]
+        + [whole(x) for x in (*tops, *bottoms)],
+        out_specs=[whole(x) for x in outs],
         out_shape=outs,
+        scratch_shapes=[pltpu.VMEM((rows, 2 * width), F32)],
         compiler_params=params(40),
         cost_estimate=cost(8 * rows * width * channels, 2 * (rows + 4 * width) * channels),
         name="project",
-    )(place, *pieces, turned, *tops, *bottoms)
+    )(all_rows, turned, *tops, *bottoms)
     return results[0], results[1], results[2 : 2 + ny], results[2 + ny :]
 
 
@@ -566,10 +567,6 @@
     top = added([move(top[f], xl=a, xh=b) for f, (a, b) in enumerate(FLIPS)])
     bottom = added([move(bottom[d], y=-d) for d in range(ny)])
     return jnp.concatenate([top, bottom], axis=1).T
-
-
-def mirrored(lines):
-    return jnp.roll(lines[:, ::-1], 1, axis=1)
 
 
 def shards(tokens_in, short_filter, long_filter, out_weight, cotangent):
@@ -586,31 +583,35 @@
 
     block = jnp.arange(2 * ny, dtype=jnp.int32)
     place = ((y - block // 2) % ny) * 2 + (block + xl) % 2
-    step = jnp.arange(2 * nz, dtype=jnp.int32)
-    near = jnp.array([0, -1, 1, 2], jnp.int32)[step % nz]
-    row_place = (z + near) % nz * 2 + (step // nz + c) % 2
     size = 3 * channels // LANES + groups // 8
     each = size // (2 * nz)
     tile = jnp.arange(size, dtype=jnp.int32)
-    places = ((tile // (nz * each) + c) % 2 * nz + (tile // each - z) % nz) * each + tile % each
+    core_step, z_step = (tile // (nz * each) + c) % 2, (tile // each - z) % nz
+    spread_to = (core_step * nz + z_step) * each + tile % each
+    collect_from = (z_step * 2 + core_step) * each + tile % each
 
     rim = along(tokens[rows - RIM :], 1)
-    rim, out_weight = lax.optimization_barrier((rim, out_weight))
-    wide_top, tall_bottom = gather_near(out_weight)
     mine = lax.dynamic_slice_in_dim(upstream, xh * span, span, 0)
     others = move(lax.dynamic_slice_in_dim(upstream, (1 - xh) * span, span, 0), xh=1)
+    query, key, value, mixer = features_call(tokens, rim, short_filter)
+    mixer, others, out_weight = lax.optimization_barrier((mixer, others, out_weight))
+    mixer_prev = along(mixer, 1)
+    wide_top, tall_bottom = gather_near(out_weight)
+    lines = long_filter.astype(F32)
+    mixed, gated = mix_call(place, lines, mixer_prev, mixer, query)
+    gated, wide_top, tall_bottom = lax.optimization_barrier((gated, wide_top, tall_bottom))
+    all_rows = lax.all_gather(gated, ("z", "c"), axis=0, tiled=True)
+    tops, bottoms = gather_far(wide_top, tall_bottom)
     cotangents = jnp.concatenate([mine, others], axis=1)
-
-    lines = long_filter.astype(F32)
-    query, key, value, mixer = features_call(tokens, rim, short_filter)
-    mixer, wide_top, tall_bottom = lax.optimization_barrier((mixer, wide_top, tall_bottom))
-    tops, bottoms = gather_far(wide_top, tall_bottom)
-    mixer_prev = along(mixer, 1)
-    mixed, gated = mix_call(place, mirrored(lines), mixer_prev, mixer, query)
-    cotangents, gated = lax.optimization_barrier((cotangents, gated))
     partial = gate_matmul(cotangents, tops, bottoms)
+    partial, all_rows = lax.optimization_barrier((partial, all_rows))
     gate_grad = lax.psum_scatter(partial, ("z", "c"), scatter_dimension=0, tiled=True)
-    pieces = line_gather(gated)
+
+    own, other, top_grads, bottom_grads = project(all_rows, cotangents.T, tops, bottoms)
+    grad_weight = plane_scatter_sum(top_grads, bottom_grads)
+    theirs = move(other, xh=1)
+    output = jnp.where(xh == 0, jnp.concatenate([own, theirs], axis=0), jnp.concatenate([theirs, own], axis=0))
+    gate_grad, grad_weight, output = lax.optimization_barrier((gate_grad, grad_weight, output))
 
     grad_mixed, query_grad = gate_call(place, gate_grad, query, mixed)
     grad_next = along(grad_mixed, -1)
@@ -623,14 +624,11 @@
         lines, short_taps, grad_mixed, grad_next, key, value, tokens, rim
     )
     other_next = along(other_grads[:, :RIM], -1)
-    grad_short, grad_long = total_over_devices(places, query_sum, key_sum, value_sum, long_sum, short_taps)
+    grad_short, grad_long = total_over_devices(
+        spread_to, collect_from, query_sum, key_sum, value_sum, long_sum, short_taps
+    )
     grad_tokens = short_adjoint_call(other_grads, other_next, short_filter, 1, grad_tokens)
-
-    own, other, top_grads, bottom_grads = project(row_place, pieces, cotangents.T, tops, bottoms)
-    grad_weight = plane_scatter_sum(top_grads, bottom_grads)
-    theirs = move(other, xh=1)
-    output = jnp.where(xh == 0, jnp.concatenate([own, theirs], axis=0), jnp.concatenate([theirs, own], axis=0))
-    return output[None], grad_tokens[None], grad_short, mirrored(grad_long), grad_weight
+    return output[None], grad_tokens[None], grad_short, grad_long, grad_weight
 
 
 def solution(mesh):

time: 307 us -> 315 us (1.026)
  starting transfers between devices: 97.7 us -> 75.8 us
  waiting for transfers between devices: 73.1 us -> 84.6 us
  local copies, waits for them, and re-layouts: 33.8 us -> 44 us
  other arithmetic: 8.51 us -> 12.6 us
  Pallas kernels: 78.2 us -> 81.4 us
    all_gather x0 -> x1, waiting for transfers between devices: none -> 24.5 us  [shards(): all_rows = lax.all_gather(gated, ('z', 'c'), axis=0, tiled=True)]
    ppermute x49 -> x40, starting transfers between devices: 75.9 us -> 55.6 us  [move(): return lax.ppermute(x, axes, pairs)]
    ppermute x49 -> x40, waiting for transfers between devices: 70.5 us -> 54.1 us  [move(): return lax.ppermute(x, axes, pairs)]
    unnamed x78 -> x95, local copies, waits for them, and re-layouts: 22.9 us -> 33.7 us
    slice x8 -> x0, local copies, waits for them, and re-layouts: 4.88 us -> none  [the longest x5 2.67 us: mirrored(): return jnp.roll(lines[:, ::-1], 1, axis=1)]
    ppermute x5, waiting for transfers between devices: 2.6 us -> 5.95 us  [along(): return lax.ppermute(x, LINE, pairs)]
  transfers between devices with their start and end apart: 55 -> 47, of which waited for: 16 -> 20; matrix products, arithmetic and copies ran while one was open for 5% -> 6% of each run, Pallas kernels for 23% -> 16%
where the time goes in v4:
time: 315 us; the launch traced here: 313 us
  waiting for transfers between devices  84.6 us (27%)
  Pallas kernels  81.4 us (26%)
  starting transfers between devices  75.8 us (24%)
  local copies, waits for them, and re-layouts  44 us (14%)
  between operations  14.5 us (5%)
  other arithmetic  12.6 us (4%)
    ppermute x40, starting transfers between devices, move(): return lax.ppermute(x, axes, pairs)  55.6 us
    ppermute x40, waiting for transfers between devices, move(): return lax.ppermute(x, axes, pairs)  54.1 us
    unnamed x95, local copies, waits for them, and re-layouts  33.7 us
    all_gather x1, waiting for transfers between devices, shards(): all_rows = lax.all_gather(gated, ('z', 'c'), axis=0, tiled=True)  24.5 us
    ppermute x5, starting transfers between devices, along(): return lax.ppermute(x, LINE, pairs)  20.1 us
    pallas_call x1, Pallas kernels, unmix_call(): pl.pallas_call(functools.partial(unmix_kernel, per_group, short_taps), gr...  13.9 us
    pallas_call x1, Pallas kernels, project(): pl.pallas_call(functools.partial(project_kernel, ny), grid=(ny,), in_spec...  13.7 us
    pallas_call x1, Pallas kernels, long_grad_call(): pl.pallas_call(functools.partial(long_grad_kernel, per_group, short_taps)...  12.1 us
  transfers between devices with their start and end apart: 47, of which 20 were waited for; matrix products, arithmetic and copies ran while one was open for 6% of the time, Pallas kernels for 16%

profile of v4, /device:TPU:1, one launch (start us, length us, event | category | flops | bytes accessed | tf_op | source)
XLA Modules:
  0.0 312.9 jit_solution(1197404550309085433)
XLA Ops:
  7.2 2.4 constant_dynamic-slice_fusion.1
  9.6 2.0 copy.12
  11.7 3.6 %collective-permute-start.1 = (bf16[1024,256]{0,1:T(8,128)(2,1)}, bf16[1024,256]{0,1:T(8,128)(2,1)S(1)}, u32[]{:S(2)}, u32[]{:S(2)}) collective-permute-start(bf16[1024,256]{0,1:T(8,128)(2,1)} %bitcast.56), channel_id=1, source_target_pairs={{0,8},{8,0},{1,9},{9,1},{2,10},{10,2},{3,11},{11,3},{4,12},{12,4},... | collective-permute-start | bytes 1572872 | tf_op jit(solution)/shard_map/ppermute | solution.py:38
  15.3 4.4 %collective-permute-start = (bf16[8,12288]{1,0:T(8,128)(2,1)S(1)}, bf16[8,12288]{1,0:T(8,128)(2,1)S(1)}, u32[]{:S(2)}, u32[]{:S(2)}) collective-permute-start(bf16[8,12288]{1,0:T(8,128)(2,1)S(1)} %slice_bitcast_fusion), channel_id=1, source_target_pairs={{0,1},{1,2},{2,3},{3,4},{4,5},{5,6},{6,7},{7,8},{8,9},{9,10},{10,1... | collective-permute-start | bytes 589832 | tf_op jit(solution)/shard_map/ppermute | solution.py:26
  19.7 2.6 collective-permute-done.refs_3_.refs_4_.refs_5_.key_rim_ref.value_rim_ref.rim_ref
  22.3 8.2 %features.1 = (bf16[128,4096]{1,0:T(8,128)(2,1)S(1)}, bf16[128,4096]{1,0:T(8,128)(2,1)S(1)}, bf16[128,4096]{1,0:T(8,128)(2,1)S(1)}, bf16[128,4096]{1,0:T(8,128)(2,1)}) custom-call(bf16[128,12288]{1,0:T(8,128)(2,1)S(1)} %bitcast.45, bf16[128,12288]{1,0:T(8,128)(2,1)S(1)} %bitcast.46, bf16[128,12288]{1,0:T(8,128)(2,1)S(1)} %bitcast.47, ...), custom_call_target="tpu_custom_call" | custom-call | bytes 1572864 | tf_op jit(solution)/shard_map/features/pallas_call | solution.py:97
  34.3 4.4 %collective-permute-start.2 = (bf16[128,4096]{1,0:T(8,128)(2,1)}, bf16[128,4096]{1,0:T(8,128)(2,1)}, u32[]{:S(2)}, u32[]{:S(2)}) collective-permute-start(bf16[128,4096]{1,0:T(8,128)(2,1)} %get-tuple-element.45.cur_ref), channel_id=1, source_target_pairs={{0,1},{1,2},{2,3},{3,4},{4,5},{5,6},{6,7},{7,8},{8,9},{9,10},{10,1... | collective-permute-start | bytes 3145736 | tf_op jit(solution)/shard_map/ppermute | solution.py:26
  40.4 3.0 collective-permute-start.3
  43.4 2.7 collective-permute-start.8
  46.1 1.7 collective-permute-start.7
  49.0 2.0 pad_maximum_fusion.1.refs_1_.refs_2_
  51.6 1.8 collective-permute-done.6
  53.4 1.8 pad_maximum_fusion.2.refs_5_.refs_6_
  55.2 10.6 %mix.1 = (bf16[128,4096]{1,0:T(8,128)(2,1)S(1)}, bf16[128,4096]{1,0:T(8,128)(2,1)S(1)}) custom-call(s32[8]{0:T(128)S(1)} %fusion.6.place, f32[256,128]{1,0:T(8,128)S(1)} %convert_element_type.63.lines_ref, bf16[128,4096]{1,0:T(8,128)(2,1)} %collective-permute-done.2.prev_ref, bf16[128,4096]{1,0:T(8,128)(2,1)} %get-tuple-element.45.cur_ref, ...), custom_call_target="tpu_custom_call" | custom-call | bytes 1048576 | tf_op jit(solution)/shard_map/mix/pallas_call | solution.py:162
  69.1 2.0 collective-permute-start.11
  71.1 1.4 collective-permute-start.13
  72.5 10.5 %collective-permute-done.9.refs_2_.refs_3_ = bf16[4,256,256]{2,1,0:T(8,128)(2,1)S(1)} collective-permute-done((bf16[4,256,256]{2,1,0:T(8,128)(2,1)}, bf16[4,256,256]{2,1,0:T(8,128)(2,1)S(1)}, u32[]{:S(2)}, u32[]{:S(2)}) %collective-permute-start.9) | collective-permute-done | bytes 524320 | tf_op jit(solution)/shard_map/ppermute | solution.py:38
  84.3 2.0 copy.11
  86.4 2.9 fusion.15
  89.3 2.3 copy.13.refs_0_
  91.6 7.5 %collective-permute-done.14.refs_8_.refs_9_ = bf16[4,256,256]{2,1,0:T(8,128)(2,1)} collective-permute-done((bf16[4,256,256]{2,1,0:T(8,128)(2,1)}, bf16[4,256,256]{2,1,0:T(8,128)(2,1)}, u32[]{:S(2)}, u32[]{:S(2)}) %collective-permute-start.14) | collective-permute-done | bytes 524320 | tf_op jit(solution)/shard_map/ppermute | solution.py:38
  99.0 1.3 copy-done.21
  103.5 6.5 %gate_matmul.1 = bf16[1024,4096]{1,0:T(8,128)(2,1)S(1)} custom-call(bf16[1024,512]{1,0:T(8,128)(2,1)S(1)} %copy-done.21, bf16[4,256,256]{2,1,0:T(8,128)(2,1)S(1)} %copy-done.31, bf16[4,256,256]{2,1,0:T(8,128)(2,1)S(1)} %copy-done.41, bf16[4,256,256]{2,1,0:T(8,128)(2,1)} %collective-permute-done.10.refs_3_.refs_4_, ...), custom_call_target="tpu_custom_call" | custom-call | flops 4294967296 | bytes 12582912 | tf_op jit(solution)/shard_map/gate_matmul/pallas_call | solution.py:483
  110.0 3.3 %copy-done.2 = bf16[1024,4096]{1,0:T(8,128)(2,1)} copy-done((bf16[1024,4096]{1,0:T(8,128)(2,1)}, bf16[1024,4096]{1,0:T(8,128)(2,1)S(1)}, u32[]{:S(2)}) %copy-start.2) | copy-done | bytes 8388632
  113.3 24.5 %all-gather.2.cloned.1.call-done.refs_0_ = bf16[1024,4096]{1,0:T(8,128)(2,1)} async-done(((bf16[128,4096]{1,0:T(8,128)(2,1)}), bf16[1024,4096]{1,0:T(8,128)(2,1)}) %all-gather.2.cloned.1.call-update) | async-done | bytes 8388624 | tf_op jit(solution)/shard_map/all_gather | solution.py:603
  142.2 13.7 %project.1 = (bf16[1024,256]{1,0:T(8,128)(2,1)S(1)}, bf16[1024,256]{1,0:T(8,128)(2,1)S(1)}, bf16[4,256,256]{2,1,0:T(8,128)(2,1)S(1)}, bf16[4,256,256]{2,1,0:T(8,...) custom-call(bf16[1024,4096]{1,0:T(8,128)(2,1)} %all-gather.2.cloned., ...), custom_call_target="tpu_custom_call" | custom-call | flops 8589934592 | bytes 16777216 | tf_op jit(solution)/shard_map/project/pallas_call | solution.py:541
  161.6 2.4 collective-permute-start.23
  164.1 1.4 collective-permute-start.21
  166.7 2.4 collective-permute-start.16
  169.1 7.3 %collective-permute-done.23 = bf16[4,256,256]{2,1,0:T(8,128)(2,1)} collective-permute-done((bf16[4,256,256]{2,1,0:T(8,128)(2,1)}, bf16[4,256,256]{2,1,0:T(8,128)(2,1)}, u32[]{:S(2)}, u32[]{:S(2)}) %collective-permute-start.23) | collective-permute-done | bytes 524320 | tf_op jit(solution)/shard_map/ppermute | solution.py:38
  176.4 2.5 collective-permute-start.15
  178.9 1.5 collective-permute-start.27
  180.4 8.2 %collective-permute-done.21 = bf16[4,256,256]{2,1,0:T(8,128)(2,1)} collective-permute-done((bf16[4,256,256]{2,1,0:T(8,128)(2,1)}, bf16[4,256,256]{2,1,0:T(8,128)(2,1)}, u32[]{:S(2)}, u32[]{:S(2)}) %collective-permute-start.21) | collective-permute-done | bytes 524320 | tf_op jit(solution)/shard_map/ppermute | solution.py:38
  188.5 1.8 add_convert_fusion
  190.4 1.3 collective-permute-start.26
  191.7 2.4 collective-permute-start.25
  195.6 2.5 collective-permute-start.20
  198.1 1.6 collective-permute-done.27
  199.7 1.3 maximum_select_fusion
  200.9 3.6 %collective-permute-start.18 = (bf16[256,256]{1,0:T(8,128)(2,1)S(1)}, bf16[256,256]{1,0:T(8,128)(2,1)S(1)}, u32[]{:S(2)}, u32[]{:S(2)}) collective-permute-start(bf16[256,256]{1,0:T(8,128)(2,1)S(1)} %get-tuple-element.90), channel_id=1, source_target_pairs={{0,8},{8,0},{1,9},{9,1},{2,10},{10,2},{3,11},{11,3},{4,12},{12,4},... | collective-permute-start | bytes 393224 | tf_op jit(solution)/shard_map/ppermute | solution.py:38
  204.6 3.2 %collective-permute-done.18 = bf16[256,256]{1,0:T(8,128)(2,1)S(1)} collective-permute-done((bf16[256,256]{1,0:T(8,128)(2,1)S(1)}, bf16[256,256]{1,0:T(8,128)(2,1)S(1)}, u32[]{:S(2)}, u32[]{:S(2)}) %collective-permute-start.18) | collective-permute-done | bytes 131104 | tf_op jit(solution)/shard_map/ppermute | solution.py:38
  208.8 1.2 copy-done.8
  212.4 3.6 %gate_back.1 = (bf16[128,4096]{1,0:T(8,128)(2,1)}, bf16[128,4096]{1,0:T(8,128)(2,1)S(1)}) custom-call(s32[8]{0:T(128)S(1)} %fusion.6.place, bf16[128,4096]{1,0:T(8,128)(2,1)S(1)} %copy-done.19, bf16[128,4096]{1,0:T(8,128)(2,1)S(1)} %copy-done.8, bf16[128,4096]{1,0:T(8,128)(2,1)S(1)} %copy-done.18), custom_call_target="tpu_custom_call" | custom-call | flops 1048576 | bytes 5242880 | tf_op jit(solution)/shard_map/gate_back/pallas_call | solution.py:190
  217.0 4.8 %collective-permute-start.28 = (bf16[128,4096]{1,0:T(8,128)(2,1)}, bf16[128,4096]{1,0:T(8,128)(2,1)}, u32[]{:S(2)}, u32[]{:S(2)}) collective-permute-start(bf16[128,4096]{1,0:T(8,128)(2,1)} %get-tuple-element.67.grad_ref), channel_id=1, source_target_pairs={{1,0},{2,1},{3,2},{4,3},{5,4},{6,5},{7,6},{8,7},{9,8},{10,9},{11,1... | collective-permute-start | bytes 3145736 | tf_op jit(solution)/shard_map/ppermute | solution.py:26
  224.1 12.1 %long_grad.1 = (f32[256,128]{1,0:T(8,128)S(1)}, f32[8,4096]{1,0:T(8,128)S(1)}) custom-call(bf16[128,4096]{1,0:T(8,128)(2,1)} %collective-permute-done.2.prev_ref, bf16[128,4096]{1,0:T(8,128)(2,1)} %get-tuple-element.45.cur_ref, bf16[128,4096]{1,0:T(8,128)(2,1)} %get-tuple-element.67.grad_ref, bf16[128,4096]{1,0:T(8,128)(2,1)S(1)} %copy-done.12, ...), custom_call_target="tpu_custom_call" | custom-call | flops 2147483648 | bytes 5242880 | tf_op jit(solution)/shard_map/long_grad/pallas_call | solution.py:251
  236.2 13.9 %unmix.1 = (bf16[2,128,4096]{2,1,0:T(8,128)(2,1)S(1)}, f32[8,4096]{1,0:T(8,128)S(1)}, f32[8,4096]{1,0:T(8,128)S(1)}) custom-call(f32[256,128]{1,0:T(8,128)S(1)} %copy-done.15, bf16[128,4096]{1,0:T(8,128)(2,1)} %get-tuple-element.67.grad_ref, bf16[128,4096]{1,0:T(8,128)(2,1)} %collective-permute-done.28.next_ref, bf16[128,4096]{1,0:T(8,128)(2,1)S(1)} %copy-done.23, ...), custom_call_target="tpu_custom_call" | custom-call | flops 2147483648 | bytes 8388608 | tf_op jit(solution)/shard_map/unmix/pallas_call | solution.py:306
  250.9 1.5 collective-permute-done.31
  252.5 2.8 collective-permute-start.34
  256.0 2.1 collective-permute-done.34
  258.1 2.0 collective-permute-done.33
  260.0 1.6 collective-permute-done.32
  261.7 1.3 collective-permute-start.36
  263.0 1.5 collective-permute-start.37
  264.4 1.5 collective-permute-start.35
  266.1 3.0 collective-permute-done.35
  270.1 1.4 collective-permute-start.40
  271.8 2.0 collective-permute-done.39
  275.0 3.8 %collective-permute-start.41 = (f32[16,8,128]{2,1,0:T(8,128)S(1)}, f32[16,8,128]{2,1,0:T(8,128)S(1)}, u32[]{:S(2)}, u32[]{:S(2)}) collective-permute-start(f32[16,8,128]{2,1,0:T(8,128)S(1)} %add_add_fusion), channel_id=1, source_target_pairs={{0,1},{1,0},{2,3},{3,2},{4,5},{5,4},{6,7},{7,6},{8,9},{9,8},{10,11... | collective-permute-start | bytes 196616 | tf_op jit(solution)/shard_map/ppermute | solution.py:38
  279.5 1.9 collective-permute-start.29
  283.6 4.6 %collective-permute-start.30 = (bf16[8,4096]{1,0:T(8,128)(2,1)S(1)}, bf16[8,4096]{1,0:T(8,128)(2,1)S(1)}, u32[]{:S(2)}, u32[]{:S(2)}) collective-permute-start(bf16[8,4096]{1,0:T(8,128)(2,1)S(1)} %slice.67), channel_id=1, source_target_pairs={{1,0},{2,1},{3,2},{4,3},{5,4},{6,5},{7,6},{8,7},{9,8},{10,9},{11,1... | collective-permute-start | bytes 196616 | tf_op jit(solution)/shard_map/ppermute | solution.py:26
  289.2 3.4 %collective-permute-done.30 = bf16[8,4096]{1,0:T(8,128)(2,1)S(1)} collective-permute-done((bf16[8,4096]{1,0:T(8,128)(2,1)S(1)}, bf16[8,4096]{1,0:T(8,128)(2,1)S(1)}, u32[]{:S(2)}, u32[]{:S(2)}) %collective-permute-start.30) | collective-permute-done | bytes 65568 | tf_op jit(solution)/shard_map/ppermute | solution.py:26
  294.1 3.2 %short_adjoint.2.refs_0_ = bf16[128,12288]{1,0:T(8,128)(2,1)} custom-call(bf16[1,128,4096]{2,1,0:T(8,128)(2,1)S(1)} %bitcast.51, bf16[1,8,4096]{2,1,0:T(8,128)(2,1)S(1)} %bitcast.52, f32[7,12288]{1,0:T(8,128)S(1)} %copy-done.1), custom_call_target="tpu_custom_call" | custom-call | flops 7340032 | bytes 2097152 | tf_op jit(solution)/shard_map/short_adjoint/pallas_call | solution.py:338
  297.3 6.8 %short_adjoint.3 = bf16[128,12288]{1,0:T(8,128)(2,1)} custom-call(bf16[2,128,4096]{2,1,0:T(8,128)(2,1)S(1)} %copy-done.10, bf16[2,8,4096]{2,1,0:T(8,128)(2,1)} %collective-permute-done.29.rim_ref, f32[7,12288]{1,0:T(8,128)S(1)} %copy-done.1, bf16[128,12288]{1,0:T(8,128)(2,1)} %short_adjoint.2.refs_0_), custom_call_target="tpu_custom_call", output_to_operand_aliasing={{}: (3, {})} | custom-call | flops 14680064 | bytes 4194304 | tf_op jit(solution)/shard_map/short_adjoint/pallas_call | solution.py:338
  304.1 2.0 collect.1
  (167 shorter events, 43.9 us)
Async XLA Ops:
  7.2 8.1 %copy-start = (bf16[1,128,12288]{2,1,0:T(8,128)(2,1)S(1)}, bf16[1,128,12288]{2,1,0:T(8,128)(2,1)}, u32[]{:S(2)}) copy-start(bf16[1,128,12288]{2,1,0:T(8,128)(2,1)} %param.5) | copy-start | bytes 9437188
  7.2 15.1 %copy-start.1 = (f32[7,12288]{1,0:T(8,128)S(1)}, f32[7,12288]{1,0:T(8,128)}, u32[]{:S(2)}) copy-start(f32[7,12288]{1,0:T(8,128)} %filter_ref.3) | copy-start | bytes 1032196
  7.2 130.6 %all-gather.2.cloned.1.call-start = ((), (), s32[]{:S(2)}) async-start(), calls=%async_computation.1 | async-start | bytes 9437184 | tf_op jit(solution)/shard_map/all_gather | solution.py:603
  11.7 21.8 %collective-permute-start.1 = (bf16[1024,256]{0,1:T(8,128)(2,1)}, bf16[1024,256]{0,1:T(8,128)(2,1)S(1)}, u32[]{:S(2)}, u32[]{:S(2)}) collective-permute-start(bf16[1024,256]{0,1:T(8,128)(2,1)} %bitcast.56), channel_id=1, source_target_pairs={{0,8},{8,0},{1,9},{9,1},{2,10},{10,2},{3,11},{11,3},{4,12},{12,4},... | collective-permute-start | bytes 1572872 | tf_op jit(solution)/shard_map/ppermute | solution.py:38
  15.3 7.0 %collective-permute-start = (bf16[8,12288]{1,0:T(8,128)(2,1)S(1)}, bf16[8,12288]{1,0:T(8,128)(2,1)S(1)}, u32[]{:S(2)}, u32[]{:S(2)}) collective-permute-start(bf16[8,12288]{1,0:T(8,128)(2,1)S(1)} %slice_bitcast_fusion), channel_id=1, source_target_pairs={{0,1},{1,2},{2,3},{3,4},{4,5},{5,6},{6,7},{7,8},{8,9},{9,10},{10,1... | collective-permute-start | bytes 589832 | tf_op jit(solution)/shard_map/ppermute | solution.py:26
  22.2 8.3 %copy-start.3 = (bf16[8,12288]{1,0:T(8,128)(2,1)}, bf16[8,12288]{1,0:T(8,128)(2,1)S(1)}, u32[]{:S(2)}) copy-start(bf16[8,12288]{1,0:T(8,128)(2,1)S(1)} %collective-permute-done.refs_3_.refs_4_.refs_5_.key_rim_ref.value_rim_ref.rim_ref) | copy-start | bytes 589828
  22.3 16.4 %copy-start.46 = (bf16[512,256]{1,0:T(8,128)(2,1)S(1)}, bf16[512,256]{1,0:T(8,128)(2,1)}, u32[]{:S(2)}) copy-start(bf16[512,256]{1,0:T(8,128)(2,1)} %param.8) | copy-start | bytes 786436
  34.3 20.9 %collective-permute-start.2 = (bf16[128,4096]{1,0:T(8,128)(2,1)}, bf16[128,4096]{1,0:T(8,128)(2,1)}, u32[]{:S(2)}, u32[]{:S(2)}) collective-permute-start(bf16[128,4096]{1,0:T(8,128)(2,1)} %get-tuple-element.45.cur_ref), channel_id=1, source_target_pairs={{0,1},{1,2},{2,3},{3,4},{4,5},{5,6},{6,7},{7,8},{8,9},{9,10},{10,1... | collective-permute-start | bytes 3145736 | tf_op jit(solution)/shard_map/ppermute | solution.py:26
  39.5 6.6 %collective-permute-start.5 = (bf16[256,256]{1,0:T(8,128)(2,1)}, bf16[256,256]{1,0:T(8,128)(2,1)}, u32[]{:S(2)}, u32[]{:S(2)}) collective-permute-start(bf16[256,256]{1,0:T(8,128)(2,1)} %get-tuple-element.102), channel_id=1, source_target_pairs={{0,24},{8,16},{16,8},{24,0},{1,25},{9,17},{17,9},{25,1},{2,26},{10... | collective-permute-start | bytes 393224 | tf_op jit(solution)/shard_map/ppermute | solution.py:38
  40.4 7.4 %collective-permute-start.4 = (bf16[256,256]{1,0:T(8,128)(2,1)}, bf16[256,256]{1,0:T(8,128)(2,1)}, u32[]{:S(2)}, u32[]{:S(2)}) collective-permute-start(bf16[256,256]{1,0:T(8,128)(2,1)} %get-tuple-element.102), channel_id=1, source_target_pairs={{0,16},{16,0},{1,17},{17,1},{2,18},{18,2},{3,19},{19,3},{4,20},{20... | collective-permute-start | bytes 393224 | tf_op jit(solution)/shard_map/ppermute | solution.py:38
  40.4 8.7 %collective-permute-start.3 = (bf16[256,256]{1,0:T(8,128)(2,1)}, bf16[256,256]{1,0:T(8,128)(2,1)}, u32[]{:S(2)}, u32[]{:S(2)}) collective-permute-start(bf16[256,256]{1,0:T(8,128)(2,1)} %get-tuple-element.102), channel_id=1, source_target_pairs={{0,8},{8,0},{1,9},{9,1},{2,10},{10,2},{3,11},{11,3},{4,12},{12,4},... | collective-permute-start | bytes 393224 | tf_op jit(solution)/shard_map/ppermute | solution.py:38
  43.4 11.9 %copy-start.7 = (bf16[128,4096]{1,0:T(8,128)(2,1)S(1)}, bf16[128,4096]{1,0:T(8,128)(2,1)}, u32[]{:S(2)}) copy-start(bf16[128,4096]{1,0:T(8,128)(2,1)} %copy-done.6) | copy-start | bytes 3145732
  43.4 7.7 %collective-permute-start.8 = (bf16[256,256]{1,0:T(8,128)(2,1)}, bf16[256,256]{1,0:T(8,128)(2,1)S(1)}, u32[]{:S(2)}, u32[]{:S(2)}) collective-permute-start(bf16[256,256]{1,0:T(8,128)(2,1)} %get-tuple-element.101), channel_id=1, source_target_pairs={{0,96},{32,0},{64,32},{96,64},{1,97},{33,1},{65,33},{97,65},{2,98}... | collective-permute-start | bytes 393224 | tf_op jit(solution)/shard_map/ppermute | solution.py:38
  46.1 5.5 %collective-permute-start.7 = (bf16[256,256]{1,0:T(8,128)(2,1)}, bf16[256,256]{1,0:T(8,128)(2,1)S(1)}, u32[]{:S(2)}, u32[]{:S(2)}) collective-permute-start(bf16[256,256]{1,0:T(8,128)(2,1)} %get-tuple-element.101), channel_id=1, source_target_pairs={{0,64},{32,96},{64,0},{96,32},{1,65},{33,97},{65,1},{97,33},{2,66}... | collective-permute-start | bytes 393224 | tf_op jit(solution)/shard_map/ppermute | solution.py:38
  47.8 5.7 %collective-permute-start.6 = (bf16[256,256]{1,0:T(8,128)(2,1)}, bf16[256,256]{1,0:T(8,128)(2,1)S(1)}, u32[]{:S(2)}, u32[]{:S(2)}) collective-permute-start(bf16[256,256]{1,0:T(8,128)(2,1)} %get-tuple-element.101), channel_id=1, source_target_pairs={{0,32},{32,64},{64,96},{96,0},{1,33},{33,65},{65,97},{97,1},{2,34}... | collective-permute-start | bytes 393224 | tf_op jit(solution)/shard_map/ppermute | solution.py:38
  49.0 16.8 %copy-start.14 = (f32[256,128]{1,0:T(8,128)}, f32[256,128]{1,0:T(8,128)S(1)}, u32[]{:S(2)}) copy-start(f32[256,128]{1,0:T(8,128)S(1)} %convert_element_type.63.lines_ref) | copy-start | bytes 393220
  67.8 140.9 %reduce-scatter.2.cloned.1.call-start = ((), (), s32[]{:S(2)}) async-start(), calls=%async_computation.2 | async-start | bytes 9437184 | tf_op jit(solution)/shard_map/reduce_scatter | solution.py:608
  67.9 15.1 %collective-permute-start.9 = (bf16[4,256,256]{2,1,0:T(8,128)(2,1)}, bf16[4,256,256]{2,1,0:T(8,128)(2,1)S(1)}, u32[]{:S(2)}, u32[]{:S(2)}) collective-permute-start(bf16[4,256,256]{2,1,0:T(8,128)(2,1)} %pad_maximum_fusion.1.refs_1_.refs_2_), channel_id=1, source_target_pairs={{0,32},{32,64},{64,96},{96,0},{1,33},{33,65},{65,97},{97,1},{2,34}... | collective-permute-start | bytes 1572872 | tf_op jit(solution)/shard_map/ppermute | solution.py:38
  68.0 23.6 %collective-permute-start.10 = (bf16[4,256,256]{2,1,0:T(8,128)(2,1)}, bf16[4,256,256]{2,1,0:T(8,128)(2,1)}, u32[]{:S(2)}, u32[]{:S(2)}) collective-permute-start(bf16[4,256,256]{2,1,0:T(8,128)(2,1)} %pad_maximum_fusion.1.refs_1_.refs_2_), channel_id=1, source_target_pairs={{0,64},{32,96},{64,0},{96,32},{1,65},{33,97},{65,1},{97,33},{2,66}... | collective-permute-start | bytes 1572872 | tf_op jit(solution)/shard_map/ppermute | solution.py:38
  69.1 22.4 %collective-permute-start.11 = (bf16[4,256,256]{2,1,0:T(8,128)(2,1)}, bf16[4,256,256]{2,1,0:T(8,128)(2,1)}, u32[]{:S(2)}, u32[]{:S(2)}) collective-permute-start(bf16[4,256,256]{2,1,0:T(8,128)(2,1)} %pad_maximum_fusion.1.refs_1_.refs_2_), channel_id=1, source_target_pairs={{0,96},{32,0},{64,32},{96,64},{1,97},{33,1},{65,33},{97,65},{2,98}... | collective-permute-start | bytes 1572872 | tf_op jit(solution)/shard_map/ppermute | solution.py:38
  71.1 20.4 %collective-permute-start.12 = (bf16[4,256,256]{2,1,0:T(8,128)(2,1)}, bf16[4,256,256]{2,1,0:T(8,128)(2,1)}, u32[]{:S(2)}, u32[]{:S(2)}) collective-permute-start(bf16[4,256,256]{2,1,0:T(8,128)(2,1)} %pad_maximum_fusion.2.refs_5_.refs_6_), channel_id=1, source_target_pairs={{0,8},{8,0},{1,9},{9,1},{2,10},{10,2},{3,11},{11,3},{4,12},{12,4},... | collective-permute-start | bytes 1572872 | tf_op jit(solution)/shard_map/ppermute | solution.py:38
  71.1 20.4 %collective-permute-start.13 = (bf16[4,256,256]{2,1,0:T(8,128)(2,1)}, bf16[4,256,256]{2,1,0:T(8,128)(2,1)}, u32[]{:S(2)}, u32[]{:S(2)}) collective-permute-start(bf16[4,256,256]{2,1,0:T(8,128)(2,1)} %pad_maximum_fusion.2.refs_5_.refs_6_), channel_id=1, source_target_pairs={{0,16},{16,0},{1,17},{17,1},{2,18},{18,2},{3,19},{19,3},{4,20},{20... | collective-permute-start | bytes 1572872 | tf_op jit(solution)/shard_map/ppermute | solution.py:38
  83.9 15.2 %collective-permute-start.14 = (bf16[4,256,256]{2,1,0:T(8,128)(2,1)}, bf16[4,256,256]{2,1,0:T(8,128)(2,1)}, u32[]{:S(2)}, u32[]{:S(2)}) collective-permute-start(bf16[4,256,256]{2,1,0:T(8,128)(2,1)} %pad_maximum_fusion.2.refs_5_.refs_6_), channel_id=1, source_target_pairs={{0,24},{8,16},{16,8},{24,0},{1,25},{9,17},{17,9},{25,1},{2,26},{10... | collective-permute-start | bytes 1572872 | tf_op jit(solution)/shard_map/ppermute | solution.py:38
  110.0 3.3 %copy-start.2 = (bf16[1024,4096]{1,0:T(8,128)(2,1)}, bf16[1024,4096]{1,0:T(8,128)(2,1)S(1)}, u32[]{:S(2)}) copy-start(bf16[1024,4096]{1,0:T(8,128)(2,1)S(1)} %gate_matmul.1) | copy-start | bytes 25165828
  161.6 14.8 %collective-permute-start.23 = (bf16[4,256,256]{2,1,0:T(8,128)(2,1)}, bf16[4,256,256]{2,1,0:T(8,128)(2,1)}, u32[]{:S(2)}, u32[]{:S(2)}) collective-permute-start(bf16[4,256,256]{2,1,0:T(8,128)(2,1)} %get-tuple-element.61), channel_id=1, source_target_pairs={{0,24},{8,16},{16,8},{24,0},{1,25},{9,17},{17,9},{25,1},{2,26},{10... | collective-permute-start | bytes 1572872 | tf_op jit(solution)/shard_map/ppermute | solution.py:38
  164.1 14.9 %collective-permute-start.22 = (bf16[4,256,256]{2,1,0:T(8,128)(2,1)}, bf16[4,256,256]{2,1,0:T(8,128)(2,1)}, u32[]{:S(2)}, u32[]{:S(2)}) collective-permute-start(bf16[4,256,256]{2,1,0:T(8,128)(2,1)} %get-tuple-element.60), channel_id=1, source_target_pairs={{0,16},{16,0},{1,17},{17,1},{2,18},{18,2},{3,19},{19,3},{4,20},{20... | collective-permute-start | bytes 1572872 | tf_op jit(solution)/shard_map/ppermute | solution.py:38
  164.1 24.5 %collective-permute-start.21 = (bf16[4,256,256]{2,1,0:T(8,128)(2,1)}, bf16[4,256,256]{2,1,0:T(8,128)(2,1)}, u32[]{:S(2)}, u32[]{:S(2)}) collective-permute-start(bf16[4,256,256]{2,1,0:T(8,128)(2,1)} %get-tuple-element.59), channel_id=1, source_target_pairs={{0,8},{8,0},{1,9},{9,1},{2,10},{10,2},{3,11},{11,3},{4,12},{12,4},... | collective-permute-start | bytes 1572872 | tf_op jit(solution)/shard_map/ppermute | solution.py:38
  165.5 29.8 %copy-start.29 = (bf16[4,256,256]{2,1,0:T(8,128)(2,1)S(1)}, bf16[4,256,256]{2,1,0:T(8,128)(2,1)}, u32[]{:S(2)}) copy-start(bf16[4,256,256]{2,1,0:T(8,128)(2,1)} %copy-done.28) | copy-start | bytes 1572868
  165.5 26.2 %collective-permute-start.17 = (bf16[4,256,256]{2,1,0:T(8,128)(2,1)}, bf16[4,256,256]{2,1,0:T(8,128)(2,1)S(1)}, u32[]{:S(2)}, u32[]{:S(2)}) collective-permute-start(bf16[4,256,256]{2,1,0:T(8,128)(2,1)} %copy-done.43), channel_id=1, source_target_pairs={{0,32},{32,64},{64,96},{96,0},{1,33},{33,65},{65,97},{97,1},{2,34}... | collective-permute-start | bytes 1572872 | tf_op jit(solution)/shard_map/ppermute | solution.py:38
  166.7 27.4 %collective-permute-start.16 = (bf16[4,256,256]{2,1,0:T(8,128)(2,1)}, bf16[4,256,256]{2,1,0:T(8,128)(2,1)S(1)}, u32[]{:S(2)}, u32[]{:S(2)}) collective-permute-start(bf16[4,256,256]{2,1,0:T(8,128)(2,1)} %copy-done.39), channel_id=1, source_target_pairs={{0,64},{32,96},{64,0},{96,32},{1,65},{33,97},{65,1},{97,33},{2,66}... | collective-permute-start | bytes 1572872 | tf_op jit(solution)/shard_map/ppermute | solution.py:38
  176.4 18.8 %collective-permute-start.15 = (bf16[4,256,256]{2,1,0:T(8,128)(2,1)}, bf16[4,256,256]{2,1,0:T(8,128)(2,1)S(1)}, u32[]{:S(2)}, u32[]{:S(2)}) collective-permute-start(bf16[4,256,256]{2,1,0:T(8,128)(2,1)} %copy-done.38), channel_id=1, source_target_pairs={{0,96},{32,0},{64,32},{96,64},{1,97},{33,1},{65,33},{97,65},{2,98}... | collective-permute-start | bytes 1572872 | tf_op jit(solution)/shard_map/ppermute | solution.py:38
  178.9 20.8 %collective-permute-start.27 = (bf16[1024,256]{1,0:T(8,128)(2,1)}, bf16[1024,256]{1,0:T(8,128)(2,1)S(1)}, u32[]{:S(2)}, u32[]{:S(2)}) collective-permute-start(bf16[1024,256]{1,0:T(8,128)(2,1)} %copy-done.37), channel_id=1, source_target_pairs={{0,8},{8,0},{1,9},{9,1},{2,10},{10,2},{3,11},{11,3},{4,12},{12,4},... | collective-permute-start | bytes 1572872 | tf_op jit(solution)/shard_map/ppermute | solution.py:38
  190.3 9.3 %copy-start.27 = (bf16[1024,256]{1,0:T(8,128)(2,1)S(1)}, bf16[1024,256]{1,0:T(8,128)(2,1)}, u32[]{:S(2)}) copy-start(bf16[1024,256]{1,0:T(8,128)(2,1)} %copy-done.26) | copy-start | bytes 1572868
  190.4 10.6 %collective-permute-start.26 = (bf16[256,256]{1,0:T(8,128)(2,1)S(1)}, bf16[256,256]{1,0:T(8,128)(2,1)S(1)}, u32[]{:S(2)}, u32[]{:S(2)}) collective-permute-start(bf16[256,256]{1,0:T(8,128)(2,1)S(1)} %get-tuple-element.94), channel_id=1, source_target_pairs={{0,32},{32,64},{64,96},{96,0},{1,33},{33,65},{65,97},{97,1},{2,34}... | collective-permute-start | bytes 393224 | tf_op jit(solution)/shard_map/ppermute | solution.py:38
  191.7 12.9 %collective-permute-start.25 = (bf16[256,256]{1,0:T(8,128)(2,1)S(1)}, bf16[256,256]{1,0:T(8,128)(2,1)S(1)}, u32[]{:S(2)}, u32[]{:S(2)}) collective-permute-start(bf16[256,256]{1,0:T(8,128)(2,1)S(1)} %get-tuple-element.95), channel_id=1, source_target_pairs={{0,64},{32,96},{64,0},{96,32},{1,65},{33,97},{65,1},{97,33},{2,66}... | collective-permute-start | bytes 393224 | tf_op jit(solution)/shard_map/ppermute | solution.py:38
  194.1 10.4 %collective-permute-start.24 = (bf16[256,256]{1,0:T(8,128)(2,1)S(1)}, bf16[256,256]{1,0:T(8,128)(2,1)S(1)}, u32[]{:S(2)}, u32[]{:S(2)}) collective-permute-start(bf16[256,256]{1,0:T(8,128)(2,1)S(1)} %get-tuple-element.93), channel_id=1, source_target_pairs={{0,96},{32,0},{64,32},{96,64},{1,97},{33,1},{65,33},{97,65},{2,98}... | collective-permute-start | bytes 393224 | tf_op jit(solution)/shard_map/ppermute | solution.py:38
  195.6 9.0 %collective-permute-start.20 = (bf16[256,256]{1,0:T(8,128)(2,1)S(1)}, bf16[256,256]{1,0:T(8,128)(2,1)S(1)}, u32[]{:S(2)}, u32[]{:S(2)}) collective-permute-start(bf16[256,256]{1,0:T(8,128)(2,1)S(1)} %get-tuple-element.91), channel_id=1, source_target_pairs={{0,24},{8,16},{16,8},{24,0},{1,25},{9,17},{17,9},{25,1},{2,26},{10... | collective-permute-start | bytes 393224 | tf_op jit(solution)/shard_map/ppermute | solution.py:38
  199.7 5.0 %collective-permute-start.19 = (bf16[256,256]{1,0:T(8,128)(2,1)S(1)}, bf16[256,256]{1,0:T(8,128)(2,1)S(1)}, u32[]{:S(2)}, u32[]{:S(2)}) collective-permute-start(bf16[256,256]{1,0:T(8,128)(2,1)S(1)} %get-tuple-element.92), channel_id=1, source_target_pairs={{0,16},{16,0},{1,17},{17,1},{2,18},{18,2},{3,19},{19,3},{4,20},{20... | collective-permute-start | bytes 393224 | tf_op jit(solution)/shard_map/ppermute | solution.py:38
  200.9 6.9 %collective-permute-start.18 = (bf16[256,256]{1,0:T(8,128)(2,1)S(1)}, bf16[256,256]{1,0:T(8,128)(2,1)S(1)}, u32[]{:S(2)}, u32[]{:S(2)}) collective-permute-start(bf16[256,256]{1,0:T(8,128)(2,1)S(1)} %get-tuple-element.90), channel_id=1, source_target_pairs={{0,8},{8,0},{1,9},{9,1},{2,10},{10,2},{3,11},{11,3},{4,12},{12,4},... | collective-permute-start | bytes 393224 | tf_op jit(solution)/shard_map/ppermute | solution.py:38
  217.0 19.1 %collective-permute-start.28 = (bf16[128,4096]{1,0:T(8,128)(2,1)}, bf16[128,4096]{1,0:T(8,128)(2,1)}, u32[]{:S(2)}, u32[]{:S(2)}) collective-permute-start(bf16[128,4096]{1,0:T(8,128)(2,1)} %get-tuple-element.67.grad_ref), channel_id=1, source_target_pairs={{1,0},{2,1},{3,2},{4,3},{5,4},{6,5},{7,6},{8,7},{9,8},{10,9},{11,1... | collective-permute-start | bytes 3145736 | tf_op jit(solution)/shard_map/ppermute | solution.py:26
  224.0 12.1 %copy-start.5 = (bf16[8,12288]{1,0:T(8,128)(2,1)S(1)}, bf16[8,12288]{1,0:T(8,128)(2,1)}, u32[]{:S(2)}) copy-start(bf16[8,12288]{1,0:T(8,128)(2,1)} %copy-done.3) | copy-start | bytes 589828
  224.0 12.1 %copy-start.15 = (f32[256,128]{1,0:T(8,128)S(1)}, f32[256,128]{1,0:T(8,128)}, u32[]{:S(2)}) copy-start(f32[256,128]{1,0:T(8,128)} %copy-done.14) | copy-start | bytes 393220
  224.0 12.1 %copy-start.23 = (bf16[128,4096]{1,0:T(8,128)(2,1)S(1)}, bf16[128,4096]{1,0:T(8,128)(2,1)}, u32[]{:S(2)}) copy-start(bf16[128,4096]{1,0:T(8,128)(2,1)} %copy-done.22) | copy-start | bytes 3145732
  224.1 12.1 %copy-start.25 = (bf16[128,4096]{1,0:T(8,128)(2,1)S(1)}, bf16[128,4096]{1,0:T(8,128)(2,1)}, u32[]{:S(2)}) copy-start(bf16[128,4096]{1,0:T(8,128)(2,1)} %copy-done.24) | copy-start | bytes 3145732
  250.1 28.7 %copy-start.9 = (bf16[2,128,4096]{2,1,0:T(8,128)(2,1)}, bf16[2,128,4096]{2,1,0:T(8,128)(2,1)S(1)}, u32[]{:S(2)}) copy-start(bf16[2,128,4096]{2,1,0:T(8,128)(2,1)S(1)} %get-tuple-element.70.grads_ref) | copy-start | bytes 6291460
  250.1 33.5 %copy-start.13 = (bf16[128,4096]{1,0:T(8,128)(2,1)S(1)}, bf16[128,4096]{1,0:T(8,128)(2,1)}, u32[]{:S(2)}) copy-start(bf16[128,4096]{1,0:T(8,128)(2,1)} %copy-done.11) | copy-start | bytes 3145732
  250.1 38.1 %copy-start.44 = (f32[512,256]{0,1:T(8,128)S(1)}, f32[512,256]{0,1:T(8,128)}, u32[]{:S(2)}) copy-start(f32[512,256]{0,1:T(8,128)} %maximum_bitcast_fusion) | copy-start | bytes 1572868
  250.8 1.6 collective-permute-start.31
  252.5 5.6 %collective-permute-start.34 = (f32[16,8,128]{2,1,0:T(8,128)S(1)}, f32[16,8,128]{2,1,0:T(8,128)S(1)}, u32[]{:S(2)}, u32[]{:S(2)}) collective-permute-start(f32[16,8,128]{2,1,0:T(8,128)S(1)} %get-tuple-element.97), channel_id=1, source_target_pairs={{0,6},{2,0},{4,2},{6,4},{1,7},{3,1},{5,3},{7,5},{8,14},{10,8},{12,... | collective-permute-start | bytes 196616 | tf_op jit(solution)/shard_map/ppermute | solution.py:38
  255.3 4.7 %collective-permute-start.33 = (f32[16,8,128]{2,1,0:T(8,128)S(1)}, f32[16,8,128]{2,1,0:T(8,128)S(1)}, u32[]{:S(2)}, u32[]{:S(2)}) collective-permute-start(f32[16,8,128]{2,1,0:T(8,128)S(1)} %get-tuple-element.98), channel_id=1, source_target_pairs={{0,4},{2,6},{4,0},{6,2},{1,5},{3,7},{5,1},{7,3},{8,12},{10,14},{12... | collective-permute-start | bytes 196616 | tf_op jit(solution)/shard_map/ppermute | solution.py:38
  255.3 6.4 %collective-permute-start.32 = (f32[16,8,128]{2,1,0:T(8,128)S(1)}, f32[16,8,128]{2,1,0:T(8,128)S(1)}, u32[]{:S(2)}, u32[]{:S(2)}) collective-permute-start(f32[16,8,128]{2,1,0:T(8,128)S(1)} %get-tuple-element.96), channel_id=1, source_target_pairs={{0,2},{2,4},{4,6},{6,0},{1,3},{3,5},{5,7},{7,1},{8,10},{10,12},{12... | collective-permute-start | bytes 196616 | tf_op jit(solution)/shard_map/ppermute | solution.py:38
  261.7 4.4 %collective-permute-start.36 = (f32[16,8,128]{2,1,0:T(8,128)S(1)}, f32[16,8,128]{2,1,0:T(8,128)S(1)}, u32[]{:S(2)}, u32[]{:S(2)}) collective-permute-start(f32[16,8,128]{2,1,0:T(8,128)S(1)} %fusion.5), channel_id=1, source_target_pairs={{0,32},{32,64},{64,96},{96,0},{1,33},{33,65},{65,97},{97,1},{2,34}... | collective-permute-start | bytes 196616 | tf_op jit(solution)/shard_map/ppermute | solution.py:38
  263.0 3.1 collective-permute-start.37
  264.4 4.6 %collective-permute-start.35 = (f32[16,8,128]{2,1,0:T(8,128)S(1)}, f32[16,8,128]{2,1,0:T(8,128)S(1)}, u32[]{:S(2)}, u32[]{:S(2)}) collective-permute-start(f32[16,8,128]{2,1,0:T(8,128)S(1)} %fusion.5), channel_id=1, source_target_pairs={{0,64},{32,96},{64,0},{96,32},{1,65},{33,97},{65,1},{97,33},{2,66}... | collective-permute-start | bytes 196616 | tf_op jit(solution)/shard_map/ppermute | solution.py:38
  269.1 4.7 %collective-permute-start.39 = (f32[16,8,128]{2,1,0:T(8,128)S(1)}, f32[16,8,128]{2,1,0:T(8,128)S(1)}, u32[]{:S(2)}, u32[]{:S(2)}) collective-permute-start(f32[16,8,128]{2,1,0:T(8,128)S(1)} %add_add_fusion.1), channel_id=1, source_target_pairs={{0,8},{8,0},{1,9},{9,1},{2,10},{10,2},{3,11},{11,3},{4,12},{12,4},... | collective-permute-start | bytes 196616 | tf_op jit(solution)/shard_map/ppermute | solution.py:38
  270.1 4.4 %collective-permute-start.40 = (f32[16,8,128]{2,1,0:T(8,128)S(1)}, f32[16,8,128]{2,1,0:T(8,128)S(1)}, u32[]{:S(2)}, u32[]{:S(2)}) collective-permute-start(f32[16,8,128]{2,1,0:T(8,128)S(1)} %add_add_fusion.1), channel_id=1, source_target_pairs={{0,24},{8,16},{16,8},{24,0},{1,25},{9,17},{17,9},{25,1},{2,26},{10... | collective-permute-start | bytes 196616 | tf_op jit(solution)/shard_map/ppermute | solution.py:38
  271.5 3.5 %collective-permute-start.38 = (f32[16,8,128]{2,1,0:T(8,128)S(1)}, f32[16,8,128]{2,1,0:T(8,128)S(1)}, u32[]{:S(2)}, u32[]{:S(2)}) collective-permute-start(f32[16,8,128]{2,1,0:T(8,128)S(1)} %add_add_fusion.1), channel_id=1, source_target_pairs={{0,16},{16,0},{1,17},{17,1},{2,18},{18,2},{3,19},{19,3},{4,20},{20... | collective-permute-start | bytes 196616 | tf_op jit(solution)/shard_map/ppermute | solution.py:38
  275.0 6.4 %collective-permute-start.41 = (f32[16,8,128]{2,1,0:T(8,128)S(1)}, f32[16,8,128]{2,1,0:T(8,128)S(1)}, u32[]{:S(2)}, u32[]{:S(2)}) collective-permute-start(f32[16,8,128]{2,1,0:T(8,128)S(1)} %add_add_fusion), channel_id=1, source_target_pairs={{0,1},{1,0},{2,3},{3,2},{4,5},{5,4},{6,7},{7,6},{8,9},{9,8},{10,11... | collective-permute-start | bytes 196616 | tf_op jit(solution)/shard_map/ppermute | solution.py:38
  279.5 17.8 %collective-permute-start.29 = (bf16[2,8,4096]{2,1,0:T(8,128)(2,1)}, bf16[2,8,4096]{2,1,0:T(8,128)(2,1)}, u32[]{:S(2)}, u32[]{:S(2)}) collective-permute-start(bf16[2,8,4096]{2,1,0:T(8,128)(2,1)} %slice.66), channel_id=1, source_target_pairs={{1,0},{2,1},{3,2},{4,3},{5,4},{6,5},{7,6},{8,7},{9,8},{10,9},{11,1... | collective-permute-start | bytes 393224 | tf_op jit(solution)/shard_map/ppermute | solution.py:26
  282.1 22.0 %collective-permute-start.42 = (f32[32,8,128]{2,1,0:T(8,128)}, f32[32,8,128]{2,1,0:T(8,128)}, u32[]{:S(2)}, u32[]{:S(2)}) collective-permute-start(f32[32,8,128]{2,1,0:T(8,128)} %pad_maximum_fusion.3.refs_0_), channel_id=1, source_target_pairs={{0,6},{2,0},{4,2},{6,4},{1,7},{3,1},{5,3},{7,5},{8,14},{10,8},{12,... | collective-permute-start | bytes 393224 | tf_op jit(solution)/shard_map/ppermute | solution.py:38
  282.4 21.7 %collective-permute-start.43 = (f32[32,8,128]{2,1,0:T(8,128)}, f32[32,8,128]{2,1,0:T(8,128)}, u32[]{:S(2)}, u32[]{:S(2)}) collective-permute-start(f32[32,8,128]{2,1,0:T(8,128)} %pad_maximum_fusion.3.refs_0_), channel_id=1, source_target_pairs={{0,4},{2,6},{4,0},{6,2},{1,5},{3,7},{5,1},{7,3},{8,12},{10,14},{12... | collective-permute-start | bytes 393224 | tf_op jit(solution)/shard_map/ppermute | solution.py:38
  282.9 21.2 %collective-permute-start.44 = (f32[32,8,128]{2,1,0:T(8,128)}, f32[32,8,128]{2,1,0:T(8,128)}, u32[]{:S(2)}, u32[]{:S(2)}) collective-permute-start(f32[32,8,128]{2,1,0:T(8,128)} %pad_maximum_fusion.3.refs_0_), channel_id=1, source_target_pairs={{0,2},{2,4},{4,6},{6,0},{1,3},{3,5},{5,7},{7,1},{8,10},{10,12},{12... | collective-permute-start | bytes 393224 | tf_op jit(solution)/shard_map/ppermute | solution.py:38
  283.6 9.0 %collective-permute-start.30 = (bf16[8,4096]{1,0:T(8,128)(2,1)S(1)}, bf16[8,4096]{1,0:T(8,128)(2,1)S(1)}, u32[]{:S(2)}, u32[]{:S(2)}) collective-permute-start(bf16[8,4096]{1,0:T(8,128)(2,1)S(1)} %slice.67), channel_id=1, source_target_pairs={{1,0},{2,1},{3,2},{4,3},{5,4},{6,5},{7,6},{8,7},{9,8},{10,9},{11,1... | collective-permute-start | bytes 196616 | tf_op jit(solution)/shard_map/ppermute | solution.py:26
  294.1 3.2 %copy-start.10 = (bf16[2,128,4096]{2,1,0:T(8,128)(2,1)S(1)}, bf16[2,128,4096]{2,1,0:T(8,128)(2,1)}, u32[]{:S(2)}) copy-start(bf16[2,128,4096]{2,1,0:T(8,128)(2,1)} %copy-done.9) | copy-start | bytes 6291460
  (30 other events, 29.3 us)
Sparse Core Ops, SparseCore 0:
  68.0 69.8 all-gather.1
  140.2 51.5 reduce-scatter.1

commit v5 on v4

--- a/solution.py
+++ b/solution.py
@@ -52,6 +52,19 @@
     return pltpu.CompilerParams(vmem_limit_bytes=mib * MIB)
 
 
+def hbm_call(kernel, *, out_shape, loose=(), **options):
+    single = not isinstance(out_shape, (list, tuple))
+    shapes = [out_shape] if single else out_shape
+    placed = [pltpu.HBM(x.shape, x.dtype) for x in shapes]
+    call = pl.pallas_call(kernel, out_shape=placed[0] if single else placed, **options)
+
+    def run(*args):
+        held = [x if i in loose else pltpu.with_memory_space_constraint(x, pltpu.HBM) for i, x in enumerate(args)]
+        return call(*held)
+
+    return run
+
+
 def cost(flops, moved):
     return pl.CostEstimate(flops=int(flops), bytes_accessed=int(moved), transcendentals=0)
 
@@ -94,8 +107,9 @@
         features_kernel(taps, refs[0:3], refs[3:6], refs[6:9], *refs[9:])
 
     out = jax.ShapeDtypeStruct((rows, channels), BF16)
-    return pl.pallas_call(
+    return hbm_call(
         body,
+        loose=(3, 4, 5),
         grid=(steps,),
         in_specs=[spec(rows, p) for p in range(3)]
         + [spec(RIM, p) for p in range(3)]
@@ -159,8 +173,9 @@
     width = channels // steps
     wide = pl.BlockSpec((rows, width), lambda i, place: (0, i))
     out = jax.ShapeDtypeStruct((rows, channels), BF16)
-    return pl.pallas_call(
+    return hbm_call(
         functools.partial(mix_kernel, per_group),
+        loose=(0, 1, 2),
         grid_spec=pltpu.PrefetchScalarGridSpec(
             num_scalar_prefetch=1,
             grid=(steps,),
@@ -187,8 +202,9 @@
     width = channels // steps
     wide = pl.BlockSpec((rows, width), lambda i, place: (0, i))
     out = jax.ShapeDtypeStruct((rows, channels), BF16)
-    return pl.pallas_call(
+    return hbm_call(
         gate_kernel,
+        loose=(0,),
         grid_spec=pltpu.PrefetchScalarGridSpec(
             num_scalar_prefetch=1,
             grid=(steps,),
@@ -248,7 +264,7 @@
     steps = channels // width
     wide = pl.BlockSpec((rows, width), lambda i: (0, i))
     packed = LANES // per_group
-    return pl.pallas_call(
+    return hbm_call(
         functools.partial(long_grad_kernel, per_group, short_taps),
         grid=(steps,),
         in_specs=[wide] * 5 + [pl.BlockSpec((RIM, width), lambda i: (0, i))],
@@ -303,8 +319,9 @@
     wide = spec(rows, 0)
     packed = LANES // per_group
     sums = jax.ShapeDtypeStruct((8, channels), F32)
-    return pl.pallas_call(
+    return hbm_call(
         functools.partial(unmix_kernel, per_group, short_taps),
+        loose=(0, 2),
         grid=(steps,),
         in_specs=[pl.BlockSpec((width // per_group, taps), lambda i: (i, 0))]
         + [wide] * 4
@@ -335,8 +352,9 @@
     steps = channels // width
     result = pl.BlockSpec((rows, width), lambda p, i: (0, (p + first) * steps + i))
     given = [] if out is None else [out]
-    return pl.pallas_call(
+    return hbm_call(
         functools.partial(short_adjoint_kernel, short_taps),
+        loose=(1,),
         grid=(parts, steps),
         in_specs=[
             pl.BlockSpec((1, rows, width), lambda p, i: (p, 0, i)),
@@ -480,8 +498,9 @@
     ny = len(tops)
     channels = 4 * ny * tops[0].shape[1]
     height = rows // 2
-    return pl.pallas_call(
+    return hbm_call(
         functools.partial(gate_matmul_kernel, ny),
+        loose=range(5 + ny),
         grid=(rows // height,),
         in_specs=[pl.BlockSpec((height, depth), lambda i: (i, 0))] + [whole(x) for x in (*tops, *bottoms)],
         out_specs=pl.BlockSpec((height, channels), lambda i: (i, 0)),
@@ -538,8 +557,9 @@
         + [jax.ShapeDtypeStruct((4, width, size), BF16)] * ny
         + [jax.ShapeDtypeStruct((ny, width, size), BF16)] * 4
     )
-    results = pl.pallas_call(
+    results = hbm_call(
         functools.partial(project_kernel, ny),
+        loose=range(1, 6 + ny),
         grid=(ny,),
         in_specs=[pl.BlockSpec((rows, channels // ny), lambda i: (0, i)), whole(turned)]
         + [whole(x) for x in (*tops, *bottoms)],
@@ -591,17 +611,16 @@
     collect_from = (z_step * 2 + core_step) * each + tile % each
 
     rim = along(tokens[rows - RIM :], 1)
+    lines = long_filter.astype(F32)
+    query, key, value, mixer = features_call(tokens, rim, short_filter)
+    mixer_prev = along(mixer, 1)
+    mixed, gated = mix_call(place, lines, mixer_prev, mixer, query)
+    gated, out_weight, upstream = lax.optimization_barrier((gated, out_weight, upstream))
+    all_rows = lax.all_gather(gated, ("z", "c"), axis=0, tiled=True)
+    wide_top, tall_bottom = gather_near(out_weight)
+    tops, bottoms = gather_far(wide_top, tall_bottom)
     mine = lax.dynamic_slice_in_dim(upstream, xh * span, span, 0)
     others = move(lax.dynamic_slice_in_dim(upstream, (1 - xh) * span, span, 0), xh=1)
-    query, key, value, mixer = features_call(tokens, rim, short_filter)
-    mixer, others, out_weight = lax.optimization_barrier((mixer, others, out_weight))
-    mixer_prev = along(mixer, 1)
-    wide_top, tall_bottom = gather_near(out_weight)
-    lines = long_filter.astype(F32)
-    mixed, gated = mix_call(place, lines, mixer_prev, mixer, query)
-    gated, wide_top, tall_bottom = lax.optimization_barrier((gated, wide_top, tall_bottom))
-    all_rows = lax.all_gather(gated, ("z", "c"), axis=0, tiled=True)
-    tops, bottoms = gather_far(wide_top, tall_bottom)
     cotangents = jnp.concatenate([mine, others], axis=1)
     partial = gate_matmul(cotangents, tops, bottoms)
     partial, all_rows = lax.optimization_barrier((partial, all_rows))

time: 315 us -> 297 us (0.943)
  local copies, waits for them, and re-layouts: 44 us -> 9.7 us
  starting transfers between devices: 75.8 us -> 90.7 us
  Pallas kernels: 81.4 us -> 93 us
  other arithmetic: 12.6 us -> 4.46 us
    unnamed x95 -> x30, local copies, waits for them, and re-layouts: 33.7 us -> 5.33 us
    ppermute x40, starting transfers between devices: 55.6 us -> 71.5 us  [move(): return lax.ppermute(x, axes, pairs)]
    reduce_scatter x1, waiting for transfers between devices: 0.01 us -> 14.5 us  [shards(): lax.psum_scatter(partial, ('z', 'c'), scatter_dimension=0, tiled=True)]
    all_gather x1, waiting for transfers between devices: 24.5 us -> 11 us  [shards(): all_rows = lax.all_gather(gated, ('z', 'c'), axis=0, tiled=True)]
    ppermute x40, waiting for transfers between devices: 54.1 us -> 41.5 us  [move(): return lax.ppermute(x, axes, pairs)]
    pallas_call x9, Pallas kernels: 78.6 us -> 90.8 us  [run(): return call(*held)]
    ppermute x5, waiting for transfers between devices: 5.95 us -> 16.8 us  [along(): return lax.ppermute(x, LINE, pairs)]
    dynamic_slice x2 -> x1, local copies, waits for them, and re-layouts: 4.44 us -> 0.07 us  [shards(): mine = lax.dynamic_slice_in_dim(upstream, xh * span, span, 0)]
  transfers between devices with their start and end apart: 47 -> 47, of which waited for: 20 -> 28; matrix products, arithmetic and copies ran while one was open for 6% -> 3% of each run, Pallas kernels for 16% -> 16%
where the time goes in v5:
time: 297 us; the launch traced here: 296 us
  Pallas kernels  93 us (31%)
  starting transfers between devices  90.7 us (31%)
  waiting for transfers between devices  83.9 us (28%)
  between operations  14.4 us (5%)
  local copies, waits for them, and re-layouts  9.7 us (3%)
  other arithmetic  4.46 us (2%)
    pallas_call x9, Pallas kernels, run(): return call(*held)  90.8 us
    ppermute x40, starting transfers between devices, move(): return lax.ppermute(x, axes, pairs)  71.5 us
    ppermute x40, waiting for transfers between devices, move(): return lax.ppermute(x, axes, pairs)  41.5 us
    ppermute x5, starting transfers between devices, along(): return lax.ppermute(x, LINE, pairs)  19.1 us
    ppermute x5, waiting for transfers between devices, along(): return lax.ppermute(x, LINE, pairs)  16.8 us
    reduce_scatter x1, waiting for transfers between devices, shards(): lax.psum_scatter(partial, ('z', 'c'), scatter_dimension=0, tiled=True)  14.5 us
    all_gather x1, waiting for transfers between devices, shards(): all_rows = lax.all_gather(gated, ('z', 'c'), axis=0, tiled=True)  11 us
  transfers between devices with their start and end apart: 47, of which 28 were waited for; matrix products, arithmetic and copies ran while one was open for 3% of the time, Pallas kernels for 16%

profile of v5, /device:TPU:1, one launch (start us, length us, event | category | flops | bytes accessed | tf_op | source)
XLA Modules:
  0.0 296.1 jit_solution(2130735418852249889)
XLA Ops:
  8.2 4.9 %collective-permute-start = (bf16[8,12288]{1,0:T(8,128)(2,1)S(1)}, bf16[8,12288]{1,0:T(8,128)(2,1)S(1)}, u32[]{:S(2)}, u32[]{:S(2)}) collective-permute-start(bf16[8,12288]{1,0:T(8,128)(2,1)S(1)} %slice_bitcast_fusion), channel_id=1, source_target_pairs={{0,1},{1,2},{2,3},{3,4},{4,5},{5,6},{6,7},{7,8},{8,9},{9,10},{10,1... | collective-permute-start | bytes 589832 | tf_op jit(solution)/shard_map/ppermute | solution.py:26
  13.1 2.6 collective-permute-done.refs_3_.refs_4_.refs_5_.key_rim_ref.value_rim_ref.rim_ref
  15.7 9.8 %features.1 = (bf16[128,4096]{1,0:T(8,128)(2,1)}, bf16[128,4096]{1,0:T(8,128)(2,1)}, bf16[128,4096]{1,0:T(8,128)(2,1)}, bf16[128,4096]{1,0:T(8,128)(2,1)}) custom-call(bf16[128,12288]{1,0:T(8,128)(2,1)} %bitcast.45, bf16[128,12288]{1,0:T(8,128)(2,1)} %bitcast.46, bf16[128,12288]{1,0:T(8,128)(2,1)} %bitcast.47, ...), custom_call_target="tpu_custom_call" | custom-call | bytes 1572864 | tf_op jit(solution)/shard_map/features/pallas_call | solution.py:63
  25.5 4.4 %collective-permute-start.1 = (bf16[128,4096]{1,0:T(8,128)(2,1)}, bf16[128,4096]{1,0:T(8,128)(2,1)S(1)}, u32[]{:S(2)}, u32[]{:S(2)}) collective-permute-start(bf16[128,4096]{1,0:T(8,128)(2,1)} %get-tuple-element.40.cur_ref), channel_id=1, source_target_pairs={{0,1},{1,2},{2,3},{3,4},{4,5},{5,6},{6,7},{7,8},{8,9},{9,10},{10,1... | collective-permute-start | bytes 3145736 | tf_op jit(solution)/shard_map/ppermute | solution.py:26
  30.6 11.3 %collective-permute-done.1.prev_ref = bf16[128,4096]{1,0:T(8,128)(2,1)S(1)} collective-permute-done((bf16[128,4096]{1,0:T(8,128)(2,1)}, bf16[128,4096]{1,0:T(8,128)(2,1)S(1)}, u32[]{:S(2)}, u32[]{:S(2)}) %collective-permute-start.1) | collective-permute-done | bytes 1048608 | tf_op jit(solution)/shard_map/ppermute | solution.py:26
  41.9 11.3 %mix.1 = (bf16[128,4096]{1,0:T(8,128)(2,1)}, bf16[128,4096]{1,0:T(8,128)(2,1)}) custom-call(s32[8]{0:T(128)S(1)} %fusion.6.place, f32[256,128]{1,0:T(8,128)S(1)} %convert_element_type.63.lines_ref, bf16[128,4096]{1,0:T(8,128)(2,1)S(1)} %collective-permute-done.1.prev_ref, bf16[128,4096]{1,0:T(8,128)(2,1)} %get-tuple-element.40.cur_ref, ...), custom_call_target="tpu_custom_call" | custom-call | bytes 1048576 | tf_op jit(solution)/shard_map/mix/pallas_call | solution.py:63
  53.3 2.6 collective-permute-start.5
  55.9 1.4 collective-permute-start.3
  57.3 1.7 collective-permute-start.2
  59.7 1.5 collective-permute-done.3
  61.3 1.4 collective-permute-start.6
  62.6 1.5 collective-permute-start.11
  64.1 1.6 collective-permute-start.10
  66.7 2.6 collective-permute-start.7
  69.4 4.2 %collective-permute-done.10 = bf16[256,256]{1,0:T(8,128)(2,1)S(1)} collective-permute-done((bf16[256,256]{1,0:T(8,128)(2,1)S(1)}, bf16[256,256]{1,0:T(8,128)(2,1)S(1)}, u32[]{:S(2)}, u32[]{:S(2)}) %collective-permute-start.10) | collective-permute-done | bytes 131104 | tf_op jit(solution)/shard_map/ppermute | solution.py:38
  73.8 1.3 collective-permute-start.12
  75.1 1.6 collective-permute-start.13
  78.4 1.1 fusion.15
  79.5 1.5 copy.12.refs_0_
  81.0 3.2 %collective-permute-done.7.refs_3_.refs_4_ = bf16[4,256,256]{2,1,0:T(8,128)(2,1)} collective-permute-done((bf16[4,256,256]{2,1,0:T(8,128)(2,1)S(1)}, bf16[4,256,256]{2,1,0:T(8,128)(2,1)}, u32[]{:S(2)}, u32[]{:S(2)}) %collective-permute-start.7) | collective-permute-done | bytes 524320 | tf_op jit(solution)/shard_map/ppermute | solution.py:38
  84.2 1.2 collective-permute-done.8.refs_4_.refs_5_
  85.4 3.9 %collective-permute-done.13.refs_7_.refs_8_ = bf16[4,256,256]{2,1,0:T(8,128)(2,1)} collective-permute-done((bf16[4,256,256]{2,1,0:T(8,128)(2,1)S(1)}, bf16[4,256,256]{2,1,0:T(8,128)(2,1)}, u32[]{:S(2)}, u32[]{:S(2)}) %collective-permute-start.13) | collective-permute-done | bytes 524320 | tf_op jit(solution)/shard_map/ppermute | solution.py:38
  90.5 8.5 %gate_matmul.1 = bf16[1024,4096]{1,0:T(8,128)(2,1)} custom-call(bf16[1024,512]{1,0:T(8,128)(2,1)S(1)} %copy.12.refs_0_, bf16[4,256,256]{2,1,0:T(8,128)(2,1)S(1)} %pad_maximum_fusion.1.refs_1_.refs_2_, bf16[4,256,256]{2,1,0:T(8,128)(2,1)S(1)} %copy-done.7, bf16[4,256,256]{2,1,0:T(8,128)(2,1)} %collective-permute-done.7.refs_3_.refs_4_, ...), custom_call_target="tpu_custom_call" | custom-call | flops 4294967296 | bytes 12582912 | tf_op jit(solution)/shard_map/gate_matmul/pallas_call | solution.py:63
  99.0 11.0 %all-gather.2.cloned.1.call-done.refs_0_ = bf16[1024,4096]{1,0:T(8,128)(2,1)} async-done(((bf16[128,4096]{1,0:T(8,128)(2,1)}), bf16[1024,4096]{1,0:T(8,128)(2,1)}) %all-gather.2.cloned.1.call-update) | async-done | bytes 8388624 | tf_op jit(solution)/shard_map/all_gather | solution.py:619
  110.0 15.1 %project.1 = (bf16[1024,256]{1,0:T(8,128)(2,1)}, bf16[1024,256]{1,0:T(8,128)(2,1)}, bf16[4,256,256]{2,1,0:T(8,128)(2,1)}, bf16[4,256,256]{2,1,0:T(8,128)(2,1)}, ...) custom-call(bf16[1024,4096]{1,0:T(8,128)(2,1)} %all-gather.2.cloned., ...), custom_call_target="tpu_custom_call" | custom-call | flops 8589934592 | bytes 16777216 | tf_op jit(solution)/shard_map/project/pallas_call | solution.py:63
  125.1 2.5 collective-permute-start.23
  127.6 1.4 collective-permute-start.21
  129.0 1.2 collective-permute-start.17
  130.2 2.4 collective-permute-start.16
  132.7 1.9 collective-permute-done.23
  134.6 3.5 %collective-permute-start.15 = (bf16[4,256,256]{2,1,0:T(8,128)(2,1)}, bf16[4,256,256]{2,1,0:T(8,128)(2,1)S(1)}, u32[]{:S(2)}, u32[]{:S(2)}) collective-permute-start(bf16[4,256,256]{2,1,0:T(8,128)(2,1)} %get-tuple-element.49), channel_id=1, source_target_pairs={{0,96},{32,0},{64,32},{96,64},{1,97},{33,1},{65,33},{97,65},{2,98}... | collective-permute-start | bytes 1572872 | tf_op jit(solution)/shard_map/ppermute | solution.py:38
  138.2 2.0 collective-permute-start.27
  140.2 5.2 %collective-permute-done.21 = bf16[4,256,256]{2,1,0:T(8,128)(2,1)S(1)} collective-permute-done((bf16[4,256,256]{2,1,0:T(8,128)(2,1)}, bf16[4,256,256]{2,1,0:T(8,128)(2,1)S(1)}, u32[]{:S(2)}, u32[]{:S(2)}) %collective-permute-start.21) | collective-permute-done | bytes 524320 | tf_op jit(solution)/shard_map/ppermute | solution.py:38
  145.4 1.3 add_convert_fusion
  146.8 2.0 collective-permute-start.26
  148.8 4.2 %collective-permute-start.25 = (bf16[256,256]{1,0:T(8,128)(2,1)S(1)}, bf16[256,256]{1,0:T(8,128)(2,1)S(1)}, u32[]{:S(2)}, u32[]{:S(2)}) collective-permute-start(bf16[256,256]{1,0:T(8,128)(2,1)S(1)} %get-tuple-element.89), channel_id=1, source_target_pairs={{0,64},{32,96},{64,0},{96,32},{1,65},{33,97},{65,1},{97,33},{2,66}... | collective-permute-start | bytes 393224 | tf_op jit(solution)/shard_map/ppermute | solution.py:38
  152.9 1.3 collective-permute-start.24
  154.6 2.6 collective-permute-start.20
  157.1 1.3 maximum_select_fusion
  158.4 1.7 collective-permute-done.26
  160.1 1.9 collective-permute-start.18
  162.1 2.9 collective-permute-done.20
  165.0 2.0 collective-permute-done.18
  167.1 14.5 %reduce-scatter.2.cloned.1.call-done.gate_grad_ref = bf16[128,4096]{1,0:T(8,128)(2,1)} async-done(((bf16[1024,4096]{1,0:T(8,128)(2,1)}), bf16[128,4096]{1,0:T(8,128)(2,1)}) %reduce-scatter.2.cloned.1.call-update) | async-done | bytes 1048592 | tf_op jit(solution)/shard_map/reduce_scatter | solution.py:627
  181.7 6.7 %gate_back.1 = (bf16[128,4096]{1,0:T(8,128)(2,1)}, bf16[128,4096]{1,0:T(8,128)(2,1)}) custom-call(s32[8]{0:T(128)S(1)} %fusion.6.place, bf16[128,4096]{1,0:T(8,128)(2,1)} %reduce-scatter.2.cloned.1.call-done.gate_grad_ref, bf16[128,4096]{1,0:T(8,128)(2,1)} %get-tuple-element.41.query_ref, bf16[128,4096]{1,0:T(8,128)(2,1)} %get-tuple-element.60.mixed_ref), custom_call_target="tpu_custom_call" | custom-call | flops 1048576 | bytes 5242880 | tf_op jit(solution)/shard_map/gate_back/pallas_call | solution.py:63
  188.3 3.5 %collective-permute-start.28 = (bf16[128,4096]{1,0:T(8,128)(2,1)}, bf16[128,4096]{1,0:T(8,128)(2,1)S(1)}, u32[]{:S(2)}, u32[]{:S(2)}) collective-permute-start(bf16[128,4096]{1,0:T(8,128)(2,1)} %get-tuple-element.61.grad_ref), channel_id=1, source_target_pairs={{1,0},{2,1},{3,2},{4,3},{5,4},{6,5},{7,6},{8,7},{9,8},{10,9},{11,1... | collective-permute-start | bytes 3145736 | tf_op jit(solution)/shard_map/ppermute | solution.py:26
  191.8 12.4 %long_grad.1 = (f32[256,128]{1,0:T(8,128)}, f32[8,4096]{1,0:T(8,128)}) custom-call(bf16[128,4096]{1,0:T(8,128)(2,1)} %copy-done.1, bf16[128,4096]{1,0:T(8,128)(2,1)} %get-tuple-element.40.cur_ref, bf16[128,4096]{1,0:T(8,128)(2,1)} %get-tuple-element.61.grad_ref, bf16[128,4096]{1,0:T(8,128)(2,1)} %get-tuple-element.65.feature_ref, ...), custom_call_target="tpu_custom_call" | custom-call | flops 2147483648 | bytes 5242880 | tf_op jit(solution)/shard_map/long_grad/pallas_call | solution.py:63
  204.7 14.9 %unmix.1 = (bf16[2,128,4096]{2,1,0:T(8,128)(2,1)}, f32[8,4096]{1,0:T(8,128)}, f32[8,4096]{1,0:T(8,128)}) custom-call(f32[256,128]{1,0:T(8,128)S(1)} %convert_element_type.63.lines_ref, bf16[128,4096]{1,0:T(8,128)(2,1)} %get-tuple-element.61.grad_ref, bf16[128,4096]{1,0:T(8,128)(2,1)S(1)} %collective-permute-done.28.next_ref, ...), custom_call_target="tpu_custom_call" | custom-call | flops 2147483648 | bytes 8388608 | tf_op jit(solution)/shard_map/unmix/pallas_call | solution.py:63
  222.2 1.5 collective-permute-done.31
  223.8 12.7 %collective-permute-start.34 = (f32[16,8,128]{2,1,0:T(8,128)S(1)}, f32[16,8,128]{2,1,0:T(8,128)S(1)}, u32[]{:S(2)}, u32[]{:S(2)}) collective-permute-start(f32[16,8,128]{2,1,0:T(8,128)S(1)} %get-tuple-element.91), channel_id=1, source_target_pairs={{0,6},{2,0},{4,2},{6,4},{1,7},{3,1},{5,3},{7,5},{8,14},{10,8},{12,... | collective-permute-start | bytes 196616 | tf_op jit(solution)/shard_map/ppermute | solution.py:38
  237.8 3.4 %collective-permute-done.33 = f32[16,8,128]{2,1,0:T(8,128)S(1)} collective-permute-done((f32[16,8,128]{2,1,0:T(8,128)S(1)}, f32[16,8,128]{2,1,0:T(8,128)S(1)}, u32[]{:S(2)}, u32[]{:S(2)}) %collective-permute-start.33) | collective-permute-done | bytes 65568 | tf_op jit(solution)/shard_map/ppermute | solution.py:38
  241.2 2.1 collective-permute-done.32
  244.2 1.9 collective-permute-start.37
  246.1 4.3 %collective-permute-start.35 = (f32[16,8,128]{2,1,0:T(8,128)S(1)}, f32[16,8,128]{2,1,0:T(8,128)S(1)}, u32[]{:S(2)}, u32[]{:S(2)}) collective-permute-start(f32[16,8,128]{2,1,0:T(8,128)S(1)} %fusion.5), channel_id=1, source_target_pairs={{0,64},{32,96},{64,0},{96,32},{1,65},{33,97},{65,1},{97,33},{2,66}... | collective-permute-start | bytes 196616 | tf_op jit(solution)/shard_map/ppermute | solution.py:38
  250.4 1.8 collective-permute-done.35
  252.6 2.6 collective-permute-start.40
  255.2 1.8 collective-permute-done.39
  258.4 3.8 %collective-permute-start.41 = (f32[16,8,128]{2,1,0:T(8,128)S(1)}, f32[16,8,128]{2,1,0:T(8,128)S(1)}, u32[]{:S(2)}, u32[]{:S(2)}) collective-permute-start(f32[16,8,128]{2,1,0:T(8,128)S(1)} %add_add_fusion), channel_id=1, source_target_pairs={{0,1},{1,0},{2,3},{3,2},{4,5},{5,4},{6,7},{7,6},{8,9},{9,8},{10,11... | collective-permute-start | bytes 196616 | tf_op jit(solution)/shard_map/ppermute | solution.py:38
  263.1 1.9 collective-permute-start.29
  267.6 4.4 %collective-permute-start.30 = (bf16[8,4096]{1,0:T(8,128)(2,1)S(1)}, bf16[8,4096]{1,0:T(8,128)(2,1)S(1)}, u32[]{:S(2)}, u32[]{:S(2)}) collective-permute-start(bf16[8,4096]{1,0:T(8,128)(2,1)S(1)} %slice.67), channel_id=1, source_target_pairs={{1,0},{2,1},{3,2},{4,3},{5,4},{6,5},{7,6},{8,7},{9,8},{10,9},{11,1... | collective-permute-start | bytes 196616 | tf_op jit(solution)/shard_map/ppermute | solution.py:26
  273.1 2.4 collective-permute-done.30
  275.5 4.5 %short_adjoint.2.refs_0_ = bf16[128,12288]{1,0:T(8,128)(2,1)} custom-call(bf16[1,128,4096]{2,1,0:T(8,128)(2,1)} %bitcast.53, bf16[1,8,4096]{2,1,0:T(8,128)(2,1)S(1)} %bitcast.44, f32[7,12288]{1,0:T(8,128)} %filter_ref.3), custom_call_target="tpu_custom_call" | custom-call | flops 7340032 | bytes 2097152 | tf_op jit(solution)/shard_map/short_adjoint/pallas_call | solution.py:63
  280.0 7.8 %short_adjoint.3 = bf16[128,12288]{1,0:T(8,128)(2,1)} custom-call(bf16[2,128,4096]{2,1,0:T(8,128)(2,1)} %get-tuple-element.64.grads_ref, bf16[2,8,4096]{2,1,0:T(8,128)(2,1)S(1)} %collective-permute-done.29.rim_ref, f32[7,12288]{1,0:T(8,128)} %filter_ref.3, bf16[128,12288]{1,0:T(8,128)(2,1)} %short_adjoint.2.refs_0_), custom_call_target="tpu_custom_call", output_to_operand_aliasing={{}: (3, {})} | custom-call | flops 14680064 | bytes 4194304 | tf_op jit(solution)/shard_map/short_adjoint/pallas_call | solution.py:63
  287.8 1.5 collect.1
  (100 shorter events, 18.7 us)
Async XLA Ops:
  7.2 102.8 %all-gather.2.cloned.1.call-start = ((), (), s32[]{:S(2)}) async-start(), calls=%async_computation.1 | async-start | bytes 9437184 | tf_op jit(solution)/shard_map/all_gather | solution.py:619
  8.2 7.5 %collective-permute-start = (bf16[8,12288]{1,0:T(8,128)(2,1)S(1)}, bf16[8,12288]{1,0:T(8,128)(2,1)S(1)}, u32[]{:S(2)}, u32[]{:S(2)}) collective-permute-start(bf16[8,12288]{1,0:T(8,128)(2,1)S(1)} %slice_bitcast_fusion), channel_id=1, source_target_pairs={{0,1},{1,2},{2,3},{3,4},{4,5},{5,6},{6,7},{7,8},{8,9},{9,10},{10,1... | collective-permute-start | bytes 589832 | tf_op jit(solution)/shard_map/ppermute | solution.py:26
  15.7 9.8 %copy-start = (bf16[8,12288]{1,0:T(8,128)(2,1)}, bf16[8,12288]{1,0:T(8,128)(2,1)S(1)}, u32[]{:S(2)}) copy-start(bf16[8,12288]{1,0:T(8,128)(2,1)S(1)} %collective-permute-done.refs_3_.refs_4_.refs_5_.key_rim_ref.value_rim_ref.rim_ref) | copy-start | bytes 589828
  15.7 14.2 %copy-start.13 = (bf16[256,128]{1,0:T(8,128)(2,1)S(1)}, bf16[256,128]{1,0:T(8,128)(2,1)}, u32[]{:S(2)}) copy-start(bf16[256,128]{1,0:T(8,128)(2,1)} %param.7) | copy-start | bytes 196612
  15.7 14.2 %copy-start.9 = (bf16[1,2048,256]{2,1,0:T(8,128)(2,1)S(1)}, bf16[1,2048,256]{2,1,0:T(8,128)(2,1)}, u32[]{:S(2)}) copy-start(bf16[1,2048,256]{2,1,0:T(8,128)(2,1)} %param.9) | copy-start | bytes 3145732
  25.5 16.4 %collective-permute-start.1 = (bf16[128,4096]{1,0:T(8,128)(2,1)}, bf16[128,4096]{1,0:T(8,128)(2,1)S(1)}, u32[]{:S(2)}, u32[]{:S(2)}) collective-permute-start(bf16[128,4096]{1,0:T(8,128)(2,1)} %get-tuple-element.40.cur_ref), channel_id=1, source_target_pairs={{0,1},{1,2},{2,3},{3,4},{4,5},{5,6},{6,7},{7,8},{8,9},{9,10},{10,1... | collective-permute-start | bytes 3145736 | tf_op jit(solution)/shard_map/ppermute | solution.py:26
  41.9 11.3 %copy-start.1 = (bf16[128,4096]{1,0:T(8,128)(2,1)}, bf16[128,4096]{1,0:T(8,128)(2,1)S(1)}, u32[]{:S(2)}) copy-start(bf16[128,4096]{1,0:T(8,128)(2,1)S(1)} %collective-permute-done.1.prev_ref) | copy-start | bytes 3145732
  41.9 11.3 %copy-start.12 = (bf16[512,256]{1,0:T(8,128)(2,1)S(1)}, bf16[512,256]{1,0:T(8,128)(2,1)}, u32[]{:S(2)}) copy-start(bf16[512,256]{1,0:T(8,128)(2,1)} %param.8) | copy-start | bytes 786436
  53.2 128.5 %reduce-scatter.2.cloned.1.call-start = ((), (), s32[]{:S(2)}) async-start(), calls=%async_computation.2 | async-start | bytes 9437184 | tf_op jit(solution)/shard_map/reduce_scatter | solution.py:627
  53.3 5.7 %collective-permute-start.5 = (bf16[256,256]{1,0:T(8,128)(2,1)S(1)}, bf16[256,256]{1,0:T(8,128)(2,1)S(1)}, u32[]{:S(2)}, u32[]{:S(2)}) collective-permute-start(bf16[256,256]{1,0:T(8,128)(2,1)S(1)} %get-tuple-element.96), channel_id=1, source_target_pairs={{0,24},{8,16},{16,8},{24,0},{1,25},{9,17},{17,9},{25,1},{2,26},{10... | collective-permute-start | bytes 393224 | tf_op jit(solution)/shard_map/ppermute | solution.py:38
  55.9 3.8 %collective-permute-start.4 = (bf16[256,256]{1,0:T(8,128)(2,1)S(1)}, bf16[256,256]{1,0:T(8,128)(2,1)S(1)}, u32[]{:S(2)}, u32[]{:S(2)}) collective-permute-start(bf16[256,256]{1,0:T(8,128)(2,1)S(1)} %get-tuple-element.96), channel_id=1, source_target_pairs={{0,16},{16,0},{1,17},{17,1},{2,18},{18,2},{3,19},{19,3},{4,20},{20... | collective-permute-start | bytes 393224 | tf_op jit(solution)/shard_map/ppermute | solution.py:38
  55.9 5.3 %collective-permute-start.3 = (bf16[256,256]{1,0:T(8,128)(2,1)S(1)}, bf16[256,256]{1,0:T(8,128)(2,1)S(1)}, u32[]{:S(2)}, u32[]{:S(2)}) collective-permute-start(bf16[256,256]{1,0:T(8,128)(2,1)S(1)} %get-tuple-element.96), channel_id=1, source_target_pairs={{0,8},{8,0},{1,9},{9,1},{2,10},{10,2},{3,11},{11,3},{4,12},{12,4},... | collective-permute-start | bytes 393224 | tf_op jit(solution)/shard_map/ppermute | solution.py:38
  57.3 17.8 %collective-permute-start.2 = (bf16[1024,256]{0,1:T(8,128)(2,1)S(1)}, bf16[1024,256]{0,1:T(8,128)(2,1)S(1)}, u32[]{:S(2)}, u32[]{:S(2)}) collective-permute-start(bf16[1024,256]{0,1:T(8,128)(2,1)S(1)} %get-tuple-element.83), channel_id=1, source_target_pairs={{0,8},{8,0},{1,9},{9,1},{2,10},{10,2},{3,11},{11,3},{4,12},{12,4},... | collective-permute-start | bytes 1572872 | tf_op jit(solution)/shard_map/ppermute | solution.py:38
  61.3 15.5 %collective-permute-start.6 = (bf16[4,256,256]{2,1,0:T(8,128)(2,1)S(1)}, bf16[4,256,256]{2,1,0:T(8,128)(2,1)S(1)}, u32[]{:S(2)}, u32[]{:S(2)}) collective-permute-start(bf16[4,256,256]{2,1,0:T(8,128)(2,1)S(1)} %pad_maximum_fusion.1.refs_1_.refs_2_), channel_id=1, source_target_pairs={{0,32},{32,64},{64,96},{96,0},{1,33},{33,65},{65,97},{97,1},{2,34}... | collective-permute-start | bytes 1572872 | tf_op jit(solution)/shard_map/ppermute | solution.py:38
  62.6 4.1 %collective-permute-start.11 = (bf16[256,256]{1,0:T(8,128)(2,1)S(1)}, bf16[256,256]{1,0:T(8,128)(2,1)S(1)}, u32[]{:S(2)}, u32[]{:S(2)}) collective-permute-start(bf16[256,256]{1,0:T(8,128)(2,1)S(1)} %get-tuple-element.95), channel_id=1, source_target_pairs={{0,96},{32,0},{64,32},{96,64},{1,97},{33,1},{65,33},{97,65},{2,98}... | collective-permute-start | bytes 393224 | tf_op jit(solution)/shard_map/ppermute | solution.py:38
  64.1 9.4 %collective-permute-start.10 = (bf16[256,256]{1,0:T(8,128)(2,1)S(1)}, bf16[256,256]{1,0:T(8,128)(2,1)S(1)}, u32[]{:S(2)}, u32[]{:S(2)}) collective-permute-start(bf16[256,256]{1,0:T(8,128)(2,1)S(1)} %get-tuple-element.95), channel_id=1, source_target_pairs={{0,64},{32,96},{64,0},{96,32},{1,65},{33,97},{65,1},{97,33},{2,66}... | collective-permute-start | bytes 393224 | tf_op jit(solution)/shard_map/ppermute | solution.py:38
  65.7 8.0 %collective-permute-start.9 = (bf16[256,256]{1,0:T(8,128)(2,1)S(1)}, bf16[256,256]{1,0:T(8,128)(2,1)S(1)}, u32[]{:S(2)}, u32[]{:S(2)}) collective-permute-start(bf16[256,256]{1,0:T(8,128)(2,1)S(1)} %get-tuple-element.95), channel_id=1, source_target_pairs={{0,32},{32,64},{64,96},{96,0},{1,33},{33,65},{65,97},{97,1},{2,34}... | collective-permute-start | bytes 393224 | tf_op jit(solution)/shard_map/ppermute | solution.py:38
  66.7 17.5 %collective-permute-start.7 = (bf16[4,256,256]{2,1,0:T(8,128)(2,1)S(1)}, bf16[4,256,256]{2,1,0:T(8,128)(2,1)}, u32[]{:S(2)}, u32[]{:S(2)}) collective-permute-start(bf16[4,256,256]{2,1,0:T(8,128)(2,1)S(1)} %pad_maximum_fusion.1.refs_1_.refs_2_), channel_id=1, source_target_pairs={{0,64},{32,96},{64,0},{96,32},{1,65},{33,97},{65,1},{97,33},{2,66}... | collective-permute-start | bytes 1572872 | tf_op jit(solution)/shard_map/ppermute | solution.py:38
  73.5 11.9 %collective-permute-start.8 = (bf16[4,256,256]{2,1,0:T(8,128)(2,1)S(1)}, bf16[4,256,256]{2,1,0:T(8,128)(2,1)}, u32[]{:S(2)}, u32[]{:S(2)}) collective-permute-start(bf16[4,256,256]{2,1,0:T(8,128)(2,1)S(1)} %pad_maximum_fusion.1.refs_1_.refs_2_), channel_id=1, source_target_pairs={{0,96},{32,0},{64,32},{96,64},{1,97},{33,1},{65,33},{97,65},{2,98}... | collective-permute-start | bytes 1572872 | tf_op jit(solution)/shard_map/ppermute | solution.py:38
  73.8 11.6 %collective-permute-start.12 = (bf16[4,256,256]{2,1,0:T(8,128)(2,1)S(1)}, bf16[4,256,256]{2,1,0:T(8,128)(2,1)}, u32[]{:S(2)}, u32[]{:S(2)}) collective-permute-start(bf16[4,256,256]{2,1,0:T(8,128)(2,1)S(1)} %pad_maximum_fusion.2.refs_5_.refs_6_), channel_id=1, source_target_pairs={{0,8},{8,0},{1,9},{9,1},{2,10},{10,2},{3,11},{11,3},{4,12},{12,4},... | collective-permute-start | bytes 1572872 | tf_op jit(solution)/shard_map/ppermute | solution.py:38
  75.1 14.2 %collective-permute-start.13 = (bf16[4,256,256]{2,1,0:T(8,128)(2,1)S(1)}, bf16[4,256,256]{2,1,0:T(8,128)(2,1)}, u32[]{:S(2)}, u32[]{:S(2)}) collective-permute-start(bf16[4,256,256]{2,1,0:T(8,128)(2,1)S(1)} %pad_maximum_fusion.2.refs_5_.refs_6_), channel_id=1, source_target_pairs={{0,16},{16,0},{1,17},{17,1},{2,18},{18,2},{3,19},{19,3},{4,20},{20... | collective-permute-start | bytes 1572872 | tf_op jit(solution)/shard_map/ppermute | solution.py:38
  76.8 0.8 copy-start.6
  77.6 11.9 %collective-permute-start.14 = (bf16[4,256,256]{2,1,0:T(8,128)(2,1)S(1)}, bf16[4,256,256]{2,1,0:T(8,128)(2,1)}, u32[]{:S(2)}, u32[]{:S(2)}) collective-permute-start(bf16[4,256,256]{2,1,0:T(8,128)(2,1)S(1)} %pad_maximum_fusion.2.refs_5_.refs_6_), channel_id=1, source_target_pairs={{0,24},{8,16},{16,8},{24,0},{1,25},{9,17},{17,9},{25,1},{2,26},{10... | collective-permute-start | bytes 1572872 | tf_op jit(solution)/shard_map/ppermute | solution.py:38
  89.4 1.1 copy-start.7
  99.0 11.1 %copy-start.8 = (bf16[4,256,256]{2,1,0:T(8,128)(2,1)S(1)}, bf16[4,256,256]{2,1,0:T(8,128)(2,1)}, u32[]{:S(2)}) copy-start(bf16[4,256,256]{2,1,0:T(8,128)(2,1)} %copy-done.6) | copy-start | bytes 1572868
  125.1 29.1 %copy-start.11 = (bf16[4,256,256]{2,1,0:T(8,128)(2,1)S(1)}, bf16[4,256,256]{2,1,0:T(8,128)(2,1)}, u32[]{:S(2)}) copy-start(bf16[4,256,256]{2,1,0:T(8,128)(2,1)} %get-tuple-element.48) | copy-start | bytes 1572868
  125.1 9.5 %collective-permute-start.23 = (bf16[4,256,256]{2,1,0:T(8,128)(2,1)}, bf16[4,256,256]{2,1,0:T(8,128)(2,1)S(1)}, u32[]{:S(2)}, u32[]{:S(2)}) collective-permute-start(bf16[4,256,256]{2,1,0:T(8,128)(2,1)} %get-tuple-element.55), channel_id=1, source_target_pairs={{0,24},{8,16},{16,8},{24,0},{1,25},{9,17},{17,9},{25,1},{2,26},{10... | collective-permute-start | bytes 1572872 | tf_op jit(solution)/shard_map/ppermute | solution.py:38
  127.6 10.6 %collective-permute-start.22 = (bf16[4,256,256]{2,1,0:T(8,128)(2,1)}, bf16[4,256,256]{2,1,0:T(8,128)(2,1)S(1)}, u32[]{:S(2)}, u32[]{:S(2)}) collective-permute-start(bf16[4,256,256]{2,1,0:T(8,128)(2,1)} %get-tuple-element.54), channel_id=1, source_target_pairs={{0,16},{16,0},{1,17},{17,1},{2,18},{18,2},{3,19},{19,3},{4,20},{20... | collective-permute-start | bytes 1572872 | tf_op jit(solution)/shard_map/ppermute | solution.py:38
  127.6 17.8 %collective-permute-start.21 = (bf16[4,256,256]{2,1,0:T(8,128)(2,1)}, bf16[4,256,256]{2,1,0:T(8,128)(2,1)S(1)}, u32[]{:S(2)}, u32[]{:S(2)}) collective-permute-start(bf16[4,256,256]{2,1,0:T(8,128)(2,1)} %get-tuple-element.53), channel_id=1, source_target_pairs={{0,8},{8,0},{1,9},{9,1},{2,10},{10,2},{3,11},{11,3},{4,12},{12,4},... | collective-permute-start | bytes 1572872 | tf_op jit(solution)/shard_map/ppermute | solution.py:38
  129.0 19.7 %collective-permute-start.17 = (bf16[4,256,256]{2,1,0:T(8,128)(2,1)}, bf16[4,256,256]{2,1,0:T(8,128)(2,1)S(1)}, u32[]{:S(2)}, u32[]{:S(2)}) collective-permute-start(bf16[4,256,256]{2,1,0:T(8,128)(2,1)} %get-tuple-element.51), channel_id=1, source_target_pairs={{0,32},{32,64},{64,96},{96,0},{1,33},{33,65},{65,97},{97,1},{2,34}... | collective-permute-start | bytes 1572872 | tf_op jit(solution)/shard_map/ppermute | solution.py:38
  130.2 22.7 %collective-permute-start.16 = (bf16[4,256,256]{2,1,0:T(8,128)(2,1)}, bf16[4,256,256]{2,1,0:T(8,128)(2,1)S(1)}, u32[]{:S(2)}, u32[]{:S(2)}) collective-permute-start(bf16[4,256,256]{2,1,0:T(8,128)(2,1)} %get-tuple-element.50), channel_id=1, source_target_pairs={{0,64},{32,96},{64,0},{96,32},{1,65},{33,97},{65,1},{97,33},{2,66}... | collective-permute-start | bytes 1572872 | tf_op jit(solution)/shard_map/ppermute | solution.py:38
  134.6 19.6 %collective-permute-start.15 = (bf16[4,256,256]{2,1,0:T(8,128)(2,1)}, bf16[4,256,256]{2,1,0:T(8,128)(2,1)S(1)}, u32[]{:S(2)}, u32[]{:S(2)}) collective-permute-start(bf16[4,256,256]{2,1,0:T(8,128)(2,1)} %get-tuple-element.49), channel_id=1, source_target_pairs={{0,96},{32,0},{64,32},{96,64},{1,97},{33,1},{65,33},{97,65},{2,98}... | collective-permute-start | bytes 1572872 | tf_op jit(solution)/shard_map/ppermute | solution.py:38
  138.2 19.0 %collective-permute-start.27 = (bf16[1024,256]{1,0:T(8,128)(2,1)}, bf16[1024,256]{1,0:T(8,128)(2,1)S(1)}, u32[]{:S(2)}, u32[]{:S(2)}) collective-permute-start(bf16[1024,256]{1,0:T(8,128)(2,1)} %get-tuple-element.57), channel_id=1, source_target_pairs={{0,8},{8,0},{1,9},{9,1},{2,10},{10,2},{3,11},{11,3},{4,12},{12,4},... | collective-permute-start | bytes 1572872 | tf_op jit(solution)/shard_map/ppermute | solution.py:38
  146.7 10.4 %copy-start.10 = (bf16[1024,256]{1,0:T(8,128)(2,1)S(1)}, bf16[1024,256]{1,0:T(8,128)(2,1)}, u32[]{:S(2)}) copy-start(bf16[1024,256]{1,0:T(8,128)(2,1)} %get-tuple-element.56) | copy-start | bytes 1572868
  146.8 13.3 %collective-permute-start.26 = (bf16[256,256]{1,0:T(8,128)(2,1)S(1)}, bf16[256,256]{1,0:T(8,128)(2,1)S(1)}, u32[]{:S(2)}, u32[]{:S(2)}) collective-permute-start(bf16[256,256]{1,0:T(8,128)(2,1)S(1)} %get-tuple-element.88), channel_id=1, source_target_pairs={{0,32},{32,64},{64,96},{96,0},{1,33},{33,65},{65,97},{97,1},{2,34}... | collective-permute-start | bytes 393224 | tf_op jit(solution)/shard_map/ppermute | solution.py:38
  148.8 13.2 %collective-permute-start.25 = (bf16[256,256]{1,0:T(8,128)(2,1)S(1)}, bf16[256,256]{1,0:T(8,128)(2,1)S(1)}, u32[]{:S(2)}, u32[]{:S(2)}) collective-permute-start(bf16[256,256]{1,0:T(8,128)(2,1)S(1)} %get-tuple-element.89), channel_id=1, source_target_pairs={{0,64},{32,96},{64,0},{96,32},{1,65},{33,97},{65,1},{97,33},{2,66}... | collective-permute-start | bytes 393224 | tf_op jit(solution)/shard_map/ppermute | solution.py:38
  152.9 9.1 %collective-permute-start.24 = (bf16[256,256]{1,0:T(8,128)(2,1)S(1)}, bf16[256,256]{1,0:T(8,128)(2,1)S(1)}, u32[]{:S(2)}, u32[]{:S(2)}) collective-permute-start(bf16[256,256]{1,0:T(8,128)(2,1)S(1)} %get-tuple-element.87), channel_id=1, source_target_pairs={{0,96},{32,0},{64,32},{96,64},{1,97},{33,1},{65,33},{97,65},{2,98}... | collective-permute-start | bytes 393224 | tf_op jit(solution)/shard_map/ppermute | solution.py:38
  154.6 10.4 %collective-permute-start.20 = (bf16[256,256]{1,0:T(8,128)(2,1)S(1)}, bf16[256,256]{1,0:T(8,128)(2,1)S(1)}, u32[]{:S(2)}, u32[]{:S(2)}) collective-permute-start(bf16[256,256]{1,0:T(8,128)(2,1)S(1)} %get-tuple-element.85), channel_id=1, source_target_pairs={{0,24},{8,16},{16,8},{24,0},{1,25},{9,17},{17,9},{25,1},{2,26},{10... | collective-permute-start | bytes 393224 | tf_op jit(solution)/shard_map/ppermute | solution.py:38
  157.1 7.8 %collective-permute-start.19 = (bf16[256,256]{1,0:T(8,128)(2,1)S(1)}, bf16[256,256]{1,0:T(8,128)(2,1)S(1)}, u32[]{:S(2)}, u32[]{:S(2)}) collective-permute-start(bf16[256,256]{1,0:T(8,128)(2,1)S(1)} %get-tuple-element.86), channel_id=1, source_target_pairs={{0,16},{16,0},{1,17},{17,1},{2,18},{18,2},{3,19},{19,3},{4,20},{20... | collective-permute-start | bytes 393224 | tf_op jit(solution)/shard_map/ppermute | solution.py:38
  160.1 6.9 %collective-permute-start.18 = (bf16[256,256]{1,0:T(8,128)(2,1)S(1)}, bf16[256,256]{1,0:T(8,128)(2,1)S(1)}, u32[]{:S(2)}, u32[]{:S(2)}) collective-permute-start(bf16[256,256]{1,0:T(8,128)(2,1)S(1)} %get-tuple-element.84), channel_id=1, source_target_pairs={{0,8},{8,0},{1,9},{9,1},{2,10},{10,2},{3,11},{11,3},{4,12},{12,4},... | collective-permute-start | bytes 393224 | tf_op jit(solution)/shard_map/ppermute | solution.py:38
  188.3 16.3 %collective-permute-start.28 = (bf16[128,4096]{1,0:T(8,128)(2,1)}, bf16[128,4096]{1,0:T(8,128)(2,1)S(1)}, u32[]{:S(2)}, u32[]{:S(2)}) collective-permute-start(bf16[128,4096]{1,0:T(8,128)(2,1)} %get-tuple-element.61.grad_ref), channel_id=1, source_target_pairs={{1,0},{2,1},{3,2},{4,3},{5,4},{6,5},{7,6},{8,7},{9,8},{10,9},{11,1... | collective-permute-start | bytes 3145736 | tf_op jit(solution)/shard_map/ppermute | solution.py:26
  204.7 14.9 %copy-start.2 = (f32[256,128]{1,0:T(8,128)S(1)}, f32[256,128]{1,0:T(8,128)}, u32[]{:S(2)}) copy-start(f32[256,128]{1,0:T(8,128)} %get-tuple-element.69.long_ref) | copy-start | bytes 393220
  204.7 14.9 %copy-start.3 = (f32[8,4096]{1,0:T(8,128)S(1)}, f32[8,4096]{1,0:T(8,128)}, u32[]{:S(2)}) copy-start(f32[8,4096]{1,0:T(8,128)} %get-tuple-element.66.query_ref) | copy-start | bytes 393220
  219.6 0.9 copy-start.4
  220.5 0.9 copy-start.5
  222.1 1.6 collective-permute-start.31
  223.8 14.1 %collective-permute-start.34 = (f32[16,8,128]{2,1,0:T(8,128)S(1)}, f32[16,8,128]{2,1,0:T(8,128)S(1)}, u32[]{:S(2)}, u32[]{:S(2)}) collective-permute-start(f32[16,8,128]{2,1,0:T(8,128)S(1)} %get-tuple-element.91), channel_id=1, source_target_pairs={{0,6},{2,0},{4,2},{6,4},{1,7},{3,1},{5,3},{7,5},{8,14},{10,8},{12,... | collective-permute-start | bytes 196616 | tf_op jit(solution)/shard_map/ppermute | solution.py:38
  236.5 4.7 %collective-permute-start.33 = (f32[16,8,128]{2,1,0:T(8,128)S(1)}, f32[16,8,128]{2,1,0:T(8,128)S(1)}, u32[]{:S(2)}, u32[]{:S(2)}) collective-permute-start(f32[16,8,128]{2,1,0:T(8,128)S(1)} %get-tuple-element.92), channel_id=1, source_target_pairs={{0,4},{2,6},{4,0},{6,2},{1,5},{3,7},{5,1},{7,3},{8,12},{10,14},{12... | collective-permute-start | bytes 196616 | tf_op jit(solution)/shard_map/ppermute | solution.py:38
  236.9 6.4 %collective-permute-start.32 = (f32[16,8,128]{2,1,0:T(8,128)S(1)}, f32[16,8,128]{2,1,0:T(8,128)S(1)}, u32[]{:S(2)}, u32[]{:S(2)}) collective-permute-start(f32[16,8,128]{2,1,0:T(8,128)S(1)} %get-tuple-element.90), channel_id=1, source_target_pairs={{0,2},{2,4},{4,6},{6,0},{1,3},{3,5},{5,7},{7,1},{8,10},{10,12},{12... | collective-permute-start | bytes 196616 | tf_op jit(solution)/shard_map/ppermute | solution.py:38
  243.3 7.1 %collective-permute-start.36 = (f32[16,8,128]{2,1,0:T(8,128)S(1)}, f32[16,8,128]{2,1,0:T(8,128)S(1)}, u32[]{:S(2)}, u32[]{:S(2)}) collective-permute-start(f32[16,8,128]{2,1,0:T(8,128)S(1)} %fusion.5), channel_id=1, source_target_pairs={{0,32},{32,64},{64,96},{96,0},{1,33},{33,65},{65,97},{97,1},{2,34}... | collective-permute-start | bytes 196616 | tf_op jit(solution)/shard_map/ppermute | solution.py:38
  244.2 6.2 %collective-permute-start.37 = (f32[16,8,128]{2,1,0:T(8,128)S(1)}, f32[16,8,128]{2,1,0:T(8,128)S(1)}, u32[]{:S(2)}, u32[]{:S(2)}) collective-permute-start(f32[16,8,128]{2,1,0:T(8,128)S(1)} %fusion.5), channel_id=1, source_target_pairs={{0,96},{32,0},{64,32},{96,64},{1,97},{33,1},{65,33},{97,65},{2,98}... | collective-permute-start | bytes 196616 | tf_op jit(solution)/shard_map/ppermute | solution.py:38
  246.1 6.2 %collective-permute-start.35 = (f32[16,8,128]{2,1,0:T(8,128)S(1)}, f32[16,8,128]{2,1,0:T(8,128)S(1)}, u32[]{:S(2)}, u32[]{:S(2)}) collective-permute-start(f32[16,8,128]{2,1,0:T(8,128)S(1)} %fusion.5), channel_id=1, source_target_pairs={{0,64},{32,96},{64,0},{96,32},{1,65},{33,97},{65,1},{97,33},{2,66}... | collective-permute-start | bytes 196616 | tf_op jit(solution)/shard_map/ppermute | solution.py:38
  252.3 4.8 %collective-permute-start.39 = (f32[16,8,128]{2,1,0:T(8,128)S(1)}, f32[16,8,128]{2,1,0:T(8,128)S(1)}, u32[]{:S(2)}, u32[]{:S(2)}) collective-permute-start(f32[16,8,128]{2,1,0:T(8,128)S(1)} %add_add_fusion.1), channel_id=1, source_target_pairs={{0,8},{8,0},{1,9},{9,1},{2,10},{10,2},{3,11},{11,3},{4,12},{12,4},... | collective-permute-start | bytes 196616 | tf_op jit(solution)/shard_map/ppermute | solution.py:38
  252.6 5.0 %collective-permute-start.40 = (f32[16,8,128]{2,1,0:T(8,128)S(1)}, f32[16,8,128]{2,1,0:T(8,128)S(1)}, u32[]{:S(2)}, u32[]{:S(2)}) collective-permute-start(f32[16,8,128]{2,1,0:T(8,128)S(1)} %add_add_fusion.1), channel_id=1, source_target_pairs={{0,24},{8,16},{16,8},{24,0},{1,25},{9,17},{17,9},{25,1},{2,26},{10... | collective-permute-start | bytes 196616 | tf_op jit(solution)/shard_map/ppermute | solution.py:38
  255.2 3.1 %collective-permute-start.38 = (f32[16,8,128]{2,1,0:T(8,128)S(1)}, f32[16,8,128]{2,1,0:T(8,128)S(1)}, u32[]{:S(2)}, u32[]{:S(2)}) collective-permute-start(f32[16,8,128]{2,1,0:T(8,128)S(1)} %add_add_fusion.1), channel_id=1, source_target_pairs={{0,16},{16,0},{1,17},{17,1},{2,18},{18,2},{3,19},{19,3},{4,20},{20... | collective-permute-start | bytes 196616 | tf_op jit(solution)/shard_map/ppermute | solution.py:38
  258.4 6.7 %collective-permute-start.41 = (f32[16,8,128]{2,1,0:T(8,128)S(1)}, f32[16,8,128]{2,1,0:T(8,128)S(1)}, u32[]{:S(2)}, u32[]{:S(2)}) collective-permute-start(f32[16,8,128]{2,1,0:T(8,128)S(1)} %add_add_fusion), channel_id=1, source_target_pairs={{0,1},{1,0},{2,3},{3,2},{4,5},{5,4},{6,7},{7,6},{8,9},{9,8},{10,11... | collective-permute-start | bytes 196616 | tf_op jit(solution)/shard_map/ppermute | solution.py:38
  263.1 16.9 %collective-permute-start.29 = (bf16[2,8,4096]{2,1,0:T(8,128)(2,1)S(1)}, bf16[2,8,4096]{2,1,0:T(8,128)(2,1)S(1)}, u32[]{:S(2)}, u32[]{:S(2)}) collective-permute-start(bf16[2,8,4096]{2,1,0:T(8,128)(2,1)S(1)} %slice.66), channel_id=1, source_target_pairs={{1,0},{2,1},{3,2},{4,3},{5,4},{6,5},{7,6},{8,7},{9,8},{10,9},{11,1... | collective-permute-start | bytes 393224 | tf_op jit(solution)/shard_map/ppermute | solution.py:26
  265.0 22.8 %collective-permute-start.42 = (f32[32,8,128]{2,1,0:T(8,128)S(1)}, f32[32,8,128]{2,1,0:T(8,128)S(1)}, u32[]{:S(2)}, u32[]{:S(2)}) collective-permute-start(f32[32,8,128]{2,1,0:T(8,128)S(1)} %pad_maximum_fusion.3.refs_0_), channel_id=1, source_target_pairs={{0,6},{2,0},{4,2},{6,4},{1,7},{3,1},{5,3},{7,5},{8,14},{10,8},{12,... | collective-permute-start | bytes 393224 | tf_op jit(solution)/shard_map/ppermute | solution.py:38
  265.7 22.1 %collective-permute-start.43 = (f32[32,8,128]{2,1,0:T(8,128)S(1)}, f32[32,8,128]{2,1,0:T(8,128)S(1)}, u32[]{:S(2)}, u32[]{:S(2)}) collective-permute-start(f32[32,8,128]{2,1,0:T(8,128)S(1)} %pad_maximum_fusion.3.refs_0_), channel_id=1, source_target_pairs={{0,4},{2,6},{4,0},{6,2},{1,5},{3,7},{5,1},{7,3},{8,12},{10,14},{12... | collective-permute-start | bytes 393224 | tf_op jit(solution)/shard_map/ppermute | solution.py:38
  266.0 21.8 %collective-permute-start.44 = (f32[32,8,128]{2,1,0:T(8,128)S(1)}, f32[32,8,128]{2,1,0:T(8,128)S(1)}, u32[]{:S(2)}, u32[]{:S(2)}) collective-permute-start(f32[32,8,128]{2,1,0:T(8,128)S(1)} %pad_maximum_fusion.3.refs_0_), channel_id=1, source_target_pairs={{0,2},{2,4},{4,6},{6,0},{1,3},{3,5},{5,7},{7,1},{8,10},{10,12},{12... | collective-permute-start | bytes 393224 | tf_op jit(solution)/shard_map/ppermute | solution.py:38
  267.6 7.9 %collective-permute-start.30 = (bf16[8,4096]{1,0:T(8,128)(2,1)S(1)}, bf16[8,4096]{1,0:T(8,128)(2,1)S(1)}, u32[]{:S(2)}, u32[]{:S(2)}) collective-permute-start(bf16[8,4096]{1,0:T(8,128)(2,1)S(1)} %slice.67), channel_id=1, source_target_pairs={{1,0},{2,1},{3,2},{4,3},{5,4},{6,5},{7,6},{8,7},{9,8},{10,9},{11,1... | collective-permute-start | bytes 196616 | tf_op jit(solution)/shard_map/ppermute | solution.py:26
Sparse Core Ops, SparseCore 0:
  53.3 56.6 all-gather.1
  112.4 69.2 reduce-scatter.1

commit v6 on v5

--- a/solution.py
+++ b/solution.py
@@ -12,6 +12,7 @@
 LANES = 128
 RIM = 8
 MIB = 1024 * 1024
+WIDTH = 1024
 F32 = jnp.float32
 BF16 = jnp.bfloat16
 
@@ -55,7 +56,7 @@
 def hbm_call(kernel, *, out_shape, loose=(), **options):
     single = not isinstance(out_shape, (list, tuple))
     shapes = [out_shape] if single else out_shape
-    placed = [pltpu.HBM(x.shape, x.dtype) for x in shapes]
+    placed = [pltpu.HBM(x.shape, x.dtype) if x.size * x.dtype.itemsize > 256 * 1024 else x for x in shapes]
     call = pl.pallas_call(kernel, out_shape=placed[0] if single else placed, **options)
 
     def run(*args):
@@ -76,28 +77,37 @@
     return width
 
 
-def features_kernel(short_taps, tokens, rims, filters, query_ref, key_ref, value_ref, mixer_ref):
-    rows = tokens[0].shape[0]
-
-    def filtered(part):
-        ext = jnp.concatenate([rims[part][...].astype(F32), tokens[part][...].astype(F32)], axis=0)
-        total = filters[part][0:1, :] * ext[RIM : RIM + rows]
+def extend(ext, rim, rows_of, at):
+    ext[0:RIM, :] = rim[:, at].astype(F32)
+    ext[RIM:, :] = rows_of.astype(F32)
+
+
+def features_kernel(short_taps, tokens, rims, filters, query_ref, key_ref, value_ref, mixer_ref, ext):
+    rows, width = tokens[0].shape
+
+    def filtered(part, block, at):
+        own = ext.at[(3 * block + part) % ext.shape[0]]
+        extend(own, rims[part], tokens[part][:, at], at)
+        taps = filters[part][:, at]
+        total = taps[0:1] * own[RIM : RIM + rows, :]
         for tap in range(1, short_taps):
-            total = total + filters[part][tap : tap + 1, :] * ext[RIM - tap : RIM - tap + rows]
+            total = total + taps[tap : tap + 1] * own[RIM - tap : RIM - tap + rows, :]
         return total
 
-    query_ref[...] = filtered(0).astype(BF16)
-    key, value = filtered(1), filtered(2)
-    key_ref[...] = key.astype(BF16)
-    value_ref[...] = value.astype(BF16)
-    mixer_ref[...] = (key * value).astype(BF16)
+    for block in range(width // LANES):
+        at = pl.ds(block * LANES, LANES)
+        query_ref[:, at] = filtered(0, block, at).astype(BF16)
+        key, value = filtered(1, block, at), filtered(2, block, at)
+        key_ref[:, at] = key.astype(BF16)
+        value_ref[:, at] = value.astype(BF16)
+        mixer_ref[:, at] = (key * value).astype(BF16)
 
 
 def features_call(tokens, rim, filters):
     rows, wide = tokens.shape
     channels = wide // 3
     taps = filters.shape[0]
-    width = block_width(channels, 512)
+    width = block_width(channels, WIDTH)
     steps = channels // width
 
     def spec(height, part):
@@ -116,6 +126,7 @@
         + [spec(taps, p) for p in range(3)],
         out_specs=[pl.BlockSpec((rows, width), lambda i: (0, i))] * 4,
         out_shape=[out] * 4,
+        scratch_shapes=[pltpu.VMEM((6, RIM + rows, LANES), F32)],
         compiler_params=params(),
         cost_estimate=cost(0, rows * wide),
         name="features",
@@ -130,7 +141,8 @@
 
 def mirror(size):
     row, lane = lane_row((size, size))
-    return jnp.where((row + lane) % size == 0, 1.0, 0.0)
+    both = row + lane
+    return jnp.where((both == 0) | (both == size), 1.0, 0.0)
 
 
 def circulant(line, taps):
@@ -139,77 +151,78 @@
 
 
 def pick_groups(product, rows, per_group):
-    lane = lax.broadcasted_iota(jnp.int32, (rows, LANES), 1) // per_group
+    lane = lax.broadcasted_iota(jnp.int32, (rows, LANES), 1)
     total = product[0:rows]
     for g in range(1, LANES // per_group):
-        total = jnp.where(lane == g, product[g * rows : (g + 1) * rows], total)
+        total = jnp.where(lane >= g * per_group, product[g * rows : (g + 1) * rows], total)
     return total
 
 
-def mix_kernel(per_group, place, lines_ref, prev_ref, cur_ref, query_ref, mixed_ref, gated_ref, table):
+def mix_kernel(per_group, lines_ref, prev_ref, cur_ref, query_ref, mixed_ref, gated_ref, table, lines):
     rows, width = cur_ref.shape
     row, lane = lane_row((rows, rows))
     above = lane > row
     packed = LANES // per_group
-    lines = jnp.dot(lines_ref[...].astype(BF16), mirror(rows).astype(BF16), preferred_element_type=F32)
+    lines[...] = jnp.dot(lines_ref[...].astype(BF16), mirror(rows).astype(BF16), preferred_element_type=F32)
     for block in range(width // LANES):
         at = pl.ds(block * LANES, LANES)
+        own = table.at[block % 2]
         for g in range(packed):
             ring = circulant(lines[block * packed + g : block * packed + g + 1, :], rows)
-            table[g * rows : (g + 1) * rows, 0:rows] = jnp.where(above, ring, 0.0).astype(BF16)
-            table[g * rows : (g + 1) * rows, rows : 2 * rows] = jnp.where(above, 0.0, ring).astype(BF16)
+            own[g * rows : (g + 1) * rows, 0:rows] = jnp.where(above, ring, 0.0).astype(BF16)
+            own[g * rows : (g + 1) * rows, rows : 2 * rows] = jnp.where(above, 0.0, ring).astype(BF16)
         window = jnp.concatenate([prev_ref[:, at], cur_ref[:, at]], axis=0)
-        product = jnp.dot(table[...], window, preferred_element_type=F32)
+        product = jnp.dot(own[...], window, preferred_element_type=F32)
         mixed = pick_groups(product, rows, per_group)
         mixed_ref[:, at] = mixed.astype(BF16)
         gated_ref[:, at] = (query_ref[:, at].astype(F32) * mixed).astype(BF16)
 
 
-def mix_call(place, lines, prev, cur, query):
+def mix_call(lines, prev, cur, query):
     rows, channels = cur.shape
     groups, taps = lines.shape
     per_group = channels // groups
-    steps = place.shape[0]
-    width = channels // steps
-    wide = pl.BlockSpec((rows, width), lambda i, place: (0, i))
+    width = block_width(channels, WIDTH)
+    steps = channels // width
+    wide = pl.BlockSpec((rows, width), lambda i: (0, i))
     out = jax.ShapeDtypeStruct((rows, channels), BF16)
     return hbm_call(
         functools.partial(mix_kernel, per_group),
-        loose=(0, 1, 2),
-        grid_spec=pltpu.PrefetchScalarGridSpec(
-            num_scalar_prefetch=1,
-            grid=(steps,),
-            in_specs=[pl.BlockSpec((width // per_group, taps), lambda i, place: (i, 0)), wide, wide, wide],
-            out_specs=[wide, pl.BlockSpec((rows, width), lambda i, place: (0, place[i]))],
-            scratch_shapes=[pltpu.VMEM((LANES // per_group * rows, 2 * rows), BF16)],
-        ),
+        loose=(0, 1),
+        grid=(steps,),
+        in_specs=[pl.BlockSpec((width // per_group, taps), lambda i: (i, 0)), wide, wide, wide],
+        out_specs=[wide, wide],
         out_shape=[out, out],
+        scratch_shapes=[
+            pltpu.VMEM((2, LANES // per_group * rows, 2 * rows), BF16),
+            pltpu.VMEM((width // per_group, taps), F32),
+        ],
         compiler_params=params(),
         cost_estimate=cost(0, 2 * rows * channels),
         name="mix",
-    )(place, lines, prev, cur, query)
+    )(lines, prev, cur, query)
 
 
 def gate_kernel(place, gate_grad_ref, query_ref, mixed_ref, grad_ref, feature_ref):
-    gate_grad = gate_grad_ref[...].astype(F32)
-    grad_ref[...] = (gate_grad * query_ref[...].astype(F32)).astype(BF16)
-    feature_ref[...] = (gate_grad * mixed_ref[...].astype(F32)).astype(BF16)
+    width = query_ref.shape[1] // place.shape[0]
+    for i in range(place.shape[0]):
+        at = pl.ds(i * width, width)
+        gate_grad = gate_grad_ref[:, pl.ds(pl.multiple_of(place[i] * width, width), width)].astype(F32)
+        grad_ref[:, at] = (gate_grad * query_ref[:, at].astype(F32)).astype(BF16)
+        feature_ref[:, at] = (gate_grad * mixed_ref[:, at].astype(F32)).astype(BF16)
 
 
 def gate_call(place, gate_grad, query, mixed):
     rows, channels = query.shape
-    steps = place.shape[0]
-    width = channels // steps
-    wide = pl.BlockSpec((rows, width), lambda i, place: (0, i))
     out = jax.ShapeDtypeStruct((rows, channels), BF16)
     return hbm_call(
         gate_kernel,
         loose=(0,),
         grid_spec=pltpu.PrefetchScalarGridSpec(
             num_scalar_prefetch=1,
-            grid=(steps,),
-            in_specs=[pl.BlockSpec((rows, width), lambda i, place: (0, place[i])), wide, wide],
-            out_specs=[wide, wide],
+            grid=(2,),
+            in_specs=[pl.BlockSpec((rows // 2, channels), lambda i, place: (i, 0))] * 3,
+            out_specs=[pl.BlockSpec((rows // 2, channels), lambda i, place: (i, 0))] * 2,
         ),
         out_shape=[out, out],
         compiler_params=params(),
@@ -218,49 +231,53 @@
     )(place, gate_grad, query, mixed)
 
 
-def tap_sums(short_taps, grads, tokens_ref, rim_ref, out_ref):
+def tap_sums(short_taps, grad, tokens_ref, rim_ref, out_ref, at, ext):
     rows = tokens_ref.shape[0]
-    ext = jnp.concatenate([rim_ref[...].astype(F32), tokens_ref[...].astype(F32)], axis=0)
+    extend(ext, rim_ref, tokens_ref[:, at], at)
+    grad = grad.astype(F32)
     for tap in range(short_taps):
-        out_ref[tap : tap + 1, :] = jnp.sum(grads * ext[RIM - tap : RIM - tap + rows], axis=0, keepdims=True)
-    out_ref[short_taps:8, :] = jnp.zeros((8 - short_taps, out_ref.shape[1]), F32)
+        out_ref[tap : tap + 1, at] = jnp.sum(grad * ext[RIM - tap : RIM - tap + rows, :], axis=0, keepdims=True)
+    out_ref[short_taps:8, at] = jnp.zeros((8 - short_taps, LANES), F32)
 
 
 def long_grad_kernel(
-    per_group, short_taps, prev_ref, cur_ref, grad_ref, feature_ref, tokens_ref, rim_ref, long_ref, short_ref, fold
+    per_group, short_taps, prev_ref, cur_ref, grad_ref, feature_ref, tokens_ref, rim_ref, long_ref, short_ref, fold, masked, ext
 ):
     rows, width = cur_ref.shape
     row, lane = lane_row((rows, rows))
     above = lane > row
-    member = lax.broadcasted_iota(jnp.int32, (rows, LANES), 1) // per_group
+    member = lax.broadcasted_iota(jnp.int32, (rows, LANES), 1)
     packed = LANES // per_group
     sums = []
     for block in range(width // LANES):
         at = pl.ds(block * LANES, LANES)
         window = jnp.concatenate([prev_ref[:, at], cur_ref[:, at]], axis=0)
         grad_wide = grad_ref[:, at].astype(F32)
+        own = masked.at[block % 2]
         for g in range(packed):
-            own = jnp.where(member == g, grad_wide, 0.0).astype(BF16)
-            pairs = lax.dot_general(own, window, (((1,), (1,)), ((), ())), preferred_element_type=F32)
-            ring = jnp.where(above, pairs[:, 0:rows], pairs[:, rows : 2 * rows])
+            own[g * rows : (g + 1) * rows, :] = jnp.where((member >= g * per_group) & (member < (g + 1) * per_group), grad_wide, 0.0).astype(BF16)
+        pairs = lax.dot_general(own[...], window, (((1,), (1,)), ((), ())), preferred_element_type=F32)
+        for g in range(packed):
+            pair = pairs[g * rows : (g + 1) * rows]
+            ring = jnp.where(above, pair[:, 0:rows], pair[:, rows : 2 * rows])
             total = ring[0:8]
             for tile in range(1, rows // 8):
                 total = total + pltpu.roll(ring[8 * tile : 8 * tile + 8], rows - 8 * tile, 1)
-            fold[g * 8 : (g + 1) * 8, :] = total
-        total = fold[pl.ds(0, packed, stride=8), :]
+            fold[block % 2, g * 8 : (g + 1) * 8, :] = total
+        total = fold[block % 2, pl.ds(0, packed, stride=8), :]
         for step in range(1, 8):
-            total = total + pltpu.roll(fold[pl.ds(step, packed, stride=8), :], rows - step, 1)
+            total = total + pltpu.roll(fold[block % 2, pl.ds(step, packed, stride=8), :], rows - step, 1)
         sums.append(total)
+        tap_sums(short_taps, feature_ref[:, at], tokens_ref, rim_ref, short_ref, at, ext.at[block % 2])
     long_ref[...] = jnp.dot(
         jnp.concatenate(sums, axis=0), mirror(rows), precision=lax.Precision.HIGHEST, preferred_element_type=F32
     )
-    tap_sums(short_taps, feature_ref[...].astype(F32), tokens_ref, rim_ref, short_ref)
 
 
 def long_grad_call(groups, short_taps, prev, cur, grad, feature, tokens, rim):
     rows, channels = cur.shape
     per_group = channels // groups
-    width = block_width(channels, 512)
+    width = block_width(channels, WIDTH)
     steps = channels // width
     wide = pl.BlockSpec((rows, width), lambda i: (0, i))
     packed = LANES // per_group
@@ -276,7 +293,11 @@
             jax.ShapeDtypeStruct((groups, rows), F32),
             jax.ShapeDtypeStruct((8, channels), F32),
         ],
-        scratch_shapes=[pltpu.VMEM((packed * 8, LANES), F32)],
+        scratch_shapes=[
+            pltpu.VMEM((2, packed * 8, LANES), F32),
+            pltpu.VMEM((2, packed * rows, LANES), BF16),
+            pltpu.VMEM((2, RIM + rows, LANES), F32),
+        ],
         compiler_params=params(),
         cost_estimate=cost(2 * groups * rows * 2 * rows * LANES, 10 * rows * channels),
         name="long_grad",
@@ -285,7 +306,7 @@
 
 def unmix_kernel(
     per_group, short_taps, lines_ref, grad_ref, next_ref, key_ref, value_ref, key_tokens_ref, value_tokens_ref,
-    key_rim_ref, value_rim_ref, feature_ref, key_sum_ref, value_sum_ref, table,
+    key_rim_ref, value_rim_ref, feature_ref, key_sum_ref, value_sum_ref, table, ext,
 ):
     rows, width = grad_ref.shape
     row, lane = lane_row((rows, rows))
@@ -293,24 +314,28 @@
     packed = LANES // per_group
     for block in range(width // LANES):
         at = pl.ds(block * LANES, LANES)
+        own = table.at[block % 2]
         for g in range(packed):
             ring = circulant(lines_ref[block * packed + g : block * packed + g + 1, :], rows)
-            table[g * rows : (g + 1) * rows, 0:rows] = jnp.where(below, 0.0, ring).astype(BF16)
-            table[g * rows : (g + 1) * rows, rows : 2 * rows] = jnp.where(below, ring, 0.0).astype(BF16)
+            own[g * rows : (g + 1) * rows, 0:rows] = jnp.where(below, 0.0, ring).astype(BF16)
+            own[g * rows : (g + 1) * rows, rows : 2 * rows] = jnp.where(below, ring, 0.0).astype(BF16)
         window = jnp.concatenate([grad_ref[:, at], next_ref[:, at]], axis=0)
-        product = jnp.dot(table[...], window, preferred_element_type=F32)
+        product = jnp.dot(own[...], window, preferred_element_type=F32)
         grad_mixer = pick_groups(product, rows, per_group)
-        feature_ref[0, :, at] = (grad_mixer * value_ref[:, at].astype(F32)).astype(BF16)
-        feature_ref[1, :, at] = (grad_mixer * key_ref[:, at].astype(F32)).astype(BF16)
-    tap_sums(short_taps, feature_ref[0].astype(F32), key_tokens_ref, key_rim_ref, key_sum_ref)
-    tap_sums(short_taps, feature_ref[1].astype(F32), value_tokens_ref, value_rim_ref, value_sum_ref)
+        key_grad = (grad_mixer * value_ref[:, at].astype(F32)).astype(BF16)
+        value_grad = (grad_mixer * key_ref[:, at].astype(F32)).astype(BF16)
+        feature_ref[0, :, at] = key_grad
+        feature_ref[1, :, at] = value_grad
+        slot = 2 * (block % 2)
+        tap_sums(short_taps, key_grad, key_tokens_ref, key_rim_ref, key_sum_ref, at, ext.at[slot])
+        tap_sums(short_taps, value_grad, value_tokens_ref, value_rim_ref, value_sum_ref, at, ext.at[slot + 1])
 
 
 def unmix_call(lines, short_taps, grad, grad_next, key, value, tokens, rim):
     rows, channels = grad.shape
     groups, taps = lines.shape
     per_group = channels // groups
-    width = block_width(channels, 512)
+    width = block_width(channels, WIDTH)
     steps = channels // width
 
     def spec(height, part):
@@ -328,7 +353,7 @@
         + [spec(rows, 1), spec(rows, 2), spec(RIM, 1), spec(RIM, 2)],
         out_specs=[pl.BlockSpec((2, rows, width), lambda i: (0, 0, i)), spec(8, 0), spec(8, 0)],
         out_shape=[jax.ShapeDtypeStruct((2, rows, channels), BF16), sums, sums],
-        scratch_shapes=[pltpu.VMEM((packed * rows, 2 * rows), BF16)],
+        scratch_shapes=[pltpu.VMEM((2, packed * rows, 2 * rows), BF16), pltpu.VMEM((4, RIM + rows, LANES), F32)],
         compiler_params=params(),
         cost_estimate=cost(2 * groups * rows * 2 * rows * LANES, 16 * rows * channels),
         name="unmix",
@@ -336,19 +361,24 @@
 
 
 def short_adjoint_kernel(short_taps, grads_ref, rim_ref, filter_ref, *refs):
-    out_ref = refs[-1]
-    rows = out_ref.shape[0]
-    ext = jnp.concatenate([grads_ref[0].astype(F32), rim_ref[0].astype(F32)], axis=0)
-    total = filter_ref[0:1, :] * ext[0:rows]
-    for tap in range(1, short_taps):
-        total = total + filter_ref[tap : tap + 1, :] * ext[tap : tap + rows]
-    out_ref[...] = total.astype(BF16)
+    out_ref, ext = refs[-2:]
+    rows, width = out_ref.shape
+    for block in range(width // LANES):
+        at = pl.ds(block * LANES, LANES)
+        own = ext.at[block % 2]
+        own[0:rows, :] = grads_ref[0, :, at].astype(F32)
+        own[rows:, :] = rim_ref[0, :, at].astype(F32)
+        taps = filter_ref[:, at]
+        total = taps[0:1] * own[0:rows, :]
+        for tap in range(1, short_taps):
+            total = total + taps[tap : tap + 1] * own[tap : tap + rows, :]
+        out_ref[:, at] = total.astype(BF16)
 
 
 def short_adjoint_call(grads, rim, filters, first, out):
     parts, rows, channels = grads.shape
     short_taps = filters.shape[0]
-    width = block_width(channels, 1024)
+    width = block_width(channels, 2 * WIDTH)
     steps = channels // width
     result = pl.BlockSpec((rows, width), lambda p, i: (0, (p + first) * steps + i))
     given = [] if out is None else [out]
@@ -365,6 +395,7 @@
         out_specs=result,
         out_shape=jax.ShapeDtypeStruct((rows, 3 * channels), BF16),
         input_output_aliases={3: 0} if given else {},
+        scratch_shapes=[pltpu.VMEM((2, rows + RIM, LANES), F32)],
         compiler_params=params(),
         cost_estimate=cost(2 * parts * short_taps * rows * channels, 4 * parts * rows * channels),
         name="short_adjoint",
@@ -454,14 +485,12 @@
     ny = lax.axis_size("y")
     half = shard.shape[0] // 2
     top, bottom = shard[:half], shard[half:]
-    return (
-        jnp.stack([move(top, xl=a, xh=b) for a, b in FLIPS]),
-        jnp.stack([move(bottom, y=d) for d in range(ny)]),
-    )
+    return [move(top, xl=a, xh=b) for a, b in FLIPS], [move(bottom, y=d) for d in range(ny)]
 
 
 def gather_far(wide_top, tall_bottom):
     ny = lax.axis_size("y")
+    wide_top, tall_bottom = jnp.stack(wide_top), jnp.stack(tall_bottom)
     return (
         [move(wide_top, y=d) for d in range(ny)],
         [move(tall_bottom, xl=a, xh=b) for a, b in FLIPS],
@@ -511,13 +540,16 @@
     )(cotangents, *tops, *bottoms)
 
 
-def project_kernel(ny, *refs):
+def project_kernel(ny, origin, *refs):
     rows_ref, turned_ref, tops, bottoms = refs[0], refs[1], refs[2 : 2 + ny], refs[2 + ny : 6 + ny]
     own_ref, other_ref = refs[6 + ny : 8 + ny]
     top_grads, bottom_grads = refs[8 + ny : 8 + 2 * ny], refs[8 + 2 * ny : 12 + 2 * ny]
     total = refs[12 + 2 * ny]
     step = pl.program_id(0)
-    rows = rows_ref[...]
+    height = rows_ref.shape[1] // 2
+    rows = jnp.concatenate(
+        [rows_ref[:, pl.ds(pl.multiple_of(origin[2 * step + a] % 2 * height, height), height)] for a in range(2)], axis=1
+    )
     width = own_ref.shape[1]
     size = tops[0].shape[1]
     grads = jnp.dot(turned_ref[...], rows, preferred_element_type=F32).astype(BF16)
@@ -546,7 +578,7 @@
         other_ref[...] = total[:, width:].astype(BF16)
 
 
-def project(all_rows, turned, tops, bottoms):
+def project(origin, all_rows, turned, tops, bottoms):
     rows, channels = all_rows.shape
     ny = len(tops)
     size = tops[0].shape[1]
@@ -559,17 +591,20 @@
     )
     results = hbm_call(
         functools.partial(project_kernel, ny),
-        loose=range(1, 6 + ny),
-        grid=(ny,),
-        in_specs=[pl.BlockSpec((rows, channels // ny), lambda i: (0, i)), whole(turned)]
-        + [whole(x) for x in (*tops, *bottoms)],
-        out_specs=[whole(x) for x in outs],
+        loose=(0, *range(2, 7 + ny)),
+        grid_spec=pltpu.PrefetchScalarGridSpec(
+            num_scalar_prefetch=1,
+            grid=(ny,),
+            in_specs=[pl.BlockSpec((rows, channels // ny), lambda i, origin: (0, origin[2 * i] // 2)), whole(turned)]
+            + [whole(x) for x in (*tops, *bottoms)],
+            out_specs=[whole(x) for x in outs],
+            scratch_shapes=[pltpu.VMEM((rows, 2 * width), F32)],
+        ),
         out_shape=outs,
-        scratch_shapes=[pltpu.VMEM((rows, 2 * width), F32)],
         compiler_params=params(40),
         cost_estimate=cost(8 * rows * width * channels, 2 * (rows + 4 * width) * channels),
         name="project",
-    )(all_rows, turned, *tops, *bottoms)
+    )(origin, all_rows, turned, *tops, *bottoms)
     return results[0], results[1], results[2 : 2 + ny], results[2 + ny :]
 
 
@@ -603,6 +638,7 @@
 
     block = jnp.arange(2 * ny, dtype=jnp.int32)
     place = ((y - block // 2) % ny) * 2 + (block + xl) % 2
+    origin = place
     size = 3 * channels // LANES + groups // 8
     each = size // (2 * nz)
     tile = jnp.arange(size, dtype=jnp.int32)
@@ -613,11 +649,13 @@
     rim = along(tokens[rows - RIM :], 1)
     lines = long_filter.astype(F32)
     query, key, value, mixer = features_call(tokens, rim, short_filter)
+    mixer, out_weight = lax.optimization_barrier((mixer, out_weight))
     mixer_prev = along(mixer, 1)
-    mixed, gated = mix_call(place, lines, mixer_prev, mixer, query)
-    gated, out_weight, upstream = lax.optimization_barrier((gated, out_weight, upstream))
+    wide_top, tall_bottom = gather_near(out_weight)
+    mixer_prev, wide_top, tall_bottom = lax.optimization_barrier((mixer_prev, wide_top, tall_bottom))
+    mixed, gated = mix_call(lines, mixer_prev, mixer, query)
+    mixed, wide_top, tall_bottom, upstream = lax.optimization_barrier((mixed, wide_top, tall_bottom, upstream))
     all_rows = lax.all_gather(gated, ("z", "c"), axis=0, tiled=True)
-    wide_top, tall_bottom = gather_near(out_weight)
     tops, bottoms = gather_far(wide_top, tall_bottom)
     mine = lax.dynamic_slice_in_dim(upstream, xh * span, span, 0)
     others = move(lax.dynamic_slice_in_dim(upstream, (1 - xh) * span, span, 0), xh=1)
@@ -626,7 +664,7 @@
     partial, all_rows = lax.optimization_barrier((partial, all_rows))
     gate_grad = lax.psum_scatter(partial, ("z", "c"), scatter_dimension=0, tiled=True)
 
-    own, other, top_grads, bottom_grads = project(all_rows, cotangents.T, tops, bottoms)
+    own, other, top_grads, bottom_grads = project(origin, all_rows, cotangents.T, tops, bottoms)
     grad_weight = plane_scatter_sum(top_grads, bottom_grads)
     theirs = move(other, xh=1)
     output = jnp.where(xh == 0, jnp.concatenate([own, theirs], axis=0), jnp.concatenate([theirs, own], axis=0))
@@ -638,6 +676,9 @@
     grad_tokens = short_adjoint_call(query_grad[None], query_next[None], short_filter, 0, None)
     long_sum, query_sum = long_grad_call(
         groups, short_taps, mixer_prev, mixer, grad_mixed, query_grad, tokens, rim
+    )
+    grad_next, grad_tokens, long_sum, query_sum = lax.optimization_barrier(
+        (grad_next, grad_tokens, long_sum, query_sum)
     )
     other_grads, key_sum, value_sum = unmix_call(
         lines, short_taps, grad_mixed, grad_next, key, value, tokens, rim

time: 297 us -> 265 us (0.89)
  Pallas kernels: 93 us -> 75.5 us
  starting transfers between devices: 90.7 us -> 77.1 us
    ppermute x40, waiting for transfers between devices: 41.5 us -> 59.1 us  [move(): return lax.ppermute(x, axes, pairs)]
    pallas_call x9, Pallas kernels: 90.8 us -> 73.3 us  [run(): return call(*held)]
    reduce_scatter x1, waiting for transfers between devices: 14.5 us -> 0.02 us  [shards(): lax.psum_scatter(partial, ('z', 'c'), scatter_dimension=0, tiled=True)]
    ppermute x40, starting transfers between devices: 71.5 us -> 59.1 us  [move(): return lax.ppermute(x, axes, pairs)]
    ppermute x5, waiting for transfers between devices: 16.8 us -> 6.83 us  [along(): return lax.ppermute(x, LINE, pairs)]
    all_gather x1, waiting for transfers between devices: 11 us -> 18.8 us  [shards(): all_rows = lax.all_gather(gated, ('z', 'c'), axis=0, tiled=True)]
  transfers between devices with their start and end apart: 47 -> 47, of which waited for: 28 -> 25; matrix products, arithmetic and copies ran while one was open for 3% -> 4% of each run, Pallas kernels for 16% -> 16%
where the time goes in v6:
time: 265 us; the launch traced here: 264 us
  waiting for transfers between devices  84.7 us (32%)
  starting transfers between devices  77.1 us (29%)
  Pallas kernels  75.5 us (28%)
  between operations  14.4 us (5%)
  local copies, waits for them, and re-layouts  7.87 us (3%)
  other arithmetic  4.49 us (2%)
    pallas_call x9, Pallas kernels, run(): return call(*held)  73.3 us
    ppermute x40, starting transfers between devices, move(): return lax.ppermute(x, axes, pairs)  59.1 us
    ppermute x40, waiting for transfers between devices, move(): return lax.ppermute(x, axes, pairs)  59.1 us
    all_gather x1, waiting for transfers between devices, shards(): all_rows = lax.all_gather(gated, ('z', 'c'), axis=0, tiled=True)  18.8 us
    ppermute x5, starting transfers between devices, along(): return lax.ppermute(x, LINE, pairs)  18 us
    ppermute x5, waiting for transfers between devices, along(): return lax.ppermute(x, LINE, pairs)  6.83 us
  transfers between devices with their start and end apart: 47, of which 25 were waited for; matrix products, arithmetic and copies ran while one was open for 4% of the time, Pallas kernels for 16%

profile of v6, /device:TPU:1, one launch (start us, length us, event | category | flops | bytes accessed | tf_op | source)
XLA Modules:
  0.0 264.1 jit_solution(2868120665278068514)
XLA Ops:
  8.2 4.9 %collective-permute-start = (bf16[8,12288]{1,0:T(8,128)(2,1)S(1)}, bf16[8,12288]{1,0:T(8,128)(2,1)S(1)}, u32[]{:S(2)}, u32[]{:S(2)}) collective-permute-start(bf16[8,12288]{1,0:T(8,128)(2,1)S(1)} %slice_bitcast_fusion), channel_id=1, source_target_pairs={{0,1},{1,2},{2,3},{3,4},{4,5},{5,6},{6,7},{7,8},{8,9},{9,10},{10,1... | collective-permute-start | bytes 589832 | tf_op jit(solution)/shard_map/ppermute | solution.py:27
  13.1 2.6 collective-permute-done.refs_3_.refs_4_.refs_5_.rim_ref.key_rim_ref.value_rim_ref
  15.7 6.8 %features.1 = (bf16[128,4096]{1,0:T(8,128)(2,1)}, bf16[128,4096]{1,0:T(8,128)(2,1)}, bf16[128,4096]{1,0:T(8,128)(2,1)}, bf16[128,4096]{1,0:T(8,128)(2,1)}) custom-call(bf16[128,12288]{1,0:T(8,128)(2,1)} %bitcast.43, bf16[128,12288]{1,0:T(8,128)(2,1)} %bitcast.44, bf16[128,12288]{1,0:T(8,128)(2,1)} %bitcast.45, ...), custom_call_target="tpu_custom_call" | custom-call | bytes 1572864 | tf_op jit(solution)/shard_map/features/pallas_call | solution.py:64
  22.5 4.4 %collective-permute-start.1 = (bf16[128,4096]{1,0:T(8,128)(2,1)}, bf16[128,4096]{1,0:T(8,128)(2,1)S(1)}, u32[]{:S(2)}, u32[]{:S(2)}) collective-permute-start(bf16[128,4096]{1,0:T(8,128)(2,1)} %get-tuple-element.63.cur_ref), channel_id=1, source_target_pairs={{0,1},{1,2},{2,3},{3,4},{4,5},{5,6},{6,7},{7,8},{8,9},{9,10},{10,1... | collective-permute-start | bytes 3145736 | tf_op jit(solution)/shard_map/ppermute | solution.py:27
  26.9 2.8 %collective-permute-start.2 = (bf16[256,256]{1,0:T(8,128)(2,1)S(1)}, bf16[256,256]{1,0:T(8,128)(2,1)S(1)}, u32[]{:S(2)}, u32[]{:S(2)}) collective-permute-start(bf16[256,256]{1,0:T(8,128)(2,1)S(1)} %get-tuple-element.77), channel_id=1, source_target_pairs={{0,8},{8,0},{1,9},{9,1},{2,10},{10,2},{3,11},{11,3},{4,12},{12,4},... | collective-permute-start | bytes 393224 | tf_op jit(solution)/shard_map/ppermute | solution.py:39
  30.6 1.3 collective-permute-start.5
  32.3 2.9 %collective-permute-start.6 = (bf16[256,256]{1,0:T(8,128)(2,1)S(1)}, bf16[256,256]{1,0:T(8,128)(2,1)S(1)}, u32[]{:S(2)}, u32[]{:S(2)}) collective-permute-start(bf16[256,256]{1,0:T(8,128)(2,1)S(1)} %get-tuple-element.81), channel_id=1, source_target_pairs={{0,64},{32,96},{64,0},{96,32},{1,65},{33,97},{65,1},{97,33},{2,66}... | collective-permute-start | bytes 393224 | tf_op jit(solution)/shard_map/ppermute | solution.py:39
  35.3 1.8 collective-permute-start.7
  37.1 1.4 collective-permute-done.6
  38.5 1.2 collective-permute-done.7
  39.7 9.7 %mix.1 = (bf16[128,4096]{1,0:T(8,128)(2,1)}, bf16[128,4096]{1,0:T(8,128)(2,1)}) custom-call(f32[256,128]{1,0:T(8,128)S(1)} %convert_element_type.63.lines_ref, bf16[128,4096]{1,0:T(8,128)(2,1)S(1)} %collective-permute-done.1.prev_ref, bf16[128,4096]{1,0:T(8,128)(2,1)} %get-tuple-element.63.cur_ref, bf16[128,4096]{1,0:T(8,128)(2,1)} %get-tuple-element.66.query_ref), custom_call_target="tpu_custom_call" | custom-call | bytes 1048576 | tf_op jit(solution)/shard_map/mix/pallas_call | solution.py:64
  50.3 2.9 %collective-permute-start.8 = (bf16[1024,256]{0,1:T(8,128)(2,1)S(1)}, bf16[1024,256]{0,1:T(8,128)(2,1)S(1)}, u32[]{:S(2)}, u32[]{:S(2)}) collective-permute-start(bf16[1024,256]{0,1:T(8,128)(2,1)S(1)} %get-tuple-element.127), channel_id=1, source_target_pairs={{0,8},{8,0},{1,9},{9,1},{2,10},{10,2},{3,11},{11,3},{4,12},{12,4},... | collective-permute-start | bytes 1572872 | tf_op jit(solution)/shard_map/ppermute | solution.py:39
  54.3 3.2 %collective-permute-start.10 = (bf16[4,256,256]{2,1,0:T(8,128)(2,1)S(1)}, bf16[4,256,256]{2,1,0:T(8,128)(2,1)}, u32[]{:S(2)}, u32[]{:S(2)}) collective-permute-start(bf16[4,256,256]{2,1,0:T(8,128)(2,1)S(1)} %pad_maximum_fusion.1.refs_1_.refs_2_), channel_id=1, source_target_pairs={{0,64},{32,96},{64,0},{96,32},{1,65},{33,97},{65,1},{97,33},{2,66}... | collective-permute-start | bytes 1572872 | tf_op jit(solution)/shard_map/ppermute | solution.py:39
  57.8 2.1 collective-permute-done.8
  59.9 1.4 collective-permute-start.13
  61.3 1.9 collective-permute-done.9.refs_2_.refs_3_
  64.3 1.2 fusion.15
  65.5 1.5 copy.12.refs_0_
  67.0 5.3 %collective-permute-done.10.refs_3_.refs_4_ = bf16[4,256,256]{2,1,0:T(8,128)(2,1)} collective-permute-done((bf16[4,256,256]{2,1,0:T(8,128)(2,1)S(1)}, bf16[4,256,256]{2,1,0:T(8,128)(2,1)}, u32[]{:S(2)}, u32[]{:S(2)}) %collective-permute-start.10) | collective-permute-done | bytes 524320 | tf_op jit(solution)/shard_map/ppermute | solution.py:39
  72.3 2.6 collective-permute-done.11.refs_4_.refs_5_
  75.0 4.7 %collective-permute-done.13.refs_7_.refs_8_ = bf16[4,256,256]{2,1,0:T(8,128)(2,1)} collective-permute-done((bf16[4,256,256]{2,1,0:T(8,128)(2,1)S(1)}, bf16[4,256,256]{2,1,0:T(8,128)(2,1)}, u32[]{:S(2)}, u32[]{:S(2)}) %collective-permute-start.13) | collective-permute-done | bytes 524320 | tf_op jit(solution)/shard_map/ppermute | solution.py:39
  79.6 6.0 %collective-permute-done.14.refs_8_.refs_9_ = bf16[4,256,256]{2,1,0:T(8,128)(2,1)} collective-permute-done((bf16[4,256,256]{2,1,0:T(8,128)(2,1)S(1)}, bf16[4,256,256]{2,1,0:T(8,128)(2,1)}, u32[]{:S(2)}, u32[]{:S(2)}) %collective-permute-start.14) | collective-permute-done | bytes 524320 | tf_op jit(solution)/shard_map/ppermute | solution.py:39
  86.7 8.6 %gate_matmul.1 = bf16[1024,4096]{1,0:T(8,128)(2,1)} custom-call(bf16[1024,512]{1,0:T(8,128)(2,1)S(1)} %copy.12.refs_0_, bf16[4,256,256]{2,1,0:T(8,128)(2,1)S(1)} %pad_maximum_fusion.1.refs_1_.refs_2_, bf16[4,256,256]{2,1,0:T(8,128)(2,1)S(1)} %copy-done.3, bf16[4,256,256]{2,1,0:T(8,128)(2,1)} %collective-permute-done.10.refs_3_.refs_4_, ...), custom_call_target="tpu_custom_call" | custom-call | flops 4294967296 | bytes 12582912 | tf_op jit(solution)/shard_map/gate_matmul/pallas_call | solution.py:64
  95.3 18.8 %all-gather.2.cloned.1.call-done.refs_0_ = bf16[1024,4096]{1,0:T(8,128)(2,1)} async-done(((bf16[128,4096]{1,0:T(8,128)(2,1)}), bf16[1024,4096]{1,0:T(8,128)(2,1)}) %all-gather.2.cloned.1.call-update) | async-done | bytes 8388624 | tf_op jit(solution)/shard_map/all_gather | solution.py:658
  114.1 15.7 %project.1 = (bf16[1024,256]{1,0:T(8,128)(2,1)}, bf16[1024,256]{1,0:T(8,128)(2,1)}, bf16[4,256,256]{2,1,0:T(8,128)(2,1)}, bf16[4,256,256]{2,1,0:T(8,128)(2,1)}, ...) custom-call(s32[8]{0:T(128)S(1)} %fusion.6.origin.place, ...), custom_call_target="tpu_custom_call" | custom-call | flops 8589934592 | bytes 16777216 | tf_op jit(solution)/shard_map/project/pallas_call | solution.py:64
  129.9 2.5 collective-permute-start.23
  132.3 1.5 collective-permute-start.21
  133.8 1.2 collective-permute-start.17
  135.0 2.4 collective-permute-start.16
  137.5 7.3 %collective-permute-done.23 = bf16[4,256,256]{2,1,0:T(8,128)(2,1)S(1)} collective-permute-done((bf16[4,256,256]{2,1,0:T(8,128)(2,1)}, bf16[4,256,256]{2,1,0:T(8,128)(2,1)S(1)}, u32[]{:S(2)}, u32[]{:S(2)}) %collective-permute-start.23) | collective-permute-done | bytes 524320 | tf_op jit(solution)/shard_map/ppermute | solution.py:39
  144.7 2.5 collective-permute-start.15
  147.2 1.5 collective-permute-start.27
  148.7 8.0 %collective-permute-done.21 = bf16[4,256,256]{2,1,0:T(8,128)(2,1)S(1)} collective-permute-done((bf16[4,256,256]{2,1,0:T(8,128)(2,1)}, bf16[4,256,256]{2,1,0:T(8,128)(2,1)S(1)}, u32[]{:S(2)}, u32[]{:S(2)}) %collective-permute-start.21) | collective-permute-done | bytes 524320 | tf_op jit(solution)/shard_map/ppermute | solution.py:39
  156.7 1.3 add_convert_fusion
  158.1 1.3 collective-permute-start.26
  159.4 2.5 collective-permute-start.25
  163.3 2.5 collective-permute-start.20
  165.8 2.2 collective-permute-done.27
  168.1 1.3 maximum_select_fusion
  169.3 3.5 %collective-permute-start.18 = (bf16[256,256]{1,0:T(8,128)(2,1)S(1)}, bf16[256,256]{1,0:T(8,128)(2,1)S(1)}, u32[]{:S(2)}, u32[]{:S(2)}) collective-permute-start(bf16[256,256]{1,0:T(8,128)(2,1)S(1)} %get-tuple-element.128), channel_id=1, source_target_pairs={{0,8},{8,0},{1,9},{9,1},{2,10},{10,2},{3,11},{11,3},{4,12},{12,4},... | collective-permute-start | bytes 393224 | tf_op jit(solution)/shard_map/ppermute | solution.py:39
  172.9 3.2 %collective-permute-done.18 = bf16[256,256]{1,0:T(8,128)(2,1)S(1)} collective-permute-done((bf16[256,256]{1,0:T(8,128)(2,1)S(1)}, bf16[256,256]{1,0:T(8,128)(2,1)S(1)}, u32[]{:S(2)}, u32[]{:S(2)}) %collective-permute-start.18) | collective-permute-done | bytes 131104 | tf_op jit(solution)/shard_map/ppermute | solution.py:39
  176.2 3.6 %gate_back.1 = (bf16[128,4096]{1,0:T(8,128)(2,1)}, bf16[128,4096]{1,0:T(8,128)(2,1)}) custom-call(s32[8]{0:T(128)S(1)} %fusion.6.origin.place, bf16[128,4096]{1,0:T(8,128)(2,1)} %reduce-scatter.2.cloned.1.call-done.gate_grad_ref, bf16[128,4096]{1,0:T(8,128)(2,1)} %get-tuple-element.66.query_ref, bf16[128,4096]{1,0:T(8,128)(2,1)} %get-tuple-element.100.mixed_ref), custom_call_target="tpu_custom_call" | custom-call | flops 1048576 | bytes 5242880 | tf_op jit(solution)/shard_map/gate_back/pallas_call | solution.py:64
  179.8 4.6 %collective-permute-start.28 = (bf16[128,4096]{1,0:T(8,128)(2,1)}, bf16[128,4096]{1,0:T(8,128)(2,1)S(1)}, u32[]{:S(2)}, u32[]{:S(2)}) collective-permute-start(bf16[128,4096]{1,0:T(8,128)(2,1)} %get-tuple-element.101.grad_ref), channel_id=1, source_target_pairs={{1,0},{2,1},{3,2},{4,3},{5,4},{6,5},{7,6},{8,7},{9,8},{10,9},{11,1... | collective-permute-start | bytes 3145736 | tf_op jit(solution)/shard_map/ppermute | solution.py:27
  185.3 2.1 collective-permute-start.29
  187.4 9.2 %long_grad.1 = (f32[256,128]{1,0:T(8,128)S(1)}, f32[8,4096]{1,0:T(8,128)S(1)}) custom-call(bf16[128,4096]{1,0:T(8,128)(2,1)} %copy-done.1, bf16[128,4096]{1,0:T(8,128)(2,1)} %get-tuple-element.63.cur_ref, bf16[128,4096]{1,0:T(8,128)(2,1)} %get-tuple-element.101.grad_ref, bf16[128,4096]{1,0:T(8,128)(2,1)} %get-tuple-element.102.feature_ref, ...), custom_call_target="tpu_custom_call" | custom-call | flops 2147483648 | bytes 5242880 | tf_op jit(solution)/shard_map/long_grad/pallas_call | solution.py:64
  196.6 1.4 collective-permute-done.29
  198.0 3.2 %short_adjoint.2.refs_0_ = bf16[128,12288]{1,0:T(8,128)(2,1)} custom-call(bf16[1,128,4096]{2,1,0:T(8,128)(2,1)} %bitcast.51, bf16[1,8,4096]{2,1,0:T(8,128)(2,1)S(1)} %bitcast.42, f32[7,12288]{1,0:T(8,128)} %filter_ref.3), custom_call_target="tpu_custom_call" | custom-call | flops 7340032 | bytes 2097152 | tf_op jit(solution)/shard_map/short_adjoint/pallas_call | solution.py:64
  201.2 11.4 %unmix.1 = (bf16[2,128,4096]{2,1,0:T(8,128)(2,1)}, f32[8,4096]{1,0:T(8,128)S(1)}, f32[8,4096]{1,0:T(8,128)S(1)}) custom-call(f32[256,128]{1,0:T(8,128)S(1)} %convert_element_type.63.lines_ref, bf16[128,4096]{1,0:T(8,128)(2,1)} %get-tuple-element.101.grad_ref, bf16[128,4096]{1,0:T(8,128)(2,1)S(1)} %collective-permute-done.28.next_ref, ...), custom_call_target="tpu_custom_call" | custom-call | flops 2147483648 | bytes 8388608 | tf_op jit(solution)/shard_map/unmix/pallas_call | solution.py:64
  213.4 1.5 collective-permute-done.31
  214.9 4.4 %collective-permute-start.34 = (f32[16,8,128]{2,1,0:T(8,128)S(1)}, f32[16,8,128]{2,1,0:T(8,128)S(1)}, u32[]{:S(2)}, u32[]{:S(2)}) collective-permute-start(f32[16,8,128]{2,1,0:T(8,128)S(1)} %get-tuple-element.135), channel_id=1, source_target_pairs={{0,6},{2,0},{4,2},{6,4},{1,7},{3,1},{5,3},{7,5},{8,14},{10,8},{12,... | collective-permute-start | bytes 196616 | tf_op jit(solution)/shard_map/ppermute | solution.py:39
  220.0 2.1 collective-permute-done.34
  222.1 2.0 collective-permute-done.33
  224.1 1.6 collective-permute-done.32
  225.7 1.3 collective-permute-start.36
  227.0 1.5 collective-permute-start.37
  228.5 1.5 collective-permute-start.35
  230.1 3.0 %collective-permute-done.35 = f32[16,8,128]{2,1,0:T(8,128)S(1)} collective-permute-done((f32[16,8,128]{2,1,0:T(8,128)S(1)}, f32[16,8,128]{2,1,0:T(8,128)S(1)}, u32[]{:S(2)}, u32[]{:S(2)}) %collective-permute-start.35) | collective-permute-done | bytes 65568 | tf_op jit(solution)/shard_map/ppermute | solution.py:39
  233.2 1.5 collective-permute-start.40
  235.9 2.1 collective-permute-done.39
  238.3 3.8 %collective-permute-start.41 = (f32[16,8,128]{2,1,0:T(8,128)S(1)}, f32[16,8,128]{2,1,0:T(8,128)S(1)}, u32[]{:S(2)}, u32[]{:S(2)}) collective-permute-start(f32[16,8,128]{2,1,0:T(8,128)S(1)} %add_add_fusion), channel_id=1, source_target_pairs={{0,1},{1,0},{2,3},{3,2},{4,5},{5,4},{6,7},{7,6},{8,9},{9,8},{10,11... | collective-permute-start | bytes 196616 | tf_op jit(solution)/shard_map/ppermute | solution.py:39
  243.1 1.9 collective-permute-start.30
  247.8 2.9 %collective-permute-done.30.rim_ref = bf16[2,8,4096]{2,1,0:T(8,128)(2,1)S(1)} collective-permute-done((bf16[2,8,4096]{2,1,0:T(8,128)(2,1)S(1)}, bf16[2,8,4096]{2,1,0:T(8,128)(2,1)S(1)}, u32[]{:S(2)}, u32[]{:S(2)}) %collective-permute-start.30) | collective-permute-done | bytes 131104 | tf_op jit(solution)/shard_map/ppermute | solution.py:27
  250.7 5.1 %short_adjoint.3 = bf16[128,12288]{1,0:T(8,128)(2,1)} custom-call(bf16[2,128,4096]{2,1,0:T(8,128)(2,1)} %get-tuple-element.108.grads_ref, bf16[2,8,4096]{2,1,0:T(8,128)(2,1)S(1)} %collective-permute-done.30.rim_ref, f32[7,12288]{1,0:T(8,128)} %filter_ref.3, bf16[128,12288]{1,0:T(8,128)(2,1)} %short_adjoint.2.refs_0_), custom_call_target="tpu_custom_call", output_to_operand_aliasing={{}: (3, {})} | custom-call | flops 14680064 | bytes 4194304 | tf_op jit(solution)/shard_map/short_adjoint/pallas_call | solution.py:64
  255.8 1.5 collect.1
  (92 shorter events, 16.4 us)
Async XLA Ops:
  7.2 106.9 %all-gather.2.cloned.1.call-start = ((), (), s32[]{:S(2)}) async-start(), calls=%async_computation.1 | async-start | bytes 9437184 | tf_op jit(solution)/shard_map/all_gather | solution.py:658
  8.2 7.5 %collective-permute-start = (bf16[8,12288]{1,0:T(8,128)(2,1)S(1)}, bf16[8,12288]{1,0:T(8,128)(2,1)S(1)}, u32[]{:S(2)}, u32[]{:S(2)}) collective-permute-start(bf16[8,12288]{1,0:T(8,128)(2,1)S(1)} %slice_bitcast_fusion), channel_id=1, source_target_pairs={{0,1},{1,2},{2,3},{3,4},{4,5},{5,6},{6,7},{7,8},{8,9},{9,10},{10,1... | collective-permute-start | bytes 589832 | tf_op jit(solution)/shard_map/ppermute | solution.py:27
  15.7 6.8 %copy-start = (bf16[8,12288]{1,0:T(8,128)(2,1)}, bf16[8,12288]{1,0:T(8,128)(2,1)S(1)}, u32[]{:S(2)}) copy-start(bf16[8,12288]{1,0:T(8,128)(2,1)S(1)} %collective-permute-done.refs_3_.refs_4_.refs_5_.rim_ref.key_rim_ref.value_rim_ref) | copy-start | bytes 589828
  15.7 11.2 %copy-start.8 = (bf16[512,256]{1,0:T(8,128)(2,1)S(1)}, bf16[512,256]{1,0:T(8,128)(2,1)}, u32[]{:S(2)}) copy-start(bf16[512,256]{1,0:T(8,128)(2,1)} %param.8) | copy-start | bytes 786436
  15.7 21.3 %copy-start.9 = (bf16[256,128]{1,0:T(8,128)(2,1)S(1)}, bf16[256,128]{1,0:T(8,128)(2,1)}, u32[]{:S(2)}) copy-start(bf16[256,128]{1,0:T(8,128)(2,1)} %param.7) | copy-start | bytes 196612
  22.5 17.2 %collective-permute-start.1 = (bf16[128,4096]{1,0:T(8,128)(2,1)}, bf16[128,4096]{1,0:T(8,128)(2,1)S(1)}, u32[]{:S(2)}, u32[]{:S(2)}) collective-permute-start(bf16[128,4096]{1,0:T(8,128)(2,1)} %get-tuple-element.63.cur_ref), channel_id=1, source_target_pairs={{0,1},{1,2},{2,3},{3,4},{4,5},{5,6},{6,7},{7,8},{8,9},{9,10},{10,1... | collective-permute-start | bytes 3145736 | tf_op jit(solution)/shard_map/ppermute | solution.py:27
  26.9 5.4 %collective-permute-start.2 = (bf16[256,256]{1,0:T(8,128)(2,1)S(1)}, bf16[256,256]{1,0:T(8,128)(2,1)S(1)}, u32[]{:S(2)}, u32[]{:S(2)}) collective-permute-start(bf16[256,256]{1,0:T(8,128)(2,1)S(1)} %get-tuple-element.77), channel_id=1, source_target_pairs={{0,8},{8,0},{1,9},{9,1},{2,10},{10,2},{3,11},{11,3},{4,12},{12,4},... | collective-permute-start | bytes 393224 | tf_op jit(solution)/shard_map/ppermute | solution.py:39
  29.8 5.5 %collective-permute-start.3 = (bf16[256,256]{1,0:T(8,128)(2,1)S(1)}, bf16[256,256]{1,0:T(8,128)(2,1)S(1)}, u32[]{:S(2)}, u32[]{:S(2)}) collective-permute-start(bf16[256,256]{1,0:T(8,128)(2,1)S(1)} %get-tuple-element.77), channel_id=1, source_target_pairs={{0,16},{16,0},{1,17},{17,1},{2,18},{18,2},{3,19},{19,3},{4,20},{20... | collective-permute-start | bytes 393224 | tf_op jit(solution)/shard_map/ppermute | solution.py:39
  30.1 7.0 %collective-permute-start.4 = (bf16[256,256]{1,0:T(8,128)(2,1)S(1)}, bf16[256,256]{1,0:T(8,128)(2,1)S(1)}, u32[]{:S(2)}, u32[]{:S(2)}) collective-permute-start(bf16[256,256]{1,0:T(8,128)(2,1)S(1)} %get-tuple-element.77), channel_id=1, source_target_pairs={{0,24},{8,16},{16,8},{24,0},{1,25},{9,17},{17,9},{25,1},{2,26},{10... | collective-permute-start | bytes 393224 | tf_op jit(solution)/shard_map/ppermute | solution.py:39
  30.6 6.4 %collective-permute-start.5 = (bf16[256,256]{1,0:T(8,128)(2,1)S(1)}, bf16[256,256]{1,0:T(8,128)(2,1)S(1)}, u32[]{:S(2)}, u32[]{:S(2)}) collective-permute-start(bf16[256,256]{1,0:T(8,128)(2,1)S(1)} %get-tuple-element.81), channel_id=1, source_target_pairs={{0,32},{32,64},{64,96},{96,0},{1,33},{33,65},{65,97},{97,1},{2,34}... | collective-permute-start | bytes 393224 | tf_op jit(solution)/shard_map/ppermute | solution.py:39
  32.3 6.2 %collective-permute-start.6 = (bf16[256,256]{1,0:T(8,128)(2,1)S(1)}, bf16[256,256]{1,0:T(8,128)(2,1)S(1)}, u32[]{:S(2)}, u32[]{:S(2)}) collective-permute-start(bf16[256,256]{1,0:T(8,128)(2,1)S(1)} %get-tuple-element.81), channel_id=1, source_target_pairs={{0,64},{32,96},{64,0},{96,32},{1,65},{33,97},{65,1},{97,33},{2,66}... | collective-permute-start | bytes 393224 | tf_op jit(solution)/shard_map/ppermute | solution.py:39
  35.3 4.4 %collective-permute-start.7 = (bf16[256,256]{1,0:T(8,128)(2,1)S(1)}, bf16[256,256]{1,0:T(8,128)(2,1)S(1)}, u32[]{:S(2)}, u32[]{:S(2)}) collective-permute-start(bf16[256,256]{1,0:T(8,128)(2,1)S(1)} %get-tuple-element.81), channel_id=1, source_target_pairs={{0,96},{32,0},{64,32},{96,64},{1,97},{33,1},{65,33},{97,65},{2,98}... | collective-permute-start | bytes 393224 | tf_op jit(solution)/shard_map/ppermute | solution.py:39
  39.7 9.7 %copy-start.1 = (bf16[128,4096]{1,0:T(8,128)(2,1)}, bf16[128,4096]{1,0:T(8,128)(2,1)S(1)}, u32[]{:S(2)}) copy-start(bf16[128,4096]{1,0:T(8,128)(2,1)S(1)} %collective-permute-done.1.prev_ref) | copy-start | bytes 3145732
  39.7 9.8 %copy-start.5 = (bf16[1,2048,256]{2,1,0:T(8,128)(2,1)S(1)}, bf16[1,2048,256]{2,1,0:T(8,128)(2,1)}, u32[]{:S(2)}) copy-start(bf16[1,2048,256]{2,1,0:T(8,128)(2,1)} %param.9) | copy-start | bytes 3145732
  49.5 126.8 %reduce-scatter.2.cloned.1.call-start = ((), (), s32[]{:S(2)}) async-start(), calls=%async_computation.2 | async-start | bytes 9437184 | tf_op jit(solution)/shard_map/reduce_scatter | solution.py:665
  50.3 9.6 %collective-permute-start.8 = (bf16[1024,256]{0,1:T(8,128)(2,1)S(1)}, bf16[1024,256]{0,1:T(8,128)(2,1)S(1)}, u32[]{:S(2)}, u32[]{:S(2)}) collective-permute-start(bf16[1024,256]{0,1:T(8,128)(2,1)S(1)} %get-tuple-element.127), channel_id=1, source_target_pairs={{0,8},{8,0},{1,9},{9,1},{2,10},{10,2},{3,11},{11,3},{4,12},{12,4},... | collective-permute-start | bytes 1572872 | tf_op jit(solution)/shard_map/ppermute | solution.py:39
  53.3 9.9 %collective-permute-start.9 = (bf16[4,256,256]{2,1,0:T(8,128)(2,1)S(1)}, bf16[4,256,256]{2,1,0:T(8,128)(2,1)S(1)}, u32[]{:S(2)}, u32[]{:S(2)}) collective-permute-start(bf16[4,256,256]{2,1,0:T(8,128)(2,1)S(1)} %pad_maximum_fusion.1.refs_1_.refs_2_), channel_id=1, source_target_pairs={{0,32},{32,64},{64,96},{96,0},{1,33},{33,65},{65,97},{97,1},{2,34}... | collective-permute-start | bytes 1572872 | tf_op jit(solution)/shard_map/ppermute | solution.py:39
  54.3 18.0 %collective-permute-start.10 = (bf16[4,256,256]{2,1,0:T(8,128)(2,1)S(1)}, bf16[4,256,256]{2,1,0:T(8,128)(2,1)}, u32[]{:S(2)}, u32[]{:S(2)}) collective-permute-start(bf16[4,256,256]{2,1,0:T(8,128)(2,1)S(1)} %pad_maximum_fusion.1.refs_1_.refs_2_), channel_id=1, source_target_pairs={{0,64},{32,96},{64,0},{96,32},{1,65},{33,97},{65,1},{97,33},{2,66}... | collective-permute-start | bytes 1572872 | tf_op jit(solution)/shard_map/ppermute | solution.py:39
  57.5 17.5 %collective-permute-start.11 = (bf16[4,256,256]{2,1,0:T(8,128)(2,1)S(1)}, bf16[4,256,256]{2,1,0:T(8,128)(2,1)}, u32[]{:S(2)}, u32[]{:S(2)}) collective-permute-start(bf16[4,256,256]{2,1,0:T(8,128)(2,1)S(1)} %pad_maximum_fusion.1.refs_1_.refs_2_), channel_id=1, source_target_pairs={{0,96},{32,0},{64,32},{96,64},{1,97},{33,1},{65,33},{97,65},{2,98}... | collective-permute-start | bytes 1572872 | tf_op jit(solution)/shard_map/ppermute | solution.py:39
  57.7 17.3 %collective-permute-start.12 = (bf16[4,256,256]{2,1,0:T(8,128)(2,1)S(1)}, bf16[4,256,256]{2,1,0:T(8,128)(2,1)}, u32[]{:S(2)}, u32[]{:S(2)}) collective-permute-start(bf16[4,256,256]{2,1,0:T(8,128)(2,1)S(1)} %pad_maximum_fusion.2.refs_5_.refs_6_), channel_id=1, source_target_pairs={{0,8},{8,0},{1,9},{9,1},{2,10},{10,2},{3,11},{11,3},{4,12},{12,4},... | collective-permute-start | bytes 1572872 | tf_op jit(solution)/shard_map/ppermute | solution.py:39
  59.9 19.7 %collective-permute-start.13 = (bf16[4,256,256]{2,1,0:T(8,128)(2,1)S(1)}, bf16[4,256,256]{2,1,0:T(8,128)(2,1)}, u32[]{:S(2)}, u32[]{:S(2)}) collective-permute-start(bf16[4,256,256]{2,1,0:T(8,128)(2,1)S(1)} %pad_maximum_fusion.2.refs_5_.refs_6_), channel_id=1, source_target_pairs={{0,16},{16,0},{1,17},{17,1},{2,18},{18,2},{3,19},{19,3},{4,20},{20... | collective-permute-start | bytes 1572872 | tf_op jit(solution)/shard_map/ppermute | solution.py:39
  63.2 0.8 copy-start.2
  64.0 21.6 %collective-permute-start.14 = (bf16[4,256,256]{2,1,0:T(8,128)(2,1)S(1)}, bf16[4,256,256]{2,1,0:T(8,128)(2,1)}, u32[]{:S(2)}, u32[]{:S(2)}) collective-permute-start(bf16[4,256,256]{2,1,0:T(8,128)(2,1)S(1)} %pad_maximum_fusion.2.refs_5_.refs_6_), channel_id=1, source_target_pairs={{0,24},{8,16},{16,8},{24,0},{1,25},{9,17},{17,9},{25,1},{2,26},{10... | collective-permute-start | bytes 1572872 | tf_op jit(solution)/shard_map/ppermute | solution.py:39
  85.6 1.0 copy-start.3
  95.3 18.8 %copy-start.4 = (bf16[4,256,256]{2,1,0:T(8,128)(2,1)S(1)}, bf16[4,256,256]{2,1,0:T(8,128)(2,1)}, u32[]{:S(2)}) copy-start(bf16[4,256,256]{2,1,0:T(8,128)(2,1)} %copy-done.2) | copy-start | bytes 1572868
  129.9 33.2 %copy-start.7 = (bf16[4,256,256]{2,1,0:T(8,128)(2,1)S(1)}, bf16[4,256,256]{2,1,0:T(8,128)(2,1)}, u32[]{:S(2)}) copy-start(bf16[4,256,256]{2,1,0:T(8,128)(2,1)} %get-tuple-element.88) | copy-start | bytes 1572868
  129.9 14.9 %collective-permute-start.23 = (bf16[4,256,256]{2,1,0:T(8,128)(2,1)}, bf16[4,256,256]{2,1,0:T(8,128)(2,1)S(1)}, u32[]{:S(2)}, u32[]{:S(2)}) collective-permute-start(bf16[4,256,256]{2,1,0:T(8,128)(2,1)} %get-tuple-element.95), channel_id=1, source_target_pairs={{0,24},{8,16},{16,8},{24,0},{1,25},{9,17},{17,9},{25,1},{2,26},{10... | collective-permute-start | bytes 1572872 | tf_op jit(solution)/shard_map/ppermute | solution.py:39
  132.3 14.9 %collective-permute-start.22 = (bf16[4,256,256]{2,1,0:T(8,128)(2,1)}, bf16[4,256,256]{2,1,0:T(8,128)(2,1)S(1)}, u32[]{:S(2)}, u32[]{:S(2)}) collective-permute-start(bf16[4,256,256]{2,1,0:T(8,128)(2,1)} %get-tuple-element.94), channel_id=1, source_target_pairs={{0,16},{16,0},{1,17},{17,1},{2,18},{18,2},{3,19},{19,3},{4,20},{20... | collective-permute-start | bytes 1572872 | tf_op jit(solution)/shard_map/ppermute | solution.py:39
  132.3 24.4 %collective-permute-start.21 = (bf16[4,256,256]{2,1,0:T(8,128)(2,1)}, bf16[4,256,256]{2,1,0:T(8,128)(2,1)S(1)}, u32[]{:S(2)}, u32[]{:S(2)}) collective-permute-start(bf16[4,256,256]{2,1,0:T(8,128)(2,1)} %get-tuple-element.93), channel_id=1, source_target_pairs={{0,8},{8,0},{1,9},{9,1},{2,10},{10,2},{3,11},{11,3},{4,12},{12,4},... | collective-permute-start | bytes 1572872 | tf_op jit(solution)/shard_map/ppermute | solution.py:39
  133.8 25.6 %collective-permute-start.17 = (bf16[4,256,256]{2,1,0:T(8,128)(2,1)}, bf16[4,256,256]{2,1,0:T(8,128)(2,1)S(1)}, u32[]{:S(2)}, u32[]{:S(2)}) collective-permute-start(bf16[4,256,256]{2,1,0:T(8,128)(2,1)} %get-tuple-element.91), channel_id=1, source_target_pairs={{0,32},{32,64},{64,96},{96,0},{1,33},{33,65},{65,97},{97,1},{2,34}... | collective-permute-start | bytes 1572872 | tf_op jit(solution)/shard_map/ppermute | solution.py:39
  135.0 26.8 %collective-permute-start.16 = (bf16[4,256,256]{2,1,0:T(8,128)(2,1)}, bf16[4,256,256]{2,1,0:T(8,128)(2,1)S(1)}, u32[]{:S(2)}, u32[]{:S(2)}) collective-permute-start(bf16[4,256,256]{2,1,0:T(8,128)(2,1)} %get-tuple-element.90), channel_id=1, source_target_pairs={{0,64},{32,96},{64,0},{96,32},{1,65},{33,97},{65,1},{97,33},{2,66}... | collective-permute-start | bytes 1572872 | tf_op jit(solution)/shard_map/ppermute | solution.py:39
  144.7 18.3 %collective-permute-start.15 = (bf16[4,256,256]{2,1,0:T(8,128)(2,1)}, bf16[4,256,256]{2,1,0:T(8,128)(2,1)S(1)}, u32[]{:S(2)}, u32[]{:S(2)}) collective-permute-start(bf16[4,256,256]{2,1,0:T(8,128)(2,1)} %get-tuple-element.89), channel_id=1, source_target_pairs={{0,96},{32,0},{64,32},{96,64},{1,97},{33,1},{65,33},{97,65},{2,98}... | collective-permute-start | bytes 1572872 | tf_op jit(solution)/shard_map/ppermute | solution.py:39
  147.2 20.7 %collective-permute-start.27 = (bf16[1024,256]{1,0:T(8,128)(2,1)}, bf16[1024,256]{1,0:T(8,128)(2,1)S(1)}, u32[]{:S(2)}, u32[]{:S(2)}) collective-permute-start(bf16[1024,256]{1,0:T(8,128)(2,1)} %get-tuple-element.97), channel_id=1, source_target_pairs={{0,8},{8,0},{1,9},{9,1},{2,10},{10,2},{3,11},{11,3},{4,12},{12,4},... | collective-permute-start | bytes 1572872 | tf_op jit(solution)/shard_map/ppermute | solution.py:39
  158.1 10.0 %copy-start.6 = (bf16[1024,256]{1,0:T(8,128)(2,1)S(1)}, bf16[1024,256]{1,0:T(8,128)(2,1)}, u32[]{:S(2)}) copy-start(bf16[1024,256]{1,0:T(8,128)(2,1)} %get-tuple-element.96) | copy-start | bytes 1572868
  158.1 11.2 %collective-permute-start.26 = (bf16[256,256]{1,0:T(8,128)(2,1)S(1)}, bf16[256,256]{1,0:T(8,128)(2,1)S(1)}, u32[]{:S(2)}, u32[]{:S(2)}) collective-permute-start(bf16[256,256]{1,0:T(8,128)(2,1)S(1)} %get-tuple-element.132), channel_id=1, source_target_pairs={{0,32},{32,64},{64,96},{96,0},{1,33},{33,65},{65,97},{97,1},{2,34}... | collective-permute-start | bytes 393224 | tf_op jit(solution)/shard_map/ppermute | solution.py:39
  159.4 13.4 %collective-permute-start.25 = (bf16[256,256]{1,0:T(8,128)(2,1)S(1)}, bf16[256,256]{1,0:T(8,128)(2,1)S(1)}, u32[]{:S(2)}, u32[]{:S(2)}) collective-permute-start(bf16[256,256]{1,0:T(8,128)(2,1)S(1)} %get-tuple-element.133), channel_id=1, source_target_pairs={{0,64},{32,96},{64,0},{96,32},{1,65},{33,97},{65,1},{97,33},{2,66}... | collective-permute-start | bytes 393224 | tf_op jit(solution)/shard_map/ppermute | solution.py:39
  161.9 11.0 %collective-permute-start.24 = (bf16[256,256]{1,0:T(8,128)(2,1)S(1)}, bf16[256,256]{1,0:T(8,128)(2,1)S(1)}, u32[]{:S(2)}, u32[]{:S(2)}) collective-permute-start(bf16[256,256]{1,0:T(8,128)(2,1)S(1)} %get-tuple-element.131), channel_id=1, source_target_pairs={{0,96},{32,0},{64,32},{96,64},{1,97},{33,1},{65,33},{97,65},{2,98}... | collective-permute-start | bytes 393224 | tf_op jit(solution)/shard_map/ppermute | solution.py:39
  163.3 9.5 %collective-permute-start.20 = (bf16[256,256]{1,0:T(8,128)(2,1)S(1)}, bf16[256,256]{1,0:T(8,128)(2,1)S(1)}, u32[]{:S(2)}, u32[]{:S(2)}) collective-permute-start(bf16[256,256]{1,0:T(8,128)(2,1)S(1)} %get-tuple-element.129), channel_id=1, source_target_pairs={{0,24},{8,16},{16,8},{24,0},{1,25},{9,17},{17,9},{25,1},{2,26},{10... | collective-permute-start | bytes 393224 | tf_op jit(solution)/shard_map/ppermute | solution.py:39
  168.0 4.9 %collective-permute-start.19 = (bf16[256,256]{1,0:T(8,128)(2,1)S(1)}, bf16[256,256]{1,0:T(8,128)(2,1)S(1)}, u32[]{:S(2)}, u32[]{:S(2)}) collective-permute-start(bf16[256,256]{1,0:T(8,128)(2,1)S(1)} %get-tuple-element.130), channel_id=1, source_target_pairs={{0,16},{16,0},{1,17},{17,1},{2,18},{18,2},{3,19},{19,3},{4,20},{20... | collective-permute-start | bytes 393224 | tf_op jit(solution)/shard_map/ppermute | solution.py:39
  169.3 6.8 %collective-permute-start.18 = (bf16[256,256]{1,0:T(8,128)(2,1)S(1)}, bf16[256,256]{1,0:T(8,128)(2,1)S(1)}, u32[]{:S(2)}, u32[]{:S(2)}) collective-permute-start(bf16[256,256]{1,0:T(8,128)(2,1)S(1)} %get-tuple-element.128), channel_id=1, source_target_pairs={{0,8},{8,0},{1,9},{9,1},{2,10},{10,2},{3,11},{11,3},{4,12},{12,4},... | collective-permute-start | bytes 393224 | tf_op jit(solution)/shard_map/ppermute | solution.py:39
  179.8 21.4 %collective-permute-start.28 = (bf16[128,4096]{1,0:T(8,128)(2,1)}, bf16[128,4096]{1,0:T(8,128)(2,1)S(1)}, u32[]{:S(2)}, u32[]{:S(2)}) collective-permute-start(bf16[128,4096]{1,0:T(8,128)(2,1)} %get-tuple-element.101.grad_ref), channel_id=1, source_target_pairs={{1,0},{2,1},{3,2},{4,3},{5,4},{6,5},{7,6},{8,7},{9,8},{10,9},{11,1... | collective-permute-start | bytes 3145736 | tf_op jit(solution)/shard_map/ppermute | solution.py:27
  185.3 12.7 %collective-permute-start.29 = (bf16[8,4096]{1,0:T(8,128)(2,1)S(1)}, bf16[8,4096]{1,0:T(8,128)(2,1)S(1)}, u32[]{:S(2)}, u32[]{:S(2)}) collective-permute-start(bf16[8,4096]{1,0:T(8,128)(2,1)S(1)} %slice.66), channel_id=1, source_target_pairs={{1,0},{2,1},{3,2},{4,3},{5,4},{6,5},{7,6},{8,7},{9,8},{10,9},{11,1... | collective-permute-start | bytes 196616 | tf_op jit(solution)/shard_map/ppermute | solution.py:27
  213.3 1.6 collective-permute-start.31
  214.9 7.2 %collective-permute-start.34 = (f32[16,8,128]{2,1,0:T(8,128)S(1)}, f32[16,8,128]{2,1,0:T(8,128)S(1)}, u32[]{:S(2)}, u32[]{:S(2)}) collective-permute-start(f32[16,8,128]{2,1,0:T(8,128)S(1)} %get-tuple-element.135), channel_id=1, source_target_pairs={{0,6},{2,0},{4,2},{6,4},{1,7},{3,1},{5,3},{7,5},{8,14},{10,8},{12,... | collective-permute-start | bytes 196616 | tf_op jit(solution)/shard_map/ppermute | solution.py:39
  219.4 4.7 %collective-permute-start.33 = (f32[16,8,128]{2,1,0:T(8,128)S(1)}, f32[16,8,128]{2,1,0:T(8,128)S(1)}, u32[]{:S(2)}, u32[]{:S(2)}) collective-permute-start(f32[16,8,128]{2,1,0:T(8,128)S(1)} %get-tuple-element.136), channel_id=1, source_target_pairs={{0,4},{2,6},{4,0},{6,2},{1,5},{3,7},{5,1},{7,3},{8,12},{10,14},{12... | collective-permute-start | bytes 196616 | tf_op jit(solution)/shard_map/ppermute | solution.py:39
  219.4 6.4 %collective-permute-start.32 = (f32[16,8,128]{2,1,0:T(8,128)S(1)}, f32[16,8,128]{2,1,0:T(8,128)S(1)}, u32[]{:S(2)}, u32[]{:S(2)}) collective-permute-start(f32[16,8,128]{2,1,0:T(8,128)S(1)} %get-tuple-element.134), channel_id=1, source_target_pairs={{0,2},{2,4},{4,6},{6,0},{1,3},{3,5},{5,7},{7,1},{8,10},{10,12},{12... | collective-permute-start | bytes 196616 | tf_op jit(solution)/shard_map/ppermute | solution.py:39
  225.7 4.4 %collective-permute-start.36 = (f32[16,8,128]{2,1,0:T(8,128)S(1)}, f32[16,8,128]{2,1,0:T(8,128)S(1)}, u32[]{:S(2)}, u32[]{:S(2)}) collective-permute-start(f32[16,8,128]{2,1,0:T(8,128)S(1)} %fusion.5), channel_id=1, source_target_pairs={{0,32},{32,64},{64,96},{96,0},{1,33},{33,65},{65,97},{97,1},{2,34}... | collective-permute-start | bytes 196616 | tf_op jit(solution)/shard_map/ppermute | solution.py:39
  227.0 3.1 %collective-permute-start.37 = (f32[16,8,128]{2,1,0:T(8,128)S(1)}, f32[16,8,128]{2,1,0:T(8,128)S(1)}, u32[]{:S(2)}, u32[]{:S(2)}) collective-permute-start(f32[16,8,128]{2,1,0:T(8,128)S(1)} %fusion.5), channel_id=1, source_target_pairs={{0,96},{32,0},{64,32},{96,64},{1,97},{33,1},{65,33},{97,65},{2,98}... | collective-permute-start | bytes 196616 | tf_op jit(solution)/shard_map/ppermute | solution.py:39
  228.5 4.6 %collective-permute-start.35 = (f32[16,8,128]{2,1,0:T(8,128)S(1)}, f32[16,8,128]{2,1,0:T(8,128)S(1)}, u32[]{:S(2)}, u32[]{:S(2)}) collective-permute-start(f32[16,8,128]{2,1,0:T(8,128)S(1)} %fusion.5), channel_id=1, source_target_pairs={{0,64},{32,96},{64,0},{96,32},{1,65},{33,97},{65,1},{97,33},{2,66}... | collective-permute-start | bytes 196616 | tf_op jit(solution)/shard_map/ppermute | solution.py:39
  233.1 4.8 %collective-permute-start.39 = (f32[16,8,128]{2,1,0:T(8,128)S(1)}, f32[16,8,128]{2,1,0:T(8,128)S(1)}, u32[]{:S(2)}, u32[]{:S(2)}) collective-permute-start(f32[16,8,128]{2,1,0:T(8,128)S(1)} %add_add_fusion.1), channel_id=1, source_target_pairs={{0,8},{8,0},{1,9},{9,1},{2,10},{10,2},{3,11},{11,3},{4,12},{12,4},... | collective-permute-start | bytes 196616 | tf_op jit(solution)/shard_map/ppermute | solution.py:39
  233.2 5.1 %collective-permute-start.40 = (f32[16,8,128]{2,1,0:T(8,128)S(1)}, f32[16,8,128]{2,1,0:T(8,128)S(1)}, u32[]{:S(2)}, u32[]{:S(2)}) collective-permute-start(f32[16,8,128]{2,1,0:T(8,128)S(1)} %add_add_fusion.1), channel_id=1, source_target_pairs={{0,24},{8,16},{16,8},{24,0},{1,25},{9,17},{17,9},{25,1},{2,26},{10... | collective-permute-start | bytes 196616 | tf_op jit(solution)/shard_map/ppermute | solution.py:39
  234.8 3.6 %collective-permute-start.38 = (f32[16,8,128]{2,1,0:T(8,128)S(1)}, f32[16,8,128]{2,1,0:T(8,128)S(1)}, u32[]{:S(2)}, u32[]{:S(2)}) collective-permute-start(f32[16,8,128]{2,1,0:T(8,128)S(1)} %add_add_fusion.1), channel_id=1, source_target_pairs={{0,16},{16,0},{1,17},{17,1},{2,18},{18,2},{3,19},{19,3},{4,20},{20... | collective-permute-start | bytes 196616 | tf_op jit(solution)/shard_map/ppermute | solution.py:39
  238.3 6.7 %collective-permute-start.41 = (f32[16,8,128]{2,1,0:T(8,128)S(1)}, f32[16,8,128]{2,1,0:T(8,128)S(1)}, u32[]{:S(2)}, u32[]{:S(2)}) collective-permute-start(f32[16,8,128]{2,1,0:T(8,128)S(1)} %add_add_fusion), channel_id=1, source_target_pairs={{0,1},{1,0},{2,3},{3,2},{4,5},{5,4},{6,7},{7,6},{8,9},{9,8},{10,11... | collective-permute-start | bytes 196616 | tf_op jit(solution)/shard_map/ppermute | solution.py:39
  243.1 7.6 %collective-permute-start.30 = (bf16[2,8,4096]{2,1,0:T(8,128)(2,1)S(1)}, bf16[2,8,4096]{2,1,0:T(8,128)(2,1)S(1)}, u32[]{:S(2)}, u32[]{:S(2)}) collective-permute-start(bf16[2,8,4096]{2,1,0:T(8,128)(2,1)S(1)} %slice.67), channel_id=1, source_target_pairs={{1,0},{2,1},{3,2},{4,3},{5,4},{6,5},{7,6},{8,7},{9,8},{10,9},{11,1... | collective-permute-start | bytes 393224 | tf_op jit(solution)/shard_map/ppermute | solution.py:27
  245.0 10.8 %collective-permute-start.42 = (f32[32,8,128]{2,1,0:T(8,128)S(1)}, f32[32,8,128]{2,1,0:T(8,128)S(1)}, u32[]{:S(2)}, u32[]{:S(2)}) collective-permute-start(f32[32,8,128]{2,1,0:T(8,128)S(1)} %pad_maximum_fusion.3.refs_0_), channel_id=1, source_target_pairs={{0,6},{2,0},{4,2},{6,4},{1,7},{3,1},{5,3},{7,5},{8,14},{10,8},{12,... | collective-permute-start | bytes 393224 | tf_op jit(solution)/shard_map/ppermute | solution.py:39
  245.7 10.1 %collective-permute-start.43 = (f32[32,8,128]{2,1,0:T(8,128)S(1)}, f32[32,8,128]{2,1,0:T(8,128)S(1)}, u32[]{:S(2)}, u32[]{:S(2)}) collective-permute-start(f32[32,8,128]{2,1,0:T(8,128)S(1)} %pad_maximum_fusion.3.refs_0_), channel_id=1, source_target_pairs={{0,4},{2,6},{4,0},{6,2},{1,5},{3,7},{5,1},{7,3},{8,12},{10,14},{12... | collective-permute-start | bytes 393224 | tf_op jit(solution)/shard_map/ppermute | solution.py:39
  246.0 9.8 %collective-permute-start.44 = (f32[32,8,128]{2,1,0:T(8,128)S(1)}, f32[32,8,128]{2,1,0:T(8,128)S(1)}, u32[]{:S(2)}, u32[]{:S(2)}) collective-permute-start(f32[32,8,128]{2,1,0:T(8,128)S(1)} %pad_maximum_fusion.3.refs_0_), channel_id=1, source_target_pairs={{0,2},{2,4},{4,6},{6,0},{1,3},{3,5},{5,7},{7,1},{8,10},{10,12},{12... | collective-permute-start | bytes 393224 | tf_op jit(solution)/shard_map/ppermute | solution.py:39
Sparse Core Ops, SparseCore 0:
  49.6 64.4 all-gather.1
  116.5 51.5 reduce-scatter.1

commit v7 on v6

--- a/solution.py
+++ b/solution.py
@@ -388,7 +388,7 @@
         grid=(parts, steps),
         in_specs=[
             pl.BlockSpec((1, rows, width), lambda p, i: (p, 0, i)),
-            pl.BlockSpec((1, RIM, width), lambda p, i: (p, 0, i)),
+            pl.BlockSpec((1, RIM, width), lambda p, i: (p + first, 0, i)),
             pl.BlockSpec((short_taps, width), lambda p, i: (0, (p + first) * steps + i)),
         ]
         + [pl.BlockSpec(memory_space=pl.ANY)] * len(given),
@@ -439,7 +439,7 @@
     return pl.BlockSpec(memory_space=pltpu.VMEM)
 
 
-def total_over_devices(spread_to, collect_from, query_sum, key_sum, value_sum, long_sum, short_taps):
+def total_over_devices(spread_to, collect_from, query_sum, key_sum, value_sum, long_sum, short_taps, beside):
     ny, nz = lax.axis_size("y"), lax.axis_size("z")
     channels = query_sum.shape[1]
     count = 3 * channels // LANES + long_sum.shape[0] // 8
@@ -455,12 +455,13 @@
     part = own + move(other, c=1)
     size = count // 2 // nz
     part = sum([move(part[d * size : (d + 1) * size], z=d) for d in range(1, nz)], part[:size])
-    whole = paired_sum([part] + [move(part, y=d) for d in range(1, ny)])
+    terms, beside = lax.optimization_barrier(([part] + [move(part, y=d) for d in range(1, ny)], beside))
+    whole = paired_sum(terms)
     whole = paired_sum([move(whole, xl=a, xh=b) for a, b in FLIPS])
     line = jnp.concatenate([whole, move(whole, c=1)], axis=0)
     lines = [move(line, z=-d) for d in range(nz)]
     groups, taps = long_sum.shape
-    return pl.pallas_call(
+    short, long = pl.pallas_call(
         collect_kernel,
         in_specs=[pl.BlockSpec(memory_space=pltpu.SMEM)] + [in_vmem()] * nz,
         out_specs=[in_vmem(), in_vmem()],
@@ -472,6 +473,7 @@
         compiler_params=params(),
         name="collect",
     )(collect_from, *lines)
+    return short, long, beside
 
 
 def paired_sum(terms):
@@ -540,31 +542,69 @@
     )(cotangents, *tops, *bottoms)
 
 
-def project_kernel(ny, origin, *refs):
-    rows_ref, turned_ref, tops, bottoms = refs[0], refs[1], refs[2 : 2 + ny], refs[2 + ny : 6 + ny]
-    own_ref, other_ref = refs[6 + ny : 8 + ny]
-    top_grads, bottom_grads = refs[8 + ny : 8 + 2 * ny], refs[8 + 2 * ny : 12 + 2 * ny]
-    total = refs[12 + 2 * ny]
+def picked(origin, step, rows_ref):
+    height = rows_ref.shape[1] // 2
+    at = [pl.multiple_of(origin[2 * step + a] % 2 * height, height) for a in range(2)]
+    return jnp.concatenate([rows_ref[:, pl.ds(x, height)] for x in at], axis=1)
+
+
+def weight_grad_kernel(ny, origin, rows_ref, turned_ref, *refs):
+    top_grads, bottom_grads = refs[:ny], refs[ny:]
     step = pl.program_id(0)
-    height = rows_ref.shape[1] // 2
-    rows = jnp.concatenate(
-        [rows_ref[:, pl.ds(pl.multiple_of(origin[2 * step + a] % 2 * height, height), height)] for a in range(2)], axis=1
-    )
-    width = own_ref.shape[1]
-    size = tops[0].shape[1]
+    size = bottom_grads[0].shape[2]
+    width = bottom_grads[0].shape[1]
+    rows = picked(origin, step, rows_ref)
     grads = jnp.dot(turned_ref[...], rows, preferred_element_type=F32).astype(BF16)
-    for a in range(2):
-        for b in range(2):
-            at = (2 * a + 1) * size
-            bottom_grads[2 * a + b][step] = grads[b * width : (b + 1) * width, at : at + size]
+    for f in range(4):
+        a, b = f // 2, f % 2
+        at = (2 * a + 1) * size
+        bottom_grads[f][step] = grads[b * width : (b + 1) * width, at : at + size]
     for d in range(ny):
 
         @pl.when(step == d)
         def _(d=d):
-            for a in range(2):
-                for b in range(2):
-                    at = 2 * a * size
-                    top_grads[d][2 * a + b] = grads[b * width : (b + 1) * width, at : at + size]
+            for f in range(4):
+                a, b = f // 2, f % 2
+                at = 2 * a * size
+                top_grads[d][f] = grads[b * width : (b + 1) * width, at : at + size]
+
+
+def rows_of(origin, all_rows, ny):
+    rows, channels = all_rows.shape
+    return pl.BlockSpec((rows, channels // ny), lambda i, origin: (0, origin[2 * i] // 2))
+
+
+def weight_grad(origin, all_rows, turned, ny):
+    rows, channels = all_rows.shape
+    size = channels // (4 * ny)
+    width = turned.shape[0] // 2
+    outs = [jax.ShapeDtypeStruct((4, width, size), BF16)] * ny + [jax.ShapeDtypeStruct((ny, width, size), BF16)] * 4
+    results = hbm_call(
+        functools.partial(weight_grad_kernel, ny),
+        loose=(0, 2),
+        grid_spec=pltpu.PrefetchScalarGridSpec(
+            num_scalar_prefetch=1,
+            grid=(ny,),
+            in_specs=[rows_of(origin, all_rows, ny), whole(turned)],
+            out_specs=[whole(x) for x in outs],
+        ),
+        out_shape=outs,
+        compiler_params=params(40),
+        cost_estimate=cost(4 * rows * width * channels, 2 * (rows + 2 * width) * channels),
+        name="weight_grad",
+    )(origin, all_rows, turned)
+    return results[:ny], results[ny:]
+
+
+def output_kernel(ny, origin, rows_ref, *refs):
+    tops, bottoms, own_ref, other_ref, total = refs[:ny], refs[ny : ny + 4], refs[-3], refs[-2], refs[-1]
+    step = pl.program_id(0)
+    width = own_ref.shape[1]
+    rows = picked(origin, step, rows_ref)
+    for d in range(ny):
+
+        @pl.when(step == d)
+        def _(d=d):
             right = jnp.concatenate(piece_rows(tops, bottoms, d), axis=0)
             product = jnp.dot(rows, right, preferred_element_type=F32)
             if d == 0:
@@ -578,34 +618,26 @@
         other_ref[...] = total[:, width:].astype(BF16)
 
 
-def project(origin, all_rows, turned, tops, bottoms):
+def output_call(origin, all_rows, tops, bottoms):
     rows, channels = all_rows.shape
     ny = len(tops)
-    size = tops[0].shape[1]
-    width = turned.shape[0] // 2
+    width = tops[0].shape[2]
     half = jax.ShapeDtypeStruct((rows, width), BF16)
-    outs = (
-        [half, half]
-        + [jax.ShapeDtypeStruct((4, width, size), BF16)] * ny
-        + [jax.ShapeDtypeStruct((ny, width, size), BF16)] * 4
-    )
-    results = hbm_call(
-        functools.partial(project_kernel, ny),
-        loose=(0, *range(2, 7 + ny)),
+    return hbm_call(
+        functools.partial(output_kernel, ny),
+        loose=(0, *range(2, 6 + ny)),
         grid_spec=pltpu.PrefetchScalarGridSpec(
             num_scalar_prefetch=1,
             grid=(ny,),
-            in_specs=[pl.BlockSpec((rows, channels // ny), lambda i, origin: (0, origin[2 * i] // 2)), whole(turned)]
-            + [whole(x) for x in (*tops, *bottoms)],
-            out_specs=[whole(x) for x in outs],
+            in_specs=[rows_of(origin, all_rows, ny)] + [whole(x) for x in (*tops, *bottoms)],
+            out_specs=[whole(half)] * 2,
             scratch_shapes=[pltpu.VMEM((rows, 2 * width), F32)],
         ),
-        out_shape=outs,
-        compiler_params=params(40),
-        cost_estimate=cost(8 * rows * width * channels, 2 * (rows + 4 * width) * channels),
-        name="project",
-    )(origin, all_rows, turned, *tops, *bottoms)
-    return results[0], results[1], results[2 : 2 + ny], results[2 + ny :]
+        out_shape=[half, half],
+        compiler_params=params(32),
+        cost_estimate=cost(4 * rows * width * channels, 2 * (rows + 2 * width) * channels),
+        name="output",
+    )(origin, all_rows, *tops, *bottoms)
 
 
 def plane_scatter_sum(top_grads, bottom_grads):
@@ -664,7 +696,8 @@
     partial, all_rows = lax.optimization_barrier((partial, all_rows))
     gate_grad = lax.psum_scatter(partial, ("z", "c"), scatter_dimension=0, tiled=True)
 
-    own, other, top_grads, bottom_grads = project(origin, all_rows, cotangents.T, tops, bottoms)
+    top_grads, bottom_grads = weight_grad(origin, all_rows, cotangents.T, ny)
+    own, other = output_call(origin, all_rows, tops, bottoms)
     grad_weight = plane_scatter_sum(top_grads, bottom_grads)
     theirs = move(other, xh=1)
     output = jnp.where(xh == 0, jnp.concatenate([own, theirs], axis=0), jnp.concatenate([theirs, own], axis=0))
@@ -672,22 +705,18 @@
 
     grad_mixed, query_grad = gate_call(place, gate_grad, query, mixed)
     grad_next = along(grad_mixed, -1)
-    query_next = along(query_grad[:RIM], -1)
-    grad_tokens = short_adjoint_call(query_grad[None], query_next[None], short_filter, 0, None)
     long_sum, query_sum = long_grad_call(
         groups, short_taps, mixer_prev, mixer, grad_mixed, query_grad, tokens, rim
-    )
-    grad_next, grad_tokens, long_sum, query_sum = lax.optimization_barrier(
-        (grad_next, grad_tokens, long_sum, query_sum)
     )
     other_grads, key_sum, value_sum = unmix_call(
         lines, short_taps, grad_mixed, grad_next, key, value, tokens, rim
     )
-    other_next = along(other_grads[:, :RIM], -1)
-    grad_short, grad_long = total_over_devices(
-        spread_to, collect_from, query_sum, key_sum, value_sum, long_sum, short_taps
+    edge = along(jnp.concatenate([query_grad[None, :RIM], other_grads[:, :RIM]], axis=0), -1)
+    grad_tokens = short_adjoint_call(query_grad[None], edge, short_filter, 0, None)
+    grad_short, grad_long, grad_tokens = total_over_devices(
+        spread_to, collect_from, query_sum, key_sum, value_sum, long_sum, short_taps, grad_tokens
     )
-    grad_tokens = short_adjoint_call(other_grads, other_next, short_filter, 1, grad_tokens)
+    grad_tokens = short_adjoint_call(other_grads, edge, short_filter, 1, grad_tokens)
     return output[None], grad_tokens[None], grad_short, grad_long, grad_weight
 
 

time: 265 us -> 253 us (0.955)
  waiting for transfers between devices: 84.7 us -> 70 us
  Pallas kernels: 75.5 us -> 79.6 us
    ppermute x40, waiting for transfers between devices: 59.1 us -> 44.8 us  [move(): return lax.ppermute(x, axes, pairs)]
    pallas_call x9 -> x10, Pallas kernels: 73.3 us -> 77.2 us  [run(): return call(*held)]
    ppermute x5 -> x4, starting transfers between devices: 18 us -> 16.9 us  [along(): return lax.ppermute(x, LINE, pairs)]
    ppermute x5 -> x4, waiting for transfers between devices: 6.83 us -> 6.28 us  [along(): return lax.ppermute(x, LINE, pairs)]
  transfers between devices with their start and end apart: 47 -> 46, of which waited for: 25 -> 21; matrix products, arithmetic and copies ran while one was open for 4% -> 4% of each run, Pallas kernels for 16% -> 18%
where the time goes in v7:
time: 253 us; the launch traced here: 252 us
  Pallas kernels  79.6 us (31%)
  starting transfers between devices  75.7 us (30%)
  waiting for transfers between devices  70 us (28%)
  between operations  14.4 us (6%)
  local copies, waits for them, and re-layouts  7.88 us (3%)
  other arithmetic  4.68 us (2%)
    pallas_call x10, Pallas kernels, run(): return call(*held)  77.2 us
    ppermute x40, starting transfers between devices, move(): return lax.ppermute(x, axes, pairs)  58.8 us
    ppermute x40, waiting for transfers between devices, move(): return lax.ppermute(x, axes, pairs)  44.8 us
    all_gather x1, waiting for transfers between devices, shards(): all_rows = lax.all_gather(gated, ('z', 'c'), axis=0, tiled=True)  18.8 us
    ppermute x4, starting transfers between devices, along(): return lax.ppermute(x, LINE, pairs)  16.9 us
    ppermute x4, waiting for transfers between devices, along(): return lax.ppermute(x, LINE, pairs)  6.28 us
  transfers between devices with their start and end apart: 46, of which 21 were waited for; matrix products, arithmetic and copies ran while one was open for 4% of the time, Pallas kernels for 18%

profile of v7, /device:TPU:1, one launch (start us, length us, event | category | flops | bytes accessed | tf_op | source)
XLA Modules:
  0.0 252.3 jit_solution(11663799069198414560)
XLA Ops:
  8.2 4.9 %collective-permute-start = (bf16[8,12288]{1,0:T(8,128)(2,1)S(1)}, bf16[8,12288]{1,0:T(8,128)(2,1)S(1)}, u32[]{:S(2)}, u32[]{:S(2)}) collective-permute-start(bf16[8,12288]{1,0:T(8,128)(2,1)S(1)} %slice_bitcast_fusion), channel_id=1, source_target_pairs={{0,1},{1,2},{2,3},{3,4},{4,5},{5,6},{6,7},{7,8},{8,9},{9,10},{10,1... | collective-permute-start | bytes 589832 | tf_op jit(solution)/shard_map/ppermute | solution.py:27
  13.1 2.6 %collective-permute-done.refs_3_.refs_4_.refs_5_.key_rim_ref.value_rim_ref.rim_ref = bf16[8,12288]{1,0:T(8,128)(2,1)S(1)} collective-permute-done((bf16[8,12288]{1,0:T(8,128)(2,1)S(1)}, bf16[8,12288]{1,0:T(8,128)(2,1)S(1)}, u32[]{:S(2)}, u32[]{:S(2)}) %collective-permute-start) | collective-permute-done | bytes 196640 | tf_op jit(solution)/shard_map/ppermute | solution.py:27
  15.7 6.8 %features.1 = (bf16[128,4096]{1,0:T(8,128)(2,1)}, bf16[128,4096]{1,0:T(8,128)(2,1)}, bf16[128,4096]{1,0:T(8,128)(2,1)}, bf16[128,4096]{1,0:T(8,128)(2,1)}) custom-call(bf16[128,12288]{1,0:T(8,128)(2,1)} %bitcast.43, bf16[128,12288]{1,0:T(8,128)(2,1)} %bitcast.44, bf16[128,12288]{1,0:T(8,128)(2,1)} %bitcast.45, ...), custom_call_target="tpu_custom_call" | custom-call | bytes 1572864 | tf_op jit(solution)/shard_map/features/pallas_call | solution.py:64
  22.5 4.4 %collective-permute-start.1 = (bf16[128,4096]{1,0:T(8,128)(2,1)}, bf16[128,4096]{1,0:T(8,128)(2,1)S(1)}, u32[]{:S(2)}, u32[]{:S(2)}) collective-permute-start(bf16[128,4096]{1,0:T(8,128)(2,1)} %get-tuple-element.64.cur_ref), channel_id=1, source_target_pairs={{0,1},{1,2},{2,3},{3,4},{4,5},{5,6},{6,7},{7,8},{8,9},{9,10},{10,1... | collective-permute-start | bytes 3145736 | tf_op jit(solution)/shard_map/ppermute | solution.py:27
  26.9 2.8 %collective-permute-start.2 = (bf16[256,256]{1,0:T(8,128)(2,1)S(1)}, bf16[256,256]{1,0:T(8,128)(2,1)S(1)}, u32[]{:S(2)}, u32[]{:S(2)}) collective-permute-start(bf16[256,256]{1,0:T(8,128)(2,1)S(1)} %get-tuple-element.78), channel_id=1, source_target_pairs={{0,8},{8,0},{1,9},{9,1},{2,10},{10,2},{3,11},{11,3},{4,12},{12,4},... | collective-permute-start | bytes 393224 | tf_op jit(solution)/shard_map/ppermute | solution.py:39
  30.6 1.3 collective-permute-start.5
  32.3 2.9 %collective-permute-start.6 = (bf16[256,256]{1,0:T(8,128)(2,1)S(1)}, bf16[256,256]{1,0:T(8,128)(2,1)S(1)}, u32[]{:S(2)}, u32[]{:S(2)}) collective-permute-start(bf16[256,256]{1,0:T(8,128)(2,1)S(1)} %get-tuple-element.82), channel_id=1, source_target_pairs={{0,64},{32,96},{64,0},{96,32},{1,65},{33,97},{65,1},{97,33},{2,66}... | collective-permute-start | bytes 393224 | tf_op jit(solution)/shard_map/ppermute | solution.py:39
  35.2 1.8 collective-permute-start.7
  37.1 1.4 collective-permute-done.6
  38.5 1.2 collective-permute-done.7
  39.7 9.7 %mix.1 = (bf16[128,4096]{1,0:T(8,128)(2,1)}, bf16[128,4096]{1,0:T(8,128)(2,1)}) custom-call(f32[256,128]{1,0:T(8,128)S(1)} %convert_element_type.63.lines_ref, bf16[128,4096]{1,0:T(8,128)(2,1)S(1)} %collective-permute-done.1.prev_ref, bf16[128,4096]{1,0:T(8,128)(2,1)} %get-tuple-element.64.cur_ref, bf16[128,4096]{1,0:T(8,128)(2,1)} %get-tuple-element.67.query_ref), custom_call_target="tpu_custom_call" | custom-call | bytes 1048576 | tf_op jit(solution)/shard_map/mix/pallas_call | solution.py:64
  50.3 2.9 %collective-permute-start.8 = (bf16[1024,256]{0,1:T(8,128)(2,1)S(1)}, bf16[1024,256]{0,1:T(8,128)(2,1)S(1)}, u32[]{:S(2)}, u32[]{:S(2)}) collective-permute-start(bf16[1024,256]{0,1:T(8,128)(2,1)S(1)} %get-tuple-element.129), channel_id=1, source_target_pairs={{0,8},{8,0},{1,9},{9,1},{2,10},{10,2},{3,11},{11,3},{4,12},{12,4},... | collective-permute-start | bytes 1572872 | tf_op jit(solution)/shard_map/ppermute | solution.py:39
  53.2 1.0 collective-permute-start.9
  54.3 3.2 %collective-permute-start.10 = (bf16[4,256,256]{2,1,0:T(8,128)(2,1)S(1)}, bf16[4,256,256]{2,1,0:T(8,128)(2,1)}, u32[]{:S(2)}, u32[]{:S(2)}) collective-permute-start(bf16[4,256,256]{2,1,0:T(8,128)(2,1)S(1)} %pad_maximum_fusion.1.refs_1_.refs_0_), channel_id=1, source_target_pairs={{0,64},{32,96},{64,0},{96,32},{1,65},{33,97},{65,1},{97,33},{2,66}... | collective-permute-start | bytes 1572872 | tf_op jit(solution)/shard_map/ppermute | solution.py:39
  57.8 2.1 collective-permute-done.8
  59.9 1.4 collective-permute-start.13
  61.3 1.9 collective-permute-done.9.refs_2_.refs_1_
  64.3 1.2 fusion.15
  65.5 1.5 copy.12.refs_0_
  67.0 5.3 %collective-permute-done.10.refs_3_.refs_2_ = bf16[4,256,256]{2,1,0:T(8,128)(2,1)} collective-permute-done((bf16[4,256,256]{2,1,0:T(8,128)(2,1)S(1)}, bf16[4,256,256]{2,1,0:T(8,128)(2,1)}, u32[]{:S(2)}, u32[]{:S(2)}) %collective-permute-start.10) | collective-permute-done | bytes 524320 | tf_op jit(solution)/shard_map/ppermute | solution.py:39
  72.3 2.6 %collective-permute-done.11.refs_4_.refs_3_ = bf16[4,256,256]{2,1,0:T(8,128)(2,1)} collective-permute-done((bf16[4,256,256]{2,1,0:T(8,128)(2,1)S(1)}, bf16[4,256,256]{2,1,0:T(8,128)(2,1)}, u32[]{:S(2)}, u32[]{:S(2)}) %collective-permute-start.11) | collective-permute-done | bytes 524320 | tf_op jit(solution)/shard_map/ppermute | solution.py:39
  75.0 4.7 %collective-permute-done.13.refs_7_.refs_6_ = bf16[4,256,256]{2,1,0:T(8,128)(2,1)} collective-permute-done((bf16[4,256,256]{2,1,0:T(8,128)(2,1)S(1)}, bf16[4,256,256]{2,1,0:T(8,128)(2,1)}, u32[]{:S(2)}, u32[]{:S(2)}) %collective-permute-start.13) | collective-permute-done | bytes 524320 | tf_op jit(solution)/shard_map/ppermute | solution.py:39
  79.6 6.0 %collective-permute-done.14.refs_8_.refs_7_ = bf16[4,256,256]{2,1,0:T(8,128)(2,1)} collective-permute-done((bf16[4,256,256]{2,1,0:T(8,128)(2,1)S(1)}, bf16[4,256,256]{2,1,0:T(8,128)(2,1)}, u32[]{:S(2)}, u32[]{:S(2)}) %collective-permute-start.14) | collective-permute-done | bytes 524320 | tf_op jit(solution)/shard_map/ppermute | solution.py:39
  85.6 1.0 copy-done.3
  86.7 8.6 %gate_matmul.1 = bf16[1024,4096]{1,0:T(8,128)(2,1)} custom-call(bf16[1024,512]{1,0:T(8,128)(2,1)S(1)} %copy.12.refs_0_, bf16[4,256,256]{2,1,0:T(8,128)(2,1)S(1)} %pad_maximum_fusion.1.refs_1_.refs_0_, bf16[4,256,256]{2,1,0:T(8,128)(2,1)S(1)} %copy-done.3, bf16[4,256,256]{2,1,0:T(8,128)(2,1)} %collective-permute-done.10.refs_3_.refs_2_, ...), custom_call_target="tpu_custom_call" | custom-call | flops 4294967296 | bytes 12582912 | tf_op jit(solution)/shard_map/gate_matmul/pallas_call | solution.py:64
  95.3 18.8 %all-gather.2.cloned.1.call-done.rows_ref = bf16[1024,4096]{1,0:T(8,128)(2,1)} async-done(((bf16[128,4096]{1,0:T(8,128)(2,1)}), bf16[1024,4096]{1,0:T(8,128)(2,1)}) %all-gather.2.cloned.1.call-update) | async-done | bytes 8388624 | tf_op jit(solution)/shard_map/all_gather | solution.py:690
  114.1 9.9 %weight_grad.1 = (bf16[4,256,256]{2,1,0:T(8,128)(2,1)}, bf16[4,256,256]{2,1,0:T(8,128)(2,1)}, bf16[4,256,256]{2,1,0:T(8,128)(2,1)}, bf16[4,256,256]{2,1,0:T(8,12...) custom-call(s32[8]{0:T(128)S(1)} %fusion.6.origin.place, ...), custom_call_target="tpu_custom_call" | custom-call | flops 4294967296 | bytes 12582912 | tf_op jit(solution)/shard_map/weight_grad/pallas_call | solution.py:64
  124.0 2.4 collective-permute-start.23
  126.4 1.5 collective-permute-start.21
  127.8 1.2 collective-permute-start.17
  129.0 2.4 collective-permute-start.16
  131.5 9.9 %output.1 = (bf16[1024,256]{1,0:T(8,128)(2,1)}, bf16[1024,256]{1,0:T(8,128)(2,1)}) custom-call(s32[8]{0:T(128)S(1)} %fusion.6.origin.place, bf16[1024,4096]{1,0:T(8,128)(2,1)} %all-gather.2.cloned.1.call-done.rows_ref, bf16[4,256,256]{2,1,0:T(8,128)(2,1)S(1)} %pad_maximum_fusion.1.refs_1_.refs_0_, bf16[4,256,256]{2,1,0:T(8,128)(2,1)S(1)} %copy-done.4, ...), custom_call_target="tpu_custom_call" | custom-call | flops 4294967296 | bytes 12582912 | tf_op jit(solution)/shard_map/output/pallas_call | solution.py:64
  141.4 1.3 collective-permute-start.15
  142.6 1.5 collective-permute-start.27
  144.2 6.7 %collective-permute-done.21 = bf16[4,256,256]{2,1,0:T(8,128)(2,1)} collective-permute-done((bf16[4,256,256]{2,1,0:T(8,128)(2,1)}, bf16[4,256,256]{2,1,0:T(8,128)(2,1)}, u32[]{:S(2)}, u32[]{:S(2)}) %collective-permute-start.21) | collective-permute-done | bytes 524320 | tf_op jit(solution)/shard_map/ppermute | solution.py:39
  150.9 1.5 add_convert_fusion
  152.4 1.3 collective-permute-start.26
  153.7 2.4 collective-permute-start.25
  156.1 1.2 collective-permute-start.24
  157.6 2.5 collective-permute-start.20
  160.1 1.9 collective-permute-done.27
  162.1 1.3 maximum_select_fusion
  163.4 3.5 %collective-permute-start.18 = (bf16[256,256]{1,0:T(8,128)(2,1)S(1)}, bf16[256,256]{1,0:T(8,128)(2,1)S(1)}, u32[]{:S(2)}, u32[]{:S(2)}) collective-permute-start(bf16[256,256]{1,0:T(8,128)(2,1)S(1)} %get-tuple-element.130), channel_id=1, source_target_pairs={{0,8},{8,0},{1,9},{9,1},{2,10},{10,2},{3,11},{11,3},{4,12},{12,4},... | collective-permute-start | bytes 393224 | tf_op jit(solution)/shard_map/ppermute | solution.py:39
  167.0 3.2 %collective-permute-done.18 = bf16[256,256]{1,0:T(8,128)(2,1)S(1)} collective-permute-done((bf16[256,256]{1,0:T(8,128)(2,1)S(1)}, bf16[256,256]{1,0:T(8,128)(2,1)S(1)}, u32[]{:S(2)}, u32[]{:S(2)}) %collective-permute-start.18) | collective-permute-done | bytes 131104 | tf_op jit(solution)/shard_map/ppermute | solution.py:39
  170.3 3.6 %gate_back.1 = (bf16[128,4096]{1,0:T(8,128)(2,1)}, bf16[128,4096]{1,0:T(8,128)(2,1)}) custom-call(s32[8]{0:T(128)S(1)} %fusion.6.origin.place, bf16[128,4096]{1,0:T(8,128)(2,1)} %reduce-scatter.2.cloned.1.call-done.gate_grad_ref, bf16[128,4096]{1,0:T(8,128)(2,1)} %get-tuple-element.67.query_ref, bf16[128,4096]{1,0:T(8,128)(2,1)} %get-tuple-element.101.mixed_ref), custom_call_target="tpu_custom_call" | custom-call | flops 1048576 | bytes 5242880 | tf_op jit(solution)/shard_map/gate_back/pallas_call | solution.py:64
  173.9 4.6 %collective-permute-start.28 = (bf16[128,4096]{1,0:T(8,128)(2,1)}, bf16[128,4096]{1,0:T(8,128)(2,1)S(1)}, u32[]{:S(2)}, u32[]{:S(2)}) collective-permute-start(bf16[128,4096]{1,0:T(8,128)(2,1)} %get-tuple-element.102.grad_ref), channel_id=1, source_target_pairs={{1,0},{2,1},{3,2},{4,3},{5,4},{6,5},{7,6},{8,7},{9,8},{10,9},{11,1... | collective-permute-start | bytes 3145736 | tf_op jit(solution)/shard_map/ppermute | solution.py:27
  178.5 9.1 %long_grad.1 = (f32[256,128]{1,0:T(8,128)S(1)}, f32[8,4096]{1,0:T(8,128)S(1)}) custom-call(bf16[128,4096]{1,0:T(8,128)(2,1)} %copy-done.1, bf16[128,4096]{1,0:T(8,128)(2,1)} %get-tuple-element.64.cur_ref, bf16[128,4096]{1,0:T(8,128)(2,1)} %get-tuple-element.102.grad_ref, bf16[128,4096]{1,0:T(8,128)(2,1)} %get-tuple-element.106.feature_ref, ...), custom_call_target="tpu_custom_call" | custom-call | flops 2147483648 | bytes 5242880 | tf_op jit(solution)/shard_map/long_grad/pallas_call | solution.py:64
  187.7 3.7 %collective-permute-done.28.next_ref = bf16[128,4096]{1,0:T(8,128)(2,1)S(1)} collective-permute-done((bf16[128,4096]{1,0:T(8,128)(2,1)}, bf16[128,4096]{1,0:T(8,128)(2,1)S(1)}, u32[]{:S(2)}, u32[]{:S(2)}) %collective-permute-start.28) | collective-permute-done | bytes 1048608 | tf_op jit(solution)/shard_map/ppermute | solution.py:27
  191.3 11.3 %unmix.1 = (bf16[2,128,4096]{2,1,0:T(8,128)(2,1)}, f32[8,4096]{1,0:T(8,128)S(1)}, f32[8,4096]{1,0:T(8,128)S(1)}) custom-call(f32[256,128]{1,0:T(8,128)S(1)} %convert_element_type.63.lines_ref, bf16[128,4096]{1,0:T(8,128)(2,1)} %get-tuple-element.102.grad_ref, bf16[128,4096]{1,0:T(8,128)(2,1)S(1)} %collective-permute-done.28.next_ref, ...), custom_call_target="tpu_custom_call" | custom-call | flops 2147483648 | bytes 8388608 | tf_op jit(solution)/shard_map/unmix/pallas_call | solution.py:64
  205.5 4.4 %collective-permute-start.33 = (f32[16,8,128]{2,1,0:T(8,128)S(1)}, f32[16,8,128]{2,1,0:T(8,128)S(1)}, u32[]{:S(2)}, u32[]{:S(2)}) collective-permute-start(f32[16,8,128]{2,1,0:T(8,128)S(1)} %get-tuple-element.137), channel_id=1, source_target_pairs={{0,6},{2,0},{4,2},{6,4},{1,7},{3,1},{5,3},{7,5},{8,14},{10,8},{12,... | collective-permute-start | bytes 196616 | tf_op jit(solution)/shard_map/ppermute | solution.py:39
  210.6 3.0 %collective-permute-start.29 = (bf16[3,8,4096]{2,1,0:T(8,128)(2,1)S(1)}, bf16[3,8,4096]{2,1,0:T(8,128)(2,1)S(1)}, u32[]{:S(2)}, u32[]{:S(2)}) collective-permute-start(bf16[3,8,4096]{2,1,0:T(8,128)(2,1)S(1)} %pad_maximum_fusion.3), channel_id=1, source_target_pairs={{1,0},{2,1},{3,2},{4,3},{5,4},{6,5},{7,6},{8,7},{9,8},{10,9},{11,1... | collective-permute-start | bytes 589832 | tf_op jit(solution)/shard_map/ppermute | solution.py:27
  213.6 1.0 collective-permute-done.32
  215.4 1.3 collective-permute-start.34
  216.7 2.4 collective-permute-start.35
  219.1 1.2 collective-permute-start.36
  220.3 3.2 %short_adjoint.2.refs_0_ = bf16[128,12288]{1,0:T(8,128)(2,1)} custom-call(bf16[1,128,4096]{2,1,0:T(8,128)(2,1)} %bitcast.51, bf16[3,8,4096]{2,1,0:T(8,128)(2,1)S(1)} %collective-permute-done.29.rim_ref, f32[7,12288]{1,0:T(8,128)} %filter_ref.3), custom_call_target="tpu_custom_call" | custom-call | flops 7340032 | bytes 2097152 | tf_op jit(solution)/shard_map/short_adjoint/pallas_call | solution.py:64
  223.6 1.5 collective-permute-start.39
  225.1 1.1 collective-permute-start.37
  226.3 2.1 collective-permute-done.38
  228.7 3.9 %collective-permute-start.40 = (f32[16,8,128]{2,1,0:T(8,128)S(1)}, f32[16,8,128]{2,1,0:T(8,128)S(1)}, u32[]{:S(2)}, u32[]{:S(2)}) collective-permute-start(f32[16,8,128]{2,1,0:T(8,128)S(1)} %add_add_fusion), channel_id=1, source_target_pairs={{0,1},{1,0},{2,3},{3,2},{4,5},{5,4},{6,7},{7,6},{8,9},{9,8},{10,11... | collective-permute-start | bytes 196616 | tf_op jit(solution)/shard_map/ppermute | solution.py:39
  233.6 1.3 collective-permute-start.41
  236.6 5.1 %short_adjoint.3 = bf16[128,12288]{1,0:T(8,128)(2,1)} custom-call(bf16[2,128,4096]{2,1,0:T(8,128)(2,1)} %get-tuple-element.105.grads_ref, bf16[3,8,4096]{2,1,0:T(8,128)(2,1)S(1)} %collective-permute-done.29.rim_ref, f32[7,12288]{1,0:T(8,128)} %filter_ref.3, bf16[128,12288]{1,0:T(8,128)(2,1)} %short_adjoint.2.refs_0_), custom_call_target="tpu_custom_call", output_to_operand_aliasing={{}: (3, {})} | custom-call | flops 14680064 | bytes 4194304 | tf_op jit(solution)/shard_map/short_adjoint/pallas_call | solution.py:64
  241.7 2.3 collective-permute-done.43.refs_3_
  244.0 1.5 collect.1
  (96 shorter events, 12.8 us)
Async XLA Ops:
  7.2 106.9 %all-gather.2.cloned.1.call-start = ((), (), s32[]{:S(2)}) async-start(), calls=%async_computation.1 | async-start | bytes 9437184 | tf_op jit(solution)/shard_map/all_gather | solution.py:690
  8.2 7.5 %collective-permute-start = (bf16[8,12288]{1,0:T(8,128)(2,1)S(1)}, bf16[8,12288]{1,0:T(8,128)(2,1)S(1)}, u32[]{:S(2)}, u32[]{:S(2)}) collective-permute-start(bf16[8,12288]{1,0:T(8,128)(2,1)S(1)} %slice_bitcast_fusion), channel_id=1, source_target_pairs={{0,1},{1,2},{2,3},{3,4},{4,5},{5,6},{6,7},{7,8},{8,9},{9,10},{10,1... | collective-permute-start | bytes 589832 | tf_op jit(solution)/shard_map/ppermute | solution.py:27
  15.7 6.8 %copy-start = (bf16[8,12288]{1,0:T(8,128)(2,1)}, bf16[8,12288]{1,0:T(8,128)(2,1)S(1)}, u32[]{:S(2)}) copy-start(bf16[8,12288]{1,0:T(8,128)(2,1)S(1)} %collective-permute-done.refs_3_.refs_4_.refs_5_.key_rim_ref.value_rim_ref.rim_ref) | copy-start | bytes 589828
  15.7 11.2 %copy-start.9 = (bf16[512,256]{1,0:T(8,128)(2,1)S(1)}, bf16[512,256]{1,0:T(8,128)(2,1)}, u32[]{:S(2)}) copy-start(bf16[512,256]{1,0:T(8,128)(2,1)} %param.8) | copy-start | bytes 786436
  15.7 21.3 %copy-start.10 = (bf16[256,128]{1,0:T(8,128)(2,1)S(1)}, bf16[256,128]{1,0:T(8,128)(2,1)}, u32[]{:S(2)}) copy-start(bf16[256,128]{1,0:T(8,128)(2,1)} %param.7) | copy-start | bytes 196612
  22.5 17.2 %collective-permute-start.1 = (bf16[128,4096]{1,0:T(8,128)(2,1)}, bf16[128,4096]{1,0:T(8,128)(2,1)S(1)}, u32[]{:S(2)}, u32[]{:S(2)}) collective-permute-start(bf16[128,4096]{1,0:T(8,128)(2,1)} %get-tuple-element.64.cur_ref), channel_id=1, source_target_pairs={{0,1},{1,2},{2,3},{3,4},{4,5},{5,6},{6,7},{7,8},{8,9},{9,10},{10,1... | collective-permute-start | bytes 3145736 | tf_op jit(solution)/shard_map/ppermute | solution.py:27
  26.9 5.4 %collective-permute-start.2 = (bf16[256,256]{1,0:T(8,128)(2,1)S(1)}, bf16[256,256]{1,0:T(8,128)(2,1)S(1)}, u32[]{:S(2)}, u32[]{:S(2)}) collective-permute-start(bf16[256,256]{1,0:T(8,128)(2,1)S(1)} %get-tuple-element.78), channel_id=1, source_target_pairs={{0,8},{8,0},{1,9},{9,1},{2,10},{10,2},{3,11},{11,3},{4,12},{12,4},... | collective-permute-start | bytes 393224 | tf_op jit(solution)/shard_map/ppermute | solution.py:39
  29.7 5.5 %collective-permute-start.3 = (bf16[256,256]{1,0:T(8,128)(2,1)S(1)}, bf16[256,256]{1,0:T(8,128)(2,1)S(1)}, u32[]{:S(2)}, u32[]{:S(2)}) collective-permute-start(bf16[256,256]{1,0:T(8,128)(2,1)S(1)} %get-tuple-element.78), channel_id=1, source_target_pairs={{0,16},{16,0},{1,17},{17,1},{2,18},{18,2},{3,19},{19,3},{4,20},{20... | collective-permute-start | bytes 393224 | tf_op jit(solution)/shard_map/ppermute | solution.py:39
  30.1 7.0 %collective-permute-start.4 = (bf16[256,256]{1,0:T(8,128)(2,1)S(1)}, bf16[256,256]{1,0:T(8,128)(2,1)S(1)}, u32[]{:S(2)}, u32[]{:S(2)}) collective-permute-start(bf16[256,256]{1,0:T(8,128)(2,1)S(1)} %get-tuple-element.78), channel_id=1, source_target_pairs={{0,24},{8,16},{16,8},{24,0},{1,25},{9,17},{17,9},{25,1},{2,26},{10... | collective-permute-start | bytes 393224 | tf_op jit(solution)/shard_map/ppermute | solution.py:39
  30.6 6.4 %collective-permute-start.5 = (bf16[256,256]{1,0:T(8,128)(2,1)S(1)}, bf16[256,256]{1,0:T(8,128)(2,1)S(1)}, u32[]{:S(2)}, u32[]{:S(2)}) collective-permute-start(bf16[256,256]{1,0:T(8,128)(2,1)S(1)} %get-tuple-element.82), channel_id=1, source_target_pairs={{0,32},{32,64},{64,96},{96,0},{1,33},{33,65},{65,97},{97,1},{2,34}... | collective-permute-start | bytes 393224 | tf_op jit(solution)/shard_map/ppermute | solution.py:39
  32.3 6.2 %collective-permute-start.6 = (bf16[256,256]{1,0:T(8,128)(2,1)S(1)}, bf16[256,256]{1,0:T(8,128)(2,1)S(1)}, u32[]{:S(2)}, u32[]{:S(2)}) collective-permute-start(bf16[256,256]{1,0:T(8,128)(2,1)S(1)} %get-tuple-element.82), channel_id=1, source_target_pairs={{0,64},{32,96},{64,0},{96,32},{1,65},{33,97},{65,1},{97,33},{2,66}... | collective-permute-start | bytes 393224 | tf_op jit(solution)/shard_map/ppermute | solution.py:39
  35.2 4.4 %collective-permute-start.7 = (bf16[256,256]{1,0:T(8,128)(2,1)S(1)}, bf16[256,256]{1,0:T(8,128)(2,1)S(1)}, u32[]{:S(2)}, u32[]{:S(2)}) collective-permute-start(bf16[256,256]{1,0:T(8,128)(2,1)S(1)} %get-tuple-element.82), channel_id=1, source_target_pairs={{0,96},{32,0},{64,32},{96,64},{1,97},{33,1},{65,33},{97,65},{2,98}... | collective-permute-start | bytes 393224 | tf_op jit(solution)/shard_map/ppermute | solution.py:39
  39.7 9.7 %copy-start.1 = (bf16[128,4096]{1,0:T(8,128)(2,1)}, bf16[128,4096]{1,0:T(8,128)(2,1)S(1)}, u32[]{:S(2)}) copy-start(bf16[128,4096]{1,0:T(8,128)(2,1)S(1)} %collective-permute-done.1.prev_ref) | copy-start | bytes 3145732
  39.7 9.8 %copy-start.5 = (bf16[1,2048,256]{2,1,0:T(8,128)(2,1)S(1)}, bf16[1,2048,256]{2,1,0:T(8,128)(2,1)}, u32[]{:S(2)}) copy-start(bf16[1,2048,256]{2,1,0:T(8,128)(2,1)} %param.9) | copy-start | bytes 3145732
  49.4 120.8 %reduce-scatter.2.cloned.1.call-start = ((), (), s32[]{:S(2)}) async-start(), calls=%async_computation.2 | async-start | bytes 9437184 | tf_op jit(solution)/shard_map/reduce_scatter | solution.py:697
  50.3 9.6 %collective-permute-start.8 = (bf16[1024,256]{0,1:T(8,128)(2,1)S(1)}, bf16[1024,256]{0,1:T(8,128)(2,1)S(1)}, u32[]{:S(2)}, u32[]{:S(2)}) collective-permute-start(bf16[1024,256]{0,1:T(8,128)(2,1)S(1)} %get-tuple-element.129), channel_id=1, source_target_pairs={{0,8},{8,0},{1,9},{9,1},{2,10},{10,2},{3,11},{11,3},{4,12},{12,4},... | collective-permute-start | bytes 1572872 | tf_op jit(solution)/shard_map/ppermute | solution.py:39
  53.2 9.9 %collective-permute-start.9 = (bf16[4,256,256]{2,1,0:T(8,128)(2,1)S(1)}, bf16[4,256,256]{2,1,0:T(8,128)(2,1)S(1)}, u32[]{:S(2)}, u32[]{:S(2)}) collective-permute-start(bf16[4,256,256]{2,1,0:T(8,128)(2,1)S(1)} %pad_maximum_fusion.1.refs_1_.refs_0_), channel_id=1, source_target_pairs={{0,32},{32,64},{64,96},{96,0},{1,33},{33,65},{65,97},{97,1},{2,34}... | collective-permute-start | bytes 1572872 | tf_op jit(solution)/shard_map/ppermute | solution.py:39
  54.3 18.0 %collective-permute-start.10 = (bf16[4,256,256]{2,1,0:T(8,128)(2,1)S(1)}, bf16[4,256,256]{2,1,0:T(8,128)(2,1)}, u32[]{:S(2)}, u32[]{:S(2)}) collective-permute-start(bf16[4,256,256]{2,1,0:T(8,128)(2,1)S(1)} %pad_maximum_fusion.1.refs_1_.refs_0_), channel_id=1, source_target_pairs={{0,64},{32,96},{64,0},{96,32},{1,65},{33,97},{65,1},{97,33},{2,66}... | collective-permute-start | bytes 1572872 | tf_op jit(solution)/shard_map/ppermute | solution.py:39
  57.5 17.5 %collective-permute-start.11 = (bf16[4,256,256]{2,1,0:T(8,128)(2,1)S(1)}, bf16[4,256,256]{2,1,0:T(8,128)(2,1)}, u32[]{:S(2)}, u32[]{:S(2)}) collective-permute-start(bf16[4,256,256]{2,1,0:T(8,128)(2,1)S(1)} %pad_maximum_fusion.1.refs_1_.refs_0_), channel_id=1, source_target_pairs={{0,96},{32,0},{64,32},{96,64},{1,97},{33,1},{65,33},{97,65},{2,98}... | collective-permute-start | bytes 1572872 | tf_op jit(solution)/shard_map/ppermute | solution.py:39
  57.7 17.3 %collective-permute-start.12 = (bf16[4,256,256]{2,1,0:T(8,128)(2,1)S(1)}, bf16[4,256,256]{2,1,0:T(8,128)(2,1)}, u32[]{:S(2)}, u32[]{:S(2)}) collective-permute-start(bf16[4,256,256]{2,1,0:T(8,128)(2,1)S(1)} %pad_maximum_fusion.2.refs_5_.refs_4_), channel_id=1, source_target_pairs={{0,8},{8,0},{1,9},{9,1},{2,10},{10,2},{3,11},{11,3},{4,12},{12,4},... | collective-permute-start | bytes 1572872 | tf_op jit(solution)/shard_map/ppermute | solution.py:39
  59.9 19.7 %collective-permute-start.13 = (bf16[4,256,256]{2,1,0:T(8,128)(2,1)S(1)}, bf16[4,256,256]{2,1,0:T(8,128)(2,1)}, u32[]{:S(2)}, u32[]{:S(2)}) collective-permute-start(bf16[4,256,256]{2,1,0:T(8,128)(2,1)S(1)} %pad_maximum_fusion.2.refs_5_.refs_4_), channel_id=1, source_target_pairs={{0,16},{16,0},{1,17},{17,1},{2,18},{18,2},{3,19},{19,3},{4,20},{20... | collective-permute-start | bytes 1572872 | tf_op jit(solution)/shard_map/ppermute | solution.py:39
  63.2 0.8 copy-start.2
  64.0 21.7 %collective-permute-start.14 = (bf16[4,256,256]{2,1,0:T(8,128)(2,1)S(1)}, bf16[4,256,256]{2,1,0:T(8,128)(2,1)}, u32[]{:S(2)}, u32[]{:S(2)}) collective-permute-start(bf16[4,256,256]{2,1,0:T(8,128)(2,1)S(1)} %pad_maximum_fusion.2.refs_5_.refs_4_), channel_id=1, source_target_pairs={{0,24},{8,16},{16,8},{24,0},{1,25},{9,17},{17,9},{25,1},{2,26},{10... | collective-permute-start | bytes 1572872 | tf_op jit(solution)/shard_map/ppermute | solution.py:39
  85.6 1.0 copy-start.3
  114.1 17.4 %copy-start.4 = (bf16[4,256,256]{2,1,0:T(8,128)(2,1)S(1)}, bf16[4,256,256]{2,1,0:T(8,128)(2,1)}, u32[]{:S(2)}) copy-start(bf16[4,256,256]{2,1,0:T(8,128)(2,1)} %copy-done.2) | copy-start | bytes 1572868
  124.0 17.4 %collective-permute-start.23 = (bf16[4,256,256]{2,1,0:T(8,128)(2,1)}, bf16[4,256,256]{2,1,0:T(8,128)(2,1)S(1)}, u32[]{:S(2)}, u32[]{:S(2)}) collective-permute-start(bf16[4,256,256]{2,1,0:T(8,128)(2,1)} %get-tuple-element.96), channel_id=1, source_target_pairs={{0,24},{8,16},{16,8},{24,0},{1,25},{9,17},{17,9},{25,1},{2,26},{10... | collective-permute-start | bytes 1572872 | tf_op jit(solution)/shard_map/ppermute | solution.py:39
  126.4 16.3 %collective-permute-start.22 = (bf16[4,256,256]{2,1,0:T(8,128)(2,1)}, bf16[4,256,256]{2,1,0:T(8,128)(2,1)}, u32[]{:S(2)}, u32[]{:S(2)}) collective-permute-start(bf16[4,256,256]{2,1,0:T(8,128)(2,1)} %get-tuple-element.95), channel_id=1, source_target_pairs={{0,16},{16,0},{1,17},{17,1},{2,18},{18,2},{3,19},{19,3},{4,20},{20... | collective-permute-start | bytes 1572872 | tf_op jit(solution)/shard_map/ppermute | solution.py:39
  126.4 24.5 %collective-permute-start.21 = (bf16[4,256,256]{2,1,0:T(8,128)(2,1)}, bf16[4,256,256]{2,1,0:T(8,128)(2,1)}, u32[]{:S(2)}, u32[]{:S(2)}) collective-permute-start(bf16[4,256,256]{2,1,0:T(8,128)(2,1)} %get-tuple-element.94), channel_id=1, source_target_pairs={{0,8},{8,0},{1,9},{9,1},{2,10},{10,2},{3,11},{11,3},{4,12},{12,4},... | collective-permute-start | bytes 1572872 | tf_op jit(solution)/shard_map/ppermute | solution.py:39
  127.8 25.9 %collective-permute-start.17 = (bf16[4,256,256]{2,1,0:T(8,128)(2,1)}, bf16[4,256,256]{2,1,0:T(8,128)(2,1)S(1)}, u32[]{:S(2)}, u32[]{:S(2)}) collective-permute-start(bf16[4,256,256]{2,1,0:T(8,128)(2,1)} %get-tuple-element.92), channel_id=1, source_target_pairs={{0,32},{32,64},{64,96},{96,0},{1,33},{33,65},{65,97},{97,1},{2,34}... | collective-permute-start | bytes 1572872 | tf_op jit(solution)/shard_map/ppermute | solution.py:39
  129.0 12.3 %copy-start.11 = (bf16[4,256,256]{2,1,0:T(8,128)(2,1)S(1)}, bf16[4,256,256]{2,1,0:T(8,128)(2,1)}, u32[]{:S(2)}) copy-start(bf16[4,256,256]{2,1,0:T(8,128)(2,1)} %get-tuple-element.90) | copy-start | bytes 1572868
  129.0 21.8 %copy-start.8 = (bf16[4,256,256]{2,1,0:T(8,128)(2,1)S(1)}, bf16[4,256,256]{2,1,0:T(8,128)(2,1)}, u32[]{:S(2)}) copy-start(bf16[4,256,256]{2,1,0:T(8,128)(2,1)} %get-tuple-element.93) | copy-start | bytes 1572868
  129.0 27.1 %collective-permute-start.16 = (bf16[4,256,256]{2,1,0:T(8,128)(2,1)}, bf16[4,256,256]{2,1,0:T(8,128)(2,1)S(1)}, u32[]{:S(2)}, u32[]{:S(2)}) collective-permute-start(bf16[4,256,256]{2,1,0:T(8,128)(2,1)} %get-tuple-element.91), channel_id=1, source_target_pairs={{0,64},{32,96},{64,0},{96,32},{1,65},{33,97},{65,1},{97,33},{2,66}... | collective-permute-start | bytes 1572872 | tf_op jit(solution)/shard_map/ppermute | solution.py:39
  141.4 16.0 %copy-start.6 = (bf16[4,256,256]{2,1,0:T(8,128)(2,1)S(1)}, bf16[4,256,256]{2,1,0:T(8,128)(2,1)}, u32[]{:S(2)}) copy-start(bf16[4,256,256]{2,1,0:T(8,128)(2,1)} %get-tuple-element.89) | copy-start | bytes 1572868
  141.4 15.9 %collective-permute-start.15 = (bf16[4,256,256]{2,1,0:T(8,128)(2,1)S(1)}, bf16[4,256,256]{2,1,0:T(8,128)(2,1)S(1)}, u32[]{:S(2)}, u32[]{:S(2)}) collective-permute-start(bf16[4,256,256]{2,1,0:T(8,128)(2,1)S(1)} %copy-done.11), channel_id=1, source_target_pairs={{0,96},{32,0},{64,32},{96,64},{1,97},{33,1},{65,33},{97,65},{2,98}... | collective-permute-start | bytes 1572872 | tf_op jit(solution)/shard_map/ppermute | solution.py:39
  142.6 19.4 %collective-permute-start.27 = (bf16[1024,256]{1,0:T(8,128)(2,1)}, bf16[1024,256]{1,0:T(8,128)(2,1)S(1)}, u32[]{:S(2)}, u32[]{:S(2)}) collective-permute-start(bf16[1024,256]{1,0:T(8,128)(2,1)} %get-tuple-element.98), channel_id=1, source_target_pairs={{0,8},{8,0},{1,9},{9,1},{2,10},{10,2},{3,11},{11,3},{4,12},{12,4},... | collective-permute-start | bytes 1572872 | tf_op jit(solution)/shard_map/ppermute | solution.py:39
  152.4 9.7 %copy-start.7 = (bf16[1024,256]{1,0:T(8,128)(2,1)S(1)}, bf16[1024,256]{1,0:T(8,128)(2,1)}, u32[]{:S(2)}) copy-start(bf16[1024,256]{1,0:T(8,128)(2,1)} %get-tuple-element.97) | copy-start | bytes 1572868
  152.4 10.9 %collective-permute-start.26 = (bf16[256,256]{1,0:T(8,128)(2,1)S(1)}, bf16[256,256]{1,0:T(8,128)(2,1)S(1)}, u32[]{:S(2)}, u32[]{:S(2)}) collective-permute-start(bf16[256,256]{1,0:T(8,128)(2,1)S(1)} %get-tuple-element.134), channel_id=1, source_target_pairs={{0,32},{32,64},{64,96},{96,0},{1,33},{33,65},{65,97},{97,1},{2,34}... | collective-permute-start | bytes 393224 | tf_op jit(solution)/shard_map/ppermute | solution.py:39
  153.7 13.1 %collective-permute-start.25 = (bf16[256,256]{1,0:T(8,128)(2,1)S(1)}, bf16[256,256]{1,0:T(8,128)(2,1)S(1)}, u32[]{:S(2)}, u32[]{:S(2)}) collective-permute-start(bf16[256,256]{1,0:T(8,128)(2,1)S(1)} %get-tuple-element.135), channel_id=1, source_target_pairs={{0,64},{32,96},{64,0},{96,32},{1,65},{33,97},{65,1},{97,33},{2,66}... | collective-permute-start | bytes 393224 | tf_op jit(solution)/shard_map/ppermute | solution.py:39
  156.1 10.7 %collective-permute-start.24 = (bf16[256,256]{1,0:T(8,128)(2,1)S(1)}, bf16[256,256]{1,0:T(8,128)(2,1)S(1)}, u32[]{:S(2)}, u32[]{:S(2)}) collective-permute-start(bf16[256,256]{1,0:T(8,128)(2,1)S(1)} %get-tuple-element.133), channel_id=1, source_target_pairs={{0,96},{32,0},{64,32},{96,64},{1,97},{33,1},{65,33},{97,65},{2,98}... | collective-permute-start | bytes 393224 | tf_op jit(solution)/shard_map/ppermute | solution.py:39
  157.6 9.3 %collective-permute-start.20 = (bf16[256,256]{1,0:T(8,128)(2,1)S(1)}, bf16[256,256]{1,0:T(8,128)(2,1)S(1)}, u32[]{:S(2)}, u32[]{:S(2)}) collective-permute-start(bf16[256,256]{1,0:T(8,128)(2,1)S(1)} %get-tuple-element.131), channel_id=1, source_target_pairs={{0,24},{8,16},{16,8},{24,0},{1,25},{9,17},{17,9},{25,1},{2,26},{10... | collective-permute-start | bytes 393224 | tf_op jit(solution)/shard_map/ppermute | solution.py:39
  162.0 4.9 %collective-permute-start.19 = (bf16[256,256]{1,0:T(8,128)(2,1)S(1)}, bf16[256,256]{1,0:T(8,128)(2,1)S(1)}, u32[]{:S(2)}, u32[]{:S(2)}) collective-permute-start(bf16[256,256]{1,0:T(8,128)(2,1)S(1)} %get-tuple-element.132), channel_id=1, source_target_pairs={{0,16},{16,0},{1,17},{17,1},{2,18},{18,2},{3,19},{19,3},{4,20},{20... | collective-permute-start | bytes 393224 | tf_op jit(solution)/shard_map/ppermute | solution.py:39
  163.4 6.8 %collective-permute-start.18 = (bf16[256,256]{1,0:T(8,128)(2,1)S(1)}, bf16[256,256]{1,0:T(8,128)(2,1)S(1)}, u32[]{:S(2)}, u32[]{:S(2)}) collective-permute-start(bf16[256,256]{1,0:T(8,128)(2,1)S(1)} %get-tuple-element.130), channel_id=1, source_target_pairs={{0,8},{8,0},{1,9},{9,1},{2,10},{10,2},{3,11},{11,3},{4,12},{12,4},... | collective-permute-start | bytes 393224 | tf_op jit(solution)/shard_map/ppermute | solution.py:39
  173.9 17.5 %collective-permute-start.28 = (bf16[128,4096]{1,0:T(8,128)(2,1)}, bf16[128,4096]{1,0:T(8,128)(2,1)S(1)}, u32[]{:S(2)}, u32[]{:S(2)}) collective-permute-start(bf16[128,4096]{1,0:T(8,128)(2,1)} %get-tuple-element.102.grad_ref), channel_id=1, source_target_pairs={{1,0},{2,1},{3,2},{4,3},{5,4},{6,5},{7,6},{8,7},{9,8},{10,9},{11,1... | collective-permute-start | bytes 3145736 | tf_op jit(solution)/shard_map/ppermute | solution.py:27
  203.6 1.9 collective-permute-start.30
  205.5 8.1 %collective-permute-start.33 = (f32[16,8,128]{2,1,0:T(8,128)S(1)}, f32[16,8,128]{2,1,0:T(8,128)S(1)}, u32[]{:S(2)}, u32[]{:S(2)}) collective-permute-start(f32[16,8,128]{2,1,0:T(8,128)S(1)} %get-tuple-element.137), channel_id=1, source_target_pairs={{0,6},{2,0},{4,2},{6,4},{1,7},{3,1},{5,3},{7,5},{8,14},{10,8},{12,... | collective-permute-start | bytes 196616 | tf_op jit(solution)/shard_map/ppermute | solution.py:39
  209.9 4.7 %collective-permute-start.32 = (f32[16,8,128]{2,1,0:T(8,128)S(1)}, f32[16,8,128]{2,1,0:T(8,128)S(1)}, u32[]{:S(2)}, u32[]{:S(2)}) collective-permute-start(f32[16,8,128]{2,1,0:T(8,128)S(1)} %get-tuple-element.138), channel_id=1, source_target_pairs={{0,4},{2,6},{4,0},{6,2},{1,5},{3,7},{5,1},{7,3},{8,12},{10,14},{12... | collective-permute-start | bytes 196616 | tf_op jit(solution)/shard_map/ppermute | solution.py:39
  209.9 5.5 %collective-permute-start.31 = (f32[16,8,128]{2,1,0:T(8,128)S(1)}, f32[16,8,128]{2,1,0:T(8,128)S(1)}, u32[]{:S(2)}, u32[]{:S(2)}) collective-permute-start(f32[16,8,128]{2,1,0:T(8,128)S(1)} %get-tuple-element.136), channel_id=1, source_target_pairs={{0,2},{2,4},{4,6},{6,0},{1,3},{3,5},{5,7},{7,1},{8,10},{10,12},{12... | collective-permute-start | bytes 196616 | tf_op jit(solution)/shard_map/ppermute | solution.py:39
  210.6 9.7 %collective-permute-start.29 = (bf16[3,8,4096]{2,1,0:T(8,128)(2,1)S(1)}, bf16[3,8,4096]{2,1,0:T(8,128)(2,1)S(1)}, u32[]{:S(2)}, u32[]{:S(2)}) collective-permute-start(bf16[3,8,4096]{2,1,0:T(8,128)(2,1)S(1)} %pad_maximum_fusion.3), channel_id=1, source_target_pairs={{1,0},{2,1},{3,2},{4,3},{5,4},{6,5},{7,6},{8,7},{9,8},{10,9},{11,1... | collective-permute-start | bytes 589832 | tf_op jit(solution)/shard_map/ppermute | solution.py:27
  215.4 8.1 %collective-permute-start.34 = (f32[16,8,128]{2,1,0:T(8,128)S(1)}, f32[16,8,128]{2,1,0:T(8,128)S(1)}, u32[]{:S(2)}, u32[]{:S(2)}) collective-permute-start(f32[16,8,128]{2,1,0:T(8,128)S(1)} %fusion.5), channel_id=1, source_target_pairs={{0,32},{32,64},{64,96},{96,0},{1,33},{33,65},{65,97},{97,1},{2,34}... | collective-permute-start | bytes 196616 | tf_op jit(solution)/shard_map/ppermute | solution.py:39
  216.7 6.8 %collective-permute-start.35 = (f32[16,8,128]{2,1,0:T(8,128)S(1)}, f32[16,8,128]{2,1,0:T(8,128)S(1)}, u32[]{:S(2)}, u32[]{:S(2)}) collective-permute-start(f32[16,8,128]{2,1,0:T(8,128)S(1)} %fusion.5), channel_id=1, source_target_pairs={{0,64},{32,96},{64,0},{96,32},{1,65},{33,97},{65,1},{97,33},{2,66}... | collective-permute-start | bytes 196616 | tf_op jit(solution)/shard_map/ppermute | solution.py:39
  219.1 4.4 %collective-permute-start.36 = (f32[16,8,128]{2,1,0:T(8,128)S(1)}, f32[16,8,128]{2,1,0:T(8,128)S(1)}, u32[]{:S(2)}, u32[]{:S(2)}) collective-permute-start(f32[16,8,128]{2,1,0:T(8,128)S(1)} %fusion.5), channel_id=1, source_target_pairs={{0,96},{32,0},{64,32},{96,64},{1,97},{33,1},{65,33},{97,65},{2,98}... | collective-permute-start | bytes 196616 | tf_op jit(solution)/shard_map/ppermute | solution.py:39
  223.5 4.8 %collective-permute-start.38 = (f32[16,8,128]{2,1,0:T(8,128)S(1)}, f32[16,8,128]{2,1,0:T(8,128)S(1)}, u32[]{:S(2)}, u32[]{:S(2)}) collective-permute-start(f32[16,8,128]{2,1,0:T(8,128)S(1)} %add_add_fusion.1), channel_id=1, source_target_pairs={{0,8},{8,0},{1,9},{9,1},{2,10},{10,2},{3,11},{11,3},{4,12},{12,4},... | collective-permute-start | bytes 196616 | tf_op jit(solution)/shard_map/ppermute | solution.py:39
  223.6 5.1 %collective-permute-start.39 = (f32[16,8,128]{2,1,0:T(8,128)S(1)}, f32[16,8,128]{2,1,0:T(8,128)S(1)}, u32[]{:S(2)}, u32[]{:S(2)}) collective-permute-start(f32[16,8,128]{2,1,0:T(8,128)S(1)} %add_add_fusion.1), channel_id=1, source_target_pairs={{0,24},{8,16},{16,8},{24,0},{1,25},{9,17},{17,9},{25,1},{2,26},{10... | collective-permute-start | bytes 196616 | tf_op jit(solution)/shard_map/ppermute | solution.py:39
  225.1 3.6 %collective-permute-start.37 = (f32[16,8,128]{2,1,0:T(8,128)S(1)}, f32[16,8,128]{2,1,0:T(8,128)S(1)}, u32[]{:S(2)}, u32[]{:S(2)}) collective-permute-start(f32[16,8,128]{2,1,0:T(8,128)S(1)} %add_add_fusion.1), channel_id=1, source_target_pairs={{0,16},{16,0},{1,17},{17,1},{2,18},{18,2},{3,19},{19,3},{4,20},{20... | collective-permute-start | bytes 196616 | tf_op jit(solution)/shard_map/ppermute | solution.py:39
  228.7 4.8 %collective-permute-start.40 = (f32[16,8,128]{2,1,0:T(8,128)S(1)}, f32[16,8,128]{2,1,0:T(8,128)S(1)}, u32[]{:S(2)}, u32[]{:S(2)}) collective-permute-start(f32[16,8,128]{2,1,0:T(8,128)S(1)} %add_add_fusion), channel_id=1, source_target_pairs={{0,1},{1,0},{2,3},{3,2},{4,5},{5,4},{6,7},{7,6},{8,9},{9,8},{10,11... | collective-permute-start | bytes 196616 | tf_op jit(solution)/shard_map/ppermute | solution.py:39
  233.6 8.1 %collective-permute-start.41 = (f32[32,8,128]{2,1,0:T(8,128)S(1)}, f32[32,8,128]{2,1,0:T(8,128)S(1)}, u32[]{:S(2)}, u32[]{:S(2)}) collective-permute-start(f32[32,8,128]{2,1,0:T(8,128)S(1)} %pad_maximum_fusion.4.refs_0_), channel_id=1, source_target_pairs={{0,6},{2,0},{4,2},{6,4},{1,7},{3,1},{5,3},{7,5},{8,14},{10,8},{12,... | collective-permute-start | bytes 393224 | tf_op jit(solution)/shard_map/ppermute | solution.py:39
  234.9 6.9 %collective-permute-start.42 = (f32[32,8,128]{2,1,0:T(8,128)S(1)}, f32[32,8,128]{2,1,0:T(8,128)S(1)}, u32[]{:S(2)}, u32[]{:S(2)}) collective-permute-start(f32[32,8,128]{2,1,0:T(8,128)S(1)} %pad_maximum_fusion.4.refs_0_), channel_id=1, source_target_pairs={{0,4},{2,6},{4,0},{6,2},{1,5},{3,7},{5,1},{7,3},{8,12},{10,14},{12... | collective-permute-start | bytes 393224 | tf_op jit(solution)/shard_map/ppermute | solution.py:39
  234.9 9.1 %collective-permute-start.43 = (f32[32,8,128]{2,1,0:T(8,128)S(1)}, f32[32,8,128]{2,1,0:T(8,128)S(1)}, u32[]{:S(2)}, u32[]{:S(2)}) collective-permute-start(f32[32,8,128]{2,1,0:T(8,128)S(1)} %pad_maximum_fusion.4.refs_0_), channel_id=1, source_target_pairs={{0,2},{2,4},{4,6},{6,0},{1,3},{3,5},{5,7},{7,1},{8,10},{10,12},{12... | collective-permute-start | bytes 393224 | tf_op jit(solution)/shard_map/ppermute | solution.py:39
Sparse Core Ops, SparseCore 0:
  49.6 64.4 all-gather.1
  116.5 51.5 reduce-scatter.1

commit v8 on v7

--- a/solution.py
+++ b/solution.py
@@ -306,12 +306,13 @@
 
 def unmix_kernel(
     per_group, short_taps, lines_ref, grad_ref, next_ref, key_ref, value_ref, key_tokens_ref, value_tokens_ref,
-    key_rim_ref, value_rim_ref, feature_ref, key_sum_ref, value_sum_ref, table, ext,
+    key_rim_ref, value_rim_ref, query_grad_ref, feature_ref, key_sum_ref, value_sum_ref, edge_ref, table, ext,
 ):
     rows, width = grad_ref.shape
     row, lane = lane_row((rows, rows))
     below = lane < row
     packed = LANES // per_group
+    edge_ref[0] = query_grad_ref[0:RIM, :]
     for block in range(width // LANES):
         at = pl.ds(block * LANES, LANES)
         own = table.at[block % 2]
@@ -326,15 +327,16 @@
         value_grad = (grad_mixer * key_ref[:, at].astype(F32)).astype(BF16)
         feature_ref[0, :, at] = key_grad
         feature_ref[1, :, at] = value_grad
+        edge_ref[1, :, at] = key_grad[0:RIM]
+        edge_ref[2, :, at] = value_grad[0:RIM]
         slot = 2 * (block % 2)
         tap_sums(short_taps, key_grad, key_tokens_ref, key_rim_ref, key_sum_ref, at, ext.at[slot])
         tap_sums(short_taps, value_grad, value_tokens_ref, value_rim_ref, value_sum_ref, at, ext.at[slot + 1])
 
 
-def unmix_call(lines, short_taps, grad, grad_next, key, value, tokens, rim):
+def unmix_call(lines, short_taps, grad, grad_next, key, value, tokens, rim, query_grad):
     rows, channels = grad.shape
-    groups, taps = lines.shape
-    per_group = channels // groups
+    per_group = channels // lines.shape[0]
     width = block_width(channels, WIDTH)
     steps = channels // width
 
@@ -342,22 +344,34 @@
         return pl.BlockSpec((height, width), lambda i, part=part: (0, i + part * steps))
 
     wide = spec(rows, 0)
-    packed = LANES // per_group
     sums = jax.ShapeDtypeStruct((8, channels), F32)
     return hbm_call(
         functools.partial(unmix_kernel, per_group, short_taps),
         loose=(0, 2),
         grid=(steps,),
-        in_specs=[pl.BlockSpec((width // per_group, taps), lambda i: (i, 0))]
+        in_specs=[pl.BlockSpec((width // per_group, rows), lambda i: (i, 0))]
         + [wide] * 4
-        + [spec(rows, 1), spec(rows, 2), spec(RIM, 1), spec(RIM, 2)],
-        out_specs=[pl.BlockSpec((2, rows, width), lambda i: (0, 0, i)), spec(8, 0), spec(8, 0)],
-        out_shape=[jax.ShapeDtypeStruct((2, rows, channels), BF16), sums, sums],
-        scratch_shapes=[pltpu.VMEM((2, packed * rows, 2 * rows), BF16), pltpu.VMEM((4, RIM + rows, LANES), F32)],
+        + [spec(rows, 1), spec(rows, 2), spec(RIM, 1), spec(RIM, 2), spec(2 * RIM, 0)],
+        out_specs=[
+            pl.BlockSpec((2, rows, width), lambda i: (0, 0, i)),
+            spec(8, 0),
+            spec(8, 0),
+            pl.BlockSpec((3, RIM, width), lambda i: (0, 0, i)),
+        ],
+        out_shape=[
+            jax.ShapeDtypeStruct((2, rows, channels), BF16),
+            sums,
+            sums,
+            jax.ShapeDtypeStruct((3, RIM, channels), BF16),
+        ],
+        scratch_shapes=[
+            pltpu.VMEM((2, LANES // per_group * rows, 2 * rows), BF16),
+            pltpu.VMEM((4, RIM + rows, LANES), F32),
+        ],
         compiler_params=params(),
-        cost_estimate=cost(2 * groups * rows * 2 * rows * LANES, 16 * rows * channels),
+        cost_estimate=cost(2 * channels * rows * 2 * rows * LANES // per_group, 16 * rows * channels),
         name="unmix",
-    )(lines, grad, grad_next, key, value, tokens, tokens, rim, rim)
+    )(lines, grad, grad_next, key, value, tokens, tokens, rim, rim, query_grad)
 
 
 def short_adjoint_kernel(short_taps, grads_ref, rim_ref, filter_ref, *refs):
@@ -483,11 +497,12 @@
     return paired_sum([terms[i] + terms[i + half] for i in range(half)])
 
 
-def gather_near(shard):
-    ny = lax.axis_size("y")
-    half = shard.shape[0] // 2
-    top, bottom = shard[:half], shard[half:]
-    return [move(top, xl=a, xh=b) for a, b in FLIPS], [move(bottom, y=d) for d in range(ny)]
+def gather_tall(shard):
+    return [move(shard[shard.shape[0] // 2 :], y=d) for d in range(lax.axis_size("y"))]
+
+
+def gather_wide(shard):
+    return [move(shard[: shard.shape[0] // 2], xl=a, xh=b) for a, b in FLIPS]
 
 
 def gather_far(wide_top, tall_bottom):
@@ -683,10 +698,11 @@
     query, key, value, mixer = features_call(tokens, rim, short_filter)
     mixer, out_weight = lax.optimization_barrier((mixer, out_weight))
     mixer_prev = along(mixer, 1)
-    wide_top, tall_bottom = gather_near(out_weight)
-    mixer_prev, wide_top, tall_bottom = lax.optimization_barrier((mixer_prev, wide_top, tall_bottom))
+    tall_bottom = gather_tall(out_weight)
+    mixer_prev, tall_bottom = lax.optimization_barrier((mixer_prev, tall_bottom))
     mixed, gated = mix_call(lines, mixer_prev, mixer, query)
-    mixed, wide_top, tall_bottom, upstream = lax.optimization_barrier((mixed, wide_top, tall_bottom, upstream))
+    mixed, out_weight, tall_bottom, upstream = lax.optimization_barrier((mixed, out_weight, tall_bottom, upstream))
+    wide_top = gather_wide(out_weight)
     all_rows = lax.all_gather(gated, ("z", "c"), axis=0, tiled=True)
     tops, bottoms = gather_far(wide_top, tall_bottom)
     mine = lax.dynamic_slice_in_dim(upstream, xh * span, span, 0)
@@ -708,10 +724,10 @@
     long_sum, query_sum = long_grad_call(
         groups, short_taps, mixer_prev, mixer, grad_mixed, query_grad, tokens, rim
     )
-    other_grads, key_sum, value_sum = unmix_call(
-        lines, short_taps, grad_mixed, grad_next, key, value, tokens, rim
+    other_grads, key_sum, value_sum, edge = unmix_call(
+        lines, short_taps, grad_mixed, grad_next, key, value, tokens, rim, query_grad
     )
-    edge = along(jnp.concatenate([query_grad[None, :RIM], other_grads[:, :RIM]], axis=0), -1)
+    edge = along(edge, -1)
     grad_tokens = short_adjoint_call(query_grad[None], edge, short_filter, 0, None)
     grad_short, grad_long, grad_tokens = total_over_devices(
         spread_to, collect_from, query_sum, key_sum, value_sum, long_sum, short_taps, grad_tokens

time: 253 us -> 261 us (1.032)
  waiting for transfers between devices: 70 us -> 79 us
    ppermute x40, waiting for transfers between devices: 44.8 us -> 67.4 us  [move(): return lax.ppermute(x, axes, pairs)]
    all_gather x1, waiting for transfers between devices: 18.8 us -> 0.01 us  [shards(): all_rows = lax.all_gather(gated, ('z', 'c'), axis=0, tiled=True)]
    ppermute x4, waiting for transfers between devices: 6.28 us -> 10.3 us  [along(): return lax.ppermute(x, LINE, pairs)]
  transfers between devices with their start and end apart: 46 -> 46, of which waited for: 21 -> 23; matrix products, arithmetic and copies ran while one was open for 4% -> 3% of each run, Pallas kernels for 18% -> 18%
where the time goes in v8:
time: 261 us; the launch traced here: 260 us
  Pallas kernels  79.5 us (30%)
  waiting for transfers between devices  79 us (30%)
  starting transfers between devices  76.8 us (29%)
  between operations  14.4 us (6%)
  local copies, waits for them, and re-layouts  6.15 us (2%)
  other arithmetic  4.65 us (2%)
    pallas_call x10, Pallas kernels, run(): return call(*held)  77.2 us
    ppermute x40, waiting for transfers between devices, move(): return lax.ppermute(x, axes, pairs)  67.4 us
    ppermute x40, starting transfers between devices, move(): return lax.ppermute(x, axes, pairs)  59.8 us
    ppermute x4, starting transfers between devices, along(): return lax.ppermute(x, LINE, pairs)  16.9 us
    ppermute x4, waiting for transfers between devices, along(): return lax.ppermute(x, LINE, pairs)  10.3 us
  transfers between devices with their start and end apart: 46, of which 23 were waited for; matrix products, arithmetic and copies ran while one was open for 3% of the time, Pallas kernels for 18%

profile of v8, /device:TPU:1, one launch (start us, length us, event | category | flops | bytes accessed | tf_op | source)
XLA Modules:
  0.0 260.5 jit_solution(12002092257896216661)
XLA Ops:
  8.2 4.9 %collective-permute-start = (bf16[8,12288]{1,0:T(8,128)(2,1)S(1)}, bf16[8,12288]{1,0:T(8,128)(2,1)S(1)}, u32[]{:S(2)}, u32[]{:S(2)}) collective-permute-start(bf16[8,12288]{1,0:T(8,128)(2,1)S(1)} %slice_bitcast_fusion), channel_id=1, source_target_pairs={{0,1},{1,2},{2,3},{3,4},{4,5},{5,6},{6,7},{7,8},{8,9},{9,10},{10,1... | collective-permute-start | bytes 589832 | tf_op jit(solution)/shard_map/ppermute | solution.py:27
  13.1 2.6 collective-permute-done.refs_3_.refs_4_.refs_5_.key_rim_ref.value_rim_ref.rim_ref
  15.7 6.8 %features.1 = (bf16[128,4096]{1,0:T(8,128)(2,1)}, bf16[128,4096]{1,0:T(8,128)(2,1)}, bf16[128,4096]{1,0:T(8,128)(2,1)}, bf16[128,4096]{1,0:T(8,128)(2,1)}) custom-call(bf16[128,12288]{1,0:T(8,128)(2,1)} %bitcast.42, bf16[128,12288]{1,0:T(8,128)(2,1)} %bitcast.43, bf16[128,12288]{1,0:T(8,128)(2,1)} %bitcast.44, ...), custom_call_target="tpu_custom_call" | custom-call | bytes 1572864 | tf_op jit(solution)/shard_map/features/pallas_call | solution.py:64
  22.5 4.4 %collective-permute-start.1 = (bf16[128,4096]{1,0:T(8,128)(2,1)}, bf16[128,4096]{1,0:T(8,128)(2,1)S(1)}, u32[]{:S(2)}, u32[]{:S(2)}) collective-permute-start(bf16[128,4096]{1,0:T(8,128)(2,1)} %get-tuple-element.58.cur_ref), channel_id=1, source_target_pairs={{0,1},{1,2},{2,3},{3,4},{4,5},{5,6},{6,7},{7,8},{8,9},{9,10},{10,1... | collective-permute-start | bytes 3145736 | tf_op jit(solution)/shard_map/ppermute | solution.py:27
  26.9 1.4 collective-permute-start.2
  28.3 2.6 %collective-permute-start.3 = (bf16[256,256]{1,0:T(8,128)(2,1)S(1)}, bf16[256,256]{1,0:T(8,128)(2,1)S(1)}, u32[]{:S(2)}, u32[]{:S(2)}) collective-permute-start(bf16[256,256]{1,0:T(8,128)(2,1)S(1)} %slice.56), channel_id=1, source_target_pairs={{0,64},{32,96},{64,0},{96,32},{1,65},{33,97},{65,1},{97,33},{2,66}... | collective-permute-start | bytes 393224 | tf_op jit(solution)/shard_map/ppermute | solution.py:39
  30.9 1.1 collective-permute-start.4
  32.7 3.3 %collective-permute-done.3 = bf16[256,256]{1,0:T(8,128)(2,1)S(1)} collective-permute-done((bf16[256,256]{1,0:T(8,128)(2,1)S(1)}, bf16[256,256]{1,0:T(8,128)(2,1)S(1)}, u32[]{:S(2)}, u32[]{:S(2)}) %collective-permute-start.3) | collective-permute-done | bytes 131104 | tf_op jit(solution)/shard_map/ppermute | solution.py:39
  36.0 2.9 %collective-permute-done.1.prev_ref = bf16[128,4096]{1,0:T(8,128)(2,1)S(1)} collective-permute-done((bf16[128,4096]{1,0:T(8,128)(2,1)}, bf16[128,4096]{1,0:T(8,128)(2,1)S(1)}, u32[]{:S(2)}, u32[]{:S(2)}) %collective-permute-start.1) | collective-permute-done | bytes 1048608 | tf_op jit(solution)/shard_map/ppermute | solution.py:27
  38.9 9.7 %mix.1 = (bf16[128,4096]{1,0:T(8,128)(2,1)}, bf16[128,4096]{1,0:T(8,128)(2,1)}) custom-call(f32[256,128]{1,0:T(8,128)S(1)} %convert_element_type.63.lines_ref, bf16[128,4096]{1,0:T(8,128)(2,1)S(1)} %collective-permute-done.1.prev_ref, bf16[128,4096]{1,0:T(8,128)(2,1)} %get-tuple-element.58.cur_ref, bf16[128,4096]{1,0:T(8,128)(2,1)} %get-tuple-element.61.query_ref), custom_call_target="tpu_custom_call" | custom-call | bytes 1048576 | tf_op jit(solution)/shard_map/mix/pallas_call | solution.py:64
  49.5 2.8 %collective-permute-start.5 = (bf16[1024,256]{0,1:T(8,128)(2,1)S(1)}, bf16[1024,256]{0,1:T(8,128)(2,1)S(1)}, u32[]{:S(2)}, u32[]{:S(2)}) collective-permute-start(bf16[1024,256]{0,1:T(8,128)(2,1)S(1)} %get-tuple-element.117), channel_id=1, source_target_pairs={{0,8},{8,0},{1,9},{9,1},{2,10},{10,2},{3,11},{11,3},{4,12},{12,4},... | collective-permute-start | bytes 1572872 | tf_op jit(solution)/shard_map/ppermute | solution.py:39
  52.7 2.6 collective-permute-start.8
  55.3 1.4 collective-permute-start.6
  56.6 23.8 %collective-permute-done.8 = bf16[256,256]{1,0:T(8,128)(2,1)S(1)} collective-permute-done((bf16[256,256]{1,0:T(8,128)(2,1)S(1)}, bf16[256,256]{1,0:T(8,128)(2,1)S(1)}, u32[]{:S(2)}, u32[]{:S(2)}) %collective-permute-start.8) | collective-permute-done | bytes 131104 | tf_op jit(solution)/shard_map/ppermute | solution.py:39
  80.5 1.2 collective-permute-start.13
  81.7 1.8 collective-permute-start.14
  83.6 1.4 collective-permute-start.9
  84.9 2.6 %collective-permute-start.10 = (bf16[4,256,256]{2,1,0:T(8,128)(2,1)S(1)}, bf16[4,256,256]{2,1,0:T(8,128)(2,1)}, u32[]{:S(2)}, u32[]{:S(2)}) collective-permute-start(bf16[4,256,256]{2,1,0:T(8,128)(2,1)S(1)} %pad_maximum_fusion.1.refs_1_.refs_0_), channel_id=1, source_target_pairs={{0,64},{32,96},{64,0},{96,32},{1,65},{33,97},{65,1},{97,33},{2,66}... | collective-permute-start | bytes 1572872 | tf_op jit(solution)/shard_map/ppermute | solution.py:39
  88.4 1.1 collective-permute-start.11
  89.4 1.2 fusion.15
  90.6 1.5 copy.12.refs_0_
  92.1 1.6 collective-permute-done.13.refs_7_.refs_6_
  93.7 2.1 collective-permute-done.14.refs_8_.refs_7_
  95.8 1.8 collective-permute-done.9.refs_2_.refs_1_
  97.6 12.3 %collective-permute-done.10.refs_3_.refs_2_ = bf16[4,256,256]{2,1,0:T(8,128)(2,1)} collective-permute-done((bf16[4,256,256]{2,1,0:T(8,128)(2,1)S(1)}, bf16[4,256,256]{2,1,0:T(8,128)(2,1)}, u32[]{:S(2)}, u32[]{:S(2)}) %collective-permute-start.10) | collective-permute-done | bytes 524320 | tf_op jit(solution)/shard_map/ppermute | solution.py:39
  109.9 1.0 copy-done.3
  111.0 8.5 %gate_matmul.1 = bf16[1024,4096]{1,0:T(8,128)(2,1)} custom-call(bf16[1024,512]{1,0:T(8,128)(2,1)S(1)} %copy.12.refs_0_, bf16[4,256,256]{2,1,0:T(8,128)(2,1)S(1)} %pad_maximum_fusion.1.refs_1_.refs_0_, bf16[4,256,256]{2,1,0:T(8,128)(2,1)} %collective-permute-done.9.refs_2_.refs_1_, bf16[4,256,256]{2,1,0:T(8,128)(2,1)} %collective-permute-done.10.refs_3_.refs_2_, ...), custom_call_target="tpu_custom_call" | custom-call | flops 4294967296 | bytes 12582912 | tf_op jit(solution)/shard_map/gate_matmul/pallas_call | solution.py:64
  119.5 9.9 %weight_grad.1 = (bf16[4,256,256]{2,1,0:T(8,128)(2,1)}, bf16[4,256,256]{2,1,0:T(8,128)(2,1)}, bf16[4,256,256]{2,1,0:T(8,128)(2,1)}, bf16[4,256,256]{2,1,0:T(8,12...) custom-call(s32[8]{0:T(128)S(1)} %fusion.6.origin.place, ...), custom_call_target="tpu_custom_call" | custom-call | flops 4294967296 | bytes 12582912 | tf_op jit(solution)/shard_map/weight_grad/pallas_call | solution.py:64
  130.2 3.0 %collective-permute-start.21 = (bf16[4,256,256]{2,1,0:T(8,128)(2,1)}, bf16[4,256,256]{2,1,0:T(8,128)(2,1)}, u32[]{:S(2)}, u32[]{:S(2)}) collective-permute-start(bf16[4,256,256]{2,1,0:T(8,128)(2,1)} %get-tuple-element.81), channel_id=1, source_target_pairs={{0,8},{8,0},{1,9},{9,1},{2,10},{10,2},{3,11},{11,3},{4,12},{12,4},... | collective-permute-start | bytes 1572872 | tf_op jit(solution)/shard_map/ppermute | solution.py:39
  133.3 3.0 %collective-permute-start.17 = (bf16[4,256,256]{2,1,0:T(8,128)(2,1)}, bf16[4,256,256]{2,1,0:T(8,128)(2,1)S(1)}, u32[]{:S(2)}, u32[]{:S(2)}) collective-permute-start(bf16[4,256,256]{2,1,0:T(8,128)(2,1)} %get-tuple-element.79), channel_id=1, source_target_pairs={{0,32},{32,64},{64,96},{96,0},{1,33},{33,65},{65,97},{97,1},{2,34}... | collective-permute-start | bytes 1572872 | tf_op jit(solution)/shard_map/ppermute | solution.py:39
  136.3 1.4 collective-permute-start.16
  137.7 9.9 %output.1 = (bf16[1024,256]{1,0:T(8,128)(2,1)}, bf16[1024,256]{1,0:T(8,128)(2,1)}) custom-call(s32[8]{0:T(128)S(1)} %fusion.6.origin.place, bf16[1024,4096]{1,0:T(8,128)(2,1)} %all-gather.2.cloned.1.call-done.rows_ref, bf16[4,256,256]{2,1,0:T(8,128)(2,1)S(1)} %pad_maximum_fusion.1.refs_1_.refs_0_, ...), custom_call_target="tpu_custom_call" | custom-call | flops 4294967296 | bytes 12582912 | tf_op jit(solution)/shard_map/output/pallas_call | solution.py:64
  147.6 1.1 collective-permute-start.15
  148.8 5.8 %collective-permute-done.21 = bf16[4,256,256]{2,1,0:T(8,128)(2,1)} collective-permute-done((bf16[4,256,256]{2,1,0:T(8,128)(2,1)}, bf16[4,256,256]{2,1,0:T(8,128)(2,1)}, u32[]{:S(2)}, u32[]{:S(2)}) %collective-permute-start.21) | collective-permute-done | bytes 524320 | tf_op jit(solution)/shard_map/ppermute | solution.py:39
  154.6 1.5 add_convert_fusion
  156.1 4.4 %collective-permute-start.26 = (bf16[256,256]{1,0:T(8,128)(2,1)S(1)}, bf16[256,256]{1,0:T(8,128)(2,1)S(1)}, u32[]{:S(2)}, u32[]{:S(2)}) collective-permute-start(bf16[256,256]{1,0:T(8,128)(2,1)S(1)} %get-tuple-element.122), channel_id=1, source_target_pairs={{0,32},{32,64},{64,96},{96,0},{1,33},{33,65},{65,97},{97,1},{2,34}... | collective-permute-start | bytes 393224 | tf_op jit(solution)/shard_map/ppermute | solution.py:39
  160.6 1.5 collective-permute-start.25
  163.4 1.0 collective-permute-start.20
  164.4 1.3 collective-permute-done.27
  165.7 1.3 maximum_select_fusion
  167.0 2.1 collective-permute-start.18
  169.9 2.4 collective-permute-done.18
  172.5 1.2 reduce-scatter.2.cloned.1.call-done.gate_grad_ref
  173.8 3.6 %gate_back.1 = (bf16[128,4096]{1,0:T(8,128)(2,1)}, bf16[128,4096]{1,0:T(8,128)(2,1)}) custom-call(s32[8]{0:T(128)S(1)} %fusion.6.origin.place, bf16[128,4096]{1,0:T(8,128)(2,1)} %reduce-scatter.2.cloned.1.call-done.gate_grad_ref, bf16[128,4096]{1,0:T(8,128)(2,1)} %get-tuple-element.61.query_ref, bf16[128,4096]{1,0:T(8,128)(2,1)} %get-tuple-element.88.mixed_ref), custom_call_target="tpu_custom_call" | custom-call | flops 1048576 | bytes 5242880 | tf_op jit(solution)/shard_map/gate_back/pallas_call | solution.py:64
  177.3 5.0 %collective-permute-start.28 = (bf16[128,4096]{1,0:T(8,128)(2,1)}, bf16[128,4096]{1,0:T(8,128)(2,1)S(1)}, u32[]{:S(2)}, u32[]{:S(2)}) collective-permute-start(bf16[128,4096]{1,0:T(8,128)(2,1)} %get-tuple-element.89.grad_ref), channel_id=1, source_target_pairs={{1,0},{2,1},{3,2},{4,3},{5,4},{6,5},{7,6},{8,7},{9,8},{10,9},{11,1... | collective-permute-start | bytes 3145736 | tf_op jit(solution)/shard_map/ppermute | solution.py:27
  182.3 9.1 %long_grad.1 = (f32[256,128]{1,0:T(8,128)S(1)}, f32[8,4096]{1,0:T(8,128)S(1)}) custom-call(bf16[128,4096]{1,0:T(8,128)(2,1)} %copy-done.1, bf16[128,4096]{1,0:T(8,128)(2,1)} %get-tuple-element.58.cur_ref, bf16[128,4096]{1,0:T(8,128)(2,1)} %get-tuple-element.89.grad_ref, bf16[128,4096]{1,0:T(8,128)(2,1)} %get-tuple-element.92.query_grad_ref.feature_ref, ...), custom_call_target="tpu_custom_call" | custom-call | flops 2147483648 | bytes 5242880 | tf_op jit(solution)/shard_map/long_grad/pallas_call | solution.py:64
  191.5 4.8 %collective-permute-done.28.next_ref = bf16[128,4096]{1,0:T(8,128)(2,1)S(1)} collective-permute-done((bf16[128,4096]{1,0:T(8,128)(2,1)}, bf16[128,4096]{1,0:T(8,128)(2,1)S(1)}, u32[]{:S(2)}, u32[]{:S(2)}) %collective-permute-start.28) | collective-permute-done | bytes 1048608 | tf_op jit(solution)/shard_map/ppermute | solution.py:27
  196.3 11.3 %unmix.1 = (bf16[2,128,4096]{2,1,0:T(8,128)(2,1)}, f32[8,4096]{1,0:T(8,128)S(1)}, f32[8,4096]{1,0:T(8,128)S(1)}, bf16[3,8,4096]{2,1,0:T(8,128)(2,1)S(1)}) custom-call(f32[256,128]{1,0:T(8,128)S(1)} %convert_element_type.63.lines_ref, bf16[128,4096]{1,0:T(8,128)(2,1)} %get-tuple-element.89.grad_ref, bf16[128,4096]{1,0:T(8,128)(2,1)S(1)} %collective-permute-done.28.next_ref, ...), custom_call_target="tpu_custom_call" | custom-call | flops 2147483648 | bytes 8388608 | tf_op jit(solution)/shard_map/unmix/pallas_call | solution.py:64
  208.6 1.5 collective-permute-done.30
  210.2 6.0 %collective-permute-start.33 = (f32[16,8,128]{2,1,0:T(8,128)S(1)}, f32[16,8,128]{2,1,0:T(8,128)S(1)}, u32[]{:S(2)}, u32[]{:S(2)}) collective-permute-start(f32[16,8,128]{2,1,0:T(8,128)S(1)} %get-tuple-element.125), channel_id=1, source_target_pairs={{0,6},{2,0},{4,2},{6,4},{1,7},{3,1},{5,3},{7,5},{8,14},{10,8},{12,... | collective-permute-start | bytes 196616 | tf_op jit(solution)/shard_map/ppermute | solution.py:39
  216.9 2.6 %collective-permute-start.29 = (bf16[3,8,4096]{2,1,0:T(8,128)(2,1)S(1)}, bf16[3,8,4096]{2,1,0:T(8,128)(2,1)S(1)}, u32[]{:S(2)}, u32[]{:S(2)}) collective-permute-start(bf16[3,8,4096]{2,1,0:T(8,128)(2,1)S(1)} %get-tuple-element.94), channel_id=1, source_target_pairs={{1,0},{2,1},{3,2},{4,3},{5,4},{6,5},{7,6},{8,7},{9,8},{10,9},{11,1... | collective-permute-start | bytes 589832 | tf_op jit(solution)/shard_map/ppermute | solution.py:27
  219.5 1.4 collective-permute-done.32
  220.9 1.6 collective-permute-done.31
  222.6 3.2 %collective-permute-start.34 = (f32[16,8,128]{2,1,0:T(8,128)S(1)}, f32[16,8,128]{2,1,0:T(8,128)S(1)}, u32[]{:S(2)}, u32[]{:S(2)}) collective-permute-start(f32[16,8,128]{2,1,0:T(8,128)S(1)} %fusion.5), channel_id=1, source_target_pairs={{0,32},{32,64},{64,96},{96,0},{1,33},{33,65},{65,97},{97,1},{2,34}... | collective-permute-start | bytes 196616 | tf_op jit(solution)/shard_map/ppermute | solution.py:39
  225.8 1.2 collective-permute-start.35
  227.0 1.3 collective-permute-start.36
  228.3 3.2 %short_adjoint.2.refs_0_ = bf16[128,12288]{1,0:T(8,128)(2,1)} custom-call(bf16[1,128,4096]{2,1,0:T(8,128)(2,1)} %bitcast.49, bf16[3,8,4096]{2,1,0:T(8,128)(2,1)S(1)} %collective-permute-done.29.rim_ref, f32[7,12288]{1,0:T(8,128)} %filter_ref.3), custom_call_target="tpu_custom_call" | custom-call | flops 7340032 | bytes 2097152 | tf_op jit(solution)/shard_map/short_adjoint/pallas_call | solution.py:64
  232.1 2.6 collective-permute-start.39
  234.7 1.6 collective-permute-done.38
  236.9 1.2 collective-permute-done.37
  238.1 2.8 %collective-permute-start.40 = (f32[16,8,128]{2,1,0:T(8,128)S(1)}, f32[16,8,128]{2,1,0:T(8,128)S(1)}, u32[]{:S(2)}, u32[]{:S(2)}) collective-permute-start(f32[16,8,128]{2,1,0:T(8,128)S(1)} %add_add_fusion), channel_id=1, source_target_pairs={{0,1},{1,0},{2,3},{3,2},{4,5},{5,4},{6,7},{7,6},{8,9},{9,8},{10,11... | collective-permute-start | bytes 196616 | tf_op jit(solution)/shard_map/ppermute | solution.py:39
  244.6 5.1 %short_adjoint.3 = bf16[128,12288]{1,0:T(8,128)(2,1)} custom-call(bf16[2,128,4096]{2,1,0:T(8,128)(2,1)} %get-tuple-element.93.grads_ref, bf16[3,8,4096]{2,1,0:T(8,128)(2,1)S(1)} %collective-permute-done.29.rim_ref, f32[7,12288]{1,0:T(8,128)} %filter_ref.3, bf16[128,12288]{1,0:T(8,128)(2,1)} %short_adjoint.2.refs_0_), custom_call_target="tpu_custom_call", output_to_operand_aliasing={{}: (3, {})} | custom-call | flops 14680064 | bytes 4194304 | tf_op jit(solution)/shard_map/short_adjoint/pallas_call | solution.py:64
  249.7 2.5 collective-permute-done.43.refs_3_
  252.2 1.5 collect.1
  (94 shorter events, 13.8 us)
Async XLA Ops:
  7.2 112.3 %all-gather.2.cloned.1.call-start = ((), (), s32[]{:S(2)}) async-start(), calls=%async_computation.1 | async-start | bytes 9437184 | tf_op jit(solution)/shard_map/all_gather | solution.py:706
  8.2 7.5 %collective-permute-start = (bf16[8,12288]{1,0:T(8,128)(2,1)S(1)}, bf16[8,12288]{1,0:T(8,128)(2,1)S(1)}, u32[]{:S(2)}, u32[]{:S(2)}) collective-permute-start(bf16[8,12288]{1,0:T(8,128)(2,1)S(1)} %slice_bitcast_fusion), channel_id=1, source_target_pairs={{0,1},{1,2},{2,3},{3,4},{4,5},{5,6},{6,7},{7,8},{8,9},{9,10},{10,1... | collective-permute-start | bytes 589832 | tf_op jit(solution)/shard_map/ppermute | solution.py:27
  15.7 6.8 %copy-start = (bf16[8,12288]{1,0:T(8,128)(2,1)}, bf16[8,12288]{1,0:T(8,128)(2,1)S(1)}, u32[]{:S(2)}) copy-start(bf16[8,12288]{1,0:T(8,128)(2,1)S(1)} %collective-permute-done.refs_3_.refs_4_.refs_5_.key_rim_ref.value_rim_ref.rim_ref) | copy-start | bytes 589828
  15.7 11.2 %copy-start.9 = (bf16[512,256]{1,0:T(8,128)(2,1)S(1)}, bf16[512,256]{1,0:T(8,128)(2,1)}, u32[]{:S(2)}) copy-start(bf16[512,256]{1,0:T(8,128)(2,1)} %param.8) | copy-start | bytes 786436
  15.7 16.3 %copy-start.10 = (bf16[256,128]{1,0:T(8,128)(2,1)S(1)}, bf16[256,128]{1,0:T(8,128)(2,1)}, u32[]{:S(2)}) copy-start(bf16[256,128]{1,0:T(8,128)(2,1)} %param.7) | copy-start | bytes 196612
  22.5 16.4 %collective-permute-start.1 = (bf16[128,4096]{1,0:T(8,128)(2,1)}, bf16[128,4096]{1,0:T(8,128)(2,1)S(1)}, u32[]{:S(2)}, u32[]{:S(2)}) collective-permute-start(bf16[128,4096]{1,0:T(8,128)(2,1)} %get-tuple-element.58.cur_ref), channel_id=1, source_target_pairs={{0,1},{1,2},{2,3},{3,4},{4,5},{5,6},{6,7},{7,8},{8,9},{9,10},{10,1... | collective-permute-start | bytes 3145736 | tf_op jit(solution)/shard_map/ppermute | solution.py:27
  26.9 5.8 %collective-permute-start.2 = (bf16[256,256]{1,0:T(8,128)(2,1)S(1)}, bf16[256,256]{1,0:T(8,128)(2,1)S(1)}, u32[]{:S(2)}, u32[]{:S(2)}) collective-permute-start(bf16[256,256]{1,0:T(8,128)(2,1)S(1)} %slice.56), channel_id=1, source_target_pairs={{0,32},{32,64},{64,96},{96,0},{1,33},{33,65},{65,97},{97,1},{2,34}... | collective-permute-start | bytes 393224 | tf_op jit(solution)/shard_map/ppermute | solution.py:39
  28.3 7.7 %collective-permute-start.3 = (bf16[256,256]{1,0:T(8,128)(2,1)S(1)}, bf16[256,256]{1,0:T(8,128)(2,1)S(1)}, u32[]{:S(2)}, u32[]{:S(2)}) collective-permute-start(bf16[256,256]{1,0:T(8,128)(2,1)S(1)} %slice.56), channel_id=1, source_target_pairs={{0,64},{32,96},{64,0},{96,32},{1,65},{33,97},{65,1},{97,33},{2,66}... | collective-permute-start | bytes 393224 | tf_op jit(solution)/shard_map/ppermute | solution.py:39
  30.9 5.1 %collective-permute-start.4 = (bf16[256,256]{1,0:T(8,128)(2,1)S(1)}, bf16[256,256]{1,0:T(8,128)(2,1)S(1)}, u32[]{:S(2)}, u32[]{:S(2)}) collective-permute-start(bf16[256,256]{1,0:T(8,128)(2,1)S(1)} %slice.56), channel_id=1, source_target_pairs={{0,96},{32,0},{64,32},{96,64},{1,97},{33,1},{65,33},{97,65},{2,98}... | collective-permute-start | bytes 393224 | tf_op jit(solution)/shard_map/ppermute | solution.py:39
  38.9 9.7 %copy-start.1 = (bf16[128,4096]{1,0:T(8,128)(2,1)}, bf16[128,4096]{1,0:T(8,128)(2,1)S(1)}, u32[]{:S(2)}) copy-start(bf16[128,4096]{1,0:T(8,128)(2,1)S(1)} %collective-permute-done.1.prev_ref) | copy-start | bytes 3145732
  38.9 9.8 %copy-start.5 = (bf16[1,2048,256]{2,1,0:T(8,128)(2,1)S(1)}, bf16[1,2048,256]{2,1,0:T(8,128)(2,1)}, u32[]{:S(2)}) copy-start(bf16[1,2048,256]{2,1,0:T(8,128)(2,1)} %param.9) | copy-start | bytes 3145732
  48.7 125.1 %reduce-scatter.2.cloned.1.call-start = ((), (), s32[]{:S(2)}) async-start(), calls=%async_computation.2 | async-start | bytes 9437184 | tf_op jit(solution)/shard_map/reduce_scatter | solution.py:713
  49.5 35.5 %collective-permute-start.5 = (bf16[1024,256]{0,1:T(8,128)(2,1)S(1)}, bf16[1024,256]{0,1:T(8,128)(2,1)S(1)}, u32[]{:S(2)}, u32[]{:S(2)}) collective-permute-start(bf16[1024,256]{0,1:T(8,128)(2,1)S(1)} %get-tuple-element.117), channel_id=1, source_target_pairs={{0,8},{8,0},{1,9},{9,1},{2,10},{10,2},{3,11},{11,3},{4,12},{12,4},... | collective-permute-start | bytes 1572872 | tf_op jit(solution)/shard_map/ppermute | solution.py:39
  52.4 35.2 %collective-permute-start.12 = (bf16[4,256,256]{2,1,0:T(8,128)(2,1)S(1)}, bf16[4,256,256]{2,1,0:T(8,128)(2,1)S(1)}, u32[]{:S(2)}, u32[]{:S(2)}) collective-permute-start(bf16[4,256,256]{2,1,0:T(8,128)(2,1)S(1)} %pad_maximum_fusion.2.refs_5_.refs_4_), channel_id=1, source_target_pairs={{0,8},{8,0},{1,9},{9,1},{2,10},{10,2},{3,11},{11,3},{4,12},{12,4},... | collective-permute-start | bytes 1572872 | tf_op jit(solution)/shard_map/ppermute | solution.py:39
  52.7 27.8 %collective-permute-start.8 = (bf16[256,256]{1,0:T(8,128)(2,1)S(1)}, bf16[256,256]{1,0:T(8,128)(2,1)S(1)}, u32[]{:S(2)}, u32[]{:S(2)}) collective-permute-start(bf16[256,256]{1,0:T(8,128)(2,1)S(1)} %get-tuple-element.128), channel_id=1, source_target_pairs={{0,24},{8,16},{16,8},{24,0},{1,25},{9,17},{17,9},{25,1},{2,26},{10... | collective-permute-start | bytes 393224 | tf_op jit(solution)/shard_map/ppermute | solution.py:39
  55.3 26.4 %collective-permute-start.7 = (bf16[256,256]{1,0:T(8,128)(2,1)S(1)}, bf16[256,256]{1,0:T(8,128)(2,1)S(1)}, u32[]{:S(2)}, u32[]{:S(2)}) collective-permute-start(bf16[256,256]{1,0:T(8,128)(2,1)S(1)} %get-tuple-element.128), channel_id=1, source_target_pairs={{0,16},{16,0},{1,17},{17,1},{2,18},{18,2},{3,19},{19,3},{4,20},{20... | collective-permute-start | bytes 393224 | tf_op jit(solution)/shard_map/ppermute | solution.py:39
  55.3 28.2 %collective-permute-start.6 = (bf16[256,256]{1,0:T(8,128)(2,1)S(1)}, bf16[256,256]{1,0:T(8,128)(2,1)S(1)}, u32[]{:S(2)}, u32[]{:S(2)}) collective-permute-start(bf16[256,256]{1,0:T(8,128)(2,1)S(1)} %get-tuple-element.128), channel_id=1, source_target_pairs={{0,8},{8,0},{1,9},{9,1},{2,10},{10,2},{3,11},{11,3},{4,12},{12,4},... | collective-permute-start | bytes 393224 | tf_op jit(solution)/shard_map/ppermute | solution.py:39
  80.5 13.2 %collective-permute-start.13 = (bf16[4,256,256]{2,1,0:T(8,128)(2,1)S(1)}, bf16[4,256,256]{2,1,0:T(8,128)(2,1)}, u32[]{:S(2)}, u32[]{:S(2)}) collective-permute-start(bf16[4,256,256]{2,1,0:T(8,128)(2,1)S(1)} %pad_maximum_fusion.2.refs_5_.refs_4_), channel_id=1, source_target_pairs={{0,16},{16,0},{1,17},{17,1},{2,18},{18,2},{3,19},{19,3},{4,20},{20... | collective-permute-start | bytes 1572872 | tf_op jit(solution)/shard_map/ppermute | solution.py:39
  81.7 14.1 %collective-permute-start.14 = (bf16[4,256,256]{2,1,0:T(8,128)(2,1)S(1)}, bf16[4,256,256]{2,1,0:T(8,128)(2,1)}, u32[]{:S(2)}, u32[]{:S(2)}) collective-permute-start(bf16[4,256,256]{2,1,0:T(8,128)(2,1)S(1)} %pad_maximum_fusion.2.refs_5_.refs_4_), channel_id=1, source_target_pairs={{0,24},{8,16},{16,8},{24,0},{1,25},{9,17},{17,9},{25,1},{2,26},{10... | collective-permute-start | bytes 1572872 | tf_op jit(solution)/shard_map/ppermute | solution.py:39
  83.6 14.0 %collective-permute-start.9 = (bf16[4,256,256]{2,1,0:T(8,128)(2,1)S(1)}, bf16[4,256,256]{2,1,0:T(8,128)(2,1)}, u32[]{:S(2)}, u32[]{:S(2)}) collective-permute-start(bf16[4,256,256]{2,1,0:T(8,128)(2,1)S(1)} %pad_maximum_fusion.1.refs_1_.refs_0_), channel_id=1, source_target_pairs={{0,32},{32,64},{64,96},{96,0},{1,33},{33,65},{65,97},{97,1},{2,34}... | collective-permute-start | bytes 1572872 | tf_op jit(solution)/shard_map/ppermute | solution.py:39
  84.9 25.0 %collective-permute-start.10 = (bf16[4,256,256]{2,1,0:T(8,128)(2,1)S(1)}, bf16[4,256,256]{2,1,0:T(8,128)(2,1)}, u32[]{:S(2)}, u32[]{:S(2)}) collective-permute-start(bf16[4,256,256]{2,1,0:T(8,128)(2,1)S(1)} %pad_maximum_fusion.1.refs_1_.refs_0_), channel_id=1, source_target_pairs={{0,64},{32,96},{64,0},{96,32},{1,65},{33,97},{65,1},{97,33},{2,66}... | collective-permute-start | bytes 1572872 | tf_op jit(solution)/shard_map/ppermute | solution.py:39
  87.6 0.8 copy-start.2
  88.4 21.6 %collective-permute-start.11 = (bf16[4,256,256]{2,1,0:T(8,128)(2,1)S(1)}, bf16[4,256,256]{2,1,0:T(8,128)(2,1)}, u32[]{:S(2)}, u32[]{:S(2)}) collective-permute-start(bf16[4,256,256]{2,1,0:T(8,128)(2,1)S(1)} %pad_maximum_fusion.1.refs_1_.refs_0_), channel_id=1, source_target_pairs={{0,96},{32,0},{64,32},{96,64},{1,97},{33,1},{65,33},{97,65},{2,98}... | collective-permute-start | bytes 1572872 | tf_op jit(solution)/shard_map/ppermute | solution.py:39
  109.9 1.0 copy-start.3
  119.5 18.2 %copy-start.4 = (bf16[4,256,256]{2,1,0:T(8,128)(2,1)S(1)}, bf16[4,256,256]{2,1,0:T(8,128)(2,1)}, u32[]{:S(2)}) copy-start(bf16[4,256,256]{2,1,0:T(8,128)(2,1)} %copy-done.2) | copy-start | bytes 1572868
  129.4 18.2 %collective-permute-start.23 = (bf16[4,256,256]{2,1,0:T(8,128)(2,1)}, bf16[4,256,256]{2,1,0:T(8,128)(2,1)S(1)}, u32[]{:S(2)}, u32[]{:S(2)}) collective-permute-start(bf16[4,256,256]{2,1,0:T(8,128)(2,1)} %get-tuple-element.83), channel_id=1, source_target_pairs={{0,24},{8,16},{16,8},{24,0},{1,25},{9,17},{17,9},{25,1},{2,26},{10... | collective-permute-start | bytes 1572872 | tf_op jit(solution)/shard_map/ppermute | solution.py:39
  130.2 18.6 %collective-permute-start.22 = (bf16[4,256,256]{2,1,0:T(8,128)(2,1)}, bf16[4,256,256]{2,1,0:T(8,128)(2,1)}, u32[]{:S(2)}, u32[]{:S(2)}) collective-permute-start(bf16[4,256,256]{2,1,0:T(8,128)(2,1)} %get-tuple-element.82), channel_id=1, source_target_pairs={{0,16},{16,0},{1,17},{17,1},{2,18},{18,2},{3,19},{19,3},{4,20},{20... | collective-permute-start | bytes 1572872 | tf_op jit(solution)/shard_map/ppermute | solution.py:39
  130.2 24.3 %collective-permute-start.21 = (bf16[4,256,256]{2,1,0:T(8,128)(2,1)}, bf16[4,256,256]{2,1,0:T(8,128)(2,1)}, u32[]{:S(2)}, u32[]{:S(2)}) collective-permute-start(bf16[4,256,256]{2,1,0:T(8,128)(2,1)} %get-tuple-element.81), channel_id=1, source_target_pairs={{0,8},{8,0},{1,9},{9,1},{2,10},{10,2},{3,11},{11,3},{4,12},{12,4},... | collective-permute-start | bytes 1572872 | tf_op jit(solution)/shard_map/ppermute | solution.py:39
  133.3 27.3 %collective-permute-start.17 = (bf16[4,256,256]{2,1,0:T(8,128)(2,1)}, bf16[4,256,256]{2,1,0:T(8,128)(2,1)S(1)}, u32[]{:S(2)}, u32[]{:S(2)}) collective-permute-start(bf16[4,256,256]{2,1,0:T(8,128)(2,1)} %get-tuple-element.79), channel_id=1, source_target_pairs={{0,32},{32,64},{64,96},{96,0},{1,33},{33,65},{65,97},{97,1},{2,34}... | collective-permute-start | bytes 1572872 | tf_op jit(solution)/shard_map/ppermute | solution.py:39
  136.3 11.4 %copy-start.11 = (bf16[4,256,256]{2,1,0:T(8,128)(2,1)S(1)}, bf16[4,256,256]{2,1,0:T(8,128)(2,1)}, u32[]{:S(2)}) copy-start(bf16[4,256,256]{2,1,0:T(8,128)(2,1)} %get-tuple-element.77) | copy-start | bytes 1572868
  136.3 18.3 %copy-start.8 = (bf16[4,256,256]{2,1,0:T(8,128)(2,1)S(1)}, bf16[4,256,256]{2,1,0:T(8,128)(2,1)}, u32[]{:S(2)}) copy-start(bf16[4,256,256]{2,1,0:T(8,128)(2,1)} %get-tuple-element.80) | copy-start | bytes 1572868
  136.3 25.8 %collective-permute-start.16 = (bf16[4,256,256]{2,1,0:T(8,128)(2,1)}, bf16[4,256,256]{2,1,0:T(8,128)(2,1)S(1)}, u32[]{:S(2)}, u32[]{:S(2)}) collective-permute-start(bf16[4,256,256]{2,1,0:T(8,128)(2,1)} %get-tuple-element.78), channel_id=1, source_target_pairs={{0,64},{32,96},{64,0},{96,32},{1,65},{33,97},{65,1},{97,33},{2,66}... | collective-permute-start | bytes 1572872 | tf_op jit(solution)/shard_map/ppermute | solution.py:39
  147.6 15.4 %copy-start.6 = (bf16[4,256,256]{2,1,0:T(8,128)(2,1)S(1)}, bf16[4,256,256]{2,1,0:T(8,128)(2,1)}, u32[]{:S(2)}) copy-start(bf16[4,256,256]{2,1,0:T(8,128)(2,1)} %get-tuple-element.76) | copy-start | bytes 1572868
  147.6 15.4 %collective-permute-start.15 = (bf16[4,256,256]{2,1,0:T(8,128)(2,1)S(1)}, bf16[4,256,256]{2,1,0:T(8,128)(2,1)S(1)}, u32[]{:S(2)}, u32[]{:S(2)}) collective-permute-start(bf16[4,256,256]{2,1,0:T(8,128)(2,1)S(1)} %copy-done.11), channel_id=1, source_target_pairs={{0,96},{32,0},{64,32},{96,64},{1,97},{33,1},{65,33},{97,65},{2,98}... | collective-permute-start | bytes 1572872 | tf_op jit(solution)/shard_map/ppermute | solution.py:39
  148.8 16.9 %collective-permute-start.27 = (bf16[1024,256]{1,0:T(8,128)(2,1)}, bf16[1024,256]{1,0:T(8,128)(2,1)S(1)}, u32[]{:S(2)}, u32[]{:S(2)}) collective-permute-start(bf16[1024,256]{1,0:T(8,128)(2,1)} %get-tuple-element.85), channel_id=1, source_target_pairs={{0,8},{8,0},{1,9},{9,1},{2,10},{10,2},{3,11},{11,3},{4,12},{12,4},... | collective-permute-start | bytes 1572872 | tf_op jit(solution)/shard_map/ppermute | solution.py:39
  156.1 9.6 %copy-start.7 = (bf16[1024,256]{1,0:T(8,128)(2,1)S(1)}, bf16[1024,256]{1,0:T(8,128)(2,1)}, u32[]{:S(2)}) copy-start(bf16[1024,256]{1,0:T(8,128)(2,1)} %get-tuple-element.84) | copy-start | bytes 1572868
  156.1 10.9 %collective-permute-start.26 = (bf16[256,256]{1,0:T(8,128)(2,1)S(1)}, bf16[256,256]{1,0:T(8,128)(2,1)S(1)}, u32[]{:S(2)}, u32[]{:S(2)}) collective-permute-start(bf16[256,256]{1,0:T(8,128)(2,1)S(1)} %get-tuple-element.122), channel_id=1, source_target_pairs={{0,32},{32,64},{64,96},{96,0},{1,33},{33,65},{65,97},{97,1},{2,34}... | collective-permute-start | bytes 393224 | tf_op jit(solution)/shard_map/ppermute | solution.py:39
  160.6 8.5 %collective-permute-start.25 = (bf16[256,256]{1,0:T(8,128)(2,1)S(1)}, bf16[256,256]{1,0:T(8,128)(2,1)S(1)}, u32[]{:S(2)}, u32[]{:S(2)}) collective-permute-start(bf16[256,256]{1,0:T(8,128)(2,1)S(1)} %get-tuple-element.123), channel_id=1, source_target_pairs={{0,64},{32,96},{64,0},{96,32},{1,65},{33,97},{65,1},{97,33},{2,66}... | collective-permute-start | bytes 393224 | tf_op jit(solution)/shard_map/ppermute | solution.py:39
  162.1 7.0 %collective-permute-start.24 = (bf16[256,256]{1,0:T(8,128)(2,1)S(1)}, bf16[256,256]{1,0:T(8,128)(2,1)S(1)}, u32[]{:S(2)}, u32[]{:S(2)}) collective-permute-start(bf16[256,256]{1,0:T(8,128)(2,1)S(1)} %get-tuple-element.121), channel_id=1, source_target_pairs={{0,96},{32,0},{64,32},{96,64},{1,97},{33,1},{65,33},{97,65},{2,98}... | collective-permute-start | bytes 393224 | tf_op jit(solution)/shard_map/ppermute | solution.py:39
  163.4 6.5 %collective-permute-start.20 = (bf16[256,256]{1,0:T(8,128)(2,1)S(1)}, bf16[256,256]{1,0:T(8,128)(2,1)S(1)}, u32[]{:S(2)}, u32[]{:S(2)}) collective-permute-start(bf16[256,256]{1,0:T(8,128)(2,1)S(1)} %get-tuple-element.119), channel_id=1, source_target_pairs={{0,24},{8,16},{16,8},{24,0},{1,25},{9,17},{17,9},{25,1},{2,26},{10... | collective-permute-start | bytes 393224 | tf_op jit(solution)/shard_map/ppermute | solution.py:39
  165.7 4.2 %collective-permute-start.19 = (bf16[256,256]{1,0:T(8,128)(2,1)S(1)}, bf16[256,256]{1,0:T(8,128)(2,1)S(1)}, u32[]{:S(2)}, u32[]{:S(2)}) collective-permute-start(bf16[256,256]{1,0:T(8,128)(2,1)S(1)} %get-tuple-element.120), channel_id=1, source_target_pairs={{0,16},{16,0},{1,17},{17,1},{2,18},{18,2},{3,19},{19,3},{4,20},{20... | collective-permute-start | bytes 393224 | tf_op jit(solution)/shard_map/ppermute | solution.py:39
  167.0 5.4 %collective-permute-start.18 = (bf16[256,256]{1,0:T(8,128)(2,1)S(1)}, bf16[256,256]{1,0:T(8,128)(2,1)S(1)}, u32[]{:S(2)}, u32[]{:S(2)}) collective-permute-start(bf16[256,256]{1,0:T(8,128)(2,1)S(1)} %get-tuple-element.118), channel_id=1, source_target_pairs={{0,8},{8,0},{1,9},{9,1},{2,10},{10,2},{3,11},{11,3},{4,12},{12,4},... | collective-permute-start | bytes 393224 | tf_op jit(solution)/shard_map/ppermute | solution.py:39
  177.3 19.0 %collective-permute-start.28 = (bf16[128,4096]{1,0:T(8,128)(2,1)}, bf16[128,4096]{1,0:T(8,128)(2,1)S(1)}, u32[]{:S(2)}, u32[]{:S(2)}) collective-permute-start(bf16[128,4096]{1,0:T(8,128)(2,1)} %get-tuple-element.89.grad_ref), channel_id=1, source_target_pairs={{1,0},{2,1},{3,2},{4,3},{5,4},{6,5},{7,6},{8,7},{9,8},{10,9},{11,1... | collective-permute-start | bytes 3145736 | tf_op jit(solution)/shard_map/ppermute | solution.py:27
  208.6 1.6 collective-permute-start.30
  210.2 9.3 %collective-permute-start.33 = (f32[16,8,128]{2,1,0:T(8,128)S(1)}, f32[16,8,128]{2,1,0:T(8,128)S(1)}, u32[]{:S(2)}, u32[]{:S(2)}) collective-permute-start(f32[16,8,128]{2,1,0:T(8,128)S(1)} %get-tuple-element.125), channel_id=1, source_target_pairs={{0,6},{2,0},{4,2},{6,4},{1,7},{3,1},{5,3},{7,5},{8,14},{10,8},{12,... | collective-permute-start | bytes 196616 | tf_op jit(solution)/shard_map/ppermute | solution.py:39
  216.2 4.7 %collective-permute-start.32 = (f32[16,8,128]{2,1,0:T(8,128)S(1)}, f32[16,8,128]{2,1,0:T(8,128)S(1)}, u32[]{:S(2)}, u32[]{:S(2)}) collective-permute-start(f32[16,8,128]{2,1,0:T(8,128)S(1)} %get-tuple-element.126), channel_id=1, source_target_pairs={{0,4},{2,6},{4,0},{6,2},{1,5},{3,7},{5,1},{7,3},{8,12},{10,14},{12... | collective-permute-start | bytes 196616 | tf_op jit(solution)/shard_map/ppermute | solution.py:39
  216.2 6.4 %collective-permute-start.31 = (f32[16,8,128]{2,1,0:T(8,128)S(1)}, f32[16,8,128]{2,1,0:T(8,128)S(1)}, u32[]{:S(2)}, u32[]{:S(2)}) collective-permute-start(f32[16,8,128]{2,1,0:T(8,128)S(1)} %get-tuple-element.124), channel_id=1, source_target_pairs={{0,2},{2,4},{4,6},{6,0},{1,3},{3,5},{5,7},{7,1},{8,10},{10,12},{12... | collective-permute-start | bytes 196616 | tf_op jit(solution)/shard_map/ppermute | solution.py:39
  216.9 11.4 %collective-permute-start.29 = (bf16[3,8,4096]{2,1,0:T(8,128)(2,1)S(1)}, bf16[3,8,4096]{2,1,0:T(8,128)(2,1)S(1)}, u32[]{:S(2)}, u32[]{:S(2)}) collective-permute-start(bf16[3,8,4096]{2,1,0:T(8,128)(2,1)S(1)} %get-tuple-element.94), channel_id=1, source_target_pairs={{1,0},{2,1},{3,2},{4,3},{5,4},{6,5},{7,6},{8,7},{9,8},{10,9},{11,1... | collective-permute-start | bytes 589832 | tf_op jit(solution)/shard_map/ppermute | solution.py:27
  222.6 8.9 %collective-permute-start.34 = (f32[16,8,128]{2,1,0:T(8,128)S(1)}, f32[16,8,128]{2,1,0:T(8,128)S(1)}, u32[]{:S(2)}, u32[]{:S(2)}) collective-permute-start(f32[16,8,128]{2,1,0:T(8,128)S(1)} %fusion.5), channel_id=1, source_target_pairs={{0,32},{32,64},{64,96},{96,0},{1,33},{33,65},{65,97},{97,1},{2,34}... | collective-permute-start | bytes 196616 | tf_op jit(solution)/shard_map/ppermute | solution.py:39
  225.8 5.7 %collective-permute-start.35 = (f32[16,8,128]{2,1,0:T(8,128)S(1)}, f32[16,8,128]{2,1,0:T(8,128)S(1)}, u32[]{:S(2)}, u32[]{:S(2)}) collective-permute-start(f32[16,8,128]{2,1,0:T(8,128)S(1)} %fusion.5), channel_id=1, source_target_pairs={{0,64},{32,96},{64,0},{96,32},{1,65},{33,97},{65,1},{97,33},{2,66}... | collective-permute-start | bytes 196616 | tf_op jit(solution)/shard_map/ppermute | solution.py:39
  227.0 4.5 %collective-permute-start.36 = (f32[16,8,128]{2,1,0:T(8,128)S(1)}, f32[16,8,128]{2,1,0:T(8,128)S(1)}, u32[]{:S(2)}, u32[]{:S(2)}) collective-permute-start(f32[16,8,128]{2,1,0:T(8,128)S(1)} %fusion.5), channel_id=1, source_target_pairs={{0,96},{32,0},{64,32},{96,64},{1,97},{33,1},{65,33},{97,65},{2,98}... | collective-permute-start | bytes 196616 | tf_op jit(solution)/shard_map/ppermute | solution.py:39
  231.5 4.8 %collective-permute-start.38 = (f32[16,8,128]{2,1,0:T(8,128)S(1)}, f32[16,8,128]{2,1,0:T(8,128)S(1)}, u32[]{:S(2)}, u32[]{:S(2)}) collective-permute-start(f32[16,8,128]{2,1,0:T(8,128)S(1)} %add_add_fusion.1), channel_id=1, source_target_pairs={{0,8},{8,0},{1,9},{9,1},{2,10},{10,2},{3,11},{11,3},{4,12},{12,4},... | collective-permute-start | bytes 196616 | tf_op jit(solution)/shard_map/ppermute | solution.py:39
  232.1 4.8 %collective-permute-start.39 = (f32[16,8,128]{2,1,0:T(8,128)S(1)}, f32[16,8,128]{2,1,0:T(8,128)S(1)}, u32[]{:S(2)}, u32[]{:S(2)}) collective-permute-start(f32[16,8,128]{2,1,0:T(8,128)S(1)} %add_add_fusion.1), channel_id=1, source_target_pairs={{0,24},{8,16},{16,8},{24,0},{1,25},{9,17},{17,9},{25,1},{2,26},{10... | collective-permute-start | bytes 196616 | tf_op jit(solution)/shard_map/ppermute | solution.py:39
  234.6 3.4 %collective-permute-start.37 = (f32[16,8,128]{2,1,0:T(8,128)S(1)}, f32[16,8,128]{2,1,0:T(8,128)S(1)}, u32[]{:S(2)}, u32[]{:S(2)}) collective-permute-start(f32[16,8,128]{2,1,0:T(8,128)S(1)} %add_add_fusion.1), channel_id=1, source_target_pairs={{0,16},{16,0},{1,17},{17,1},{2,18},{18,2},{3,19},{19,3},{4,20},{20... | collective-permute-start | bytes 196616 | tf_op jit(solution)/shard_map/ppermute | solution.py:39
  238.1 3.7 %collective-permute-start.40 = (f32[16,8,128]{2,1,0:T(8,128)S(1)}, f32[16,8,128]{2,1,0:T(8,128)S(1)}, u32[]{:S(2)}, u32[]{:S(2)}) collective-permute-start(f32[16,8,128]{2,1,0:T(8,128)S(1)} %add_add_fusion), channel_id=1, source_target_pairs={{0,1},{1,0},{2,3},{3,2},{4,5},{5,4},{6,7},{7,6},{8,9},{9,8},{10,11... | collective-permute-start | bytes 196616 | tf_op jit(solution)/shard_map/ppermute | solution.py:39
  241.8 7.9 %collective-permute-start.41 = (f32[32,8,128]{2,1,0:T(8,128)S(1)}, f32[32,8,128]{2,1,0:T(8,128)S(1)}, u32[]{:S(2)}, u32[]{:S(2)}) collective-permute-start(f32[32,8,128]{2,1,0:T(8,128)S(1)} %pad_maximum_fusion.3.refs_0_), channel_id=1, source_target_pairs={{0,6},{2,0},{4,2},{6,4},{1,7},{3,1},{5,3},{7,5},{8,14},{10,8},{12,... | collective-permute-start | bytes 393224 | tf_op jit(solution)/shard_map/ppermute | solution.py:39
  242.5 7.3 %collective-permute-start.42 = (f32[32,8,128]{2,1,0:T(8,128)S(1)}, f32[32,8,128]{2,1,0:T(8,128)S(1)}, u32[]{:S(2)}, u32[]{:S(2)}) collective-permute-start(f32[32,8,128]{2,1,0:T(8,128)S(1)} %pad_maximum_fusion.3.refs_0_), channel_id=1, source_target_pairs={{0,4},{2,6},{4,0},{6,2},{1,5},{3,7},{5,1},{7,3},{8,12},{10,14},{12... | collective-permute-start | bytes 393224 | tf_op jit(solution)/shard_map/ppermute | solution.py:39
  242.8 9.4 %collective-permute-start.43 = (f32[32,8,128]{2,1,0:T(8,128)S(1)}, f32[32,8,128]{2,1,0:T(8,128)S(1)}, u32[]{:S(2)}, u32[]{:S(2)}) collective-permute-start(f32[32,8,128]{2,1,0:T(8,128)S(1)} %pad_maximum_fusion.3.refs_0_), channel_id=1, source_target_pairs={{0,2},{2,4},{4,6},{6,0},{1,3},{3,5},{5,7},{7,1},{8,10},{10,12},{12... | collective-permute-start | bytes 393224 | tf_op jit(solution)/shard_map/ppermute | solution.py:39
Sparse Core Ops, SparseCore 0:
  48.8 56.6 all-gather.1
  119.6 54.0 reduce-scatter.1

commit v9 on v8

--- a/solution.py
+++ b/solution.py
@@ -655,20 +655,21 @@
     )(origin, all_rows, *tops, *bottoms)
 
 
-def plane_scatter_sum(top_grads, bottom_grads):
+def added(terms):
+    total = terms[0].astype(F32)
+    for term in terms[1:]:
+        total = total + term.astype(F32)
+    return total
+
+
+def plane_scatter(top_grads, bottom_grads, beside):
     ny = len(top_grads)
-
-    def added(terms):
-        total = terms[0].astype(F32)
-        for term in terms[1:]:
-            total = total + term.astype(F32)
-        return total
-
     top = added([move(top_grads[d], y=-d) for d in range(ny)]).astype(BF16)
     bottom = added([move(bottom_grads[f], xl=a, xh=b) for f, (a, b) in enumerate(FLIPS)]).astype(BF16)
-    top = added([move(top[f], xl=a, xh=b) for f, (a, b) in enumerate(FLIPS)])
-    bottom = added([move(bottom[d], y=-d) for d in range(ny)])
-    return jnp.concatenate([top, bottom], axis=1).T
+    top, bottom, beside = lax.optimization_barrier((top, bottom, beside))
+    top = [move(top[f], xl=a, xh=b) for f, (a, b) in enumerate(FLIPS)]
+    bottom = [move(bottom[d], y=-d) for d in range(ny)]
+    return top, bottom, beside
 
 
 def shards(tokens_in, short_filter, long_filter, out_weight, cotangent):
@@ -698,11 +699,11 @@
     query, key, value, mixer = features_call(tokens, rim, short_filter)
     mixer, out_weight = lax.optimization_barrier((mixer, out_weight))
     mixer_prev = along(mixer, 1)
+    wide_top = gather_wide(out_weight)
+    mixer_prev, wide_top = lax.optimization_barrier((mixer_prev, wide_top))
+    mixed, gated = mix_call(lines, mixer_prev, mixer, query)
+    mixed, out_weight, wide_top, upstream = lax.optimization_barrier((mixed, out_weight, wide_top, upstream))
     tall_bottom = gather_tall(out_weight)
-    mixer_prev, tall_bottom = lax.optimization_barrier((mixer_prev, tall_bottom))
-    mixed, gated = mix_call(lines, mixer_prev, mixer, query)
-    mixed, out_weight, tall_bottom, upstream = lax.optimization_barrier((mixed, out_weight, tall_bottom, upstream))
-    wide_top = gather_wide(out_weight)
     all_rows = lax.all_gather(gated, ("z", "c"), axis=0, tiled=True)
     tops, bottoms = gather_far(wide_top, tall_bottom)
     mine = lax.dynamic_slice_in_dim(upstream, xh * span, span, 0)
@@ -714,16 +715,18 @@
 
     top_grads, bottom_grads = weight_grad(origin, all_rows, cotangents.T, ny)
     own, other = output_call(origin, all_rows, tops, bottoms)
-    grad_weight = plane_scatter_sum(top_grads, bottom_grads)
-    theirs = move(other, xh=1)
-    output = jnp.where(xh == 0, jnp.concatenate([own, theirs], axis=0), jnp.concatenate([theirs, own], axis=0))
-    gate_grad, grad_weight, output = lax.optimization_barrier((gate_grad, grad_weight, output))
+    top, bottom, other = plane_scatter(top_grads, bottom_grads, other)
+    gate_grad, top, bottom, other = lax.optimization_barrier((gate_grad, top, bottom, other))
 
     grad_mixed, query_grad = gate_call(place, gate_grad, query, mixed)
     grad_next = along(grad_mixed, -1)
     long_sum, query_sum = long_grad_call(
         groups, short_taps, mixer_prev, mixer, grad_mixed, query_grad, tokens, rim
     )
+    grad_weight = jnp.concatenate([added(top), added(bottom)], axis=1).T
+    theirs = move(other, xh=1)
+    grad_next, grad_weight, theirs = lax.optimization_barrier((grad_next, grad_weight, theirs))
+    output = jnp.where(xh == 0, jnp.concatenate([own, theirs], axis=0), jnp.concatenate([theirs, own], axis=0))
     other_grads, key_sum, value_sum, edge = unmix_call(
         lines, short_taps, grad_mixed, grad_next, key, value, tokens, rim, query_grad
     )

time: 261 us -> 258 us (0.989)
  waiting for transfers between devices: 79 us -> 73.2 us
  starting transfers between devices: 76.8 us -> 80.5 us
    ppermute x40, waiting for transfers between devices: 67.4 us -> 54.6 us  [move(): return lax.ppermute(x, axes, pairs)]
    all_gather x1, waiting for transfers between devices: 0.01 us -> 12.4 us  [shards(): all_rows = lax.all_gather(gated, ('z', 'c'), axis=0, tiled=True)]
    ppermute x4, waiting for transfers between devices: 10.3 us -> 6 us  [along(): return lax.ppermute(x, LINE, pairs)]
    ppermute x40, starting transfers between devices: 59.8 us -> 62.7 us  [move(): return lax.ppermute(x, axes, pairs)]
  transfers between devices with their start and end apart: 46 -> 46, of which waited for: 23 -> 28; matrix products, arithmetic and copies ran while one was open for 3% -> 3% of each run, Pallas kernels for 18% -> 18%
where the time goes in v9:
time: 258 us; the launch traced here: 257 us
  starting transfers between devices  80.5 us (31%)
  Pallas kernels  79.5 us (31%)
  waiting for transfers between devices  73.2 us (28%)
  between operations  14.4 us (6%)
  local copies, waits for them, and re-layouts  6.13 us (2%)
  other arithmetic  3.31 us (1%)
    pallas_call x10, Pallas kernels, run(): return call(*held)  77.4 us
    ppermute x40, starting transfers between devices, move(): return lax.ppermute(x, axes, pairs)  62.7 us
    ppermute x40, waiting for transfers between devices, move(): return lax.ppermute(x, axes, pairs)  54.6 us
    ppermute x4, starting transfers between devices, along(): return lax.ppermute(x, LINE, pairs)  17.7 us
    all_gather x1, waiting for transfers between devices, shards(): all_rows = lax.all_gather(gated, ('z', 'c'), axis=0, tiled=True)  12.4 us
    ppermute x4, waiting for transfers between devices, along(): return lax.ppermute(x, LINE, pairs)  6 us
  transfers between devices with their start and end apart: 46, of which 28 were waited for; matrix products, arithmetic and copies ran while one was open for 3% of the time, Pallas kernels for 18%

profile of v9, /device:TPU:1, one launch (start us, length us, event | category | flops | bytes accessed | tf_op | source)
XLA Modules:
  0.0 257.1 jit_solution(14356772213186143618)
XLA Ops:
  7.2 0.9 slice_bitcast_fusion
  8.2 4.9 %collective-permute-start = (bf16[8,12288]{1,0:T(8,128)(2,1)S(1)}, bf16[8,12288]{1,0:T(8,128)(2,1)S(1)}, u32[]{:S(2)}, u32[]{:S(2)}) collective-permute-start(bf16[8,12288]{1,0:T(8,128)(2,1)S(1)} %slice_bitcast_fusion), channel_id=1, source_target_pairs={{0,1},{1,2},{2,3},{3,4},{4,5},{5,6},{6,7},{7,8},{8,9},{9,10},{10,1... | collective-permute-start | bytes 589832 | tf_op jit(solution)/shard_map/ppermute | solution.py:27
  13.1 2.6 %collective-permute-done.refs_3_.refs_4_.refs_5_.key_rim_ref.value_rim_ref.rim_ref = bf16[8,12288]{1,0:T(8,128)(2,1)S(1)} collective-permute-done((bf16[8,12288]{1,0:T(8,128)(2,1)S(1)}, bf16[8,12288]{1,0:T(8,128)(2,1)S(1)}, u32[]{:S(2)}, u32[]{:S(2)}) %collective-permute-start) | collective-permute-done | bytes 196640 | tf_op jit(solution)/shard_map/ppermute | solution.py:27
  15.7 6.8 %features.1 = (bf16[128,4096]{1,0:T(8,128)(2,1)}, bf16[128,4096]{1,0:T(8,128)(2,1)}, bf16[128,4096]{1,0:T(8,128)(2,1)}, bf16[128,4096]{1,0:T(8,128)(2,1)}) custom-call(bf16[128,12288]{1,0:T(8,128)(2,1)} %bitcast.37, bf16[128,12288]{1,0:T(8,128)(2,1)} %bitcast.38, bf16[128,12288]{1,0:T(8,128)(2,1)} %bitcast.39, ...), custom_call_target="tpu_custom_call" | custom-call | bytes 1572864 | tf_op jit(solution)/shard_map/features/pallas_call | solution.py:64
  22.5 4.4 %collective-permute-start.1 = (bf16[128,4096]{1,0:T(8,128)(2,1)}, bf16[128,4096]{1,0:T(8,128)(2,1)S(1)}, u32[]{:S(2)}, u32[]{:S(2)}) collective-permute-start(bf16[128,4096]{1,0:T(8,128)(2,1)} %get-tuple-element.71.cur_ref), channel_id=1, source_target_pairs={{0,1},{1,2},{2,3},{3,4},{4,5},{5,6},{6,7},{7,8},{8,9},{9,10},{10,1... | collective-permute-start | bytes 3145736 | tf_op jit(solution)/shard_map/ppermute | solution.py:27
  26.9 2.8 %collective-permute-start.2 = (bf16[256,256]{1,0:T(8,128)(2,1)S(1)}, bf16[256,256]{1,0:T(8,128)(2,1)S(1)}, u32[]{:S(2)}, u32[]{:S(2)}) collective-permute-start(bf16[256,256]{1,0:T(8,128)(2,1)S(1)} %slice.56), channel_id=1, source_target_pairs={{0,8},{8,0},{1,9},{9,1},{2,10},{10,2},{3,11},{11,3},{4,12},{12,4},... | collective-permute-start | bytes 393224 | tf_op jit(solution)/shard_map/ppermute | solution.py:39
  30.6 1.7 collective-permute-done.2
  32.3 2.0 collective-permute-done.3
  34.3 1.9 collective-permute-done.4
  36.2 2.8 %collective-permute-done.1.prev_ref = bf16[128,4096]{1,0:T(8,128)(2,1)S(1)} collective-permute-done((bf16[128,4096]{1,0:T(8,128)(2,1)}, bf16[128,4096]{1,0:T(8,128)(2,1)S(1)}, u32[]{:S(2)}, u32[]{:S(2)}) %collective-permute-start.1) | collective-permute-done | bytes 1048608 | tf_op jit(solution)/shard_map/ppermute | solution.py:27
  38.9 9.8 %mix.1 = (bf16[128,4096]{1,0:T(8,128)(2,1)}, bf16[128,4096]{1,0:T(8,128)(2,1)}) custom-call(f32[256,128]{1,0:T(8,128)S(1)} %convert_element_type.57.lines_ref, bf16[128,4096]{1,0:T(8,128)(2,1)S(1)} %collective-permute-done.1.prev_ref, bf16[128,4096]{1,0:T(8,128)(2,1)} %get-tuple-element.71.cur_ref, bf16[128,4096]{1,0:T(8,128)(2,1)} %get-tuple-element.74.query_ref), custom_call_target="tpu_custom_call" | custom-call | bytes 1048576 | tf_op jit(solution)/shard_map/mix/pallas_call | solution.py:64
  49.5 1.4 collective-permute-start.6
  51.0 2.8 %collective-permute-start.5 = (bf16[1024,256]{0,1:T(8,128)(2,1)S(1)}, bf16[1024,256]{0,1:T(8,128)(2,1)S(1)}, u32[]{:S(2)}, u32[]{:S(2)}) collective-permute-start(bf16[1024,256]{0,1:T(8,128)(2,1)S(1)} %get-tuple-element.143), channel_id=1, source_target_pairs={{0,8},{8,0},{1,9},{9,1},{2,10},{10,2},{3,11},{11,3},{4,12},{12,4},... | collective-permute-start | bytes 1572872 | tf_op jit(solution)/shard_map/ppermute | solution.py:39
  53.8 1.5 collective-permute-start.11
  55.4 2.6 %collective-permute-start.10 = (bf16[256,256]{1,0:T(8,128)(2,1)S(1)}, bf16[256,256]{1,0:T(8,128)(2,1)S(1)}, u32[]{:S(2)}, u32[]{:S(2)}) collective-permute-start(bf16[256,256]{1,0:T(8,128)(2,1)S(1)} %get-tuple-element.156), channel_id=1, source_target_pairs={{0,64},{32,96},{64,0},{96,32},{1,65},{33,97},{65,1},{97,33},{2,66}... | collective-permute-start | bytes 393224 | tf_op jit(solution)/shard_map/ppermute | solution.py:39
  58.0 2.6 %collective-permute-start.7 = (bf16[4,256,256]{2,1,0:T(8,128)(2,1)S(1)}, bf16[4,256,256]{2,1,0:T(8,128)(2,1)}, u32[]{:S(2)}, u32[]{:S(2)}) collective-permute-start(bf16[4,256,256]{2,1,0:T(8,128)(2,1)S(1)} %pad_maximum_fusion.1.refs_1_.refs_0_), channel_id=1, source_target_pairs={{0,64},{32,96},{64,0},{96,32},{1,65},{33,97},{65,1},{97,33},{2,66}... | collective-permute-start | bytes 1572872 | tf_op jit(solution)/shard_map/ppermute | solution.py:39
  60.6 5.6 %collective-permute-done.9 = bf16[256,256]{1,0:T(8,128)(2,1)S(1)} collective-permute-done((bf16[256,256]{1,0:T(8,128)(2,1)S(1)}, bf16[256,256]{1,0:T(8,128)(2,1)S(1)}, u32[]{:S(2)}, u32[]{:S(2)}) %collective-permute-start.9) | collective-permute-done | bytes 131104 | tf_op jit(solution)/shard_map/ppermute | solution.py:39
  66.2 1.5 collective-permute-start.8
  67.7 1.1 collective-permute-done.10
  69.0 0.8 copy-done.2
  69.9 3.1 %collective-permute-start.14 = (bf16[4,256,256]{2,1,0:T(8,128)(2,1)S(1)}, bf16[4,256,256]{2,1,0:T(8,128)(2,1)}, u32[]{:S(2)}, u32[]{:S(2)}) collective-permute-start(bf16[4,256,256]{2,1,0:T(8,128)(2,1)S(1)} %pad_maximum_fusion.2.refs_5_.refs_4_), channel_id=1, source_target_pairs={{0,24},{8,16},{16,8},{24,0},{1,25},{9,17},{17,9},{25,1},{2,26},{10... | collective-permute-start | bytes 1572872 | tf_op jit(solution)/shard_map/ppermute | solution.py:39
  73.0 1.1 fusion.11
  74.2 1.5 copy.12.refs_0_
  75.7 3.5 %collective-permute-done.7.refs_3_.refs_2_ = bf16[4,256,256]{2,1,0:T(8,128)(2,1)} collective-permute-done((bf16[4,256,256]{2,1,0:T(8,128)(2,1)S(1)}, bf16[4,256,256]{2,1,0:T(8,128)(2,1)}, u32[]{:S(2)}, u32[]{:S(2)}) %collective-permute-start.7) | collective-permute-done | bytes 524320 | tf_op jit(solution)/shard_map/ppermute | solution.py:39
  79.2 2.8 %collective-permute-done.8.refs_4_.refs_3_ = bf16[4,256,256]{2,1,0:T(8,128)(2,1)} collective-permute-done((bf16[4,256,256]{2,1,0:T(8,128)(2,1)S(1)}, bf16[4,256,256]{2,1,0:T(8,128)(2,1)}, u32[]{:S(2)}, u32[]{:S(2)}) %collective-permute-start.8) | collective-permute-done | bytes 524320 | tf_op jit(solution)/shard_map/ppermute | solution.py:39
  82.3 4.6 %collective-permute-done.14.refs_8_.refs_7_ = bf16[4,256,256]{2,1,0:T(8,128)(2,1)} collective-permute-done((bf16[4,256,256]{2,1,0:T(8,128)(2,1)S(1)}, bf16[4,256,256]{2,1,0:T(8,128)(2,1)}, u32[]{:S(2)}, u32[]{:S(2)}) %collective-permute-start.14) | collective-permute-done | bytes 524320 | tf_op jit(solution)/shard_map/ppermute | solution.py:39
  87.0 1.0 copy-done.3
  88.0 8.5 %gate_matmul.1 = bf16[1024,4096]{1,0:T(8,128)(2,1)} custom-call(bf16[1024,512]{1,0:T(8,128)(2,1)S(1)} %copy.12.refs_0_, bf16[4,256,256]{2,1,0:T(8,128)(2,1)S(1)} %pad_maximum_fusion.1.refs_1_.refs_0_, bf16[4,256,256]{2,1,0:T(8,128)(2,1)S(1)} %copy-done.3, bf16[4,256,256]{2,1,0:T(8,128)(2,1)} %collective-permute-done.7.refs_3_.refs_2_, ...), custom_call_target="tpu_custom_call" | custom-call | flops 4294967296 | bytes 12582912 | tf_op jit(solution)/shard_map/gate_matmul/pallas_call | solution.py:64
  96.6 12.4 %all-gather.2.cloned.1.call-done.rows_ref = bf16[1024,4096]{1,0:T(8,128)(2,1)} async-done(((bf16[128,4096]{1,0:T(8,128)(2,1)}), bf16[1024,4096]{1,0:T(8,128)(2,1)}) %all-gather.2.cloned.1.call-update) | async-done | bytes 8388624 | tf_op jit(solution)/shard_map/all_gather | solution.py:707
  109.0 9.9 %weight_grad.1 = (bf16[4,256,256]{2,1,0:T(8,128)(2,1)}, bf16[4,256,256]{2,1,0:T(8,128)(2,1)}, bf16[4,256,256]{2,1,0:T(8,128)(2,1)}, bf16[4,256,256]{2,1,0:T(8,12...) custom-call(s32[8]{0:T(128)S(1)} %fusion.2.origin.place, ...), custom_call_target="tpu_custom_call" | custom-call | flops 4294967296 | bytes 12582912 | tf_op jit(solution)/shard_map/weight_grad/pallas_call | solution.py:64
  118.9 2.7 %collective-permute-start.18 = (bf16[4,256,256]{2,1,0:T(8,128)(2,1)}, bf16[4,256,256]{2,1,0:T(8,128)(2,1)S(1)}, u32[]{:S(2)}, u32[]{:S(2)}) collective-permute-start(bf16[4,256,256]{2,1,0:T(8,128)(2,1)} %get-tuple-element.95), channel_id=1, source_target_pairs={{0,8},{8,0},{1,9},{9,1},{2,10},{10,2},{3,11},{11,3},{4,12},{12,4},... | collective-permute-start | bytes 1572872 | tf_op jit(solution)/shard_map/ppermute | solution.py:39
  122.5 2.5 collective-permute-start.15
  125.4 8.5 %collective-permute-done.18 = bf16[4,256,256]{2,1,0:T(8,128)(2,1)S(1)} collective-permute-done((bf16[4,256,256]{2,1,0:T(8,128)(2,1)}, bf16[4,256,256]{2,1,0:T(8,128)(2,1)S(1)}, u32[]{:S(2)}, u32[]{:S(2)}) %collective-permute-start.18) | collective-permute-done | bytes 524320 | tf_op jit(solution)/shard_map/ppermute | solution.py:39
  133.9 1.2 collective-permute-start.17
  135.1 9.9 %output.1 = (bf16[1024,256]{1,0:T(8,128)(2,1)}, bf16[1024,256]{1,0:T(8,128)(2,1)}) custom-call(s32[8]{0:T(128)S(1)} %fusion.2.origin.place, bf16[1024,4096]{1,0:T(8,128)(2,1)} %all-gather.2.cloned.1.call-done.rows_ref, bf16[4,256,256]{2,1,0:T(8,128)(2,1)S(1)} %pad_maximum_fusion.1.refs_1_.refs_0_, bf16[4,256,256]{2,1,0:T(8,128)(2,1)S(1)} %copy-done.4, ...), custom_call_target="tpu_custom_call" | custom-call | flops 4294967296 | bytes 12582912 | tf_op jit(solution)/shard_map/output/pallas_call | solution.py:64
  146.1 5.2 %collective-permute-done.17 = bf16[4,256,256]{2,1,0:T(8,128)(2,1)S(1)} collective-permute-done((bf16[4,256,256]{2,1,0:T(8,128)(2,1)}, bf16[4,256,256]{2,1,0:T(8,128)(2,1)S(1)}, u32[]{:S(2)}, u32[]{:S(2)}) %collective-permute-start.17) | collective-permute-done | bytes 524320 | tf_op jit(solution)/shard_map/ppermute | solution.py:39
  151.6 2.5 collective-permute-start.21
  155.4 1.6 collective-permute-done.21
  157.0 2.9 %collective-permute-done.22 = bf16[256,256]{1,0:T(8,128)(2,1)S(1)} collective-permute-done((bf16[256,256]{1,0:T(8,128)(2,1)S(1)}, bf16[256,256]{1,0:T(8,128)(2,1)S(1)}, u32[]{:S(2)}, u32[]{:S(2)}) %collective-permute-start.22) | collective-permute-done | bytes 131104 | tf_op jit(solution)/shard_map/ppermute | solution.py:39
  159.8 1.0 collective-permute-done.23
  160.9 1.7 collective-permute-done.26
  162.9 3.6 %gate_back.1 = (bf16[128,4096]{1,0:T(8,128)(2,1)}, bf16[128,4096]{1,0:T(8,128)(2,1)}) custom-call(s32[8]{0:T(128)S(1)} %fusion.2.origin.place, bf16[128,4096]{1,0:T(8,128)(2,1)} %reduce-scatter.2.cloned.1.call-done.gate_grad_ref, bf16[128,4096]{1,0:T(8,128)(2,1)} %get-tuple-element.74.query_ref, bf16[128,4096]{1,0:T(8,128)(2,1)} %get-tuple-element.103.mixed_ref), custom_call_target="tpu_custom_call" | custom-call | flops 1048576 | bytes 5242880 | tf_op jit(solution)/shard_map/gate_back/pallas_call | solution.py:64
  166.5 5.6 %collective-permute-start.27 = (bf16[128,4096]{1,0:T(8,128)(2,1)}, bf16[128,4096]{1,0:T(8,128)(2,1)S(1)}, u32[]{:S(2)}, u32[]{:S(2)}) collective-permute-start(bf16[128,4096]{1,0:T(8,128)(2,1)} %get-tuple-element.104.grad_ref), channel_id=1, source_target_pairs={{1,0},{2,1},{3,2},{4,3},{5,4},{6,5},{7,6},{8,7},{9,8},{10,9},{11,1... | collective-permute-start | bytes 3145736 | tf_op jit(solution)/shard_map/ppermute | solution.py:27
  172.1 2.6 %collective-permute-start.28 = (bf16[1024,256]{1,0:T(8,128)(2,1)S(1)}, bf16[1024,256]{1,0:T(8,128)(2,1)S(1)}, u32[]{:S(2)}, u32[]{:S(2)}) collective-permute-start(bf16[1024,256]{1,0:T(8,128)(2,1)S(1)} %copy-done.11), channel_id=1, source_target_pairs={{0,8},{8,0},{1,9},{9,1},{2,10},{10,2},{3,11},{11,3},{4,12},{12,4},... | collective-permute-start | bytes 1572872 | tf_op jit(solution)/shard_map/ppermute | solution.py:39
  174.9 9.1 %long_grad.1 = (f32[256,128]{1,0:T(8,128)S(1)}, f32[8,4096]{1,0:T(8,128)S(1)}) custom-call(bf16[128,4096]{1,0:T(8,128)(2,1)} %copy-done.1, bf16[128,4096]{1,0:T(8,128)(2,1)} %get-tuple-element.71.cur_ref, bf16[128,4096]{1,0:T(8,128)(2,1)} %get-tuple-element.104.grad_ref, bf16[128,4096]{1,0:T(8,128)(2,1)} %get-tuple-element.118.query_grad_ref.feature_ref, ...), custom_call_target="tpu_custom_call" | custom-call | flops 2147483648 | bytes 5242880 | tf_op jit(solution)/shard_map/long_grad/pallas_call | solution.py:64
  184.0 3.0 %collective-permute-done.28 = bf16[1024,256]{1,0:T(8,128)(2,1)S(1)} collective-permute-done((bf16[1024,256]{1,0:T(8,128)(2,1)S(1)}, bf16[1024,256]{1,0:T(8,128)(2,1)S(1)}, u32[]{:S(2)}, u32[]{:S(2)}) %collective-permute-start.28) | collective-permute-done | bytes 524320 | tf_op jit(solution)/shard_map/ppermute | solution.py:39
  187.0 11.4 %unmix.1 = (bf16[2,128,4096]{2,1,0:T(8,128)(2,1)}, f32[8,4096]{1,0:T(8,128)S(1)}, f32[8,4096]{1,0:T(8,128)S(1)}, bf16[3,8,4096]{2,1,0:T(8,128)(2,1)S(1)}) custom-call(f32[256,128]{1,0:T(8,128)S(1)} %convert_element_type.57.lines_ref, bf16[128,4096]{1,0:T(8,128)(2,1)} %get-tuple-element.104.grad_ref, bf16[128,4096]{1,0:T(8,128)(2,1)S(1)} %collective-permute-done.27.next_ref, ...), custom_call_target="tpu_custom_call" | custom-call | flops 2147483648 | bytes 8388608 | tf_op jit(solution)/shard_map/unmix/pallas_call | solution.py:64
  199.0 12.5 %collective-permute-start.30 = (f32[64,8,128]{2,1,0:T(8,128)S(1)}, f32[64,8,128]{2,1,0:T(8,128)S(1)}, u32[]{:S(2)}, u32[]{:S(2)}) collective-permute-start(f32[64,8,128]{2,1,0:T(8,128)S(1)} %get-tuple-element.126), channel_id=1, source_target_pairs={{0,1},{1,0},{2,3},{3,2},{4,5},{5,4},{6,7},{7,6},{8,9},{9,8},{10,11... | collective-permute-start | bytes 786440 | tf_op jit(solution)/shard_map/ppermute | solution.py:39
  211.6 1.2 collective-permute-done.30
  213.0 2.6 %collective-permute-start.33 = (f32[16,8,128]{2,1,0:T(8,128)S(1)}, f32[16,8,128]{2,1,0:T(8,128)S(1)}, u32[]{:S(2)}, u32[]{:S(2)}) collective-permute-start(f32[16,8,128]{2,1,0:T(8,128)S(1)} %get-tuple-element.153), channel_id=1, source_target_pairs={{0,6},{2,0},{4,2},{6,4},{1,7},{3,1},{5,3},{7,5},{8,14},{10,8},{12,... | collective-permute-start | bytes 196616 | tf_op jit(solution)/shard_map/ppermute | solution.py:39
  215.6 2.8 %collective-permute-start.29 = (bf16[3,8,4096]{2,1,0:T(8,128)(2,1)S(1)}, bf16[3,8,4096]{2,1,0:T(8,128)(2,1)S(1)}, u32[]{:S(2)}, u32[]{:S(2)}) collective-permute-start(bf16[3,8,4096]{2,1,0:T(8,128)(2,1)S(1)} %get-tuple-element.120), channel_id=1, source_target_pairs={{1,0},{2,1},{3,2},{4,3},{5,4},{6,5},{7,6},{8,7},{9,8},{10,9},{11,1... | collective-permute-start | bytes 589832 | tf_op jit(solution)/shard_map/ppermute | solution.py:27
  219.3 1.4 collective-permute-start.35
  220.6 1.3 collective-permute-start.36
  222.5 3.2 %short_adjoint.2.refs_0_ = bf16[128,12288]{1,0:T(8,128)(2,1)} custom-call(bf16[1,128,4096]{2,1,0:T(8,128)(2,1)} %bitcast.44, bf16[3,8,4096]{2,1,0:T(8,128)(2,1)S(1)} %collective-permute-done.29.rim_ref, f32[7,12288]{1,0:T(8,128)} %filter_ref.3), custom_call_target="tpu_custom_call" | custom-call | flops 7340032 | bytes 2097152 | tf_op jit(solution)/shard_map/short_adjoint/pallas_call | solution.py:64
  225.8 1.1 collective-permute-start.37
  226.8 2.9 %collective-permute-start.39 = (f32[16,8,128]{2,1,0:T(8,128)S(1)}, f32[16,8,128]{2,1,0:T(8,128)S(1)}, u32[]{:S(2)}, u32[]{:S(2)}) collective-permute-start(f32[16,8,128]{2,1,0:T(8,128)S(1)} %add_add_fusion.1), channel_id=1, source_target_pairs={{0,24},{8,16},{16,8},{24,0},{1,25},{9,17},{17,9},{25,1},{2,26},{10... | collective-permute-start | bytes 196616 | tf_op jit(solution)/shard_map/ppermute | solution.py:39
  229.7 1.9 collective-permute-done.38
  232.1 4.1 %collective-permute-start.40 = (f32[16,8,128]{2,1,0:T(8,128)S(1)}, f32[16,8,128]{2,1,0:T(8,128)S(1)}, u32[]{:S(2)}, u32[]{:S(2)}) collective-permute-start(f32[16,8,128]{2,1,0:T(8,128)S(1)} %add_add_fusion), channel_id=1, source_target_pairs={{0,1},{1,0},{2,3},{3,2},{4,5},{5,4},{6,7},{7,6},{8,9},{9,8},{10,11... | collective-permute-start | bytes 196616 | tf_op jit(solution)/shard_map/ppermute | solution.py:39
  236.2 1.0 copy.13
  237.2 2.4 collective-permute-start.41
  240.3 1.2 maximum_select_fusion
  241.5 5.1 %short_adjoint.3 = bf16[128,12288]{1,0:T(8,128)(2,1)} custom-call(bf16[2,128,4096]{2,1,0:T(8,128)(2,1)} %get-tuple-element.119.grads_ref, bf16[3,8,4096]{2,1,0:T(8,128)(2,1)S(1)} %collective-permute-done.29.rim_ref, f32[7,12288]{1,0:T(8,128)} %filter_ref.3, bf16[128,12288]{1,0:T(8,128)(2,1)} %short_adjoint.2.refs_0_), custom_call_target="tpu_custom_call", output_to_operand_aliasing={{}: (3, {})} | custom-call | flops 14680064 | bytes 4194304 | tf_op jit(solution)/shard_map/short_adjoint/pallas_call | solution.py:64
  246.7 2.1 collective-permute-done.43.refs_3_
  248.8 1.5 collect.1
  (93 shorter events, 10.5 us)
Async XLA Ops:
  7.2 101.8 %all-gather.2.cloned.1.call-start = ((), (), s32[]{:S(2)}) async-start(), calls=%async_computation.1 | async-start | bytes 9437184 | tf_op jit(solution)/shard_map/all_gather | solution.py:707
  8.2 7.5 %collective-permute-start = (bf16[8,12288]{1,0:T(8,128)(2,1)S(1)}, bf16[8,12288]{1,0:T(8,128)(2,1)S(1)}, u32[]{:S(2)}, u32[]{:S(2)}) collective-permute-start(bf16[8,12288]{1,0:T(8,128)(2,1)S(1)} %slice_bitcast_fusion), channel_id=1, source_target_pairs={{0,1},{1,2},{2,3},{3,4},{4,5},{5,6},{6,7},{7,8},{8,9},{9,10},{10,1... | collective-permute-start | bytes 589832 | tf_op jit(solution)/shard_map/ppermute | solution.py:27
  15.7 6.8 %copy-start = (bf16[8,12288]{1,0:T(8,128)(2,1)}, bf16[8,12288]{1,0:T(8,128)(2,1)S(1)}, u32[]{:S(2)}) copy-start(bf16[8,12288]{1,0:T(8,128)(2,1)S(1)} %collective-permute-done.refs_3_.refs_4_.refs_5_.key_rim_ref.value_rim_ref.rim_ref) | copy-start | bytes 589828
  15.7 11.2 %copy-start.9 = (bf16[512,256]{1,0:T(8,128)(2,1)S(1)}, bf16[512,256]{1,0:T(8,128)(2,1)}, u32[]{:S(2)}) copy-start(bf16[512,256]{1,0:T(8,128)(2,1)} %param.8) | copy-start | bytes 786436
  15.7 14.9 %copy-start.10 = (bf16[256,128]{1,0:T(8,128)(2,1)S(1)}, bf16[256,128]{1,0:T(8,128)(2,1)}, u32[]{:S(2)}) copy-start(bf16[256,128]{1,0:T(8,128)(2,1)} %param.7) | copy-start | bytes 196612
  22.5 16.4 %collective-permute-start.1 = (bf16[128,4096]{1,0:T(8,128)(2,1)}, bf16[128,4096]{1,0:T(8,128)(2,1)S(1)}, u32[]{:S(2)}, u32[]{:S(2)}) collective-permute-start(bf16[128,4096]{1,0:T(8,128)(2,1)} %get-tuple-element.71.cur_ref), channel_id=1, source_target_pairs={{0,1},{1,2},{2,3},{3,4},{4,5},{5,6},{6,7},{7,8},{8,9},{9,10},{10,1... | collective-permute-start | bytes 3145736 | tf_op jit(solution)/shard_map/ppermute | solution.py:27
  26.9 5.4 %collective-permute-start.2 = (bf16[256,256]{1,0:T(8,128)(2,1)S(1)}, bf16[256,256]{1,0:T(8,128)(2,1)S(1)}, u32[]{:S(2)}, u32[]{:S(2)}) collective-permute-start(bf16[256,256]{1,0:T(8,128)(2,1)S(1)} %slice.56), channel_id=1, source_target_pairs={{0,8},{8,0},{1,9},{9,1},{2,10},{10,2},{3,11},{11,3},{4,12},{12,4},... | collective-permute-start | bytes 393224 | tf_op jit(solution)/shard_map/ppermute | solution.py:39
  29.8 4.5 %collective-permute-start.3 = (bf16[256,256]{1,0:T(8,128)(2,1)S(1)}, bf16[256,256]{1,0:T(8,128)(2,1)S(1)}, u32[]{:S(2)}, u32[]{:S(2)}) collective-permute-start(bf16[256,256]{1,0:T(8,128)(2,1)S(1)} %slice.56), channel_id=1, source_target_pairs={{0,16},{16,0},{1,17},{17,1},{2,18},{18,2},{3,19},{19,3},{4,20},{20... | collective-permute-start | bytes 393224 | tf_op jit(solution)/shard_map/ppermute | solution.py:39
  30.1 6.1 %collective-permute-start.4 = (bf16[256,256]{1,0:T(8,128)(2,1)S(1)}, bf16[256,256]{1,0:T(8,128)(2,1)S(1)}, u32[]{:S(2)}, u32[]{:S(2)}) collective-permute-start(bf16[256,256]{1,0:T(8,128)(2,1)S(1)} %slice.56), channel_id=1, source_target_pairs={{0,24},{8,16},{16,8},{24,0},{1,25},{9,17},{17,9},{25,1},{2,26},{10... | collective-permute-start | bytes 393224 | tf_op jit(solution)/shard_map/ppermute | solution.py:39
  38.9 9.8 %copy-start.1 = (bf16[128,4096]{1,0:T(8,128)(2,1)}, bf16[128,4096]{1,0:T(8,128)(2,1)S(1)}, u32[]{:S(2)}) copy-start(bf16[128,4096]{1,0:T(8,128)(2,1)S(1)} %collective-permute-done.1.prev_ref) | copy-start | bytes 3145732
  38.9 9.9 %copy-start.5 = (bf16[1,2048,256]{2,1,0:T(8,128)(2,1)S(1)}, bf16[1,2048,256]{2,1,0:T(8,128)(2,1)}, u32[]{:S(2)}) copy-start(bf16[1,2048,256]{2,1,0:T(8,128)(2,1)} %param.9) | copy-start | bytes 3145732
  48.7 114.1 %reduce-scatter.2.cloned.1.call-start = ((), (), s32[]{:S(2)}) async-start(), calls=%async_computation.2 | async-start | bytes 9437184 | tf_op jit(solution)/shard_map/reduce_scatter | solution.py:714
  49.5 19.4 %collective-permute-start.6 = (bf16[4,256,256]{2,1,0:T(8,128)(2,1)S(1)}, bf16[4,256,256]{2,1,0:T(8,128)(2,1)S(1)}, u32[]{:S(2)}, u32[]{:S(2)}) collective-permute-start(bf16[4,256,256]{2,1,0:T(8,128)(2,1)S(1)} %pad_maximum_fusion.1.refs_1_.refs_0_), channel_id=1, source_target_pairs={{0,32},{32,64},{64,96},{96,0},{1,33},{33,65},{65,97},{97,1},{2,34}... | collective-permute-start | bytes 1572872 | tf_op jit(solution)/shard_map/ppermute | solution.py:39
  51.0 18.9 %collective-permute-start.5 = (bf16[1024,256]{0,1:T(8,128)(2,1)S(1)}, bf16[1024,256]{0,1:T(8,128)(2,1)S(1)}, u32[]{:S(2)}, u32[]{:S(2)}) collective-permute-start(bf16[1024,256]{0,1:T(8,128)(2,1)S(1)} %get-tuple-element.143), channel_id=1, source_target_pairs={{0,8},{8,0},{1,9},{9,1},{2,10},{10,2},{3,11},{11,3},{4,12},{12,4},... | collective-permute-start | bytes 1572872 | tf_op jit(solution)/shard_map/ppermute | solution.py:39
  53.8 4.2 %collective-permute-start.11 = (bf16[256,256]{1,0:T(8,128)(2,1)S(1)}, bf16[256,256]{1,0:T(8,128)(2,1)S(1)}, u32[]{:S(2)}, u32[]{:S(2)}) collective-permute-start(bf16[256,256]{1,0:T(8,128)(2,1)S(1)} %get-tuple-element.156), channel_id=1, source_target_pairs={{0,96},{32,0},{64,32},{96,64},{1,97},{33,1},{65,33},{97,65},{2,98}... | collective-permute-start | bytes 393224 | tf_op jit(solution)/shard_map/ppermute | solution.py:39
  55.4 10.9 %collective-permute-start.9 = (bf16[256,256]{1,0:T(8,128)(2,1)S(1)}, bf16[256,256]{1,0:T(8,128)(2,1)S(1)}, u32[]{:S(2)}, u32[]{:S(2)}) collective-permute-start(bf16[256,256]{1,0:T(8,128)(2,1)S(1)} %get-tuple-element.156), channel_id=1, source_target_pairs={{0,32},{32,64},{64,96},{96,0},{1,33},{33,65},{65,97},{97,1},{2,34}... | collective-permute-start | bytes 393224 | tf_op jit(solution)/shard_map/ppermute | solution.py:39
  55.4 13.4 %collective-permute-start.10 = (bf16[256,256]{1,0:T(8,128)(2,1)S(1)}, bf16[256,256]{1,0:T(8,128)(2,1)S(1)}, u32[]{:S(2)}, u32[]{:S(2)}) collective-permute-start(bf16[256,256]{1,0:T(8,128)(2,1)S(1)} %get-tuple-element.156), channel_id=1, source_target_pairs={{0,64},{32,96},{64,0},{96,32},{1,65},{33,97},{65,1},{97,33},{2,66}... | collective-permute-start | bytes 393224 | tf_op jit(solution)/shard_map/ppermute | solution.py:39
  58.0 21.1 %collective-permute-start.7 = (bf16[4,256,256]{2,1,0:T(8,128)(2,1)S(1)}, bf16[4,256,256]{2,1,0:T(8,128)(2,1)}, u32[]{:S(2)}, u32[]{:S(2)}) collective-permute-start(bf16[4,256,256]{2,1,0:T(8,128)(2,1)S(1)} %pad_maximum_fusion.1.refs_1_.refs_0_), channel_id=1, source_target_pairs={{0,64},{32,96},{64,0},{96,32},{1,65},{33,97},{65,1},{97,33},{2,66}... | collective-permute-start | bytes 1572872 | tf_op jit(solution)/shard_map/ppermute | solution.py:39
  66.2 15.8 %collective-permute-start.8 = (bf16[4,256,256]{2,1,0:T(8,128)(2,1)S(1)}, bf16[4,256,256]{2,1,0:T(8,128)(2,1)}, u32[]{:S(2)}, u32[]{:S(2)}) collective-permute-start(bf16[4,256,256]{2,1,0:T(8,128)(2,1)S(1)} %pad_maximum_fusion.1.refs_1_.refs_0_), channel_id=1, source_target_pairs={{0,96},{32,0},{64,32},{96,64},{1,97},{33,1},{65,33},{97,65},{2,98}... | collective-permute-start | bytes 1572872 | tf_op jit(solution)/shard_map/ppermute | solution.py:39
  68.9 13.1 %collective-permute-start.12 = (bf16[4,256,256]{2,1,0:T(8,128)(2,1)S(1)}, bf16[4,256,256]{2,1,0:T(8,128)(2,1)}, u32[]{:S(2)}, u32[]{:S(2)}) collective-permute-start(bf16[4,256,256]{2,1,0:T(8,128)(2,1)S(1)} %pad_maximum_fusion.2.refs_5_.refs_4_), channel_id=1, source_target_pairs={{0,8},{8,0},{1,9},{9,1},{2,10},{10,2},{3,11},{11,3},{4,12},{12,4},... | collective-permute-start | bytes 1572872 | tf_op jit(solution)/shard_map/ppermute | solution.py:39
  69.0 0.8 copy-start.2
  69.8 12.6 %collective-permute-start.13 = (bf16[4,256,256]{2,1,0:T(8,128)(2,1)S(1)}, bf16[4,256,256]{2,1,0:T(8,128)(2,1)}, u32[]{:S(2)}, u32[]{:S(2)}) collective-permute-start(bf16[4,256,256]{2,1,0:T(8,128)(2,1)S(1)} %pad_maximum_fusion.2.refs_5_.refs_4_), channel_id=1, source_target_pairs={{0,16},{16,0},{1,17},{17,1},{2,18},{18,2},{3,19},{19,3},{4,20},{20... | collective-permute-start | bytes 1572872 | tf_op jit(solution)/shard_map/ppermute | solution.py:39
  69.9 17.1 %collective-permute-start.14 = (bf16[4,256,256]{2,1,0:T(8,128)(2,1)S(1)}, bf16[4,256,256]{2,1,0:T(8,128)(2,1)}, u32[]{:S(2)}, u32[]{:S(2)}) collective-permute-start(bf16[4,256,256]{2,1,0:T(8,128)(2,1)S(1)} %pad_maximum_fusion.2.refs_5_.refs_4_), channel_id=1, source_target_pairs={{0,24},{8,16},{16,8},{24,0},{1,25},{9,17},{17,9},{25,1},{2,26},{10... | collective-permute-start | bytes 1572872 | tf_op jit(solution)/shard_map/ppermute | solution.py:39
  87.0 1.0 copy-start.3
  109.0 26.1 %copy-start.4 = (bf16[4,256,256]{2,1,0:T(8,128)(2,1)S(1)}, bf16[4,256,256]{2,1,0:T(8,128)(2,1)}, u32[]{:S(2)}) copy-start(bf16[4,256,256]{2,1,0:T(8,128)(2,1)} %copy-done.2) | copy-start | bytes 1572868
  118.9 15.0 %collective-permute-start.18 = (bf16[4,256,256]{2,1,0:T(8,128)(2,1)}, bf16[4,256,256]{2,1,0:T(8,128)(2,1)S(1)}, u32[]{:S(2)}, u32[]{:S(2)}) collective-permute-start(bf16[4,256,256]{2,1,0:T(8,128)(2,1)} %get-tuple-element.95), channel_id=1, source_target_pairs={{0,8},{8,0},{1,9},{9,1},{2,10},{10,2},{3,11},{11,3},{4,12},{12,4},... | collective-permute-start | bytes 1572872 | tf_op jit(solution)/shard_map/ppermute | solution.py:39
  121.6 23.7 %collective-permute-start.19 = (bf16[4,256,256]{2,1,0:T(8,128)(2,1)}, bf16[4,256,256]{2,1,0:T(8,128)(2,1)S(1)}, u32[]{:S(2)}, u32[]{:S(2)}) collective-permute-start(bf16[4,256,256]{2,1,0:T(8,128)(2,1)} %get-tuple-element.96), channel_id=1, source_target_pairs={{0,16},{16,0},{1,17},{17,1},{2,18},{18,2},{3,19},{19,3},{4,20},{20... | collective-permute-start | bytes 1572872 | tf_op jit(solution)/shard_map/ppermute | solution.py:39
  121.9 23.9 %collective-permute-start.20 = (bf16[4,256,256]{2,1,0:T(8,128)(2,1)}, bf16[4,256,256]{2,1,0:T(8,128)(2,1)S(1)}, u32[]{:S(2)}, u32[]{:S(2)}) collective-permute-start(bf16[4,256,256]{2,1,0:T(8,128)(2,1)} %get-tuple-element.97), channel_id=1, source_target_pairs={{0,24},{8,16},{16,8},{24,0},{1,25},{9,17},{17,9},{25,1},{2,26},{10... | collective-permute-start | bytes 1572872 | tf_op jit(solution)/shard_map/ppermute | solution.py:39
  122.5 23.6 %collective-permute-start.15 = (bf16[4,256,256]{2,1,0:T(8,128)(2,1)}, bf16[4,256,256]{2,1,0:T(8,128)(2,1)S(1)}, u32[]{:S(2)}, u32[]{:S(2)}) collective-permute-start(bf16[4,256,256]{2,1,0:T(8,128)(2,1)} %get-tuple-element.91), channel_id=1, source_target_pairs={{0,96},{32,0},{64,32},{96,64},{1,97},{33,1},{65,33},{97,65},{2,98}... | collective-permute-start | bytes 1572872 | tf_op jit(solution)/shard_map/ppermute | solution.py:39
  124.9 21.1 %collective-permute-start.16 = (bf16[4,256,256]{2,1,0:T(8,128)(2,1)}, bf16[4,256,256]{2,1,0:T(8,128)(2,1)S(1)}, u32[]{:S(2)}, u32[]{:S(2)}) collective-permute-start(bf16[4,256,256]{2,1,0:T(8,128)(2,1)} %get-tuple-element.92), channel_id=1, source_target_pairs={{0,64},{32,96},{64,0},{96,32},{1,65},{33,97},{65,1},{97,33},{2,66}... | collective-permute-start | bytes 1572872 | tf_op jit(solution)/shard_map/ppermute | solution.py:39
  133.9 11.9 %copy-start.8 = (bf16[4,256,256]{2,1,0:T(8,128)(2,1)S(1)}, bf16[4,256,256]{2,1,0:T(8,128)(2,1)}, u32[]{:S(2)}) copy-start(bf16[4,256,256]{2,1,0:T(8,128)(2,1)} %get-tuple-element.94) | copy-start | bytes 1572868
  133.9 17.4 %collective-permute-start.17 = (bf16[4,256,256]{2,1,0:T(8,128)(2,1)}, bf16[4,256,256]{2,1,0:T(8,128)(2,1)S(1)}, u32[]{:S(2)}, u32[]{:S(2)}) collective-permute-start(bf16[4,256,256]{2,1,0:T(8,128)(2,1)} %get-tuple-element.93), channel_id=1, source_target_pairs={{0,32},{32,64},{64,96},{96,0},{1,33},{33,65},{65,97},{97,1},{2,34}... | collective-permute-start | bytes 1572872 | tf_op jit(solution)/shard_map/ppermute | solution.py:39
  145.0 6.2 %copy-start.7 = (bf16[4,256,256]{2,1,0:T(8,128)(2,1)S(1)}, bf16[4,256,256]{2,1,0:T(8,128)(2,1)}, u32[]{:S(2)}) copy-start(bf16[4,256,256]{2,1,0:T(8,128)(2,1)} %get-tuple-element.90) | copy-start | bytes 1572868
  151.6 5.4 %collective-permute-start.21 = (bf16[256,256]{1,0:T(8,128)(2,1)S(1)}, bf16[256,256]{1,0:T(8,128)(2,1)S(1)}, u32[]{:S(2)}, u32[]{:S(2)}) collective-permute-start(bf16[256,256]{1,0:T(8,128)(2,1)S(1)} %get-tuple-element.150), channel_id=1, source_target_pairs={{0,8},{8,0},{1,9},{9,1},{2,10},{10,2},{3,11},{11,3},{4,12},{12,4},... | collective-permute-start | bytes 393224 | tf_op jit(solution)/shard_map/ppermute | solution.py:39
  154.1 5.8 %collective-permute-start.22 = (bf16[256,256]{1,0:T(8,128)(2,1)S(1)}, bf16[256,256]{1,0:T(8,128)(2,1)S(1)}, u32[]{:S(2)}, u32[]{:S(2)}) collective-permute-start(bf16[256,256]{1,0:T(8,128)(2,1)S(1)} %get-tuple-element.149), channel_id=1, source_target_pairs={{0,16},{16,0},{1,17},{17,1},{2,18},{18,2},{3,19},{19,3},{4,20},{20... | collective-permute-start | bytes 393224 | tf_op jit(solution)/shard_map/ppermute | solution.py:39
  154.3 17.8 %copy-start.11 = (bf16[1024,256]{1,0:T(8,128)(2,1)S(1)}, bf16[1024,256]{1,0:T(8,128)(2,1)}, u32[]{:S(2)}) copy-start(bf16[1024,256]{1,0:T(8,128)(2,1)} %get-tuple-element.113) | copy-start | bytes 1572868
  154.3 6.5 %collective-permute-start.23 = (bf16[256,256]{1,0:T(8,128)(2,1)S(1)}, bf16[256,256]{1,0:T(8,128)(2,1)S(1)}, u32[]{:S(2)}, u32[]{:S(2)}) collective-permute-start(bf16[256,256]{1,0:T(8,128)(2,1)S(1)} %get-tuple-element.148), channel_id=1, source_target_pairs={{0,24},{8,16},{16,8},{24,0},{1,25},{9,17},{17,9},{25,1},{2,26},{10... | collective-permute-start | bytes 393224 | tf_op jit(solution)/shard_map/ppermute | solution.py:39
  155.0 5.9 %collective-permute-start.24 = (bf16[256,256]{1,0:T(8,128)(2,1)S(1)}, bf16[256,256]{1,0:T(8,128)(2,1)S(1)}, u32[]{:S(2)}, u32[]{:S(2)}) collective-permute-start(bf16[256,256]{1,0:T(8,128)(2,1)S(1)} %get-tuple-element.146), channel_id=1, source_target_pairs={{0,96},{32,0},{64,32},{96,64},{1,97},{33,1},{65,33},{97,65},{2,98}... | collective-permute-start | bytes 393224 | tf_op jit(solution)/shard_map/ppermute | solution.py:39
  155.1 5.8 %collective-permute-start.25 = (bf16[256,256]{1,0:T(8,128)(2,1)S(1)}, bf16[256,256]{1,0:T(8,128)(2,1)S(1)}, u32[]{:S(2)}, u32[]{:S(2)}) collective-permute-start(bf16[256,256]{1,0:T(8,128)(2,1)S(1)} %get-tuple-element.145), channel_id=1, source_target_pairs={{0,64},{32,96},{64,0},{96,32},{1,65},{33,97},{65,1},{97,33},{2,66}... | collective-permute-start | bytes 393224 | tf_op jit(solution)/shard_map/ppermute | solution.py:39
  157.0 5.6 %collective-permute-start.26 = (bf16[256,256]{1,0:T(8,128)(2,1)S(1)}, bf16[256,256]{1,0:T(8,128)(2,1)S(1)}, u32[]{:S(2)}, u32[]{:S(2)}) collective-permute-start(bf16[256,256]{1,0:T(8,128)(2,1)S(1)} %get-tuple-element.144), channel_id=1, source_target_pairs={{0,32},{32,64},{64,96},{96,0},{1,33},{33,65},{65,97},{97,1},{2,34}... | collective-permute-start | bytes 393224 | tf_op jit(solution)/shard_map/ppermute | solution.py:39
  166.5 20.5 %collective-permute-start.27 = (bf16[128,4096]{1,0:T(8,128)(2,1)}, bf16[128,4096]{1,0:T(8,128)(2,1)S(1)}, u32[]{:S(2)}, u32[]{:S(2)}) collective-permute-start(bf16[128,4096]{1,0:T(8,128)(2,1)} %get-tuple-element.104.grad_ref), channel_id=1, source_target_pairs={{1,0},{2,1},{3,2},{4,3},{5,4},{6,5},{7,6},{8,7},{9,8},{10,9},{11,1... | collective-permute-start | bytes 3145736 | tf_op jit(solution)/shard_map/ppermute | solution.py:27
  172.1 14.9 %collective-permute-start.28 = (bf16[1024,256]{1,0:T(8,128)(2,1)S(1)}, bf16[1024,256]{1,0:T(8,128)(2,1)S(1)}, u32[]{:S(2)}, u32[]{:S(2)}) collective-permute-start(bf16[1024,256]{1,0:T(8,128)(2,1)S(1)} %copy-done.11), channel_id=1, source_target_pairs={{0,8},{8,0},{1,9},{9,1},{2,10},{10,2},{3,11},{11,3},{4,12},{12,4},... | collective-permute-start | bytes 1572872 | tf_op jit(solution)/shard_map/ppermute | solution.py:39
  199.0 13.7 %collective-permute-start.30 = (f32[64,8,128]{2,1,0:T(8,128)S(1)}, f32[64,8,128]{2,1,0:T(8,128)S(1)}, u32[]{:S(2)}, u32[]{:S(2)}) collective-permute-start(f32[64,8,128]{2,1,0:T(8,128)S(1)} %get-tuple-element.126), channel_id=1, source_target_pairs={{0,1},{1,0},{2,3},{3,2},{4,5},{5,4},{6,7},{7,6},{8,9},{9,8},{10,11... | collective-permute-start | bytes 786440 | tf_op jit(solution)/shard_map/ppermute | solution.py:39
  212.8 6.3 %collective-permute-start.31 = (f32[16,8,128]{2,1,0:T(8,128)S(1)}, f32[16,8,128]{2,1,0:T(8,128)S(1)}, u32[]{:S(2)}, u32[]{:S(2)}) collective-permute-start(f32[16,8,128]{2,1,0:T(8,128)S(1)} %get-tuple-element.152), channel_id=1, source_target_pairs={{0,2},{2,4},{4,6},{6,0},{1,3},{3,5},{5,7},{7,1},{8,10},{10,12},{12... | collective-permute-start | bytes 196616 | tf_op jit(solution)/shard_map/ppermute | solution.py:39
  212.9 6.3 %collective-permute-start.32 = (f32[16,8,128]{2,1,0:T(8,128)S(1)}, f32[16,8,128]{2,1,0:T(8,128)S(1)}, u32[]{:S(2)}, u32[]{:S(2)}) collective-permute-start(f32[16,8,128]{2,1,0:T(8,128)S(1)} %get-tuple-element.154), channel_id=1, source_target_pairs={{0,4},{2,6},{4,0},{6,2},{1,5},{3,7},{5,1},{7,3},{8,12},{10,14},{12... | collective-permute-start | bytes 196616 | tf_op jit(solution)/shard_map/ppermute | solution.py:39
  213.0 6.2 %collective-permute-start.33 = (f32[16,8,128]{2,1,0:T(8,128)S(1)}, f32[16,8,128]{2,1,0:T(8,128)S(1)}, u32[]{:S(2)}, u32[]{:S(2)}) collective-permute-start(f32[16,8,128]{2,1,0:T(8,128)S(1)} %get-tuple-element.153), channel_id=1, source_target_pairs={{0,6},{2,0},{4,2},{6,4},{1,7},{3,1},{5,3},{7,5},{8,14},{10,8},{12,... | collective-permute-start | bytes 196616 | tf_op jit(solution)/shard_map/ppermute | solution.py:39
  215.6 7.0 %collective-permute-start.29 = (bf16[3,8,4096]{2,1,0:T(8,128)(2,1)S(1)}, bf16[3,8,4096]{2,1,0:T(8,128)(2,1)S(1)}, u32[]{:S(2)}, u32[]{:S(2)}) collective-permute-start(bf16[3,8,4096]{2,1,0:T(8,128)(2,1)S(1)} %get-tuple-element.120), channel_id=1, source_target_pairs={{1,0},{2,1},{3,2},{4,3},{5,4},{6,5},{7,6},{8,7},{9,8},{10,9},{11,1... | collective-permute-start | bytes 589832 | tf_op jit(solution)/shard_map/ppermute | solution.py:27
  219.2 6.5 %collective-permute-start.34 = (f32[16,8,128]{2,1,0:T(8,128)S(1)}, f32[16,8,128]{2,1,0:T(8,128)S(1)}, u32[]{:S(2)}, u32[]{:S(2)}) collective-permute-start(f32[16,8,128]{2,1,0:T(8,128)S(1)} %fusion.1), channel_id=1, source_target_pairs={{0,32},{32,64},{64,96},{96,0},{1,33},{33,65},{65,97},{97,1},{2,34}... | collective-permute-start | bytes 196616 | tf_op jit(solution)/shard_map/ppermute | solution.py:39
  219.3 6.5 %collective-permute-start.35 = (f32[16,8,128]{2,1,0:T(8,128)S(1)}, f32[16,8,128]{2,1,0:T(8,128)S(1)}, u32[]{:S(2)}, u32[]{:S(2)}) collective-permute-start(f32[16,8,128]{2,1,0:T(8,128)S(1)} %fusion.1), channel_id=1, source_target_pairs={{0,64},{32,96},{64,0},{96,32},{1,65},{33,97},{65,1},{97,33},{2,66}... | collective-permute-start | bytes 196616 | tf_op jit(solution)/shard_map/ppermute | solution.py:39
  220.6 5.1 %collective-permute-start.36 = (f32[16,8,128]{2,1,0:T(8,128)S(1)}, f32[16,8,128]{2,1,0:T(8,128)S(1)}, u32[]{:S(2)}, u32[]{:S(2)}) collective-permute-start(f32[16,8,128]{2,1,0:T(8,128)S(1)} %fusion.1), channel_id=1, source_target_pairs={{0,96},{32,0},{64,32},{96,64},{1,97},{33,1},{65,33},{97,65},{2,98}... | collective-permute-start | bytes 196616 | tf_op jit(solution)/shard_map/ppermute | solution.py:39
  225.7 14.6 %copy-start.6 = (bf16[1024,256]{1,0:T(8,128)(2,1)S(1)}, bf16[1024,256]{1,0:T(8,128)(2,1)}, u32[]{:S(2)}) copy-start(bf16[1024,256]{1,0:T(8,128)(2,1)} %get-tuple-element.88) | copy-start | bytes 1572868
  225.8 3.9 %collective-permute-start.37 = (f32[16,8,128]{2,1,0:T(8,128)S(1)}, f32[16,8,128]{2,1,0:T(8,128)S(1)}, u32[]{:S(2)}, u32[]{:S(2)}) collective-permute-start(f32[16,8,128]{2,1,0:T(8,128)S(1)} %add_add_fusion.1), channel_id=1, source_target_pairs={{0,16},{16,0},{1,17},{17,1},{2,18},{18,2},{3,19},{19,3},{4,20},{20... | collective-permute-start | bytes 196616 | tf_op jit(solution)/shard_map/ppermute | solution.py:39
  226.8 4.7 %collective-permute-start.38 = (f32[16,8,128]{2,1,0:T(8,128)S(1)}, f32[16,8,128]{2,1,0:T(8,128)S(1)}, u32[]{:S(2)}, u32[]{:S(2)}) collective-permute-start(f32[16,8,128]{2,1,0:T(8,128)S(1)} %add_add_fusion.1), channel_id=1, source_target_pairs={{0,8},{8,0},{1,9},{9,1},{2,10},{10,2},{3,11},{11,3},{4,12},{12,4},... | collective-permute-start | bytes 196616 | tf_op jit(solution)/shard_map/ppermute | solution.py:39
  226.8 5.2 %collective-permute-start.39 = (f32[16,8,128]{2,1,0:T(8,128)S(1)}, f32[16,8,128]{2,1,0:T(8,128)S(1)}, u32[]{:S(2)}, u32[]{:S(2)}) collective-permute-start(f32[16,8,128]{2,1,0:T(8,128)S(1)} %add_add_fusion.1), channel_id=1, source_target_pairs={{0,24},{8,16},{16,8},{24,0},{1,25},{9,17},{17,9},{25,1},{2,26},{10... | collective-permute-start | bytes 196616 | tf_op jit(solution)/shard_map/ppermute | solution.py:39
  232.1 5.1 %collective-permute-start.40 = (f32[16,8,128]{2,1,0:T(8,128)S(1)}, f32[16,8,128]{2,1,0:T(8,128)S(1)}, u32[]{:S(2)}, u32[]{:S(2)}) collective-permute-start(f32[16,8,128]{2,1,0:T(8,128)S(1)} %add_add_fusion), channel_id=1, source_target_pairs={{0,1},{1,0},{2,3},{3,2},{4,5},{5,4},{6,7},{7,6},{8,9},{9,8},{10,11... | collective-permute-start | bytes 196616 | tf_op jit(solution)/shard_map/ppermute | solution.py:39
  237.2 9.4 %collective-permute-start.41 = (f32[32,8,128]{2,1,0:T(8,128)S(1)}, f32[32,8,128]{2,1,0:T(8,128)S(1)}, u32[]{:S(2)}, u32[]{:S(2)}) collective-permute-start(f32[32,8,128]{2,1,0:T(8,128)S(1)} %pad_maximum_fusion.3.refs_0_), channel_id=1, source_target_pairs={{0,6},{2,0},{4,2},{6,4},{1,7},{3,1},{5,3},{7,5},{8,14},{10,8},{12,... | collective-permute-start | bytes 393224 | tf_op jit(solution)/shard_map/ppermute | solution.py:39
  239.6 7.0 %collective-permute-start.42 = (f32[32,8,128]{2,1,0:T(8,128)S(1)}, f32[32,8,128]{2,1,0:T(8,128)S(1)}, u32[]{:S(2)}, u32[]{:S(2)}) collective-permute-start(f32[32,8,128]{2,1,0:T(8,128)S(1)} %pad_maximum_fusion.3.refs_0_), channel_id=1, source_target_pairs={{0,4},{2,6},{4,0},{6,2},{1,5},{3,7},{5,1},{7,3},{8,12},{10,14},{12... | collective-permute-start | bytes 393224 | tf_op jit(solution)/shard_map/ppermute | solution.py:39
  239.6 9.2 %collective-permute-start.43 = (f32[32,8,128]{2,1,0:T(8,128)S(1)}, f32[32,8,128]{2,1,0:T(8,128)S(1)}, u32[]{:S(2)}, u32[]{:S(2)}) collective-permute-start(f32[32,8,128]{2,1,0:T(8,128)S(1)} %pad_maximum_fusion.3.refs_0_), channel_id=1, source_target_pairs={{0,2},{2,4},{4,6},{6,0},{1,3},{3,5},{5,7},{7,1},{8,10},{10,12},{12... | collective-permute-start | bytes 393224 | tf_op jit(solution)/shard_map/ppermute | solution.py:39
Sparse Core Ops, SparseCore 0:
  48.9 60.0 all-gather.1
  111.3 51.5 reduce-scatter.1

commit v10 on v9

--- a/solution.py
+++ b/solution.py
@@ -78,7 +78,7 @@
 
 
 def extend(ext, rim, rows_of, at):
-    ext[0:RIM, :] = rim[:, at].astype(F32)
+    ext[0:RIM, :] = jnp.zeros((RIM, LANES), F32) if rim is None else rim[:, at].astype(F32)
     ext[RIM:, :] = rows_of.astype(F32)
 
 
@@ -87,7 +87,7 @@
 
     def filtered(part, block, at):
         own = ext.at[(3 * block + part) % ext.shape[0]]
-        extend(own, rims[part], tokens[part][:, at], at)
+        extend(own, rims and rims[part], tokens[part][:, at], at)
         taps = filters[part][:, at]
         total = taps[0:1] * own[RIM : RIM + rows, :]
         for tap in range(1, short_taps):
@@ -103,34 +103,42 @@
         mixer_ref[:, at] = (key * value).astype(BF16)
 
 
-def features_call(tokens, rim, filters):
+def features_call(tokens, filters, rim=None, given=None):
     rows, wide = tokens.shape
     channels = wide // 3
     taps = filters.shape[0]
-    width = block_width(channels, WIDTH)
+    rows = rows if given is None else 2 * RIM
+    width = channels if given else block_width(channels, WIDTH)
     steps = channels // width
 
     def spec(height, part):
         return pl.BlockSpec((height, width), lambda i, part=part: (0, i + part * steps))
 
+    held = [] if given is None else [rim] * 3
+    olds = [] if given is None else list(given)
+
     def body(*refs):
-        features_kernel(taps, refs[0:3], refs[3:6], refs[6:9], *refs[9:])
-
-    out = jax.ShapeDtypeStruct((rows, channels), BF16)
+        n = 3 + len(held)
+        rims = refs[3:n] if held else None
+        features_kernel(taps, refs[0:3], rims, refs[n : n + 3], *refs[n + 3 + len(olds) :])
+
+    out = jax.ShapeDtypeStruct((tokens.shape[0], channels), BF16)
     return hbm_call(
         body,
-        loose=(3, 4, 5),
+        loose=(3, 4, 5) if held else (),
         grid=(steps,),
         in_specs=[spec(rows, p) for p in range(3)]
-        + [spec(RIM, p) for p in range(3)]
-        + [spec(taps, p) for p in range(3)],
+        + [spec(RIM, p) for p in range(len(held))]
+        + [spec(taps, p) for p in range(3)]
+        + [pl.BlockSpec(memory_space=pl.ANY)] * len(olds),
         out_specs=[pl.BlockSpec((rows, width), lambda i: (0, i))] * 4,
         out_shape=[out] * 4,
+        input_output_aliases={9 + i: i for i in range(len(olds))},
         scratch_shapes=[pltpu.VMEM((6, RIM + rows, LANES), F32)],
         compiler_params=params(),
         cost_estimate=cost(0, rows * wide),
-        name="features",
-    )(tokens, tokens, tokens, rim, rim, rim, filters, filters, filters)
+        name="features" if given is None else "first_rows",
+    )(*[tokens] * 3, *held, *[filters] * 3, *olds)
 
 
 def lane_row(shape):
@@ -696,7 +704,9 @@
 
     rim = along(tokens[rows - RIM :], 1)
     lines = long_filter.astype(F32)
-    query, key, value, mixer = features_call(tokens, rim, short_filter)
+    parts = features_call(tokens, short_filter)
+    parts, rim = lax.optimization_barrier((parts, rim))
+    query, key, value, mixer = features_call(tokens, short_filter, rim, parts)
     mixer, out_weight = lax.optimization_barrier((mixer, out_weight))
     mixer_prev = along(mixer, 1)
     wide_top = gather_wide(out_weight)
@@ -725,12 +735,13 @@
     )
     grad_weight = jnp.concatenate([added(top), added(bottom)], axis=1).T
     theirs = move(other, xh=1)
-    grad_next, grad_weight, theirs = lax.optimization_barrier((grad_next, grad_weight, theirs))
-    output = jnp.where(xh == 0, jnp.concatenate([own, theirs], axis=0), jnp.concatenate([theirs, own], axis=0))
+    grad_next, grad_weight = lax.optimization_barrier((grad_next, grad_weight))
     other_grads, key_sum, value_sum, edge = unmix_call(
         lines, short_taps, grad_mixed, grad_next, key, value, tokens, rim, query_grad
     )
+    edge, key_sum, theirs = lax.optimization_barrier((edge, key_sum, theirs))
     edge = along(edge, -1)
+    output = jnp.where(xh == 0, jnp.concatenate([own, theirs], axis=0), jnp.concatenate([theirs, own], axis=0))
     grad_tokens = short_adjoint_call(query_grad[None], edge, short_filter, 0, None)
     grad_short, grad_long, grad_tokens = total_over_devices(
         spread_to, collect_from, query_sum, key_sum, value_sum, long_sum, short_taps, grad_tokens

time: 258 us -> 262 us (1.016)
  waiting for transfers between devices: 73.2 us -> 82 us
  starting transfers between devices: 80.5 us -> 74 us
    reduce_scatter x1, waiting for transfers between devices: 0.26 us -> 13.5 us  [shards(): lax.psum_scatter(partial, ('z', 'c'), scatter_dimension=0, tiled=True)]
    ppermute x4, starting transfers between devices: 17.7 us -> 12.7 us  [along(): return lax.ppermute(x, LINE, pairs)]
    ppermute x40, waiting for transfers between devices: 54.6 us -> 50.6 us  [move(): return lax.ppermute(x, axes, pairs)]
    ppermute x4, waiting for transfers between devices: 6 us -> 3.31 us  [along(): return lax.ppermute(x, LINE, pairs)]
    pallas_call x10 -> x11, Pallas kernels: 77.4 us -> 79.7 us  [run(): return call(*held)]
  transfers between devices with their start and end apart: 46 -> 46, of which waited for: 28 -> 26; matrix products, arithmetic and copies ran while one was open for 3% -> 3% of each run, Pallas kernels for 18% -> 24%
where the time goes in v10:
time: 262 us
  waiting for transfers between devices  82 us (31%)
  Pallas kernels  81.9 us (31%)
  starting transfers between devices  74 us (28%)
  between operations  14.4 us (5%)
  local copies, waits for them, and re-layouts  6.15 us (2%)
  other arithmetic  3.34 us (1%)
    pallas_call x11, Pallas kernels, run(): return call(*held)  79.7 us
    ppermute x40, starting transfers between devices, move(): return lax.ppermute(x, axes, pairs)  61.1 us
    ppermute x40, waiting for transfers between devices, move(): return lax.ppermute(x, axes, pairs)  50.6 us
    all_gather x1, waiting for transfers between devices, shards(): all_rows = lax.all_gather(gated, ('z', 'c'), axis=0, tiled=True)  14.4 us
    reduce_scatter x1, waiting for transfers between devices, shards(): lax.psum_scatter(partial, ('z', 'c'), scatter_dimension=0, tiled=True)  13.5 us
    ppermute x4, starting transfers between devices, along(): return lax.ppermute(x, LINE, pairs)  12.7 us
  transfers between devices with their start and end apart: 46, of which 26 were waited for; matrix products, arithmetic and copies ran while one was open for 3% of the time, Pallas kernels for 24%

profile of v10, /device:TPU:1, one launch (start us, length us, event | category | flops | bytes accessed | tf_op | source)
XLA Modules:
  0.0 261.7 jit_solution(100758862176923796)
XLA Ops:
  7.2 0.9 slice_bitcast_fusion
  8.2 4.9 %collective-permute-start = (bf16[8,12288]{1,0:T(8,128)(2,1)S(1)}, bf16[8,12288]{1,0:T(8,128)(2,1)S(1)}, u32[]{:S(2)}, u32[]{:S(2)}) collective-permute-start(bf16[8,12288]{1,0:T(8,128)(2,1)S(1)} %slice_bitcast_fusion), channel_id=1, source_target_pairs={{0,1},{1,2},{2,3},{3,4},{4,5},{5,6},{6,7},{7,8},{8,9},{9,10},{10,1... | collective-permute-start | bytes 589832 | tf_op jit(solution)/shard_map/ppermute | solution.py:27
  13.1 6.7 %features.1 = (bf16[128,4096]{1,0:T(8,128)(2,1)}, bf16[128,4096]{1,0:T(8,128)(2,1)}, bf16[128,4096]{1,0:T(8,128)(2,1)}, bf16[128,4096]{1,0:T(8,128)(2,1)}) custom-call(bf16[128,12288]{1,0:T(8,128)(2,1)} %bitcast.37, bf16[128,12288]{1,0:T(8,128)(2,1)} %bitcast.38, bf16[128,12288]{1,0:T(8,128)(2,1)} %bitcast.39, f32[7,12288]{1,0:T(8,128)} %filter_ref.3, ...), custom_call_target="tpu_custom_call" | custom-call | bytes 1572864 | tf_op jit(solution)/shard_map/features/pallas_call | solution.py:64
  19.9 2.6 first_rows.1
  22.4 1.9 collective-permute-start.1
  24.4 2.8 %collective-permute-start.2 = (bf16[256,256]{1,0:T(8,128)(2,1)S(1)}, bf16[256,256]{1,0:T(8,128)(2,1)S(1)}, u32[]{:S(2)}, u32[]{:S(2)}) collective-permute-start(bf16[256,256]{1,0:T(8,128)(2,1)S(1)} %slice.56), channel_id=1, source_target_pairs={{0,8},{8,0},{1,9},{9,1},{2,10},{10,2},{3,11},{11,3},{4,12},{12,4},... | collective-permute-start | bytes 393224 | tf_op jit(solution)/shard_map/ppermute | solution.py:39
  28.1 2.4 collective-permute-done.2
  30.5 3.0 %collective-permute-done.3 = bf16[256,256]{1,0:T(8,128)(2,1)S(1)} collective-permute-done((bf16[256,256]{1,0:T(8,128)(2,1)S(1)}, bf16[256,256]{1,0:T(8,128)(2,1)S(1)}, u32[]{:S(2)}, u32[]{:S(2)}) %collective-permute-start.3) | collective-permute-done | bytes 131104 | tf_op jit(solution)/shard_map/ppermute | solution.py:39
  33.7 2.7 %collective-permute-done.1.prev_ref = bf16[128,4096]{1,0:T(8,128)(2,1)S(1)} collective-permute-done((bf16[128,4096]{1,0:T(8,128)(2,1)}, bf16[128,4096]{1,0:T(8,128)(2,1)S(1)}, u32[]{:S(2)}, u32[]{:S(2)}) %collective-permute-start.1) | collective-permute-done | bytes 1048608 | tf_op jit(solution)/shard_map/ppermute | solution.py:27
  36.4 9.8 %mix.1 = (bf16[128,4096]{1,0:T(8,128)(2,1)}, bf16[128,4096]{1,0:T(8,128)(2,1)}) custom-call(f32[256,128]{1,0:T(8,128)S(1)} %convert_element_type.57.lines_ref, bf16[128,4096]{1,0:T(8,128)(2,1)S(1)} %collective-permute-done.1.prev_ref, bf16[128,4096]{1,0:T(8,128)(2,1)} %get-tuple-element.91.cur_ref, bf16[128,4096]{1,0:T(8,128)(2,1)} %get-tuple-element.94.query_ref), custom_call_target="tpu_custom_call" | custom-call | bytes 1048576 | tf_op jit(solution)/shard_map/mix/pallas_call | solution.py:64
  47.0 1.4 collective-permute-start.6
  48.4 2.8 %collective-permute-start.5 = (bf16[1024,256]{0,1:T(8,128)(2,1)S(1)}, bf16[1024,256]{0,1:T(8,128)(2,1)S(1)}, u32[]{:S(2)}, u32[]{:S(2)}) collective-permute-start(bf16[1024,256]{0,1:T(8,128)(2,1)S(1)} %get-tuple-element.165), channel_id=1, source_target_pairs={{0,8},{8,0},{1,9},{9,1},{2,10},{10,2},{3,11},{11,3},{4,12},{12,4},... | collective-permute-start | bytes 1572872 | tf_op jit(solution)/shard_map/ppermute | solution.py:39
  51.3 1.5 collective-permute-start.11
  52.8 2.6 %collective-permute-start.10 = (bf16[256,256]{1,0:T(8,128)(2,1)S(1)}, bf16[256,256]{1,0:T(8,128)(2,1)S(1)}, u32[]{:S(2)}, u32[]{:S(2)}) collective-permute-start(bf16[256,256]{1,0:T(8,128)(2,1)S(1)} %get-tuple-element.178), channel_id=1, source_target_pairs={{0,64},{32,96},{64,0},{96,32},{1,65},{33,97},{65,1},{97,33},{2,66}... | collective-permute-start | bytes 393224 | tf_op jit(solution)/shard_map/ppermute | solution.py:39
  55.5 2.6 %collective-permute-start.7 = (bf16[4,256,256]{2,1,0:T(8,128)(2,1)S(1)}, bf16[4,256,256]{2,1,0:T(8,128)(2,1)}, u32[]{:S(2)}, u32[]{:S(2)}) collective-permute-start(bf16[4,256,256]{2,1,0:T(8,128)(2,1)S(1)} %pad_maximum_fusion.1.refs_1_.refs_0_), channel_id=1, source_target_pairs={{0,64},{32,96},{64,0},{96,32},{1,65},{33,97},{65,1},{97,33},{2,66}... | collective-permute-start | bytes 1572872 | tf_op jit(solution)/shard_map/ppermute | solution.py:39
  58.1 4.8 %collective-permute-done.9 = bf16[256,256]{1,0:T(8,128)(2,1)S(1)} collective-permute-done((bf16[256,256]{1,0:T(8,128)(2,1)S(1)}, bf16[256,256]{1,0:T(8,128)(2,1)S(1)}, u32[]{:S(2)}, u32[]{:S(2)}) %collective-permute-start.9) | collective-permute-done | bytes 131104 | tf_op jit(solution)/shard_map/ppermute | solution.py:39
  62.9 1.5 collective-permute-start.8
  64.4 1.1 collective-permute-done.10
  67.0 2.8 %collective-permute-start.14 = (bf16[4,256,256]{2,1,0:T(8,128)(2,1)S(1)}, bf16[4,256,256]{2,1,0:T(8,128)(2,1)}, u32[]{:S(2)}, u32[]{:S(2)}) collective-permute-start(bf16[4,256,256]{2,1,0:T(8,128)(2,1)S(1)} %pad_maximum_fusion.2.refs_5_.refs_4_), channel_id=1, source_target_pairs={{0,24},{8,16},{16,8},{24,0},{1,25},{9,17},{17,9},{25,1},{2,26},{10... | collective-permute-start | bytes 1572872 | tf_op jit(solution)/shard_map/ppermute | solution.py:39
  69.7 1.1 fusion.11
  70.9 1.5 copy.16.refs_0_
  72.4 2.8 %collective-permute-done.7.refs_3_.refs_2_ = bf16[4,256,256]{2,1,0:T(8,128)(2,1)} collective-permute-done((bf16[4,256,256]{2,1,0:T(8,128)(2,1)S(1)}, bf16[4,256,256]{2,1,0:T(8,128)(2,1)}, u32[]{:S(2)}, u32[]{:S(2)}) %collective-permute-start.7) | collective-permute-done | bytes 524320 | tf_op jit(solution)/shard_map/ppermute | solution.py:39
  75.1 4.0 %collective-permute-done.8.refs_4_.refs_3_ = bf16[4,256,256]{2,1,0:T(8,128)(2,1)} collective-permute-done((bf16[4,256,256]{2,1,0:T(8,128)(2,1)S(1)}, bf16[4,256,256]{2,1,0:T(8,128)(2,1)}, u32[]{:S(2)}, u32[]{:S(2)}) %collective-permute-start.8) | collective-permute-done | bytes 524320 | tf_op jit(solution)/shard_map/ppermute | solution.py:39
  79.8 3.1 %collective-permute-done.14.refs_8_.refs_7_ = bf16[4,256,256]{2,1,0:T(8,128)(2,1)} collective-permute-done((bf16[4,256,256]{2,1,0:T(8,128)(2,1)S(1)}, bf16[4,256,256]{2,1,0:T(8,128)(2,1)}, u32[]{:S(2)}, u32[]{:S(2)}) %collective-permute-start.14) | collective-permute-done | bytes 524320 | tf_op jit(solution)/shard_map/ppermute | solution.py:39
  82.9 1.1 copy-done.3
  83.9 8.5 %gate_matmul.1 = bf16[1024,4096]{1,0:T(8,128)(2,1)} custom-call(bf16[1024,512]{1,0:T(8,128)(2,1)S(1)} %copy.16.refs_0_, bf16[4,256,256]{2,1,0:T(8,128)(2,1)S(1)} %pad_maximum_fusion.1.refs_1_.refs_0_, bf16[4,256,256]{2,1,0:T(8,128)(2,1)S(1)} %copy-done.3, bf16[4,256,256]{2,1,0:T(8,128)(2,1)} %collective-permute-done.7.refs_3_.refs_2_, ...), custom_call_target="tpu_custom_call" | custom-call | flops 4294967296 | bytes 12582912 | tf_op jit(solution)/shard_map/gate_matmul/pallas_call | solution.py:64
  92.4 14.4 %all-gather.2.cloned.1.call-done.rows_ref = bf16[1024,4096]{1,0:T(8,128)(2,1)} async-done(((bf16[128,4096]{1,0:T(8,128)(2,1)}), bf16[1024,4096]{1,0:T(8,128)(2,1)}) %all-gather.2.cloned.1.call-update) | async-done | bytes 8388624 | tf_op jit(solution)/shard_map/all_gather | solution.py:717
  106.9 9.9 %weight_grad.1 = (bf16[4,256,256]{2,1,0:T(8,128)(2,1)}, bf16[4,256,256]{2,1,0:T(8,128)(2,1)}, bf16[4,256,256]{2,1,0:T(8,128)(2,1)}, bf16[4,256,256]{2,1,0:T(8,12...) custom-call(s32[8]{0:T(128)S(1)} %fusion.2.origin.place, ...), custom_call_target="tpu_custom_call" | custom-call | flops 4294967296 | bytes 12582912 | tf_op jit(solution)/shard_map/weight_grad/pallas_call | solution.py:64
  116.8 2.7 %collective-permute-start.18 = (bf16[4,256,256]{2,1,0:T(8,128)(2,1)}, bf16[4,256,256]{2,1,0:T(8,128)(2,1)S(1)}, u32[]{:S(2)}, u32[]{:S(2)}) collective-permute-start(bf16[4,256,256]{2,1,0:T(8,128)(2,1)} %get-tuple-element.115), channel_id=1, source_target_pairs={{0,8},{8,0},{1,9},{9,1},{2,10},{10,2},{3,11},{11,3},{4,12},{12,4},... | collective-permute-start | bytes 1572872 | tf_op jit(solution)/shard_map/ppermute | solution.py:39
  120.4 2.5 collective-permute-start.15
  123.4 8.5 %collective-permute-done.18 = bf16[4,256,256]{2,1,0:T(8,128)(2,1)S(1)} collective-permute-done((bf16[4,256,256]{2,1,0:T(8,128)(2,1)}, bf16[4,256,256]{2,1,0:T(8,128)(2,1)S(1)}, u32[]{:S(2)}, u32[]{:S(2)}) %collective-permute-start.18) | collective-permute-done | bytes 524320 | tf_op jit(solution)/shard_map/ppermute | solution.py:39
  131.8 1.2 collective-permute-start.17
  133.1 9.8 %output.1 = (bf16[1024,256]{1,0:T(8,128)(2,1)}, bf16[1024,256]{1,0:T(8,128)(2,1)}) custom-call(s32[8]{0:T(128)S(1)} %fusion.2.origin.place, bf16[1024,4096]{1,0:T(8,128)(2,1)} %all-gather.2.cloned.1.call-done.rows_ref, bf16[4,256,256]{2,1,0:T(8,128)(2,1)S(1)} %pad_maximum_fusion.1.refs_1_.refs_0_, bf16[4,256,256]{2,1,0:T(8,128)(2,1)S(1)} %copy-done.4, ...), custom_call_target="tpu_custom_call" | custom-call | flops 4294967296 | bytes 12582912 | tf_op jit(solution)/shard_map/output/pallas_call | solution.py:64
  144.0 5.2 %collective-permute-done.17 = bf16[4,256,256]{2,1,0:T(8,128)(2,1)S(1)} collective-permute-done((bf16[4,256,256]{2,1,0:T(8,128)(2,1)}, bf16[4,256,256]{2,1,0:T(8,128)(2,1)S(1)}, u32[]{:S(2)}, u32[]{:S(2)}) %collective-permute-start.17) | collective-permute-done | bytes 524320 | tf_op jit(solution)/shard_map/ppermute | solution.py:39
  149.5 2.5 collective-permute-start.21
  153.2 1.7 collective-permute-done.21
  154.9 2.8 %collective-permute-done.22 = bf16[256,256]{1,0:T(8,128)(2,1)S(1)} collective-permute-done((bf16[256,256]{1,0:T(8,128)(2,1)S(1)}, bf16[256,256]{1,0:T(8,128)(2,1)S(1)}, u32[]{:S(2)}, u32[]{:S(2)}) %collective-permute-start.22) | collective-permute-done | bytes 131104 | tf_op jit(solution)/shard_map/ppermute | solution.py:39
  157.8 1.1 collective-permute-done.23
  158.9 1.8 collective-permute-done.26
  160.7 13.5 %reduce-scatter.2.cloned.1.call-done.gate_grad_ref = bf16[128,4096]{1,0:T(8,128)(2,1)} async-done(((bf16[1024,4096]{1,0:T(8,128)(2,1)}), bf16[128,4096]{1,0:T(8,128)(2,1)}) %reduce-scatter.2.cloned.1.call-update) | async-done | bytes 1048592 | tf_op jit(solution)/shard_map/reduce_scatter | solution.py:724
  174.2 3.6 %gate_back.1 = (bf16[128,4096]{1,0:T(8,128)(2,1)}, bf16[128,4096]{1,0:T(8,128)(2,1)}) custom-call(s32[8]{0:T(128)S(1)} %fusion.2.origin.place, bf16[128,4096]{1,0:T(8,128)(2,1)} %reduce-scatter.2.cloned.1.call-done.gate_grad_ref, bf16[128,4096]{1,0:T(8,128)(2,1)} %get-tuple-element.94.query_ref, bf16[128,4096]{1,0:T(8,128)(2,1)} %get-tuple-element.123.mixed_ref), custom_call_target="tpu_custom_call" | custom-call | flops 1048576 | bytes 5242880 | tf_op jit(solution)/shard_map/gate_back/pallas_call | solution.py:64
  177.8 3.3 %collective-permute-start.27 = (bf16[128,4096]{1,0:T(8,128)(2,1)}, bf16[128,4096]{1,0:T(8,128)(2,1)S(1)}, u32[]{:S(2)}, u32[]{:S(2)}) collective-permute-start(bf16[128,4096]{1,0:T(8,128)(2,1)} %get-tuple-element.124.grad_ref), channel_id=1, source_target_pairs={{1,0},{2,1},{3,2},{4,3},{5,4},{6,5},{7,6},{8,7},{9,8},{10,9},{11,1... | collective-permute-start | bytes 3145736 | tf_op jit(solution)/shard_map/ppermute | solution.py:27
  181.1 3.0 %collective-permute-start.28 = (bf16[1024,256]{1,0:T(8,128)(2,1)S(1)}, bf16[1024,256]{1,0:T(8,128)(2,1)S(1)}, u32[]{:S(2)}, u32[]{:S(2)}) collective-permute-start(bf16[1024,256]{1,0:T(8,128)(2,1)S(1)} %copy-done.11), channel_id=1, source_target_pairs={{0,8},{8,0},{1,9},{9,1},{2,10},{10,2},{3,11},{11,3},{4,12},{12,4},... | collective-permute-start | bytes 1572872 | tf_op jit(solution)/shard_map/ppermute | solution.py:39
  184.3 9.1 %long_grad.1 = (f32[256,128]{1,0:T(8,128)S(1)}, f32[8,4096]{1,0:T(8,128)S(1)}) custom-call(bf16[128,4096]{1,0:T(8,128)(2,1)} %copy-done.1, bf16[128,4096]{1,0:T(8,128)(2,1)} %get-tuple-element.91.cur_ref, bf16[128,4096]{1,0:T(8,128)(2,1)} %get-tuple-element.124.grad_ref, bf16[128,4096]{1,0:T(8,128)(2,1)} %get-tuple-element.136.query_grad_ref.feature_ref, ...), custom_call_target="tpu_custom_call" | custom-call | flops 2147483648 | bytes 5242880 | tf_op jit(solution)/shard_map/long_grad/pallas_call | solution.py:64
  194.1 11.4 %unmix.1 = (bf16[2,128,4096]{2,1,0:T(8,128)(2,1)}, f32[8,4096]{1,0:T(8,128)S(1)}, f32[8,4096]{1,0:T(8,128)S(1)}, bf16[3,8,4096]{2,1,0:T(8,128)(2,1)S(1)}) custom-call(f32[256,128]{1,0:T(8,128)S(1)} %convert_element_type.57.lines_ref, bf16[128,4096]{1,0:T(8,128)(2,1)} %get-tuple-element.124.grad_ref, bf16[128,4096]{1,0:T(8,128)(2,1)S(1)} %collective-permute-done.27.next_ref, ...), custom_call_target="tpu_custom_call" | custom-call | flops 2147483648 | bytes 8388608 | tf_op jit(solution)/shard_map/unmix/pallas_call | solution.py:64
  206.2 4.3 %collective-permute-start.30 = (f32[64,8,128]{2,1,0:T(8,128)S(1)}, f32[64,8,128]{2,1,0:T(8,128)S(1)}, u32[]{:S(2)}, u32[]{:S(2)}) collective-permute-start(f32[64,8,128]{2,1,0:T(8,128)S(1)} %get-tuple-element.148), channel_id=1, source_target_pairs={{0,1},{1,0},{2,3},{3,2},{4,5},{5,4},{6,7},{7,6},{8,9},{9,8},{10,11... | collective-permute-start | bytes 786440 | tf_op jit(solution)/shard_map/ppermute | solution.py:39
  210.5 1.2 collective-permute-done.30
  211.8 7.8 %collective-permute-start.32 = (f32[16,8,128]{2,1,0:T(8,128)S(1)}, f32[16,8,128]{2,1,0:T(8,128)S(1)}, u32[]{:S(2)}, u32[]{:S(2)}) collective-permute-start(f32[16,8,128]{2,1,0:T(8,128)S(1)} %get-tuple-element.176), channel_id=1, source_target_pairs={{0,4},{2,6},{4,0},{6,2},{1,5},{3,7},{5,1},{7,3},{8,12},{10,14},{12... | collective-permute-start | bytes 196616 | tf_op jit(solution)/shard_map/ppermute | solution.py:39
  219.6 2.6 collective-permute-start.29
  222.3 0.9 collective-permute-done.32
  223.1 1.3 collective-permute-start.34
  224.4 2.4 collective-permute-start.35
  226.9 1.2 collective-permute-start.36
  228.0 3.2 %short_adjoint.2.refs_0_ = bf16[128,12288]{1,0:T(8,128)(2,1)} custom-call(bf16[1,128,4096]{2,1,0:T(8,128)(2,1)} %bitcast.47, bf16[3,8,4096]{2,1,0:T(8,128)(2,1)S(1)} %collective-permute-done.29.rim_ref, f32[7,12288]{1,0:T(8,128)} %filter_ref.3), custom_call_target="tpu_custom_call" | custom-call | flops 7340032 | bytes 2097152 | tf_op jit(solution)/shard_map/short_adjoint/pallas_call | solution.py:64
  231.3 1.3 collective-permute-start.37
  232.5 2.7 %collective-permute-start.39 = (f32[16,8,128]{2,1,0:T(8,128)S(1)}, f32[16,8,128]{2,1,0:T(8,128)S(1)}, u32[]{:S(2)}, u32[]{:S(2)}) collective-permute-start(f32[16,8,128]{2,1,0:T(8,128)S(1)} %add_add_fusion.1), channel_id=1, source_target_pairs={{0,24},{8,16},{16,8},{24,0},{1,25},{9,17},{17,9},{25,1},{2,26},{10... | collective-permute-start | bytes 196616 | tf_op jit(solution)/shard_map/ppermute | solution.py:39
  235.2 2.0 collective-permute-done.38
  237.6 4.3 %collective-permute-start.40 = (f32[16,8,128]{2,1,0:T(8,128)S(1)}, f32[16,8,128]{2,1,0:T(8,128)S(1)}, u32[]{:S(2)}, u32[]{:S(2)}) collective-permute-start(f32[16,8,128]{2,1,0:T(8,128)S(1)} %add_add_fusion), channel_id=1, source_target_pairs={{0,1},{1,0},{2,3},{3,2},{4,5},{5,4},{6,7},{7,6},{8,9},{9,8},{10,11... | collective-permute-start | bytes 196616 | tf_op jit(solution)/shard_map/ppermute | solution.py:39
  241.9 1.0 copy.17
  242.9 1.2 collective-permute-start.41
  244.8 1.2 maximum_select_fusion
  246.0 5.1 %short_adjoint.3 = bf16[128,12288]{1,0:T(8,128)(2,1)} custom-call(bf16[2,128,4096]{2,1,0:T(8,128)(2,1)} %get-tuple-element.141.grads_ref, bf16[3,8,4096]{2,1,0:T(8,128)(2,1)S(1)} %collective-permute-done.29.rim_ref, f32[7,12288]{1,0:T(8,128)} %filter_ref.3, bf16[128,12288]{1,0:T(8,128)(2,1)} %short_adjoint.2.refs_0_), custom_call_target="tpu_custom_call", output_to_operand_aliasing={{}: (3, {})} | custom-call | flops 14680064 | bytes 4194304 | tf_op jit(solution)/shard_map/short_adjoint/pallas_call | solution.py:64
  251.2 2.2 collective-permute-done.43.refs_3_
  253.4 1.5 collect.1
  (94 shorter events, 11.1 us)
Async XLA Ops:
  7.2 99.7 %all-gather.2.cloned.1.call-start = ((), (), s32[]{:S(2)}) async-start(), calls=%async_computation.1 | async-start | bytes 9437184 | tf_op jit(solution)/shard_map/all_gather | solution.py:717
  8.2 11.7 %collective-permute-start = (bf16[8,12288]{1,0:T(8,128)(2,1)S(1)}, bf16[8,12288]{1,0:T(8,128)(2,1)S(1)}, u32[]{:S(2)}, u32[]{:S(2)}) collective-permute-start(bf16[8,12288]{1,0:T(8,128)(2,1)S(1)} %slice_bitcast_fusion), channel_id=1, source_target_pairs={{0,1},{1,2},{2,3},{3,4},{4,5},{5,6},{6,7},{7,8},{8,9},{9,10},{10,1... | collective-permute-start | bytes 589832 | tf_op jit(solution)/shard_map/ppermute | solution.py:27
  19.8 2.6 copy-start
  19.8 4.5 %copy-start.9 = (bf16[512,256]{1,0:T(8,128)(2,1)S(1)}, bf16[512,256]{1,0:T(8,128)(2,1)}, u32[]{:S(2)}) copy-start(bf16[512,256]{1,0:T(8,128)(2,1)} %param.8) | copy-start | bytes 786436
  19.9 8.2 %copy-start.10 = (bf16[256,128]{1,0:T(8,128)(2,1)S(1)}, bf16[256,128]{1,0:T(8,128)(2,1)}, u32[]{:S(2)}) copy-start(bf16[256,128]{1,0:T(8,128)(2,1)} %param.7) | copy-start | bytes 196612
  22.4 14.0 %collective-permute-start.1 = (bf16[128,4096]{1,0:T(8,128)(2,1)}, bf16[128,4096]{1,0:T(8,128)(2,1)S(1)}, u32[]{:S(2)}, u32[]{:S(2)}) collective-permute-start(bf16[128,4096]{1,0:T(8,128)(2,1)} %get-tuple-element.91.cur_ref), channel_id=1, source_target_pairs={{0,1},{1,2},{2,3},{3,4},{4,5},{5,6},{6,7},{7,8},{8,9},{9,10},{10,1... | collective-permute-start | bytes 3145736 | tf_op jit(solution)/shard_map/ppermute | solution.py:27
  24.4 6.1 %collective-permute-start.2 = (bf16[256,256]{1,0:T(8,128)(2,1)S(1)}, bf16[256,256]{1,0:T(8,128)(2,1)S(1)}, u32[]{:S(2)}, u32[]{:S(2)}) collective-permute-start(bf16[256,256]{1,0:T(8,128)(2,1)S(1)} %slice.56), channel_id=1, source_target_pairs={{0,8},{8,0},{1,9},{9,1},{2,10},{10,2},{3,11},{11,3},{4,12},{12,4},... | collective-permute-start | bytes 393224 | tf_op jit(solution)/shard_map/ppermute | solution.py:39
  27.2 6.2 %collective-permute-start.3 = (bf16[256,256]{1,0:T(8,128)(2,1)S(1)}, bf16[256,256]{1,0:T(8,128)(2,1)S(1)}, u32[]{:S(2)}, u32[]{:S(2)}) collective-permute-start(bf16[256,256]{1,0:T(8,128)(2,1)S(1)} %slice.56), channel_id=1, source_target_pairs={{0,16},{16,0},{1,17},{17,1},{2,18},{18,2},{3,19},{19,3},{4,20},{20... | collective-permute-start | bytes 393224 | tf_op jit(solution)/shard_map/ppermute | solution.py:39
  27.5 6.2 %collective-permute-start.4 = (bf16[256,256]{1,0:T(8,128)(2,1)S(1)}, bf16[256,256]{1,0:T(8,128)(2,1)S(1)}, u32[]{:S(2)}, u32[]{:S(2)}) collective-permute-start(bf16[256,256]{1,0:T(8,128)(2,1)S(1)} %slice.56), channel_id=1, source_target_pairs={{0,24},{8,16},{16,8},{24,0},{1,25},{9,17},{17,9},{25,1},{2,26},{10... | collective-permute-start | bytes 393224 | tf_op jit(solution)/shard_map/ppermute | solution.py:39
  36.4 9.8 %copy-start.1 = (bf16[128,4096]{1,0:T(8,128)(2,1)}, bf16[128,4096]{1,0:T(8,128)(2,1)S(1)}, u32[]{:S(2)}) copy-start(bf16[128,4096]{1,0:T(8,128)(2,1)S(1)} %collective-permute-done.1.prev_ref) | copy-start | bytes 3145732
  36.4 9.9 %copy-start.5 = (bf16[1,2048,256]{2,1,0:T(8,128)(2,1)S(1)}, bf16[1,2048,256]{2,1,0:T(8,128)(2,1)}, u32[]{:S(2)}) copy-start(bf16[1,2048,256]{2,1,0:T(8,128)(2,1)} %param.9) | copy-start | bytes 3145732
  46.2 128.0 %reduce-scatter.2.cloned.1.call-start = ((), (), s32[]{:S(2)}) async-start(), calls=%async_computation.2 | async-start | bytes 9437184 | tf_op jit(solution)/shard_map/reduce_scatter | solution.py:724
  47.0 18.7 %collective-permute-start.6 = (bf16[4,256,256]{2,1,0:T(8,128)(2,1)S(1)}, bf16[4,256,256]{2,1,0:T(8,128)(2,1)S(1)}, u32[]{:S(2)}, u32[]{:S(2)}) collective-permute-start(bf16[4,256,256]{2,1,0:T(8,128)(2,1)S(1)} %pad_maximum_fusion.1.refs_1_.refs_0_), channel_id=1, source_target_pairs={{0,32},{32,64},{64,96},{96,0},{1,33},{33,65},{65,97},{97,1},{2,34}... | collective-permute-start | bytes 1572872 | tf_op jit(solution)/shard_map/ppermute | solution.py:39
  48.4 18.5 %collective-permute-start.5 = (bf16[1024,256]{0,1:T(8,128)(2,1)S(1)}, bf16[1024,256]{0,1:T(8,128)(2,1)S(1)}, u32[]{:S(2)}, u32[]{:S(2)}) collective-permute-start(bf16[1024,256]{0,1:T(8,128)(2,1)S(1)} %get-tuple-element.165), channel_id=1, source_target_pairs={{0,8},{8,0},{1,9},{9,1},{2,10},{10,2},{3,11},{11,3},{4,12},{12,4},... | collective-permute-start | bytes 1572872 | tf_op jit(solution)/shard_map/ppermute | solution.py:39
  51.3 4.2 %collective-permute-start.11 = (bf16[256,256]{1,0:T(8,128)(2,1)S(1)}, bf16[256,256]{1,0:T(8,128)(2,1)S(1)}, u32[]{:S(2)}, u32[]{:S(2)}) collective-permute-start(bf16[256,256]{1,0:T(8,128)(2,1)S(1)} %get-tuple-element.178), channel_id=1, source_target_pairs={{0,96},{32,0},{64,32},{96,64},{1,97},{33,1},{65,33},{97,65},{2,98}... | collective-permute-start | bytes 393224 | tf_op jit(solution)/shard_map/ppermute | solution.py:39
  52.8 10.1 %collective-permute-start.9 = (bf16[256,256]{1,0:T(8,128)(2,1)S(1)}, bf16[256,256]{1,0:T(8,128)(2,1)S(1)}, u32[]{:S(2)}, u32[]{:S(2)}) collective-permute-start(bf16[256,256]{1,0:T(8,128)(2,1)S(1)} %get-tuple-element.178), channel_id=1, source_target_pairs={{0,32},{32,64},{64,96},{96,0},{1,33},{33,65},{65,97},{97,1},{2,34}... | collective-permute-start | bytes 393224 | tf_op jit(solution)/shard_map/ppermute | solution.py:39
  52.8 12.7 %collective-permute-start.10 = (bf16[256,256]{1,0:T(8,128)(2,1)S(1)}, bf16[256,256]{1,0:T(8,128)(2,1)S(1)}, u32[]{:S(2)}, u32[]{:S(2)}) collective-permute-start(bf16[256,256]{1,0:T(8,128)(2,1)S(1)} %get-tuple-element.178), channel_id=1, source_target_pairs={{0,64},{32,96},{64,0},{96,32},{1,65},{33,97},{65,1},{97,33},{2,66}... | collective-permute-start | bytes 393224 | tf_op jit(solution)/shard_map/ppermute | solution.py:39
  55.5 19.7 %collective-permute-start.7 = (bf16[4,256,256]{2,1,0:T(8,128)(2,1)S(1)}, bf16[4,256,256]{2,1,0:T(8,128)(2,1)}, u32[]{:S(2)}, u32[]{:S(2)}) collective-permute-start(bf16[4,256,256]{2,1,0:T(8,128)(2,1)S(1)} %pad_maximum_fusion.1.refs_1_.refs_0_), channel_id=1, source_target_pairs={{0,64},{32,96},{64,0},{96,32},{1,65},{33,97},{65,1},{97,33},{2,66}... | collective-permute-start | bytes 1572872 | tf_op jit(solution)/shard_map/ppermute | solution.py:39
  62.9 16.3 %collective-permute-start.8 = (bf16[4,256,256]{2,1,0:T(8,128)(2,1)S(1)}, bf16[4,256,256]{2,1,0:T(8,128)(2,1)}, u32[]{:S(2)}, u32[]{:S(2)}) collective-permute-start(bf16[4,256,256]{2,1,0:T(8,128)(2,1)S(1)} %pad_maximum_fusion.1.refs_1_.refs_0_), channel_id=1, source_target_pairs={{0,96},{32,0},{64,32},{96,64},{1,97},{33,1},{65,33},{97,65},{2,98}... | collective-permute-start | bytes 1572872 | tf_op jit(solution)/shard_map/ppermute | solution.py:39
  65.6 13.6 %collective-permute-start.12 = (bf16[4,256,256]{2,1,0:T(8,128)(2,1)S(1)}, bf16[4,256,256]{2,1,0:T(8,128)(2,1)}, u32[]{:S(2)}, u32[]{:S(2)}) collective-permute-start(bf16[4,256,256]{2,1,0:T(8,128)(2,1)S(1)} %pad_maximum_fusion.2.refs_5_.refs_4_), channel_id=1, source_target_pairs={{0,8},{8,0},{1,9},{9,1},{2,10},{10,2},{3,11},{11,3},{4,12},{12,4},... | collective-permute-start | bytes 1572872 | tf_op jit(solution)/shard_map/ppermute | solution.py:39
  65.7 0.8 copy-start.2
  66.5 13.3 %collective-permute-start.13 = (bf16[4,256,256]{2,1,0:T(8,128)(2,1)S(1)}, bf16[4,256,256]{2,1,0:T(8,128)(2,1)}, u32[]{:S(2)}, u32[]{:S(2)}) collective-permute-start(bf16[4,256,256]{2,1,0:T(8,128)(2,1)S(1)} %pad_maximum_fusion.2.refs_5_.refs_4_), channel_id=1, source_target_pairs={{0,16},{16,0},{1,17},{17,1},{2,18},{18,2},{3,19},{19,3},{4,20},{20... | collective-permute-start | bytes 1572872 | tf_op jit(solution)/shard_map/ppermute | solution.py:39
  67.0 15.9 %collective-permute-start.14 = (bf16[4,256,256]{2,1,0:T(8,128)(2,1)S(1)}, bf16[4,256,256]{2,1,0:T(8,128)(2,1)}, u32[]{:S(2)}, u32[]{:S(2)}) collective-permute-start(bf16[4,256,256]{2,1,0:T(8,128)(2,1)S(1)} %pad_maximum_fusion.2.refs_5_.refs_4_), channel_id=1, source_target_pairs={{0,24},{8,16},{16,8},{24,0},{1,25},{9,17},{17,9},{25,1},{2,26},{10... | collective-permute-start | bytes 1572872 | tf_op jit(solution)/shard_map/ppermute | solution.py:39
  82.9 1.1 copy-start.3
  106.9 26.1 %copy-start.4 = (bf16[4,256,256]{2,1,0:T(8,128)(2,1)S(1)}, bf16[4,256,256]{2,1,0:T(8,128)(2,1)}, u32[]{:S(2)}) copy-start(bf16[4,256,256]{2,1,0:T(8,128)(2,1)} %copy-done.2) | copy-start | bytes 1572868
  116.8 15.0 %collective-permute-start.18 = (bf16[4,256,256]{2,1,0:T(8,128)(2,1)}, bf16[4,256,256]{2,1,0:T(8,128)(2,1)S(1)}, u32[]{:S(2)}, u32[]{:S(2)}) collective-permute-start(bf16[4,256,256]{2,1,0:T(8,128)(2,1)} %get-tuple-element.115), channel_id=1, source_target_pairs={{0,8},{8,0},{1,9},{9,1},{2,10},{10,2},{3,11},{11,3},{4,12},{12,4},... | collective-permute-start | bytes 1572872 | tf_op jit(solution)/shard_map/ppermute | solution.py:39
  119.5 23.7 %collective-permute-start.19 = (bf16[4,256,256]{2,1,0:T(8,128)(2,1)}, bf16[4,256,256]{2,1,0:T(8,128)(2,1)S(1)}, u32[]{:S(2)}, u32[]{:S(2)}) collective-permute-start(bf16[4,256,256]{2,1,0:T(8,128)(2,1)} %get-tuple-element.116), channel_id=1, source_target_pairs={{0,16},{16,0},{1,17},{17,1},{2,18},{18,2},{3,19},{19,3},{4,20},{20... | collective-permute-start | bytes 1572872 | tf_op jit(solution)/shard_map/ppermute | solution.py:39
  119.8 23.9 %collective-permute-start.20 = (bf16[4,256,256]{2,1,0:T(8,128)(2,1)}, bf16[4,256,256]{2,1,0:T(8,128)(2,1)S(1)}, u32[]{:S(2)}, u32[]{:S(2)}) collective-permute-start(bf16[4,256,256]{2,1,0:T(8,128)(2,1)} %get-tuple-element.117), channel_id=1, source_target_pairs={{0,24},{8,16},{16,8},{24,0},{1,25},{9,17},{17,9},{25,1},{2,26},{10... | collective-permute-start | bytes 1572872 | tf_op jit(solution)/shard_map/ppermute | solution.py:39
  120.4 23.6 %collective-permute-start.15 = (bf16[4,256,256]{2,1,0:T(8,128)(2,1)}, bf16[4,256,256]{2,1,0:T(8,128)(2,1)S(1)}, u32[]{:S(2)}, u32[]{:S(2)}) collective-permute-start(bf16[4,256,256]{2,1,0:T(8,128)(2,1)} %get-tuple-element.111), channel_id=1, source_target_pairs={{0,96},{32,0},{64,32},{96,64},{1,97},{33,1},{65,33},{97,65},{2,98}... | collective-permute-start | bytes 1572872 | tf_op jit(solution)/shard_map/ppermute | solution.py:39
  122.8 21.1 %collective-permute-start.16 = (bf16[4,256,256]{2,1,0:T(8,128)(2,1)}, bf16[4,256,256]{2,1,0:T(8,128)(2,1)S(1)}, u32[]{:S(2)}, u32[]{:S(2)}) collective-permute-start(bf16[4,256,256]{2,1,0:T(8,128)(2,1)} %get-tuple-element.112), channel_id=1, source_target_pairs={{0,64},{32,96},{64,0},{96,32},{1,65},{33,97},{65,1},{97,33},{2,66}... | collective-permute-start | bytes 1572872 | tf_op jit(solution)/shard_map/ppermute | solution.py:39
  131.8 11.9 %copy-start.8 = (bf16[4,256,256]{2,1,0:T(8,128)(2,1)S(1)}, bf16[4,256,256]{2,1,0:T(8,128)(2,1)}, u32[]{:S(2)}) copy-start(bf16[4,256,256]{2,1,0:T(8,128)(2,1)} %get-tuple-element.114) | copy-start | bytes 1572868
  131.8 17.4 %collective-permute-start.17 = (bf16[4,256,256]{2,1,0:T(8,128)(2,1)}, bf16[4,256,256]{2,1,0:T(8,128)(2,1)S(1)}, u32[]{:S(2)}, u32[]{:S(2)}) collective-permute-start(bf16[4,256,256]{2,1,0:T(8,128)(2,1)} %get-tuple-element.113), channel_id=1, source_target_pairs={{0,32},{32,64},{64,96},{96,0},{1,33},{33,65},{65,97},{97,1},{2,34}... | collective-permute-start | bytes 1572872 | tf_op jit(solution)/shard_map/ppermute | solution.py:39
  142.9 6.3 %copy-start.7 = (bf16[4,256,256]{2,1,0:T(8,128)(2,1)S(1)}, bf16[4,256,256]{2,1,0:T(8,128)(2,1)}, u32[]{:S(2)}) copy-start(bf16[4,256,256]{2,1,0:T(8,128)(2,1)} %get-tuple-element.110) | copy-start | bytes 1572868
  149.5 5.4 %collective-permute-start.21 = (bf16[256,256]{1,0:T(8,128)(2,1)S(1)}, bf16[256,256]{1,0:T(8,128)(2,1)S(1)}, u32[]{:S(2)}, u32[]{:S(2)}) collective-permute-start(bf16[256,256]{1,0:T(8,128)(2,1)S(1)} %get-tuple-element.172), channel_id=1, source_target_pairs={{0,8},{8,0},{1,9},{9,1},{2,10},{10,2},{3,11},{11,3},{4,12},{12,4},... | collective-permute-start | bytes 393224 | tf_op jit(solution)/shard_map/ppermute | solution.py:39
  152.0 5.8 %collective-permute-start.22 = (bf16[256,256]{1,0:T(8,128)(2,1)S(1)}, bf16[256,256]{1,0:T(8,128)(2,1)S(1)}, u32[]{:S(2)}, u32[]{:S(2)}) collective-permute-start(bf16[256,256]{1,0:T(8,128)(2,1)S(1)} %get-tuple-element.171), channel_id=1, source_target_pairs={{0,16},{16,0},{1,17},{17,1},{2,18},{18,2},{3,19},{19,3},{4,20},{20... | collective-permute-start | bytes 393224 | tf_op jit(solution)/shard_map/ppermute | solution.py:39
  152.2 28.9 %copy-start.11 = (bf16[1024,256]{1,0:T(8,128)(2,1)S(1)}, bf16[1024,256]{1,0:T(8,128)(2,1)}, u32[]{:S(2)}) copy-start(bf16[1024,256]{1,0:T(8,128)(2,1)} %get-tuple-element.139) | copy-start | bytes 1572868
  152.3 6.6 %collective-permute-start.23 = (bf16[256,256]{1,0:T(8,128)(2,1)S(1)}, bf16[256,256]{1,0:T(8,128)(2,1)S(1)}, u32[]{:S(2)}, u32[]{:S(2)}) collective-permute-start(bf16[256,256]{1,0:T(8,128)(2,1)S(1)} %get-tuple-element.170), channel_id=1, source_target_pairs={{0,24},{8,16},{16,8},{24,0},{1,25},{9,17},{17,9},{25,1},{2,26},{10... | collective-permute-start | bytes 393224 | tf_op jit(solution)/shard_map/ppermute | solution.py:39
  152.9 6.0 %collective-permute-start.24 = (bf16[256,256]{1,0:T(8,128)(2,1)S(1)}, bf16[256,256]{1,0:T(8,128)(2,1)S(1)}, u32[]{:S(2)}, u32[]{:S(2)}) collective-permute-start(bf16[256,256]{1,0:T(8,128)(2,1)S(1)} %get-tuple-element.168), channel_id=1, source_target_pairs={{0,96},{32,0},{64,32},{96,64},{1,97},{33,1},{65,33},{97,65},{2,98}... | collective-permute-start | bytes 393224 | tf_op jit(solution)/shard_map/ppermute | solution.py:39
  153.0 5.9 %collective-permute-start.25 = (bf16[256,256]{1,0:T(8,128)(2,1)S(1)}, bf16[256,256]{1,0:T(8,128)(2,1)S(1)}, u32[]{:S(2)}, u32[]{:S(2)}) collective-permute-start(bf16[256,256]{1,0:T(8,128)(2,1)S(1)} %get-tuple-element.167), channel_id=1, source_target_pairs={{0,64},{32,96},{64,0},{96,32},{1,65},{33,97},{65,1},{97,33},{2,66}... | collective-permute-start | bytes 393224 | tf_op jit(solution)/shard_map/ppermute | solution.py:39
  154.9 5.7 %collective-permute-start.26 = (bf16[256,256]{1,0:T(8,128)(2,1)S(1)}, bf16[256,256]{1,0:T(8,128)(2,1)S(1)}, u32[]{:S(2)}, u32[]{:S(2)}) collective-permute-start(bf16[256,256]{1,0:T(8,128)(2,1)S(1)} %get-tuple-element.166), channel_id=1, source_target_pairs={{0,32},{32,64},{64,96},{96,0},{1,33},{33,65},{65,97},{97,1},{2,34}... | collective-permute-start | bytes 393224 | tf_op jit(solution)/shard_map/ppermute | solution.py:39
  177.8 16.3 %collective-permute-start.27 = (bf16[128,4096]{1,0:T(8,128)(2,1)}, bf16[128,4096]{1,0:T(8,128)(2,1)S(1)}, u32[]{:S(2)}, u32[]{:S(2)}) collective-permute-start(bf16[128,4096]{1,0:T(8,128)(2,1)} %get-tuple-element.124.grad_ref), channel_id=1, source_target_pairs={{1,0},{2,1},{3,2},{4,3},{5,4},{6,5},{7,6},{8,7},{9,8},{10,9},{11,1... | collective-permute-start | bytes 3145736 | tf_op jit(solution)/shard_map/ppermute | solution.py:27
  181.1 24.4 %collective-permute-start.28 = (bf16[1024,256]{1,0:T(8,128)(2,1)S(1)}, bf16[1024,256]{1,0:T(8,128)(2,1)S(1)}, u32[]{:S(2)}, u32[]{:S(2)}) collective-permute-start(bf16[1024,256]{1,0:T(8,128)(2,1)S(1)} %copy-done.11), channel_id=1, source_target_pairs={{0,8},{8,0},{1,9},{9,1},{2,10},{10,2},{3,11},{11,3},{4,12},{12,4},... | collective-permute-start | bytes 1572872 | tf_op jit(solution)/shard_map/ppermute | solution.py:39
  206.2 5.5 %collective-permute-start.30 = (f32[64,8,128]{2,1,0:T(8,128)S(1)}, f32[64,8,128]{2,1,0:T(8,128)S(1)}, u32[]{:S(2)}, u32[]{:S(2)}) collective-permute-start(f32[64,8,128]{2,1,0:T(8,128)S(1)} %get-tuple-element.148), channel_id=1, source_target_pairs={{0,1},{1,0},{2,3},{3,2},{4,5},{5,4},{6,7},{7,6},{8,9},{9,8},{10,11... | collective-permute-start | bytes 786440 | tf_op jit(solution)/shard_map/ppermute | solution.py:39
  211.8 10.5 %collective-permute-start.31 = (f32[16,8,128]{2,1,0:T(8,128)S(1)}, f32[16,8,128]{2,1,0:T(8,128)S(1)}, u32[]{:S(2)}, u32[]{:S(2)}) collective-permute-start(f32[16,8,128]{2,1,0:T(8,128)S(1)} %get-tuple-element.174), channel_id=1, source_target_pairs={{0,2},{2,4},{4,6},{6,0},{1,3},{3,5},{5,7},{7,1},{8,10},{10,12},{12... | collective-permute-start | bytes 196616 | tf_op jit(solution)/shard_map/ppermute | solution.py:39
  211.8 11.3 %collective-permute-start.32 = (f32[16,8,128]{2,1,0:T(8,128)S(1)}, f32[16,8,128]{2,1,0:T(8,128)S(1)}, u32[]{:S(2)}, u32[]{:S(2)}) collective-permute-start(f32[16,8,128]{2,1,0:T(8,128)S(1)} %get-tuple-element.176), channel_id=1, source_target_pairs={{0,4},{2,6},{4,0},{6,2},{1,5},{3,7},{5,1},{7,3},{8,12},{10,14},{12... | collective-permute-start | bytes 196616 | tf_op jit(solution)/shard_map/ppermute | solution.py:39
  219.6 3.5 %collective-permute-start.33 = (f32[16,8,128]{2,1,0:T(8,128)S(1)}, f32[16,8,128]{2,1,0:T(8,128)S(1)}, u32[]{:S(2)}, u32[]{:S(2)}) collective-permute-start(f32[16,8,128]{2,1,0:T(8,128)S(1)} %get-tuple-element.175), channel_id=1, source_target_pairs={{0,6},{2,0},{4,2},{6,4},{1,7},{3,1},{5,3},{7,5},{8,14},{10,8},{12,... | collective-permute-start | bytes 196616 | tf_op jit(solution)/shard_map/ppermute | solution.py:39
  219.6 8.4 %collective-permute-start.29 = (bf16[3,8,4096]{2,1,0:T(8,128)(2,1)S(1)}, bf16[3,8,4096]{2,1,0:T(8,128)(2,1)S(1)}, u32[]{:S(2)}, u32[]{:S(2)}) collective-permute-start(bf16[3,8,4096]{2,1,0:T(8,128)(2,1)S(1)} %get-tuple-element.142), channel_id=1, source_target_pairs={{1,0},{2,1},{3,2},{4,3},{5,4},{6,5},{7,6},{8,7},{9,8},{10,9},{11,1... | collective-permute-start | bytes 589832 | tf_op jit(solution)/shard_map/ppermute | solution.py:27
  223.1 8.1 %collective-permute-start.34 = (f32[16,8,128]{2,1,0:T(8,128)S(1)}, f32[16,8,128]{2,1,0:T(8,128)S(1)}, u32[]{:S(2)}, u32[]{:S(2)}) collective-permute-start(f32[16,8,128]{2,1,0:T(8,128)S(1)} %fusion.1), channel_id=1, source_target_pairs={{0,32},{32,64},{64,96},{96,0},{1,33},{33,65},{65,97},{97,1},{2,34}... | collective-permute-start | bytes 196616 | tf_op jit(solution)/shard_map/ppermute | solution.py:39
  224.4 6.8 %collective-permute-start.35 = (f32[16,8,128]{2,1,0:T(8,128)S(1)}, f32[16,8,128]{2,1,0:T(8,128)S(1)}, u32[]{:S(2)}, u32[]{:S(2)}) collective-permute-start(f32[16,8,128]{2,1,0:T(8,128)S(1)} %fusion.1), channel_id=1, source_target_pairs={{0,64},{32,96},{64,0},{96,32},{1,65},{33,97},{65,1},{97,33},{2,66}... | collective-permute-start | bytes 196616 | tf_op jit(solution)/shard_map/ppermute | solution.py:39
  226.9 4.4 %collective-permute-start.36 = (f32[16,8,128]{2,1,0:T(8,128)S(1)}, f32[16,8,128]{2,1,0:T(8,128)S(1)}, u32[]{:S(2)}, u32[]{:S(2)}) collective-permute-start(f32[16,8,128]{2,1,0:T(8,128)S(1)} %fusion.1), channel_id=1, source_target_pairs={{0,96},{32,0},{64,32},{96,64},{1,97},{33,1},{65,33},{97,65},{2,98}... | collective-permute-start | bytes 196616 | tf_op jit(solution)/shard_map/ppermute | solution.py:39
  231.2 13.6 %copy-start.6 = (bf16[1024,256]{1,0:T(8,128)(2,1)S(1)}, bf16[1024,256]{1,0:T(8,128)(2,1)}, u32[]{:S(2)}) copy-start(bf16[1024,256]{1,0:T(8,128)(2,1)} %get-tuple-element.108) | copy-start | bytes 1572868
  231.3 3.9 %collective-permute-start.37 = (f32[16,8,128]{2,1,0:T(8,128)S(1)}, f32[16,8,128]{2,1,0:T(8,128)S(1)}, u32[]{:S(2)}, u32[]{:S(2)}) collective-permute-start(f32[16,8,128]{2,1,0:T(8,128)S(1)} %add_add_fusion.1), channel_id=1, source_target_pairs={{0,16},{16,0},{1,17},{17,1},{2,18},{18,2},{3,19},{19,3},{4,20},{20... | collective-permute-start | bytes 196616 | tf_op jit(solution)/shard_map/ppermute | solution.py:39
  232.5 4.7 %collective-permute-start.38 = (f32[16,8,128]{2,1,0:T(8,128)S(1)}, f32[16,8,128]{2,1,0:T(8,128)S(1)}, u32[]{:S(2)}, u32[]{:S(2)}) collective-permute-start(f32[16,8,128]{2,1,0:T(8,128)S(1)} %add_add_fusion.1), channel_id=1, source_target_pairs={{0,8},{8,0},{1,9},{9,1},{2,10},{10,2},{3,11},{11,3},{4,12},{12,4},... | collective-permute-start | bytes 196616 | tf_op jit(solution)/shard_map/ppermute | solution.py:39
  232.5 5.0 %collective-permute-start.39 = (f32[16,8,128]{2,1,0:T(8,128)S(1)}, f32[16,8,128]{2,1,0:T(8,128)S(1)}, u32[]{:S(2)}, u32[]{:S(2)}) collective-permute-start(f32[16,8,128]{2,1,0:T(8,128)S(1)} %add_add_fusion.1), channel_id=1, source_target_pairs={{0,24},{8,16},{16,8},{24,0},{1,25},{9,17},{17,9},{25,1},{2,26},{10... | collective-permute-start | bytes 196616 | tf_op jit(solution)/shard_map/ppermute | solution.py:39
  237.6 5.4 %collective-permute-start.40 = (f32[16,8,128]{2,1,0:T(8,128)S(1)}, f32[16,8,128]{2,1,0:T(8,128)S(1)}, u32[]{:S(2)}, u32[]{:S(2)}) collective-permute-start(f32[16,8,128]{2,1,0:T(8,128)S(1)} %add_add_fusion), channel_id=1, source_target_pairs={{0,1},{1,0},{2,3},{3,2},{4,5},{5,4},{6,7},{7,6},{8,9},{9,8},{10,11... | collective-permute-start | bytes 196616 | tf_op jit(solution)/shard_map/ppermute | solution.py:39
  242.9 8.2 %collective-permute-start.41 = (f32[32,8,128]{2,1,0:T(8,128)S(1)}, f32[32,8,128]{2,1,0:T(8,128)S(1)}, u32[]{:S(2)}, u32[]{:S(2)}) collective-permute-start(f32[32,8,128]{2,1,0:T(8,128)S(1)} %pad_maximum_fusion.3.refs_0_), channel_id=1, source_target_pairs={{0,6},{2,0},{4,2},{6,4},{1,7},{3,1},{5,3},{7,5},{8,14},{10,8},{12,... | collective-permute-start | bytes 393224 | tf_op jit(solution)/shard_map/ppermute | solution.py:39
  244.1 7.1 %collective-permute-start.42 = (f32[32,8,128]{2,1,0:T(8,128)S(1)}, f32[32,8,128]{2,1,0:T(8,128)S(1)}, u32[]{:S(2)}, u32[]{:S(2)}) collective-permute-start(f32[32,8,128]{2,1,0:T(8,128)S(1)} %pad_maximum_fusion.3.refs_0_), channel_id=1, source_target_pairs={{0,4},{2,6},{4,0},{6,2},{1,5},{3,7},{5,1},{7,3},{8,12},{10,14},{12... | collective-permute-start | bytes 393224 | tf_op jit(solution)/shard_map/ppermute | solution.py:39
  244.1 9.3 %collective-permute-start.43 = (f32[32,8,128]{2,1,0:T(8,128)S(1)}, f32[32,8,128]{2,1,0:T(8,128)S(1)}, u32[]{:S(2)}, u32[]{:S(2)}) collective-permute-start(f32[32,8,128]{2,1,0:T(8,128)S(1)} %pad_maximum_fusion.3.refs_0_), channel_id=1, source_target_pairs={{0,2},{2,4},{4,6},{6,0},{1,3},{3,5},{5,7},{7,1},{8,10},{10,12},{12... | collective-permute-start | bytes 393224 | tf_op jit(solution)/shard_map/ppermute | solution.py:39
Sparse Core Ops, SparseCore 0:
  46.3 60.5 all-gather.1
  109.3 64.8 reduce-scatter.1

commit v11 on v10

--- a/solution.py
+++ b/solution.py
@@ -397,31 +397,31 @@
         out_ref[:, at] = total.astype(BF16)
 
 
-def short_adjoint_call(grads, rim, filters, first, out):
-    parts, rows, channels = grads.shape
+def short_adjoint_call(grads, rim, filters, given, part, out):
+    _, rows, channels = grads.shape
     short_taps = filters.shape[0]
     width = block_width(channels, 2 * WIDTH)
     steps = channels // width
-    result = pl.BlockSpec((rows, width), lambda p, i: (0, (p + first) * steps + i))
-    given = [] if out is None else [out]
+    result = pl.BlockSpec((rows, width), lambda i: (0, part * steps + i))
+    olds = [] if out is None else [out]
     return hbm_call(
         functools.partial(short_adjoint_kernel, short_taps),
         loose=(1,),
-        grid=(parts, steps),
+        grid=(steps,),
         in_specs=[
-            pl.BlockSpec((1, rows, width), lambda p, i: (p, 0, i)),
-            pl.BlockSpec((1, RIM, width), lambda p, i: (p + first, 0, i)),
-            pl.BlockSpec((short_taps, width), lambda p, i: (0, (p + first) * steps + i)),
+            pl.BlockSpec((1, rows, width), lambda i: (given, 0, i)),
+            pl.BlockSpec((1, RIM, width), lambda i: (part, 0, i)),
+            pl.BlockSpec((short_taps, width), lambda i: (0, part * steps + i)),
         ]
-        + [pl.BlockSpec(memory_space=pl.ANY)] * len(given),
+        + [pl.BlockSpec(memory_space=pl.ANY)] * len(olds),
         out_specs=result,
         out_shape=jax.ShapeDtypeStruct((rows, 3 * channels), BF16),
-        input_output_aliases={3: 0} if given else {},
+        input_output_aliases={3: 0} if olds else {},
         scratch_shapes=[pltpu.VMEM((2, rows + RIM, LANES), F32)],
         compiler_params=params(),
-        cost_estimate=cost(2 * parts * short_taps * rows * channels, 4 * parts * rows * channels),
+        cost_estimate=cost(2 * short_taps * rows * channels, 4 * rows * channels),
         name="short_adjoint",
-    )(grads, rim, filters, *given)
+    )(grads, rim, filters, *olds)
 
 
 def spread_kernel(place, query_ref, key_ref, value_ref, long_ref, own_ref, other_ref):
@@ -461,7 +461,7 @@
     return pl.BlockSpec(memory_space=pltpu.VMEM)
 
 
-def total_over_devices(spread_to, collect_from, query_sum, key_sum, value_sum, long_sum, short_taps, beside):
+def total_over_devices(spread_to, collect_from, query_sum, key_sum, value_sum, long_sum, short_taps, first, after, last):
     ny, nz = lax.axis_size("y"), lax.axis_size("z")
     channels = query_sum.shape[1]
     count = 3 * channels // LANES + long_sum.shape[0] // 8
@@ -477,9 +477,11 @@
     part = own + move(other, c=1)
     size = count // 2 // nz
     part = sum([move(part[d * size : (d + 1) * size], z=d) for d in range(1, nz)], part[:size])
-    terms, beside = lax.optimization_barrier(([part] + [move(part, y=d) for d in range(1, ny)], beside))
+    terms, first = lax.optimization_barrier(([part] + [move(part, y=d) for d in range(1, ny)], first))
     whole = paired_sum(terms)
-    whole = paired_sum([move(whole, xl=a, xh=b) for a, b in FLIPS])
+    terms = [move(whole, xl=a, xh=b) for a, b in FLIPS]
+    terms, beside, last = lax.optimization_barrier((terms, after(first), last))
+    whole = paired_sum(terms)
     line = jnp.concatenate([whole, move(whole, c=1)], axis=0)
     lines = [move(line, z=-d) for d in range(nz)]
     groups, taps = long_sum.shape
@@ -495,7 +497,7 @@
         compiler_params=params(),
         name="collect",
     )(collect_from, *lines)
-    return short, long, beside
+    return short, long, beside, last
 
 
 def paired_sum(terms):
@@ -707,17 +709,18 @@
     parts = features_call(tokens, short_filter)
     parts, rim = lax.optimization_barrier((parts, rim))
     query, key, value, mixer = features_call(tokens, short_filter, rim, parts)
-    mixer, out_weight = lax.optimization_barrier((mixer, out_weight))
+    mixer, out_weight, half = lax.optimization_barrier((mixer, out_weight, xh))
     mixer_prev = along(mixer, 1)
+    others = move(lax.dynamic_slice_in_dim(upstream, (1 - half) * span, span, 0), xh=1)
+    tall_bottom = gather_tall(out_weight)
+    mixer_prev, tall_bottom, others = lax.optimization_barrier((mixer_prev, tall_bottom, others))
+    mixed, gated = mix_call(lines, mixer_prev, mixer, query)
+    mixed, out_weight, half = lax.optimization_barrier((mixed, out_weight, half))
     wide_top = gather_wide(out_weight)
-    mixer_prev, wide_top = lax.optimization_barrier((mixer_prev, wide_top))
-    mixed, gated = mix_call(lines, mixer_prev, mixer, query)
-    mixed, out_weight, wide_top, upstream = lax.optimization_barrier((mixed, out_weight, wide_top, upstream))
-    tall_bottom = gather_tall(out_weight)
+    wide_top, tall_bottom = lax.optimization_barrier((wide_top, tall_bottom))
     all_rows = lax.all_gather(gated, ("z", "c"), axis=0, tiled=True)
     tops, bottoms = gather_far(wide_top, tall_bottom)
-    mine = lax.dynamic_slice_in_dim(upstream, xh * span, span, 0)
-    others = move(lax.dynamic_slice_in_dim(upstream, (1 - xh) * span, span, 0), xh=1)
+    mine = lax.dynamic_slice_in_dim(upstream, half * span, span, 0)
     cotangents = jnp.concatenate([mine, others], axis=1)
     partial = gate_matmul(cotangents, tops, bottoms)
     partial, all_rows = lax.optimization_barrier((partial, all_rows))
@@ -742,11 +745,15 @@
     edge, key_sum, theirs = lax.optimization_barrier((edge, key_sum, theirs))
     edge = along(edge, -1)
     output = jnp.where(xh == 0, jnp.concatenate([own, theirs], axis=0), jnp.concatenate([theirs, own], axis=0))
-    grad_tokens = short_adjoint_call(query_grad[None], edge, short_filter, 0, None)
-    grad_short, grad_long, grad_tokens = total_over_devices(
-        spread_to, collect_from, query_sum, key_sum, value_sum, long_sum, short_taps, grad_tokens
+    query_part = short_adjoint_call(query_grad[None], edge, short_filter, 0, 0, None)
+
+    def key_part(query_part):
+        return short_adjoint_call(other_grads, edge, short_filter, 0, 1, query_part)
+
+    grad_short, grad_long, grad_tokens, output = total_over_devices(
+        spread_to, collect_from, query_sum, key_sum, value_sum, long_sum, short_taps, query_part, key_part, output
     )
-    grad_tokens = short_adjoint_call(other_grads, edge, short_filter, 1, grad_tokens)
+    grad_tokens = short_adjoint_call(other_grads, edge, short_filter, 1, 2, grad_tokens)
     return output[None], grad_tokens[None], grad_short, grad_long, grad_weight
 
 

time: 262 us -> 256 us (0.977)
  waiting for transfers between devices: 82 us -> 72.1 us
    reduce_scatter x1, waiting for transfers between devices: 13.5 us -> 0.24 us  [shards(): lax.psum_scatter(partial, ('z', 'c'), scatter_dimension=0, tiled=True)]
    all_gather x1, waiting for transfers between devices: 14.4 us -> 22.9 us  [shards(): all_rows = lax.all_gather(gated, ('z', 'c'), axis=0, tiled=True)]
    ppermute x40, starting transfers between devices: 61.1 us -> 57.1 us  [move(): return lax.ppermute(x, axes, pairs)]
    ppermute x40, waiting for transfers between devices: 50.6 us -> 47.2 us  [move(): return lax.ppermute(x, axes, pairs)]
    pallas_call x11 -> x12, Pallas kernels: 79.7 us -> 81.3 us  [run(): return call(*held)]
  transfers between devices with their start and end apart: 46 -> 46, of which waited for: 26 -> 25; matrix products, arithmetic and copies ran while one was open for 3% -> 4% of each run, Pallas kernels for 24% -> 26%
where the time goes in v11:
time: 256 us; the launch traced here: 255 us
  Pallas kernels  83.5 us (33%)
  starting transfers between devices  72.3 us (28%)
  waiting for transfers between devices  72.1 us (28%)
  between operations  14.5 us (6%)
  local copies, waits for them, and re-layouts  6.94 us (3%)
  other arithmetic  5.68 us (2%)
    pallas_call x12, Pallas kernels, run(): return call(*held)  81.3 us
    ppermute x40, starting transfers between devices, move(): return lax.ppermute(x, axes, pairs)  57.1 us
    ppermute x40, waiting for transfers between devices, move(): return lax.ppermute(x, axes, pairs)  47.2 us
    all_gather x1, waiting for transfers between devices, shards(): all_rows = lax.all_gather(gated, ('z', 'c'), axis=0, tiled=True)  22.9 us
    ppermute x4, starting transfers between devices, along(): return lax.ppermute(x, LINE, pairs)  15 us
  transfers between devices with their start and end apart: 46, of which 25 were waited for; matrix products, arithmetic and copies ran while one was open for 4% of the time, Pallas kernels for 26%

profile of v11, /device:TPU:1, one launch (start us, length us, event | category | flops | bytes accessed | tf_op | source)
XLA Modules:
  0.0 255.0 jit_solution(5965868531864491433)
XLA Ops:
  7.2 1.0 slice_bitcast_fusion
  8.3 4.9 %collective-permute-start = (bf16[8,12288]{1,0:T(8,128)(2,1)S(1)}, bf16[8,12288]{1,0:T(8,128)(2,1)S(1)}, u32[]{:S(2)}, u32[]{:S(2)}) collective-permute-start(bf16[8,12288]{1,0:T(8,128)(2,1)S(1)} %slice_bitcast_fusion), channel_id=1, source_target_pairs={{0,1},{1,2},{2,3},{3,4},{4,5},{5,6},{6,7},{7,8},{8,9},{9,10},{10,1... | collective-permute-start | bytes 589832 | tf_op jit(solution)/shard_map/ppermute | solution.py:27
  13.2 6.7 %features.1 = (bf16[128,4096]{1,0:T(8,128)(2,1)}, bf16[128,4096]{1,0:T(8,128)(2,1)}, bf16[128,4096]{1,0:T(8,128)(2,1)}, bf16[128,4096]{1,0:T(8,128)(2,1)}) custom-call(bf16[128,12288]{1,0:T(8,128)(2,1)} %bitcast.36, bf16[128,12288]{1,0:T(8,128)(2,1)} %bitcast.37, bf16[128,12288]{1,0:T(8,128)(2,1)} %bitcast.38, f32[7,12288]{1,0:T(8,128)} %filter_ref.5, ...), custom_call_target="tpu_custom_call" | custom-call | bytes 1572864 | tf_op jit(solution)/shard_map/features/pallas_call | solution.py:64
  19.9 2.6 %first_rows.1 = (bf16[128,4096]{1,0:T(8,128)(2,1)}, bf16[128,4096]{1,0:T(8,128)(2,1)}, bf16[128,4096]{1,0:T(8,128)(2,1)}, bf16[128,4096]{1,0:T(8,128)(2,1)}) custom-call(bf16[128,12288]{1,0:T(8,128)(2,1)} %bitcast.39, bf16[128,12288]{1,0:T(8,128)(2,1)} %bitcast.40, ...), custom_call_target="tpu_custom_call", output_to_operand_aliasing={{0}: (9, {}), {1}: (10, {}), {2}: (11, {}), {3}: (12, {})} | custom-call | bytes 196608 | tf_op jit(solution)/shard_map/first_rows/pallas_call | solution.py:64
  22.5 1.9 collective-permute-start.1
  24.7 2.8 %collective-permute-start.5 = (bf16[1024,256]{0,1:T(8,128)(2,1)S(1)}, bf16[1024,256]{0,1:T(8,128)(2,1)S(1)}, u32[]{:S(2)}, u32[]{:S(2)}) collective-permute-start(bf16[1024,256]{0,1:T(8,128)(2,1)S(1)} %bitcast.49), channel_id=1, source_target_pairs={{0,8},{8,0},{1,9},{9,1},{2,10},{10,2},{3,11},{11,3},{4,12},{12,4},... | collective-permute-start | bytes 1572872 | tf_op jit(solution)/shard_map/ppermute | solution.py:39
  27.5 0.9 slice.56
  28.4 1.4 collective-permute-start.2
  29.8 2.6 %collective-permute-start.3 = (bf16[256,256]{1,0:T(8,128)(2,1)S(1)}, bf16[256,256]{1,0:T(8,128)(2,1)S(1)}, u32[]{:S(2)}, u32[]{:S(2)}) collective-permute-start(bf16[256,256]{1,0:T(8,128)(2,1)S(1)} %slice.56), channel_id=1, source_target_pairs={{0,64},{32,96},{64,0},{96,32},{1,65},{33,97},{65,1},{97,33},{2,66}... | collective-permute-start | bytes 393224 | tf_op jit(solution)/shard_map/ppermute | solution.py:39
  32.4 1.1 collective-permute-start.4
  34.4 3.7 %collective-permute-done.3 = bf16[256,256]{1,0:T(8,128)(2,1)S(1)} collective-permute-done((bf16[256,256]{1,0:T(8,128)(2,1)S(1)}, bf16[256,256]{1,0:T(8,128)(2,1)S(1)}, u32[]{:S(2)}, u32[]{:S(2)}) %collective-permute-start.3) | collective-permute-done | bytes 131104 | tf_op jit(solution)/shard_map/ppermute | solution.py:39
  38.0 1.2 collective-permute-done.5
  39.3 9.9 %mix.1 = (bf16[128,4096]{1,0:T(8,128)(2,1)}, bf16[128,4096]{1,0:T(8,128)(2,1)}) custom-call(f32[256,128]{1,0:T(8,128)S(1)} %convert_element_type.57.lines_ref, bf16[128,4096]{1,0:T(8,128)(2,1)S(1)} %collective-permute-done.1.prev_ref, bf16[128,4096]{1,0:T(8,128)(2,1)} %get-tuple-element.103.cur_ref, bf16[128,4096]{1,0:T(8,128)(2,1)} %get-tuple-element.107.query_ref), custom_call_target="tpu_custom_call" | custom-call | bytes 1048576 | tf_op jit(solution)/shard_map/mix/pallas_call | solution.py:64
  49.3 2.9 %collective-permute-start.6 = (bf16[256,256]{1,0:T(8,128)(2,1)S(1)}, bf16[256,256]{1,0:T(8,128)(2,1)S(1)}, u32[]{:S(2)}, u32[]{:S(2)}) collective-permute-start(bf16[256,256]{1,0:T(8,128)(2,1)S(1)} %slice.57), channel_id=1, source_target_pairs={{0,8},{8,0},{1,9},{9,1},{2,10},{10,2},{3,11},{11,3},{4,12},{12,4},... | collective-permute-start | bytes 393224 | tf_op jit(solution)/shard_map/ppermute | solution.py:39
  53.0 1.7 collective-permute-done.6
  54.7 1.6 collective-permute-done.7
  56.3 1.3 collective-permute-done.8
  57.7 1.5 collective-permute-start.12
  59.4 1.6 collective-permute-start.14
  61.1 3.0 %collective-permute-start.10 = (bf16[4,256,256]{2,1,0:T(8,128)(2,1)S(1)}, bf16[4,256,256]{2,1,0:T(8,128)(2,1)}, u32[]{:S(2)}, u32[]{:S(2)}) collective-permute-start(bf16[4,256,256]{2,1,0:T(8,128)(2,1)S(1)} %pad_maximum_fusion.1.refs_1_.refs_0_), channel_id=1, source_target_pairs={{0,64},{32,96},{64,0},{96,32},{1,65},{33,97},{65,1},{97,33},{2,66}... | collective-permute-start | bytes 1572872 | tf_op jit(solution)/shard_map/ppermute | solution.py:39
  64.8 5.4 %collective-permute-done.12.refs_6_.refs_5_ = bf16[4,256,256]{2,1,0:T(8,128)(2,1)S(1)} collective-permute-done((bf16[4,256,256]{2,1,0:T(8,128)(2,1)S(1)}, bf16[4,256,256]{2,1,0:T(8,128)(2,1)S(1)}, u32[]{:S(2)}, u32[]{:S(2)}) %collective-permute-start.12) | collective-permute-done | bytes 524320 | tf_op jit(solution)/shard_map/ppermute | solution.py:39
  70.2 1.3 collective-permute-start.9
  71.5 1.0 copy.17
  72.5 2.6 %fusion.11 = (bf16[512,1024]{1,0:T(8,128)(2,1)S(1)}, bf16[1024,512]{0,1:T(8,128)(2,1)}) fusion(bf16[1024,256]{0,1:T(8,128)(2,1)} %copy-done.10, bf16[1024,256]{0,1:T(8,128)(2,1)} %bitcast.47), kind=kLoop, calls=%fused_computation.61 | loop fusion | flops 2097152 | bytes 3145728 | tf_op jit(solution)/shard_map/transpose | solution.py:729
  75.1 1.5 copy.18.refs_0_
  77.1 2.8 %collective-permute-done.9.refs_2_.refs_1_ = bf16[4,256,256]{2,1,0:T(8,128)(2,1)} collective-permute-done((bf16[4,256,256]{2,1,0:T(8,128)(2,1)S(1)}, bf16[4,256,256]{2,1,0:T(8,128)(2,1)}, u32[]{:S(2)}, u32[]{:S(2)}) %collective-permute-start.9) | collective-permute-done | bytes 524320 | tf_op jit(solution)/shard_map/ppermute | solution.py:39
  79.9 1.1 copy-done.5
  80.9 8.5 %gate_matmul.1 = bf16[1024,4096]{1,0:T(8,128)(2,1)} custom-call(bf16[1024,512]{1,0:T(8,128)(2,1)S(1)} %copy.18.refs_0_, bf16[4,256,256]{2,1,0:T(8,128)(2,1)S(1)} %pad_maximum_fusion.1.refs_1_.refs_0_, bf16[4,256,256]{2,1,0:T(8,128)(2,1)} %collective-permute-done.9.refs_2_.refs_1_, bf16[4,256,256]{2,1,0:T(8,128)(2,1)} %collective-permute-done.10.refs_3_.refs_2_, ...), custom_call_target="tpu_custom_call" | custom-call | flops 4294967296 | bytes 12582912 | tf_op jit(solution)/shard_map/gate_matmul/pallas_call | solution.py:64
  89.4 22.9 %all-gather.2.cloned.1.call-done.rows_ref = bf16[1024,4096]{1,0:T(8,128)(2,1)} async-done(((bf16[128,4096]{1,0:T(8,128)(2,1)}), bf16[1024,4096]{1,0:T(8,128)(2,1)}) %all-gather.2.cloned.1.call-update) | async-done | bytes 8388624 | tf_op jit(solution)/shard_map/all_gather | solution.py:721
  112.4 9.9 %weight_grad.1 = (bf16[4,256,256]{2,1,0:T(8,128)(2,1)}, bf16[4,256,256]{2,1,0:T(8,128)(2,1)}, bf16[4,256,256]{2,1,0:T(8,128)(2,1)}, bf16[4,256,256]{2,1,0:T(8,12...) custom-call(s32[8]{0:T(128)S(1)} %fusion.2.origin.place, ...), custom_call_target="tpu_custom_call" | custom-call | flops 4294967296 | bytes 12582912 | tf_op jit(solution)/shard_map/weight_grad/pallas_call | solution.py:64
  122.3 2.7 %collective-permute-start.18 = (bf16[4,256,256]{2,1,0:T(8,128)(2,1)}, bf16[4,256,256]{2,1,0:T(8,128)(2,1)S(1)}, u32[]{:S(2)}, u32[]{:S(2)}) collective-permute-start(bf16[4,256,256]{2,1,0:T(8,128)(2,1)} %get-tuple-element.132), channel_id=1, source_target_pairs={{0,8},{8,0},{1,9},{9,1},{2,10},{10,2},{3,11},{11,3},{4,12},{12,4},... | collective-permute-start | bytes 1572872 | tf_op jit(solution)/shard_map/ppermute | solution.py:39
  125.9 2.5 collective-permute-start.15
  128.9 8.5 %collective-permute-done.18 = bf16[4,256,256]{2,1,0:T(8,128)(2,1)S(1)} collective-permute-done((bf16[4,256,256]{2,1,0:T(8,128)(2,1)}, bf16[4,256,256]{2,1,0:T(8,128)(2,1)S(1)}, u32[]{:S(2)}, u32[]{:S(2)}) %collective-permute-start.18) | collective-permute-done | bytes 524320 | tf_op jit(solution)/shard_map/ppermute | solution.py:39
  137.3 1.2 collective-permute-start.17
  138.5 10.0 %output.1 = (bf16[1024,256]{1,0:T(8,128)(2,1)}, bf16[1024,256]{1,0:T(8,128)(2,1)}) custom-call(s32[8]{0:T(128)S(1)} %fusion.2.origin.place, bf16[1024,4096]{1,0:T(8,128)(2,1)} %all-gather.2.cloned.1.call-done.rows_ref, bf16[4,256,256]{2,1,0:T(8,128)(2,1)S(1)} %pad_maximum_fusion.1.refs_1_.refs_0_, ...), custom_call_target="tpu_custom_call" | custom-call | flops 4294967296 | bytes 12582912 | tf_op jit(solution)/shard_map/output/pallas_call | solution.py:64
  149.5 5.2 %collective-permute-done.17 = bf16[4,256,256]{2,1,0:T(8,128)(2,1)S(1)} collective-permute-done((bf16[4,256,256]{2,1,0:T(8,128)(2,1)}, bf16[4,256,256]{2,1,0:T(8,128)(2,1)S(1)}, u32[]{:S(2)}, u32[]{:S(2)}) %collective-permute-start.17) | collective-permute-done | bytes 524320 | tf_op jit(solution)/shard_map/ppermute | solution.py:39
  155.0 2.5 collective-permute-start.21
  158.8 1.6 collective-permute-done.21
  160.4 2.9 %collective-permute-done.22 = bf16[256,256]{1,0:T(8,128)(2,1)S(1)} collective-permute-done((bf16[256,256]{1,0:T(8,128)(2,1)S(1)}, bf16[256,256]{1,0:T(8,128)(2,1)S(1)}, u32[]{:S(2)}, u32[]{:S(2)}) %collective-permute-start.22) | collective-permute-done | bytes 131104 | tf_op jit(solution)/shard_map/ppermute | solution.py:39
  163.3 1.0 collective-permute-done.23
  164.3 1.7 collective-permute-done.26
  166.3 3.6 %gate_back.1 = (bf16[128,4096]{1,0:T(8,128)(2,1)}, bf16[128,4096]{1,0:T(8,128)(2,1)}) custom-call(s32[8]{0:T(128)S(1)} %fusion.2.origin.place, bf16[128,4096]{1,0:T(8,128)(2,1)} %reduce-scatter.2.cloned.1.call-done.gate_grad_ref, bf16[128,4096]{1,0:T(8,128)(2,1)} %get-tuple-element.107.query_ref, bf16[128,4096]{1,0:T(8,128)(2,1)} %get-tuple-element.140.mixed_ref), custom_call_target="tpu_custom_call" | custom-call | flops 1048576 | bytes 5242880 | tf_op jit(solution)/shard_map/gate_back/pallas_call | solution.py:64
  169.9 5.6 %collective-permute-start.27 = (bf16[128,4096]{1,0:T(8,128)(2,1)}, bf16[128,4096]{1,0:T(8,128)(2,1)S(1)}, u32[]{:S(2)}, u32[]{:S(2)}) collective-permute-start(bf16[128,4096]{1,0:T(8,128)(2,1)} %get-tuple-element.141.grad_ref), channel_id=1, source_target_pairs={{1,0},{2,1},{3,2},{4,3},{5,4},{6,5},{7,6},{8,7},{9,8},{10,9},{11,1... | collective-permute-start | bytes 3145736 | tf_op jit(solution)/shard_map/ppermute | solution.py:27
  175.5 2.8 %collective-permute-start.28 = (bf16[1024,256]{1,0:T(8,128)(2,1)}, bf16[1024,256]{1,0:T(8,128)(2,1)S(1)}, u32[]{:S(2)}, u32[]{:S(2)}) collective-permute-start(bf16[1024,256]{1,0:T(8,128)(2,1)} %get-tuple-element.157), channel_id=1, source_target_pairs={{0,8},{8,0},{1,9},{9,1},{2,10},{10,2},{3,11},{11,3},{4,12},{12,4},... | collective-permute-start | bytes 1572872 | tf_op jit(solution)/shard_map/ppermute | solution.py:39
  178.5 9.1 %long_grad.1 = (f32[256,128]{1,0:T(8,128)S(1)}, f32[8,4096]{1,0:T(8,128)S(1)}) custom-call(bf16[128,4096]{1,0:T(8,128)(2,1)} %copy-done.3, bf16[128,4096]{1,0:T(8,128)(2,1)} %get-tuple-element.103.cur_ref, bf16[128,4096]{1,0:T(8,128)(2,1)} %get-tuple-element.141.grad_ref, bf16[128,4096]{1,0:T(8,128)(2,1)} %get-tuple-element.142.feature_ref.query_grad_ref, ...), custom_call_target="tpu_custom_call" | custom-call | flops 2147483648 | bytes 5242880 | tf_op jit(solution)/shard_map/long_grad/pallas_call | solution.py:64
  188.5 11.3 %unmix.1 = (bf16[2,128,4096]{2,1,0:T(8,128)(2,1)}, f32[8,4096]{1,0:T(8,128)S(1)}, f32[8,4096]{1,0:T(8,128)S(1)}, bf16[3,8,4096]{2,1,0:T(8,128)(2,1)S(1)}) custom-call(f32[256,128]{1,0:T(8,128)S(1)} %convert_element_type.57.lines_ref, bf16[128,4096]{1,0:T(8,128)(2,1)} %get-tuple-element.141.grad_ref, bf16[128,4096]{1,0:T(8,128)(2,1)S(1)} %collective-permute-done.27.next_ref, ...), custom_call_target="tpu_custom_call" | custom-call | flops 2147483648 | bytes 8388608 | tf_op jit(solution)/shard_map/unmix/pallas_call | solution.py:64
  200.5 2.7 %collective-permute-start.29 = (f32[64,8,128]{2,1,0:T(8,128)S(1)}, f32[64,8,128]{2,1,0:T(8,128)S(1)}, u32[]{:S(2)}, u32[]{:S(2)}) collective-permute-start(f32[64,8,128]{2,1,0:T(8,128)S(1)} %get-tuple-element.162), channel_id=1, source_target_pairs={{0,1},{1,0},{2,3},{3,2},{4,5},{5,4},{6,7},{7,6},{8,9},{9,8},{10,11... | collective-permute-start | bytes 786440 | tf_op jit(solution)/shard_map/ppermute | solution.py:39
  203.3 1.2 collective-permute-done.29
  204.6 9.0 %collective-permute-start.31 = (f32[16,8,128]{2,1,0:T(8,128)S(1)}, f32[16,8,128]{2,1,0:T(8,128)S(1)}, u32[]{:S(2)}, u32[]{:S(2)}) collective-permute-start(f32[16,8,128]{2,1,0:T(8,128)S(1)} %get-tuple-element.198), channel_id=1, source_target_pairs={{0,4},{2,6},{4,0},{6,2},{1,5},{3,7},{5,1},{7,3},{8,12},{10,14},{12... | collective-permute-start | bytes 196616 | tf_op jit(solution)/shard_map/ppermute | solution.py:39
  213.5 2.6 %collective-permute-start.36 = (bf16[3,8,4096]{2,1,0:T(8,128)(2,1)S(1)}, bf16[3,8,4096]{2,1,0:T(8,128)(2,1)S(1)}, u32[]{:S(2)}, u32[]{:S(2)}) collective-permute-start(bf16[3,8,4096]{2,1,0:T(8,128)(2,1)S(1)} %get-tuple-element.163), channel_id=1, source_target_pairs={{1,0},{2,1},{3,2},{4,3},{5,4},{6,5},{7,6},{8,7},{9,8},{10,9},{11,1... | collective-permute-start | bytes 589832 | tf_op jit(solution)/shard_map/ppermute | solution.py:27
  217.1 1.9 collective-permute-start.34
  219.1 1.1 collective-permute-start.35
  221.1 3.2 %short_adjoint.3.refs_0_ = bf16[128,12288]{1,0:T(8,128)(2,1)} custom-call(bf16[1,128,4096]{2,1,0:T(8,128)(2,1)} %bitcast.46, bf16[3,8,4096]{2,1,0:T(8,128)(2,1)S(1)} %collective-permute-done.36.rim_ref, f32[7,12288]{1,0:T(8,128)} %filter_ref.5), custom_call_target="tpu_custom_call" | custom-call | flops 7340032 | bytes 2097152 | tf_op jit(solution)/shard_map/short_adjoint/pallas_call | solution.py:64
  224.9 2.9 %collective-permute-start.39 = (f32[16,8,128]{2,1,0:T(8,128)S(1)}, f32[16,8,128]{2,1,0:T(8,128)S(1)}, u32[]{:S(2)}, u32[]{:S(2)}) collective-permute-start(f32[16,8,128]{2,1,0:T(8,128)S(1)} %add_add_fusion.1), channel_id=1, source_target_pairs={{0,24},{8,16},{16,8},{24,0},{1,25},{9,17},{17,9},{25,1},{2,26},{10... | collective-permute-start | bytes 196616 | tf_op jit(solution)/shard_map/ppermute | solution.py:39
  227.7 1.2 maximum_select_fusion
  229.0 3.2 %short_adjoint.4.refs_0_ = bf16[128,12288]{1,0:T(8,128)(2,1)} custom-call(bf16[2,128,4096]{2,1,0:T(8,128)(2,1)} %get-tuple-element.168.grads_ref, bf16[3,8,4096]{2,1,0:T(8,128)(2,1)S(1)} %collective-permute-done.36.rim_ref, f32[7,12288]{1,0:T(8,128)} %filter_ref.5, bf16[128,12288]{1,0:T(8,128)(2,1)} %short_adjoint.3.refs_0_), custom_call_target="tpu_custom_call", output_to_operand_aliasing={{}: (3, {})} | custom-call | flops 7340032 | bytes 2097152 | tf_op jit(solution)/shard_map/short_adjoint/pallas_call | solution.py:64
  232.2 2.4 collective-permute-start.40
  234.6 0.9 collective-permute-done.40
  235.5 1.4 collective-permute-start.41
  237.7 1.0 copy.19
  238.7 3.3 %short_adjoint.5 = bf16[128,12288]{1,0:T(8,128)(2,1)} custom-call(bf16[2,128,4096]{2,1,0:T(8,128)(2,1)} %get-tuple-element.168.grads_ref, bf16[3,8,4096]{2,1,0:T(8,128)(2,1)S(1)} %collective-permute-done.36.rim_ref, f32[7,12288]{1,0:T(8,128)} %filter_ref.5, bf16[128,12288]{1,0:T(8,128)(2,1)} %short_adjoint.4.refs_0_), custom_call_target="tpu_custom_call", output_to_operand_aliasing={{}: (3, {})} | custom-call | flops 7340032 | bytes 2097152 | tf_op jit(solution)/shard_map/short_adjoint/pallas_call | solution.py:64
  242.0 0.9 collective-permute-done.42.refs_2_
  242.9 3.8 %collective-permute-done.43.refs_3_ = f32[32,8,128]{2,1,0:T(8,128)S(1)} collective-permute-done((f32[32,8,128]{2,1,0:T(8,128)S(1)}, f32[32,8,128]{2,1,0:T(8,128)S(1)}, u32[]{:S(2)}, u32[]{:S(2)}) %collective-permute-start.43) | collective-permute-done | bytes 131104 | tf_op jit(solution)/shard_map/ppermute | solution.py:39
  246.7 1.5 collect.1
  (105 shorter events, 13.1 us)
Async XLA Ops:
  7.2 17.3 %copy-start = (bf16[1,2048,256]{2,1,0:T(8,128)(2,1)S(1)}, bf16[1,2048,256]{2,1,0:T(8,128)(2,1)}, u32[]{:S(2)}) copy-start(bf16[1,2048,256]{2,1,0:T(8,128)(2,1)} %param.9) | copy-start | bytes 3145732
  7.2 105.2 %all-gather.2.cloned.1.call-start = ((), (), s32[]{:S(2)}) async-start(), calls=%async_computation.1 | async-start | bytes 9437184 | tf_op jit(solution)/shard_map/all_gather | solution.py:721
  8.3 11.7 %collective-permute-start = (bf16[8,12288]{1,0:T(8,128)(2,1)S(1)}, bf16[8,12288]{1,0:T(8,128)(2,1)S(1)}, u32[]{:S(2)}, u32[]{:S(2)}) collective-permute-start(bf16[8,12288]{1,0:T(8,128)(2,1)S(1)} %slice_bitcast_fusion), channel_id=1, source_target_pairs={{0,1},{1,2},{2,3},{3,4},{4,5},{5,6},{6,7},{7,8},{8,9},{9,10},{10,1... | collective-permute-start | bytes 589832 | tf_op jit(solution)/shard_map/ppermute | solution.py:27
  19.9 2.6 %copy-start.2 = (bf16[8,12288]{1,0:T(8,128)(2,1)}, bf16[8,12288]{1,0:T(8,128)(2,1)S(1)}, u32[]{:S(2)}) copy-start(bf16[8,12288]{1,0:T(8,128)(2,1)S(1)} %collective-permute-done.refs_3_.refs_4_.refs_5_.rim_ref.key_rim_ref.value_rim_ref) | copy-start | bytes 589828
  22.5 16.7 %collective-permute-start.1 = (bf16[128,4096]{1,0:T(8,128)(2,1)}, bf16[128,4096]{1,0:T(8,128)(2,1)S(1)}, u32[]{:S(2)}, u32[]{:S(2)}) collective-permute-start(bf16[128,4096]{1,0:T(8,128)(2,1)} %get-tuple-element.103.cur_ref), channel_id=1, source_target_pairs={{0,1},{1,2},{2,3},{3,4},{4,5},{5,6},{6,7},{7,8},{8,9},{9,10},{10,1... | collective-permute-start | bytes 3145736 | tf_op jit(solution)/shard_map/ppermute | solution.py:27
  24.7 14.5 %collective-permute-start.5 = (bf16[1024,256]{0,1:T(8,128)(2,1)S(1)}, bf16[1024,256]{0,1:T(8,128)(2,1)S(1)}, u32[]{:S(2)}, u32[]{:S(2)}) collective-permute-start(bf16[1024,256]{0,1:T(8,128)(2,1)S(1)} %bitcast.49), channel_id=1, source_target_pairs={{0,8},{8,0},{1,9},{9,1},{2,10},{10,2},{3,11},{11,3},{4,12},{12,4},... | collective-permute-start | bytes 1572872 | tf_op jit(solution)/shard_map/ppermute | solution.py:39
  28.4 5.9 %collective-permute-start.2 = (bf16[256,256]{1,0:T(8,128)(2,1)S(1)}, bf16[256,256]{1,0:T(8,128)(2,1)S(1)}, u32[]{:S(2)}, u32[]{:S(2)}) collective-permute-start(bf16[256,256]{1,0:T(8,128)(2,1)S(1)} %slice.56), channel_id=1, source_target_pairs={{0,32},{32,64},{64,96},{96,0},{1,33},{33,65},{65,97},{97,1},{2,34}... | collective-permute-start | bytes 393224 | tf_op jit(solution)/shard_map/ppermute | solution.py:39
  29.8 8.2 %collective-permute-start.3 = (bf16[256,256]{1,0:T(8,128)(2,1)S(1)}, bf16[256,256]{1,0:T(8,128)(2,1)S(1)}, u32[]{:S(2)}, u32[]{:S(2)}) collective-permute-start(bf16[256,256]{1,0:T(8,128)(2,1)S(1)} %slice.56), channel_id=1, source_target_pairs={{0,64},{32,96},{64,0},{96,32},{1,65},{33,97},{65,1},{97,33},{2,66}... | collective-permute-start | bytes 393224 | tf_op jit(solution)/shard_map/ppermute | solution.py:39
  32.4 5.6 %collective-permute-start.4 = (bf16[256,256]{1,0:T(8,128)(2,1)S(1)}, bf16[256,256]{1,0:T(8,128)(2,1)S(1)}, u32[]{:S(2)}, u32[]{:S(2)}) collective-permute-start(bf16[256,256]{1,0:T(8,128)(2,1)S(1)} %slice.56), channel_id=1, source_target_pairs={{0,96},{32,0},{64,32},{96,64},{1,97},{33,1},{65,33},{97,65},{2,98}... | collective-permute-start | bytes 393224 | tf_op jit(solution)/shard_map/ppermute | solution.py:39
  38.0 1.2 copy-start.12
  38.0 1.2 copy-start.14
  39.2 18.4 %copy-start.10 = (bf16[1024,256]{0,1:T(8,128)(2,1)}, bf16[1024,256]{0,1:T(8,128)(2,1)S(1)}, u32[]{:S(2)}) copy-start(bf16[1024,256]{0,1:T(8,128)(2,1)S(1)} %collective-permute-done.5) | copy-start | bytes 1572868
  39.2 10.0 %copy-start.3 = (bf16[128,4096]{1,0:T(8,128)(2,1)}, bf16[128,4096]{1,0:T(8,128)(2,1)S(1)}, u32[]{:S(2)}) copy-start(bf16[128,4096]{1,0:T(8,128)(2,1)S(1)} %collective-permute-done.1.prev_ref) | copy-start | bytes 3145732
  39.2 10.1 %copy-start.11 = (bf16[512,256]{1,0:T(8,128)(2,1)S(1)}, bf16[512,256]{1,0:T(8,128)(2,1)}, u32[]{:S(2)}) copy-start(bf16[512,256]{1,0:T(8,128)(2,1)} %param.8) | copy-start | bytes 786436
  39.3 18.3 %copy-start.13 = (bf16[256,256]{1,0:T(8,128)(2,1)S(1)}, bf16[256,256]{1,0:T(8,128)(2,1)}, u32[]{:S(2)}) copy-start(bf16[256,256]{1,0:T(8,128)(2,1)} %copy-done.12) | copy-start | bytes 393220
  39.3 18.3 %copy-start.15 = (bf16[256,256]{1,0:T(8,128)(2,1)S(1)}, bf16[256,256]{1,0:T(8,128)(2,1)}, u32[]{:S(2)}) copy-start(bf16[256,256]{1,0:T(8,128)(2,1)} %copy-done.14) | copy-start | bytes 393220
  49.3 117.0 %reduce-scatter.2.cloned.1.call-start = ((), (), s32[]{:S(2)}) async-start(), calls=%async_computation.2 | async-start | bytes 9437184 | tf_op jit(solution)/shard_map/reduce_scatter | solution.py:727
  49.3 5.4 %collective-permute-start.6 = (bf16[256,256]{1,0:T(8,128)(2,1)S(1)}, bf16[256,256]{1,0:T(8,128)(2,1)S(1)}, u32[]{:S(2)}, u32[]{:S(2)}) collective-permute-start(bf16[256,256]{1,0:T(8,128)(2,1)S(1)} %slice.57), channel_id=1, source_target_pairs={{0,8},{8,0},{1,9},{9,1},{2,10},{10,2},{3,11},{11,3},{4,12},{12,4},... | collective-permute-start | bytes 393224 | tf_op jit(solution)/shard_map/ppermute | solution.py:39
  52.2 4.1 %collective-permute-start.7 = (bf16[256,256]{1,0:T(8,128)(2,1)S(1)}, bf16[256,256]{1,0:T(8,128)(2,1)S(1)}, u32[]{:S(2)}, u32[]{:S(2)}) collective-permute-start(bf16[256,256]{1,0:T(8,128)(2,1)S(1)} %slice.57), channel_id=1, source_target_pairs={{0,16},{16,0},{1,17},{17,1},{2,18},{18,2},{3,19},{19,3},{4,20},{20... | collective-permute-start | bytes 393224 | tf_op jit(solution)/shard_map/ppermute | solution.py:39
  52.5 5.0 %collective-permute-start.8 = (bf16[256,256]{1,0:T(8,128)(2,1)S(1)}, bf16[256,256]{1,0:T(8,128)(2,1)S(1)}, u32[]{:S(2)}, u32[]{:S(2)}) collective-permute-start(bf16[256,256]{1,0:T(8,128)(2,1)S(1)} %slice.57), channel_id=1, source_target_pairs={{0,24},{8,16},{16,8},{24,0},{1,25},{9,17},{17,9},{25,1},{2,26},{10... | collective-permute-start | bytes 393224 | tf_op jit(solution)/shard_map/ppermute | solution.py:39
  57.7 12.5 %collective-permute-start.12 = (bf16[4,256,256]{2,1,0:T(8,128)(2,1)S(1)}, bf16[4,256,256]{2,1,0:T(8,128)(2,1)S(1)}, u32[]{:S(2)}, u32[]{:S(2)}) collective-permute-start(bf16[4,256,256]{2,1,0:T(8,128)(2,1)S(1)} %pad_maximum_fusion.2.refs_5_.refs_4_), channel_id=1, source_target_pairs={{0,8},{8,0},{1,9},{9,1},{2,10},{10,2},{3,11},{11,3},{4,12},{12,4},... | collective-permute-start | bytes 1572872 | tf_op jit(solution)/shard_map/ppermute | solution.py:39
  59.1 17.5 %collective-permute-start.13 = (bf16[4,256,256]{2,1,0:T(8,128)(2,1)S(1)}, bf16[4,256,256]{2,1,0:T(8,128)(2,1)}, u32[]{:S(2)}, u32[]{:S(2)}) collective-permute-start(bf16[4,256,256]{2,1,0:T(8,128)(2,1)S(1)} %pad_maximum_fusion.2.refs_5_.refs_4_), channel_id=1, source_target_pairs={{0,16},{16,0},{1,17},{17,1},{2,18},{18,2},{3,19},{19,3},{4,20},{20... | collective-permute-start | bytes 1572872 | tf_op jit(solution)/shard_map/ppermute | solution.py:39
  59.4 17.2 %collective-permute-start.14 = (bf16[4,256,256]{2,1,0:T(8,128)(2,1)S(1)}, bf16[4,256,256]{2,1,0:T(8,128)(2,1)}, u32[]{:S(2)}, u32[]{:S(2)}) collective-permute-start(bf16[4,256,256]{2,1,0:T(8,128)(2,1)S(1)} %pad_maximum_fusion.2.refs_5_.refs_4_), channel_id=1, source_target_pairs={{0,24},{8,16},{16,8},{24,0},{1,25},{9,17},{17,9},{25,1},{2,26},{10... | collective-permute-start | bytes 1572872 | tf_op jit(solution)/shard_map/ppermute | solution.py:39
  61.1 15.6 %collective-permute-start.10 = (bf16[4,256,256]{2,1,0:T(8,128)(2,1)S(1)}, bf16[4,256,256]{2,1,0:T(8,128)(2,1)}, u32[]{:S(2)}, u32[]{:S(2)}) collective-permute-start(bf16[4,256,256]{2,1,0:T(8,128)(2,1)S(1)} %pad_maximum_fusion.1.refs_1_.refs_0_), channel_id=1, source_target_pairs={{0,64},{32,96},{64,0},{96,32},{1,65},{33,97},{65,1},{97,33},{2,66}... | collective-permute-start | bytes 1572872 | tf_op jit(solution)/shard_map/ppermute | solution.py:39
  64.1 13.0 %collective-permute-start.11 = (bf16[4,256,256]{2,1,0:T(8,128)(2,1)S(1)}, bf16[4,256,256]{2,1,0:T(8,128)(2,1)}, u32[]{:S(2)}, u32[]{:S(2)}) collective-permute-start(bf16[4,256,256]{2,1,0:T(8,128)(2,1)S(1)} %pad_maximum_fusion.1.refs_1_.refs_0_), channel_id=1, source_target_pairs={{0,96},{32,0},{64,32},{96,64},{1,97},{33,1},{65,33},{97,65},{2,98}... | collective-permute-start | bytes 1572872 | tf_op jit(solution)/shard_map/ppermute | solution.py:39
  70.2 4.9 %copy-start.4 = (bf16[4,256,256]{2,1,0:T(8,128)(2,1)}, bf16[4,256,256]{2,1,0:T(8,128)(2,1)S(1)}, u32[]{:S(2)}) copy-start(bf16[4,256,256]{2,1,0:T(8,128)(2,1)S(1)} %collective-permute-done.12.refs_6_.refs_5_) | copy-start | bytes 1572868
  70.2 9.7 %collective-permute-start.9 = (bf16[4,256,256]{2,1,0:T(8,128)(2,1)S(1)}, bf16[4,256,256]{2,1,0:T(8,128)(2,1)}, u32[]{:S(2)}, u32[]{:S(2)}) collective-permute-start(bf16[4,256,256]{2,1,0:T(8,128)(2,1)S(1)} %pad_maximum_fusion.1.refs_1_.refs_0_), channel_id=1, source_target_pairs={{0,32},{32,64},{64,96},{96,0},{1,33},{33,65},{65,97},{97,1},{2,34}... | collective-permute-start | bytes 1572872 | tf_op jit(solution)/shard_map/ppermute | solution.py:39
  79.9 1.1 copy-start.5
  112.4 26.1 %copy-start.6 = (bf16[4,256,256]{2,1,0:T(8,128)(2,1)S(1)}, bf16[4,256,256]{2,1,0:T(8,128)(2,1)}, u32[]{:S(2)}) copy-start(bf16[4,256,256]{2,1,0:T(8,128)(2,1)} %copy-done.4) | copy-start | bytes 1572868
  122.3 15.0 %collective-permute-start.18 = (bf16[4,256,256]{2,1,0:T(8,128)(2,1)}, bf16[4,256,256]{2,1,0:T(8,128)(2,1)S(1)}, u32[]{:S(2)}, u32[]{:S(2)}) collective-permute-start(bf16[4,256,256]{2,1,0:T(8,128)(2,1)} %get-tuple-element.132), channel_id=1, source_target_pairs={{0,8},{8,0},{1,9},{9,1},{2,10},{10,2},{3,11},{11,3},{4,12},{12,4},... | collective-permute-start | bytes 1572872 | tf_op jit(solution)/shard_map/ppermute | solution.py:39
  125.0 23.7 %collective-permute-start.19 = (bf16[4,256,256]{2,1,0:T(8,128)(2,1)}, bf16[4,256,256]{2,1,0:T(8,128)(2,1)S(1)}, u32[]{:S(2)}, u32[]{:S(2)}) collective-permute-start(bf16[4,256,256]{2,1,0:T(8,128)(2,1)} %get-tuple-element.133), channel_id=1, source_target_pairs={{0,16},{16,0},{1,17},{17,1},{2,18},{18,2},{3,19},{19,3},{4,20},{20... | collective-permute-start | bytes 1572872 | tf_op jit(solution)/shard_map/ppermute | solution.py:39
  125.3 23.9 %collective-permute-start.20 = (bf16[4,256,256]{2,1,0:T(8,128)(2,1)}, bf16[4,256,256]{2,1,0:T(8,128)(2,1)S(1)}, u32[]{:S(2)}, u32[]{:S(2)}) collective-permute-start(bf16[4,256,256]{2,1,0:T(8,128)(2,1)} %get-tuple-element.134), channel_id=1, source_target_pairs={{0,24},{8,16},{16,8},{24,0},{1,25},{9,17},{17,9},{25,1},{2,26},{10... | collective-permute-start | bytes 1572872 | tf_op jit(solution)/shard_map/ppermute | solution.py:39
  125.9 23.6 %collective-permute-start.15 = (bf16[4,256,256]{2,1,0:T(8,128)(2,1)}, bf16[4,256,256]{2,1,0:T(8,128)(2,1)S(1)}, u32[]{:S(2)}, u32[]{:S(2)}) collective-permute-start(bf16[4,256,256]{2,1,0:T(8,128)(2,1)} %get-tuple-element.128), channel_id=1, source_target_pairs={{0,96},{32,0},{64,32},{96,64},{1,97},{33,1},{65,33},{97,65},{2,98}... | collective-permute-start | bytes 1572872 | tf_op jit(solution)/shard_map/ppermute | solution.py:39
  128.3 21.2 %collective-permute-start.16 = (bf16[4,256,256]{2,1,0:T(8,128)(2,1)}, bf16[4,256,256]{2,1,0:T(8,128)(2,1)S(1)}, u32[]{:S(2)}, u32[]{:S(2)}) collective-permute-start(bf16[4,256,256]{2,1,0:T(8,128)(2,1)} %get-tuple-element.129), channel_id=1, source_target_pairs={{0,64},{32,96},{64,0},{96,32},{1,65},{33,97},{65,1},{97,33},{2,66}... | collective-permute-start | bytes 1572872 | tf_op jit(solution)/shard_map/ppermute | solution.py:39
  137.3 11.9 %copy-start.9 = (bf16[4,256,256]{2,1,0:T(8,128)(2,1)S(1)}, bf16[4,256,256]{2,1,0:T(8,128)(2,1)}, u32[]{:S(2)}) copy-start(bf16[4,256,256]{2,1,0:T(8,128)(2,1)} %get-tuple-element.131) | copy-start | bytes 1572868
  137.3 17.4 %collective-permute-start.17 = (bf16[4,256,256]{2,1,0:T(8,128)(2,1)}, bf16[4,256,256]{2,1,0:T(8,128)(2,1)S(1)}, u32[]{:S(2)}, u32[]{:S(2)}) collective-permute-start(bf16[4,256,256]{2,1,0:T(8,128)(2,1)} %get-tuple-element.130), channel_id=1, source_target_pairs={{0,32},{32,64},{64,96},{96,0},{1,33},{33,65},{65,97},{97,1},{2,34}... | collective-permute-start | bytes 1572872 | tf_op jit(solution)/shard_map/ppermute | solution.py:39
  148.5 6.2 %copy-start.8 = (bf16[4,256,256]{2,1,0:T(8,128)(2,1)S(1)}, bf16[4,256,256]{2,1,0:T(8,128)(2,1)}, u32[]{:S(2)}) copy-start(bf16[4,256,256]{2,1,0:T(8,128)(2,1)} %get-tuple-element.127) | copy-start | bytes 1572868
  155.0 5.4 %collective-permute-start.21 = (bf16[256,256]{1,0:T(8,128)(2,1)S(1)}, bf16[256,256]{1,0:T(8,128)(2,1)S(1)}, u32[]{:S(2)}, u32[]{:S(2)}) collective-permute-start(bf16[256,256]{1,0:T(8,128)(2,1)S(1)} %get-tuple-element.194), channel_id=1, source_target_pairs={{0,8},{8,0},{1,9},{9,1},{2,10},{10,2},{3,11},{11,3},{4,12},{12,4},... | collective-permute-start | bytes 393224 | tf_op jit(solution)/shard_map/ppermute | solution.py:39
  157.5 5.8 %collective-permute-start.22 = (bf16[256,256]{1,0:T(8,128)(2,1)S(1)}, bf16[256,256]{1,0:T(8,128)(2,1)S(1)}, u32[]{:S(2)}, u32[]{:S(2)}) collective-permute-start(bf16[256,256]{1,0:T(8,128)(2,1)S(1)} %get-tuple-element.193), channel_id=1, source_target_pairs={{0,16},{16,0},{1,17},{17,1},{2,18},{18,2},{3,19},{19,3},{4,20},{20... | collective-permute-start | bytes 393224 | tf_op jit(solution)/shard_map/ppermute | solution.py:39
  157.8 6.5 %collective-permute-start.23 = (bf16[256,256]{1,0:T(8,128)(2,1)S(1)}, bf16[256,256]{1,0:T(8,128)(2,1)S(1)}, u32[]{:S(2)}, u32[]{:S(2)}) collective-permute-start(bf16[256,256]{1,0:T(8,128)(2,1)S(1)} %get-tuple-element.192), channel_id=1, source_target_pairs={{0,24},{8,16},{16,8},{24,0},{1,25},{9,17},{17,9},{25,1},{2,26},{10... | collective-permute-start | bytes 393224 | tf_op jit(solution)/shard_map/ppermute | solution.py:39
  158.4 5.9 %collective-permute-start.24 = (bf16[256,256]{1,0:T(8,128)(2,1)S(1)}, bf16[256,256]{1,0:T(8,128)(2,1)S(1)}, u32[]{:S(2)}, u32[]{:S(2)}) collective-permute-start(bf16[256,256]{1,0:T(8,128)(2,1)S(1)} %get-tuple-element.190), channel_id=1, source_target_pairs={{0,96},{32,0},{64,32},{96,64},{1,97},{33,1},{65,33},{97,65},{2,98}... | collective-permute-start | bytes 393224 | tf_op jit(solution)/shard_map/ppermute | solution.py:39
  158.5 5.8 %collective-permute-start.25 = (bf16[256,256]{1,0:T(8,128)(2,1)S(1)}, bf16[256,256]{1,0:T(8,128)(2,1)S(1)}, u32[]{:S(2)}, u32[]{:S(2)}) collective-permute-start(bf16[256,256]{1,0:T(8,128)(2,1)S(1)} %get-tuple-element.189), channel_id=1, source_target_pairs={{0,64},{32,96},{64,0},{96,32},{1,65},{33,97},{65,1},{97,33},{2,66}... | collective-permute-start | bytes 393224 | tf_op jit(solution)/shard_map/ppermute | solution.py:39
  160.4 5.6 %collective-permute-start.26 = (bf16[256,256]{1,0:T(8,128)(2,1)S(1)}, bf16[256,256]{1,0:T(8,128)(2,1)S(1)}, u32[]{:S(2)}, u32[]{:S(2)}) collective-permute-start(bf16[256,256]{1,0:T(8,128)(2,1)S(1)} %get-tuple-element.188), channel_id=1, source_target_pairs={{0,32},{32,64},{64,96},{96,0},{1,33},{33,65},{65,97},{97,1},{2,34}... | collective-permute-start | bytes 393224 | tf_op jit(solution)/shard_map/ppermute | solution.py:39
  169.9 18.6 %collective-permute-start.27 = (bf16[128,4096]{1,0:T(8,128)(2,1)}, bf16[128,4096]{1,0:T(8,128)(2,1)S(1)}, u32[]{:S(2)}, u32[]{:S(2)}) collective-permute-start(bf16[128,4096]{1,0:T(8,128)(2,1)} %get-tuple-element.141.grad_ref), channel_id=1, source_target_pairs={{1,0},{2,1},{3,2},{4,3},{5,4},{6,5},{7,6},{8,7},{9,8},{10,9},{11,1... | collective-permute-start | bytes 3145736 | tf_op jit(solution)/shard_map/ppermute | solution.py:27
  175.5 24.3 %collective-permute-start.28 = (bf16[1024,256]{1,0:T(8,128)(2,1)}, bf16[1024,256]{1,0:T(8,128)(2,1)S(1)}, u32[]{:S(2)}, u32[]{:S(2)}) collective-permute-start(bf16[1024,256]{1,0:T(8,128)(2,1)} %get-tuple-element.157), channel_id=1, source_target_pairs={{0,8},{8,0},{1,9},{9,1},{2,10},{10,2},{3,11},{11,3},{4,12},{12,4},... | collective-permute-start | bytes 1572872 | tf_op jit(solution)/shard_map/ppermute | solution.py:39
  200.5 3.9 %collective-permute-start.29 = (f32[64,8,128]{2,1,0:T(8,128)S(1)}, f32[64,8,128]{2,1,0:T(8,128)S(1)}, u32[]{:S(2)}, u32[]{:S(2)}) collective-permute-start(f32[64,8,128]{2,1,0:T(8,128)S(1)} %get-tuple-element.162), channel_id=1, source_target_pairs={{0,1},{1,0},{2,3},{3,2},{4,5},{5,4},{6,7},{7,6},{8,9},{9,8},{10,11... | collective-permute-start | bytes 786440 | tf_op jit(solution)/shard_map/ppermute | solution.py:39
  204.5 11.7 %collective-permute-start.30 = (f32[16,8,128]{2,1,0:T(8,128)S(1)}, f32[16,8,128]{2,1,0:T(8,128)S(1)}, u32[]{:S(2)}, u32[]{:S(2)}) collective-permute-start(f32[16,8,128]{2,1,0:T(8,128)S(1)} %get-tuple-element.196), channel_id=1, source_target_pairs={{0,2},{2,4},{4,6},{6,0},{1,3},{3,5},{5,7},{7,1},{8,10},{10,12},{12... | collective-permute-start | bytes 196616 | tf_op jit(solution)/shard_map/ppermute | solution.py:39
  204.6 12.5 %collective-permute-start.31 = (f32[16,8,128]{2,1,0:T(8,128)S(1)}, f32[16,8,128]{2,1,0:T(8,128)S(1)}, u32[]{:S(2)}, u32[]{:S(2)}) collective-permute-start(f32[16,8,128]{2,1,0:T(8,128)S(1)} %get-tuple-element.198), channel_id=1, source_target_pairs={{0,4},{2,6},{4,0},{6,2},{1,5},{3,7},{5,1},{7,3},{8,12},{10,14},{12... | collective-permute-start | bytes 196616 | tf_op jit(solution)/shard_map/ppermute | solution.py:39
  213.5 3.5 %collective-permute-start.32 = (f32[16,8,128]{2,1,0:T(8,128)S(1)}, f32[16,8,128]{2,1,0:T(8,128)S(1)}, u32[]{:S(2)}, u32[]{:S(2)}) collective-permute-start(f32[16,8,128]{2,1,0:T(8,128)S(1)} %get-tuple-element.197), channel_id=1, source_target_pairs={{0,6},{2,0},{4,2},{6,4},{1,7},{3,1},{5,3},{7,5},{8,14},{10,8},{12,... | collective-permute-start | bytes 196616 | tf_op jit(solution)/shard_map/ppermute | solution.py:39
  213.5 7.6 %collective-permute-start.36 = (bf16[3,8,4096]{2,1,0:T(8,128)(2,1)S(1)}, bf16[3,8,4096]{2,1,0:T(8,128)(2,1)S(1)}, u32[]{:S(2)}, u32[]{:S(2)}) collective-permute-start(bf16[3,8,4096]{2,1,0:T(8,128)(2,1)S(1)} %get-tuple-element.163), channel_id=1, source_target_pairs={{1,0},{2,1},{3,2},{4,3},{5,4},{6,5},{7,6},{8,7},{9,8},{10,9},{11,1... | collective-permute-start | bytes 589832 | tf_op jit(solution)/shard_map/ppermute | solution.py:27
  217.0 7.3 %collective-permute-start.33 = (f32[16,8,128]{2,1,0:T(8,128)S(1)}, f32[16,8,128]{2,1,0:T(8,128)S(1)}, u32[]{:S(2)}, u32[]{:S(2)}) collective-permute-start(f32[16,8,128]{2,1,0:T(8,128)S(1)} %fusion.1), channel_id=1, source_target_pairs={{0,32},{32,64},{64,96},{96,0},{1,33},{33,65},{65,97},{97,1},{2,34}... | collective-permute-start | bytes 196616 | tf_op jit(solution)/shard_map/ppermute | solution.py:39
  217.1 7.2 %collective-permute-start.34 = (f32[16,8,128]{2,1,0:T(8,128)S(1)}, f32[16,8,128]{2,1,0:T(8,128)S(1)}, u32[]{:S(2)}, u32[]{:S(2)}) collective-permute-start(f32[16,8,128]{2,1,0:T(8,128)S(1)} %fusion.1), channel_id=1, source_target_pairs={{0,64},{32,96},{64,0},{96,32},{1,65},{33,97},{65,1},{97,33},{2,66}... | collective-permute-start | bytes 196616 | tf_op jit(solution)/shard_map/ppermute | solution.py:39
  219.1 5.3 %collective-permute-start.35 = (f32[16,8,128]{2,1,0:T(8,128)S(1)}, f32[16,8,128]{2,1,0:T(8,128)S(1)}, u32[]{:S(2)}, u32[]{:S(2)}) collective-permute-start(f32[16,8,128]{2,1,0:T(8,128)S(1)} %fusion.1), channel_id=1, source_target_pairs={{0,96},{32,0},{64,32},{96,64},{1,97},{33,1},{65,33},{97,65},{2,98}... | collective-permute-start | bytes 196616 | tf_op jit(solution)/shard_map/ppermute | solution.py:39
  221.1 6.6 %copy-start.7 = (bf16[1024,256]{1,0:T(8,128)(2,1)S(1)}, bf16[1024,256]{1,0:T(8,128)(2,1)}, u32[]{:S(2)}) copy-start(bf16[1024,256]{1,0:T(8,128)(2,1)} %get-tuple-element.170) | copy-start | bytes 1572868
  224.4 7.8 %collective-permute-start.37 = (f32[16,8,128]{2,1,0:T(8,128)S(1)}, f32[16,8,128]{2,1,0:T(8,128)S(1)}, u32[]{:S(2)}, u32[]{:S(2)}) collective-permute-start(f32[16,8,128]{2,1,0:T(8,128)S(1)} %add_add_fusion.1), channel_id=1, source_target_pairs={{0,8},{8,0},{1,9},{9,1},{2,10},{10,2},{3,11},{11,3},{4,12},{12,4},... | collective-permute-start | bytes 196616 | tf_op jit(solution)/shard_map/ppermute | solution.py:39
  224.5 7.7 %collective-permute-start.38 = (f32[16,8,128]{2,1,0:T(8,128)S(1)}, f32[16,8,128]{2,1,0:T(8,128)S(1)}, u32[]{:S(2)}, u32[]{:S(2)}) collective-permute-start(f32[16,8,128]{2,1,0:T(8,128)S(1)} %add_add_fusion.1), channel_id=1, source_target_pairs={{0,16},{16,0},{1,17},{17,1},{2,18},{18,2},{3,19},{19,3},{4,20},{20... | collective-permute-start | bytes 196616 | tf_op jit(solution)/shard_map/ppermute | solution.py:39
  224.9 7.3 %collective-permute-start.39 = (f32[16,8,128]{2,1,0:T(8,128)S(1)}, f32[16,8,128]{2,1,0:T(8,128)S(1)}, u32[]{:S(2)}, u32[]{:S(2)}) collective-permute-start(f32[16,8,128]{2,1,0:T(8,128)S(1)} %add_add_fusion.1), channel_id=1, source_target_pairs={{0,24},{8,16},{16,8},{24,0},{1,25},{9,17},{17,9},{25,1},{2,26},{10... | collective-permute-start | bytes 196616 | tf_op jit(solution)/shard_map/ppermute | solution.py:39
  232.2 3.3 %collective-permute-start.40 = (f32[16,8,128]{2,1,0:T(8,128)S(1)}, f32[16,8,128]{2,1,0:T(8,128)S(1)}, u32[]{:S(2)}, u32[]{:S(2)}) collective-permute-start(f32[16,8,128]{2,1,0:T(8,128)S(1)} %add_add_fusion), channel_id=1, source_target_pairs={{0,1},{1,0},{2,3},{3,2},{4,5},{5,4},{6,7},{7,6},{8,9},{9,8},{10,11... | collective-permute-start | bytes 196616 | tf_op jit(solution)/shard_map/ppermute | solution.py:39
  235.5 6.5 %collective-permute-start.41 = (f32[32,8,128]{2,1,0:T(8,128)S(1)}, f32[32,8,128]{2,1,0:T(8,128)S(1)}, u32[]{:S(2)}, u32[]{:S(2)}) collective-permute-start(f32[32,8,128]{2,1,0:T(8,128)S(1)} %pad_maximum_fusion.3.refs_0_), channel_id=1, source_target_pairs={{0,6},{2,0},{4,2},{6,4},{1,7},{3,1},{5,3},{7,5},{8,14},{10,8},{12,... | collective-permute-start | bytes 393224 | tf_op jit(solution)/shard_map/ppermute | solution.py:39
  237.0 5.9 %collective-permute-start.42 = (f32[32,8,128]{2,1,0:T(8,128)S(1)}, f32[32,8,128]{2,1,0:T(8,128)S(1)}, u32[]{:S(2)}, u32[]{:S(2)}) collective-permute-start(f32[32,8,128]{2,1,0:T(8,128)S(1)} %pad_maximum_fusion.3.refs_0_), channel_id=1, source_target_pairs={{0,4},{2,6},{4,0},{6,2},{1,5},{3,7},{5,1},{7,3},{8,12},{10,14},{12... | collective-permute-start | bytes 393224 | tf_op jit(solution)/shard_map/ppermute | solution.py:39
  237.3 9.4 %collective-permute-start.43 = (f32[32,8,128]{2,1,0:T(8,128)S(1)}, f32[32,8,128]{2,1,0:T(8,128)S(1)}, u32[]{:S(2)}, u32[]{:S(2)}) collective-permute-start(f32[32,8,128]{2,1,0:T(8,128)S(1)} %pad_maximum_fusion.3.refs_0_), channel_id=1, source_target_pairs={{0,2},{2,4},{4,6},{6,0},{1,3},{3,5},{5,7},{7,1},{8,10},{10,12},{12... | collective-permute-start | bytes 393224 | tf_op jit(solution)/shard_map/ppermute | solution.py:39
  238.7 9.4 %copy-start.1 = (bf16[1,2048,256]{2,1,0:T(8,128)(2,1)S(1)}, bf16[1,2048,256]{2,1,0:T(8,128)(2,1)}, u32[]{:S(2)}) copy-start(bf16[1,2048,256]{2,1,0:T(8,128)(2,1)} %param.9) | copy-start | bytes 3145732
Sparse Core Ops, SparseCore 0:
  49.4 62.9 all-gather.1
  114.7 51.5 reduce-scatter.1

commit v12 on v11

--- a/solution.py
+++ b/solution.py
@@ -461,7 +461,7 @@
     return pl.BlockSpec(memory_space=pltpu.VMEM)
 
 
-def total_over_devices(spread_to, collect_from, query_sum, key_sum, value_sum, long_sum, short_taps, first, after, last):
+def total_over_devices(spread_to, collect_from, query_sum, key_sum, value_sum, long_sum, short_taps, first, after):
     ny, nz = lax.axis_size("y"), lax.axis_size("z")
     channels = query_sum.shape[1]
     count = 3 * channels // LANES + long_sum.shape[0] // 8
@@ -480,7 +480,7 @@
     terms, first = lax.optimization_barrier(([part] + [move(part, y=d) for d in range(1, ny)], first))
     whole = paired_sum(terms)
     terms = [move(whole, xl=a, xh=b) for a, b in FLIPS]
-    terms, beside, last = lax.optimization_barrier((terms, after(first), last))
+    terms, beside = lax.optimization_barrier((terms, after(first)))
     whole = paired_sum(terms)
     line = jnp.concatenate([whole, move(whole, c=1)], axis=0)
     lines = [move(line, z=-d) for d in range(nz)]
@@ -497,7 +497,7 @@
         compiler_params=params(),
         name="collect",
     )(collect_from, *lines)
-    return short, long, beside, last
+    return short, long, beside
 
 
 def paired_sum(terms):
@@ -672,14 +672,13 @@
     return total
 
 
-def plane_scatter(top_grads, bottom_grads, beside):
+def plane_scatter(top_grads, bottom_grads):
     ny = len(top_grads)
     top = added([move(top_grads[d], y=-d) for d in range(ny)]).astype(BF16)
     bottom = added([move(bottom_grads[f], xl=a, xh=b) for f, (a, b) in enumerate(FLIPS)]).astype(BF16)
-    top, bottom, beside = lax.optimization_barrier((top, bottom, beside))
     top = [move(top[f], xl=a, xh=b) for f, (a, b) in enumerate(FLIPS)]
     bottom = [move(bottom[d], y=-d) for d in range(ny)]
-    return top, bottom, beside
+    return top, bottom
 
 
 def shards(tokens_in, short_filter, long_filter, out_weight, cotangent):
@@ -709,17 +708,17 @@
     parts = features_call(tokens, short_filter)
     parts, rim = lax.optimization_barrier((parts, rim))
     query, key, value, mixer = features_call(tokens, short_filter, rim, parts)
-    mixer, out_weight, half = lax.optimization_barrier((mixer, out_weight, xh))
+    mixer, out_weight = lax.optimization_barrier((mixer, out_weight))
     mixer_prev = along(mixer, 1)
-    others = move(lax.dynamic_slice_in_dim(upstream, (1 - half) * span, span, 0), xh=1)
     tall_bottom = gather_tall(out_weight)
-    mixer_prev, tall_bottom, others = lax.optimization_barrier((mixer_prev, tall_bottom, others))
+    mixer_prev, tall_bottom = lax.optimization_barrier((mixer_prev, tall_bottom))
     mixed, gated = mix_call(lines, mixer_prev, mixer, query)
-    mixed, out_weight, half = lax.optimization_barrier((mixed, out_weight, half))
+    mixed, out_weight, half = lax.optimization_barrier((mixed, out_weight, xh))
     wide_top = gather_wide(out_weight)
-    wide_top, tall_bottom = lax.optimization_barrier((wide_top, tall_bottom))
+    wide_top, tall_bottom, half = lax.optimization_barrier((wide_top, tall_bottom, half))
     all_rows = lax.all_gather(gated, ("z", "c"), axis=0, tiled=True)
     tops, bottoms = gather_far(wide_top, tall_bottom)
+    others = move(lax.dynamic_slice_in_dim(upstream, (1 - half) * span, span, 0), xh=1)
     mine = lax.dynamic_slice_in_dim(upstream, half * span, span, 0)
     cotangents = jnp.concatenate([mine, others], axis=1)
     partial = gate_matmul(cotangents, tops, bottoms)
@@ -728,8 +727,10 @@
 
     top_grads, bottom_grads = weight_grad(origin, all_rows, cotangents.T, ny)
     own, other = output_call(origin, all_rows, tops, bottoms)
-    top, bottom, other = plane_scatter(top_grads, bottom_grads, other)
-    gate_grad, top, bottom, other = lax.optimization_barrier((gate_grad, top, bottom, other))
+    top, bottom = plane_scatter(top_grads, bottom_grads)
+    theirs = move(other, xh=1)
+    output = jnp.where(xh == 0, jnp.concatenate([own, theirs], axis=0), jnp.concatenate([theirs, own], axis=0))
+    gate_grad, top, bottom, output = lax.optimization_barrier((gate_grad, top, bottom, output))
 
     grad_mixed, query_grad = gate_call(place, gate_grad, query, mixed)
     grad_next = along(grad_mixed, -1)
@@ -737,21 +738,18 @@
         groups, short_taps, mixer_prev, mixer, grad_mixed, query_grad, tokens, rim
     )
     grad_weight = jnp.concatenate([added(top), added(bottom)], axis=1).T
-    theirs = move(other, xh=1)
     grad_next, grad_weight = lax.optimization_barrier((grad_next, grad_weight))
     other_grads, key_sum, value_sum, edge = unmix_call(
         lines, short_taps, grad_mixed, grad_next, key, value, tokens, rim, query_grad
     )
-    edge, key_sum, theirs = lax.optimization_barrier((edge, key_sum, theirs))
     edge = along(edge, -1)
-    output = jnp.where(xh == 0, jnp.concatenate([own, theirs], axis=0), jnp.concatenate([theirs, own], axis=0))
     query_part = short_adjoint_call(query_grad[None], edge, short_filter, 0, 0, None)
 
     def key_part(query_part):
         return short_adjoint_call(other_grads, edge, short_filter, 0, 1, query_part)
 
-    grad_short, grad_long, grad_tokens, output = total_over_devices(
-        spread_to, collect_from, query_sum, key_sum, value_sum, long_sum, short_taps, query_part, key_part, output
+    grad_short, grad_long, grad_tokens = total_over_devices(
+        spread_to, collect_from, query_sum, key_sum, value_sum, long_sum, short_taps, query_part, key_part
     )
     grad_tokens = short_adjoint_call(other_grads, edge, short_filter, 1, 2, grad_tokens)
     return output[None], grad_tokens[None], grad_short, grad_long, grad_weight

time: 256 us -> 248 us (0.969)
  waiting for transfers between devices: 72.1 us -> 65 us
    all_gather x1, waiting for transfers between devices: 22.9 us -> 7.96 us  [shards(): all_rows = lax.all_gather(gated, ('z', 'c'), axis=0, tiled=True)]
    ppermute x4, waiting for transfers between devices: 1.76 us -> 5.86 us  [along(): return lax.ppermute(x, LINE, pairs)]
    ppermute x40, waiting for transfers between devices: 47.2 us -> 51.1 us  [move(): return lax.ppermute(x, axes, pairs)]
  transfers between devices with their start and end apart: 46 -> 46, of which waited for: 25 -> 24; matrix products, arithmetic and copies ran while one was open for 4% -> 3% of each run, Pallas kernels for 26% -> 22%
where the time goes in v12:
time: 248 us
  Pallas kernels  83.2 us (34%)
  starting transfers between devices  74.2 us (30%)
  waiting for transfers between devices  65 us (26%)
  between operations  14.4 us (6%)
  other arithmetic  5.6 us (2%)
  local copies, waits for them, and re-layouts  5.13 us (2%)
    pallas_call x12, Pallas kernels, run(): return call(*held)  81 us
    ppermute x40, starting transfers between devices, move(): return lax.ppermute(x, axes, pairs)  56.7 us
    ppermute x40, waiting for transfers between devices, move(): return lax.ppermute(x, axes, pairs)  51.1 us
    ppermute x4, starting transfers between devices, along(): return lax.ppermute(x, LINE, pairs)  17.5 us
    all_gather x1, waiting for transfers between devices, shards(): all_rows = lax.all_gather(gated, ('z', 'c'), axis=0, tiled=True)  7.96 us
    ppermute x4, waiting for transfers between devices, along(): return lax.ppermute(x, LINE, pairs)  5.86 us
  transfers between devices with their start and end apart: 46, of which 24 were waited for; matrix products, arithmetic and copies ran while one was open for 3% of the time, Pallas kernels for 22%

profile of v12, /device:TPU:1, one launch (start us, length us, event | category | flops | bytes accessed | tf_op | source)
XLA Modules:
  0.0 247.5 jit_solution(14552298032364443053)
XLA Ops:
  8.2 4.9 %collective-permute-start = (bf16[8,12288]{1,0:T(8,128)(2,1)S(1)}, bf16[8,12288]{1,0:T(8,128)(2,1)S(1)}, u32[]{:S(2)}, u32[]{:S(2)}) collective-permute-start(bf16[8,12288]{1,0:T(8,128)(2,1)S(1)} %slice_bitcast_fusion), channel_id=1, source_target_pairs={{0,1},{1,2},{2,3},{3,4},{4,5},{5,6},{6,7},{7,8},{8,9},{9,10},{10,1... | collective-permute-start | bytes 589832 | tf_op jit(solution)/shard_map/ppermute | solution.py:27
  13.1 6.7 %features.1 = (bf16[128,4096]{1,0:T(8,128)(2,1)}, bf16[128,4096]{1,0:T(8,128)(2,1)}, bf16[128,4096]{1,0:T(8,128)(2,1)}, bf16[128,4096]{1,0:T(8,128)(2,1)}) custom-call(bf16[128,12288]{1,0:T(8,128)(2,1)} %bitcast.36, bf16[128,12288]{1,0:T(8,128)(2,1)} %bitcast.37, bf16[128,12288]{1,0:T(8,128)(2,1)} %bitcast.38, f32[7,12288]{1,0:T(8,128)} %filter_ref.5, ...), custom_call_target="tpu_custom_call" | custom-call | bytes 1572864 | tf_op jit(solution)/shard_map/features/pallas_call | solution.py:64
  19.9 2.6 %first_rows.1 = (bf16[128,4096]{1,0:T(8,128)(2,1)}, bf16[128,4096]{1,0:T(8,128)(2,1)}, bf16[128,4096]{1,0:T(8,128)(2,1)}, bf16[128,4096]{1,0:T(8,128)(2,1)}) custom-call(bf16[128,12288]{1,0:T(8,128)(2,1)} %bitcast.39, bf16[128,12288]{1,0:T(8,128)(2,1)} %bitcast.40, ...), custom_call_target="tpu_custom_call", output_to_operand_aliasing={{0}: (9, {}), {1}: (10, {}), {2}: (11, {}), {3}: (12, {})} | custom-call | bytes 196608 | tf_op jit(solution)/shard_map/first_rows/pallas_call | solution.py:64
  22.4 1.9 collective-permute-start.1
  24.4 1.4 collective-permute-start.2
  25.7 2.6 %collective-permute-start.3 = (bf16[256,256]{1,0:T(8,128)(2,1)S(1)}, bf16[256,256]{1,0:T(8,128)(2,1)S(1)}, u32[]{:S(2)}, u32[]{:S(2)}) collective-permute-start(bf16[256,256]{1,0:T(8,128)(2,1)S(1)} %slice.56), channel_id=1, source_target_pairs={{0,64},{32,96},{64,0},{96,32},{1,65},{33,97},{65,1},{97,33},{2,66}... | collective-permute-start | bytes 393224 | tf_op jit(solution)/shard_map/ppermute | solution.py:39
  28.4 1.1 collective-permute-start.4
  30.3 3.9 %collective-permute-done.3 = bf16[256,256]{1,0:T(8,128)(2,1)S(1)} collective-permute-done((bf16[256,256]{1,0:T(8,128)(2,1)S(1)}, bf16[256,256]{1,0:T(8,128)(2,1)S(1)}, u32[]{:S(2)}, u32[]{:S(2)}) %collective-permute-start.3) | collective-permute-done | bytes 131104 | tf_op jit(solution)/shard_map/ppermute | solution.py:39
  34.2 2.2 collective-permute-done.1.prev_ref
  36.4 9.7 %mix.1 = (bf16[128,4096]{1,0:T(8,128)(2,1)}, bf16[128,4096]{1,0:T(8,128)(2,1)}) custom-call(f32[256,128]{1,0:T(8,128)S(1)} %convert_element_type.57.lines_ref, bf16[128,4096]{1,0:T(8,128)(2,1)S(1)} %collective-permute-done.1.prev_ref, bf16[128,4096]{1,0:T(8,128)(2,1)} %get-tuple-element.95.cur_ref, bf16[128,4096]{1,0:T(8,128)(2,1)} %get-tuple-element.98.query_ref), custom_call_target="tpu_custom_call" | custom-call | bytes 1048576 | tf_op jit(solution)/shard_map/mix/pallas_call | solution.py:64
  46.2 2.8 %collective-permute-start.5 = (bf16[256,256]{1,0:T(8,128)(2,1)S(1)}, bf16[256,256]{1,0:T(8,128)(2,1)S(1)}, u32[]{:S(2)}, u32[]{:S(2)}) collective-permute-start(bf16[256,256]{1,0:T(8,128)(2,1)S(1)} %slice.57), channel_id=1, source_target_pairs={{0,8},{8,0},{1,9},{9,1},{2,10},{10,2},{3,11},{11,3},{4,12},{12,4},... | collective-permute-start | bytes 393224 | tf_op jit(solution)/shard_map/ppermute | solution.py:39
  49.9 1.7 collective-permute-done.5
  51.6 1.5 collective-permute-done.6
  53.1 1.3 collective-permute-done.7
  54.7 1.5 collective-permute-start.8
  56.2 1.4 collective-permute-start.9
  57.6 2.6 %collective-permute-start.10 = (bf16[4,256,256]{2,1,0:T(8,128)(2,1)S(1)}, bf16[4,256,256]{2,1,0:T(8,128)(2,1)}, u32[]{:S(2)}, u32[]{:S(2)}) collective-permute-start(bf16[4,256,256]{2,1,0:T(8,128)(2,1)S(1)} %pad_maximum_fusion.1.refs_1_.refs_0_), channel_id=1, source_target_pairs={{0,64},{32,96},{64,0},{96,32},{1,65},{33,97},{65,1},{97,33},{2,66}... | collective-permute-start | bytes 1572872 | tf_op jit(solution)/shard_map/ppermute | solution.py:39
  60.2 1.1 collective-permute-start.11
  61.3 1.1 pad_maximum_fusion.2.refs_5_.refs_4_
  62.3 1.7 collective-permute-start.12
  64.0 1.1 collective-permute-done.8
  65.9 2.7 %collective-permute-start.14 = (bf16[4,256,256]{2,1,0:T(8,128)(2,1)S(1)}, bf16[4,256,256]{2,1,0:T(8,128)(2,1)}, u32[]{:S(2)}, u32[]{:S(2)}) collective-permute-start(bf16[4,256,256]{2,1,0:T(8,128)(2,1)S(1)} %pad_maximum_fusion.2.refs_5_.refs_4_), channel_id=1, source_target_pairs={{0,24},{8,16},{16,8},{24,0},{1,25},{9,17},{17,9},{25,1},{2,26},{10... | collective-permute-start | bytes 1572872 | tf_op jit(solution)/shard_map/ppermute | solution.py:39
  68.8 1.1 fusion.11
  69.9 1.5 copy.18.refs_0_
  71.4 1.2 collective-permute-done.10.refs_3_.refs_2_
  72.7 10.1 %collective-permute-done.13.refs_7_.refs_6_ = bf16[4,256,256]{2,1,0:T(8,128)(2,1)} collective-permute-done((bf16[4,256,256]{2,1,0:T(8,128)(2,1)S(1)}, bf16[4,256,256]{2,1,0:T(8,128)(2,1)}, u32[]{:S(2)}, u32[]{:S(2)}) %collective-permute-start.13) | collective-permute-done | bytes 524320 | tf_op jit(solution)/shard_map/ppermute | solution.py:39
  83.6 1.1 copy-done.3
  84.7 8.6 %gate_matmul.1 = bf16[1024,4096]{1,0:T(8,128)(2,1)} custom-call(bf16[1024,512]{1,0:T(8,128)(2,1)S(1)} %copy.18.refs_0_, bf16[4,256,256]{2,1,0:T(8,128)(2,1)S(1)} %pad_maximum_fusion.1.refs_1_.refs_0_, bf16[4,256,256]{2,1,0:T(8,128)(2,1)S(1)} %copy-done.3, bf16[4,256,256]{2,1,0:T(8,128)(2,1)} %collective-permute-done.10.refs_3_.refs_2_, ...), custom_call_target="tpu_custom_call" | custom-call | flops 4294967296 | bytes 12582912 | tf_op jit(solution)/shard_map/gate_matmul/pallas_call | solution.py:64
  93.3 8.0 %all-gather.2.cloned.1.call-done.rows_ref = bf16[1024,4096]{1,0:T(8,128)(2,1)} async-done(((bf16[128,4096]{1,0:T(8,128)(2,1)}), bf16[1024,4096]{1,0:T(8,128)(2,1)}) %all-gather.2.cloned.1.call-update) | async-done | bytes 8388624 | tf_op jit(solution)/shard_map/all_gather | solution.py:719
  101.3 9.9 %weight_grad.1 = (bf16[4,256,256]{2,1,0:T(8,128)(2,1)}, bf16[4,256,256]{2,1,0:T(8,128)(2,1)}, bf16[4,256,256]{2,1,0:T(8,128)(2,1)}, bf16[4,256,256]{2,1,0:T(8,12...) custom-call(s32[8]{0:T(128)S(1)} %fusion.2.origin.place, ...), custom_call_target="tpu_custom_call" | custom-call | flops 4294967296 | bytes 12582912 | tf_op jit(solution)/shard_map/weight_grad/pallas_call | solution.py:64
  111.2 1.2 collective-permute-start.17
  112.4 3.2 %collective-permute-start.16 = (bf16[4,256,256]{2,1,0:T(8,128)(2,1)}, bf16[4,256,256]{2,1,0:T(8,128)(2,1)}, u32[]{:S(2)}, u32[]{:S(2)}) collective-permute-start(bf16[4,256,256]{2,1,0:T(8,128)(2,1)} %get-tuple-element.120), channel_id=1, source_target_pairs={{0,64},{32,96},{64,0},{96,32},{1,65},{33,97},{65,1},{97,33},{2,66}... | collective-permute-start | bytes 1572872 | tf_op jit(solution)/shard_map/ppermute | solution.py:39
  115.6 2.1 collective-permute-start.15
  118.4 9.9 %output.1 = (bf16[1024,256]{1,0:T(8,128)(2,1)}, bf16[1024,256]{1,0:T(8,128)(2,1)}) custom-call(s32[8]{0:T(128)S(1)} %fusion.2.origin.place, bf16[1024,4096]{1,0:T(8,128)(2,1)} %all-gather.2.cloned.1.call-done.rows_ref, bf16[4,256,256]{2,1,0:T(8,128)(2,1)S(1)} %pad_maximum_fusion.1.refs_1_.refs_0_, bf16[4,256,256]{2,1,0:T(8,128)(2,1)S(1)} %copy-done.4, ...), custom_call_target="tpu_custom_call" | custom-call | flops 4294967296 | bytes 12582912 | tf_op jit(solution)/shard_map/output/pallas_call | solution.py:64
  128.3 3.2 %collective-permute-start.21 = (bf16[4,256,256]{2,1,0:T(8,128)(2,1)S(1)}, bf16[4,256,256]{2,1,0:T(8,128)(2,1)S(1)}, u32[]{:S(2)}, u32[]{:S(2)}) collective-permute-start(bf16[4,256,256]{2,1,0:T(8,128)(2,1)S(1)} %copy-done.13), channel_id=1, source_target_pairs={{0,8},{8,0},{1,9},{9,1},{2,10},{10,2},{3,11},{11,3},{4,12},{12,4},... | collective-permute-start | bytes 1572872 | tf_op jit(solution)/shard_map/ppermute | solution.py:39
  131.5 3.4 %collective-permute-done.16 = bf16[4,256,256]{2,1,0:T(8,128)(2,1)} collective-permute-done((bf16[4,256,256]{2,1,0:T(8,128)(2,1)}, bf16[4,256,256]{2,1,0:T(8,128)(2,1)}, u32[]{:S(2)}, u32[]{:S(2)}) %collective-permute-start.16) | collective-permute-done | bytes 524320 | tf_op jit(solution)/shard_map/ppermute | solution.py:39
  134.9 2.8 %collective-permute-start.27 = (bf16[1024,256]{1,0:T(8,128)(2,1)}, bf16[1024,256]{1,0:T(8,128)(2,1)S(1)}, u32[]{:S(2)}, u32[]{:S(2)}) collective-permute-start(bf16[1024,256]{1,0:T(8,128)(2,1)} %get-tuple-element.127), channel_id=1, source_target_pairs={{0,8},{8,0},{1,9},{9,1},{2,10},{10,2},{3,11},{11,3},{4,12},{12,4},... | collective-permute-start | bytes 1572872 | tf_op jit(solution)/shard_map/ppermute | solution.py:39
  137.7 1.5 add_convert_fusion.1
  139.2 1.1 collective-permute-start.18
  140.9 1.7 collective-permute-start.20
  142.9 3.0 %collective-permute-start.24 = (bf16[256,256]{1,0:T(8,128)(2,1)S(1)}, bf16[256,256]{1,0:T(8,128)(2,1)S(1)}, u32[]{:S(2)}, u32[]{:S(2)}) collective-permute-start(bf16[256,256]{1,0:T(8,128)(2,1)S(1)} %get-tuple-element.176), channel_id=1, source_target_pairs={{0,96},{32,0},{64,32},{96,64},{1,97},{33,1},{65,33},{97,65},{2,98}... | collective-permute-start | bytes 393224 | tf_op jit(solution)/shard_map/ppermute | solution.py:39
  145.9 6.4 %collective-permute-done.27 = bf16[1024,256]{1,0:T(8,128)(2,1)S(1)} collective-permute-done((bf16[1024,256]{1,0:T(8,128)(2,1)}, bf16[1024,256]{1,0:T(8,128)(2,1)S(1)}, u32[]{:S(2)}, u32[]{:S(2)}) %collective-permute-start.27) | collective-permute-done | bytes 524320 | tf_op jit(solution)/shard_map/ppermute | solution.py:39
  152.3 2.8 %collective-permute-done.18 = bf16[256,256]{1,0:T(8,128)(2,1)S(1)} collective-permute-done((bf16[256,256]{1,0:T(8,128)(2,1)S(1)}, bf16[256,256]{1,0:T(8,128)(2,1)S(1)}, u32[]{:S(2)}, u32[]{:S(2)}) %collective-permute-start.18) | collective-permute-done | bytes 131104 | tf_op jit(solution)/shard_map/ppermute | solution.py:39
  155.1 1.3 maximum_select_fusion
  156.7 5.7 %collective-permute-done.20 = bf16[256,256]{1,0:T(8,128)(2,1)S(1)} collective-permute-done((bf16[256,256]{1,0:T(8,128)(2,1)S(1)}, bf16[256,256]{1,0:T(8,128)(2,1)S(1)}, u32[]{:S(2)}, u32[]{:S(2)}) %collective-permute-start.20) | collective-permute-done | bytes 131104 | tf_op jit(solution)/shard_map/ppermute | solution.py:39
  162.4 3.6 %gate_back.1 = (bf16[128,4096]{1,0:T(8,128)(2,1)}, bf16[128,4096]{1,0:T(8,128)(2,1)}) custom-call(s32[8]{0:T(128)S(1)} %fusion.2.origin.place, bf16[128,4096]{1,0:T(8,128)(2,1)} %reduce-scatter.2.cloned.1.call-done.gate_grad_ref, bf16[128,4096]{1,0:T(8,128)(2,1)} %get-tuple-element.98.query_ref, bf16[128,4096]{1,0:T(8,128)(2,1)} %get-tuple-element.130.mixed_ref), custom_call_target="tpu_custom_call" | custom-call | flops 1048576 | bytes 5242880 | tf_op jit(solution)/shard_map/gate_back/pallas_call | solution.py:64
  166.0 7.7 %collective-permute-start.28 = (bf16[128,4096]{1,0:T(8,128)(2,1)}, bf16[128,4096]{1,0:T(8,128)(2,1)S(1)}, u32[]{:S(2)}, u32[]{:S(2)}) collective-permute-start(bf16[128,4096]{1,0:T(8,128)(2,1)} %get-tuple-element.131.grad_ref), channel_id=1, source_target_pairs={{1,0},{2,1},{3,2},{4,3},{5,4},{6,5},{7,6},{8,7},{9,8},{10,9},{11,1... | collective-permute-start | bytes 3145736 | tf_op jit(solution)/shard_map/ppermute | solution.py:27
  174.0 9.1 %long_grad.1 = (f32[256,128]{1,0:T(8,128)S(1)}, f32[8,4096]{1,0:T(8,128)S(1)}) custom-call(bf16[128,4096]{1,0:T(8,128)(2,1)} %copy-done.1, bf16[128,4096]{1,0:T(8,128)(2,1)} %get-tuple-element.95.cur_ref, bf16[128,4096]{1,0:T(8,128)(2,1)} %get-tuple-element.131.grad_ref, bf16[128,4096]{1,0:T(8,128)(2,1)} %get-tuple-element.143.query_grad_ref.feature_ref, ...), custom_call_target="tpu_custom_call" | custom-call | flops 2147483648 | bytes 5242880 | tf_op jit(solution)/shard_map/long_grad/pallas_call | solution.py:64
  183.1 3.7 %collective-permute-done.28.next_ref = bf16[128,4096]{1,0:T(8,128)(2,1)S(1)} collective-permute-done((bf16[128,4096]{1,0:T(8,128)(2,1)}, bf16[128,4096]{1,0:T(8,128)(2,1)S(1)}, u32[]{:S(2)}, u32[]{:S(2)}) %collective-permute-start.28) | collective-permute-done | bytes 1048608 | tf_op jit(solution)/shard_map/ppermute | solution.py:27
  186.8 11.4 %unmix.1 = (bf16[2,128,4096]{2,1,0:T(8,128)(2,1)}, f32[8,4096]{1,0:T(8,128)S(1)}, f32[8,4096]{1,0:T(8,128)S(1)}, bf16[3,8,4096]{2,1,0:T(8,128)(2,1)S(1)}) custom-call(f32[256,128]{1,0:T(8,128)S(1)} %convert_element_type.57.lines_ref, bf16[128,4096]{1,0:T(8,128)(2,1)} %get-tuple-element.131.grad_ref, bf16[128,4096]{1,0:T(8,128)(2,1)S(1)} %collective-permute-done.28.next_ref, ...), custom_call_target="tpu_custom_call" | custom-call | flops 2147483648 | bytes 8388608 | tf_op jit(solution)/shard_map/unmix/pallas_call | solution.py:64
  199.0 1.5 collective-permute-done.30
  200.5 4.5 %collective-permute-start.33 = (f32[16,8,128]{2,1,0:T(8,128)S(1)}, f32[16,8,128]{2,1,0:T(8,128)S(1)}, u32[]{:S(2)}, u32[]{:S(2)}) collective-permute-start(f32[16,8,128]{2,1,0:T(8,128)S(1)} %get-tuple-element.183), channel_id=1, source_target_pairs={{0,6},{2,0},{4,2},{6,4},{1,7},{3,1},{5,3},{7,5},{8,14},{10,8},{12,... | collective-permute-start | bytes 196616 | tf_op jit(solution)/shard_map/ppermute | solution.py:39
  206.2 2.9 %collective-permute-start.29 = (bf16[3,8,4096]{2,1,0:T(8,128)(2,1)S(1)}, bf16[3,8,4096]{2,1,0:T(8,128)(2,1)S(1)}, u32[]{:S(2)}, u32[]{:S(2)}) collective-permute-start(bf16[3,8,4096]{2,1,0:T(8,128)(2,1)S(1)} %get-tuple-element.145), channel_id=1, source_target_pairs={{1,0},{2,1},{3,2},{4,3},{5,4},{6,5},{7,6},{8,7},{9,8},{10,9},{11,1... | collective-permute-start | bytes 589832 | tf_op jit(solution)/shard_map/ppermute | solution.py:27
  209.7 2.1 collective-permute-done.31
  212.7 2.0 collective-permute-start.36
  214.8 3.2 %short_adjoint.3.refs_0_ = bf16[128,12288]{1,0:T(8,128)(2,1)} custom-call(bf16[1,128,4096]{2,1,0:T(8,128)(2,1)} %bitcast.46, bf16[3,8,4096]{2,1,0:T(8,128)(2,1)S(1)} %collective-permute-done.29.rim_ref, f32[7,12288]{1,0:T(8,128)} %filter_ref.5), custom_call_target="tpu_custom_call" | custom-call | flops 7340032 | bytes 2097152 | tf_op jit(solution)/shard_map/short_adjoint/pallas_call | solution.py:64
  219.8 1.7 collective-permute-start.39
  221.5 3.2 %short_adjoint.4.refs_0_ = bf16[128,12288]{1,0:T(8,128)(2,1)} custom-call(bf16[2,128,4096]{2,1,0:T(8,128)(2,1)} %get-tuple-element.144.grads_ref, bf16[3,8,4096]{2,1,0:T(8,128)(2,1)S(1)} %collective-permute-done.29.rim_ref, f32[7,12288]{1,0:T(8,128)} %filter_ref.5, bf16[128,12288]{1,0:T(8,128)(2,1)} %short_adjoint.3.refs_0_), custom_call_target="tpu_custom_call", output_to_operand_aliasing={{}: (3, {})} | custom-call | flops 7340032 | bytes 2097152 | tf_op jit(solution)/shard_map/short_adjoint/pallas_call | solution.py:64
  224.8 3.0 %collective-permute-start.40 = (f32[16,8,128]{2,1,0:T(8,128)S(1)}, f32[16,8,128]{2,1,0:T(8,128)S(1)}, u32[]{:S(2)}, u32[]{:S(2)}) collective-permute-start(f32[16,8,128]{2,1,0:T(8,128)S(1)} %add_add_fusion), channel_id=1, source_target_pairs={{0,1},{1,0},{2,3},{3,2},{4,5},{5,4},{6,7},{7,6},{8,9},{9,8},{10,11... | collective-permute-start | bytes 196616 | tf_op jit(solution)/shard_map/ppermute | solution.py:39
  228.7 1.5 collective-permute-start.41
  231.8 3.2 %short_adjoint.5 = bf16[128,12288]{1,0:T(8,128)(2,1)} custom-call(bf16[2,128,4096]{2,1,0:T(8,128)(2,1)} %get-tuple-element.144.grads_ref, bf16[3,8,4096]{2,1,0:T(8,128)(2,1)S(1)} %collective-permute-done.29.rim_ref, f32[7,12288]{1,0:T(8,128)} %filter_ref.5, bf16[128,12288]{1,0:T(8,128)(2,1)} %short_adjoint.4.refs_0_), custom_call_target="tpu_custom_call", output_to_operand_aliasing={{}: (3, {})} | custom-call | flops 7340032 | bytes 2097152 | tf_op jit(solution)/shard_map/short_adjoint/pallas_call | solution.py:64
  235.0 1.3 collective-permute-done.42.refs_2_
  236.3 2.9 %collective-permute-done.43.refs_3_ = f32[32,8,128]{2,1,0:T(8,128)S(1)} collective-permute-done((f32[32,8,128]{2,1,0:T(8,128)S(1)}, f32[32,8,128]{2,1,0:T(8,128)S(1)}, u32[]{:S(2)}, u32[]{:S(2)}) %collective-permute-start.43) | collective-permute-done | bytes 131104 | tf_op jit(solution)/shard_map/ppermute | solution.py:39
  239.2 1.5 collect.1
  (100 shorter events, 15.1 us)
Async XLA Ops:
  7.2 94.1 %all-gather.2.cloned.1.call-start = ((), (), s32[]{:S(2)}) async-start(), calls=%async_computation.1 | async-start | bytes 9437184 | tf_op jit(solution)/shard_map/all_gather | solution.py:719
  8.2 11.7 %collective-permute-start = (bf16[8,12288]{1,0:T(8,128)(2,1)S(1)}, bf16[8,12288]{1,0:T(8,128)(2,1)S(1)}, u32[]{:S(2)}, u32[]{:S(2)}) collective-permute-start(bf16[8,12288]{1,0:T(8,128)(2,1)S(1)} %slice_bitcast_fusion), channel_id=1, source_target_pairs={{0,1},{1,2},{2,3},{3,4},{4,5},{5,6},{6,7},{7,8},{8,9},{9,10},{10,1... | collective-permute-start | bytes 589832 | tf_op jit(solution)/shard_map/ppermute | solution.py:27
  19.8 2.6 %copy-start = (bf16[8,12288]{1,0:T(8,128)(2,1)}, bf16[8,12288]{1,0:T(8,128)(2,1)S(1)}, u32[]{:S(2)}) copy-start(bf16[8,12288]{1,0:T(8,128)(2,1)S(1)} %collective-permute-done.refs_3_.refs_4_.refs_5_.key_rim_ref.value_rim_ref.rim_ref) | copy-start | bytes 589828
  19.8 4.5 %copy-start.9 = (bf16[512,256]{1,0:T(8,128)(2,1)S(1)}, bf16[512,256]{1,0:T(8,128)(2,1)}, u32[]{:S(2)}) copy-start(bf16[512,256]{1,0:T(8,128)(2,1)} %param.8) | copy-start | bytes 786436
  19.9 9.6 %copy-start.12 = (bf16[256,128]{1,0:T(8,128)(2,1)S(1)}, bf16[256,128]{1,0:T(8,128)(2,1)}, u32[]{:S(2)}) copy-start(bf16[256,128]{1,0:T(8,128)(2,1)} %param.7) | copy-start | bytes 196612
  22.4 14.0 %collective-permute-start.1 = (bf16[128,4096]{1,0:T(8,128)(2,1)}, bf16[128,4096]{1,0:T(8,128)(2,1)S(1)}, u32[]{:S(2)}, u32[]{:S(2)}) collective-permute-start(bf16[128,4096]{1,0:T(8,128)(2,1)} %get-tuple-element.95.cur_ref), channel_id=1, source_target_pairs={{0,1},{1,2},{2,3},{3,4},{4,5},{5,6},{6,7},{7,8},{8,9},{9,10},{10,1... | collective-permute-start | bytes 3145736 | tf_op jit(solution)/shard_map/ppermute | solution.py:27
  24.4 5.9 %collective-permute-start.2 = (bf16[256,256]{1,0:T(8,128)(2,1)S(1)}, bf16[256,256]{1,0:T(8,128)(2,1)S(1)}, u32[]{:S(2)}, u32[]{:S(2)}) collective-permute-start(bf16[256,256]{1,0:T(8,128)(2,1)S(1)} %slice.56), channel_id=1, source_target_pairs={{0,32},{32,64},{64,96},{96,0},{1,33},{33,65},{65,97},{97,1},{2,34}... | collective-permute-start | bytes 393224 | tf_op jit(solution)/shard_map/ppermute | solution.py:39
  25.7 8.5 %collective-permute-start.3 = (bf16[256,256]{1,0:T(8,128)(2,1)S(1)}, bf16[256,256]{1,0:T(8,128)(2,1)S(1)}, u32[]{:S(2)}, u32[]{:S(2)}) collective-permute-start(bf16[256,256]{1,0:T(8,128)(2,1)S(1)} %slice.56), channel_id=1, source_target_pairs={{0,64},{32,96},{64,0},{96,32},{1,65},{33,97},{65,1},{97,33},{2,66}... | collective-permute-start | bytes 393224 | tf_op jit(solution)/shard_map/ppermute | solution.py:39
  28.4 5.8 %collective-permute-start.4 = (bf16[256,256]{1,0:T(8,128)(2,1)S(1)}, bf16[256,256]{1,0:T(8,128)(2,1)S(1)}, u32[]{:S(2)}, u32[]{:S(2)}) collective-permute-start(bf16[256,256]{1,0:T(8,128)(2,1)S(1)} %slice.56), channel_id=1, source_target_pairs={{0,96},{32,0},{64,32},{96,64},{1,97},{33,1},{65,33},{97,65},{2,98}... | collective-permute-start | bytes 393224 | tf_op jit(solution)/shard_map/ppermute | solution.py:39
  34.2 21.9 %copy-start.10 = (bf16[256,256]{1,0:T(8,128)(2,1)}, bf16[256,256]{1,0:T(8,128)(2,1)S(1)}, u32[]{:S(2)}) copy-start(bf16[256,256]{1,0:T(8,128)(2,1)S(1)} %collective-permute-done.3) | copy-start | bytes 393220
  34.2 21.9 %copy-start.11 = (bf16[256,256]{1,0:T(8,128)(2,1)}, bf16[256,256]{1,0:T(8,128)(2,1)S(1)}, u32[]{:S(2)}) copy-start(bf16[256,256]{1,0:T(8,128)(2,1)S(1)} %collective-permute-done.4) | copy-start | bytes 393220
  36.4 9.7 %copy-start.1 = (bf16[128,4096]{1,0:T(8,128)(2,1)}, bf16[128,4096]{1,0:T(8,128)(2,1)S(1)}, u32[]{:S(2)}) copy-start(bf16[128,4096]{1,0:T(8,128)(2,1)S(1)} %collective-permute-done.1.prev_ref) | copy-start | bytes 3145732
  36.4 18.0 %copy-start.5 = (bf16[1,2048,256]{2,1,0:T(8,128)(2,1)S(1)}, bf16[1,2048,256]{2,1,0:T(8,128)(2,1)}, u32[]{:S(2)}) copy-start(bf16[1,2048,256]{2,1,0:T(8,128)(2,1)} %param.9) | copy-start | bytes 3145732
  46.1 116.3 %reduce-scatter.2.cloned.1.call-start = ((), (), s32[]{:S(2)}) async-start(), calls=%async_computation.2 | async-start | bytes 9437184 | tf_op jit(solution)/shard_map/reduce_scatter | solution.py:726
  46.2 5.4 %collective-permute-start.5 = (bf16[256,256]{1,0:T(8,128)(2,1)S(1)}, bf16[256,256]{1,0:T(8,128)(2,1)S(1)}, u32[]{:S(2)}, u32[]{:S(2)}) collective-permute-start(bf16[256,256]{1,0:T(8,128)(2,1)S(1)} %slice.57), channel_id=1, source_target_pairs={{0,8},{8,0},{1,9},{9,1},{2,10},{10,2},{3,11},{11,3},{4,12},{12,4},... | collective-permute-start | bytes 393224 | tf_op jit(solution)/shard_map/ppermute | solution.py:39
  49.0 4.1 %collective-permute-start.6 = (bf16[256,256]{1,0:T(8,128)(2,1)S(1)}, bf16[256,256]{1,0:T(8,128)(2,1)S(1)}, u32[]{:S(2)}, u32[]{:S(2)}) collective-permute-start(bf16[256,256]{1,0:T(8,128)(2,1)S(1)} %slice.57), channel_id=1, source_target_pairs={{0,16},{16,0},{1,17},{17,1},{2,18},{18,2},{3,19},{19,3},{4,20},{20... | collective-permute-start | bytes 393224 | tf_op jit(solution)/shard_map/ppermute | solution.py:39
  49.3 5.0 %collective-permute-start.7 = (bf16[256,256]{1,0:T(8,128)(2,1)S(1)}, bf16[256,256]{1,0:T(8,128)(2,1)S(1)}, u32[]{:S(2)}, u32[]{:S(2)}) collective-permute-start(bf16[256,256]{1,0:T(8,128)(2,1)S(1)} %slice.57), channel_id=1, source_target_pairs={{0,24},{8,16},{16,8},{24,0},{1,25},{9,17},{17,9},{25,1},{2,26},{10... | collective-permute-start | bytes 393224 | tf_op jit(solution)/shard_map/ppermute | solution.py:39
  54.7 10.4 %collective-permute-start.8 = (bf16[1024,256]{0,1:T(8,128)(2,1)S(1)}, bf16[1024,256]{0,1:T(8,128)(2,1)S(1)}, u32[]{:S(2)}, u32[]{:S(2)}) collective-permute-start(bf16[1024,256]{0,1:T(8,128)(2,1)S(1)} %bitcast.49), channel_id=1, source_target_pairs={{0,8},{8,0},{1,9},{9,1},{2,10},{10,2},{3,11},{11,3},{4,12},{12,4},... | collective-permute-start | bytes 1572872 | tf_op jit(solution)/shard_map/ppermute | solution.py:39
  56.2 9.7 %collective-permute-start.9 = (bf16[4,256,256]{2,1,0:T(8,128)(2,1)S(1)}, bf16[4,256,256]{2,1,0:T(8,128)(2,1)S(1)}, u32[]{:S(2)}, u32[]{:S(2)}) collective-permute-start(bf16[4,256,256]{2,1,0:T(8,128)(2,1)S(1)} %pad_maximum_fusion.1.refs_1_.refs_0_), channel_id=1, source_target_pairs={{0,32},{32,64},{64,96},{96,0},{1,33},{33,65},{65,97},{97,1},{2,34}... | collective-permute-start | bytes 1572872 | tf_op jit(solution)/shard_map/ppermute | solution.py:39
  57.6 15.1 %collective-permute-start.10 = (bf16[4,256,256]{2,1,0:T(8,128)(2,1)S(1)}, bf16[4,256,256]{2,1,0:T(8,128)(2,1)}, u32[]{:S(2)}, u32[]{:S(2)}) collective-permute-start(bf16[4,256,256]{2,1,0:T(8,128)(2,1)S(1)} %pad_maximum_fusion.1.refs_1_.refs_0_), channel_id=1, source_target_pairs={{0,64},{32,96},{64,0},{96,32},{1,65},{33,97},{65,1},{97,33},{2,66}... | collective-permute-start | bytes 1572872 | tf_op jit(solution)/shard_map/ppermute | solution.py:39
  60.2 12.5 %collective-permute-start.11 = (bf16[4,256,256]{2,1,0:T(8,128)(2,1)S(1)}, bf16[4,256,256]{2,1,0:T(8,128)(2,1)}, u32[]{:S(2)}, u32[]{:S(2)}) collective-permute-start(bf16[4,256,256]{2,1,0:T(8,128)(2,1)S(1)} %pad_maximum_fusion.1.refs_1_.refs_0_), channel_id=1, source_target_pairs={{0,96},{32,0},{64,32},{96,64},{1,97},{33,1},{65,33},{97,65},{2,98}... | collective-permute-start | bytes 1572872 | tf_op jit(solution)/shard_map/ppermute | solution.py:39
  62.3 10.4 %collective-permute-start.12 = (bf16[4,256,256]{2,1,0:T(8,128)(2,1)S(1)}, bf16[4,256,256]{2,1,0:T(8,128)(2,1)}, u32[]{:S(2)}, u32[]{:S(2)}) collective-permute-start(bf16[4,256,256]{2,1,0:T(8,128)(2,1)S(1)} %pad_maximum_fusion.2.refs_5_.refs_4_), channel_id=1, source_target_pairs={{0,8},{8,0},{1,9},{9,1},{2,10},{10,2},{3,11},{11,3},{4,12},{12,4},... | collective-permute-start | bytes 1572872 | tf_op jit(solution)/shard_map/ppermute | solution.py:39
  65.1 17.8 %collective-permute-start.13 = (bf16[4,256,256]{2,1,0:T(8,128)(2,1)S(1)}, bf16[4,256,256]{2,1,0:T(8,128)(2,1)}, u32[]{:S(2)}, u32[]{:S(2)}) collective-permute-start(bf16[4,256,256]{2,1,0:T(8,128)(2,1)S(1)} %pad_maximum_fusion.2.refs_5_.refs_4_), channel_id=1, source_target_pairs={{0,16},{16,0},{1,17},{17,1},{2,18},{18,2},{3,19},{19,3},{4,20},{20... | collective-permute-start | bytes 1572872 | tf_op jit(solution)/shard_map/ppermute | solution.py:39
  65.9 2.9 %copy-start.2 = (bf16[4,256,256]{2,1,0:T(8,128)(2,1)}, bf16[4,256,256]{2,1,0:T(8,128)(2,1)S(1)}, u32[]{:S(2)}) copy-start(bf16[4,256,256]{2,1,0:T(8,128)(2,1)S(1)} %collective-permute-done.9.refs_2_.refs_1_) | copy-start | bytes 1572868
  65.9 17.7 %collective-permute-start.14 = (bf16[4,256,256]{2,1,0:T(8,128)(2,1)S(1)}, bf16[4,256,256]{2,1,0:T(8,128)(2,1)}, u32[]{:S(2)}, u32[]{:S(2)}) collective-permute-start(bf16[4,256,256]{2,1,0:T(8,128)(2,1)S(1)} %pad_maximum_fusion.2.refs_5_.refs_4_), channel_id=1, source_target_pairs={{0,24},{8,16},{16,8},{24,0},{1,25},{9,17},{17,9},{25,1},{2,26},{10... | collective-permute-start | bytes 1572872 | tf_op jit(solution)/shard_map/ppermute | solution.py:39
  83.6 1.1 copy-start.3
  101.3 17.1 %copy-start.4 = (bf16[4,256,256]{2,1,0:T(8,128)(2,1)S(1)}, bf16[4,256,256]{2,1,0:T(8,128)(2,1)}, u32[]{:S(2)}) copy-start(bf16[4,256,256]{2,1,0:T(8,128)(2,1)} %copy-done.2) | copy-start | bytes 1572868
  111.2 17.1 %collective-permute-start.17 = (bf16[4,256,256]{2,1,0:T(8,128)(2,1)}, bf16[4,256,256]{2,1,0:T(8,128)(2,1)S(1)}, u32[]{:S(2)}, u32[]{:S(2)}) collective-permute-start(bf16[4,256,256]{2,1,0:T(8,128)(2,1)} %get-tuple-element.121), channel_id=1, source_target_pairs={{0,32},{32,64},{64,96},{96,0},{1,33},{33,65},{65,97},{97,1},{2,34}... | collective-permute-start | bytes 1572872 | tf_op jit(solution)/shard_map/ppermute | solution.py:39
  112.4 22.5 %collective-permute-start.16 = (bf16[4,256,256]{2,1,0:T(8,128)(2,1)}, bf16[4,256,256]{2,1,0:T(8,128)(2,1)}, u32[]{:S(2)}, u32[]{:S(2)}) collective-permute-start(bf16[4,256,256]{2,1,0:T(8,128)(2,1)} %get-tuple-element.120), channel_id=1, source_target_pairs={{0,64},{32,96},{64,0},{96,32},{1,65},{33,97},{65,1},{97,33},{2,66}... | collective-permute-start | bytes 1572872 | tf_op jit(solution)/shard_map/ppermute | solution.py:39
  115.6 22.1 %collective-permute-start.15 = (bf16[4,256,256]{2,1,0:T(8,128)(2,1)}, bf16[4,256,256]{2,1,0:T(8,128)(2,1)}, u32[]{:S(2)}, u32[]{:S(2)}) collective-permute-start(bf16[4,256,256]{2,1,0:T(8,128)(2,1)} %get-tuple-element.119), channel_id=1, source_target_pairs={{0,96},{32,0},{64,32},{96,64},{1,97},{33,1},{65,33},{97,65},{2,98}... | collective-permute-start | bytes 1572872 | tf_op jit(solution)/shard_map/ppermute | solution.py:39
  117.7 22.7 %collective-permute-start.23 = (bf16[4,256,256]{2,1,0:T(8,128)(2,1)}, bf16[4,256,256]{2,1,0:T(8,128)(2,1)S(1)}, u32[]{:S(2)}, u32[]{:S(2)}) collective-permute-start(bf16[4,256,256]{2,1,0:T(8,128)(2,1)} %get-tuple-element.125), channel_id=1, source_target_pairs={{0,24},{8,16},{16,8},{24,0},{1,25},{9,17},{17,9},{25,1},{2,26},{10... | collective-permute-start | bytes 1572872 | tf_op jit(solution)/shard_map/ppermute | solution.py:39
  118.4 9.9 %copy-start.13 = (bf16[4,256,256]{2,1,0:T(8,128)(2,1)S(1)}, bf16[4,256,256]{2,1,0:T(8,128)(2,1)}, u32[]{:S(2)}) copy-start(bf16[4,256,256]{2,1,0:T(8,128)(2,1)} %get-tuple-element.123) | copy-start | bytes 1572868
  118.4 19.3 %copy-start.8 = (bf16[4,256,256]{2,1,0:T(8,128)(2,1)S(1)}, bf16[4,256,256]{2,1,0:T(8,128)(2,1)}, u32[]{:S(2)}) copy-start(bf16[4,256,256]{2,1,0:T(8,128)(2,1)} %get-tuple-element.118) | copy-start | bytes 1572868
  118.4 22.5 %collective-permute-start.22 = (bf16[4,256,256]{2,1,0:T(8,128)(2,1)}, bf16[4,256,256]{2,1,0:T(8,128)(2,1)S(1)}, u32[]{:S(2)}, u32[]{:S(2)}) collective-permute-start(bf16[4,256,256]{2,1,0:T(8,128)(2,1)} %get-tuple-element.124), channel_id=1, source_target_pairs={{0,16},{16,0},{1,17},{17,1},{2,18},{18,2},{3,19},{19,3},{4,20},{20... | collective-permute-start | bytes 1572872 | tf_op jit(solution)/shard_map/ppermute | solution.py:39
  128.3 14.3 %copy-start.7 = (bf16[4,256,256]{2,1,0:T(8,128)(2,1)S(1)}, bf16[4,256,256]{2,1,0:T(8,128)(2,1)}, u32[]{:S(2)}) copy-start(bf16[4,256,256]{2,1,0:T(8,128)(2,1)} %get-tuple-element.122) | copy-start | bytes 1572868
  128.3 14.3 %collective-permute-start.21 = (bf16[4,256,256]{2,1,0:T(8,128)(2,1)S(1)}, bf16[4,256,256]{2,1,0:T(8,128)(2,1)S(1)}, u32[]{:S(2)}, u32[]{:S(2)}) collective-permute-start(bf16[4,256,256]{2,1,0:T(8,128)(2,1)S(1)} %copy-done.13), channel_id=1, source_target_pairs={{0,8},{8,0},{1,9},{9,1},{2,10},{10,2},{3,11},{11,3},{4,12},{12,4},... | collective-permute-start | bytes 1572872 | tf_op jit(solution)/shard_map/ppermute | solution.py:39
  134.9 17.4 %collective-permute-start.27 = (bf16[1024,256]{1,0:T(8,128)(2,1)}, bf16[1024,256]{1,0:T(8,128)(2,1)S(1)}, u32[]{:S(2)}, u32[]{:S(2)}) collective-permute-start(bf16[1024,256]{1,0:T(8,128)(2,1)} %get-tuple-element.127), channel_id=1, source_target_pairs={{0,8},{8,0},{1,9},{9,1},{2,10},{10,2},{3,11},{11,3},{4,12},{12,4},... | collective-permute-start | bytes 1572872 | tf_op jit(solution)/shard_map/ppermute | solution.py:39
  139.2 15.9 %copy-start.6 = (bf16[1024,256]{1,0:T(8,128)(2,1)S(1)}, bf16[1024,256]{1,0:T(8,128)(2,1)}, u32[]{:S(2)}) copy-start(bf16[1024,256]{1,0:T(8,128)(2,1)} %get-tuple-element.126) | copy-start | bytes 1572868
  139.2 15.8 %collective-permute-start.18 = (bf16[256,256]{1,0:T(8,128)(2,1)S(1)}, bf16[256,256]{1,0:T(8,128)(2,1)S(1)}, u32[]{:S(2)}, u32[]{:S(2)}) collective-permute-start(bf16[256,256]{1,0:T(8,128)(2,1)S(1)} %get-tuple-element.180), channel_id=1, source_target_pairs={{0,8},{8,0},{1,9},{9,1},{2,10},{10,2},{3,11},{11,3},{4,12},{12,4},... | collective-permute-start | bytes 393224 | tf_op jit(solution)/shard_map/ppermute | solution.py:39
  140.4 16.3 %collective-permute-start.19 = (bf16[256,256]{1,0:T(8,128)(2,1)S(1)}, bf16[256,256]{1,0:T(8,128)(2,1)S(1)}, u32[]{:S(2)}, u32[]{:S(2)}) collective-permute-start(bf16[256,256]{1,0:T(8,128)(2,1)S(1)} %get-tuple-element.179), channel_id=1, source_target_pairs={{0,16},{16,0},{1,17},{17,1},{2,18},{18,2},{3,19},{19,3},{4,20},{20... | collective-permute-start | bytes 393224 | tf_op jit(solution)/shard_map/ppermute | solution.py:39
  140.9 21.5 %collective-permute-start.20 = (bf16[256,256]{1,0:T(8,128)(2,1)S(1)}, bf16[256,256]{1,0:T(8,128)(2,1)S(1)}, u32[]{:S(2)}, u32[]{:S(2)}) collective-permute-start(bf16[256,256]{1,0:T(8,128)(2,1)S(1)} %get-tuple-element.178), channel_id=1, source_target_pairs={{0,24},{8,16},{16,8},{24,0},{1,25},{9,17},{17,9},{25,1},{2,26},{10... | collective-permute-start | bytes 393224 | tf_op jit(solution)/shard_map/ppermute | solution.py:39
  142.9 19.5 %collective-permute-start.24 = (bf16[256,256]{1,0:T(8,128)(2,1)S(1)}, bf16[256,256]{1,0:T(8,128)(2,1)S(1)}, u32[]{:S(2)}, u32[]{:S(2)}) collective-permute-start(bf16[256,256]{1,0:T(8,128)(2,1)S(1)} %get-tuple-element.176), channel_id=1, source_target_pairs={{0,96},{32,0},{64,32},{96,64},{1,97},{33,1},{65,33},{97,65},{2,98}... | collective-permute-start | bytes 393224 | tf_op jit(solution)/shard_map/ppermute | solution.py:39
  152.3 10.1 %collective-permute-start.25 = (bf16[256,256]{1,0:T(8,128)(2,1)S(1)}, bf16[256,256]{1,0:T(8,128)(2,1)S(1)}, u32[]{:S(2)}, u32[]{:S(2)}) collective-permute-start(bf16[256,256]{1,0:T(8,128)(2,1)S(1)} %get-tuple-element.175), channel_id=1, source_target_pairs={{0,64},{32,96},{64,0},{96,32},{1,65},{33,97},{65,1},{97,33},{2,66}... | collective-permute-start | bytes 393224 | tf_op jit(solution)/shard_map/ppermute | solution.py:39
  155.1 7.3 %collective-permute-start.26 = (bf16[256,256]{1,0:T(8,128)(2,1)S(1)}, bf16[256,256]{1,0:T(8,128)(2,1)S(1)}, u32[]{:S(2)}, u32[]{:S(2)}) collective-permute-start(bf16[256,256]{1,0:T(8,128)(2,1)S(1)} %get-tuple-element.174), channel_id=1, source_target_pairs={{0,32},{32,64},{64,96},{96,0},{1,33},{33,65},{65,97},{97,1},{2,34}... | collective-permute-start | bytes 393224 | tf_op jit(solution)/shard_map/ppermute | solution.py:39
  166.0 20.8 %collective-permute-start.28 = (bf16[128,4096]{1,0:T(8,128)(2,1)}, bf16[128,4096]{1,0:T(8,128)(2,1)S(1)}, u32[]{:S(2)}, u32[]{:S(2)}) collective-permute-start(bf16[128,4096]{1,0:T(8,128)(2,1)} %get-tuple-element.131.grad_ref), channel_id=1, source_target_pairs={{1,0},{2,1},{3,2},{4,3},{5,4},{6,5},{7,6},{8,7},{9,8},{10,9},{11,1... | collective-permute-start | bytes 3145736 | tf_op jit(solution)/shard_map/ppermute | solution.py:27
  198.9 1.6 collective-permute-start.30
  200.5 8.5 %collective-permute-start.33 = (f32[16,8,128]{2,1,0:T(8,128)S(1)}, f32[16,8,128]{2,1,0:T(8,128)S(1)}, u32[]{:S(2)}, u32[]{:S(2)}) collective-permute-start(f32[16,8,128]{2,1,0:T(8,128)S(1)} %get-tuple-element.183), channel_id=1, source_target_pairs={{0,6},{2,0},{4,2},{6,4},{1,7},{3,1},{5,3},{7,5},{8,14},{10,8},{12,... | collective-permute-start | bytes 196616 | tf_op jit(solution)/shard_map/ppermute | solution.py:39
  205.0 4.7 %collective-permute-start.32 = (f32[16,8,128]{2,1,0:T(8,128)S(1)}, f32[16,8,128]{2,1,0:T(8,128)S(1)}, u32[]{:S(2)}, u32[]{:S(2)}) collective-permute-start(f32[16,8,128]{2,1,0:T(8,128)S(1)} %get-tuple-element.184), channel_id=1, source_target_pairs={{0,4},{2,6},{4,0},{6,2},{1,5},{3,7},{5,1},{7,3},{8,12},{10,14},{12... | collective-permute-start | bytes 196616 | tf_op jit(solution)/shard_map/ppermute | solution.py:39
  205.4 6.4 %collective-permute-start.31 = (f32[16,8,128]{2,1,0:T(8,128)S(1)}, f32[16,8,128]{2,1,0:T(8,128)S(1)}, u32[]{:S(2)}, u32[]{:S(2)}) collective-permute-start(f32[16,8,128]{2,1,0:T(8,128)S(1)} %get-tuple-element.182), channel_id=1, source_target_pairs={{0,2},{2,4},{4,6},{6,0},{1,3},{3,5},{5,7},{7,1},{8,10},{10,12},{12... | collective-permute-start | bytes 196616 | tf_op jit(solution)/shard_map/ppermute | solution.py:39
  206.2 8.6 %collective-permute-start.29 = (bf16[3,8,4096]{2,1,0:T(8,128)(2,1)S(1)}, bf16[3,8,4096]{2,1,0:T(8,128)(2,1)S(1)}, u32[]{:S(2)}, u32[]{:S(2)}) collective-permute-start(bf16[3,8,4096]{2,1,0:T(8,128)(2,1)S(1)} %get-tuple-element.145), channel_id=1, source_target_pairs={{1,0},{2,1},{3,2},{4,3},{5,4},{6,5},{7,6},{8,7},{9,8},{10,9},{11,1... | collective-permute-start | bytes 589832 | tf_op jit(solution)/shard_map/ppermute | solution.py:27
  211.9 6.1 %collective-permute-start.34 = (f32[16,8,128]{2,1,0:T(8,128)S(1)}, f32[16,8,128]{2,1,0:T(8,128)S(1)}, u32[]{:S(2)}, u32[]{:S(2)}) collective-permute-start(f32[16,8,128]{2,1,0:T(8,128)S(1)} %fusion.1), channel_id=1, source_target_pairs={{0,32},{32,64},{64,96},{96,0},{1,33},{33,65},{65,97},{97,1},{2,34}... | collective-permute-start | bytes 196616 | tf_op jit(solution)/shard_map/ppermute | solution.py:39
  212.3 5.7 %collective-permute-start.35 = (f32[16,8,128]{2,1,0:T(8,128)S(1)}, f32[16,8,128]{2,1,0:T(8,128)S(1)}, u32[]{:S(2)}, u32[]{:S(2)}) collective-permute-start(f32[16,8,128]{2,1,0:T(8,128)S(1)} %fusion.1), channel_id=1, source_target_pairs={{0,64},{32,96},{64,0},{96,32},{1,65},{33,97},{65,1},{97,33},{2,66}... | collective-permute-start | bytes 196616 | tf_op jit(solution)/shard_map/ppermute | solution.py:39
  212.7 5.2 %collective-permute-start.36 = (f32[16,8,128]{2,1,0:T(8,128)S(1)}, f32[16,8,128]{2,1,0:T(8,128)S(1)}, u32[]{:S(2)}, u32[]{:S(2)}) collective-permute-start(f32[16,8,128]{2,1,0:T(8,128)S(1)} %fusion.1), channel_id=1, source_target_pairs={{0,96},{32,0},{64,32},{96,64},{1,97},{33,1},{65,33},{97,65},{2,98}... | collective-permute-start | bytes 196616 | tf_op jit(solution)/shard_map/ppermute | solution.py:39
  218.0 6.7 %collective-permute-start.37 = (f32[16,8,128]{2,1,0:T(8,128)S(1)}, f32[16,8,128]{2,1,0:T(8,128)S(1)}, u32[]{:S(2)}, u32[]{:S(2)}) collective-permute-start(f32[16,8,128]{2,1,0:T(8,128)S(1)} %add_add_fusion.1), channel_id=1, source_target_pairs={{0,8},{8,0},{1,9},{9,1},{2,10},{10,2},{3,11},{11,3},{4,12},{12,4},... | collective-permute-start | bytes 196616 | tf_op jit(solution)/shard_map/ppermute | solution.py:39
  218.8 5.9 %collective-permute-start.38 = (f32[16,8,128]{2,1,0:T(8,128)S(1)}, f32[16,8,128]{2,1,0:T(8,128)S(1)}, u32[]{:S(2)}, u32[]{:S(2)}) collective-permute-start(f32[16,8,128]{2,1,0:T(8,128)S(1)} %add_add_fusion.1), channel_id=1, source_target_pairs={{0,16},{16,0},{1,17},{17,1},{2,18},{18,2},{3,19},{19,3},{4,20},{20... | collective-permute-start | bytes 196616 | tf_op jit(solution)/shard_map/ppermute | solution.py:39
  219.8 4.9 %collective-permute-start.39 = (f32[16,8,128]{2,1,0:T(8,128)S(1)}, f32[16,8,128]{2,1,0:T(8,128)S(1)}, u32[]{:S(2)}, u32[]{:S(2)}) collective-permute-start(f32[16,8,128]{2,1,0:T(8,128)S(1)} %add_add_fusion.1), channel_id=1, source_target_pairs={{0,24},{8,16},{16,8},{24,0},{1,25},{9,17},{17,9},{25,1},{2,26},{10... | collective-permute-start | bytes 196616 | tf_op jit(solution)/shard_map/ppermute | solution.py:39
  224.8 3.9 %collective-permute-start.40 = (f32[16,8,128]{2,1,0:T(8,128)S(1)}, f32[16,8,128]{2,1,0:T(8,128)S(1)}, u32[]{:S(2)}, u32[]{:S(2)}) collective-permute-start(f32[16,8,128]{2,1,0:T(8,128)S(1)} %add_add_fusion), channel_id=1, source_target_pairs={{0,1},{1,0},{2,3},{3,2},{4,5},{5,4},{6,7},{7,6},{8,9},{9,8},{10,11... | collective-permute-start | bytes 196616 | tf_op jit(solution)/shard_map/ppermute | solution.py:39
  228.7 6.3 %collective-permute-start.41 = (f32[32,8,128]{2,1,0:T(8,128)S(1)}, f32[32,8,128]{2,1,0:T(8,128)S(1)}, u32[]{:S(2)}, u32[]{:S(2)}) collective-permute-start(f32[32,8,128]{2,1,0:T(8,128)S(1)} %pad_maximum_fusion.3.refs_0_), channel_id=1, source_target_pairs={{0,6},{2,0},{4,2},{6,4},{1,7},{3,1},{5,3},{7,5},{8,14},{10,8},{12,... | collective-permute-start | bytes 393224 | tf_op jit(solution)/shard_map/ppermute | solution.py:39
  230.1 6.2 %collective-permute-start.42 = (f32[32,8,128]{2,1,0:T(8,128)S(1)}, f32[32,8,128]{2,1,0:T(8,128)S(1)}, u32[]{:S(2)}, u32[]{:S(2)}) collective-permute-start(f32[32,8,128]{2,1,0:T(8,128)S(1)} %pad_maximum_fusion.3.refs_0_), channel_id=1, source_target_pairs={{0,4},{2,6},{4,0},{6,2},{1,5},{3,7},{5,1},{7,3},{8,12},{10,14},{12... | collective-permute-start | bytes 393224 | tf_op jit(solution)/shard_map/ppermute | solution.py:39
  230.1 9.1 %collective-permute-start.43 = (f32[32,8,128]{2,1,0:T(8,128)S(1)}, f32[32,8,128]{2,1,0:T(8,128)S(1)}, u32[]{:S(2)}, u32[]{:S(2)}) collective-permute-start(f32[32,8,128]{2,1,0:T(8,128)S(1)} %pad_maximum_fusion.3.refs_0_), channel_id=1, source_target_pairs={{0,2},{2,4},{4,6},{6,0},{1,3},{3,5},{5,7},{7,1},{8,10},{10,12},{12... | collective-permute-start | bytes 393224 | tf_op jit(solution)/shard_map/ppermute | solution.py:39
Sparse Core Ops, SparseCore 0:
  46.2 54.9 all-gather.1
  103.6 54.7 reduce-scatter.1

commit v13 on v12

--- a/solution.py
+++ b/solution.py
@@ -672,13 +672,14 @@
     return total
 
 
-def plane_scatter(top_grads, bottom_grads):
+def plane_scatter(top_grads, bottom_grads, beside):
     ny = len(top_grads)
     top = added([move(top_grads[d], y=-d) for d in range(ny)]).astype(BF16)
     bottom = added([move(bottom_grads[f], xl=a, xh=b) for f, (a, b) in enumerate(FLIPS)]).astype(BF16)
+    top, bottom, beside = lax.optimization_barrier((top, bottom, beside))
     top = [move(top[f], xl=a, xh=b) for f, (a, b) in enumerate(FLIPS)]
     bottom = [move(bottom[d], y=-d) for d in range(ny)]
-    return top, bottom
+    return top, bottom, beside
 
 
 def shards(tokens_in, short_filter, long_filter, out_weight, cotangent):
@@ -727,10 +728,8 @@
 
     top_grads, bottom_grads = weight_grad(origin, all_rows, cotangents.T, ny)
     own, other = output_call(origin, all_rows, tops, bottoms)
-    top, bottom = plane_scatter(top_grads, bottom_grads)
-    theirs = move(other, xh=1)
-    output = jnp.where(xh == 0, jnp.concatenate([own, theirs], axis=0), jnp.concatenate([theirs, own], axis=0))
-    gate_grad, top, bottom, output = lax.optimization_barrier((gate_grad, top, bottom, output))
+    top, bottom, other = plane_scatter(top_grads, bottom_grads, other)
+    gate_grad, top, bottom, other = lax.optimization_barrier((gate_grad, top, bottom, other))
 
     grad_mixed, query_grad = gate_call(place, gate_grad, query, mixed)
     grad_next = along(grad_mixed, -1)
@@ -738,10 +737,15 @@
         groups, short_taps, mixer_prev, mixer, grad_mixed, query_grad, tokens, rim
     )
     grad_weight = jnp.concatenate([added(top), added(bottom)], axis=1).T
-    grad_next, grad_weight = lax.optimization_barrier((grad_next, grad_weight))
+    grad_next, grad_weight, other, long_sum, query_sum = lax.optimization_barrier(
+        (grad_next, grad_weight, other, long_sum, query_sum)
+    )
+    theirs = move(other, xh=1)
     other_grads, key_sum, value_sum, edge = unmix_call(
         lines, short_taps, grad_mixed, grad_next, key, value, tokens, rim, query_grad
     )
+    edge, key_sum, theirs = lax.optimization_barrier((edge, key_sum, theirs))
+    output = jnp.where(xh == 0, jnp.concatenate([own, theirs], axis=0), jnp.concatenate([theirs, own], axis=0))
     edge = along(edge, -1)
     query_part = short_adjoint_call(query_grad[None], edge, short_filter, 0, 0, None)
 

time: 248 us -> 246 us (level)
  starting transfers between devices: 74.2 us -> 70.1 us
  waiting for transfers between devices: 65 us -> 68.1 us
    ppermute x40, waiting for transfers between devices: 51.1 us -> 39.1 us  [move(): return lax.ppermute(x, axes, pairs)]
    reduce_scatter x1, waiting for transfers between devices: 0.02 us -> 11.4 us  [shards(): lax.psum_scatter(partial, ('z', 'c'), scatter_dimension=0, tiled=True)]
    ppermute x4, starting transfers between devices: 17.5 us -> 12.7 us  [along(): return lax.ppermute(x, LINE, pairs)]
    all_gather x1, waiting for transfers between devices: 7.96 us -> 11.3 us  [shards(): all_rows = lax.all_gather(gated, ('z', 'c'), axis=0, tiled=True)]
  transfers between devices with their start and end apart: 46 -> 46, of which waited for: 24 -> 28; matrix products, arithmetic and copies ran while one was open for 3% -> 3% of each run, Pallas kernels for 22% -> 27%
where the time goes in v13:
time: 246 us; the launch traced here: 245 us
  Pallas kernels  83.3 us (34%)
  starting transfers between devices  70.1 us (28%)
  waiting for transfers between devices  68.1 us (28%)
  between operations  14.4 us (6%)
  local copies, waits for them, and re-layouts  5.12 us (2%)
  other arithmetic  4.34 us (2%)
    pallas_call x12, Pallas kernels, run(): return call(*held)  81.1 us
    ppermute x40, starting transfers between devices, move(): return lax.ppermute(x, axes, pairs)  57.3 us
    ppermute x40, waiting for transfers between devices, move(): return lax.ppermute(x, axes, pairs)  39.1 us
    ppermute x4, starting transfers between devices, along(): return lax.ppermute(x, LINE, pairs)  12.7 us
    reduce_scatter x1, waiting for transfers between devices, shards(): lax.psum_scatter(partial, ('z', 'c'), scatter_dimension=0, tiled=True)  11.4 us
    all_gather x1, waiting for transfers between devices, shards(): all_rows = lax.all_gather(gated, ('z', 'c'), axis=0, tiled=True)  11.3 us
    ppermute x4, waiting for transfers between devices, along(): return lax.ppermute(x, LINE, pairs)  6.29 us
  transfers between devices with their start and end apart: 46, of which 28 were waited for; matrix products, arithmetic and copies ran while one was open for 3% of the time, Pallas kernels for 27%

profile of v13, /device:TPU:1, one launch (start us, length us, event | category | flops | bytes accessed | tf_op | source)
XLA Modules:
  0.0 245.3 jit_solution(7932601279482931101)
XLA Ops:
  8.2 4.9 %collective-permute-start = (bf16[8,12288]{1,0:T(8,128)(2,1)S(1)}, bf16[8,12288]{1,0:T(8,128)(2,1)S(1)}, u32[]{:S(2)}, u32[]{:S(2)}) collective-permute-start(bf16[8,12288]{1,0:T(8,128)(2,1)S(1)} %slice_bitcast_fusion), channel_id=1, source_target_pairs={{0,1},{1,2},{2,3},{3,4},{4,5},{5,6},{6,7},{7,8},{8,9},{9,10},{10,1... | collective-permute-start | bytes 589832 | tf_op jit(solution)/shard_map/ppermute | solution.py:27
  13.1 6.7 %features.1 = (bf16[128,4096]{1,0:T(8,128)(2,1)}, bf16[128,4096]{1,0:T(8,128)(2,1)}, bf16[128,4096]{1,0:T(8,128)(2,1)}, bf16[128,4096]{1,0:T(8,128)(2,1)}) custom-call(bf16[128,12288]{1,0:T(8,128)(2,1)} %bitcast.37, bf16[128,12288]{1,0:T(8,128)(2,1)} %bitcast.38, bf16[128,12288]{1,0:T(8,128)(2,1)} %bitcast.39, f32[7,12288]{1,0:T(8,128)} %filter_ref.5, ...), custom_call_target="tpu_custom_call" | custom-call | bytes 1572864 | tf_op jit(solution)/shard_map/features/pallas_call | solution.py:64
  19.9 2.6 %first_rows.1 = (bf16[128,4096]{1,0:T(8,128)(2,1)}, bf16[128,4096]{1,0:T(8,128)(2,1)}, bf16[128,4096]{1,0:T(8,128)(2,1)}, bf16[128,4096]{1,0:T(8,128)(2,1)}) custom-call(bf16[128,12288]{1,0:T(8,128)(2,1)} %bitcast.40, bf16[128,12288]{1,0:T(8,128)(2,1)} %bitcast.41, ...), custom_call_target="tpu_custom_call", output_to_operand_aliasing={{0}: (9, {}), {1}: (10, {}), {2}: (11, {}), {3}: (12, {})} | custom-call | bytes 196608 | tf_op jit(solution)/shard_map/first_rows/pallas_call | solution.py:64
  22.4 1.9 collective-permute-start.1
  24.4 1.4 collective-permute-start.2
  25.8 2.6 %collective-permute-start.3 = (bf16[256,256]{1,0:T(8,128)(2,1)S(1)}, bf16[256,256]{1,0:T(8,128)(2,1)S(1)}, u32[]{:S(2)}, u32[]{:S(2)}) collective-permute-start(bf16[256,256]{1,0:T(8,128)(2,1)S(1)} %slice.56), channel_id=1, source_target_pairs={{0,64},{32,96},{64,0},{96,32},{1,65},{33,97},{65,1},{97,33},{2,66}... | collective-permute-start | bytes 393224 | tf_op jit(solution)/shard_map/ppermute | solution.py:39
  28.4 1.1 collective-permute-start.4
  30.3 3.9 %collective-permute-done.3 = bf16[256,256]{1,0:T(8,128)(2,1)S(1)} collective-permute-done((bf16[256,256]{1,0:T(8,128)(2,1)S(1)}, bf16[256,256]{1,0:T(8,128)(2,1)S(1)}, u32[]{:S(2)}, u32[]{:S(2)}) %collective-permute-start.3) | collective-permute-done | bytes 131104 | tf_op jit(solution)/shard_map/ppermute | solution.py:39
  34.2 2.2 collective-permute-done.1.prev_ref
  36.4 9.8 %mix.1 = (bf16[128,4096]{1,0:T(8,128)(2,1)}, bf16[128,4096]{1,0:T(8,128)(2,1)}) custom-call(f32[256,128]{1,0:T(8,128)S(1)} %convert_element_type.57.lines_ref, bf16[128,4096]{1,0:T(8,128)(2,1)S(1)} %collective-permute-done.1.prev_ref, bf16[128,4096]{1,0:T(8,128)(2,1)} %get-tuple-element.104.cur_ref, bf16[128,4096]{1,0:T(8,128)(2,1)} %get-tuple-element.107.query_ref), custom_call_target="tpu_custom_call" | custom-call | bytes 1048576 | tf_op jit(solution)/shard_map/mix/pallas_call | solution.py:64
  46.3 2.8 %collective-permute-start.5 = (bf16[256,256]{1,0:T(8,128)(2,1)S(1)}, bf16[256,256]{1,0:T(8,128)(2,1)S(1)}, u32[]{:S(2)}, u32[]{:S(2)}) collective-permute-start(bf16[256,256]{1,0:T(8,128)(2,1)S(1)} %slice.57), channel_id=1, source_target_pairs={{0,8},{8,0},{1,9},{9,1},{2,10},{10,2},{3,11},{11,3},{4,12},{12,4},... | collective-permute-start | bytes 393224 | tf_op jit(solution)/shard_map/ppermute | solution.py:39
  50.0 1.7 collective-permute-done.5
  51.7 1.6 collective-permute-done.6
  53.3 1.3 collective-permute-done.7
  54.6 1.5 collective-permute-start.12
  56.4 1.7 collective-permute-start.8
  58.0 1.7 collective-permute-start.14
  59.7 1.1 pad_maximum_fusion.1.refs_1_.refs_0_
  60.8 3.0 %collective-permute-start.10 = (bf16[4,256,256]{2,1,0:T(8,128)(2,1)S(1)}, bf16[4,256,256]{2,1,0:T(8,128)(2,1)}, u32[]{:S(2)}, u32[]{:S(2)}) collective-permute-start(bf16[4,256,256]{2,1,0:T(8,128)(2,1)S(1)} %pad_maximum_fusion.1.refs_1_.refs_0_), channel_id=1, source_target_pairs={{0,64},{32,96},{64,0},{96,32},{1,65},{33,97},{65,1},{97,33},{2,66}... | collective-permute-start | bytes 1572872 | tf_op jit(solution)/shard_map/ppermute | solution.py:39
  63.8 1.3 collective-permute-done.12.refs_6_.refs_5_
  65.1 2.7 %collective-permute-start.11 = (bf16[4,256,256]{2,1,0:T(8,128)(2,1)S(1)}, bf16[4,256,256]{2,1,0:T(8,128)(2,1)}, u32[]{:S(2)}, u32[]{:S(2)}) collective-permute-start(bf16[4,256,256]{2,1,0:T(8,128)(2,1)S(1)} %pad_maximum_fusion.1.refs_1_.refs_0_), channel_id=1, source_target_pairs={{0,96},{32,0},{64,32},{96,64},{1,97},{33,1},{65,33},{97,65},{2,98}... | collective-permute-start | bytes 1572872 | tf_op jit(solution)/shard_map/ppermute | solution.py:39
  67.8 2.9 %collective-permute-done.8 = bf16[1024,256]{0,1:T(8,128)(2,1)S(1)} collective-permute-done((bf16[1024,256]{0,1:T(8,128)(2,1)S(1)}, bf16[1024,256]{0,1:T(8,128)(2,1)S(1)}, u32[]{:S(2)}, u32[]{:S(2)}) %collective-permute-start.8) | collective-permute-done | bytes 524320 | tf_op jit(solution)/shard_map/ppermute | solution.py:39
  70.7 1.3 collective-permute-start.9
  72.2 1.1 fusion.11
  73.4 1.5 copy.18.refs_0_
  74.9 2.4 collective-permute-done.13.refs_7_.refs_6_
  78.1 2.4 collective-permute-done.9.refs_2_.refs_1_
  80.4 1.1 copy-done.3
  81.5 8.5 %gate_matmul.1 = bf16[1024,4096]{1,0:T(8,128)(2,1)} custom-call(bf16[1024,512]{1,0:T(8,128)(2,1)S(1)} %copy.18.refs_0_, bf16[4,256,256]{2,1,0:T(8,128)(2,1)S(1)} %pad_maximum_fusion.1.refs_1_.refs_0_, bf16[4,256,256]{2,1,0:T(8,128)(2,1)} %collective-permute-done.9.refs_2_.refs_1_, bf16[4,256,256]{2,1,0:T(8,128)(2,1)} %collective-permute-done.10.refs_3_.refs_2_, ...), custom_call_target="tpu_custom_call" | custom-call | flops 4294967296 | bytes 12582912 | tf_op jit(solution)/shard_map/gate_matmul/pallas_call | solution.py:64
  90.0 11.3 %all-gather.2.cloned.1.call-done.rows_ref = bf16[1024,4096]{1,0:T(8,128)(2,1)} async-done(((bf16[128,4096]{1,0:T(8,128)(2,1)}), bf16[1024,4096]{1,0:T(8,128)(2,1)}) %all-gather.2.cloned.1.call-update) | async-done | bytes 8388624 | tf_op jit(solution)/shard_map/all_gather | solution.py:720
  101.3 9.9 %weight_grad.1 = (bf16[4,256,256]{2,1,0:T(8,128)(2,1)}, bf16[4,256,256]{2,1,0:T(8,128)(2,1)}, bf16[4,256,256]{2,1,0:T(8,128)(2,1)}, bf16[4,256,256]{2,1,0:T(8,12...) custom-call(s32[8]{0:T(128)S(1)} %fusion.2.origin.place, ...), custom_call_target="tpu_custom_call" | custom-call | flops 4294967296 | bytes 12582912 | tf_op jit(solution)/shard_map/weight_grad/pallas_call | solution.py:64
  111.2 2.7 %collective-permute-start.18 = (bf16[4,256,256]{2,1,0:T(8,128)(2,1)}, bf16[4,256,256]{2,1,0:T(8,128)(2,1)S(1)}, u32[]{:S(2)}, u32[]{:S(2)}) collective-permute-start(bf16[4,256,256]{2,1,0:T(8,128)(2,1)} %get-tuple-element.133), channel_id=1, source_target_pairs={{0,8},{8,0},{1,9},{9,1},{2,10},{10,2},{3,11},{11,3},{4,12},{12,4},... | collective-permute-start | bytes 1572872 | tf_op jit(solution)/shard_map/ppermute | solution.py:39
  114.8 2.5 %collective-permute-start.15 = (bf16[4,256,256]{2,1,0:T(8,128)(2,1)}, bf16[4,256,256]{2,1,0:T(8,128)(2,1)S(1)}, u32[]{:S(2)}, u32[]{:S(2)}) collective-permute-start(bf16[4,256,256]{2,1,0:T(8,128)(2,1)} %get-tuple-element.129), channel_id=1, source_target_pairs={{0,96},{32,0},{64,32},{96,64},{1,97},{33,1},{65,33},{97,65},{2,98}... | collective-permute-start | bytes 1572872 | tf_op jit(solution)/shard_map/ppermute | solution.py:39
  117.8 3.3 %collective-permute-done.18 = bf16[4,256,256]{2,1,0:T(8,128)(2,1)S(1)} collective-permute-done((bf16[4,256,256]{2,1,0:T(8,128)(2,1)}, bf16[4,256,256]{2,1,0:T(8,128)(2,1)S(1)}, u32[]{:S(2)}, u32[]{:S(2)}) %collective-permute-start.18) | collective-permute-done | bytes 524320 | tf_op jit(solution)/shard_map/ppermute | solution.py:39
  121.1 1.2 collective-permute-start.17
  122.3 9.9 %output.1 = (bf16[1024,256]{1,0:T(8,128)(2,1)}, bf16[1024,256]{1,0:T(8,128)(2,1)}) custom-call(s32[8]{0:T(128)S(1)} %fusion.2.origin.place, bf16[1024,4096]{1,0:T(8,128)(2,1)} %all-gather.2.cloned.1.call-done.rows_ref, bf16[4,256,256]{2,1,0:T(8,128)(2,1)S(1)} %pad_maximum_fusion.1.refs_1_.refs_0_, ...), custom_call_target="tpu_custom_call" | custom-call | flops 4294967296 | bytes 12582912 | tf_op jit(solution)/shard_map/output/pallas_call | solution.py:64
  133.2 1.2 collective-permute-done.17
  134.8 3.1 %collective-permute-start.21 = (bf16[256,256]{1,0:T(8,128)(2,1)S(1)}, bf16[256,256]{1,0:T(8,128)(2,1)S(1)}, u32[]{:S(2)}, u32[]{:S(2)}) collective-permute-start(bf16[256,256]{1,0:T(8,128)(2,1)S(1)} %get-tuple-element.198), channel_id=1, source_target_pairs={{0,8},{8,0},{1,9},{9,1},{2,10},{10,2},{3,11},{11,3},{4,12},{12,4},... | collective-permute-start | bytes 393224 | tf_op jit(solution)/shard_map/ppermute | solution.py:39
  138.9 2.7 %collective-permute-start.24 = (bf16[256,256]{1,0:T(8,128)(2,1)S(1)}, bf16[256,256]{1,0:T(8,128)(2,1)S(1)}, u32[]{:S(2)}, u32[]{:S(2)}) collective-permute-start(bf16[256,256]{1,0:T(8,128)(2,1)S(1)} %get-tuple-element.194), channel_id=1, source_target_pairs={{0,96},{32,0},{64,32},{96,64},{1,97},{33,1},{65,33},{97,65},{2,98}... | collective-permute-start | bytes 393224 | tf_op jit(solution)/shard_map/ppermute | solution.py:39
  143.8 1.1 collective-permute-done.24
  144.9 2.1 collective-permute-done.25
  147.0 1.7 collective-permute-done.26
  148.7 11.4 %reduce-scatter.2.cloned.1.call-done.gate_grad_ref = bf16[128,4096]{1,0:T(8,128)(2,1)} async-done(((bf16[1024,4096]{1,0:T(8,128)(2,1)}), bf16[128,4096]{1,0:T(8,128)(2,1)}) %reduce-scatter.2.cloned.1.call-update) | async-done | bytes 1048592 | tf_op jit(solution)/shard_map/reduce_scatter | solution.py:727
  160.1 3.6 %gate_back.1 = (bf16[128,4096]{1,0:T(8,128)(2,1)}, bf16[128,4096]{1,0:T(8,128)(2,1)}) custom-call(s32[8]{0:T(128)S(1)} %fusion.2.origin.place, bf16[128,4096]{1,0:T(8,128)(2,1)} %reduce-scatter.2.cloned.1.call-done.gate_grad_ref, bf16[128,4096]{1,0:T(8,128)(2,1)} %get-tuple-element.107.query_ref, bf16[128,4096]{1,0:T(8,128)(2,1)} %get-tuple-element.141.mixed_ref), custom_call_target="tpu_custom_call" | custom-call | flops 1048576 | bytes 5242880 | tf_op jit(solution)/shard_map/gate_back/pallas_call | solution.py:64
  163.7 3.3 %collective-permute-start.27 = (bf16[128,4096]{1,0:T(8,128)(2,1)}, bf16[128,4096]{1,0:T(8,128)(2,1)S(1)}, u32[]{:S(2)}, u32[]{:S(2)}) collective-permute-start(bf16[128,4096]{1,0:T(8,128)(2,1)} %get-tuple-element.142.grad_ref), channel_id=1, source_target_pairs={{1,0},{2,1},{3,2},{4,3},{5,4},{6,5},{7,6},{8,7},{9,8},{10,9},{11,1... | collective-permute-start | bytes 3145736 | tf_op jit(solution)/shard_map/ppermute | solution.py:27
  167.2 9.2 %long_grad.1 = (f32[256,128]{1,0:T(8,128)S(1)}, f32[8,4096]{1,0:T(8,128)S(1)}) custom-call(bf16[128,4096]{1,0:T(8,128)(2,1)} %copy-done.1, bf16[128,4096]{1,0:T(8,128)(2,1)} %get-tuple-element.104.cur_ref, bf16[128,4096]{1,0:T(8,128)(2,1)} %get-tuple-element.142.grad_ref, bf16[128,4096]{1,0:T(8,128)(2,1)} %get-tuple-element.152.feature_ref.query_grad_ref, ...), custom_call_target="tpu_custom_call" | custom-call | flops 2147483648 | bytes 5242880 | tf_op jit(solution)/shard_map/long_grad/pallas_call | solution.py:64
  176.4 3.6 %collective-permute-done.27.next_ref = bf16[128,4096]{1,0:T(8,128)(2,1)S(1)} collective-permute-done((bf16[128,4096]{1,0:T(8,128)(2,1)}, bf16[128,4096]{1,0:T(8,128)(2,1)S(1)}, u32[]{:S(2)}, u32[]{:S(2)}) %collective-permute-start.27) | collective-permute-done | bytes 1048608 | tf_op jit(solution)/shard_map/ppermute | solution.py:27
  180.0 2.7 %collective-permute-start.28 = (bf16[1024,256]{1,0:T(8,128)(2,1)S(1)}, bf16[1024,256]{1,0:T(8,128)(2,1)S(1)}, u32[]{:S(2)}, u32[]{:S(2)}) collective-permute-start(bf16[1024,256]{1,0:T(8,128)(2,1)S(1)} %copy-done.11), channel_id=1, source_target_pairs={{0,8},{8,0},{1,9},{9,1},{2,10},{10,2},{3,11},{11,3},{4,12},{12,4},... | collective-permute-start | bytes 1572872 | tf_op jit(solution)/shard_map/ppermute | solution.py:39
  182.7 11.4 %unmix.1 = (bf16[2,128,4096]{2,1,0:T(8,128)(2,1)}, f32[8,4096]{1,0:T(8,128)S(1)}, f32[8,4096]{1,0:T(8,128)S(1)}, bf16[3,8,4096]{2,1,0:T(8,128)(2,1)S(1)}) custom-call(f32[256,128]{1,0:T(8,128)S(1)} %convert_element_type.57.lines_ref, bf16[128,4096]{1,0:T(8,128)(2,1)} %get-tuple-element.142.grad_ref, bf16[128,4096]{1,0:T(8,128)(2,1)S(1)} %collective-permute-done.27.next_ref, ...), custom_call_target="tpu_custom_call" | custom-call | flops 2147483648 | bytes 8388608 | tf_op jit(solution)/shard_map/unmix/pallas_call | solution.py:64
  194.1 1.2 collective-permute-done.28
  196.6 1.2 collective-permute-done.30
  198.1 4.2 %collective-permute-start.32 = (f32[16,8,128]{2,1,0:T(8,128)S(1)}, f32[16,8,128]{2,1,0:T(8,128)S(1)}, u32[]{:S(2)}, u32[]{:S(2)}) collective-permute-start(f32[16,8,128]{2,1,0:T(8,128)S(1)} %get-tuple-element.202), channel_id=1, source_target_pairs={{0,4},{2,6},{4,0},{6,2},{1,5},{3,7},{5,1},{7,3},{8,12},{10,14},{12... | collective-permute-start | bytes 196616 | tf_op jit(solution)/shard_map/ppermute | solution.py:39
  202.4 2.6 %collective-permute-start.29 = (bf16[3,8,4096]{2,1,0:T(8,128)(2,1)S(1)}, bf16[3,8,4096]{2,1,0:T(8,128)(2,1)S(1)}, u32[]{:S(2)}, u32[]{:S(2)}) collective-permute-start(bf16[3,8,4096]{2,1,0:T(8,128)(2,1)S(1)} %get-tuple-element.163), channel_id=1, source_target_pairs={{1,0},{2,1},{3,2},{4,3},{5,4},{6,5},{7,6},{8,7},{9,8},{10,9},{11,1... | collective-permute-start | bytes 589832 | tf_op jit(solution)/shard_map/ppermute | solution.py:27
  206.1 2.5 %collective-permute-start.35 = (f32[16,8,128]{2,1,0:T(8,128)S(1)}, f32[16,8,128]{2,1,0:T(8,128)S(1)}, u32[]{:S(2)}, u32[]{:S(2)}) collective-permute-start(f32[16,8,128]{2,1,0:T(8,128)S(1)} %fusion.1), channel_id=1, source_target_pairs={{0,64},{32,96},{64,0},{96,32},{1,65},{33,97},{65,1},{97,33},{2,66}... | collective-permute-start | bytes 196616 | tf_op jit(solution)/shard_map/ppermute | solution.py:39
  210.0 3.2 %short_adjoint.3.refs_0_ = bf16[128,12288]{1,0:T(8,128)(2,1)} custom-call(bf16[1,128,4096]{2,1,0:T(8,128)(2,1)} %bitcast.47, bf16[3,8,4096]{2,1,0:T(8,128)(2,1)S(1)} %collective-permute-done.29.rim_ref, f32[7,12288]{1,0:T(8,128)} %filter_ref.5), custom_call_target="tpu_custom_call" | custom-call | flops 7340032 | bytes 2097152 | tf_op jit(solution)/shard_map/short_adjoint/pallas_call | solution.py:64
  213.2 2.3 collective-permute-start.37
  216.8 3.2 %short_adjoint.4.refs_0_ = bf16[128,12288]{1,0:T(8,128)(2,1)} custom-call(bf16[2,128,4096]{2,1,0:T(8,128)(2,1)} %get-tuple-element.162.grads_ref, bf16[3,8,4096]{2,1,0:T(8,128)(2,1)S(1)} %collective-permute-done.29.rim_ref, f32[7,12288]{1,0:T(8,128)} %filter_ref.5, bf16[128,12288]{1,0:T(8,128)(2,1)} %short_adjoint.3.refs_0_), custom_call_target="tpu_custom_call", output_to_operand_aliasing={{}: (3, {})} | custom-call | flops 7340032 | bytes 2097152 | tf_op jit(solution)/shard_map/short_adjoint/pallas_call | solution.py:64
  221.0 3.4 %collective-permute-start.40 = (f32[16,8,128]{2,1,0:T(8,128)S(1)}, f32[16,8,128]{2,1,0:T(8,128)S(1)}, u32[]{:S(2)}, u32[]{:S(2)}) collective-permute-start(f32[16,8,128]{2,1,0:T(8,128)S(1)} %add_add_fusion), channel_id=1, source_target_pairs={{0,1},{1,0},{2,3},{3,2},{4,5},{5,4},{6,7},{7,6},{8,9},{9,8},{10,11... | collective-permute-start | bytes 196616 | tf_op jit(solution)/shard_map/ppermute | solution.py:39
  224.4 1.0 copy.19
  225.4 1.8 collective-permute-start.41
  227.9 1.2 maximum_select_fusion
  229.2 3.2 %short_adjoint.5 = bf16[128,12288]{1,0:T(8,128)(2,1)} custom-call(bf16[2,128,4096]{2,1,0:T(8,128)(2,1)} %get-tuple-element.162.grads_ref, bf16[3,8,4096]{2,1,0:T(8,128)(2,1)S(1)} %collective-permute-done.29.rim_ref, f32[7,12288]{1,0:T(8,128)} %filter_ref.5, bf16[128,12288]{1,0:T(8,128)(2,1)} %short_adjoint.4.refs_0_), custom_call_target="tpu_custom_call", output_to_operand_aliasing={{}: (3, {})} | custom-call | flops 7340032 | bytes 2097152 | tf_op jit(solution)/shard_map/short_adjoint/pallas_call | solution.py:64
  233.3 3.6 %collective-permute-done.43.refs_3_ = f32[32,8,128]{2,1,0:T(8,128)S(1)} collective-permute-done((f32[32,8,128]{2,1,0:T(8,128)S(1)}, f32[32,8,128]{2,1,0:T(8,128)S(1)}, u32[]{:S(2)}, u32[]{:S(2)}) %collective-permute-start.43) | collective-permute-done | bytes 131104 | tf_op jit(solution)/shard_map/ppermute | solution.py:39
  237.0 1.5 collect.1
  (96 shorter events, 18.4 us)
Async XLA Ops:
  7.2 94.1 %all-gather.2.cloned.1.call-start = ((), (), s32[]{:S(2)}) async-start(), calls=%async_computation.1 | async-start | bytes 9437184 | tf_op jit(solution)/shard_map/all_gather | solution.py:720
  8.2 11.7 %collective-permute-start = (bf16[8,12288]{1,0:T(8,128)(2,1)S(1)}, bf16[8,12288]{1,0:T(8,128)(2,1)S(1)}, u32[]{:S(2)}, u32[]{:S(2)}) collective-permute-start(bf16[8,12288]{1,0:T(8,128)(2,1)S(1)} %slice_bitcast_fusion), channel_id=1, source_target_pairs={{0,1},{1,2},{2,3},{3,4},{4,5},{5,6},{6,7},{7,8},{8,9},{9,10},{10,1... | collective-permute-start | bytes 589832 | tf_op jit(solution)/shard_map/ppermute | solution.py:27
  19.8 2.6 %copy-start = (bf16[8,12288]{1,0:T(8,128)(2,1)}, bf16[8,12288]{1,0:T(8,128)(2,1)S(1)}, u32[]{:S(2)}) copy-start(bf16[8,12288]{1,0:T(8,128)(2,1)S(1)} %collective-permute-done.refs_3_.refs_4_.refs_5_.rim_ref.key_rim_ref.value_rim_ref) | copy-start | bytes 589828
  19.9 4.5 %copy-start.9 = (bf16[512,256]{1,0:T(8,128)(2,1)S(1)}, bf16[512,256]{1,0:T(8,128)(2,1)}, u32[]{:S(2)}) copy-start(bf16[512,256]{1,0:T(8,128)(2,1)} %param.8) | copy-start | bytes 786436
  19.9 9.6 %copy-start.10 = (bf16[256,128]{1,0:T(8,128)(2,1)S(1)}, bf16[256,128]{1,0:T(8,128)(2,1)}, u32[]{:S(2)}) copy-start(bf16[256,128]{1,0:T(8,128)(2,1)} %param.7) | copy-start | bytes 196612
  22.4 14.0 %collective-permute-start.1 = (bf16[128,4096]{1,0:T(8,128)(2,1)}, bf16[128,4096]{1,0:T(8,128)(2,1)S(1)}, u32[]{:S(2)}, u32[]{:S(2)}) collective-permute-start(bf16[128,4096]{1,0:T(8,128)(2,1)} %get-tuple-element.104.cur_ref), channel_id=1, source_target_pairs={{0,1},{1,2},{2,3},{3,4},{4,5},{5,6},{6,7},{7,8},{8,9},{9,10},{10,1... | collective-permute-start | bytes 3145736 | tf_op jit(solution)/shard_map/ppermute | solution.py:27
  24.4 5.9 %collective-permute-start.2 = (bf16[256,256]{1,0:T(8,128)(2,1)S(1)}, bf16[256,256]{1,0:T(8,128)(2,1)S(1)}, u32[]{:S(2)}, u32[]{:S(2)}) collective-permute-start(bf16[256,256]{1,0:T(8,128)(2,1)S(1)} %slice.56), channel_id=1, source_target_pairs={{0,32},{32,64},{64,96},{96,0},{1,33},{33,65},{65,97},{97,1},{2,34}... | collective-permute-start | bytes 393224 | tf_op jit(solution)/shard_map/ppermute | solution.py:39
  25.8 8.5 %collective-permute-start.3 = (bf16[256,256]{1,0:T(8,128)(2,1)S(1)}, bf16[256,256]{1,0:T(8,128)(2,1)S(1)}, u32[]{:S(2)}, u32[]{:S(2)}) collective-permute-start(bf16[256,256]{1,0:T(8,128)(2,1)S(1)} %slice.56), channel_id=1, source_target_pairs={{0,64},{32,96},{64,0},{96,32},{1,65},{33,97},{65,1},{97,33},{2,66}... | collective-permute-start | bytes 393224 | tf_op jit(solution)/shard_map/ppermute | solution.py:39
  28.4 5.8 %collective-permute-start.4 = (bf16[256,256]{1,0:T(8,128)(2,1)S(1)}, bf16[256,256]{1,0:T(8,128)(2,1)S(1)}, u32[]{:S(2)}, u32[]{:S(2)}) collective-permute-start(bf16[256,256]{1,0:T(8,128)(2,1)S(1)} %slice.56), channel_id=1, source_target_pairs={{0,96},{32,0},{64,32},{96,64},{1,97},{33,1},{65,33},{97,65},{2,98}... | collective-permute-start | bytes 393224 | tf_op jit(solution)/shard_map/ppermute | solution.py:39
  36.4 9.8 %copy-start.1 = (bf16[128,4096]{1,0:T(8,128)(2,1)}, bf16[128,4096]{1,0:T(8,128)(2,1)S(1)}, u32[]{:S(2)}) copy-start(bf16[128,4096]{1,0:T(8,128)(2,1)S(1)} %collective-permute-done.1.prev_ref) | copy-start | bytes 3145732
  36.4 19.7 %copy-start.5 = (bf16[1,2048,256]{2,1,0:T(8,128)(2,1)S(1)}, bf16[1,2048,256]{2,1,0:T(8,128)(2,1)}, u32[]{:S(2)}) copy-start(bf16[1,2048,256]{2,1,0:T(8,128)(2,1)} %param.9) | copy-start | bytes 3145732
  46.2 113.9 %reduce-scatter.2.cloned.1.call-start = ((), (), s32[]{:S(2)}) async-start(), calls=%async_computation.2 | async-start | bytes 9437184 | tf_op jit(solution)/shard_map/reduce_scatter | solution.py:727
  46.3 5.4 %collective-permute-start.5 = (bf16[256,256]{1,0:T(8,128)(2,1)S(1)}, bf16[256,256]{1,0:T(8,128)(2,1)S(1)}, u32[]{:S(2)}, u32[]{:S(2)}) collective-permute-start(bf16[256,256]{1,0:T(8,128)(2,1)S(1)} %slice.57), channel_id=1, source_target_pairs={{0,8},{8,0},{1,9},{9,1},{2,10},{10,2},{3,11},{11,3},{4,12},{12,4},... | collective-permute-start | bytes 393224 | tf_op jit(solution)/shard_map/ppermute | solution.py:39
  49.1 4.2 %collective-permute-start.6 = (bf16[256,256]{1,0:T(8,128)(2,1)S(1)}, bf16[256,256]{1,0:T(8,128)(2,1)}, u32[]{:S(2)}, u32[]{:S(2)}) collective-permute-start(bf16[256,256]{1,0:T(8,128)(2,1)S(1)} %slice.57), channel_id=1, source_target_pairs={{0,16},{16,0},{1,17},{17,1},{2,18},{18,2},{3,19},{19,3},{4,20},{20... | collective-permute-start | bytes 393224 | tf_op jit(solution)/shard_map/ppermute | solution.py:39
  49.4 5.1 %collective-permute-start.7 = (bf16[256,256]{1,0:T(8,128)(2,1)S(1)}, bf16[256,256]{1,0:T(8,128)(2,1)}, u32[]{:S(2)}, u32[]{:S(2)}) collective-permute-start(bf16[256,256]{1,0:T(8,128)(2,1)S(1)} %slice.57), channel_id=1, source_target_pairs={{0,24},{8,16},{16,8},{24,0},{1,25},{9,17},{17,9},{25,1},{2,26},{10... | collective-permute-start | bytes 393224 | tf_op jit(solution)/shard_map/ppermute | solution.py:39
  54.6 10.5 %collective-permute-start.12 = (bf16[4,256,256]{2,1,0:T(8,128)(2,1)S(1)}, bf16[4,256,256]{2,1,0:T(8,128)(2,1)S(1)}, u32[]{:S(2)}, u32[]{:S(2)}) collective-permute-start(bf16[4,256,256]{2,1,0:T(8,128)(2,1)S(1)} %pad_maximum_fusion.2.refs_5_.refs_4_), channel_id=1, source_target_pairs={{0,8},{8,0},{1,9},{9,1},{2,10},{10,2},{3,11},{11,3},{4,12},{12,4},... | collective-permute-start | bytes 1572872 | tf_op jit(solution)/shard_map/ppermute | solution.py:39
  56.4 14.4 %collective-permute-start.8 = (bf16[1024,256]{0,1:T(8,128)(2,1)S(1)}, bf16[1024,256]{0,1:T(8,128)(2,1)S(1)}, u32[]{:S(2)}, u32[]{:S(2)}) collective-permute-start(bf16[1024,256]{0,1:T(8,128)(2,1)S(1)} %bitcast.51), channel_id=1, source_target_pairs={{0,8},{8,0},{1,9},{9,1},{2,10},{10,2},{3,11},{11,3},{4,12},{12,4},... | collective-permute-start | bytes 1572872 | tf_op jit(solution)/shard_map/ppermute | solution.py:39
  58.0 19.2 %collective-permute-start.13 = (bf16[4,256,256]{2,1,0:T(8,128)(2,1)S(1)}, bf16[4,256,256]{2,1,0:T(8,128)(2,1)}, u32[]{:S(2)}, u32[]{:S(2)}) collective-permute-start(bf16[4,256,256]{2,1,0:T(8,128)(2,1)S(1)} %pad_maximum_fusion.2.refs_5_.refs_4_), channel_id=1, source_target_pairs={{0,16},{16,0},{1,17},{17,1},{2,18},{18,2},{3,19},{19,3},{4,20},{20... | collective-permute-start | bytes 1572872 | tf_op jit(solution)/shard_map/ppermute | solution.py:39
  58.0 20.0 %collective-permute-start.14 = (bf16[4,256,256]{2,1,0:T(8,128)(2,1)S(1)}, bf16[4,256,256]{2,1,0:T(8,128)(2,1)}, u32[]{:S(2)}, u32[]{:S(2)}) collective-permute-start(bf16[4,256,256]{2,1,0:T(8,128)(2,1)S(1)} %pad_maximum_fusion.2.refs_5_.refs_4_), channel_id=1, source_target_pairs={{0,24},{8,16},{16,8},{24,0},{1,25},{9,17},{17,9},{25,1},{2,26},{10... | collective-permute-start | bytes 1572872 | tf_op jit(solution)/shard_map/ppermute | solution.py:39
  60.8 17.3 %collective-permute-start.10 = (bf16[4,256,256]{2,1,0:T(8,128)(2,1)S(1)}, bf16[4,256,256]{2,1,0:T(8,128)(2,1)}, u32[]{:S(2)}, u32[]{:S(2)}) collective-permute-start(bf16[4,256,256]{2,1,0:T(8,128)(2,1)S(1)} %pad_maximum_fusion.1.refs_1_.refs_0_), channel_id=1, source_target_pairs={{0,64},{32,96},{64,0},{96,32},{1,65},{33,97},{65,1},{97,33},{2,66}... | collective-permute-start | bytes 1572872 | tf_op jit(solution)/shard_map/ppermute | solution.py:39
  65.1 7.1 %copy-start.2 = (bf16[4,256,256]{2,1,0:T(8,128)(2,1)}, bf16[4,256,256]{2,1,0:T(8,128)(2,1)S(1)}, u32[]{:S(2)}) copy-start(bf16[4,256,256]{2,1,0:T(8,128)(2,1)S(1)} %collective-permute-done.12.refs_6_.refs_5_) | copy-start | bytes 1572868
  65.1 12.9 %collective-permute-start.11 = (bf16[4,256,256]{2,1,0:T(8,128)(2,1)S(1)}, bf16[4,256,256]{2,1,0:T(8,128)(2,1)}, u32[]{:S(2)}, u32[]{:S(2)}) collective-permute-start(bf16[4,256,256]{2,1,0:T(8,128)(2,1)S(1)} %pad_maximum_fusion.1.refs_1_.refs_0_), channel_id=1, source_target_pairs={{0,96},{32,0},{64,32},{96,64},{1,97},{33,1},{65,33},{97,65},{2,98}... | collective-permute-start | bytes 1572872 | tf_op jit(solution)/shard_map/ppermute | solution.py:39
  70.7 9.7 %collective-permute-start.9 = (bf16[4,256,256]{2,1,0:T(8,128)(2,1)S(1)}, bf16[4,256,256]{2,1,0:T(8,128)(2,1)}, u32[]{:S(2)}, u32[]{:S(2)}) collective-permute-start(bf16[4,256,256]{2,1,0:T(8,128)(2,1)S(1)} %pad_maximum_fusion.1.refs_1_.refs_0_), channel_id=1, source_target_pairs={{0,32},{32,64},{64,96},{96,0},{1,33},{33,65},{65,97},{97,1},{2,34}... | collective-permute-start | bytes 1572872 | tf_op jit(solution)/shard_map/ppermute | solution.py:39
  80.4 1.1 copy-start.3
  101.3 21.0 %copy-start.4 = (bf16[4,256,256]{2,1,0:T(8,128)(2,1)S(1)}, bf16[4,256,256]{2,1,0:T(8,128)(2,1)}, u32[]{:S(2)}) copy-start(bf16[4,256,256]{2,1,0:T(8,128)(2,1)} %copy-done.2) | copy-start | bytes 1572868
  111.2 9.9 %collective-permute-start.18 = (bf16[4,256,256]{2,1,0:T(8,128)(2,1)}, bf16[4,256,256]{2,1,0:T(8,128)(2,1)S(1)}, u32[]{:S(2)}, u32[]{:S(2)}) collective-permute-start(bf16[4,256,256]{2,1,0:T(8,128)(2,1)} %get-tuple-element.133), channel_id=1, source_target_pairs={{0,8},{8,0},{1,9},{9,1},{2,10},{10,2},{3,11},{11,3},{4,12},{12,4},... | collective-permute-start | bytes 1572872 | tf_op jit(solution)/shard_map/ppermute | solution.py:39
  113.9 18.3 %collective-permute-start.19 = (bf16[4,256,256]{2,1,0:T(8,128)(2,1)}, bf16[4,256,256]{2,1,0:T(8,128)(2,1)S(1)}, u32[]{:S(2)}, u32[]{:S(2)}) collective-permute-start(bf16[4,256,256]{2,1,0:T(8,128)(2,1)} %get-tuple-element.134), channel_id=1, source_target_pairs={{0,16},{16,0},{1,17},{17,1},{2,18},{18,2},{3,19},{19,3},{4,20},{20... | collective-permute-start | bytes 1572872 | tf_op jit(solution)/shard_map/ppermute | solution.py:39
  114.2 18.7 %collective-permute-start.20 = (bf16[4,256,256]{2,1,0:T(8,128)(2,1)}, bf16[4,256,256]{2,1,0:T(8,128)(2,1)S(1)}, u32[]{:S(2)}, u32[]{:S(2)}) collective-permute-start(bf16[4,256,256]{2,1,0:T(8,128)(2,1)} %get-tuple-element.135), channel_id=1, source_target_pairs={{0,24},{8,16},{16,8},{24,0},{1,25},{9,17},{17,9},{25,1},{2,26},{10... | collective-permute-start | bytes 1572872 | tf_op jit(solution)/shard_map/ppermute | solution.py:39
  114.8 18.4 %collective-permute-start.15 = (bf16[4,256,256]{2,1,0:T(8,128)(2,1)}, bf16[4,256,256]{2,1,0:T(8,128)(2,1)S(1)}, u32[]{:S(2)}, u32[]{:S(2)}) collective-permute-start(bf16[4,256,256]{2,1,0:T(8,128)(2,1)} %get-tuple-element.129), channel_id=1, source_target_pairs={{0,96},{32,0},{64,32},{96,64},{1,97},{33,1},{65,33},{97,65},{2,98}... | collective-permute-start | bytes 1572872 | tf_op jit(solution)/shard_map/ppermute | solution.py:39
  117.3 15.9 %collective-permute-start.16 = (bf16[4,256,256]{2,1,0:T(8,128)(2,1)}, bf16[4,256,256]{2,1,0:T(8,128)(2,1)S(1)}, u32[]{:S(2)}, u32[]{:S(2)}) collective-permute-start(bf16[4,256,256]{2,1,0:T(8,128)(2,1)} %get-tuple-element.130), channel_id=1, source_target_pairs={{0,64},{32,96},{64,0},{96,32},{1,65},{33,97},{65,1},{97,33},{2,66}... | collective-permute-start | bytes 1572872 | tf_op jit(solution)/shard_map/ppermute | solution.py:39
  121.1 11.9 %copy-start.8 = (bf16[4,256,256]{2,1,0:T(8,128)(2,1)S(1)}, bf16[4,256,256]{2,1,0:T(8,128)(2,1)}, u32[]{:S(2)}) copy-start(bf16[4,256,256]{2,1,0:T(8,128)(2,1)} %get-tuple-element.132) | copy-start | bytes 1572868
  121.1 13.3 %collective-permute-start.17 = (bf16[4,256,256]{2,1,0:T(8,128)(2,1)}, bf16[4,256,256]{2,1,0:T(8,128)(2,1)S(1)}, u32[]{:S(2)}, u32[]{:S(2)}) collective-permute-start(bf16[4,256,256]{2,1,0:T(8,128)(2,1)} %get-tuple-element.131), channel_id=1, source_target_pairs={{0,32},{32,64},{64,96},{96,0},{1,33},{33,65},{65,97},{97,1},{2,34}... | collective-permute-start | bytes 1572872 | tf_op jit(solution)/shard_map/ppermute | solution.py:39
  132.2 2.2 copy-start.7
  134.8 7.5 %collective-permute-start.21 = (bf16[256,256]{1,0:T(8,128)(2,1)S(1)}, bf16[256,256]{1,0:T(8,128)(2,1)S(1)}, u32[]{:S(2)}, u32[]{:S(2)}) collective-permute-start(bf16[256,256]{1,0:T(8,128)(2,1)S(1)} %get-tuple-element.198), channel_id=1, source_target_pairs={{0,8},{8,0},{1,9},{9,1},{2,10},{10,2},{3,11},{11,3},{4,12},{12,4},... | collective-permute-start | bytes 393224 | tf_op jit(solution)/shard_map/ppermute | solution.py:39
  137.8 5.0 %collective-permute-start.22 = (bf16[256,256]{1,0:T(8,128)(2,1)S(1)}, bf16[256,256]{1,0:T(8,128)(2,1)S(1)}, u32[]{:S(2)}, u32[]{:S(2)}) collective-permute-start(bf16[256,256]{1,0:T(8,128)(2,1)S(1)} %get-tuple-element.197), channel_id=1, source_target_pairs={{0,16},{16,0},{1,17},{17,1},{2,18},{18,2},{3,19},{19,3},{4,20},{20... | collective-permute-start | bytes 393224 | tf_op jit(solution)/shard_map/ppermute | solution.py:39
  138.3 5.4 %collective-permute-start.23 = (bf16[256,256]{1,0:T(8,128)(2,1)S(1)}, bf16[256,256]{1,0:T(8,128)(2,1)S(1)}, u32[]{:S(2)}, u32[]{:S(2)}) collective-permute-start(bf16[256,256]{1,0:T(8,128)(2,1)S(1)} %get-tuple-element.196), channel_id=1, source_target_pairs={{0,24},{8,16},{16,8},{24,0},{1,25},{9,17},{17,9},{25,1},{2,26},{10... | collective-permute-start | bytes 393224 | tf_op jit(solution)/shard_map/ppermute | solution.py:39
  138.9 6.0 %collective-permute-start.24 = (bf16[256,256]{1,0:T(8,128)(2,1)S(1)}, bf16[256,256]{1,0:T(8,128)(2,1)S(1)}, u32[]{:S(2)}, u32[]{:S(2)}) collective-permute-start(bf16[256,256]{1,0:T(8,128)(2,1)S(1)} %get-tuple-element.194), channel_id=1, source_target_pairs={{0,96},{32,0},{64,32},{96,64},{1,97},{33,1},{65,33},{97,65},{2,98}... | collective-permute-start | bytes 393224 | tf_op jit(solution)/shard_map/ppermute | solution.py:39
  141.6 5.4 %collective-permute-start.25 = (bf16[256,256]{1,0:T(8,128)(2,1)S(1)}, bf16[256,256]{1,0:T(8,128)(2,1)S(1)}, u32[]{:S(2)}, u32[]{:S(2)}) collective-permute-start(bf16[256,256]{1,0:T(8,128)(2,1)S(1)} %get-tuple-element.193), channel_id=1, source_target_pairs={{0,64},{32,96},{64,0},{96,32},{1,65},{33,97},{65,1},{97,33},{2,66}... | collective-permute-start | bytes 393224 | tf_op jit(solution)/shard_map/ppermute | solution.py:39
  142.3 6.4 %collective-permute-start.26 = (bf16[256,256]{1,0:T(8,128)(2,1)S(1)}, bf16[256,256]{1,0:T(8,128)(2,1)S(1)}, u32[]{:S(2)}, u32[]{:S(2)}) collective-permute-start(bf16[256,256]{1,0:T(8,128)(2,1)S(1)} %get-tuple-element.192), channel_id=1, source_target_pairs={{0,32},{32,64},{64,96},{96,0},{1,33},{33,65},{65,97},{97,1},{2,34}... | collective-permute-start | bytes 393224 | tf_op jit(solution)/shard_map/ppermute | solution.py:39
  163.7 16.3 %collective-permute-start.27 = (bf16[128,4096]{1,0:T(8,128)(2,1)}, bf16[128,4096]{1,0:T(8,128)(2,1)S(1)}, u32[]{:S(2)}, u32[]{:S(2)}) collective-permute-start(bf16[128,4096]{1,0:T(8,128)(2,1)} %get-tuple-element.142.grad_ref), channel_id=1, source_target_pairs={{1,0},{2,1},{3,2},{4,3},{5,4},{6,5},{7,6},{8,7},{9,8},{10,9},{11,1... | collective-permute-start | bytes 3145736 | tf_op jit(solution)/shard_map/ppermute | solution.py:27
  167.2 12.9 %copy-start.11 = (bf16[1024,256]{1,0:T(8,128)(2,1)S(1)}, bf16[1024,256]{1,0:T(8,128)(2,1)}, u32[]{:S(2)}) copy-start(bf16[1024,256]{1,0:T(8,128)(2,1)} %get-tuple-element.160) | copy-start | bytes 1572868
  180.0 15.3 %collective-permute-start.28 = (bf16[1024,256]{1,0:T(8,128)(2,1)S(1)}, bf16[1024,256]{1,0:T(8,128)(2,1)S(1)}, u32[]{:S(2)}, u32[]{:S(2)}) collective-permute-start(bf16[1024,256]{1,0:T(8,128)(2,1)S(1)} %copy-done.11), channel_id=1, source_target_pairs={{0,8},{8,0},{1,9},{9,1},{2,10},{10,2},{3,11},{11,3},{4,12},{12,4},... | collective-permute-start | bytes 1572872 | tf_op jit(solution)/shard_map/ppermute | solution.py:39
  196.0 1.8 collective-permute-start.30
  197.8 7.2 %collective-permute-start.31 = (f32[16,8,128]{2,1,0:T(8,128)S(1)}, f32[16,8,128]{2,1,0:T(8,128)S(1)}, u32[]{:S(2)}, u32[]{:S(2)}) collective-permute-start(f32[16,8,128]{2,1,0:T(8,128)S(1)} %get-tuple-element.200), channel_id=1, source_target_pairs={{0,2},{2,4},{4,6},{6,0},{1,3},{3,5},{5,7},{7,1},{8,10},{10,12},{12... | collective-permute-start | bytes 196616 | tf_op jit(solution)/shard_map/ppermute | solution.py:39
  198.1 7.7 %collective-permute-start.32 = (f32[16,8,128]{2,1,0:T(8,128)S(1)}, f32[16,8,128]{2,1,0:T(8,128)S(1)}, u32[]{:S(2)}, u32[]{:S(2)}) collective-permute-start(f32[16,8,128]{2,1,0:T(8,128)S(1)} %get-tuple-element.202), channel_id=1, source_target_pairs={{0,4},{2,6},{4,0},{6,2},{1,5},{3,7},{5,1},{7,3},{8,12},{10,14},{12... | collective-permute-start | bytes 196616 | tf_op jit(solution)/shard_map/ppermute | solution.py:39
  202.4 3.5 %collective-permute-start.33 = (f32[16,8,128]{2,1,0:T(8,128)S(1)}, f32[16,8,128]{2,1,0:T(8,128)S(1)}, u32[]{:S(2)}, u32[]{:S(2)}) collective-permute-start(f32[16,8,128]{2,1,0:T(8,128)S(1)} %get-tuple-element.201), channel_id=1, source_target_pairs={{0,6},{2,0},{4,2},{6,4},{1,7},{3,1},{5,3},{7,5},{8,14},{10,8},{12,... | collective-permute-start | bytes 196616 | tf_op jit(solution)/shard_map/ppermute | solution.py:39
  202.4 7.6 %collective-permute-start.29 = (bf16[3,8,4096]{2,1,0:T(8,128)(2,1)S(1)}, bf16[3,8,4096]{2,1,0:T(8,128)(2,1)S(1)}, u32[]{:S(2)}, u32[]{:S(2)}) collective-permute-start(bf16[3,8,4096]{2,1,0:T(8,128)(2,1)S(1)} %get-tuple-element.163), channel_id=1, source_target_pairs={{1,0},{2,1},{3,2},{4,3},{5,4},{6,5},{7,6},{8,7},{9,8},{10,9},{11,1... | collective-permute-start | bytes 589832 | tf_op jit(solution)/shard_map/ppermute | solution.py:27
  205.9 7.3 %collective-permute-start.34 = (f32[16,8,128]{2,1,0:T(8,128)S(1)}, f32[16,8,128]{2,1,0:T(8,128)S(1)}, u32[]{:S(2)}, u32[]{:S(2)}) collective-permute-start(f32[16,8,128]{2,1,0:T(8,128)S(1)} %fusion.1), channel_id=1, source_target_pairs={{0,32},{32,64},{64,96},{96,0},{1,33},{33,65},{65,97},{97,1},{2,34}... | collective-permute-start | bytes 196616 | tf_op jit(solution)/shard_map/ppermute | solution.py:39
  206.1 7.1 %collective-permute-start.35 = (f32[16,8,128]{2,1,0:T(8,128)S(1)}, f32[16,8,128]{2,1,0:T(8,128)S(1)}, u32[]{:S(2)}, u32[]{:S(2)}) collective-permute-start(f32[16,8,128]{2,1,0:T(8,128)S(1)} %fusion.1), channel_id=1, source_target_pairs={{0,64},{32,96},{64,0},{96,32},{1,65},{33,97},{65,1},{97,33},{2,66}... | collective-permute-start | bytes 196616 | tf_op jit(solution)/shard_map/ppermute | solution.py:39
  208.6 4.6 %collective-permute-start.36 = (f32[16,8,128]{2,1,0:T(8,128)S(1)}, f32[16,8,128]{2,1,0:T(8,128)S(1)}, u32[]{:S(2)}, u32[]{:S(2)}) collective-permute-start(f32[16,8,128]{2,1,0:T(8,128)S(1)} %fusion.1), channel_id=1, source_target_pairs={{0,96},{32,0},{64,32},{96,64},{1,97},{33,1},{65,33},{97,65},{2,98}... | collective-permute-start | bytes 196616 | tf_op jit(solution)/shard_map/ppermute | solution.py:39
  213.2 6.9 %collective-permute-start.37 = (f32[16,8,128]{2,1,0:T(8,128)S(1)}, f32[16,8,128]{2,1,0:T(8,128)S(1)}, u32[]{:S(2)}, u32[]{:S(2)}) collective-permute-start(f32[16,8,128]{2,1,0:T(8,128)S(1)} %add_add_fusion.1), channel_id=1, source_target_pairs={{0,8},{8,0},{1,9},{9,1},{2,10},{10,2},{3,11},{11,3},{4,12},{12,4},... | collective-permute-start | bytes 196616 | tf_op jit(solution)/shard_map/ppermute | solution.py:39
  215.5 4.6 %collective-permute-start.38 = (f32[16,8,128]{2,1,0:T(8,128)S(1)}, f32[16,8,128]{2,1,0:T(8,128)S(1)}, u32[]{:S(2)}, u32[]{:S(2)}) collective-permute-start(f32[16,8,128]{2,1,0:T(8,128)S(1)} %add_add_fusion.1), channel_id=1, source_target_pairs={{0,16},{16,0},{1,17},{17,1},{2,18},{18,2},{3,19},{19,3},{4,20},{20... | collective-permute-start | bytes 196616 | tf_op jit(solution)/shard_map/ppermute | solution.py:39
  216.5 4.5 %collective-permute-start.39 = (f32[16,8,128]{2,1,0:T(8,128)S(1)}, f32[16,8,128]{2,1,0:T(8,128)S(1)}, u32[]{:S(2)}, u32[]{:S(2)}) collective-permute-start(f32[16,8,128]{2,1,0:T(8,128)S(1)} %add_add_fusion.1), channel_id=1, source_target_pairs={{0,24},{8,16},{16,8},{24,0},{1,25},{9,17},{17,9},{25,1},{2,26},{10... | collective-permute-start | bytes 196616 | tf_op jit(solution)/shard_map/ppermute | solution.py:39
  216.8 11.1 %copy-start.6 = (bf16[1024,256]{1,0:T(8,128)(2,1)S(1)}, bf16[1024,256]{1,0:T(8,128)(2,1)}, u32[]{:S(2)}) copy-start(bf16[1024,256]{1,0:T(8,128)(2,1)} %get-tuple-element.126) | copy-start | bytes 1572868
  221.0 4.4 %collective-permute-start.40 = (f32[16,8,128]{2,1,0:T(8,128)S(1)}, f32[16,8,128]{2,1,0:T(8,128)S(1)}, u32[]{:S(2)}, u32[]{:S(2)}) collective-permute-start(f32[16,8,128]{2,1,0:T(8,128)S(1)} %add_add_fusion), channel_id=1, source_target_pairs={{0,1},{1,0},{2,3},{3,2},{4,5},{5,4},{6,7},{7,6},{8,9},{9,8},{10,11... | collective-permute-start | bytes 196616 | tf_op jit(solution)/shard_map/ppermute | solution.py:39
  225.4 6.9 %collective-permute-start.41 = (f32[32,8,128]{2,1,0:T(8,128)S(1)}, f32[32,8,128]{2,1,0:T(8,128)S(1)}, u32[]{:S(2)}, u32[]{:S(2)}) collective-permute-start(f32[32,8,128]{2,1,0:T(8,128)S(1)} %pad_maximum_fusion.3.refs_0_), channel_id=1, source_target_pairs={{0,6},{2,0},{4,2},{6,4},{1,7},{3,1},{5,3},{7,5},{8,14},{10,8},{12,... | collective-permute-start | bytes 393224 | tf_op jit(solution)/shard_map/ppermute | solution.py:39
  227.3 6.1 %collective-permute-start.42 = (f32[32,8,128]{2,1,0:T(8,128)S(1)}, f32[32,8,128]{2,1,0:T(8,128)S(1)}, u32[]{:S(2)}, u32[]{:S(2)}) collective-permute-start(f32[32,8,128]{2,1,0:T(8,128)S(1)} %pad_maximum_fusion.3.refs_0_), channel_id=1, source_target_pairs={{0,4},{2,6},{4,0},{6,2},{1,5},{3,7},{5,1},{7,3},{8,12},{10,14},{12... | collective-permute-start | bytes 393224 | tf_op jit(solution)/shard_map/ppermute | solution.py:39
  227.6 9.4 %collective-permute-start.43 = (f32[32,8,128]{2,1,0:T(8,128)S(1)}, f32[32,8,128]{2,1,0:T(8,128)S(1)}, u32[]{:S(2)}, u32[]{:S(2)}) collective-permute-start(f32[32,8,128]{2,1,0:T(8,128)S(1)} %pad_maximum_fusion.3.refs_0_), channel_id=1, source_target_pairs={{0,2},{2,4},{4,6},{6,0},{1,3},{3,5},{5,7},{7,1},{8,10},{10,12},{12... | collective-permute-start | bytes 393224 | tf_op jit(solution)/shard_map/ppermute | solution.py:39
Sparse Core Ops, SparseCore 0:
  46.3 54.9 all-gather.1
  103.7 56.3 reduce-scatter.1

commit v14 on v13

--- a/solution.py
+++ b/solution.py
@@ -211,32 +211,28 @@
     )(lines, prev, cur, query)
 
 
-def gate_kernel(place, gate_grad_ref, query_ref, mixed_ref, grad_ref, feature_ref):
+def gate_kernel(place, gate_grad_ref, query_ref, grad_ref):
     width = query_ref.shape[1] // place.shape[0]
     for i in range(place.shape[0]):
         at = pl.ds(i * width, width)
         gate_grad = gate_grad_ref[:, pl.ds(pl.multiple_of(place[i] * width, width), width)].astype(F32)
         grad_ref[:, at] = (gate_grad * query_ref[:, at].astype(F32)).astype(BF16)
-        feature_ref[:, at] = (gate_grad * mixed_ref[:, at].astype(F32)).astype(BF16)
-
-
-def gate_call(place, gate_grad, query, mixed):
+
+
+def gate_call(place, gate_grad, query):
     rows, channels = query.shape
-    out = jax.ShapeDtypeStruct((rows, channels), BF16)
+    half = pl.BlockSpec((rows // 2, channels), lambda i, place: (i, 0))
     return hbm_call(
         gate_kernel,
         loose=(0,),
         grid_spec=pltpu.PrefetchScalarGridSpec(
-            num_scalar_prefetch=1,
-            grid=(2,),
-            in_specs=[pl.BlockSpec((rows // 2, channels), lambda i, place: (i, 0))] * 3,
-            out_specs=[pl.BlockSpec((rows // 2, channels), lambda i, place: (i, 0))] * 2,
+            num_scalar_prefetch=1, grid=(2,), in_specs=[half, half], out_specs=half
         ),
-        out_shape=[out, out],
+        out_shape=jax.ShapeDtypeStruct((rows, channels), BF16),
         compiler_params=params(),
-        cost_estimate=cost(2 * rows * channels, 10 * rows * channels),
+        cost_estimate=cost(rows * channels, 6 * rows * channels),
         name="gate_back",
-    )(place, gate_grad, query, mixed)
+    )(place, gate_grad, query)
 
 
 def tap_sums(short_taps, grad, tokens_ref, rim_ref, out_ref, at, ext):
@@ -249,8 +245,10 @@
 
 
 def long_grad_kernel(
-    per_group, short_taps, prev_ref, cur_ref, grad_ref, feature_ref, tokens_ref, rim_ref, long_ref, short_ref, fold, masked, ext
+    per_group, short_taps, place, prev_ref, cur_ref, grad_ref, gate_grad_ref, mixed_ref, tokens_ref, rim_ref,
+    long_ref, short_ref, feature_ref, fold, masked, ext,
 ):
+    step = pl.program_id(0)
     rows, width = cur_ref.shape
     row, lane = lane_row((rows, rows))
     above = lane > row
@@ -276,40 +274,59 @@
         for step in range(1, 8):
             total = total + pltpu.roll(fold[block % 2, pl.ds(step, packed, stride=8), :], rows - step, 1)
         sums.append(total)
-        tap_sums(short_taps, feature_ref[:, at], tokens_ref, rim_ref, short_ref, at, ext.at[block % 2])
+        side, inner = divmod(block * LANES, width // 2)
+        gate_at = pl.multiple_of(place[2 * step + side] % 2 * (width // 2) + inner, LANES)
+        gate_grad = gate_grad_ref[:, pl.ds(gate_at, LANES)].astype(F32)
+        feature = (gate_grad * mixed_ref[:, at].astype(F32)).astype(BF16)
+        feature_ref[:, at] = feature
+        tap_sums(short_taps, feature, tokens_ref, rim_ref, short_ref, at, ext.at[block % 2])
     long_ref[...] = jnp.dot(
         jnp.concatenate(sums, axis=0), mirror(rows), precision=lax.Precision.HIGHEST, preferred_element_type=F32
     )
 
 
-def long_grad_call(groups, short_taps, prev, cur, grad, feature, tokens, rim):
+def long_grad_call(place, groups, short_taps, prev, cur, grad, gate_grad, mixed, tokens, rim):
     rows, channels = cur.shape
     per_group = channels // groups
-    width = block_width(channels, WIDTH)
-    steps = channels // width
-    wide = pl.BlockSpec((rows, width), lambda i: (0, i))
+    steps = place.shape[0] // 2
+    width = channels // steps
+    wide = pl.BlockSpec((rows, width), lambda i, place: (0, i))
     packed = LANES // per_group
     return hbm_call(
         functools.partial(long_grad_kernel, per_group, short_taps),
-        grid=(steps,),
-        in_specs=[wide] * 5 + [pl.BlockSpec((RIM, width), lambda i: (0, i))],
-        out_specs=[
-            pl.BlockSpec((width // per_group, rows), lambda i: (i, 0)),
-            pl.BlockSpec((8, width), lambda i: (0, i)),
-        ],
+        loose=(0,),
+        grid_spec=pltpu.PrefetchScalarGridSpec(
+            num_scalar_prefetch=1,
+            grid=(steps,),
+            in_specs=[
+                wide,
+                wide,
+                wide,
+                pl.BlockSpec((rows, width), lambda i, place: (0, place[2 * i] // 2)),
+                wide,
+                wide,
+                pl.BlockSpec((RIM, width), lambda i, place: (0, i)),
+            ],
+            out_specs=[
+                pl.BlockSpec((width // per_group, rows), lambda i, place: (i, 0)),
+                pl.BlockSpec((8, width), lambda i, place: (0, i)),
+                wide,
+            ],
+            scratch_shapes=[
+                pltpu.VMEM((2, packed * 8, LANES), F32),
+                pltpu.VMEM((2, packed * rows, LANES), BF16),
+                pltpu.VMEM((2, RIM + rows, LANES), F32),
+            ],
+        ),
         out_shape=[
             jax.ShapeDtypeStruct((groups, rows), F32),
             jax.ShapeDtypeStruct((8, channels), F32),
-        ],
-        scratch_shapes=[
-            pltpu.VMEM((2, packed * 8, LANES), F32),
-            pltpu.VMEM((2, packed * rows, LANES), BF16),
-            pltpu.VMEM((2, RIM + rows, LANES), F32),
+            jax.ShapeDtypeStruct((rows, channels), BF16),
         ],
         compiler_params=params(),
-        cost_estimate=cost(2 * groups * rows * 2 * rows * LANES, 10 * rows * channels),
+        cost_estimate=cost(2 * groups * rows * 2 * rows * LANES, 14 * rows * channels),
         name="long_grad",
-    )(prev, cur, grad, feature, tokens, rim)
+    )(place, prev, cur, grad, gate_grad, mixed, tokens, rim)
 
 
 def unmix_kernel(
@@ -731,15 +748,14 @@
     top, bottom, other = plane_scatter(top_grads, bottom_grads, other)
     gate_grad, top, bottom, other = lax.optimization_barrier((gate_grad, top, bottom, other))
 
-    grad_mixed, query_grad = gate_call(place, gate_grad, query, mixed)
+    grad_mixed = gate_call(place, gate_grad, query)
     grad_next = along(grad_mixed, -1)
-    long_sum, query_sum = long_grad_call(
-        groups, short_taps, mixer_prev, mixer, grad_mixed, query_grad, tokens, rim
+    long_sum, query_sum, query_grad = long_grad_call(
+        place, groups, short_taps, mixer_prev, mixer, grad_mixed, gate_grad, mixed, tokens, rim
     )
     grad_weight = jnp.concatenate([added(top), added(bottom)], axis=1).T
-    grad_next, grad_weight, other, long_sum, query_sum = lax.optimization_barrier(
-        (grad_next, grad_weight, other, long_sum, query_sum)
-    )
+    other, long_sum, query_sum = lax.optimization_barrier((other, long_sum, query_sum))
+    grad_next, grad_weight, long_sum = lax.optimization_barrier((grad_next, grad_weight, long_sum))
     theirs = move(other, xh=1)
     other_grads, key_sum, value_sum, edge = unmix_call(
         lines, short_taps, grad_mixed, grad_next, key, value, tokens, rim, query_grad

time: 246 us -> 243 us (0.988)
  waiting for transfers between devices: 68.1 us -> 63.2 us
    ppermute x4, waiting for transfers between devices: 6.29 us -> 2.19 us  [along(): return lax.ppermute(x, LINE, pairs)]
  transfers between devices with their start and end apart: 46 -> 46, of which waited for: 28 -> 27; matrix products, arithmetic and copies ran while one was open for 3% -> 3% of each run, Pallas kernels for 27% -> 28%
where the time goes in v14:
time: 243 us
  Pallas kernels  84.6 us (35%)
  starting transfers between devices  70.8 us (29%)
  waiting for transfers between devices  63.2 us (26%)
  between operations  14.4 us (6%)
  local copies, waits for them, and re-layouts  5.12 us (2%)
  other arithmetic  4.4 us (2%)
    pallas_call x12, Pallas kernels, run(): return call(*held)  82.4 us
    ppermute x40, starting transfers between devices, move(): return lax.ppermute(x, axes, pairs)  57.8 us
    ppermute x40, waiting for transfers between devices, move(): return lax.ppermute(x, axes, pairs)  38.3 us
    ppermute x4, starting transfers between devices, along(): return lax.ppermute(x, LINE, pairs)  12.9 us
    reduce_scatter x1, waiting for transfers between devices, shards(): lax.psum_scatter(partial, ('z', 'c'), scatter_dimension=0, tiled=True)  11.4 us
    all_gather x1, waiting for transfers between devices, shards(): all_rows = lax.all_gather(gated, ('z', 'c'), axis=0, tiled=True)  11.3 us
  transfers between devices with their start and end apart: 46, of which 27 were waited for; matrix products, arithmetic and copies ran while one was open for 3% of the time, Pallas kernels for 28%

profile of v14, /device:TPU:1, one launch (start us, length us, event | category | flops | bytes accessed | tf_op | source)
XLA Modules:
  0.0 242.5 jit_solution(6354077126991064988)
XLA Ops:
  8.2 4.9 %collective-permute-start = (bf16[8,12288]{1,0:T(8,128)(2,1)S(1)}, bf16[8,12288]{1,0:T(8,128)(2,1)S(1)}, u32[]{:S(2)}, u32[]{:S(2)}) collective-permute-start(bf16[8,12288]{1,0:T(8,128)(2,1)S(1)} %slice_bitcast_fusion), channel_id=1, source_target_pairs={{0,1},{1,2},{2,3},{3,4},{4,5},{5,6},{6,7},{7,8},{8,9},{9,10},{10,1... | collective-permute-start | bytes 589832 | tf_op jit(solution)/shard_map/ppermute | solution.py:27
  13.1 6.7 %features.1 = (bf16[128,4096]{1,0:T(8,128)(2,1)}, bf16[128,4096]{1,0:T(8,128)(2,1)}, bf16[128,4096]{1,0:T(8,128)(2,1)}, bf16[128,4096]{1,0:T(8,128)(2,1)}) custom-call(bf16[128,12288]{1,0:T(8,128)(2,1)} %bitcast.37, bf16[128,12288]{1,0:T(8,128)(2,1)} %bitcast.38, bf16[128,12288]{1,0:T(8,128)(2,1)} %bitcast.39, f32[7,12288]{1,0:T(8,128)} %filter_ref.5, ...), custom_call_target="tpu_custom_call" | custom-call | bytes 1572864 | tf_op jit(solution)/shard_map/features/pallas_call | solution.py:64
  19.9 2.6 %first_rows.1 = (bf16[128,4096]{1,0:T(8,128)(2,1)}, bf16[128,4096]{1,0:T(8,128)(2,1)}, bf16[128,4096]{1,0:T(8,128)(2,1)}, bf16[128,4096]{1,0:T(8,128)(2,1)}) custom-call(bf16[128,12288]{1,0:T(8,128)(2,1)} %bitcast.40, bf16[128,12288]{1,0:T(8,128)(2,1)} %bitcast.41, ...), custom_call_target="tpu_custom_call", output_to_operand_aliasing={{0}: (9, {}), {1}: (10, {}), {2}: (11, {}), {3}: (12, {})} | custom-call | bytes 196608 | tf_op jit(solution)/shard_map/first_rows/pallas_call | solution.py:64
  22.4 1.9 collective-permute-start.1
  24.4 1.4 collective-permute-start.2
  25.7 2.6 %collective-permute-start.3 = (bf16[256,256]{1,0:T(8,128)(2,1)S(1)}, bf16[256,256]{1,0:T(8,128)(2,1)S(1)}, u32[]{:S(2)}, u32[]{:S(2)}) collective-permute-start(bf16[256,256]{1,0:T(8,128)(2,1)S(1)} %slice.56), channel_id=1, source_target_pairs={{0,64},{32,96},{64,0},{96,32},{1,65},{33,97},{65,1},{97,33},{2,66}... | collective-permute-start | bytes 393224 | tf_op jit(solution)/shard_map/ppermute | solution.py:39
  30.3 3.9 %collective-permute-done.3 = bf16[256,256]{1,0:T(8,128)(2,1)S(1)} collective-permute-done((bf16[256,256]{1,0:T(8,128)(2,1)S(1)}, bf16[256,256]{1,0:T(8,128)(2,1)S(1)}, u32[]{:S(2)}, u32[]{:S(2)}) %collective-permute-start.3) | collective-permute-done | bytes 131104 | tf_op jit(solution)/shard_map/ppermute | solution.py:39
  34.2 2.2 collective-permute-done.1.prev_ref
  36.4 9.7 %mix.1 = (bf16[128,4096]{1,0:T(8,128)(2,1)}, bf16[128,4096]{1,0:T(8,128)(2,1)}) custom-call(f32[256,128]{1,0:T(8,128)S(1)} %convert_element_type.57.lines_ref, bf16[128,4096]{1,0:T(8,128)(2,1)S(1)} %collective-permute-done.1.prev_ref, bf16[128,4096]{1,0:T(8,128)(2,1)} %get-tuple-element.104.cur_ref, bf16[128,4096]{1,0:T(8,128)(2,1)} %get-tuple-element.107.query_ref), custom_call_target="tpu_custom_call" | custom-call | bytes 1048576 | tf_op jit(solution)/shard_map/mix/pallas_call | solution.py:64
  46.3 2.8 %collective-permute-start.5 = (bf16[256,256]{1,0:T(8,128)(2,1)S(1)}, bf16[256,256]{1,0:T(8,128)(2,1)S(1)}, u32[]{:S(2)}, u32[]{:S(2)}) collective-permute-start(bf16[256,256]{1,0:T(8,128)(2,1)S(1)} %slice.57), channel_id=1, source_target_pairs={{0,8},{8,0},{1,9},{9,1},{2,10},{10,2},{3,11},{11,3},{4,12},{12,4},... | collective-permute-start | bytes 393224 | tf_op jit(solution)/shard_map/ppermute | solution.py:39
  49.9 1.7 collective-permute-done.5
  51.7 1.6 collective-permute-done.6
  53.2 1.3 collective-permute-done.7
  54.6 1.5 collective-permute-start.12
  56.3 1.7 collective-permute-start.8
  58.0 1.7 collective-permute-start.14
  59.7 1.1 pad_maximum_fusion.1.refs_1_.refs_0_
  60.8 3.0 %collective-permute-start.10 = (bf16[4,256,256]{2,1,0:T(8,128)(2,1)S(1)}, bf16[4,256,256]{2,1,0:T(8,128)(2,1)}, u32[]{:S(2)}, u32[]{:S(2)}) collective-permute-start(bf16[4,256,256]{2,1,0:T(8,128)(2,1)S(1)} %pad_maximum_fusion.1.refs_1_.refs_0_), channel_id=1, source_target_pairs={{0,64},{32,96},{64,0},{96,32},{1,65},{33,97},{65,1},{97,33},{2,66}... | collective-permute-start | bytes 1572872 | tf_op jit(solution)/shard_map/ppermute | solution.py:39
  63.7 1.4 collective-permute-done.12.refs_6_.refs_5_
  65.1 2.7 %collective-permute-start.11 = (bf16[4,256,256]{2,1,0:T(8,128)(2,1)S(1)}, bf16[4,256,256]{2,1,0:T(8,128)(2,1)}, u32[]{:S(2)}, u32[]{:S(2)}) collective-permute-start(bf16[4,256,256]{2,1,0:T(8,128)(2,1)S(1)} %pad_maximum_fusion.1.refs_1_.refs_0_), channel_id=1, source_target_pairs={{0,96},{32,0},{64,32},{96,64},{1,97},{33,1},{65,33},{97,65},{2,98}... | collective-permute-start | bytes 1572872 | tf_op jit(solution)/shard_map/ppermute | solution.py:39
  67.8 2.9 %collective-permute-done.8 = bf16[1024,256]{0,1:T(8,128)(2,1)S(1)} collective-permute-done((bf16[1024,256]{0,1:T(8,128)(2,1)S(1)}, bf16[1024,256]{0,1:T(8,128)(2,1)S(1)}, u32[]{:S(2)}, u32[]{:S(2)}) %collective-permute-start.8) | collective-permute-done | bytes 524320 | tf_op jit(solution)/shard_map/ppermute | solution.py:39
  70.7 1.3 collective-permute-start.9
  72.2 1.2 fusion.11
  73.4 1.5 copy.18.refs_0_
  74.9 2.4 collective-permute-done.13.refs_7_.refs_6_
  78.0 2.4 collective-permute-done.9.refs_2_.refs_1_
  81.5 8.5 %gate_matmul.1 = bf16[1024,4096]{1,0:T(8,128)(2,1)} custom-call(bf16[1024,512]{1,0:T(8,128)(2,1)S(1)} %copy.18.refs_0_, bf16[4,256,256]{2,1,0:T(8,128)(2,1)S(1)} %pad_maximum_fusion.1.refs_1_.refs_0_, bf16[4,256,256]{2,1,0:T(8,128)(2,1)} %collective-permute-done.9.refs_2_.refs_1_, bf16[4,256,256]{2,1,0:T(8,128)(2,1)} %collective-permute-done.10.refs_3_.refs_2_, ...), custom_call_target="tpu_custom_call" | custom-call | flops 4294967296 | bytes 12582912 | tf_op jit(solution)/shard_map/gate_matmul/pallas_call | solution.py:64
  90.0 11.3 %all-gather.2.cloned.1.call-done.rows_ref = bf16[1024,4096]{1,0:T(8,128)(2,1)} async-done(((bf16[128,4096]{1,0:T(8,128)(2,1)}), bf16[1024,4096]{1,0:T(8,128)(2,1)}) %all-gather.2.cloned.1.call-update) | async-done | bytes 8388624 | tf_op jit(solution)/shard_map/all_gather | solution.py:737
  101.3 9.9 %weight_grad.1 = (bf16[4,256,256]{2,1,0:T(8,128)(2,1)}, bf16[4,256,256]{2,1,0:T(8,128)(2,1)}, bf16[4,256,256]{2,1,0:T(8,128)(2,1)}, bf16[4,256,256]{2,1,0:T(8,12...) custom-call(s32[8]{0:T(128)S(1)} %fusion.2.origin.place, ...), custom_call_target="tpu_custom_call" | custom-call | flops 4294967296 | bytes 12582912 | tf_op jit(solution)/shard_map/weight_grad/pallas_call | solution.py:64
  111.3 2.7 %collective-permute-start.18 = (bf16[4,256,256]{2,1,0:T(8,128)(2,1)}, bf16[4,256,256]{2,1,0:T(8,128)(2,1)S(1)}, u32[]{:S(2)}, u32[]{:S(2)}) collective-permute-start(bf16[4,256,256]{2,1,0:T(8,128)(2,1)} %get-tuple-element.133), channel_id=1, source_target_pairs={{0,8},{8,0},{1,9},{9,1},{2,10},{10,2},{3,11},{11,3},{4,12},{12,4},... | collective-permute-start | bytes 1572872 | tf_op jit(solution)/shard_map/ppermute | solution.py:39
  114.8 2.5 %collective-permute-start.15 = (bf16[4,256,256]{2,1,0:T(8,128)(2,1)}, bf16[4,256,256]{2,1,0:T(8,128)(2,1)S(1)}, u32[]{:S(2)}, u32[]{:S(2)}) collective-permute-start(bf16[4,256,256]{2,1,0:T(8,128)(2,1)} %get-tuple-element.129), channel_id=1, source_target_pairs={{0,96},{32,0},{64,32},{96,64},{1,97},{33,1},{65,33},{97,65},{2,98}... | collective-permute-start | bytes 1572872 | tf_op jit(solution)/shard_map/ppermute | solution.py:39
  117.8 3.3 %collective-permute-done.18 = bf16[4,256,256]{2,1,0:T(8,128)(2,1)S(1)} collective-permute-done((bf16[4,256,256]{2,1,0:T(8,128)(2,1)}, bf16[4,256,256]{2,1,0:T(8,128)(2,1)S(1)}, u32[]{:S(2)}, u32[]{:S(2)}) %collective-permute-start.18) | collective-permute-done | bytes 524320 | tf_op jit(solution)/shard_map/ppermute | solution.py:39
  121.1 1.2 collective-permute-start.17
  122.3 9.9 %output.1 = (bf16[1024,256]{1,0:T(8,128)(2,1)}, bf16[1024,256]{1,0:T(8,128)(2,1)}) custom-call(s32[8]{0:T(128)S(1)} %fusion.2.origin.place, bf16[1024,4096]{1,0:T(8,128)(2,1)} %all-gather.2.cloned.1.call-done.rows_ref, bf16[4,256,256]{2,1,0:T(8,128)(2,1)S(1)} %pad_maximum_fusion.1.refs_1_.refs_0_, ...), custom_call_target="tpu_custom_call" | custom-call | flops 4294967296 | bytes 12582912 | tf_op jit(solution)/shard_map/output/pallas_call | solution.py:64
  133.2 1.2 collective-permute-done.17
  134.7 3.1 %collective-permute-start.21 = (bf16[256,256]{1,0:T(8,128)(2,1)S(1)}, bf16[256,256]{1,0:T(8,128)(2,1)S(1)}, u32[]{:S(2)}, u32[]{:S(2)}) collective-permute-start(bf16[256,256]{1,0:T(8,128)(2,1)S(1)} %get-tuple-element.198), channel_id=1, source_target_pairs={{0,8},{8,0},{1,9},{9,1},{2,10},{10,2},{3,11},{11,3},{4,12},{12,4},... | collective-permute-start | bytes 393224 | tf_op jit(solution)/shard_map/ppermute | solution.py:39
  138.9 2.7 %collective-permute-start.24 = (bf16[256,256]{1,0:T(8,128)(2,1)S(1)}, bf16[256,256]{1,0:T(8,128)(2,1)S(1)}, u32[]{:S(2)}, u32[]{:S(2)}) collective-permute-start(bf16[256,256]{1,0:T(8,128)(2,1)S(1)} %get-tuple-element.194), channel_id=1, source_target_pairs={{0,96},{32,0},{64,32},{96,64},{1,97},{33,1},{65,33},{97,65},{2,98}... | collective-permute-start | bytes 393224 | tf_op jit(solution)/shard_map/ppermute | solution.py:39
  143.8 1.1 collective-permute-done.24
  144.9 2.1 collective-permute-done.25
  147.0 1.7 collective-permute-done.26
  148.7 11.4 %reduce-scatter.2.cloned.1.call-done.gate_grad_ref = bf16[128,4096]{1,0:T(8,128)(2,1)} async-done(((bf16[1024,4096]{1,0:T(8,128)(2,1)}), bf16[128,4096]{1,0:T(8,128)(2,1)}) %reduce-scatter.2.cloned.1.call-update) | async-done | bytes 1048592 | tf_op jit(solution)/shard_map/reduce_scatter | solution.py:744
  160.1 3.0 %gate_back.1.grad_ref = bf16[128,4096]{1,0:T(8,128)(2,1)} custom-call(s32[8]{0:T(128)S(1)} %fusion.2.origin.place, bf16[128,4096]{1,0:T(8,128)(2,1)} %reduce-scatter.2.cloned.1.call-done.gate_grad_ref, bf16[128,4096]{1,0:T(8,128)(2,1)} %get-tuple-element.107.query_ref), custom_call_target="tpu_custom_call" | custom-call | flops 524288 | bytes 3145728 | tf_op jit(solution)/shard_map/gate_back/pallas_call | solution.py:64
  163.1 3.3 %collective-permute-start.27 = (bf16[128,4096]{1,0:T(8,128)(2,1)}, bf16[128,4096]{1,0:T(8,128)(2,1)S(1)}, u32[]{:S(2)}, u32[]{:S(2)}) collective-permute-start(bf16[128,4096]{1,0:T(8,128)(2,1)} %gate_back.1.grad_ref), channel_id=1, source_target_pairs={{1,0},{2,1},{3,2},{4,3},{5,4},{6,5},{7,6},{8,7},{9,8},{10,9},{11,1... | collective-permute-start | bytes 3145736 | tf_op jit(solution)/shard_map/ppermute | solution.py:27
  166.4 11.1 %long_grad.1 = (f32[256,128]{1,0:T(8,128)S(1)}, f32[8,4096]{1,0:T(8,128)S(1)}, bf16[128,4096]{1,0:T(8,128)(2,1)}) custom-call(s32[8]{0:T(128)S(1)} %fusion.2.origin.place, bf16[128,4096]{1,0:T(8,128)(2,1)} %copy-done.1, bf16[128,4096]{1,0:T(8,128)(2,1)} %get-tuple-element.104.cur_ref, bf16[128,4096]{1,0:T(8,128)(2,1)} %gate_back.1.grad_ref, ...), custom_call_target="tpu_custom_call" | custom-call | flops 2147483648 | bytes 7340032 | tf_op jit(solution)/shard_map/long_grad/pallas_call | solution.py:64
  177.5 2.8 %collective-permute-start.28 = (bf16[1024,256]{1,0:T(8,128)(2,1)S(1)}, bf16[1024,256]{1,0:T(8,128)(2,1)S(1)}, u32[]{:S(2)}, u32[]{:S(2)}) collective-permute-start(bf16[1024,256]{1,0:T(8,128)(2,1)S(1)} %copy-done.11), channel_id=1, source_target_pairs={{0,8},{8,0},{1,9},{9,1},{2,10},{10,2},{3,11},{11,3},{4,12},{12,4},... | collective-permute-start | bytes 1572872 | tf_op jit(solution)/shard_map/ppermute | solution.py:39
  180.6 11.4 %unmix.1 = (bf16[2,128,4096]{2,1,0:T(8,128)(2,1)}, f32[8,4096]{1,0:T(8,128)S(1)}, f32[8,4096]{1,0:T(8,128)S(1)}, bf16[3,8,4096]{2,1,0:T(8,128)(2,1)S(1)}) custom-call(f32[256,128]{1,0:T(8,128)S(1)} %convert_element_type.57.lines_ref, bf16[128,4096]{1,0:T(8,128)(2,1)} %gate_back.1.grad_ref, bf16[128,4096]{1,0:T(8,128)(2,1)S(1)} %collective-permute-done.27.next_ref, ...), custom_call_target="tpu_custom_call" | custom-call | flops 2147483648 | bytes 8388608 | tf_op jit(solution)/shard_map/unmix/pallas_call | solution.py:64
  191.9 1.2 collective-permute-done.28
  193.9 1.1 collective-permute-start.30
  195.0 1.2 collective-permute-done.30
  196.3 4.2 %collective-permute-start.32 = (f32[16,8,128]{2,1,0:T(8,128)S(1)}, f32[16,8,128]{2,1,0:T(8,128)S(1)}, u32[]{:S(2)}, u32[]{:S(2)}) collective-permute-start(f32[16,8,128]{2,1,0:T(8,128)S(1)} %get-tuple-element.202), channel_id=1, source_target_pairs={{0,4},{2,6},{4,0},{6,2},{1,5},{3,7},{5,1},{7,3},{8,12},{10,14},{12... | collective-permute-start | bytes 196616 | tf_op jit(solution)/shard_map/ppermute | solution.py:39
  200.4 2.8 %collective-permute-start.29 = (bf16[3,8,4096]{2,1,0:T(8,128)(2,1)S(1)}, bf16[3,8,4096]{2,1,0:T(8,128)(2,1)S(1)}, u32[]{:S(2)}, u32[]{:S(2)}) collective-permute-start(bf16[3,8,4096]{2,1,0:T(8,128)(2,1)S(1)} %get-tuple-element.163), channel_id=1, source_target_pairs={{1,0},{2,1},{3,2},{4,3},{5,4},{6,5},{7,6},{8,7},{9,8},{10,9},{11,1... | collective-permute-start | bytes 589832 | tf_op jit(solution)/shard_map/ppermute | solution.py:27
  204.7 2.5 %collective-permute-start.35 = (f32[16,8,128]{2,1,0:T(8,128)S(1)}, f32[16,8,128]{2,1,0:T(8,128)S(1)}, u32[]{:S(2)}, u32[]{:S(2)}) collective-permute-start(f32[16,8,128]{2,1,0:T(8,128)S(1)} %fusion.1), channel_id=1, source_target_pairs={{0,64},{32,96},{64,0},{96,32},{1,65},{33,97},{65,1},{97,33},{2,66}... | collective-permute-start | bytes 196616 | tf_op jit(solution)/shard_map/ppermute | solution.py:39
  207.2 1.1 collective-permute-start.36
  208.3 3.2 %short_adjoint.3.refs_0_ = bf16[128,12288]{1,0:T(8,128)(2,1)} custom-call(bf16[1,128,4096]{2,1,0:T(8,128)(2,1)} %bitcast.47, bf16[3,8,4096]{2,1,0:T(8,128)(2,1)S(1)} %collective-permute-done.29.rim_ref, f32[7,12288]{1,0:T(8,128)} %filter_ref.5), custom_call_target="tpu_custom_call" | custom-call | flops 7340032 | bytes 2097152 | tf_op jit(solution)/shard_map/short_adjoint/pallas_call | solution.py:64
  211.6 1.2 collective-permute-start.37
  212.8 1.4 collective-permute-start.38
  214.2 1.1 collective-permute-start.39
  215.3 3.2 %short_adjoint.4.refs_0_ = bf16[128,12288]{1,0:T(8,128)(2,1)} custom-call(bf16[2,128,4096]{2,1,0:T(8,128)(2,1)} %get-tuple-element.162.grads_ref, bf16[3,8,4096]{2,1,0:T(8,128)(2,1)S(1)} %collective-permute-done.29.rim_ref, f32[7,12288]{1,0:T(8,128)} %filter_ref.5, bf16[128,12288]{1,0:T(8,128)(2,1)} %short_adjoint.3.refs_0_), custom_call_target="tpu_custom_call", output_to_operand_aliasing={{}: (3, {})} | custom-call | flops 7340032 | bytes 2097152 | tf_op jit(solution)/shard_map/short_adjoint/pallas_call | solution.py:64
  219.4 2.3 collective-permute-start.40
  222.7 2.1 collective-permute-start.41
  225.5 1.3 maximum_select_fusion
  226.7 3.2 %short_adjoint.5 = bf16[128,12288]{1,0:T(8,128)(2,1)} custom-call(bf16[2,128,4096]{2,1,0:T(8,128)(2,1)} %get-tuple-element.162.grads_ref, bf16[3,8,4096]{2,1,0:T(8,128)(2,1)S(1)} %collective-permute-done.29.rim_ref, f32[7,12288]{1,0:T(8,128)} %filter_ref.5, bf16[128,12288]{1,0:T(8,128)(2,1)} %short_adjoint.4.refs_0_), custom_call_target="tpu_custom_call", output_to_operand_aliasing={{}: (3, {})} | custom-call | flops 7340032 | bytes 2097152 | tf_op jit(solution)/shard_map/short_adjoint/pallas_call | solution.py:64
  230.9 3.3 %collective-permute-done.43.refs_3_ = f32[32,8,128]{2,1,0:T(8,128)S(1)} collective-permute-done((f32[32,8,128]{2,1,0:T(8,128)S(1)}, f32[32,8,128]{2,1,0:T(8,128)S(1)}, u32[]{:S(2)}, u32[]{:S(2)}) %collective-permute-start.43) | collective-permute-done | bytes 131104 | tf_op jit(solution)/shard_map/ppermute | solution.py:39
  234.2 1.5 collect.1
  (96 shorter events, 18.2 us)
Async XLA Ops:
  7.2 94.1 %all-gather.2.cloned.1.call-start = ((), (), s32[]{:S(2)}) async-start(), calls=%async_computation.1 | async-start | bytes 9437184 | tf_op jit(solution)/shard_map/all_gather | solution.py:737
  8.2 11.7 %collective-permute-start = (bf16[8,12288]{1,0:T(8,128)(2,1)S(1)}, bf16[8,12288]{1,0:T(8,128)(2,1)S(1)}, u32[]{:S(2)}, u32[]{:S(2)}) collective-permute-start(bf16[8,12288]{1,0:T(8,128)(2,1)S(1)} %slice_bitcast_fusion), channel_id=1, source_target_pairs={{0,1},{1,2},{2,3},{3,4},{4,5},{5,6},{6,7},{7,8},{8,9},{9,10},{10,1... | collective-permute-start | bytes 589832 | tf_op jit(solution)/shard_map/ppermute | solution.py:27
  19.8 2.6 %copy-start = (bf16[8,12288]{1,0:T(8,128)(2,1)}, bf16[8,12288]{1,0:T(8,128)(2,1)S(1)}, u32[]{:S(2)}) copy-start(bf16[8,12288]{1,0:T(8,128)(2,1)S(1)} %collective-permute-done.refs_3_.refs_4_.refs_5_.rim_ref.key_rim_ref.value_rim_ref) | copy-start | bytes 589828
  19.8 4.5 %copy-start.9 = (bf16[512,256]{1,0:T(8,128)(2,1)S(1)}, bf16[512,256]{1,0:T(8,128)(2,1)}, u32[]{:S(2)}) copy-start(bf16[512,256]{1,0:T(8,128)(2,1)} %param.8) | copy-start | bytes 786436
  19.9 9.6 %copy-start.10 = (bf16[256,128]{1,0:T(8,128)(2,1)S(1)}, bf16[256,128]{1,0:T(8,128)(2,1)}, u32[]{:S(2)}) copy-start(bf16[256,128]{1,0:T(8,128)(2,1)} %param.7) | copy-start | bytes 196612
  22.4 14.0 %collective-permute-start.1 = (bf16[128,4096]{1,0:T(8,128)(2,1)}, bf16[128,4096]{1,0:T(8,128)(2,1)S(1)}, u32[]{:S(2)}, u32[]{:S(2)}) collective-permute-start(bf16[128,4096]{1,0:T(8,128)(2,1)} %get-tuple-element.104.cur_ref), channel_id=1, source_target_pairs={{0,1},{1,2},{2,3},{3,4},{4,5},{5,6},{6,7},{7,8},{8,9},{9,10},{10,1... | collective-permute-start | bytes 3145736 | tf_op jit(solution)/shard_map/ppermute | solution.py:27
  24.4 5.9 %collective-permute-start.2 = (bf16[256,256]{1,0:T(8,128)(2,1)S(1)}, bf16[256,256]{1,0:T(8,128)(2,1)S(1)}, u32[]{:S(2)}, u32[]{:S(2)}) collective-permute-start(bf16[256,256]{1,0:T(8,128)(2,1)S(1)} %slice.56), channel_id=1, source_target_pairs={{0,32},{32,64},{64,96},{96,0},{1,33},{33,65},{65,97},{97,1},{2,34}... | collective-permute-start | bytes 393224 | tf_op jit(solution)/shard_map/ppermute | solution.py:39
  25.7 8.5 %collective-permute-start.3 = (bf16[256,256]{1,0:T(8,128)(2,1)S(1)}, bf16[256,256]{1,0:T(8,128)(2,1)S(1)}, u32[]{:S(2)}, u32[]{:S(2)}) collective-permute-start(bf16[256,256]{1,0:T(8,128)(2,1)S(1)} %slice.56), channel_id=1, source_target_pairs={{0,64},{32,96},{64,0},{96,32},{1,65},{33,97},{65,1},{97,33},{2,66}... | collective-permute-start | bytes 393224 | tf_op jit(solution)/shard_map/ppermute | solution.py:39
  28.4 5.8 %collective-permute-start.4 = (bf16[256,256]{1,0:T(8,128)(2,1)S(1)}, bf16[256,256]{1,0:T(8,128)(2,1)S(1)}, u32[]{:S(2)}, u32[]{:S(2)}) collective-permute-start(bf16[256,256]{1,0:T(8,128)(2,1)S(1)} %slice.56), channel_id=1, source_target_pairs={{0,96},{32,0},{64,32},{96,64},{1,97},{33,1},{65,33},{97,65},{2,98}... | collective-permute-start | bytes 393224 | tf_op jit(solution)/shard_map/ppermute | solution.py:39
  36.4 9.8 %copy-start.1 = (bf16[128,4096]{1,0:T(8,128)(2,1)}, bf16[128,4096]{1,0:T(8,128)(2,1)S(1)}, u32[]{:S(2)}) copy-start(bf16[128,4096]{1,0:T(8,128)(2,1)S(1)} %collective-permute-done.1.prev_ref) | copy-start | bytes 3145732
  36.4 19.7 %copy-start.5 = (bf16[1,2048,256]{2,1,0:T(8,128)(2,1)S(1)}, bf16[1,2048,256]{2,1,0:T(8,128)(2,1)}, u32[]{:S(2)}) copy-start(bf16[1,2048,256]{2,1,0:T(8,128)(2,1)} %param.9) | copy-start | bytes 3145732
  46.2 113.9 %reduce-scatter.2.cloned.1.call-start = ((), (), s32[]{:S(2)}) async-start(), calls=%async_computation.2 | async-start | bytes 9437184 | tf_op jit(solution)/shard_map/reduce_scatter | solution.py:744
  46.3 5.4 %collective-permute-start.5 = (bf16[256,256]{1,0:T(8,128)(2,1)S(1)}, bf16[256,256]{1,0:T(8,128)(2,1)S(1)}, u32[]{:S(2)}, u32[]{:S(2)}) collective-permute-start(bf16[256,256]{1,0:T(8,128)(2,1)S(1)} %slice.57), channel_id=1, source_target_pairs={{0,8},{8,0},{1,9},{9,1},{2,10},{10,2},{3,11},{11,3},{4,12},{12,4},... | collective-permute-start | bytes 393224 | tf_op jit(solution)/shard_map/ppermute | solution.py:39
  49.1 4.2 %collective-permute-start.6 = (bf16[256,256]{1,0:T(8,128)(2,1)S(1)}, bf16[256,256]{1,0:T(8,128)(2,1)}, u32[]{:S(2)}, u32[]{:S(2)}) collective-permute-start(bf16[256,256]{1,0:T(8,128)(2,1)S(1)} %slice.57), channel_id=1, source_target_pairs={{0,16},{16,0},{1,17},{17,1},{2,18},{18,2},{3,19},{19,3},{4,20},{20... | collective-permute-start | bytes 393224 | tf_op jit(solution)/shard_map/ppermute | solution.py:39
  49.4 5.1 %collective-permute-start.7 = (bf16[256,256]{1,0:T(8,128)(2,1)S(1)}, bf16[256,256]{1,0:T(8,128)(2,1)}, u32[]{:S(2)}, u32[]{:S(2)}) collective-permute-start(bf16[256,256]{1,0:T(8,128)(2,1)S(1)} %slice.57), channel_id=1, source_target_pairs={{0,24},{8,16},{16,8},{24,0},{1,25},{9,17},{17,9},{25,1},{2,26},{10... | collective-permute-start | bytes 393224 | tf_op jit(solution)/shard_map/ppermute | solution.py:39
  54.6 10.5 %collective-permute-start.12 = (bf16[4,256,256]{2,1,0:T(8,128)(2,1)S(1)}, bf16[4,256,256]{2,1,0:T(8,128)(2,1)S(1)}, u32[]{:S(2)}, u32[]{:S(2)}) collective-permute-start(bf16[4,256,256]{2,1,0:T(8,128)(2,1)S(1)} %pad_maximum_fusion.2.refs_5_.refs_4_), channel_id=1, source_target_pairs={{0,8},{8,0},{1,9},{9,1},{2,10},{10,2},{3,11},{11,3},{4,12},{12,4},... | collective-permute-start | bytes 1572872 | tf_op jit(solution)/shard_map/ppermute | solution.py:39
  56.3 14.4 %collective-permute-start.8 = (bf16[1024,256]{0,1:T(8,128)(2,1)S(1)}, bf16[1024,256]{0,1:T(8,128)(2,1)S(1)}, u32[]{:S(2)}, u32[]{:S(2)}) collective-permute-start(bf16[1024,256]{0,1:T(8,128)(2,1)S(1)} %bitcast.51), channel_id=1, source_target_pairs={{0,8},{8,0},{1,9},{9,1},{2,10},{10,2},{3,11},{11,3},{4,12},{12,4},... | collective-permute-start | bytes 1572872 | tf_op jit(solution)/shard_map/ppermute | solution.py:39
  58.0 19.3 %collective-permute-start.13 = (bf16[4,256,256]{2,1,0:T(8,128)(2,1)S(1)}, bf16[4,256,256]{2,1,0:T(8,128)(2,1)}, u32[]{:S(2)}, u32[]{:S(2)}) collective-permute-start(bf16[4,256,256]{2,1,0:T(8,128)(2,1)S(1)} %pad_maximum_fusion.2.refs_5_.refs_4_), channel_id=1, source_target_pairs={{0,16},{16,0},{1,17},{17,1},{2,18},{18,2},{3,19},{19,3},{4,20},{20... | collective-permute-start | bytes 1572872 | tf_op jit(solution)/shard_map/ppermute | solution.py:39
  58.0 20.0 %collective-permute-start.14 = (bf16[4,256,256]{2,1,0:T(8,128)(2,1)S(1)}, bf16[4,256,256]{2,1,0:T(8,128)(2,1)}, u32[]{:S(2)}, u32[]{:S(2)}) collective-permute-start(bf16[4,256,256]{2,1,0:T(8,128)(2,1)S(1)} %pad_maximum_fusion.2.refs_5_.refs_4_), channel_id=1, source_target_pairs={{0,24},{8,16},{16,8},{24,0},{1,25},{9,17},{17,9},{25,1},{2,26},{10... | collective-permute-start | bytes 1572872 | tf_op jit(solution)/shard_map/ppermute | solution.py:39
  60.8 17.3 %collective-permute-start.10 = (bf16[4,256,256]{2,1,0:T(8,128)(2,1)S(1)}, bf16[4,256,256]{2,1,0:T(8,128)(2,1)}, u32[]{:S(2)}, u32[]{:S(2)}) collective-permute-start(bf16[4,256,256]{2,1,0:T(8,128)(2,1)S(1)} %pad_maximum_fusion.1.refs_1_.refs_0_), channel_id=1, source_target_pairs={{0,64},{32,96},{64,0},{96,32},{1,65},{33,97},{65,1},{97,33},{2,66}... | collective-permute-start | bytes 1572872 | tf_op jit(solution)/shard_map/ppermute | solution.py:39
  65.1 7.1 %copy-start.2 = (bf16[4,256,256]{2,1,0:T(8,128)(2,1)}, bf16[4,256,256]{2,1,0:T(8,128)(2,1)S(1)}, u32[]{:S(2)}) copy-start(bf16[4,256,256]{2,1,0:T(8,128)(2,1)S(1)} %collective-permute-done.12.refs_6_.refs_5_) | copy-start | bytes 1572868
  65.1 12.9 %collective-permute-start.11 = (bf16[4,256,256]{2,1,0:T(8,128)(2,1)S(1)}, bf16[4,256,256]{2,1,0:T(8,128)(2,1)}, u32[]{:S(2)}, u32[]{:S(2)}) collective-permute-start(bf16[4,256,256]{2,1,0:T(8,128)(2,1)S(1)} %pad_maximum_fusion.1.refs_1_.refs_0_), channel_id=1, source_target_pairs={{0,96},{32,0},{64,32},{96,64},{1,97},{33,1},{65,33},{97,65},{2,98}... | collective-permute-start | bytes 1572872 | tf_op jit(solution)/shard_map/ppermute | solution.py:39
  70.7 9.7 %collective-permute-start.9 = (bf16[4,256,256]{2,1,0:T(8,128)(2,1)S(1)}, bf16[4,256,256]{2,1,0:T(8,128)(2,1)}, u32[]{:S(2)}, u32[]{:S(2)}) collective-permute-start(bf16[4,256,256]{2,1,0:T(8,128)(2,1)S(1)} %pad_maximum_fusion.1.refs_1_.refs_0_), channel_id=1, source_target_pairs={{0,32},{32,64},{64,96},{96,0},{1,33},{33,65},{65,97},{97,1},{2,34}... | collective-permute-start | bytes 1572872 | tf_op jit(solution)/shard_map/ppermute | solution.py:39
  80.4 1.1 copy-start.3
  101.3 21.0 %copy-start.4 = (bf16[4,256,256]{2,1,0:T(8,128)(2,1)S(1)}, bf16[4,256,256]{2,1,0:T(8,128)(2,1)}, u32[]{:S(2)}) copy-start(bf16[4,256,256]{2,1,0:T(8,128)(2,1)} %copy-done.2) | copy-start | bytes 1572868
  111.3 9.9 %collective-permute-start.18 = (bf16[4,256,256]{2,1,0:T(8,128)(2,1)}, bf16[4,256,256]{2,1,0:T(8,128)(2,1)S(1)}, u32[]{:S(2)}, u32[]{:S(2)}) collective-permute-start(bf16[4,256,256]{2,1,0:T(8,128)(2,1)} %get-tuple-element.133), channel_id=1, source_target_pairs={{0,8},{8,0},{1,9},{9,1},{2,10},{10,2},{3,11},{11,3},{4,12},{12,4},... | collective-permute-start | bytes 1572872 | tf_op jit(solution)/shard_map/ppermute | solution.py:39
  114.0 18.3 %collective-permute-start.19 = (bf16[4,256,256]{2,1,0:T(8,128)(2,1)}, bf16[4,256,256]{2,1,0:T(8,128)(2,1)S(1)}, u32[]{:S(2)}, u32[]{:S(2)}) collective-permute-start(bf16[4,256,256]{2,1,0:T(8,128)(2,1)} %get-tuple-element.134), channel_id=1, source_target_pairs={{0,16},{16,0},{1,17},{17,1},{2,18},{18,2},{3,19},{19,3},{4,20},{20... | collective-permute-start | bytes 1572872 | tf_op jit(solution)/shard_map/ppermute | solution.py:39
  114.2 18.7 %collective-permute-start.20 = (bf16[4,256,256]{2,1,0:T(8,128)(2,1)}, bf16[4,256,256]{2,1,0:T(8,128)(2,1)S(1)}, u32[]{:S(2)}, u32[]{:S(2)}) collective-permute-start(bf16[4,256,256]{2,1,0:T(8,128)(2,1)} %get-tuple-element.135), channel_id=1, source_target_pairs={{0,24},{8,16},{16,8},{24,0},{1,25},{9,17},{17,9},{25,1},{2,26},{10... | collective-permute-start | bytes 1572872 | tf_op jit(solution)/shard_map/ppermute | solution.py:39
  114.8 18.4 %collective-permute-start.15 = (bf16[4,256,256]{2,1,0:T(8,128)(2,1)}, bf16[4,256,256]{2,1,0:T(8,128)(2,1)S(1)}, u32[]{:S(2)}, u32[]{:S(2)}) collective-permute-start(bf16[4,256,256]{2,1,0:T(8,128)(2,1)} %get-tuple-element.129), channel_id=1, source_target_pairs={{0,96},{32,0},{64,32},{96,64},{1,97},{33,1},{65,33},{97,65},{2,98}... | collective-permute-start | bytes 1572872 | tf_op jit(solution)/shard_map/ppermute | solution.py:39
  117.3 15.9 %collective-permute-start.16 = (bf16[4,256,256]{2,1,0:T(8,128)(2,1)}, bf16[4,256,256]{2,1,0:T(8,128)(2,1)S(1)}, u32[]{:S(2)}, u32[]{:S(2)}) collective-permute-start(bf16[4,256,256]{2,1,0:T(8,128)(2,1)} %get-tuple-element.130), channel_id=1, source_target_pairs={{0,64},{32,96},{64,0},{96,32},{1,65},{33,97},{65,1},{97,33},{2,66}... | collective-permute-start | bytes 1572872 | tf_op jit(solution)/shard_map/ppermute | solution.py:39
  121.1 11.8 %copy-start.8 = (bf16[4,256,256]{2,1,0:T(8,128)(2,1)S(1)}, bf16[4,256,256]{2,1,0:T(8,128)(2,1)}, u32[]{:S(2)}) copy-start(bf16[4,256,256]{2,1,0:T(8,128)(2,1)} %get-tuple-element.132) | copy-start | bytes 1572868
  121.1 13.3 %collective-permute-start.17 = (bf16[4,256,256]{2,1,0:T(8,128)(2,1)}, bf16[4,256,256]{2,1,0:T(8,128)(2,1)S(1)}, u32[]{:S(2)}, u32[]{:S(2)}) collective-permute-start(bf16[4,256,256]{2,1,0:T(8,128)(2,1)} %get-tuple-element.131), channel_id=1, source_target_pairs={{0,32},{32,64},{64,96},{96,0},{1,33},{33,65},{65,97},{97,1},{2,34}... | collective-permute-start | bytes 1572872 | tf_op jit(solution)/shard_map/ppermute | solution.py:39
  132.2 2.2 copy-start.7
  134.7 7.5 %collective-permute-start.21 = (bf16[256,256]{1,0:T(8,128)(2,1)S(1)}, bf16[256,256]{1,0:T(8,128)(2,1)S(1)}, u32[]{:S(2)}, u32[]{:S(2)}) collective-permute-start(bf16[256,256]{1,0:T(8,128)(2,1)S(1)} %get-tuple-element.198), channel_id=1, source_target_pairs={{0,8},{8,0},{1,9},{9,1},{2,10},{10,2},{3,11},{11,3},{4,12},{12,4},... | collective-permute-start | bytes 393224 | tf_op jit(solution)/shard_map/ppermute | solution.py:39
  137.8 5.0 %collective-permute-start.22 = (bf16[256,256]{1,0:T(8,128)(2,1)S(1)}, bf16[256,256]{1,0:T(8,128)(2,1)S(1)}, u32[]{:S(2)}, u32[]{:S(2)}) collective-permute-start(bf16[256,256]{1,0:T(8,128)(2,1)S(1)} %get-tuple-element.197), channel_id=1, source_target_pairs={{0,16},{16,0},{1,17},{17,1},{2,18},{18,2},{3,19},{19,3},{4,20},{20... | collective-permute-start | bytes 393224 | tf_op jit(solution)/shard_map/ppermute | solution.py:39
  138.3 5.4 %collective-permute-start.23 = (bf16[256,256]{1,0:T(8,128)(2,1)S(1)}, bf16[256,256]{1,0:T(8,128)(2,1)S(1)}, u32[]{:S(2)}, u32[]{:S(2)}) collective-permute-start(bf16[256,256]{1,0:T(8,128)(2,1)S(1)} %get-tuple-element.196), channel_id=1, source_target_pairs={{0,24},{8,16},{16,8},{24,0},{1,25},{9,17},{17,9},{25,1},{2,26},{10... | collective-permute-start | bytes 393224 | tf_op jit(solution)/shard_map/ppermute | solution.py:39
  138.9 6.0 %collective-permute-start.24 = (bf16[256,256]{1,0:T(8,128)(2,1)S(1)}, bf16[256,256]{1,0:T(8,128)(2,1)S(1)}, u32[]{:S(2)}, u32[]{:S(2)}) collective-permute-start(bf16[256,256]{1,0:T(8,128)(2,1)S(1)} %get-tuple-element.194), channel_id=1, source_target_pairs={{0,96},{32,0},{64,32},{96,64},{1,97},{33,1},{65,33},{97,65},{2,98}... | collective-permute-start | bytes 393224 | tf_op jit(solution)/shard_map/ppermute | solution.py:39
  141.6 5.4 %collective-permute-start.25 = (bf16[256,256]{1,0:T(8,128)(2,1)S(1)}, bf16[256,256]{1,0:T(8,128)(2,1)S(1)}, u32[]{:S(2)}, u32[]{:S(2)}) collective-permute-start(bf16[256,256]{1,0:T(8,128)(2,1)S(1)} %get-tuple-element.193), channel_id=1, source_target_pairs={{0,64},{32,96},{64,0},{96,32},{1,65},{33,97},{65,1},{97,33},{2,66}... | collective-permute-start | bytes 393224 | tf_op jit(solution)/shard_map/ppermute | solution.py:39
  142.3 6.4 %collective-permute-start.26 = (bf16[256,256]{1,0:T(8,128)(2,1)S(1)}, bf16[256,256]{1,0:T(8,128)(2,1)S(1)}, u32[]{:S(2)}, u32[]{:S(2)}) collective-permute-start(bf16[256,256]{1,0:T(8,128)(2,1)S(1)} %get-tuple-element.192), channel_id=1, source_target_pairs={{0,32},{32,64},{64,96},{96,0},{1,33},{33,65},{65,97},{97,1},{2,34}... | collective-permute-start | bytes 393224 | tf_op jit(solution)/shard_map/ppermute | solution.py:39
  163.1 17.4 %collective-permute-start.27 = (bf16[128,4096]{1,0:T(8,128)(2,1)}, bf16[128,4096]{1,0:T(8,128)(2,1)S(1)}, u32[]{:S(2)}, u32[]{:S(2)}) collective-permute-start(bf16[128,4096]{1,0:T(8,128)(2,1)} %gate_back.1.grad_ref), channel_id=1, source_target_pairs={{1,0},{2,1},{3,2},{4,3},{5,4},{6,5},{7,6},{8,7},{9,8},{10,9},{11,1... | collective-permute-start | bytes 3145736 | tf_op jit(solution)/shard_map/ppermute | solution.py:27
  166.4 11.1 %copy-start.11 = (bf16[1024,256]{1,0:T(8,128)(2,1)S(1)}, bf16[1024,256]{1,0:T(8,128)(2,1)}, u32[]{:S(2)}) copy-start(bf16[1024,256]{1,0:T(8,128)(2,1)} %get-tuple-element.160) | copy-start | bytes 1572868
  177.5 15.6 %collective-permute-start.28 = (bf16[1024,256]{1,0:T(8,128)(2,1)S(1)}, bf16[1024,256]{1,0:T(8,128)(2,1)S(1)}, u32[]{:S(2)}, u32[]{:S(2)}) collective-permute-start(bf16[1024,256]{1,0:T(8,128)(2,1)S(1)} %copy-done.11), channel_id=1, source_target_pairs={{0,8},{8,0},{1,9},{9,1},{2,10},{10,2},{3,11},{11,3},{4,12},{12,4},... | collective-permute-start | bytes 1572872 | tf_op jit(solution)/shard_map/ppermute | solution.py:39
  193.9 2.2 collective-permute-start.30
  196.2 7.1 %collective-permute-start.31 = (f32[16,8,128]{2,1,0:T(8,128)S(1)}, f32[16,8,128]{2,1,0:T(8,128)S(1)}, u32[]{:S(2)}, u32[]{:S(2)}) collective-permute-start(f32[16,8,128]{2,1,0:T(8,128)S(1)} %get-tuple-element.200), channel_id=1, source_target_pairs={{0,2},{2,4},{4,6},{6,0},{1,3},{3,5},{5,7},{7,1},{8,10},{10,12},{12... | collective-permute-start | bytes 196616 | tf_op jit(solution)/shard_map/ppermute | solution.py:39
  196.3 7.1 %collective-permute-start.32 = (f32[16,8,128]{2,1,0:T(8,128)S(1)}, f32[16,8,128]{2,1,0:T(8,128)S(1)}, u32[]{:S(2)}, u32[]{:S(2)}) collective-permute-start(f32[16,8,128]{2,1,0:T(8,128)S(1)} %get-tuple-element.202), channel_id=1, source_target_pairs={{0,4},{2,6},{4,0},{6,2},{1,5},{3,7},{5,1},{7,3},{8,12},{10,14},{12... | collective-permute-start | bytes 196616 | tf_op jit(solution)/shard_map/ppermute | solution.py:39
  200.4 3.4 %collective-permute-start.33 = (f32[16,8,128]{2,1,0:T(8,128)S(1)}, f32[16,8,128]{2,1,0:T(8,128)S(1)}, u32[]{:S(2)}, u32[]{:S(2)}) collective-permute-start(f32[16,8,128]{2,1,0:T(8,128)S(1)} %get-tuple-element.201), channel_id=1, source_target_pairs={{0,6},{2,0},{4,2},{6,4},{1,7},{3,1},{5,3},{7,5},{8,14},{10,8},{12,... | collective-permute-start | bytes 196616 | tf_op jit(solution)/shard_map/ppermute | solution.py:39
  200.4 7.9 %collective-permute-start.29 = (bf16[3,8,4096]{2,1,0:T(8,128)(2,1)S(1)}, bf16[3,8,4096]{2,1,0:T(8,128)(2,1)S(1)}, u32[]{:S(2)}, u32[]{:S(2)}) collective-permute-start(bf16[3,8,4096]{2,1,0:T(8,128)(2,1)S(1)} %get-tuple-element.163), channel_id=1, source_target_pairs={{1,0},{2,1},{3,2},{4,3},{5,4},{6,5},{7,6},{8,7},{9,8},{10,9},{11,1... | collective-permute-start | bytes 589832 | tf_op jit(solution)/shard_map/ppermute | solution.py:27
  203.9 7.7 %collective-permute-start.34 = (f32[16,8,128]{2,1,0:T(8,128)S(1)}, f32[16,8,128]{2,1,0:T(8,128)S(1)}, u32[]{:S(2)}, u32[]{:S(2)}) collective-permute-start(f32[16,8,128]{2,1,0:T(8,128)S(1)} %fusion.1), channel_id=1, source_target_pairs={{0,32},{32,64},{64,96},{96,0},{1,33},{33,65},{65,97},{97,1},{2,34}... | collective-permute-start | bytes 196616 | tf_op jit(solution)/shard_map/ppermute | solution.py:39
  204.7 6.9 %collective-permute-start.35 = (f32[16,8,128]{2,1,0:T(8,128)S(1)}, f32[16,8,128]{2,1,0:T(8,128)S(1)}, u32[]{:S(2)}, u32[]{:S(2)}) collective-permute-start(f32[16,8,128]{2,1,0:T(8,128)S(1)} %fusion.1), channel_id=1, source_target_pairs={{0,64},{32,96},{64,0},{96,32},{1,65},{33,97},{65,1},{97,33},{2,66}... | collective-permute-start | bytes 196616 | tf_op jit(solution)/shard_map/ppermute | solution.py:39
  207.2 4.3 %collective-permute-start.36 = (f32[16,8,128]{2,1,0:T(8,128)S(1)}, f32[16,8,128]{2,1,0:T(8,128)S(1)}, u32[]{:S(2)}, u32[]{:S(2)}) collective-permute-start(f32[16,8,128]{2,1,0:T(8,128)S(1)} %fusion.1), channel_id=1, source_target_pairs={{0,96},{32,0},{64,32},{96,64},{1,97},{33,1},{65,33},{97,65},{2,98}... | collective-permute-start | bytes 196616 | tf_op jit(solution)/shard_map/ppermute | solution.py:39
  211.6 7.0 %collective-permute-start.37 = (f32[16,8,128]{2,1,0:T(8,128)S(1)}, f32[16,8,128]{2,1,0:T(8,128)S(1)}, u32[]{:S(2)}, u32[]{:S(2)}) collective-permute-start(f32[16,8,128]{2,1,0:T(8,128)S(1)} %add_add_fusion.1), channel_id=1, source_target_pairs={{0,8},{8,0},{1,9},{9,1},{2,10},{10,2},{3,11},{11,3},{4,12},{12,4},... | collective-permute-start | bytes 196616 | tf_op jit(solution)/shard_map/ppermute | solution.py:39
  212.8 5.8 %collective-permute-start.38 = (f32[16,8,128]{2,1,0:T(8,128)S(1)}, f32[16,8,128]{2,1,0:T(8,128)S(1)}, u32[]{:S(2)}, u32[]{:S(2)}) collective-permute-start(f32[16,8,128]{2,1,0:T(8,128)S(1)} %add_add_fusion.1), channel_id=1, source_target_pairs={{0,16},{16,0},{1,17},{17,1},{2,18},{18,2},{3,19},{19,3},{4,20},{20... | collective-permute-start | bytes 196616 | tf_op jit(solution)/shard_map/ppermute | solution.py:39
  214.2 5.1 %collective-permute-start.39 = (f32[16,8,128]{2,1,0:T(8,128)S(1)}, f32[16,8,128]{2,1,0:T(8,128)S(1)}, u32[]{:S(2)}, u32[]{:S(2)}) collective-permute-start(f32[16,8,128]{2,1,0:T(8,128)S(1)} %add_add_fusion.1), channel_id=1, source_target_pairs={{0,24},{8,16},{16,8},{24,0},{1,25},{9,17},{17,9},{25,1},{2,26},{10... | collective-permute-start | bytes 196616 | tf_op jit(solution)/shard_map/ppermute | solution.py:39
  215.3 10.2 %copy-start.6 = (bf16[1024,256]{1,0:T(8,128)(2,1)S(1)}, bf16[1024,256]{1,0:T(8,128)(2,1)}, u32[]{:S(2)}) copy-start(bf16[1024,256]{1,0:T(8,128)(2,1)} %get-tuple-element.126) | copy-start | bytes 1572868
  219.4 3.3 %collective-permute-start.40 = (f32[16,8,128]{2,1,0:T(8,128)S(1)}, f32[16,8,128]{2,1,0:T(8,128)S(1)}, u32[]{:S(2)}, u32[]{:S(2)}) collective-permute-start(f32[16,8,128]{2,1,0:T(8,128)S(1)} %add_add_fusion), channel_id=1, source_target_pairs={{0,1},{1,0},{2,3},{3,2},{4,5},{5,4},{6,7},{7,6},{8,9},{9,8},{10,11... | collective-permute-start | bytes 196616 | tf_op jit(solution)/shard_map/ppermute | solution.py:39
  222.7 7.2 %collective-permute-start.41 = (f32[32,8,128]{2,1,0:T(8,128)S(1)}, f32[32,8,128]{2,1,0:T(8,128)S(1)}, u32[]{:S(2)}, u32[]{:S(2)}) collective-permute-start(f32[32,8,128]{2,1,0:T(8,128)S(1)} %pad_maximum_fusion.3.refs_0_), channel_id=1, source_target_pairs={{0,6},{2,0},{4,2},{6,4},{1,7},{3,1},{5,3},{7,5},{8,14},{10,8},{12,... | collective-permute-start | bytes 393224 | tf_op jit(solution)/shard_map/ppermute | solution.py:39
  224.8 6.1 %collective-permute-start.42 = (f32[32,8,128]{2,1,0:T(8,128)S(1)}, f32[32,8,128]{2,1,0:T(8,128)S(1)}, u32[]{:S(2)}, u32[]{:S(2)}) collective-permute-start(f32[32,8,128]{2,1,0:T(8,128)S(1)} %pad_maximum_fusion.3.refs_0_), channel_id=1, source_target_pairs={{0,4},{2,6},{4,0},{6,2},{1,5},{3,7},{5,1},{7,3},{8,12},{10,14},{12... | collective-permute-start | bytes 393224 | tf_op jit(solution)/shard_map/ppermute | solution.py:39
  224.9 9.3 %collective-permute-start.43 = (f32[32,8,128]{2,1,0:T(8,128)S(1)}, f32[32,8,128]{2,1,0:T(8,128)S(1)}, u32[]{:S(2)}, u32[]{:S(2)}) collective-permute-start(f32[32,8,128]{2,1,0:T(8,128)S(1)} %pad_maximum_fusion.3.refs_0_), channel_id=1, source_target_pairs={{0,2},{2,4},{4,6},{6,0},{1,3},{3,5},{5,7},{7,1},{8,10},{10,12},{12... | collective-permute-start | bytes 393224 | tf_op jit(solution)/shard_map/ppermute | solution.py:39
Sparse Core Ops, SparseCore 0:
  46.3 54.9 all-gather.1
  103.7 56.3 reduce-scatter.1

commit v15 on v14

--- a/solution.py
+++ b/solution.py
@@ -10,7 +10,7 @@
 from jax.sharding import PartitionSpec as P
 
 LANES = 128
-RIM = 8
+RIM = 16
 MIB = 1024 * 1024
 WIDTH = 1024
 F32 = jnp.float32

time: 243 us -> 250 us (1.029)
  starting transfers between devices: 70.8 us -> 74.8 us
    ppermute x40, waiting for transfers between devices: 38.3 us -> 42.7 us  [move(): return lax.ppermute(x, axes, pairs)]
    ppermute x40, starting transfers between devices: 57.8 us -> 62 us  [move(): return lax.ppermute(x, axes, pairs)]
  transfers between devices with their start and end apart: 46 -> 46, of which waited for: 27 -> 27; matrix products, arithmetic and copies ran while one was open for 3% -> 3% of each run, Pallas kernels for 28% -> 27%
where the time goes in v15:
time: 250 us; the launch traced here: 249 us
  Pallas kernels  85.2 us (34%)
  starting transfers between devices  74.8 us (30%)
  waiting for transfers between devices  65 us (26%)
  between operations  14.4 us (6%)
  local copies, waits for them, and re-layouts  5.21 us (2%)
  other arithmetic  4.36 us (2%)
    pallas_call x12, Pallas kernels, run(): return call(*held)  83.1 us
    ppermute x40, starting transfers between devices, move(): return lax.ppermute(x, axes, pairs)  62 us
    ppermute x40, waiting for transfers between devices, move(): return lax.ppermute(x, axes, pairs)  42.7 us
    ppermute x4, starting transfers between devices, along(): return lax.ppermute(x, LINE, pairs)  12.7 us
    all_gather x1, waiting for transfers between devices, shards(): all_rows = lax.all_gather(gated, ('z', 'c'), axis=0, tiled=True)  11.3 us
    reduce_scatter x1, waiting for transfers between devices, shards(): lax.psum_scatter(partial, ('z', 'c'), scatter_dimension=0, tiled=True)  9.3 us
  transfers between devices with their start and end apart: 46, of which 27 were waited for; matrix products, arithmetic and copies ran while one was open for 3% of the time, Pallas kernels for 27%

profile of v15, /device:TPU:1, one launch (start us, length us, event | category | flops | bytes accessed | tf_op | source)
XLA Modules:
  0.0 249.0 jit_solution(4562731645800342130)
XLA Ops:
  8.2 4.9 %collective-permute-start = (bf16[16,12288]{1,0:T(8,128)(2,1)S(1)}, bf16[16,12288]{1,0:T(8,128)(2,1)S(1)}, u32[]{:S(2)}, u32[]{:S(2)}) collective-permute-start(bf16[16,12288]{1,0:T(8,128)(2,1)S(1)} %slice_bitcast_fusion), channel_id=1, source_target_pairs={{0,1},{1,2},{2,3},{3,4},{4,5},{5,6},{6,7},{7,8},{8,9},{9,10},{10,1... | collective-permute-start | bytes 1179656 | tf_op jit(solution)/shard_map/ppermute | solution.py:27
  13.2 6.7 %features.1 = (bf16[128,4096]{1,0:T(8,128)(2,1)}, bf16[128,4096]{1,0:T(8,128)(2,1)}, bf16[128,4096]{1,0:T(8,128)(2,1)}, bf16[128,4096]{1,0:T(8,128)(2,1)}) custom-call(bf16[128,12288]{1,0:T(8,128)(2,1)} %bitcast.37, bf16[128,12288]{1,0:T(8,128)(2,1)} %bitcast.38, bf16[128,12288]{1,0:T(8,128)(2,1)} %bitcast.39, f32[7,12288]{1,0:T(8,128)} %filter_ref.5, ...), custom_call_target="tpu_custom_call" | custom-call | bytes 1572864 | tf_op jit(solution)/shard_map/features/pallas_call | solution.py:64
  19.9 3.2 %first_rows.1 = (bf16[128,4096]{1,0:T(8,128)(2,1)}, bf16[128,4096]{1,0:T(8,128)(2,1)}, bf16[128,4096]{1,0:T(8,128)(2,1)}, bf16[128,4096]{1,0:T(8,128)(2,1)}) custom-call(bf16[128,12288]{1,0:T(8,128)(2,1)} %bitcast.40, bf16[128,12288]{1,0:T(8,128)(2,1)} %bitcast.41, ...), custom_call_target="tpu_custom_call", output_to_operand_aliasing={{0}: (9, {}), {1}: (10, {}), {2}: (11, {}), {3}: (12, {})} | custom-call | bytes 393216 | tf_op jit(solution)/shard_map/first_rows/pallas_call | solution.py:64
  23.2 2.3 collective-permute-start.1
  25.5 1.4 collective-permute-start.2
  26.9 2.6 %collective-permute-start.3 = (bf16[256,256]{1,0:T(8,128)(2,1)S(1)}, bf16[256,256]{1,0:T(8,128)(2,1)S(1)}, u32[]{:S(2)}, u32[]{:S(2)}) collective-permute-start(bf16[256,256]{1,0:T(8,128)(2,1)S(1)} %slice.56), channel_id=1, source_target_pairs={{0,64},{32,96},{64,0},{96,32},{1,65},{33,97},{65,1},{97,33},{2,66}... | collective-permute-start | bytes 393224 | tf_op jit(solution)/shard_map/ppermute | solution.py:39
  30.6 1.3 collective-permute-done.2
  31.9 3.9 %collective-permute-done.3 = bf16[256,256]{1,0:T(8,128)(2,1)S(1)} collective-permute-done((bf16[256,256]{1,0:T(8,128)(2,1)S(1)}, bf16[256,256]{1,0:T(8,128)(2,1)S(1)}, u32[]{:S(2)}, u32[]{:S(2)}) %collective-permute-start.3) | collective-permute-done | bytes 131104 | tf_op jit(solution)/shard_map/ppermute | solution.py:39
  35.8 1.7 collective-permute-done.1.prev_ref
  37.6 9.7 %mix.1 = (bf16[128,4096]{1,0:T(8,128)(2,1)}, bf16[128,4096]{1,0:T(8,128)(2,1)}) custom-call(f32[256,128]{1,0:T(8,128)S(1)} %convert_element_type.57.lines_ref, bf16[128,4096]{1,0:T(8,128)(2,1)S(1)} %collective-permute-done.1.prev_ref, bf16[128,4096]{1,0:T(8,128)(2,1)} %get-tuple-element.104.cur_ref, bf16[128,4096]{1,0:T(8,128)(2,1)} %get-tuple-element.107.query_ref), custom_call_target="tpu_custom_call" | custom-call | bytes 1048576 | tf_op jit(solution)/shard_map/mix/pallas_call | solution.py:64
  47.4 2.8 %collective-permute-start.5 = (bf16[256,256]{1,0:T(8,128)(2,1)S(1)}, bf16[256,256]{1,0:T(8,128)(2,1)S(1)}, u32[]{:S(2)}, u32[]{:S(2)}) collective-permute-start(bf16[256,256]{1,0:T(8,128)(2,1)S(1)} %slice.57), channel_id=1, source_target_pairs={{0,8},{8,0},{1,9},{9,1},{2,10},{10,2},{3,11},{11,3},{4,12},{12,4},... | collective-permute-start | bytes 393224 | tf_op jit(solution)/shard_map/ppermute | solution.py:39
  51.1 1.7 collective-permute-done.5
  52.8 1.6 collective-permute-done.6
  54.4 1.3 collective-permute-done.7
  55.7 1.5 collective-permute-start.12
  57.5 1.7 collective-permute-start.8
  59.2 1.7 collective-permute-start.14
  61.9 3.0 %collective-permute-start.10 = (bf16[4,256,256]{2,1,0:T(8,128)(2,1)S(1)}, bf16[4,256,256]{2,1,0:T(8,128)(2,1)}, u32[]{:S(2)}, u32[]{:S(2)}) collective-permute-start(bf16[4,256,256]{2,1,0:T(8,128)(2,1)S(1)} %pad_maximum_fusion.1.refs_1_.refs_0_), channel_id=1, source_target_pairs={{0,64},{32,96},{64,0},{96,32},{1,65},{33,97},{65,1},{97,33},{2,66}... | collective-permute-start | bytes 1572872 | tf_op jit(solution)/shard_map/ppermute | solution.py:39
  64.9 3.1 %collective-permute-done.12.refs_6_.refs_5_ = bf16[4,256,256]{2,1,0:T(8,128)(2,1)S(1)} collective-permute-done((bf16[4,256,256]{2,1,0:T(8,128)(2,1)S(1)}, bf16[4,256,256]{2,1,0:T(8,128)(2,1)S(1)}, u32[]{:S(2)}, u32[]{:S(2)}) %collective-permute-start.12) | collective-permute-done | bytes 524320 | tf_op jit(solution)/shard_map/ppermute | solution.py:39
  68.0 2.7 %collective-permute-start.11 = (bf16[4,256,256]{2,1,0:T(8,128)(2,1)S(1)}, bf16[4,256,256]{2,1,0:T(8,128)(2,1)}, u32[]{:S(2)}, u32[]{:S(2)}) collective-permute-start(bf16[4,256,256]{2,1,0:T(8,128)(2,1)S(1)} %pad_maximum_fusion.1.refs_1_.refs_0_), channel_id=1, source_target_pairs={{0,96},{32,0},{64,32},{96,64},{1,97},{33,1},{65,33},{97,65},{2,98}... | collective-permute-start | bytes 1572872 | tf_op jit(solution)/shard_map/ppermute | solution.py:39
  70.7 2.9 %collective-permute-done.8 = bf16[1024,256]{0,1:T(8,128)(2,1)S(1)} collective-permute-done((bf16[1024,256]{0,1:T(8,128)(2,1)S(1)}, bf16[1024,256]{0,1:T(8,128)(2,1)S(1)}, u32[]{:S(2)}, u32[]{:S(2)}) %collective-permute-start.8) | collective-permute-done | bytes 524320 | tf_op jit(solution)/shard_map/ppermute | solution.py:39
  73.6 1.3 collective-permute-start.9
  75.1 1.2 fusion.11
  76.3 1.5 copy.18.refs_0_
  78.6 1.3 collective-permute-done.14.refs_8_.refs_7_
  79.9 3.4 %collective-permute-done.9.refs_2_.refs_1_ = bf16[4,256,256]{2,1,0:T(8,128)(2,1)} collective-permute-done((bf16[4,256,256]{2,1,0:T(8,128)(2,1)S(1)}, bf16[4,256,256]{2,1,0:T(8,128)(2,1)}, u32[]{:S(2)}, u32[]{:S(2)}) %collective-permute-start.9) | collective-permute-done | bytes 524320 | tf_op jit(solution)/shard_map/ppermute | solution.py:39
  84.3 8.5 %gate_matmul.1 = bf16[1024,4096]{1,0:T(8,128)(2,1)} custom-call(bf16[1024,512]{1,0:T(8,128)(2,1)S(1)} %copy.18.refs_0_, bf16[4,256,256]{2,1,0:T(8,128)(2,1)S(1)} %pad_maximum_fusion.1.refs_1_.refs_0_, bf16[4,256,256]{2,1,0:T(8,128)(2,1)} %collective-permute-done.9.refs_2_.refs_1_, bf16[4,256,256]{2,1,0:T(8,128)(2,1)} %collective-permute-done.10.refs_3_.refs_2_, ...), custom_call_target="tpu_custom_call" | custom-call | flops 4294967296 | bytes 12582912 | tf_op jit(solution)/shard_map/gate_matmul/pallas_call | solution.py:64
  92.9 11.3 %all-gather.2.cloned.1.call-done.rows_ref = bf16[1024,4096]{1,0:T(8,128)(2,1)} async-done(((bf16[128,4096]{1,0:T(8,128)(2,1)}), bf16[1024,4096]{1,0:T(8,128)(2,1)}) %all-gather.2.cloned.1.call-update) | async-done | bytes 8388624 | tf_op jit(solution)/shard_map/all_gather | solution.py:737
  104.2 9.9 %weight_grad.1 = (bf16[4,256,256]{2,1,0:T(8,128)(2,1)}, bf16[4,256,256]{2,1,0:T(8,128)(2,1)}, bf16[4,256,256]{2,1,0:T(8,128)(2,1)}, bf16[4,256,256]{2,1,0:T(8,12...) custom-call(s32[8]{0:T(128)S(1)} %fusion.2.origin.place, ...), custom_call_target="tpu_custom_call" | custom-call | flops 4294967296 | bytes 12582912 | tf_op jit(solution)/shard_map/weight_grad/pallas_call | solution.py:64
  114.1 2.7 %collective-permute-start.18 = (bf16[4,256,256]{2,1,0:T(8,128)(2,1)}, bf16[4,256,256]{2,1,0:T(8,128)(2,1)S(1)}, u32[]{:S(2)}, u32[]{:S(2)}) collective-permute-start(bf16[4,256,256]{2,1,0:T(8,128)(2,1)} %get-tuple-element.133), channel_id=1, source_target_pairs={{0,8},{8,0},{1,9},{9,1},{2,10},{10,2},{3,11},{11,3},{4,12},{12,4},... | collective-permute-start | bytes 1572872 | tf_op jit(solution)/shard_map/ppermute | solution.py:39
  117.7 2.5 collective-permute-start.15
  120.7 3.3 %collective-permute-done.18 = bf16[4,256,256]{2,1,0:T(8,128)(2,1)S(1)} collective-permute-done((bf16[4,256,256]{2,1,0:T(8,128)(2,1)}, bf16[4,256,256]{2,1,0:T(8,128)(2,1)S(1)}, u32[]{:S(2)}, u32[]{:S(2)}) %collective-permute-start.18) | collective-permute-done | bytes 524320 | tf_op jit(solution)/shard_map/ppermute | solution.py:39
  124.0 1.2 collective-permute-start.17
  125.2 9.9 %output.1 = (bf16[1024,256]{1,0:T(8,128)(2,1)}, bf16[1024,256]{1,0:T(8,128)(2,1)}) custom-call(s32[8]{0:T(128)S(1)} %fusion.2.origin.place, bf16[1024,4096]{1,0:T(8,128)(2,1)} %all-gather.2.cloned.1.call-done.rows_ref, bf16[4,256,256]{2,1,0:T(8,128)(2,1)S(1)} %pad_maximum_fusion.1.refs_1_.refs_0_, ...), custom_call_target="tpu_custom_call" | custom-call | flops 4294967296 | bytes 12582912 | tf_op jit(solution)/shard_map/output/pallas_call | solution.py:64
  135.1 1.5 collective-permute-done.20
  136.9 1.1 collective-permute-done.17
  138.3 3.7 %collective-permute-start.21 = (bf16[256,256]{1,0:T(8,128)(2,1)S(1)}, bf16[256,256]{1,0:T(8,128)(2,1)S(1)}, u32[]{:S(2)}, u32[]{:S(2)}) collective-permute-start(bf16[256,256]{1,0:T(8,128)(2,1)S(1)} %get-tuple-element.198), channel_id=1, source_target_pairs={{0,8},{8,0},{1,9},{9,1},{2,10},{10,2},{3,11},{11,3},{4,12},{12,4},... | collective-permute-start | bytes 393224 | tf_op jit(solution)/shard_map/ppermute | solution.py:39
  142.5 3.0 %collective-permute-start.24 = (bf16[256,256]{1,0:T(8,128)(2,1)S(1)}, bf16[256,256]{1,0:T(8,128)(2,1)S(1)}, u32[]{:S(2)}, u32[]{:S(2)}) collective-permute-start(bf16[256,256]{1,0:T(8,128)(2,1)S(1)} %get-tuple-element.194), channel_id=1, source_target_pairs={{0,96},{32,0},{64,32},{96,64},{1,97},{33,1},{65,33},{97,65},{2,98}... | collective-permute-start | bytes 393224 | tf_op jit(solution)/shard_map/ppermute | solution.py:39
  147.7 1.1 collective-permute-done.24
  148.9 2.1 collective-permute-done.25
  151.0 1.7 collective-permute-done.26
  152.7 9.3 %reduce-scatter.2.cloned.1.call-done.gate_grad_ref = bf16[128,4096]{1,0:T(8,128)(2,1)} async-done(((bf16[1024,4096]{1,0:T(8,128)(2,1)}), bf16[128,4096]{1,0:T(8,128)(2,1)}) %reduce-scatter.2.cloned.1.call-update) | async-done | bytes 1048592 | tf_op jit(solution)/shard_map/reduce_scatter | solution.py:744
  162.0 3.0 %gate_back.1.grad_ref = bf16[128,4096]{1,0:T(8,128)(2,1)} custom-call(s32[8]{0:T(128)S(1)} %fusion.2.origin.place, bf16[128,4096]{1,0:T(8,128)(2,1)} %reduce-scatter.2.cloned.1.call-done.gate_grad_ref, bf16[128,4096]{1,0:T(8,128)(2,1)} %get-tuple-element.107.query_ref), custom_call_target="tpu_custom_call" | custom-call | flops 524288 | bytes 3145728 | tf_op jit(solution)/shard_map/gate_back/pallas_call | solution.py:64
  165.0 3.5 %collective-permute-start.27 = (bf16[128,4096]{1,0:T(8,128)(2,1)}, bf16[128,4096]{1,0:T(8,128)(2,1)S(1)}, u32[]{:S(2)}, u32[]{:S(2)}) collective-permute-start(bf16[128,4096]{1,0:T(8,128)(2,1)} %gate_back.1.grad_ref), channel_id=1, source_target_pairs={{1,0},{2,1},{3,2},{4,3},{5,4},{6,5},{7,6},{8,7},{9,8},{10,9},{11,1... | collective-permute-start | bytes 3145736 | tf_op jit(solution)/shard_map/ppermute | solution.py:27
  168.5 11.1 %long_grad.1 = (f32[256,128]{1,0:T(8,128)S(1)}, f32[8,4096]{1,0:T(8,128)S(1)}, bf16[128,4096]{1,0:T(8,128)(2,1)}) custom-call(s32[8]{0:T(128)S(1)} %fusion.2.origin.place, bf16[128,4096]{1,0:T(8,128)(2,1)} %copy-done.1, bf16[128,4096]{1,0:T(8,128)(2,1)} %get-tuple-element.104.cur_ref, bf16[128,4096]{1,0:T(8,128)(2,1)} %gate_back.1.grad_ref, ...), custom_call_target="tpu_custom_call" | custom-call | flops 2147483648 | bytes 7340032 | tf_op jit(solution)/shard_map/long_grad/pallas_call | solution.py:64
  179.6 2.7 %collective-permute-start.28 = (bf16[1024,256]{1,0:T(8,128)(2,1)S(1)}, bf16[1024,256]{1,0:T(8,128)(2,1)S(1)}, u32[]{:S(2)}, u32[]{:S(2)}) collective-permute-start(bf16[1024,256]{1,0:T(8,128)(2,1)S(1)} %copy-done.11), channel_id=1, source_target_pairs={{0,8},{8,0},{1,9},{9,1},{2,10},{10,2},{3,11},{11,3},{4,12},{12,4},... | collective-permute-start | bytes 1572872 | tf_op jit(solution)/shard_map/ppermute | solution.py:39
  182.5 11.4 %unmix.1 = (bf16[2,128,4096]{2,1,0:T(8,128)(2,1)}, f32[8,4096]{1,0:T(8,128)S(1)}, f32[8,4096]{1,0:T(8,128)S(1)}, bf16[3,16,4096]{2,1,0:T(8,128)(2,1)}) custom-call(f32[256,128]{1,0:T(8,128)S(1)} %convert_element_type.57.lines_ref, bf16[128,4096]{1,0:T(8,128)(2,1)} %gate_back.1.grad_ref, bf16[128,4096]{1,0:T(8,128)(2,1)S(1)} %collective-permute-done.27.next_ref, ...), custom_call_target="tpu_custom_call" | custom-call | flops 2147483648 | bytes 8388608 | tf_op jit(solution)/shard_map/unmix/pallas_call | solution.py:64
  193.9 1.3 collective-permute-done.28
  196.8 1.9 collective-permute-start.29
  198.9 4.0 %collective-permute-start.32 = (f32[16,8,128]{2,1,0:T(8,128)S(1)}, f32[16,8,128]{2,1,0:T(8,128)S(1)}, u32[]{:S(2)}, u32[]{:S(2)}) collective-permute-start(f32[16,8,128]{2,1,0:T(8,128)S(1)} %get-tuple-element.202), channel_id=1, source_target_pairs={{0,4},{2,6},{4,0},{6,2},{1,5},{3,7},{5,1},{7,3},{8,12},{10,14},{12... | collective-permute-start | bytes 196616 | tf_op jit(solution)/shard_map/ppermute | solution.py:39
  202.9 1.3 collective-permute-done.31
  204.2 2.4 collective-permute-done.32
  207.9 2.4 collective-permute-start.35
  210.3 1.2 collective-permute-start.36
  211.5 3.2 %short_adjoint.3.refs_0_ = bf16[128,12288]{1,0:T(8,128)(2,1)} custom-call(bf16[1,128,4096]{2,1,0:T(8,128)(2,1)} %bitcast.47, bf16[3,16,4096]{2,1,0:T(8,128)(2,1)S(1)} %collective-permute-done.29.rim_ref, f32[7,12288]{1,0:T(8,128)} %filter_ref.5), custom_call_target="tpu_custom_call" | custom-call | flops 7340032 | bytes 2097152 | tf_op jit(solution)/shard_map/short_adjoint/pallas_call | solution.py:64
  214.7 1.5 collective-permute-start.37
  216.4 2.2 collective-permute-start.39
  218.5 3.2 %short_adjoint.4.refs_0_ = bf16[128,12288]{1,0:T(8,128)(2,1)} custom-call(bf16[2,128,4096]{2,1,0:T(8,128)(2,1)} %get-tuple-element.162.grads_ref, bf16[3,16,4096]{2,1,0:T(8,128)(2,1)S(1)} %collective-permute-done.29.rim_ref, f32[7,12288]{1,0:T(8,128)} %filter_ref.5, bf16[128,12288]{1,0:T(8,128)(2,1)} %short_adjoint.3.refs_0_), custom_call_target="tpu_custom_call", output_to_operand_aliasing={{}: (3, {})} | custom-call | flops 7340032 | bytes 2097152 | tf_op jit(solution)/shard_map/short_adjoint/pallas_call | solution.py:64
  221.8 5.7 %collective-permute-start.40 = (f32[16,8,128]{2,1,0:T(8,128)S(1)}, f32[16,8,128]{2,1,0:T(8,128)S(1)}, u32[]{:S(2)}, u32[]{:S(2)}) collective-permute-start(f32[16,8,128]{2,1,0:T(8,128)S(1)} %add_add_fusion), channel_id=1, source_target_pairs={{0,1},{1,0},{2,3},{3,2},{4,5},{5,4},{6,7},{7,6},{8,9},{9,8},{10,11... | collective-permute-start | bytes 196616 | tf_op jit(solution)/shard_map/ppermute | solution.py:39
  228.5 2.8 %collective-permute-start.41 = (f32[32,8,128]{2,1,0:T(8,128)S(1)}, f32[32,8,128]{2,1,0:T(8,128)S(1)}, u32[]{:S(2)}, u32[]{:S(2)}) collective-permute-start(f32[32,8,128]{2,1,0:T(8,128)S(1)} %pad_maximum_fusion.3.refs_0_), channel_id=1, source_target_pairs={{0,6},{2,0},{4,2},{6,4},{1,7},{3,1},{5,3},{7,5},{8,14},{10,8},{12,... | collective-permute-start | bytes 393224 | tf_op jit(solution)/shard_map/ppermute | solution.py:39
  232.0 1.3 maximum_select_fusion
  233.3 3.2 %short_adjoint.5 = bf16[128,12288]{1,0:T(8,128)(2,1)} custom-call(bf16[2,128,4096]{2,1,0:T(8,128)(2,1)} %get-tuple-element.162.grads_ref, bf16[3,16,4096]{2,1,0:T(8,128)(2,1)S(1)} %collective-permute-done.29.rim_ref, f32[7,12288]{1,0:T(8,128)} %filter_ref.5, bf16[128,12288]{1,0:T(8,128)(2,1)} %short_adjoint.4.refs_0_), custom_call_target="tpu_custom_call", output_to_operand_aliasing={{}: (3, {})} | custom-call | flops 7340032 | bytes 2097152 | tf_op jit(solution)/shard_map/short_adjoint/pallas_call | solution.py:64
  237.5 3.2 %collective-permute-done.43.refs_3_ = f32[32,8,128]{2,1,0:T(8,128)S(1)} collective-permute-done((f32[32,8,128]{2,1,0:T(8,128)S(1)}, f32[32,8,128]{2,1,0:T(8,128)S(1)}, u32[]{:S(2)}, u32[]{:S(2)}) %collective-permute-start.43) | collective-permute-done | bytes 131104 | tf_op jit(solution)/shard_map/ppermute | solution.py:39
  240.7 1.5 collect.1
  (96 shorter events, 17.4 us)
Async XLA Ops:
  7.2 97.0 %all-gather.2.cloned.1.call-start = ((), (), s32[]{:S(2)}) async-start(), calls=%async_computation.1 | async-start | bytes 9437184 | tf_op jit(solution)/shard_map/all_gather | solution.py:737
  8.2 11.7 %collective-permute-start = (bf16[16,12288]{1,0:T(8,128)(2,1)S(1)}, bf16[16,12288]{1,0:T(8,128)(2,1)S(1)}, u32[]{:S(2)}, u32[]{:S(2)}) collective-permute-start(bf16[16,12288]{1,0:T(8,128)(2,1)S(1)} %slice_bitcast_fusion), channel_id=1, source_target_pairs={{0,1},{1,2},{2,3},{3,4},{4,5},{5,6},{6,7},{7,8},{8,9},{9,10},{10,1... | collective-permute-start | bytes 1179656 | tf_op jit(solution)/shard_map/ppermute | solution.py:27
  19.9 3.3 %copy-start = (bf16[16,12288]{1,0:T(8,128)(2,1)}, bf16[16,12288]{1,0:T(8,128)(2,1)S(1)}, u32[]{:S(2)}) copy-start(bf16[16,12288]{1,0:T(8,128)(2,1)S(1)} %collective-permute-done.refs_3_.refs_4_.refs_5_.rim_ref.key_rim_ref.value_rim_ref) | copy-start | bytes 1179652
  19.9 5.6 %copy-start.9 = (bf16[512,256]{1,0:T(8,128)(2,1)S(1)}, bf16[512,256]{1,0:T(8,128)(2,1)}, u32[]{:S(2)}) copy-start(bf16[512,256]{1,0:T(8,128)(2,1)} %param.8) | copy-start | bytes 786436
  19.9 10.7 %copy-start.10 = (bf16[256,128]{1,0:T(8,128)(2,1)S(1)}, bf16[256,128]{1,0:T(8,128)(2,1)}, u32[]{:S(2)}) copy-start(bf16[256,128]{1,0:T(8,128)(2,1)} %param.7) | copy-start | bytes 196612
  23.2 14.4 %collective-permute-start.1 = (bf16[128,4096]{1,0:T(8,128)(2,1)}, bf16[128,4096]{1,0:T(8,128)(2,1)S(1)}, u32[]{:S(2)}, u32[]{:S(2)}) collective-permute-start(bf16[128,4096]{1,0:T(8,128)(2,1)} %get-tuple-element.104.cur_ref), channel_id=1, source_target_pairs={{0,1},{1,2},{2,3},{3,4},{4,5},{5,6},{6,7},{7,8},{8,9},{9,10},{10,1... | collective-permute-start | bytes 3145736 | tf_op jit(solution)/shard_map/ppermute | solution.py:27
  25.5 6.4 %collective-permute-start.2 = (bf16[256,256]{1,0:T(8,128)(2,1)S(1)}, bf16[256,256]{1,0:T(8,128)(2,1)S(1)}, u32[]{:S(2)}, u32[]{:S(2)}) collective-permute-start(bf16[256,256]{1,0:T(8,128)(2,1)S(1)} %slice.56), channel_id=1, source_target_pairs={{0,32},{32,64},{64,96},{96,0},{1,33},{33,65},{65,97},{97,1},{2,34}... | collective-permute-start | bytes 393224 | tf_op jit(solution)/shard_map/ppermute | solution.py:39
  26.9 8.9 %collective-permute-start.3 = (bf16[256,256]{1,0:T(8,128)(2,1)S(1)}, bf16[256,256]{1,0:T(8,128)(2,1)S(1)}, u32[]{:S(2)}, u32[]{:S(2)}) collective-permute-start(bf16[256,256]{1,0:T(8,128)(2,1)S(1)} %slice.56), channel_id=1, source_target_pairs={{0,64},{32,96},{64,0},{96,32},{1,65},{33,97},{65,1},{97,33},{2,66}... | collective-permute-start | bytes 393224 | tf_op jit(solution)/shard_map/ppermute | solution.py:39
  29.5 6.3 %collective-permute-start.4 = (bf16[256,256]{1,0:T(8,128)(2,1)S(1)}, bf16[256,256]{1,0:T(8,128)(2,1)S(1)}, u32[]{:S(2)}, u32[]{:S(2)}) collective-permute-start(bf16[256,256]{1,0:T(8,128)(2,1)S(1)} %slice.56), channel_id=1, source_target_pairs={{0,96},{32,0},{64,32},{96,64},{1,97},{33,1},{65,33},{97,65},{2,98}... | collective-permute-start | bytes 393224 | tf_op jit(solution)/shard_map/ppermute | solution.py:39
  37.5 9.8 %copy-start.1 = (bf16[128,4096]{1,0:T(8,128)(2,1)}, bf16[128,4096]{1,0:T(8,128)(2,1)S(1)}, u32[]{:S(2)}) copy-start(bf16[128,4096]{1,0:T(8,128)(2,1)S(1)} %collective-permute-done.1.prev_ref) | copy-start | bytes 3145732
  37.5 19.7 %copy-start.5 = (bf16[1,2048,256]{2,1,0:T(8,128)(2,1)S(1)}, bf16[1,2048,256]{2,1,0:T(8,128)(2,1)}, u32[]{:S(2)}) copy-start(bf16[1,2048,256]{2,1,0:T(8,128)(2,1)} %param.9) | copy-start | bytes 3145732
  47.3 114.6 %reduce-scatter.2.cloned.1.call-start = ((), (), s32[]{:S(2)}) async-start(), calls=%async_computation.2 | async-start | bytes 9437184 | tf_op jit(solution)/shard_map/reduce_scatter | solution.py:744
  47.4 5.4 %collective-permute-start.5 = (bf16[256,256]{1,0:T(8,128)(2,1)S(1)}, bf16[256,256]{1,0:T(8,128)(2,1)S(1)}, u32[]{:S(2)}, u32[]{:S(2)}) collective-permute-start(bf16[256,256]{1,0:T(8,128)(2,1)S(1)} %slice.57), channel_id=1, source_target_pairs={{0,8},{8,0},{1,9},{9,1},{2,10},{10,2},{3,11},{11,3},{4,12},{12,4},... | collective-permute-start | bytes 393224 | tf_op jit(solution)/shard_map/ppermute | solution.py:39
  50.2 4.2 %collective-permute-start.6 = (bf16[256,256]{1,0:T(8,128)(2,1)S(1)}, bf16[256,256]{1,0:T(8,128)(2,1)}, u32[]{:S(2)}, u32[]{:S(2)}) collective-permute-start(bf16[256,256]{1,0:T(8,128)(2,1)S(1)} %slice.57), channel_id=1, source_target_pairs={{0,16},{16,0},{1,17},{17,1},{2,18},{18,2},{3,19},{19,3},{4,20},{20... | collective-permute-start | bytes 393224 | tf_op jit(solution)/shard_map/ppermute | solution.py:39
  50.5 5.1 %collective-permute-start.7 = (bf16[256,256]{1,0:T(8,128)(2,1)S(1)}, bf16[256,256]{1,0:T(8,128)(2,1)}, u32[]{:S(2)}, u32[]{:S(2)}) collective-permute-start(bf16[256,256]{1,0:T(8,128)(2,1)S(1)} %slice.57), channel_id=1, source_target_pairs={{0,24},{8,16},{16,8},{24,0},{1,25},{9,17},{17,9},{25,1},{2,26},{10... | collective-permute-start | bytes 393224 | tf_op jit(solution)/shard_map/ppermute | solution.py:39
  55.7 12.2 %collective-permute-start.12 = (bf16[4,256,256]{2,1,0:T(8,128)(2,1)S(1)}, bf16[4,256,256]{2,1,0:T(8,128)(2,1)S(1)}, u32[]{:S(2)}, u32[]{:S(2)}) collective-permute-start(bf16[4,256,256]{2,1,0:T(8,128)(2,1)S(1)} %pad_maximum_fusion.2.refs_5_.refs_4_), channel_id=1, source_target_pairs={{0,8},{8,0},{1,9},{9,1},{2,10},{10,2},{3,11},{11,3},{4,12},{12,4},... | collective-permute-start | bytes 1572872 | tf_op jit(solution)/shard_map/ppermute | solution.py:39
  57.5 16.1 %collective-permute-start.8 = (bf16[1024,256]{0,1:T(8,128)(2,1)S(1)}, bf16[1024,256]{0,1:T(8,128)(2,1)S(1)}, u32[]{:S(2)}, u32[]{:S(2)}) collective-permute-start(bf16[1024,256]{0,1:T(8,128)(2,1)S(1)} %bitcast.51), channel_id=1, source_target_pairs={{0,8},{8,0},{1,9},{9,1},{2,10},{10,2},{3,11},{11,3},{4,12},{12,4},... | collective-permute-start | bytes 1572872 | tf_op jit(solution)/shard_map/ppermute | solution.py:39
  59.2 19.4 %collective-permute-start.13 = (bf16[4,256,256]{2,1,0:T(8,128)(2,1)S(1)}, bf16[4,256,256]{2,1,0:T(8,128)(2,1)}, u32[]{:S(2)}, u32[]{:S(2)}) collective-permute-start(bf16[4,256,256]{2,1,0:T(8,128)(2,1)S(1)} %pad_maximum_fusion.2.refs_5_.refs_4_), channel_id=1, source_target_pairs={{0,16},{16,0},{1,17},{17,1},{2,18},{18,2},{3,19},{19,3},{4,20},{20... | collective-permute-start | bytes 1572872 | tf_op jit(solution)/shard_map/ppermute | solution.py:39
  59.2 20.8 %collective-permute-start.14 = (bf16[4,256,256]{2,1,0:T(8,128)(2,1)S(1)}, bf16[4,256,256]{2,1,0:T(8,128)(2,1)}, u32[]{:S(2)}, u32[]{:S(2)}) collective-permute-start(bf16[4,256,256]{2,1,0:T(8,128)(2,1)S(1)} %pad_maximum_fusion.2.refs_5_.refs_4_), channel_id=1, source_target_pairs={{0,24},{8,16},{16,8},{24,0},{1,25},{9,17},{17,9},{25,1},{2,26},{10... | collective-permute-start | bytes 1572872 | tf_op jit(solution)/shard_map/ppermute | solution.py:39
  61.9 18.1 %collective-permute-start.10 = (bf16[4,256,256]{2,1,0:T(8,128)(2,1)S(1)}, bf16[4,256,256]{2,1,0:T(8,128)(2,1)}, u32[]{:S(2)}, u32[]{:S(2)}) collective-permute-start(bf16[4,256,256]{2,1,0:T(8,128)(2,1)S(1)} %pad_maximum_fusion.1.refs_1_.refs_0_), channel_id=1, source_target_pairs={{0,64},{32,96},{64,0},{96,32},{1,65},{33,97},{65,1},{97,33},{2,66}... | collective-permute-start | bytes 1572872 | tf_op jit(solution)/shard_map/ppermute | solution.py:39
  68.0 7.1 %copy-start.2 = (bf16[4,256,256]{2,1,0:T(8,128)(2,1)}, bf16[4,256,256]{2,1,0:T(8,128)(2,1)S(1)}, u32[]{:S(2)}) copy-start(bf16[4,256,256]{2,1,0:T(8,128)(2,1)S(1)} %collective-permute-done.12.refs_6_.refs_5_) | copy-start | bytes 1572868
  68.0 12.0 %collective-permute-start.11 = (bf16[4,256,256]{2,1,0:T(8,128)(2,1)S(1)}, bf16[4,256,256]{2,1,0:T(8,128)(2,1)}, u32[]{:S(2)}, u32[]{:S(2)}) collective-permute-start(bf16[4,256,256]{2,1,0:T(8,128)(2,1)S(1)} %pad_maximum_fusion.1.refs_1_.refs_0_), channel_id=1, source_target_pairs={{0,96},{32,0},{64,32},{96,64},{1,97},{33,1},{65,33},{97,65},{2,98}... | collective-permute-start | bytes 1572872 | tf_op jit(solution)/shard_map/ppermute | solution.py:39
  73.6 9.7 %collective-permute-start.9 = (bf16[4,256,256]{2,1,0:T(8,128)(2,1)S(1)}, bf16[4,256,256]{2,1,0:T(8,128)(2,1)}, u32[]{:S(2)}, u32[]{:S(2)}) collective-permute-start(bf16[4,256,256]{2,1,0:T(8,128)(2,1)S(1)} %pad_maximum_fusion.1.refs_1_.refs_0_), channel_id=1, source_target_pairs={{0,32},{32,64},{64,96},{96,0},{1,33},{33,65},{65,97},{97,1},{2,34}... | collective-permute-start | bytes 1572872 | tf_op jit(solution)/shard_map/ppermute | solution.py:39
  83.3 1.1 copy-start.3
  104.2 21.0 %copy-start.4 = (bf16[4,256,256]{2,1,0:T(8,128)(2,1)S(1)}, bf16[4,256,256]{2,1,0:T(8,128)(2,1)}, u32[]{:S(2)}) copy-start(bf16[4,256,256]{2,1,0:T(8,128)(2,1)} %copy-done.2) | copy-start | bytes 1572868
  114.1 9.9 %collective-permute-start.18 = (bf16[4,256,256]{2,1,0:T(8,128)(2,1)}, bf16[4,256,256]{2,1,0:T(8,128)(2,1)S(1)}, u32[]{:S(2)}, u32[]{:S(2)}) collective-permute-start(bf16[4,256,256]{2,1,0:T(8,128)(2,1)} %get-tuple-element.133), channel_id=1, source_target_pairs={{0,8},{8,0},{1,9},{9,1},{2,10},{10,2},{3,11},{11,3},{4,12},{12,4},... | collective-permute-start | bytes 1572872 | tf_op jit(solution)/shard_map/ppermute | solution.py:39
  116.8 18.3 %collective-permute-start.19 = (bf16[4,256,256]{2,1,0:T(8,128)(2,1)}, bf16[4,256,256]{2,1,0:T(8,128)(2,1)S(1)}, u32[]{:S(2)}, u32[]{:S(2)}) collective-permute-start(bf16[4,256,256]{2,1,0:T(8,128)(2,1)} %get-tuple-element.134), channel_id=1, source_target_pairs={{0,16},{16,0},{1,17},{17,1},{2,18},{18,2},{3,19},{19,3},{4,20},{20... | collective-permute-start | bytes 1572872 | tf_op jit(solution)/shard_map/ppermute | solution.py:39
  117.1 19.5 %collective-permute-start.20 = (bf16[4,256,256]{2,1,0:T(8,128)(2,1)}, bf16[4,256,256]{2,1,0:T(8,128)(2,1)S(1)}, u32[]{:S(2)}, u32[]{:S(2)}) collective-permute-start(bf16[4,256,256]{2,1,0:T(8,128)(2,1)} %get-tuple-element.135), channel_id=1, source_target_pairs={{0,24},{8,16},{16,8},{24,0},{1,25},{9,17},{17,9},{25,1},{2,26},{10... | collective-permute-start | bytes 1572872 | tf_op jit(solution)/shard_map/ppermute | solution.py:39
  117.7 19.2 %collective-permute-start.15 = (bf16[4,256,256]{2,1,0:T(8,128)(2,1)}, bf16[4,256,256]{2,1,0:T(8,128)(2,1)S(1)}, u32[]{:S(2)}, u32[]{:S(2)}) collective-permute-start(bf16[4,256,256]{2,1,0:T(8,128)(2,1)} %get-tuple-element.129), channel_id=1, source_target_pairs={{0,96},{32,0},{64,32},{96,64},{1,97},{33,1},{65,33},{97,65},{2,98}... | collective-permute-start | bytes 1572872 | tf_op jit(solution)/shard_map/ppermute | solution.py:39
  120.2 16.7 %collective-permute-start.16 = (bf16[4,256,256]{2,1,0:T(8,128)(2,1)}, bf16[4,256,256]{2,1,0:T(8,128)(2,1)S(1)}, u32[]{:S(2)}, u32[]{:S(2)}) collective-permute-start(bf16[4,256,256]{2,1,0:T(8,128)(2,1)} %get-tuple-element.130), channel_id=1, source_target_pairs={{0,64},{32,96},{64,0},{96,32},{1,65},{33,97},{65,1},{97,33},{2,66}... | collective-permute-start | bytes 1572872 | tf_op jit(solution)/shard_map/ppermute | solution.py:39
  124.0 12.6 %copy-start.8 = (bf16[4,256,256]{2,1,0:T(8,128)(2,1)S(1)}, bf16[4,256,256]{2,1,0:T(8,128)(2,1)}, u32[]{:S(2)}) copy-start(bf16[4,256,256]{2,1,0:T(8,128)(2,1)} %get-tuple-element.132) | copy-start | bytes 1572868
  124.0 14.0 %collective-permute-start.17 = (bf16[4,256,256]{2,1,0:T(8,128)(2,1)}, bf16[4,256,256]{2,1,0:T(8,128)(2,1)S(1)}, u32[]{:S(2)}, u32[]{:S(2)}) collective-permute-start(bf16[4,256,256]{2,1,0:T(8,128)(2,1)} %get-tuple-element.131), channel_id=1, source_target_pairs={{0,32},{32,64},{64,96},{96,0},{1,33},{33,65},{65,97},{97,1},{2,34}... | collective-permute-start | bytes 1572872 | tf_op jit(solution)/shard_map/ppermute | solution.py:39
  135.1 2.9 %copy-start.7 = (bf16[4,256,256]{2,1,0:T(8,128)(2,1)S(1)}, bf16[4,256,256]{2,1,0:T(8,128)(2,1)}, u32[]{:S(2)}) copy-start(bf16[4,256,256]{2,1,0:T(8,128)(2,1)} %get-tuple-element.128) | copy-start | bytes 1572868
  138.3 7.9 %collective-permute-start.21 = (bf16[256,256]{1,0:T(8,128)(2,1)S(1)}, bf16[256,256]{1,0:T(8,128)(2,1)S(1)}, u32[]{:S(2)}, u32[]{:S(2)}) collective-permute-start(bf16[256,256]{1,0:T(8,128)(2,1)S(1)} %get-tuple-element.198), channel_id=1, source_target_pairs={{0,8},{8,0},{1,9},{9,1},{2,10},{10,2},{3,11},{11,3},{4,12},{12,4},... | collective-permute-start | bytes 393224 | tf_op jit(solution)/shard_map/ppermute | solution.py:39
  142.0 4.7 %collective-permute-start.22 = (bf16[256,256]{1,0:T(8,128)(2,1)S(1)}, bf16[256,256]{1,0:T(8,128)(2,1)S(1)}, u32[]{:S(2)}, u32[]{:S(2)}) collective-permute-start(bf16[256,256]{1,0:T(8,128)(2,1)S(1)} %get-tuple-element.197), channel_id=1, source_target_pairs={{0,16},{16,0},{1,17},{17,1},{2,18},{18,2},{3,19},{19,3},{4,20},{20... | collective-permute-start | bytes 393224 | tf_op jit(solution)/shard_map/ppermute | solution.py:39
  142.3 5.4 %collective-permute-start.23 = (bf16[256,256]{1,0:T(8,128)(2,1)S(1)}, bf16[256,256]{1,0:T(8,128)(2,1)S(1)}, u32[]{:S(2)}, u32[]{:S(2)}) collective-permute-start(bf16[256,256]{1,0:T(8,128)(2,1)S(1)} %get-tuple-element.196), channel_id=1, source_target_pairs={{0,24},{8,16},{16,8},{24,0},{1,25},{9,17},{17,9},{25,1},{2,26},{10... | collective-permute-start | bytes 393224 | tf_op jit(solution)/shard_map/ppermute | solution.py:39
  142.5 6.3 %collective-permute-start.24 = (bf16[256,256]{1,0:T(8,128)(2,1)S(1)}, bf16[256,256]{1,0:T(8,128)(2,1)S(1)}, u32[]{:S(2)}, u32[]{:S(2)}) collective-permute-start(bf16[256,256]{1,0:T(8,128)(2,1)S(1)} %get-tuple-element.194), channel_id=1, source_target_pairs={{0,96},{32,0},{64,32},{96,64},{1,97},{33,1},{65,33},{97,65},{2,98}... | collective-permute-start | bytes 393224 | tf_op jit(solution)/shard_map/ppermute | solution.py:39
  145.5 5.4 %collective-permute-start.25 = (bf16[256,256]{1,0:T(8,128)(2,1)S(1)}, bf16[256,256]{1,0:T(8,128)(2,1)S(1)}, u32[]{:S(2)}, u32[]{:S(2)}) collective-permute-start(bf16[256,256]{1,0:T(8,128)(2,1)S(1)} %get-tuple-element.193), channel_id=1, source_target_pairs={{0,64},{32,96},{64,0},{96,32},{1,65},{33,97},{65,1},{97,33},{2,66}... | collective-permute-start | bytes 393224 | tf_op jit(solution)/shard_map/ppermute | solution.py:39
  146.2 6.4 %collective-permute-start.26 = (bf16[256,256]{1,0:T(8,128)(2,1)S(1)}, bf16[256,256]{1,0:T(8,128)(2,1)S(1)}, u32[]{:S(2)}, u32[]{:S(2)}) collective-permute-start(bf16[256,256]{1,0:T(8,128)(2,1)S(1)} %get-tuple-element.192), channel_id=1, source_target_pairs={{0,32},{32,64},{64,96},{96,0},{1,33},{33,65},{65,97},{97,1},{2,34}... | collective-permute-start | bytes 393224 | tf_op jit(solution)/shard_map/ppermute | solution.py:39
  165.0 17.5 %collective-permute-start.27 = (bf16[128,4096]{1,0:T(8,128)(2,1)}, bf16[128,4096]{1,0:T(8,128)(2,1)S(1)}, u32[]{:S(2)}, u32[]{:S(2)}) collective-permute-start(bf16[128,4096]{1,0:T(8,128)(2,1)} %gate_back.1.grad_ref), channel_id=1, source_target_pairs={{1,0},{2,1},{3,2},{4,3},{5,4},{6,5},{7,6},{8,7},{9,8},{10,9},{11,1... | collective-permute-start | bytes 3145736 | tf_op jit(solution)/shard_map/ppermute | solution.py:27
  168.5 11.1 %copy-start.11 = (bf16[1024,256]{1,0:T(8,128)(2,1)S(1)}, bf16[1024,256]{1,0:T(8,128)(2,1)}, u32[]{:S(2)}) copy-start(bf16[1024,256]{1,0:T(8,128)(2,1)} %get-tuple-element.160) | copy-start | bytes 1572868
  179.6 15.5 %collective-permute-start.28 = (bf16[1024,256]{1,0:T(8,128)(2,1)S(1)}, bf16[1024,256]{1,0:T(8,128)(2,1)S(1)}, u32[]{:S(2)}, u32[]{:S(2)}) collective-permute-start(bf16[1024,256]{1,0:T(8,128)(2,1)S(1)} %copy-done.11), channel_id=1, source_target_pairs={{0,8},{8,0},{1,9},{9,1},{2,10},{10,2},{3,11},{11,3},{4,12},{12,4},... | collective-permute-start | bytes 1572872 | tf_op jit(solution)/shard_map/ppermute | solution.py:39
  195.8 2.9 %collective-permute-start.30 = (f32[64,8,128]{2,1,0:T(8,128)S(1)}, f32[64,8,128]{2,1,0:T(8,128)S(1)}, u32[]{:S(2)}, u32[]{:S(2)}) collective-permute-start(f32[64,8,128]{2,1,0:T(8,128)S(1)} %get-tuple-element.169), channel_id=1, source_target_pairs={{0,1},{1,0},{2,3},{3,2},{4,5},{5,4},{6,7},{7,6},{8,9},{9,8},{10,11... | collective-permute-start | bytes 786440 | tf_op jit(solution)/shard_map/ppermute | solution.py:39
  196.8 14.7 %collective-permute-start.29 = (bf16[3,16,4096]{2,1,0:T(8,128)(2,1)}, bf16[3,16,4096]{2,1,0:T(8,128)(2,1)S(1)}, u32[]{:S(2)}, u32[]{:S(2)}) collective-permute-start(bf16[3,16,4096]{2,1,0:T(8,128)(2,1)} %get-tuple-element.163), channel_id=1, source_target_pairs={{1,0},{2,1},{3,2},{4,3},{5,4},{6,5},{7,6},{8,7},{9,8},{10,9},{11,1... | collective-permute-start | bytes 1179656 | tf_op jit(solution)/shard_map/ppermute | solution.py:27
  198.8 5.4 %collective-permute-start.31 = (f32[16,8,128]{2,1,0:T(8,128)S(1)}, f32[16,8,128]{2,1,0:T(8,128)S(1)}, u32[]{:S(2)}, u32[]{:S(2)}) collective-permute-start(f32[16,8,128]{2,1,0:T(8,128)S(1)} %get-tuple-element.200), channel_id=1, source_target_pairs={{0,2},{2,4},{4,6},{6,0},{1,3},{3,5},{5,7},{7,1},{8,10},{10,12},{12... | collective-permute-start | bytes 196616 | tf_op jit(solution)/shard_map/ppermute | solution.py:39
  198.9 7.7 %collective-permute-start.32 = (f32[16,8,128]{2,1,0:T(8,128)S(1)}, f32[16,8,128]{2,1,0:T(8,128)S(1)}, u32[]{:S(2)}, u32[]{:S(2)}) collective-permute-start(f32[16,8,128]{2,1,0:T(8,128)S(1)} %get-tuple-element.202), channel_id=1, source_target_pairs={{0,4},{2,6},{4,0},{6,2},{1,5},{3,7},{5,1},{7,3},{8,12},{10,14},{12... | collective-permute-start | bytes 196616 | tf_op jit(solution)/shard_map/ppermute | solution.py:39
  202.9 4.1 %collective-permute-start.33 = (f32[16,8,128]{2,1,0:T(8,128)S(1)}, f32[16,8,128]{2,1,0:T(8,128)S(1)}, u32[]{:S(2)}, u32[]{:S(2)}) collective-permute-start(f32[16,8,128]{2,1,0:T(8,128)S(1)} %get-tuple-element.201), channel_id=1, source_target_pairs={{0,6},{2,0},{4,2},{6,4},{1,7},{3,1},{5,3},{7,5},{8,14},{10,8},{12,... | collective-permute-start | bytes 196616 | tf_op jit(solution)/shard_map/ppermute | solution.py:39
  207.0 7.7 %collective-permute-start.34 = (f32[16,8,128]{2,1,0:T(8,128)S(1)}, f32[16,8,128]{2,1,0:T(8,128)S(1)}, u32[]{:S(2)}, u32[]{:S(2)}) collective-permute-start(f32[16,8,128]{2,1,0:T(8,128)S(1)} %fusion.1), channel_id=1, source_target_pairs={{0,32},{32,64},{64,96},{96,0},{1,33},{33,65},{65,97},{97,1},{2,34}... | collective-permute-start | bytes 196616 | tf_op jit(solution)/shard_map/ppermute | solution.py:39
  207.9 6.8 %collective-permute-start.35 = (f32[16,8,128]{2,1,0:T(8,128)S(1)}, f32[16,8,128]{2,1,0:T(8,128)S(1)}, u32[]{:S(2)}, u32[]{:S(2)}) collective-permute-start(f32[16,8,128]{2,1,0:T(8,128)S(1)} %fusion.1), channel_id=1, source_target_pairs={{0,64},{32,96},{64,0},{96,32},{1,65},{33,97},{65,1},{97,33},{2,66}... | collective-permute-start | bytes 196616 | tf_op jit(solution)/shard_map/ppermute | solution.py:39
  210.3 4.4 %collective-permute-start.36 = (f32[16,8,128]{2,1,0:T(8,128)S(1)}, f32[16,8,128]{2,1,0:T(8,128)S(1)}, u32[]{:S(2)}, u32[]{:S(2)}) collective-permute-start(f32[16,8,128]{2,1,0:T(8,128)S(1)} %fusion.1), channel_id=1, source_target_pairs={{0,96},{32,0},{64,32},{96,64},{1,97},{33,1},{65,33},{97,65},{2,98}... | collective-permute-start | bytes 196616 | tf_op jit(solution)/shard_map/ppermute | solution.py:39
  214.7 7.0 %collective-permute-start.37 = (f32[16,8,128]{2,1,0:T(8,128)S(1)}, f32[16,8,128]{2,1,0:T(8,128)S(1)}, u32[]{:S(2)}, u32[]{:S(2)}) collective-permute-start(f32[16,8,128]{2,1,0:T(8,128)S(1)} %add_add_fusion.1), channel_id=1, source_target_pairs={{0,8},{8,0},{1,9},{9,1},{2,10},{10,2},{3,11},{11,3},{4,12},{12,4},... | collective-permute-start | bytes 196616 | tf_op jit(solution)/shard_map/ppermute | solution.py:39
  216.2 5.6 %collective-permute-start.38 = (f32[16,8,128]{2,1,0:T(8,128)S(1)}, f32[16,8,128]{2,1,0:T(8,128)S(1)}, u32[]{:S(2)}, u32[]{:S(2)}) collective-permute-start(f32[16,8,128]{2,1,0:T(8,128)S(1)} %add_add_fusion.1), channel_id=1, source_target_pairs={{0,16},{16,0},{1,17},{17,1},{2,18},{18,2},{3,19},{19,3},{4,20},{20... | collective-permute-start | bytes 196616 | tf_op jit(solution)/shard_map/ppermute | solution.py:39
  216.4 5.4 %collective-permute-start.39 = (f32[16,8,128]{2,1,0:T(8,128)S(1)}, f32[16,8,128]{2,1,0:T(8,128)S(1)}, u32[]{:S(2)}, u32[]{:S(2)}) collective-permute-start(f32[16,8,128]{2,1,0:T(8,128)S(1)} %add_add_fusion.1), channel_id=1, source_target_pairs={{0,24},{8,16},{16,8},{24,0},{1,25},{9,17},{17,9},{25,1},{2,26},{10... | collective-permute-start | bytes 196616 | tf_op jit(solution)/shard_map/ppermute | solution.py:39
  218.5 13.5 %copy-start.6 = (bf16[1024,256]{1,0:T(8,128)(2,1)S(1)}, bf16[1024,256]{1,0:T(8,128)(2,1)}, u32[]{:S(2)}) copy-start(bf16[1024,256]{1,0:T(8,128)(2,1)} %get-tuple-element.126) | copy-start | bytes 1572868
  221.8 6.7 %collective-permute-start.40 = (f32[16,8,128]{2,1,0:T(8,128)S(1)}, f32[16,8,128]{2,1,0:T(8,128)S(1)}, u32[]{:S(2)}, u32[]{:S(2)}) collective-permute-start(f32[16,8,128]{2,1,0:T(8,128)S(1)} %add_add_fusion), channel_id=1, source_target_pairs={{0,1},{1,0},{2,3},{3,2},{4,5},{5,4},{6,7},{7,6},{8,9},{9,8},{10,11... | collective-permute-start | bytes 196616 | tf_op jit(solution)/shard_map/ppermute | solution.py:39
  228.5 8.2 %collective-permute-start.41 = (f32[32,8,128]{2,1,0:T(8,128)S(1)}, f32[32,8,128]{2,1,0:T(8,128)S(1)}, u32[]{:S(2)}, u32[]{:S(2)}) collective-permute-start(f32[32,8,128]{2,1,0:T(8,128)S(1)} %pad_maximum_fusion.3.refs_0_), channel_id=1, source_target_pairs={{0,6},{2,0},{4,2},{6,4},{1,7},{3,1},{5,3},{7,5},{8,14},{10,8},{12,... | collective-permute-start | bytes 393224 | tf_op jit(solution)/shard_map/ppermute | solution.py:39
  231.4 6.1 %collective-permute-start.42 = (f32[32,8,128]{2,1,0:T(8,128)S(1)}, f32[32,8,128]{2,1,0:T(8,128)S(1)}, u32[]{:S(2)}, u32[]{:S(2)}) collective-permute-start(f32[32,8,128]{2,1,0:T(8,128)S(1)} %pad_maximum_fusion.3.refs_0_), channel_id=1, source_target_pairs={{0,4},{2,6},{4,0},{6,2},{1,5},{3,7},{5,1},{7,3},{8,12},{10,14},{12... | collective-permute-start | bytes 393224 | tf_op jit(solution)/shard_map/ppermute | solution.py:39
  231.4 9.2 %collective-permute-start.43 = (f32[32,8,128]{2,1,0:T(8,128)S(1)}, f32[32,8,128]{2,1,0:T(8,128)S(1)}, u32[]{:S(2)}, u32[]{:S(2)}) collective-permute-start(f32[32,8,128]{2,1,0:T(8,128)S(1)} %pad_maximum_fusion.3.refs_0_), channel_id=1, source_target_pairs={{0,2},{2,4},{4,6},{6,0},{1,3},{3,5},{5,7},{7,1},{8,10},{10,12},{12... | collective-permute-start | bytes 393224 | tf_op jit(solution)/shard_map/ppermute | solution.py:39
Sparse Core Ops, SparseCore 0:
  47.4 56.6 all-gather.1
  106.6 55.3 reduce-scatter.1

commit v16 on v14

--- a/solution.py
+++ b/solution.py
@@ -570,7 +570,7 @@
     rows, depth = cotangents.shape
     ny = len(tops)
     channels = 4 * ny * tops[0].shape[1]
-    height = rows // 2
+    height = rows // 4
     return hbm_call(
         functools.partial(gate_matmul_kernel, ny),
         loose=range(5 + ny),

time: 243 us -> 243 us (level)
  transfers between devices with their start and end apart: 46 -> 46, of which waited for: 27 -> 26; matrix products, arithmetic and copies ran while one was open for 3% -> 3% of each run, Pallas kernels for 28% -> 28%
where the time goes in v16:
time: 243 us; the launch traced here: 242 us
  Pallas kernels  84.5 us (35%)
  starting transfers between devices  71.6 us (29%)
  waiting for transfers between devices  62.5 us (26%)
  between operations  14.4 us (6%)
  local copies, waits for them, and re-layouts  5.12 us (2%)
  other arithmetic  4.4 us (2%)
    pallas_call x12, Pallas kernels, run(): return call(*held)  82.3 us
    ppermute x40, starting transfers between devices, move(): return lax.ppermute(x, axes, pairs)  58.6 us
    ppermute x40, waiting for transfers between devices, move(): return lax.ppermute(x, axes, pairs)  37.7 us
    ppermute x4, starting transfers between devices, along(): return lax.ppermute(x, LINE, pairs)  12.9 us
    all_gather x1, waiting for transfers between devices, shards(): all_rows = lax.all_gather(gated, ('z', 'c'), axis=0, tiled=True)  11.5 us
    reduce_scatter x1, waiting for transfers between devices, shards(): lax.psum_scatter(partial, ('z', 'c'), scatter_dimension=0, tiled=True)  11.1 us
  transfers between devices with their start and end apart: 46, of which 26 were waited for; matrix products, arithmetic and copies ran while one was open for 3% of the time, Pallas kernels for 28%

profile of v16, /device:TPU:1, one launch (start us, length us, event | category | flops | bytes accessed | tf_op | source)
XLA Modules:
  0.0 242.5 jit_solution(14617169434813986067)
XLA Ops:
  8.2 4.9 %collective-permute-start = (bf16[8,12288]{1,0:T(8,128)(2,1)S(1)}, bf16[8,12288]{1,0:T(8,128)(2,1)S(1)}, u32[]{:S(2)}, u32[]{:S(2)}) collective-permute-start(bf16[8,12288]{1,0:T(8,128)(2,1)S(1)} %slice_bitcast_fusion), channel_id=1, source_target_pairs={{0,1},{1,2},{2,3},{3,4},{4,5},{5,6},{6,7},{7,8},{8,9},{9,10},{10,1... | collective-permute-start | bytes 589832 | tf_op jit(solution)/shard_map/ppermute | solution.py:27
  13.1 6.7 %features.1 = (bf16[128,4096]{1,0:T(8,128)(2,1)}, bf16[128,4096]{1,0:T(8,128)(2,1)}, bf16[128,4096]{1,0:T(8,128)(2,1)}, bf16[128,4096]{1,0:T(8,128)(2,1)}) custom-call(bf16[128,12288]{1,0:T(8,128)(2,1)} %bitcast.37, bf16[128,12288]{1,0:T(8,128)(2,1)} %bitcast.38, bf16[128,12288]{1,0:T(8,128)(2,1)} %bitcast.39, f32[7,12288]{1,0:T(8,128)} %filter_ref.5, ...), custom_call_target="tpu_custom_call" | custom-call | bytes 1572864 | tf_op jit(solution)/shard_map/features/pallas_call | solution.py:64
  19.9 2.6 %first_rows.1 = (bf16[128,4096]{1,0:T(8,128)(2,1)}, bf16[128,4096]{1,0:T(8,128)(2,1)}, bf16[128,4096]{1,0:T(8,128)(2,1)}, bf16[128,4096]{1,0:T(8,128)(2,1)}) custom-call(bf16[128,12288]{1,0:T(8,128)(2,1)} %bitcast.40, bf16[128,12288]{1,0:T(8,128)(2,1)} %bitcast.41, ...), custom_call_target="tpu_custom_call", output_to_operand_aliasing={{0}: (9, {}), {1}: (10, {}), {2}: (11, {}), {3}: (12, {})} | custom-call | bytes 196608 | tf_op jit(solution)/shard_map/first_rows/pallas_call | solution.py:64
  22.4 1.9 collective-permute-start.1
  24.4 1.4 collective-permute-start.2
  25.7 2.6 %collective-permute-start.3 = (bf16[256,256]{1,0:T(8,128)(2,1)S(1)}, bf16[256,256]{1,0:T(8,128)(2,1)S(1)}, u32[]{:S(2)}, u32[]{:S(2)}) collective-permute-start(bf16[256,256]{1,0:T(8,128)(2,1)S(1)} %slice.56), channel_id=1, source_target_pairs={{0,64},{32,96},{64,0},{96,32},{1,65},{33,97},{65,1},{97,33},{2,66}... | collective-permute-start | bytes 393224 | tf_op jit(solution)/shard_map/ppermute | solution.py:39
  28.4 1.1 collective-permute-start.4
  30.3 3.9 %collective-permute-done.3 = bf16[256,256]{1,0:T(8,128)(2,1)S(1)} collective-permute-done((bf16[256,256]{1,0:T(8,128)(2,1)S(1)}, bf16[256,256]{1,0:T(8,128)(2,1)S(1)}, u32[]{:S(2)}, u32[]{:S(2)}) %collective-permute-start.3) | collective-permute-done | bytes 131104 | tf_op jit(solution)/shard_map/ppermute | solution.py:39
  34.2 2.2 collective-permute-done.1.prev_ref
  36.4 9.7 %mix.1 = (bf16[128,4096]{1,0:T(8,128)(2,1)}, bf16[128,4096]{1,0:T(8,128)(2,1)}) custom-call(f32[256,128]{1,0:T(8,128)S(1)} %convert_element_type.57.lines_ref, bf16[128,4096]{1,0:T(8,128)(2,1)S(1)} %collective-permute-done.1.prev_ref, bf16[128,4096]{1,0:T(8,128)(2,1)} %get-tuple-element.104.cur_ref, bf16[128,4096]{1,0:T(8,128)(2,1)} %get-tuple-element.107.query_ref), custom_call_target="tpu_custom_call" | custom-call | bytes 1048576 | tf_op jit(solution)/shard_map/mix/pallas_call | solution.py:64
  46.3 2.8 %collective-permute-start.5 = (bf16[256,256]{1,0:T(8,128)(2,1)S(1)}, bf16[256,256]{1,0:T(8,128)(2,1)S(1)}, u32[]{:S(2)}, u32[]{:S(2)}) collective-permute-start(bf16[256,256]{1,0:T(8,128)(2,1)S(1)} %slice.57), channel_id=1, source_target_pairs={{0,8},{8,0},{1,9},{9,1},{2,10},{10,2},{3,11},{11,3},{4,12},{12,4},... | collective-permute-start | bytes 393224 | tf_op jit(solution)/shard_map/ppermute | solution.py:39
  49.9 1.7 collective-permute-done.5
  51.7 1.6 collective-permute-done.6
  53.2 1.3 collective-permute-done.7
  54.6 1.5 collective-permute-start.12
  56.3 1.7 collective-permute-start.8
  58.0 1.7 collective-permute-start.14
  59.7 1.1 pad_maximum_fusion.1.refs_1_.refs_0_
  60.8 3.0 %collective-permute-start.10 = (bf16[4,256,256]{2,1,0:T(8,128)(2,1)S(1)}, bf16[4,256,256]{2,1,0:T(8,128)(2,1)}, u32[]{:S(2)}, u32[]{:S(2)}) collective-permute-start(bf16[4,256,256]{2,1,0:T(8,128)(2,1)S(1)} %pad_maximum_fusion.1.refs_1_.refs_0_), channel_id=1, source_target_pairs={{0,64},{32,96},{64,0},{96,32},{1,65},{33,97},{65,1},{97,33},{2,66}... | collective-permute-start | bytes 1572872 | tf_op jit(solution)/shard_map/ppermute | solution.py:39
  63.7 1.4 collective-permute-done.12.refs_6_.refs_5_
  65.1 2.7 %collective-permute-start.11 = (bf16[4,256,256]{2,1,0:T(8,128)(2,1)S(1)}, bf16[4,256,256]{2,1,0:T(8,128)(2,1)}, u32[]{:S(2)}, u32[]{:S(2)}) collective-permute-start(bf16[4,256,256]{2,1,0:T(8,128)(2,1)S(1)} %pad_maximum_fusion.1.refs_1_.refs_0_), channel_id=1, source_target_pairs={{0,96},{32,0},{64,32},{96,64},{1,97},{33,1},{65,33},{97,65},{2,98}... | collective-permute-start | bytes 1572872 | tf_op jit(solution)/shard_map/ppermute | solution.py:39
  67.8 2.9 %collective-permute-done.8 = bf16[1024,256]{0,1:T(8,128)(2,1)S(1)} collective-permute-done((bf16[1024,256]{0,1:T(8,128)(2,1)S(1)}, bf16[1024,256]{0,1:T(8,128)(2,1)S(1)}, u32[]{:S(2)}, u32[]{:S(2)}) %collective-permute-start.8) | collective-permute-done | bytes 524320 | tf_op jit(solution)/shard_map/ppermute | solution.py:39
  70.7 1.3 collective-permute-start.9
  72.2 1.2 fusion.11
  73.4 1.5 copy.18.refs_0_
  74.9 2.4 collective-permute-done.13.refs_7_.refs_6_
  78.0 2.4 collective-permute-done.9.refs_2_.refs_1_
  81.5 8.4 %gate_matmul.1 = bf16[1024,4096]{1,0:T(8,128)(2,1)} custom-call(bf16[1024,512]{1,0:T(8,128)(2,1)S(1)} %copy.18.refs_0_, bf16[4,256,256]{2,1,0:T(8,128)(2,1)S(1)} %pad_maximum_fusion.1.refs_1_.refs_0_, bf16[4,256,256]{2,1,0:T(8,128)(2,1)} %collective-permute-done.9.refs_2_.refs_1_, bf16[4,256,256]{2,1,0:T(8,128)(2,1)} %collective-permute-done.10.refs_3_.refs_2_, ...), custom_call_target="tpu_custom_call" | custom-call | flops 4294967296 | bytes 12582912 | tf_op jit(solution)/shard_map/gate_matmul/pallas_call | solution.py:64
  89.8 11.5 %all-gather.2.cloned.1.call-done.rows_ref = bf16[1024,4096]{1,0:T(8,128)(2,1)} async-done(((bf16[128,4096]{1,0:T(8,128)(2,1)}), bf16[1024,4096]{1,0:T(8,128)(2,1)}) %all-gather.2.cloned.1.call-update) | async-done | bytes 8388624 | tf_op jit(solution)/shard_map/all_gather | solution.py:737
  101.3 9.9 %weight_grad.1 = (bf16[4,256,256]{2,1,0:T(8,128)(2,1)}, bf16[4,256,256]{2,1,0:T(8,128)(2,1)}, bf16[4,256,256]{2,1,0:T(8,128)(2,1)}, bf16[4,256,256]{2,1,0:T(8,12...) custom-call(s32[8]{0:T(128)S(1)} %fusion.2.origin.place, ...), custom_call_target="tpu_custom_call" | custom-call | flops 4294967296 | bytes 12582912 | tf_op jit(solution)/shard_map/weight_grad/pallas_call | solution.py:64
  111.3 2.7 %collective-permute-start.18 = (bf16[4,256,256]{2,1,0:T(8,128)(2,1)}, bf16[4,256,256]{2,1,0:T(8,128)(2,1)S(1)}, u32[]{:S(2)}, u32[]{:S(2)}) collective-permute-start(bf16[4,256,256]{2,1,0:T(8,128)(2,1)} %get-tuple-element.133), channel_id=1, source_target_pairs={{0,8},{8,0},{1,9},{9,1},{2,10},{10,2},{3,11},{11,3},{4,12},{12,4},... | collective-permute-start | bytes 1572872 | tf_op jit(solution)/shard_map/ppermute | solution.py:39
  114.8 2.5 %collective-permute-start.15 = (bf16[4,256,256]{2,1,0:T(8,128)(2,1)}, bf16[4,256,256]{2,1,0:T(8,128)(2,1)S(1)}, u32[]{:S(2)}, u32[]{:S(2)}) collective-permute-start(bf16[4,256,256]{2,1,0:T(8,128)(2,1)} %get-tuple-element.129), channel_id=1, source_target_pairs={{0,96},{32,0},{64,32},{96,64},{1,97},{33,1},{65,33},{97,65},{2,98}... | collective-permute-start | bytes 1572872 | tf_op jit(solution)/shard_map/ppermute | solution.py:39
  117.8 3.3 %collective-permute-done.18 = bf16[4,256,256]{2,1,0:T(8,128)(2,1)S(1)} collective-permute-done((bf16[4,256,256]{2,1,0:T(8,128)(2,1)}, bf16[4,256,256]{2,1,0:T(8,128)(2,1)S(1)}, u32[]{:S(2)}, u32[]{:S(2)}) %collective-permute-start.18) | collective-permute-done | bytes 524320 | tf_op jit(solution)/shard_map/ppermute | solution.py:39
  121.1 1.2 collective-permute-start.17
  122.3 9.9 %output.1 = (bf16[1024,256]{1,0:T(8,128)(2,1)}, bf16[1024,256]{1,0:T(8,128)(2,1)}) custom-call(s32[8]{0:T(128)S(1)} %fusion.2.origin.place, bf16[1024,4096]{1,0:T(8,128)(2,1)} %all-gather.2.cloned.1.call-done.rows_ref, bf16[4,256,256]{2,1,0:T(8,128)(2,1)S(1)} %pad_maximum_fusion.1.refs_1_.refs_0_, ...), custom_call_target="tpu_custom_call" | custom-call | flops 4294967296 | bytes 12582912 | tf_op jit(solution)/shard_map/output/pallas_call | solution.py:64
  133.4 1.2 collective-permute-done.17
  134.9 3.1 %collective-permute-start.21 = (bf16[256,256]{1,0:T(8,128)(2,1)S(1)}, bf16[256,256]{1,0:T(8,128)(2,1)S(1)}, u32[]{:S(2)}, u32[]{:S(2)}) collective-permute-start(bf16[256,256]{1,0:T(8,128)(2,1)S(1)} %get-tuple-element.198), channel_id=1, source_target_pairs={{0,8},{8,0},{1,9},{9,1},{2,10},{10,2},{3,11},{11,3},{4,12},{12,4},... | collective-permute-start | bytes 393224 | tf_op jit(solution)/shard_map/ppermute | solution.py:39
  139.1 2.7 %collective-permute-start.24 = (bf16[256,256]{1,0:T(8,128)(2,1)S(1)}, bf16[256,256]{1,0:T(8,128)(2,1)S(1)}, u32[]{:S(2)}, u32[]{:S(2)}) collective-permute-start(bf16[256,256]{1,0:T(8,128)(2,1)S(1)} %get-tuple-element.194), channel_id=1, source_target_pairs={{0,96},{32,0},{64,32},{96,64},{1,97},{33,1},{65,33},{97,65},{2,98}... | collective-permute-start | bytes 393224 | tf_op jit(solution)/shard_map/ppermute | solution.py:39
  143.9 1.2 collective-permute-done.24
  145.1 2.1 collective-permute-done.25
  147.2 1.7 collective-permute-done.26
  148.9 11.1 %reduce-scatter.2.cloned.1.call-done.gate_grad_ref = bf16[128,4096]{1,0:T(8,128)(2,1)} async-done(((bf16[1024,4096]{1,0:T(8,128)(2,1)}), bf16[128,4096]{1,0:T(8,128)(2,1)}) %reduce-scatter.2.cloned.1.call-update) | async-done | bytes 1048592 | tf_op jit(solution)/shard_map/reduce_scatter | solution.py:744
  160.0 3.0 %gate_back.1.grad_ref = bf16[128,4096]{1,0:T(8,128)(2,1)} custom-call(s32[8]{0:T(128)S(1)} %fusion.2.origin.place, bf16[128,4096]{1,0:T(8,128)(2,1)} %reduce-scatter.2.cloned.1.call-done.gate_grad_ref, bf16[128,4096]{1,0:T(8,128)(2,1)} %get-tuple-element.107.query_ref), custom_call_target="tpu_custom_call" | custom-call | flops 524288 | bytes 3145728 | tf_op jit(solution)/shard_map/gate_back/pallas_call | solution.py:64
  162.9 3.3 %collective-permute-start.27 = (bf16[128,4096]{1,0:T(8,128)(2,1)}, bf16[128,4096]{1,0:T(8,128)(2,1)S(1)}, u32[]{:S(2)}, u32[]{:S(2)}) collective-permute-start(bf16[128,4096]{1,0:T(8,128)(2,1)} %gate_back.1.grad_ref), channel_id=1, source_target_pairs={{1,0},{2,1},{3,2},{4,3},{5,4},{6,5},{7,6},{8,7},{9,8},{10,9},{11,1... | collective-permute-start | bytes 3145736 | tf_op jit(solution)/shard_map/ppermute | solution.py:27
  166.3 11.1 %long_grad.1 = (f32[256,128]{1,0:T(8,128)S(1)}, f32[8,4096]{1,0:T(8,128)S(1)}, bf16[128,4096]{1,0:T(8,128)(2,1)}) custom-call(s32[8]{0:T(128)S(1)} %fusion.2.origin.place, bf16[128,4096]{1,0:T(8,128)(2,1)} %copy-done.1, bf16[128,4096]{1,0:T(8,128)(2,1)} %get-tuple-element.104.cur_ref, bf16[128,4096]{1,0:T(8,128)(2,1)} %gate_back.1.grad_ref, ...), custom_call_target="tpu_custom_call" | custom-call | flops 2147483648 | bytes 7340032 | tf_op jit(solution)/shard_map/long_grad/pallas_call | solution.py:64
  177.4 2.7 %collective-permute-start.28 = (bf16[1024,256]{1,0:T(8,128)(2,1)S(1)}, bf16[1024,256]{1,0:T(8,128)(2,1)S(1)}, u32[]{:S(2)}, u32[]{:S(2)}) collective-permute-start(bf16[1024,256]{1,0:T(8,128)(2,1)S(1)} %copy-done.11), channel_id=1, source_target_pairs={{0,8},{8,0},{1,9},{9,1},{2,10},{10,2},{3,11},{11,3},{4,12},{12,4},... | collective-permute-start | bytes 1572872 | tf_op jit(solution)/shard_map/ppermute | solution.py:39
  180.3 11.4 %unmix.1 = (bf16[2,128,4096]{2,1,0:T(8,128)(2,1)}, f32[8,4096]{1,0:T(8,128)S(1)}, f32[8,4096]{1,0:T(8,128)S(1)}, bf16[3,8,4096]{2,1,0:T(8,128)(2,1)S(1)}) custom-call(f32[256,128]{1,0:T(8,128)S(1)} %convert_element_type.57.lines_ref, bf16[128,4096]{1,0:T(8,128)(2,1)} %gate_back.1.grad_ref, bf16[128,4096]{1,0:T(8,128)(2,1)S(1)} %collective-permute-done.27.next_ref, ...), custom_call_target="tpu_custom_call" | custom-call | flops 2147483648 | bytes 8388608 | tf_op jit(solution)/shard_map/unmix/pallas_call | solution.py:64
  191.7 1.3 collective-permute-done.28
  193.6 1.2 collective-permute-start.30
  194.8 1.2 collective-permute-done.30
  196.3 4.1 %collective-permute-start.32 = (f32[16,8,128]{2,1,0:T(8,128)S(1)}, f32[16,8,128]{2,1,0:T(8,128)S(1)}, u32[]{:S(2)}, u32[]{:S(2)}) collective-permute-start(f32[16,8,128]{2,1,0:T(8,128)S(1)} %get-tuple-element.202), channel_id=1, source_target_pairs={{0,4},{2,6},{4,0},{6,2},{1,5},{3,7},{5,1},{7,3},{8,12},{10,14},{12... | collective-permute-start | bytes 196616 | tf_op jit(solution)/shard_map/ppermute | solution.py:39
  200.4 2.8 %collective-permute-start.29 = (bf16[3,8,4096]{2,1,0:T(8,128)(2,1)S(1)}, bf16[3,8,4096]{2,1,0:T(8,128)(2,1)S(1)}, u32[]{:S(2)}, u32[]{:S(2)}) collective-permute-start(bf16[3,8,4096]{2,1,0:T(8,128)(2,1)S(1)} %get-tuple-element.163), channel_id=1, source_target_pairs={{1,0},{2,1},{3,2},{4,3},{5,4},{6,5},{7,6},{8,7},{9,8},{10,9},{11,1... | collective-permute-start | bytes 589832 | tf_op jit(solution)/shard_map/ppermute | solution.py:27
  204.9 2.5 %collective-permute-start.35 = (f32[16,8,128]{2,1,0:T(8,128)S(1)}, f32[16,8,128]{2,1,0:T(8,128)S(1)}, u32[]{:S(2)}, u32[]{:S(2)}) collective-permute-start(f32[16,8,128]{2,1,0:T(8,128)S(1)} %fusion.1), channel_id=1, source_target_pairs={{0,64},{32,96},{64,0},{96,32},{1,65},{33,97},{65,1},{97,33},{2,66}... | collective-permute-start | bytes 196616 | tf_op jit(solution)/shard_map/ppermute | solution.py:39
  207.4 1.2 collective-permute-start.36
  208.5 3.2 %short_adjoint.3.refs_0_ = bf16[128,12288]{1,0:T(8,128)(2,1)} custom-call(bf16[1,128,4096]{2,1,0:T(8,128)(2,1)} %bitcast.47, bf16[3,8,4096]{2,1,0:T(8,128)(2,1)S(1)} %collective-permute-done.29.rim_ref, f32[7,12288]{1,0:T(8,128)} %filter_ref.5), custom_call_target="tpu_custom_call" | custom-call | flops 7340032 | bytes 2097152 | tf_op jit(solution)/shard_map/short_adjoint/pallas_call | solution.py:64
  212.7 1.4 collective-permute-start.38
  214.1 1.4 collective-permute-start.39
  215.5 3.2 %short_adjoint.4.refs_0_ = bf16[128,12288]{1,0:T(8,128)(2,1)} custom-call(bf16[2,128,4096]{2,1,0:T(8,128)(2,1)} %get-tuple-element.162.grads_ref, bf16[3,8,4096]{2,1,0:T(8,128)(2,1)S(1)} %collective-permute-done.29.rim_ref, f32[7,12288]{1,0:T(8,128)} %filter_ref.5, bf16[128,12288]{1,0:T(8,128)(2,1)} %short_adjoint.3.refs_0_), custom_call_target="tpu_custom_call", output_to_operand_aliasing={{}: (3, {})} | custom-call | flops 7340032 | bytes 2097152 | tf_op jit(solution)/shard_map/short_adjoint/pallas_call | solution.py:64
  218.8 3.1 %collective-permute-start.40 = (f32[16,8,128]{2,1,0:T(8,128)S(1)}, f32[16,8,128]{2,1,0:T(8,128)S(1)}, u32[]{:S(2)}, u32[]{:S(2)}) collective-permute-start(f32[16,8,128]{2,1,0:T(8,128)S(1)} %add_add_fusion), channel_id=1, source_target_pairs={{0,1},{1,0},{2,3},{3,2},{4,5},{5,4},{6,7},{7,6},{8,9},{9,8},{10,11... | collective-permute-start | bytes 196616 | tf_op jit(solution)/shard_map/ppermute | solution.py:39
  222.9 1.8 collective-permute-start.41
  225.4 1.3 maximum_select_fusion
  226.7 3.2 %short_adjoint.5 = bf16[128,12288]{1,0:T(8,128)(2,1)} custom-call(bf16[2,128,4096]{2,1,0:T(8,128)(2,1)} %get-tuple-element.162.grads_ref, bf16[3,8,4096]{2,1,0:T(8,128)(2,1)S(1)} %collective-permute-done.29.rim_ref, f32[7,12288]{1,0:T(8,128)} %filter_ref.5, bf16[128,12288]{1,0:T(8,128)(2,1)} %short_adjoint.4.refs_0_), custom_call_target="tpu_custom_call", output_to_operand_aliasing={{}: (3, {})} | custom-call | flops 7340032 | bytes 2097152 | tf_op jit(solution)/shard_map/short_adjoint/pallas_call | solution.py:64
  230.8 3.3 %collective-permute-done.43.refs_3_ = f32[32,8,128]{2,1,0:T(8,128)S(1)} collective-permute-done((f32[32,8,128]{2,1,0:T(8,128)S(1)}, f32[32,8,128]{2,1,0:T(8,128)S(1)}, u32[]{:S(2)}, u32[]{:S(2)}) %collective-permute-start.43) | collective-permute-done | bytes 131104 | tf_op jit(solution)/shard_map/ppermute | solution.py:39
  234.2 1.5 collect.1
  (96 shorter events, 17.9 us)
Async XLA Ops:
  7.2 94.1 %all-gather.2.cloned.1.call-start = ((), (), s32[]{:S(2)}) async-start(), calls=%async_computation.1 | async-start | bytes 9437184 | tf_op jit(solution)/shard_map/all_gather | solution.py:737
  8.2 11.7 %collective-permute-start = (bf16[8,12288]{1,0:T(8,128)(2,1)S(1)}, bf16[8,12288]{1,0:T(8,128)(2,1)S(1)}, u32[]{:S(2)}, u32[]{:S(2)}) collective-permute-start(bf16[8,12288]{1,0:T(8,128)(2,1)S(1)} %slice_bitcast_fusion), channel_id=1, source_target_pairs={{0,1},{1,2},{2,3},{3,4},{4,5},{5,6},{6,7},{7,8},{8,9},{9,10},{10,1... | collective-permute-start | bytes 589832 | tf_op jit(solution)/shard_map/ppermute | solution.py:27
  19.8 2.6 %copy-start = (bf16[8,12288]{1,0:T(8,128)(2,1)}, bf16[8,12288]{1,0:T(8,128)(2,1)S(1)}, u32[]{:S(2)}) copy-start(bf16[8,12288]{1,0:T(8,128)(2,1)S(1)} %collective-permute-done.refs_3_.refs_4_.refs_5_.rim_ref.key_rim_ref.value_rim_ref) | copy-start | bytes 589828
  19.8 4.5 %copy-start.9 = (bf16[512,256]{1,0:T(8,128)(2,1)S(1)}, bf16[512,256]{1,0:T(8,128)(2,1)}, u32[]{:S(2)}) copy-start(bf16[512,256]{1,0:T(8,128)(2,1)} %param.8) | copy-start | bytes 786436
  19.9 9.6 %copy-start.10 = (bf16[256,128]{1,0:T(8,128)(2,1)S(1)}, bf16[256,128]{1,0:T(8,128)(2,1)}, u32[]{:S(2)}) copy-start(bf16[256,128]{1,0:T(8,128)(2,1)} %param.7) | copy-start | bytes 196612
  22.4 14.0 %collective-permute-start.1 = (bf16[128,4096]{1,0:T(8,128)(2,1)}, bf16[128,4096]{1,0:T(8,128)(2,1)S(1)}, u32[]{:S(2)}, u32[]{:S(2)}) collective-permute-start(bf16[128,4096]{1,0:T(8,128)(2,1)} %get-tuple-element.104.cur_ref), channel_id=1, source_target_pairs={{0,1},{1,2},{2,3},{3,4},{4,5},{5,6},{6,7},{7,8},{8,9},{9,10},{10,1... | collective-permute-start | bytes 3145736 | tf_op jit(solution)/shard_map/ppermute | solution.py:27
  24.4 5.9 %collective-permute-start.2 = (bf16[256,256]{1,0:T(8,128)(2,1)S(1)}, bf16[256,256]{1,0:T(8,128)(2,1)S(1)}, u32[]{:S(2)}, u32[]{:S(2)}) collective-permute-start(bf16[256,256]{1,0:T(8,128)(2,1)S(1)} %slice.56), channel_id=1, source_target_pairs={{0,32},{32,64},{64,96},{96,0},{1,33},{33,65},{65,97},{97,1},{2,34}... | collective-permute-start | bytes 393224 | tf_op jit(solution)/shard_map/ppermute | solution.py:39
  25.7 8.5 %collective-permute-start.3 = (bf16[256,256]{1,0:T(8,128)(2,1)S(1)}, bf16[256,256]{1,0:T(8,128)(2,1)S(1)}, u32[]{:S(2)}, u32[]{:S(2)}) collective-permute-start(bf16[256,256]{1,0:T(8,128)(2,1)S(1)} %slice.56), channel_id=1, source_target_pairs={{0,64},{32,96},{64,0},{96,32},{1,65},{33,97},{65,1},{97,33},{2,66}... | collective-permute-start | bytes 393224 | tf_op jit(solution)/shard_map/ppermute | solution.py:39
  28.4 5.8 %collective-permute-start.4 = (bf16[256,256]{1,0:T(8,128)(2,1)S(1)}, bf16[256,256]{1,0:T(8,128)(2,1)S(1)}, u32[]{:S(2)}, u32[]{:S(2)}) collective-permute-start(bf16[256,256]{1,0:T(8,128)(2,1)S(1)} %slice.56), channel_id=1, source_target_pairs={{0,96},{32,0},{64,32},{96,64},{1,97},{33,1},{65,33},{97,65},{2,98}... | collective-permute-start | bytes 393224 | tf_op jit(solution)/shard_map/ppermute | solution.py:39
  36.4 9.8 %copy-start.1 = (bf16[128,4096]{1,0:T(8,128)(2,1)}, bf16[128,4096]{1,0:T(8,128)(2,1)S(1)}, u32[]{:S(2)}) copy-start(bf16[128,4096]{1,0:T(8,128)(2,1)S(1)} %collective-permute-done.1.prev_ref) | copy-start | bytes 3145732
  36.4 19.7 %copy-start.5 = (bf16[1,2048,256]{2,1,0:T(8,128)(2,1)S(1)}, bf16[1,2048,256]{2,1,0:T(8,128)(2,1)}, u32[]{:S(2)}) copy-start(bf16[1,2048,256]{2,1,0:T(8,128)(2,1)} %param.9) | copy-start | bytes 3145732
  46.2 113.8 %reduce-scatter.2.cloned.1.call-start = ((), (), s32[]{:S(2)}) async-start(), calls=%async_computation.2 | async-start | bytes 9437184 | tf_op jit(solution)/shard_map/reduce_scatter | solution.py:744
  46.3 5.4 %collective-permute-start.5 = (bf16[256,256]{1,0:T(8,128)(2,1)S(1)}, bf16[256,256]{1,0:T(8,128)(2,1)S(1)}, u32[]{:S(2)}, u32[]{:S(2)}) collective-permute-start(bf16[256,256]{1,0:T(8,128)(2,1)S(1)} %slice.57), channel_id=1, source_target_pairs={{0,8},{8,0},{1,9},{9,1},{2,10},{10,2},{3,11},{11,3},{4,12},{12,4},... | collective-permute-start | bytes 393224 | tf_op jit(solution)/shard_map/ppermute | solution.py:39
  49.1 4.2 %collective-permute-start.6 = (bf16[256,256]{1,0:T(8,128)(2,1)S(1)}, bf16[256,256]{1,0:T(8,128)(2,1)}, u32[]{:S(2)}, u32[]{:S(2)}) collective-permute-start(bf16[256,256]{1,0:T(8,128)(2,1)S(1)} %slice.57), channel_id=1, source_target_pairs={{0,16},{16,0},{1,17},{17,1},{2,18},{18,2},{3,19},{19,3},{4,20},{20... | collective-permute-start | bytes 393224 | tf_op jit(solution)/shard_map/ppermute | solution.py:39
  49.4 5.1 %collective-permute-start.7 = (bf16[256,256]{1,0:T(8,128)(2,1)S(1)}, bf16[256,256]{1,0:T(8,128)(2,1)}, u32[]{:S(2)}, u32[]{:S(2)}) collective-permute-start(bf16[256,256]{1,0:T(8,128)(2,1)S(1)} %slice.57), channel_id=1, source_target_pairs={{0,24},{8,16},{16,8},{24,0},{1,25},{9,17},{17,9},{25,1},{2,26},{10... | collective-permute-start | bytes 393224 | tf_op jit(solution)/shard_map/ppermute | solution.py:39
  54.6 10.5 %collective-permute-start.12 = (bf16[4,256,256]{2,1,0:T(8,128)(2,1)S(1)}, bf16[4,256,256]{2,1,0:T(8,128)(2,1)S(1)}, u32[]{:S(2)}, u32[]{:S(2)}) collective-permute-start(bf16[4,256,256]{2,1,0:T(8,128)(2,1)S(1)} %pad_maximum_fusion.2.refs_5_.refs_4_), channel_id=1, source_target_pairs={{0,8},{8,0},{1,9},{9,1},{2,10},{10,2},{3,11},{11,3},{4,12},{12,4},... | collective-permute-start | bytes 1572872 | tf_op jit(solution)/shard_map/ppermute | solution.py:39
  56.3 14.4 %collective-permute-start.8 = (bf16[1024,256]{0,1:T(8,128)(2,1)S(1)}, bf16[1024,256]{0,1:T(8,128)(2,1)S(1)}, u32[]{:S(2)}, u32[]{:S(2)}) collective-permute-start(bf16[1024,256]{0,1:T(8,128)(2,1)S(1)} %bitcast.51), channel_id=1, source_target_pairs={{0,8},{8,0},{1,9},{9,1},{2,10},{10,2},{3,11},{11,3},{4,12},{12,4},... | collective-permute-start | bytes 1572872 | tf_op jit(solution)/shard_map/ppermute | solution.py:39
  58.0 19.3 %collective-permute-start.13 = (bf16[4,256,256]{2,1,0:T(8,128)(2,1)S(1)}, bf16[4,256,256]{2,1,0:T(8,128)(2,1)}, u32[]{:S(2)}, u32[]{:S(2)}) collective-permute-start(bf16[4,256,256]{2,1,0:T(8,128)(2,1)S(1)} %pad_maximum_fusion.2.refs_5_.refs_4_), channel_id=1, source_target_pairs={{0,16},{16,0},{1,17},{17,1},{2,18},{18,2},{3,19},{19,3},{4,20},{20... | collective-permute-start | bytes 1572872 | tf_op jit(solution)/shard_map/ppermute | solution.py:39
  58.0 20.0 %collective-permute-start.14 = (bf16[4,256,256]{2,1,0:T(8,128)(2,1)S(1)}, bf16[4,256,256]{2,1,0:T(8,128)(2,1)}, u32[]{:S(2)}, u32[]{:S(2)}) collective-permute-start(bf16[4,256,256]{2,1,0:T(8,128)(2,1)S(1)} %pad_maximum_fusion.2.refs_5_.refs_4_), channel_id=1, source_target_pairs={{0,24},{8,16},{16,8},{24,0},{1,25},{9,17},{17,9},{25,1},{2,26},{10... | collective-permute-start | bytes 1572872 | tf_op jit(solution)/shard_map/ppermute | solution.py:39
  60.8 17.3 %collective-permute-start.10 = (bf16[4,256,256]{2,1,0:T(8,128)(2,1)S(1)}, bf16[4,256,256]{2,1,0:T(8,128)(2,1)}, u32[]{:S(2)}, u32[]{:S(2)}) collective-permute-start(bf16[4,256,256]{2,1,0:T(8,128)(2,1)S(1)} %pad_maximum_fusion.1.refs_1_.refs_0_), channel_id=1, source_target_pairs={{0,64},{32,96},{64,0},{96,32},{1,65},{33,97},{65,1},{97,33},{2,66}... | collective-permute-start | bytes 1572872 | tf_op jit(solution)/shard_map/ppermute | solution.py:39
  65.1 7.1 %copy-start.2 = (bf16[4,256,256]{2,1,0:T(8,128)(2,1)}, bf16[4,256,256]{2,1,0:T(8,128)(2,1)S(1)}, u32[]{:S(2)}) copy-start(bf16[4,256,256]{2,1,0:T(8,128)(2,1)S(1)} %collective-permute-done.12.refs_6_.refs_5_) | copy-start | bytes 1572868
  65.1 12.9 %collective-permute-start.11 = (bf16[4,256,256]{2,1,0:T(8,128)(2,1)S(1)}, bf16[4,256,256]{2,1,0:T(8,128)(2,1)}, u32[]{:S(2)}, u32[]{:S(2)}) collective-permute-start(bf16[4,256,256]{2,1,0:T(8,128)(2,1)S(1)} %pad_maximum_fusion.1.refs_1_.refs_0_), channel_id=1, source_target_pairs={{0,96},{32,0},{64,32},{96,64},{1,97},{33,1},{65,33},{97,65},{2,98}... | collective-permute-start | bytes 1572872 | tf_op jit(solution)/shard_map/ppermute | solution.py:39
  70.7 9.7 %collective-permute-start.9 = (bf16[4,256,256]{2,1,0:T(8,128)(2,1)S(1)}, bf16[4,256,256]{2,1,0:T(8,128)(2,1)}, u32[]{:S(2)}, u32[]{:S(2)}) collective-permute-start(bf16[4,256,256]{2,1,0:T(8,128)(2,1)S(1)} %pad_maximum_fusion.1.refs_1_.refs_0_), channel_id=1, source_target_pairs={{0,32},{32,64},{64,96},{96,0},{1,33},{33,65},{65,97},{97,1},{2,34}... | collective-permute-start | bytes 1572872 | tf_op jit(solution)/shard_map/ppermute | solution.py:39
  80.4 1.1 copy-start.3
  101.3 21.0 %copy-start.4 = (bf16[4,256,256]{2,1,0:T(8,128)(2,1)S(1)}, bf16[4,256,256]{2,1,0:T(8,128)(2,1)}, u32[]{:S(2)}) copy-start(bf16[4,256,256]{2,1,0:T(8,128)(2,1)} %copy-done.2) | copy-start | bytes 1572868
  111.3 9.9 %collective-permute-start.18 = (bf16[4,256,256]{2,1,0:T(8,128)(2,1)}, bf16[4,256,256]{2,1,0:T(8,128)(2,1)S(1)}, u32[]{:S(2)}, u32[]{:S(2)}) collective-permute-start(bf16[4,256,256]{2,1,0:T(8,128)(2,1)} %get-tuple-element.133), channel_id=1, source_target_pairs={{0,8},{8,0},{1,9},{9,1},{2,10},{10,2},{3,11},{11,3},{4,12},{12,4},... | collective-permute-start | bytes 1572872 | tf_op jit(solution)/shard_map/ppermute | solution.py:39
  114.0 18.3 %collective-permute-start.19 = (bf16[4,256,256]{2,1,0:T(8,128)(2,1)}, bf16[4,256,256]{2,1,0:T(8,128)(2,1)S(1)}, u32[]{:S(2)}, u32[]{:S(2)}) collective-permute-start(bf16[4,256,256]{2,1,0:T(8,128)(2,1)} %get-tuple-element.134), channel_id=1, source_target_pairs={{0,16},{16,0},{1,17},{17,1},{2,18},{18,2},{3,19},{19,3},{4,20},{20... | collective-permute-start | bytes 1572872 | tf_op jit(solution)/shard_map/ppermute | solution.py:39
  114.2 18.8 %collective-permute-start.20 = (bf16[4,256,256]{2,1,0:T(8,128)(2,1)}, bf16[4,256,256]{2,1,0:T(8,128)(2,1)S(1)}, u32[]{:S(2)}, u32[]{:S(2)}) collective-permute-start(bf16[4,256,256]{2,1,0:T(8,128)(2,1)} %get-tuple-element.135), channel_id=1, source_target_pairs={{0,24},{8,16},{16,8},{24,0},{1,25},{9,17},{17,9},{25,1},{2,26},{10... | collective-permute-start | bytes 1572872 | tf_op jit(solution)/shard_map/ppermute | solution.py:39
  114.8 18.5 %collective-permute-start.15 = (bf16[4,256,256]{2,1,0:T(8,128)(2,1)}, bf16[4,256,256]{2,1,0:T(8,128)(2,1)S(1)}, u32[]{:S(2)}, u32[]{:S(2)}) collective-permute-start(bf16[4,256,256]{2,1,0:T(8,128)(2,1)} %get-tuple-element.129), channel_id=1, source_target_pairs={{0,96},{32,0},{64,32},{96,64},{1,97},{33,1},{65,33},{97,65},{2,98}... | collective-permute-start | bytes 1572872 | tf_op jit(solution)/shard_map/ppermute | solution.py:39
  117.3 16.1 %collective-permute-start.16 = (bf16[4,256,256]{2,1,0:T(8,128)(2,1)}, bf16[4,256,256]{2,1,0:T(8,128)(2,1)S(1)}, u32[]{:S(2)}, u32[]{:S(2)}) collective-permute-start(bf16[4,256,256]{2,1,0:T(8,128)(2,1)} %get-tuple-element.130), channel_id=1, source_target_pairs={{0,64},{32,96},{64,0},{96,32},{1,65},{33,97},{65,1},{97,33},{2,66}... | collective-permute-start | bytes 1572872 | tf_op jit(solution)/shard_map/ppermute | solution.py:39
  121.1 12.0 %copy-start.8 = (bf16[4,256,256]{2,1,0:T(8,128)(2,1)S(1)}, bf16[4,256,256]{2,1,0:T(8,128)(2,1)}, u32[]{:S(2)}) copy-start(bf16[4,256,256]{2,1,0:T(8,128)(2,1)} %get-tuple-element.132) | copy-start | bytes 1572868
  121.1 13.5 %collective-permute-start.17 = (bf16[4,256,256]{2,1,0:T(8,128)(2,1)}, bf16[4,256,256]{2,1,0:T(8,128)(2,1)S(1)}, u32[]{:S(2)}, u32[]{:S(2)}) collective-permute-start(bf16[4,256,256]{2,1,0:T(8,128)(2,1)} %get-tuple-element.131), channel_id=1, source_target_pairs={{0,32},{32,64},{64,96},{96,0},{1,33},{33,65},{65,97},{97,1},{2,34}... | collective-permute-start | bytes 1572872 | tf_op jit(solution)/shard_map/ppermute | solution.py:39
  132.2 2.3 copy-start.7
  134.9 7.5 %collective-permute-start.21 = (bf16[256,256]{1,0:T(8,128)(2,1)S(1)}, bf16[256,256]{1,0:T(8,128)(2,1)S(1)}, u32[]{:S(2)}, u32[]{:S(2)}) collective-permute-start(bf16[256,256]{1,0:T(8,128)(2,1)S(1)} %get-tuple-element.198), channel_id=1, source_target_pairs={{0,8},{8,0},{1,9},{9,1},{2,10},{10,2},{3,11},{11,3},{4,12},{12,4},... | collective-permute-start | bytes 393224 | tf_op jit(solution)/shard_map/ppermute | solution.py:39
  137.9 5.0 %collective-permute-start.22 = (bf16[256,256]{1,0:T(8,128)(2,1)S(1)}, bf16[256,256]{1,0:T(8,128)(2,1)S(1)}, u32[]{:S(2)}, u32[]{:S(2)}) collective-permute-start(bf16[256,256]{1,0:T(8,128)(2,1)S(1)} %get-tuple-element.197), channel_id=1, source_target_pairs={{0,16},{16,0},{1,17},{17,1},{2,18},{18,2},{3,19},{19,3},{4,20},{20... | collective-permute-start | bytes 393224 | tf_op jit(solution)/shard_map/ppermute | solution.py:39
  138.5 5.4 %collective-permute-start.23 = (bf16[256,256]{1,0:T(8,128)(2,1)S(1)}, bf16[256,256]{1,0:T(8,128)(2,1)S(1)}, u32[]{:S(2)}, u32[]{:S(2)}) collective-permute-start(bf16[256,256]{1,0:T(8,128)(2,1)S(1)} %get-tuple-element.196), channel_id=1, source_target_pairs={{0,24},{8,16},{16,8},{24,0},{1,25},{9,17},{17,9},{25,1},{2,26},{10... | collective-permute-start | bytes 393224 | tf_op jit(solution)/shard_map/ppermute | solution.py:39
  139.1 6.0 %collective-permute-start.24 = (bf16[256,256]{1,0:T(8,128)(2,1)S(1)}, bf16[256,256]{1,0:T(8,128)(2,1)S(1)}, u32[]{:S(2)}, u32[]{:S(2)}) collective-permute-start(bf16[256,256]{1,0:T(8,128)(2,1)S(1)} %get-tuple-element.194), channel_id=1, source_target_pairs={{0,96},{32,0},{64,32},{96,64},{1,97},{33,1},{65,33},{97,65},{2,98}... | collective-permute-start | bytes 393224 | tf_op jit(solution)/shard_map/ppermute | solution.py:39
  141.8 5.4 %collective-permute-start.25 = (bf16[256,256]{1,0:T(8,128)(2,1)S(1)}, bf16[256,256]{1,0:T(8,128)(2,1)S(1)}, u32[]{:S(2)}, u32[]{:S(2)}) collective-permute-start(bf16[256,256]{1,0:T(8,128)(2,1)S(1)} %get-tuple-element.193), channel_id=1, source_target_pairs={{0,64},{32,96},{64,0},{96,32},{1,65},{33,97},{65,1},{97,33},{2,66}... | collective-permute-start | bytes 393224 | tf_op jit(solution)/shard_map/ppermute | solution.py:39
  142.4 6.4 %collective-permute-start.26 = (bf16[256,256]{1,0:T(8,128)(2,1)S(1)}, bf16[256,256]{1,0:T(8,128)(2,1)S(1)}, u32[]{:S(2)}, u32[]{:S(2)}) collective-permute-start(bf16[256,256]{1,0:T(8,128)(2,1)S(1)} %get-tuple-element.192), channel_id=1, source_target_pairs={{0,32},{32,64},{64,96},{96,0},{1,33},{33,65},{65,97},{97,1},{2,34}... | collective-permute-start | bytes 393224 | tf_op jit(solution)/shard_map/ppermute | solution.py:39
  162.9 17.3 %collective-permute-start.27 = (bf16[128,4096]{1,0:T(8,128)(2,1)}, bf16[128,4096]{1,0:T(8,128)(2,1)S(1)}, u32[]{:S(2)}, u32[]{:S(2)}) collective-permute-start(bf16[128,4096]{1,0:T(8,128)(2,1)} %gate_back.1.grad_ref), channel_id=1, source_target_pairs={{1,0},{2,1},{3,2},{4,3},{5,4},{6,5},{7,6},{8,7},{9,8},{10,9},{11,1... | collective-permute-start | bytes 3145736 | tf_op jit(solution)/shard_map/ppermute | solution.py:27
  166.3 11.1 %copy-start.11 = (bf16[1024,256]{1,0:T(8,128)(2,1)S(1)}, bf16[1024,256]{1,0:T(8,128)(2,1)}, u32[]{:S(2)}) copy-start(bf16[1024,256]{1,0:T(8,128)(2,1)} %get-tuple-element.160) | copy-start | bytes 1572868
  177.4 15.5 %collective-permute-start.28 = (bf16[1024,256]{1,0:T(8,128)(2,1)S(1)}, bf16[1024,256]{1,0:T(8,128)(2,1)S(1)}, u32[]{:S(2)}, u32[]{:S(2)}) collective-permute-start(bf16[1024,256]{1,0:T(8,128)(2,1)S(1)} %copy-done.11), channel_id=1, source_target_pairs={{0,8},{8,0},{1,9},{9,1},{2,10},{10,2},{3,11},{11,3},{4,12},{12,4},... | collective-permute-start | bytes 1572872 | tf_op jit(solution)/shard_map/ppermute | solution.py:39
  193.6 2.4 collective-permute-start.30
  196.0 7.2 %collective-permute-start.31 = (f32[16,8,128]{2,1,0:T(8,128)S(1)}, f32[16,8,128]{2,1,0:T(8,128)S(1)}, u32[]{:S(2)}, u32[]{:S(2)}) collective-permute-start(f32[16,8,128]{2,1,0:T(8,128)S(1)} %get-tuple-element.200), channel_id=1, source_target_pairs={{0,2},{2,4},{4,6},{6,0},{1,3},{3,5},{5,7},{7,1},{8,10},{10,12},{12... | collective-permute-start | bytes 196616 | tf_op jit(solution)/shard_map/ppermute | solution.py:39
  196.3 7.1 %collective-permute-start.32 = (f32[16,8,128]{2,1,0:T(8,128)S(1)}, f32[16,8,128]{2,1,0:T(8,128)S(1)}, u32[]{:S(2)}, u32[]{:S(2)}) collective-permute-start(f32[16,8,128]{2,1,0:T(8,128)S(1)} %get-tuple-element.202), channel_id=1, source_target_pairs={{0,4},{2,6},{4,0},{6,2},{1,5},{3,7},{5,1},{7,3},{8,12},{10,14},{12... | collective-permute-start | bytes 196616 | tf_op jit(solution)/shard_map/ppermute | solution.py:39
  200.4 3.4 %collective-permute-start.33 = (f32[16,8,128]{2,1,0:T(8,128)S(1)}, f32[16,8,128]{2,1,0:T(8,128)S(1)}, u32[]{:S(2)}, u32[]{:S(2)}) collective-permute-start(f32[16,8,128]{2,1,0:T(8,128)S(1)} %get-tuple-element.201), channel_id=1, source_target_pairs={{0,6},{2,0},{4,2},{6,4},{1,7},{3,1},{5,3},{7,5},{8,14},{10,8},{12,... | collective-permute-start | bytes 196616 | tf_op jit(solution)/shard_map/ppermute | solution.py:39
  200.4 8.1 %collective-permute-start.29 = (bf16[3,8,4096]{2,1,0:T(8,128)(2,1)S(1)}, bf16[3,8,4096]{2,1,0:T(8,128)(2,1)S(1)}, u32[]{:S(2)}, u32[]{:S(2)}) collective-permute-start(bf16[3,8,4096]{2,1,0:T(8,128)(2,1)S(1)} %get-tuple-element.163), channel_id=1, source_target_pairs={{1,0},{2,1},{3,2},{4,3},{5,4},{6,5},{7,6},{8,7},{9,8},{10,9},{11,1... | collective-permute-start | bytes 589832 | tf_op jit(solution)/shard_map/ppermute | solution.py:27
  203.8 7.9 %collective-permute-start.34 = (f32[16,8,128]{2,1,0:T(8,128)S(1)}, f32[16,8,128]{2,1,0:T(8,128)S(1)}, u32[]{:S(2)}, u32[]{:S(2)}) collective-permute-start(f32[16,8,128]{2,1,0:T(8,128)S(1)} %fusion.1), channel_id=1, source_target_pairs={{0,32},{32,64},{64,96},{96,0},{1,33},{33,65},{65,97},{97,1},{2,34}... | collective-permute-start | bytes 196616 | tf_op jit(solution)/shard_map/ppermute | solution.py:39
  204.9 6.9 %collective-permute-start.35 = (f32[16,8,128]{2,1,0:T(8,128)S(1)}, f32[16,8,128]{2,1,0:T(8,128)S(1)}, u32[]{:S(2)}, u32[]{:S(2)}) collective-permute-start(f32[16,8,128]{2,1,0:T(8,128)S(1)} %fusion.1), channel_id=1, source_target_pairs={{0,64},{32,96},{64,0},{96,32},{1,65},{33,97},{65,1},{97,33},{2,66}... | collective-permute-start | bytes 196616 | tf_op jit(solution)/shard_map/ppermute | solution.py:39
  207.4 4.4 %collective-permute-start.36 = (f32[16,8,128]{2,1,0:T(8,128)S(1)}, f32[16,8,128]{2,1,0:T(8,128)S(1)}, u32[]{:S(2)}, u32[]{:S(2)}) collective-permute-start(f32[16,8,128]{2,1,0:T(8,128)S(1)} %fusion.1), channel_id=1, source_target_pairs={{0,96},{32,0},{64,32},{96,64},{1,97},{33,1},{65,33},{97,65},{2,98}... | collective-permute-start | bytes 196616 | tf_op jit(solution)/shard_map/ppermute | solution.py:39
  211.8 7.0 %collective-permute-start.37 = (f32[16,8,128]{2,1,0:T(8,128)S(1)}, f32[16,8,128]{2,1,0:T(8,128)S(1)}, u32[]{:S(2)}, u32[]{:S(2)}) collective-permute-start(f32[16,8,128]{2,1,0:T(8,128)S(1)} %add_add_fusion.1), channel_id=1, source_target_pairs={{0,8},{8,0},{1,9},{9,1},{2,10},{10,2},{3,11},{11,3},{4,12},{12,4},... | collective-permute-start | bytes 196616 | tf_op jit(solution)/shard_map/ppermute | solution.py:39
  212.7 6.0 %collective-permute-start.38 = (f32[16,8,128]{2,1,0:T(8,128)S(1)}, f32[16,8,128]{2,1,0:T(8,128)S(1)}, u32[]{:S(2)}, u32[]{:S(2)}) collective-permute-start(f32[16,8,128]{2,1,0:T(8,128)S(1)} %add_add_fusion.1), channel_id=1, source_target_pairs={{0,16},{16,0},{1,17},{17,1},{2,18},{18,2},{3,19},{19,3},{4,20},{20... | collective-permute-start | bytes 196616 | tf_op jit(solution)/shard_map/ppermute | solution.py:39
  214.1 4.6 %collective-permute-start.39 = (f32[16,8,128]{2,1,0:T(8,128)S(1)}, f32[16,8,128]{2,1,0:T(8,128)S(1)}, u32[]{:S(2)}, u32[]{:S(2)}) collective-permute-start(f32[16,8,128]{2,1,0:T(8,128)S(1)} %add_add_fusion.1), channel_id=1, source_target_pairs={{0,24},{8,16},{16,8},{24,0},{1,25},{9,17},{17,9},{25,1},{2,26},{10... | collective-permute-start | bytes 196616 | tf_op jit(solution)/shard_map/ppermute | solution.py:39
  215.5 9.9 %copy-start.6 = (bf16[1024,256]{1,0:T(8,128)(2,1)S(1)}, bf16[1024,256]{1,0:T(8,128)(2,1)}, u32[]{:S(2)}) copy-start(bf16[1024,256]{1,0:T(8,128)(2,1)} %get-tuple-element.126) | copy-start | bytes 1572868
  218.8 4.1 %collective-permute-start.40 = (f32[16,8,128]{2,1,0:T(8,128)S(1)}, f32[16,8,128]{2,1,0:T(8,128)S(1)}, u32[]{:S(2)}, u32[]{:S(2)}) collective-permute-start(f32[16,8,128]{2,1,0:T(8,128)S(1)} %add_add_fusion), channel_id=1, source_target_pairs={{0,1},{1,0},{2,3},{3,2},{4,5},{5,4},{6,7},{7,6},{8,9},{9,8},{10,11... | collective-permute-start | bytes 196616 | tf_op jit(solution)/shard_map/ppermute | solution.py:39
  222.9 6.9 %collective-permute-start.41 = (f32[32,8,128]{2,1,0:T(8,128)S(1)}, f32[32,8,128]{2,1,0:T(8,128)S(1)}, u32[]{:S(2)}, u32[]{:S(2)}) collective-permute-start(f32[32,8,128]{2,1,0:T(8,128)S(1)} %pad_maximum_fusion.3.refs_0_), channel_id=1, source_target_pairs={{0,6},{2,0},{4,2},{6,4},{1,7},{3,1},{5,3},{7,5},{8,14},{10,8},{12,... | collective-permute-start | bytes 393224 | tf_op jit(solution)/shard_map/ppermute | solution.py:39
  224.7 6.1 %collective-permute-start.42 = (f32[32,8,128]{2,1,0:T(8,128)S(1)}, f32[32,8,128]{2,1,0:T(8,128)S(1)}, u32[]{:S(2)}, u32[]{:S(2)}) collective-permute-start(f32[32,8,128]{2,1,0:T(8,128)S(1)} %pad_maximum_fusion.3.refs_0_), channel_id=1, source_target_pairs={{0,4},{2,6},{4,0},{6,2},{1,5},{3,7},{5,1},{7,3},{8,12},{10,14},{12... | collective-permute-start | bytes 393224 | tf_op jit(solution)/shard_map/ppermute | solution.py:39
  224.9 9.3 %collective-permute-start.43 = (f32[32,8,128]{2,1,0:T(8,128)S(1)}, f32[32,8,128]{2,1,0:T(8,128)S(1)}, u32[]{:S(2)}, u32[]{:S(2)}) collective-permute-start(f32[32,8,128]{2,1,0:T(8,128)S(1)} %pad_maximum_fusion.3.refs_0_), channel_id=1, source_target_pairs={{0,2},{2,4},{4,6},{6,0},{1,3},{3,5},{5,7},{7,1},{8,10},{10,12},{12... | collective-permute-start | bytes 393224 | tf_op jit(solution)/shard_map/ppermute | solution.py:39
Sparse Core Ops, SparseCore 0:
  46.3 54.9 all-gather.1
  103.7 56.2 reduce-scatter.1
